TPU v7x, 32 devices: a whole 2x2x4 slice. The times are simulated.
32 devices in a mesh: expert: 16 (over z, x, core), replica: 2 (over y).
Axes of the slice: x: 2, y: 2, z: 4, core: 2. Of those that a mesh axis runs over, the one named last changes fastest.
Arguments:
- tokens: bfloat16 [2048, 2048], P(('expert', 'replica')), may hold values from -6 to 6
- route_ids: int32 [2048, 6], P(('expert', 'replica')), may hold values from 0 to 15, all different within a row; in each aligned block of 64 rows (0 to 63, 64 to 127, ...) at most 32 rows name the same one
- gate_probs: float32 [2048, 6], P(('expert', 'replica')), may hold values from 0.05 to 0.35
- out_cot: bfloat16 [2048, 2048], P(('expert', 'replica')), may hold values from -6 to 6
- w_gate: bfloat16 [16, 2048, 768], P('expert'), may hold values from -0.125 to 0.125
- w_up: bfloat16 [16, 2048, 768], P('expert'), may hold values from -0.125 to 0.125
- w_down: bfloat16 [16, 768, 2048], P('expert'), may hold values from -0.21875 to 0.21875
Outputs:
- combined: bfloat16 [2048, 2048], P(('expert', 'replica'))
- grad_tokens: bfloat16 [2048, 2048], P(('expert', 'replica'))
- grad_gate: bfloat16 [16, 2048, 768], P('expert', 'replica')
- grad_up: bfloat16 [16, 2048, 768], P('expert', 'replica')
- grad_down: bfloat16 [16, 768, 2048], P('expert', 'replica')
Inputs may be any that keep to these rules, and one draw needn't show every extreme that they name: `route_ids`: A token's 6 experts differ. Among the 64 tokens of one device, at most 32 choose any one expert, and in every draw some device's tokens choose some expert exactly 32 times.
All inputs are finite; a program needn't handle non-finite values.
Results may differ from a plain program's by a relative error of at most 0.0095.
Values may be sent and summed in bfloat16 or wider, within the bound.
No kernel may reach another device: no remote copies, remote signals or barrier semaphores. Data moves between devices by JAX's collectives and lax.ppermute only.
A program may use at most 128 MiB of HBM per device.

v0:
```python
import jax
import jax.numpy as jnp
from jax import lax
from jax.sharding import PartitionSpec as P


def slots(routes, experts, capacity):
    flat_ids = routes.reshape(-1)
    one_hot = (flat_ids[:, None] == jnp.arange(experts, dtype=jnp.int32)[None, :]).astype(jnp.int32)
    before = jnp.cumsum(one_hot, axis=0) - one_hot
    slot_rank = jnp.sum(before * one_hot, axis=1)
    return flat_ids * capacity + slot_rank


def place(token_rows, positions, total_rows):
    return (
        jnp.zeros((total_rows, token_rows.shape[1]), token_rows.dtype).at[positions].set(token_rows)
    )


def hidden_rows(token_rows, gate_weight, up_weight):
    pre_gate = jnp.dot(token_rows, gate_weight, preferred_element_type=jnp.float32)
    pre_up = jnp.dot(token_rows, up_weight, preferred_element_type=jnp.float32)
    activation = (jax.nn.silu(pre_gate) * pre_up).astype(jnp.bfloat16)
    return (pre_gate, pre_up, activation)


def backward_rows(grad_rows, pre_gate, pre_up, gate_weight, up_weight, down_weight):
    contract = (((1,), (1,)), ((), ()))
    d_hidden = lax.dot_general(grad_rows, down_weight, contract, preferred_element_type=jnp.float32)
    sigmoid_gate = jax.nn.sigmoid(pre_gate)
    d_gate = (d_hidden * pre_up * sigmoid_gate * (1.0 + pre_gate * (1.0 - sigmoid_gate))).astype(
        jnp.bfloat16
    )
    d_up = (d_hidden * pre_gate * sigmoid_gate).astype(jnp.bfloat16)
    back_rows = lax.dot_general(d_gate, gate_weight, contract, preferred_element_type=jnp.float32)
    back_rows = back_rows + lax.dot_general(
        d_up, up_weight, contract, preferred_element_type=jnp.float32
    )
    return (back_rows.astype(jnp.bfloat16), d_gate, d_up)


def outer_sum(left, right):
    return lax.dot_general(
        left, right, (((0,), (0,)), ((), ())), preferred_element_type=jnp.float32
    )


def per_device(tokens, route_ids, gate_probs, out_cot, w_gate, w_up, w_down):
    experts = lax.axis_size("expert")
    tok_rows, features = tokens.shape
    top_count = route_ids.shape[1]
    hidden = w_gate.shape[2]
    capacity = max(2, tok_rows * top_count * 4 // (3 * experts))
    total_rows = experts * capacity
    positions = slots(route_ids, experts, capacity)
    gate_weight = w_gate[0]
    up_weight = w_up[0]
    down_weight = w_down[0]
    outgoing = place(jnp.repeat(tokens, top_count, axis=0), positions, total_rows).reshape(
        experts, capacity, features
    )
    slot_rows = lax.all_to_all(outgoing, "expert", split_axis=0, concat_axis=0, tiled=True)
    length = slot_rows.shape[1]
    flat_rows = slot_rows.reshape(-1, features)
    pre_gate, pre_up, expert_activation = hidden_rows(flat_rows, gate_weight, up_weight)
    result = jnp.dot(expert_activation, down_weight, preferred_element_type=jnp.float32).astype(
        jnp.bfloat16
    )
    returned = lax.all_to_all(
        result.reshape(experts, length, features), "expert", split_axis=0, concat_axis=0, tiled=True
    )
    results = (
        returned,
        slot_rows,
        pre_gate.reshape(experts, length, hidden),
        pre_up.reshape(experts, length, hidden),
        expert_activation.reshape(experts, length, hidden),
    )
    returned = results[0].reshape(-1, features)
    received = results[1].reshape(-1, features)
    pre_gate = results[2].reshape(-1, hidden)
    pre_up = results[3].reshape(-1, hidden)
    activation = results[4].reshape(-1, hidden)
    picked = returned[positions].reshape(tok_rows, top_count, features)
    combined = jnp.einsum("tk,tkd->td", gate_probs, picked.astype(jnp.float32)).astype(jnp.bfloat16)
    scaled = (gate_probs[:, :, None] * out_cot[:, None, :].astype(jnp.float32)).astype(jnp.bfloat16)
    grad_out = place(scaled.reshape(-1, features), positions, total_rows).reshape(
        experts, capacity, features
    )
    grads_in = lax.all_to_all(grad_out, "expert", split_axis=0, concat_axis=0, tiled=True).reshape(
        -1, features
    )
    back_rows, d_gate, d_up = backward_rows(
        grads_in, pre_gate, pre_up, gate_weight, up_weight, down_weight
    )
    returned_grad = lax.all_to_all(
        back_rows.reshape(experts, capacity, features),
        "expert",
        split_axis=0,
        concat_axis=0,
        tiled=True,
    )
    returned_grad = returned_grad.reshape(-1, features)
    grad_tokens = jnp.sum(
        returned_grad[positions].reshape(tok_rows, top_count, features).astype(jnp.float32), axis=1
    )
    grad_tokens = grad_tokens.astype(jnp.bfloat16)
    gate_up_grad = jnp.concatenate([d_gate, d_up], axis=1)
    gate_up_sum = lax.psum_scatter(
        outer_sum(received, gate_up_grad).astype(jnp.bfloat16),
        "replica",
        scatter_dimension=0,
        tiled=True,
    ).astype(jnp.float32)
    down_sum = lax.psum_scatter(
        outer_sum(activation, grads_in).astype(jnp.bfloat16),
        "replica",
        scatter_dimension=0,
        tiled=True,
    )
    grad_gate = gate_up_sum[:, :hidden].astype(jnp.bfloat16)[None]
    grad_up = gate_up_sum[:, hidden:].astype(jnp.bfloat16)[None]
    grad_down = down_sum[None]
    return (combined, grad_tokens, grad_gate, grad_up, grad_down)


def solution(mesh):
    placed = (
        P(("expert", "replica"), None),
        P(("expert", "replica"), None),
        P(("expert", "replica"), None),
        P(("expert", "replica"), None),
        P("expert", None, None),
        P("expert", None, None),
        P("expert", None, None),
    )
    return jax.shard_map(
        per_device,
        mesh=mesh,
        in_specs=placed,
        out_specs=(
            P(("expert", "replica"), None),
            P(("expert", "replica"), None),
            P("expert", "replica", None),
            P("expert", "replica", None),
            P("expert", "replica", None),
        ),
        check_vma=False,
    )
```

profile of v0, /device:TPU:0, one launch (start us, length us, event | category | flops | bytes accessed | tf_op | source)
XLA Modules:
  0.0 277.9 jit_solution(2630490425684895884)
XLA Ops:
  13.2 3.7 %reshape.129 = bf16[384,2048]{1,0:T(8,128)(2,1)} reshape(bf16[64,6,2048]{2,1,0:T(8,128)(2,1)} %broadcast_in_dim.8) | data formatting | bytes 3145728 | tf_op jit(solution)/shard_map/reshape | solution.py:60
  17.0 5.3 %scatter_custom_fusion = bf16[512,2048]{1,0:T(8,128)(2,1)} fusion(s32[384]{0:T(512)S(1)} %fusion.29, bf16[384,2048]{1,0:T(8,128)(2,1)} %reshape.129, bf16[]{:T(256)} %constant.5.clone.1), kind=kCustom, calls=%fused_computation.33 | custom fusion | bytes 2097664 | tf_op jit(solution)/shard_map/scatter | solution.py:17
  22.3 7.5 %all-to-all-start = ((bf16[16,32,2048]{2,1,0:T(8,128)(2,1)}), bf16[16,32,2048]{2,1,0:T(8,128)(2,1)}, u32[]{:S(2)}, u32[]{:S(2)}) async-start(bf16[16,32,2048]{2,1,0:T(8,128)(2,1)} %bitcast.72), calls=%async_computation | async-start | bytes 4194304 | tf_op jit(solution)/shard_map/all_to_all | solution.py:63
  32.5 4.8 %mul.71 = f32[384,2048]{1,0:T(8,128)} reshape(f32[64,6,2048]{2,1,0:T(8,128)} %mul.70) | data formatting | bytes 6291456 | tf_op jit(solution)/shard_map/mul | solution.py:87
  37.3 5.8 %scatter_custom_fusion.1 = bf16[512,2048]{1,0:T(8,128)(2,1)} fusion(s32[384]{0:T(512)S(1)} %fusion.29, f32[384,2048]{1,0:T(8,128)} %mul.71, f32[384]{0:T(512)S(1)} %mul.68, bf16[]{:T(256)} %constant.5.clone.1), kind=kCustom, calls=%fused_computation.21 | custom fusion | flops 1572864 | bytes 5244930 | tf_op jit(solution)/shard_map/scatter | solution.py:17
  43.1 27.9 %all-to-all-done = bf16[16,32,2048]{2,1,0:T(8,128)(2,1)} async-done(((bf16[16,32,2048]{2,1,0:T(8,128)(2,1)}), bf16[16,32,2048]{2,1,0:T(8,128)(2,1)}, u32[]{:S(2)}, u32[]{:S(2)}) %all-to-all-start) | async-done | bytes 2097184 | tf_op jit(solution)/shard_map/all_to_all | solution.py:63
  71.0 11.3 %all-to-all-start.2 = ((bf16[16,32,2048]{2,1,0:T(8,128)(2,1)}), bf16[16,32,2048]{2,1,0:T(8,128)(2,1)}, u32[]{:S(2)}, u32[]{:S(2)}) async-start(bf16[16,32,2048]{2,1,0:T(8,128)(2,1)} %bitcast.71), calls=%async_computation.2 | async-start | bytes 4194304 | tf_op jit(solution)/shard_map/all_to_all | solution.py:91
  82.5 5.5 %fusion.6 = f32[512,768]{1,0:T(8,128)} fusion(bf16[512,2048]{1,0:T(8,128)(2,1)} %bitcast.2, bf16[1,2048,768]{2,1,0:T(8,128)(2,1)} %param.12), kind=kOutput, calls=%fused_computation.13 | convolution fusion | flops 1610612736 | bytes 6815744 | tf_op jit(solution)/shard_map/dot_general | solution.py:23
  87.9 35.5 %all-to-all-done.2 = bf16[16,32,2048]{2,1,0:T(8,128)(2,1)} async-done(((bf16[16,32,2048]{2,1,0:T(8,128)(2,1)}), bf16[16,32,2048]{2,1,0:T(8,128)(2,1)}, u32[]{:S(2)}, u32[]{:S(2)}) %all-to-all-start.2) | async-done | bytes 2097184 | tf_op jit(solution)/shard_map/all_to_all | solution.py:91
  123.4 4.5 %fusion = f32[512,768]{1,0:T(8,128)S(1)} fusion(bf16[512,2048]{1,0:T(8,128)(2,1)} %bitcast.11, bf16[1,768,2048]{2,1,0:T(8,128)(2,1)} %param.13), kind=kOutput, calls=%fused_computation.7 | convolution fusion | flops 1610612736 | bytes 6815744 | tf_op jit(solution)/shard_map/dot_general | solution.py:30
  127.9 4.8 %multiply_convert_fusion.3 = (bf16[512,768]{1,0:T(8,128)(2,1)S(1)}, bf16[512,768]{1,0:T(8,128)(2,1)}, bf16[512,768]{1,0:T(8,128)(2,1)S(1)}) fusion(f32[512,768]{1,0:T(8,128)S(1)} %fusion, f32[512,768]{1,0:T(8,128)S(1)} %copy-done.6, bf16[512,2048]{1,0:T(8,128)(2,1)} %bitcast.2, bf16[1,2048,768]{2,1,0:T(8,128)(2,1)S(1)} %copy-done), kind=kOutput, calls=%fused_computation.28 | convolution fusion | flops 1616904192 | bytes 10747904 | tf_op jit(solution)/shard_map/dot_general | solution.py:22
  133.9 7.1 %convolution_convert_fusion = bf16[2048,1536]{1,0:T(8,128)(2,1)} fusion(bf16[512,2048]{1,0:T(8,128)(2,1)} %bitcast.2, bf16[512,768]{1,0:T(8,128)(2,1)S(1)} %get-tuple-element.9, bf16[512,768]{1,0:T(8,128)(2,1)S(1)} %get-tuple-element.7), kind=kOutput, calls=%fused_computation.4 | convolution fusion | flops 3227516928 | bytes 9961472 | tf_op jit(solution)/shard_map/dot_general | solution.py:44
  141.0 5.3 %fusion.12 = bf16[512,2048]{1,0:T(8,128)(2,1)} fusion(bf16[512,768]{1,0:T(8,128)(2,1)} %get-tuple-element.8, bf16[1,768,2048]{2,1,0:T(8,128)(2,1)} %param.13), kind=kOutput, calls=%fused_computation.20 | convolution fusion | flops 1611661312 | bytes 6029312 | tf_op jit(solution)/shard_map/dot_general | solution.py:67
  146.3 11.3 %all-to-all-start.1 = ((bf16[16,32,2048]{2,1,0:T(8,128)(2,1)}), bf16[16,32,2048]{2,1,0:T(8,128)(2,1)}, u32[]{:S(2)}, u32[]{:S(2)}) async-start(bf16[16,32,2048]{2,1,0:T(8,128)(2,1)} %bitcast.74), calls=%async_computation.1 | async-start | bytes 4194304 | tf_op jit(solution)/shard_map/all_to_all | solution.py:70
  157.8 5.3 %convolution_convert_fusion.1 = bf16[768,2048]{1,0:T(8,128)(2,1)} fusion(bf16[512,768]{1,0:T(8,128)(2,1)} %get-tuple-element.8, bf16[512,2048]{1,0:T(8,128)(2,1)} %bitcast.11), kind=kOutput, calls=%fused_computation.6 | convolution fusion | flops 1612185600 | bytes 6029312 | tf_op jit(solution)/shard_map/dot_general | solution.py:44
  163.2 4.0 %fusion.4 = f32[512,2048]{1,0:T(8,128)S(1)} fusion(bf16[512,768]{1,0:T(8,128)(2,1)} %copy-done.5, bf16[1,2048,768]{2,1,0:T(8,128)(2,1)} %param.12), kind=kOutput, calls=%fused_computation.11 | convolution fusion | flops 1610612736 | bytes 8126464 | tf_op jit(solution)/shard_map/dot_general | solution.py:37
  170.4 28.3 %all-to-all-done.1 = bf16[16,32,2048]{2,1,0:T(8,128)(2,1)} async-done(((bf16[16,32,2048]{2,1,0:T(8,128)(2,1)}), bf16[16,32,2048]{2,1,0:T(8,128)(2,1)}, u32[]{:S(2)}, u32[]{:S(2)}) %all-to-all-start.1) | async-done | bytes 2097184 | tf_op jit(solution)/shard_map/all_to_all | solution.py:70
  198.7 11.3 %all-to-all-start.3 = ((bf16[16,32,2048]{2,1,0:T(8,128)(2,1)}), bf16[16,32,2048]{2,1,0:T(8,128)(2,1)}, u32[]{:S(2)}, u32[]{:S(2)}) async-start(bf16[16,32,2048]{2,1,0:T(8,128)(2,1)} %bitcast.73), calls=%async_computation.3 | async-start | bytes 4194304 | tf_op jit(solution)/shard_map/all_to_all | solution.py:97
  210.1 6.9 %gather_fusion = bf16[384,2048]{1,0:T(8,128)(2,1)} fusion(bf16[512,2048]{1,0:T(8,128)(2,1)} %bitcast.7, s32[1024]{0:T(1024)S(1)} %pad_clamp_fusion), kind=kCustom, calls=%fused_computation | custom fusion | bytes 3147264 | tf_op jit(solution)/shard_map/gather | solution.py:85
  223.9 27.3 %all-to-all-done.3 = bf16[16,32,2048]{2,1,0:T(8,128)(2,1)} async-done(((bf16[16,32,2048]{2,1,0:T(8,128)(2,1)}), bf16[16,32,2048]{2,1,0:T(8,128)(2,1)}, u32[]{:S(2)}, u32[]{:S(2)}) %all-to-all-start.3) | async-done | bytes 2097184 | tf_op jit(solution)/shard_map/all_to_all | solution.py:97
  251.2 6.9 %gather_fusion.1 = bf16[384,2048]{1,0:T(8,128)(2,1)} fusion(bf16[512,2048]{1,0:T(8,128)(2,1)} %bitcast.13, s32[1024]{0:T(1024)S(1)} %pad_clamp_fusion), kind=kCustom, calls=%fused_computation.1 | custom fusion | bytes 3147264 | tf_op jit(solution)/shard_map/gather | solution.py:106
  258.1 3.7 %reshape.108 = bf16[64,6,2048]{2,1,0:T(8,128)(2,1)} reshape(bf16[384,2048]{1,0:T(8,128)(2,1)} %gather_fusion.1) | data formatting | bytes 3145728 | tf_op jit(solution)/shard_map/reshape | solution.py:106
  261.8 3.8 %reduce_sum.25 = bf16[64,2048]{1,0:T(8,128)(2,1)} reduce(bf16[64,6,2048]{2,1,0:T(8,128)(2,1)} %reshape.108, bf16[]{:T(256)} %constant.5.clone.1), dimensions={1}, to_apply=%region_5.6 | reduce | flops 655360 | bytes 1835010 | tf_op jit(solution)/shard_map/reduce_sum | solution.py:105
  265.5 3.7 %slice_bitcast_fusion = (bf16[1,1024,768]{2,1,0:T(8,128)(2,1)}, bf16[1,1024,768]{2,1,0:T(8,128)(2,1)}) fusion(bf16[1024,1536]{1,0:T(8,128)(2,1)} %reduce-scatter.3.cloned.1.call-done), kind=kLoop, calls=%fused_computation.22 | loop fusion | bytes 6291456 | tf_op jit(solution)/shard_map/broadcast_in_dim | solution.py:123
  (42 shorter events, 22.4 us)
Async XLA Ops:
  7.2 120.7 %copy-start = (bf16[1,2048,768]{2,1,0:T(8,128)(2,1)S(1)}, bf16[1,2048,768]{2,1,0:T(8,128)(2,1)}, u32[]{:S(2)}) copy-start(bf16[1,2048,768]{2,1,0:T(8,128)(2,1)} %param.11) | copy-start | bytes 9437188
  22.3 7.6 %copy-start.2 = (f32[64,6]{0,1:T(8,128)S(1)}, f32[64,6]{0,1:T(8,128)}, u32[]{:S(2)}) copy-start(f32[64,6]{0,1:T(8,128)} %param.9) | copy-start | bytes 4612
  22.3 7.8 %copy-start.1 = (bf16[64,2048]{1,0:T(8,128)(2,1)S(1)}, bf16[64,2048]{1,0:T(8,128)(2,1)}, u32[]{:S(2)}) copy-start(bf16[64,2048]{1,0:T(8,128)(2,1)} %param.10) | copy-start | bytes 786436
  22.3 48.7 %all-to-all-start = ((bf16[16,32,2048]{2,1,0:T(8,128)(2,1)}), bf16[16,32,2048]{2,1,0:T(8,128)(2,1)}, u32[]{:S(2)}, u32[]{:S(2)}) async-start(bf16[16,32,2048]{2,1,0:T(8,128)(2,1)} %bitcast.72), calls=%async_computation | async-start | bytes 4194304 | tf_op jit(solution)/shard_map/all_to_all | solution.py:63
  71.0 52.4 %all-to-all-start.2 = ((bf16[16,32,2048]{2,1,0:T(8,128)(2,1)}), bf16[16,32,2048]{2,1,0:T(8,128)(2,1)}, u32[]{:S(2)}, u32[]{:S(2)}) async-start(bf16[16,32,2048]{2,1,0:T(8,128)(2,1)} %bitcast.71), calls=%async_computation.2 | async-start | bytes 4194304 | tf_op jit(solution)/shard_map/all_to_all | solution.py:91
  82.2 183.3 %reduce-scatter.3.cloned.1.call-start = ((), (), s32[]{:S(2)}) async-start(), calls=%async_computation.6 | async-start | bytes 9437184 | tf_op jit(solution)/shard_map/reduce_scatter | solution.py:110
  123.4 4.5 %copy-start.6 = (f32[512,768]{1,0:T(8,128)S(1)}, f32[512,768]{1,0:T(8,128)}, u32[]{:S(2)}) copy-start(f32[512,768]{1,0:T(8,128)} %fusion.6) | copy-start | bytes 4718596
  132.7 0.9 copy-start.3
  132.7 1.1 copy-start.5
  146.3 52.4 %all-to-all-start.1 = ((bf16[16,32,2048]{2,1,0:T(8,128)(2,1)}), bf16[16,32,2048]{2,1,0:T(8,128)(2,1)}, u32[]{:S(2)}, u32[]{:S(2)}) async-start(bf16[16,32,2048]{2,1,0:T(8,128)(2,1)} %bitcast.74), calls=%async_computation.1 | async-start | bytes 4194304 | tf_op jit(solution)/shard_map/all_to_all | solution.py:70
  157.6 113.5 %reduce-scatter.5.cloned.1.call-start = ((), (), s32[]{:S(2)}) async-start(), calls=%async_computation.7 | async-start | bytes 4718592 | tf_op jit(solution)/shard_map/reduce_scatter | solution.py:116
  163.2 4.0 %copy-start.4 = (bf16[512,768]{1,0:T(8,128)(2,1)S(1)}, bf16[512,768]{1,0:T(8,128)(2,1)}, u32[]{:S(2)}) copy-start(bf16[512,768]{1,0:T(8,128)(2,1)} %copy-done.3) | copy-start | bytes 2359300
  198.7 52.4 %all-to-all-start.3 = ((bf16[16,32,2048]{2,1,0:T(8,128)(2,1)}), bf16[16,32,2048]{2,1,0:T(8,128)(2,1)}, u32[]{:S(2)}, u32[]{:S(2)}) async-start(bf16[16,32,2048]{2,1,0:T(8,128)(2,1)} %bitcast.73), calls=%async_computation.3 | async-start | bytes 4194304 | tf_op jit(solution)/shard_map/all_to_all | solution.py:97
Sparse Core Ops, SparseCore 0:
  141.1 83.5 reduce-scatter.2
  227.7 43.3 reduce-scatter.4
where the time goes:
time: 283 us; the launch traced here: 278 us
  waiting for transfers between devices  121 us (43%)
  local copies, waits for them, and re-layouts  47.7 us (17%)
  matrix products  41.9 us (15%)
  starting transfers between devices  41.8 us (15%)
  between operations  14.2 us (5%)
  other arithmetic  11.5 us (4%)
    all_to_all x1, waiting for transfers between devices, per_device(): lax.all_to_all(grad_out, 'expert', split_axis=0, concat_axis=0, tiled=True)  35.5 us
    all_to_all x1, waiting for transfers between devices, per_device(): lax.all_to_all(result.reshape(experts, length, features), 'expert', split...  28.3 us
    all_to_all x1, waiting for transfers between devices, per_device(): lax.all_to_all(outgoing, 'expert', split_axis=0, concat_axis=0, tiled=True)  27.9 us
    all_to_all x1, waiting for transfers between devices, per_device(): lax.all_to_all(back_rows.reshape(experts, capacity, features), 'expert',...  27.3 us
    dot_general x2, matrix products, outer_sum(): lax.dot_general(left, right, (((0,), (0,)), ((), ())), preferred_element_...  12.4 us
    all_to_all x1, starting transfers between devices, per_device(): lax.all_to_all(result.reshape(experts, length, features), 'expert', split...  11.3 us
    all_to_all x1, starting transfers between devices, per_device(): lax.all_to_all(grad_out, 'expert', split_axis=0, concat_axis=0, tiled=True)  11.3 us
    all_to_all x1, starting transfers between devices, per_device(): lax.all_to_all(back_rows.reshape(experts, capacity, features), 'expert',...  11.3 us
  transfers between devices with their start and end apart: 6, of which 5 were waited for; matrix products, arithmetic and copies ran while one was open for 25% of the time, Pallas kernels for 0%

commit v1 on v0

v1 whole, which is shorter than its diff:
```python
import jax
import jax.numpy as jnp
from jax import lax
from jax.sharding import PartitionSpec as P

BF = jnp.bfloat16
F32 = jnp.float32


def slots(routes, experts, capacity):
    flat_ids = routes.reshape(-1)
    one_hot = (flat_ids[:, None] == jnp.arange(experts, dtype=jnp.int32)[None, :]).astype(jnp.int32)
    before = jnp.cumsum(one_hot, axis=0) - one_hot
    slot_rank = jnp.sum(before * one_hot, axis=1)
    return flat_ids * capacity + slot_rank


def place(token_rows, positions, total_rows):
    return (
        jnp.zeros((total_rows, token_rows.shape[1]), token_rows.dtype).at[positions].set(token_rows)
    )


def hidden_rows(token_rows, gate_weight, up_weight):
    pre_gate = jnp.dot(token_rows, gate_weight, preferred_element_type=F32)
    pre_up = jnp.dot(token_rows, up_weight, preferred_element_type=F32)
    activation = (jax.nn.silu(pre_gate) * pre_up).astype(BF)
    return (pre_gate, pre_up, activation)


CONTRACT = (((1,), (1,)), ((), ()))


def hidden_grads(grad_rows, pre_gate, pre_up, down_weight):
    d_hidden = lax.dot_general(grad_rows, down_weight, CONTRACT, preferred_element_type=F32)
    sigmoid_gate = jax.nn.sigmoid(pre_gate)
    d_gate = (d_hidden * pre_up * sigmoid_gate * (1.0 + pre_gate * (1.0 - sigmoid_gate))).astype(BF)
    d_up = (d_hidden * pre_gate * sigmoid_gate).astype(BF)
    return d_gate, d_up


def input_rows(d_gate, d_up, gate_weight, up_weight):
    back_rows = lax.dot_general(d_gate, gate_weight, CONTRACT, preferred_element_type=F32)
    back_rows = back_rows + lax.dot_general(d_up, up_weight, CONTRACT, preferred_element_type=F32)
    return back_rows.astype(BF)


def outer_sum(left, right):
    return lax.dot_general(left, right, (((0,), (0,)), ((), ())), preferred_element_type=F32)


def routed_plan(tokens, route_ids, gate_probs, out_cot, w_gate, w_up, w_down):
    experts = lax.axis_size("expert")
    tok_rows, features = tokens.shape
    top_count = route_ids.shape[1]
    hidden = w_gate.shape[2]
    capacity = max(2, tok_rows * top_count * 4 // (3 * experts))
    total_rows = experts * capacity
    positions = slots(route_ids, experts, capacity)
    gate_weight, up_weight, down_weight = w_gate[0], w_up[0], w_down[0]

    def exchange(rows):
        blocks = rows.reshape(experts, capacity, features)
        return lax.all_to_all(blocks, "expert", 0, 0, tiled=True).reshape(-1, features)

    received = exchange(place(jnp.repeat(tokens, top_count, axis=0), positions, total_rows))
    pre_gate, pre_up, activation = hidden_rows(received, gate_weight, up_weight)
    result = jnp.dot(activation, down_weight, preferred_element_type=F32).astype(BF)
    picked = exchange(result)[positions].reshape(tok_rows, top_count, features)
    combined = jnp.einsum("tk,tkd->td", gate_probs, picked.astype(F32)).astype(BF)
    scaled = (gate_probs[:, :, None] * out_cot[:, None, :].astype(F32)).astype(BF)
    grads_in = exchange(place(scaled.reshape(-1, features), positions, total_rows))
    d_gate, d_up = hidden_grads(grads_in, pre_gate, pre_up, down_weight)
    back = exchange(input_rows(d_gate, d_up, gate_weight, up_weight))
    grad_tokens = jnp.sum(
        back[positions].reshape(tok_rows, top_count, features).astype(F32), axis=1
    ).astype(BF)
    gate_up_sum = lax.psum_scatter(
        outer_sum(received, jnp.concatenate([d_gate, d_up], axis=1)).astype(BF),
        "replica",
        scatter_dimension=0,
        tiled=True,
    )
    down_sum = lax.psum_scatter(
        outer_sum(activation, grads_in).astype(BF), "replica", scatter_dimension=0, tiled=True
    )
    return (
        combined,
        grad_tokens,
        gate_up_sum[:, :hidden][None],
        gate_up_sum[:, hidden:][None],
        down_sum[None],
    )


def split3(value):
    high = value.astype(BF)
    rest = value - high.astype(F32)
    mid = rest.astype(BF)
    low = (rest - mid.astype(F32)).astype(BF)
    return high, mid, low


def dense_plan(tokens, route_ids, gate_probs, out_cot, w_gate, w_up, w_down):
    experts = lax.axis_size("expert")
    tok_rows, features = tokens.shape
    top_count = route_ids.shape[1]
    hidden = w_gate.shape[2]
    capacity = max(2, tok_rows * top_count * 4 // (3 * experts))
    expert = lax.axis_index("expert")
    replica = lax.axis_index("replica")
    core = expert % 2
    gate_weight, up_weight, down_weight = w_gate[0], w_up[0], w_down[0]

    chosen = route_ids[:, :, None] == jnp.arange(experts, dtype=jnp.int32)
    share = jnp.sum(jnp.where(chosen, gate_probs[:, :, None], 0.0), axis=1)
    pad = -(3 * experts) % 128
    payload = jnp.concatenate(
        [tokens, out_cot, *split3(share), jnp.zeros((tok_rows, pad), BF)], axis=1
    )
    width = payload.shape[1]
    own = lax.all_gather(payload, "expert", axis=0, tiled=False)
    mine = lax.dynamic_index_in_dim(own.reshape(experts // 2, 2, tok_rows, width), core, 1, False)
    relay = lax.ppermute(mine, "replica", [(0, 1), (1, 0)])
    sibling = lax.ppermute(relay, "expert", [(i, i ^ 1) for i in range(experts)])
    other = jnp.stack([relay, sibling], axis=1).reshape(experts, tok_rows, width)

    together = 4
    groups = experts // together
    length = together * tok_rows
    room = together * capacity

    def pack(rows):
        rows = rows.reshape(groups, length, width)
        at = 2 * features + expert
        weight = sum(
            lax.dynamic_slice_in_dim(rows, at + i * experts, 1, 2)[:, :, 0].astype(F32)
            for i in range(3)
        )
        routed = weight > 0
        rank = jnp.cumsum(routed.astype(jnp.int32), axis=1) - 1
        pick = (rank[:, None, :] == jnp.arange(room)[None, :, None]) & routed[:, None, :]
        row_weight = jnp.sum(jnp.where(pick, weight[:, None, :], 0.0), axis=2).reshape(-1, 1)
        pick = pick.astype(BF)
        packed = jnp.einsum(
            "gst,gtd->gsd", pick, rows[:, :, : 2 * features], preferred_element_type=F32
        ).reshape(groups * room, 2 * features)
        x = packed[:, :features].astype(BF)
        cot = (row_weight * packed[:, features:]).astype(BF)
        return pick, row_weight, x, cot

    def spread(pick, rows):
        rows = rows.reshape(groups, room, features)
        return jnp.einsum("gst,gsd->gtd", pick, rows, preferred_element_type=F32).astype(BF)

    def middle(x, cot):
        pre_gate, pre_up, activation = hidden_rows(x, gate_weight, up_weight)
        d_gate, d_up = hidden_grads(cot, pre_gate, pre_up, down_weight)
        return activation, d_gate, d_up

    pick, row_weight, x, cot = pack(own)
    activation, d_gate, d_up = middle(x, cot)
    result = jnp.dot(activation, down_weight, preferred_element_type=F32).astype(BF)
    result = (row_weight * result.astype(F32)).astype(BF)
    back = input_rows(d_gate, d_up, gate_weight, up_weight)
    dense = jnp.concatenate([spread(pick, result), spread(pick, back)], axis=2)
    summed = lax.psum_scatter(
        dense.reshape(experts * tok_rows, 2 * features),
        "expert",
        scatter_dimension=0,
        tiled=True,
    )
    combined, grad_tokens = summed[:, :features], summed[:, features:]

    _, _, x2, cot2 = pack(other)
    activation2, d_gate2, d_up2 = middle(x2, cot2)
    both = lambda a, b: jnp.concatenate([a, b], axis=0)
    half = features // 2
    xs = lax.dynamic_slice_in_dim(both(x, x2), replica * half, half, 1)
    acts = lax.dynamic_slice_in_dim(
        both(activation, activation2), replica * (hidden // 2), hidden // 2, 1
    )
    grad_gate = outer_sum(xs, both(d_gate, d_gate2)).astype(BF)[None]
    grad_up = outer_sum(xs, both(d_up, d_up2)).astype(BF)[None]
    grad_down = outer_sum(acts, both(cot, cot2)).astype(BF)[None]
    return (combined, grad_tokens, grad_gate, grad_up, grad_down)


def solution(mesh):
    experts, replicas = mesh.shape["expert"], mesh.shape["replica"]
    placed = (
        P(("expert", "replica"), None),
        P(("expert", "replica"), None),
        P(("expert", "replica"), None),
        P(("expert", "replica"), None),
        P("expert", None, None),
        P("expert", None, None),
        P("expert", None, None),
    )
    small = replicas == 2 and experts <= 32 and experts % 4 == 0
    return jax.shard_map(
        dense_plan if small else routed_plan,
        mesh=mesh,
        in_specs=placed,
        out_specs=(
            P(("expert", "replica"), None),
            P(("expert", "replica"), None),
            P("expert", "replica", None),
            P("expert", "replica", None),
            P("expert", "replica", None),
        ),
        check_vma=False,
    )
```

time: 283 us -> 262 us (0.926); the launches traced: 278 us -> 261 us
  starting transfers between devices: 41.8 us -> 1.58 us
  waiting for transfers between devices: 121 us -> 150 us
  local copies, waits for them, and re-layouts: 47.7 us -> 32.9 us
  other arithmetic: 11.5 us -> 20.3 us
    all_to_all x4 -> x0, waiting for transfers between devices: 119 us -> none  [the longest x1 35.5 us: per_device(): lax.all_to_all(grad_out, 'expert', split_axis=0, concat_axis=0, tiled=True)]
    all_gather x0 -> x1, waiting for transfers between devices: none -> 79.7 us  [dense_plan(): own = lax.all_gather(payload, 'expert', axis=0, tiled=False)]
    ppermute x0 -> x2, waiting for transfers between devices: none -> 69.9 us  [the longest x1 66.1 us: dense_plan(): relay = lax.ppermute(mine, 'replica', [(0, 1), (1, 0)])]
    all_to_all x4 -> x0, starting transfers between devices: 41.3 us -> none  [the longest x1 11.3 us: per_device(): lax.all_to_all(result.reshape(experts, length, features), 'expert', split...]
    gather x2 -> x0, local copies, waits for them, and re-layouts: 13.8 us -> none  [the longest x1 6.91 us: per_device(): picked = returned[positions].reshape(tok_rows, top_count, features)]
    reshape x3 -> x0, local copies, waits for them, and re-layouts: 11.1 us -> none  [the longest x1 3.7 us: per_device(): returned_grad[positions].reshape(tok_rows, top_count, features)]
    another operation x2 -> x5, other arithmetic: 0.91 us -> 10.4 us  [the longest x1 7.91 us: dense_plan(): jnp.stack([relay, sibling], axis=1).reshape(experts, tok_rows, width)]
    another operation x0 -> x7, local copies, waits for them, and re-layouts: none -> 8.3 us  [the longest x1 7.92 us: dense_plan(): jnp.stack([relay, sibling], axis=1).reshape(experts, tok_rows, width)]
  transfers between devices with their start and end apart: 6 -> 4, of which waited for: 5 -> 3; matrix products, arithmetic and copies ran while one was open for 25% -> 28% of each run, Pallas kernels for 0% -> 0%
where the time goes in v1:
time: 262 us; the launch traced here: 261 us
  waiting for transfers between devices  150 us (57%)
  matrix products  42.6 us (16%)
  local copies, waits for them, and re-layouts  32.9 us (13%)
  other arithmetic  20.3 us (8%)
  between operations  14.4 us (5%)
    all_gather x1, waiting for transfers between devices, dense_plan(): own = lax.all_gather(payload, 'expert', axis=0, tiled=False)  79.7 us
    ppermute x1, waiting for transfers between devices, dense_plan(): relay = lax.ppermute(mine, 'replica', [(0, 1), (1, 0)])  66.1 us
    dot_general x2, matrix products, pack(): jnp.einsum('gst,gtd->gsd', pick, rows[:, :, :2 * features], preferred_ele...  9.53 us
    unnamed x44, local copies, waits for them, and re-layouts  9.06 us
    dot_general x3, matrix products, outer_sum(): lax.dot_general(left, right, (((0,), (0,)), ((), ())), preferred_element_...  9.01 us
    another operation x1, local copies, waits for them, and re-layouts, dense_plan(): jnp.stack([relay, sibling], axis=1).reshape(experts, tok_rows, width)  7.92 us
    another operation x1, other arithmetic, dense_plan(): jnp.stack([relay, sibling], axis=1).reshape(experts, tok_rows, width)  7.91 us
    concatenate x1, other arithmetic, dense_plan(): dense = jnp.concatenate([spread(pick, result), spread(pick, back)], axis=2)  7.85 us
  transfers between devices with their start and end apart: 4, of which 3 were waited for; matrix products, arithmetic and copies ran while one was open for 28% of the time, Pallas kernels for 0%

profile of v1, /device:TPU:0, one launch (start us, length us, event | category | flops | bytes accessed | tf_op | source)
XLA Modules:
  0.0 261.5 jit_solution(14212880771028440964)
XLA Ops:
  8.4 1.9 concatenate.21
  10.4 79.7 %all-gather.3.cloned.1.call-done = bf16[1024,4224]{1,0:T(8,128)(2,1)} async-done(((bf16[64,4224]{1,0:T(8,128)(2,1)}), bf16[1024,4224]{1,0:T(8,128)(2,1)}) %all-gather.3.cloned.1.call-update) | async-done | bytes 8650768 | tf_op jit(solution)/shard_map/all_gather | solution.py:122
  90.1 2.3 constant_dynamic-slice_fusion.5
  96.5 4.8 %fusion.2 = f32[4,128,4096]{2,1,0:T(8,128)S(1)} fusion(bf16[4,256,4224]{2,1,0:T(8,128)(2,1)} %bitcast.94, s32[4,256]{1,0:T(4,128)S(1)} %bitcast.100, pred[4,256]{1,0:T(4,128)(4,1)S(1)} %get-tuple-element.7), kind=kOutput, calls=%fused_computation.3 | convolution fusion | flops 1074003968 | bytes 16782336 | tf_op jit(solution)/shard_map/gst,gtd->gsd/dot_general | solution.py:145
  102.4 2.5 dynamic-slice_bitcast_fusion
  106.5 1.8 fusion.26
  112.1 2.3 multiply_convert_fusion.6
  116.2 3.3 %convolution_convert_fusion.1 = bf16[4,256,2048]{2,1,0:T(8,128)(2,1)} fusion(bf16[4,128,2048]{2,1,0:T(8,128)(2,1)S(1)} %bitcast.99, s32[4,256]{1,0:T(4,128)S(1)} %bitcast.102, pred[4,256]{1,0:T(4,128)(4,1)S(1)} %get-tuple-element.7), kind=kOutput, calls=%fused_computation.22 | convolution fusion | flops 539230208 | bytes 6296576 | tf_op jit(solution)/shard_map/gst,gsd->gtd/dot_general | solution.py:154
  121.3 1.9 add_convert_fusion
  123.2 3.5 %convolution_convert_fusion = bf16[4,256,2048]{2,1,0:T(8,128)(2,1)} fusion(bf16[4,128,2048]{2,1,0:T(8,128)(2,1)S(1)} %bitcast.98, s32[4,256]{1,0:T(4,128)S(1)} %bitcast.103, pred[4,256]{1,0:T(4,128)(4,1)S(1)} %get-tuple-element.7), kind=kOutput, calls=%fused_computation.21 | convolution fusion | flops 539230208 | bytes 6296576 | tf_op jit(solution)/shard_map/gst,gsd->gtd/dot_general | solution.py:154
  126.7 7.8 %pad_maximum_fusion.1 = bf16[4,256,4096]{2,1,0:T(8,128)(2,1)} fusion(bf16[4,256,2048]{2,1,0:T(8,128)(2,1)} %convolution_convert_fusion, bf16[4,256,2048]{2,1,0:T(8,128)(2,1)} %convolution_convert_fusion.1), kind=kLoop, calls=%fused_computation.5 | loop fusion | flops 16777216 | bytes 16777216 | tf_op jit(solution)/shard_map/concatenate | solution.py:166
  134.6 66.1 %collective-permute-done = bf16[8,64,4224]{2,1,0:T(8,128)(2,1)} collective-permute-done((bf16[8,64,4224]{2,1,0:T(8,128)(2,1)}, bf16[8,64,4224]{2,1,0:T(8,128)(2,1)}, u32[]{:S(2)}, u32[]{:S(2)}) %collective-permute-start) | collective-permute-done | bytes 4325408 | tf_op jit(solution)/shard_map/ppermute | solution.py:124
  200.7 3.9 %slice.73 = bf16[512,2048]{1,0:T(8,128)(2,1)} slice(f32[512,4096]{1,0:T(8,128)} %bitcast.88), slice={[0:512], [0:2048]} | slice | bytes 4194304 | tf_op jit(solution)/shard_map/slice | solution.py:148
  204.6 3.8 %collective-permute-done.1 = bf16[8,64,4224]{2,1,0:T(8,128)(2,1)} collective-permute-done((bf16[8,64,4224]{2,1,0:T(8,128)(2,1)}, bf16[8,64,4224]{2,1,0:T(8,128)(2,1)}, u32[]{:S(2)}, u32[]{:S(2)}) %collective-permute-start.1) | collective-permute-done | bytes 4325408 | tf_op jit(solution)/shard_map/ppermute | solution.py:125
  208.4 7.9 %pad_maximum_fusion = bf16[8,2,64,4224]{3,2,0,1:T(8,128)(2,1)} fusion(bf16[8,1,64,4224]{3,2,0,1:T(8,128)(2,1)} %bitcast.15, bf16[8,1,64,4224]{3,2,0,1:T(8,128)(2,1)} %bitcast.14), kind=kLoop, calls=%fused_computation | loop fusion | flops 4325376 | bytes 17301504 | tf_op jit(solution)/shard_map/stack | solution.py:126
  216.3 7.9 %copy.74 = bf16[8,2,64,4224]{3,2,1,0:T(8,128)(2,1)} copy(bf16[8,2,64,4224]{3,2,0,1:T(8,128)(2,1)} %pad_maximum_fusion) | data formatting | bytes 17301504 | tf_op jit(solution)/shard_map/stack | solution.py:126
  224.2 2.3 constant_dynamic-slice_fusion.2
  230.5 4.7 %fusion = f32[4,128,4096]{2,1,0:T(8,128)S(1)} fusion(bf16[4,256,4224]{2,1,0:T(8,128)(2,1)} %bitcast.83, s32[4,256]{1,0:T(4,128)S(1)} %bitcast.104, pred[4,256]{1,0:T(4,128)(4,1)S(1)} %get-tuple-element.5), kind=kOutput, calls=%fused_computation.1 | convolution fusion | flops 1074003968 | bytes 16782336 | tf_op jit(solution)/shard_map/gst,gtd->gsd/dot_general | solution.py:145
  237.7 1.8 fusion.10
  241.4 2.3 multiply_convert_fusion.1
  243.8 3.0 %fusion.38 = bf16[1,384,2048]{2,1,0:T(8,128)(2,1)} fusion(bf16[512,2048]{1,0:T(8,128)(2,1)S(1)} %fusion.4, bf16[512,2048]{1,0:T(8,128)(2,1)S(1)} %copy-done.3, s32[]{:T(128)S(6)} %select_n.49, bf16[512,768]{1,0:T(8,128)(2,1)S(1)} %copy-done.14, bf16[512,768]{1,0:T(8,128)(2,1)S(1)} %get-tuple-element.15), kind=kOutput, calls=%fused_computation.43 | convolution fusion | flops 1621360640 | bytes 7340036 | tf_op jit(solution)/shard_map/dot_general | solution.py:49
  246.8 3.0 %fusion.48 = bf16[1,1024,768]{2,1,0:T(8,128)(2,1)} fusion(bf16[512,768]{1,0:T(8,128)(2,1)S(1)} %get-tuple-element.16, bf16[512,768]{1,0:T(8,128)(2,1)S(1)} %copy-done.10, s32[]{:T(128)S(6)} %select_n.47, bf16[512,2048]{1,0:T(8,128)(2,1)S(1)} %copy-done.4, bf16[512,2048]{1,0:T(8,128)(2,1)S(1)} %slice.72), kind=kOutput, calls=%fused_computation.63 | convolution fusion | flops 1618739200 | bytes 7340036 | tf_op jit(solution)/shard_map/dot_general | solution.py:49
  249.8 3.0 %fusion.51 = bf16[1,1024,768]{2,1,0:T(8,128)(2,1)} fusion(bf16[512,768]{1,0:T(8,128)(2,1)S(1)} %get-tuple-element.17, bf16[512,768]{1,0:T(8,128)(2,1)S(1)} %copy-done.12, s32[]{:T(128)S(6)} %select_n.47, bf16[512,2048]{1,0:T(8,128)(2,1)S(1)} %copy-done.4, bf16[512,2048]{1,0:T(8,128)(2,1)S(1)} %slice.72), kind=kOutput, calls=%fused_computation.64 | convolution fusion | flops 1618739200 | bytes 7340036 | tf_op jit(solution)/shard_map/dot_general | solution.py:49
  252.8 1.9 fusion.81
  (87 shorter events, 23.6 us)
Async XLA Ops:
  7.2 104.9 %copy-start = (bf16[1,2048,768]{2,1,0:T(8,128)(2,1)S(1)}, bf16[1,2048,768]{2,1,0:T(8,128)(2,1)}, u32[]{:S(2)}) copy-start(bf16[1,2048,768]{2,1,0:T(8,128)(2,1)} %param.12) | copy-start | bytes 9437188
  7.2 83.0 %all-gather.3.cloned.1.call-start = ((), (), s32[]{:S(2)}) async-start(), calls=%async_computation.2 | async-start | bytes 9191424 | tf_op jit(solution)/shard_map/all_gather | solution.py:122
  10.3 242.4 %reduce-scatter.2.cloned.1.call-start = ((), (), s32[]{:S(2)}) async-start(), calls=%async_computation.1 | async-start | bytes 8912896 | tf_op jit(solution)/shard_map/reduce_scatter | solution.py:167
  93.7 7.8 %slice-start = ((s8[8650752]{0:T(1024)(128)(4,1)}), s8[262144]{0:T(1024)(128)(4,1)S(1)}, s32[]{:S(2)}) async-start(s8[8650752]{0:T(1024)(128)(4,1)} %bitcast.95), calls=%async_computation.3 | async-start | bytes 524288
  96.5 5.0 %slice-start.1 = ((s8[8650752]{0:T(1024)(128)(4,1)}), s8[4194304]{0:T(1024)(128)(4,1)S(1)}, s32[]{:S(2)}) async-start(s8[8650752]{0:T(1024)(128)(4,1)} %bitcast.95), calls=%async_computation.4 | async-start | bytes 8388608
  96.5 5.9 %slice-start.2 = ((s8[8650752]{0:T(1024)(128)(4,1)}), s8[4194304]{0:T(1024)(128)(4,1)S(1)}, s32[]{:S(2)}) async-start(s8[8650752]{0:T(1024)(128)(4,1)} %bitcast.95), calls=%async_computation.5 | async-start | bytes 8388608
  101.3 10.8 %copy-start.1 = (f32[4,128,4096]{2,1,0:T(8,128)}, f32[4,128,4096]{2,1,0:T(8,128)S(1)}, u32[]{:S(2)}) copy-start(f32[4,128,4096]{2,1,0:T(8,128)S(1)} %fusion.2) | copy-start | bytes 25165828
  102.4 4.1 %copy-start.7 = (bf16[1,2048,768]{2,1,0:T(8,128)(2,1)S(1)}, bf16[1,2048,768]{2,1,0:T(8,128)(2,1)}, u32[]{:S(2)}) copy-start(bf16[1,2048,768]{2,1,0:T(8,128)(2,1)} %param.11) | copy-start | bytes 9437188
  104.8 95.9 %collective-permute-start = (bf16[8,64,4224]{2,1,0:T(8,128)(2,1)}, bf16[8,64,4224]{2,1,0:T(8,128)(2,1)}, u32[]{:S(2)}, u32[]{:S(2)}) collective-permute-start(bf16[8,64,4224]{2,1,0:T(8,128)(2,1)} %dynamic-slice_bitcast_fusion), channel_id=1, source_target_pairs={{0,1},{1,0},{2,3},{3,2},{4,5},{5,4},{6,7},{7,6},{8,9},{9,8},{10,11... | collective-permute-start | bytes 12976136 | tf_op jit(solution)/shard_map/ppermute | solution.py:124
  108.3 1.9 copy-start.5
  110.2 1.8 copy-start.2
  114.4 1.8 copy-start.13
  114.4 5.1 %copy-start.11 = (bf16[512,768]{1,0:T(8,128)(2,1)}, bf16[512,768]{1,0:T(8,128)(2,1)S(1)}, u32[]{:S(2)}) copy-start(bf16[512,768]{1,0:T(8,128)(2,1)S(1)} %get-tuple-element.20) | copy-start | bytes 2359300
  114.4 6.9 %copy-start.9 = (bf16[512,768]{1,0:T(8,128)(2,1)}, bf16[512,768]{1,0:T(8,128)(2,1)S(1)}, u32[]{:S(2)}) copy-start(bf16[512,768]{1,0:T(8,128)(2,1)S(1)} %get-tuple-element.19) | copy-start | bytes 2359300
  200.7 7.7 %collective-permute-start.1 = (bf16[8,64,4224]{2,1,0:T(8,128)(2,1)}, bf16[8,64,4224]{2,1,0:T(8,128)(2,1)}, u32[]{:S(2)}, u32[]{:S(2)}) collective-permute-start(bf16[8,64,4224]{2,1,0:T(8,128)(2,1)} %collective-permute-done), channel_id=1, source_target_pairs={{0,2},{2,0},{4,6},{6,4},{8,10},{10,8},{12,14},{14,12},{16,18},{18,... | collective-permute-start | bytes 12976136 | tf_op jit(solution)/shard_map/ppermute | solution.py:125
  235.8 1.9 copy-start.6
  237.7 1.9 copy-start.8
  241.4 2.3 copy-start.3
  241.4 2.3 copy-start.14
  243.7 3.0 %copy-start.4 = (bf16[512,2048]{1,0:T(8,128)(2,1)S(1)}, bf16[512,2048]{1,0:T(8,128)(2,1)}, u32[]{:S(2)}) copy-start(bf16[512,2048]{1,0:T(8,128)(2,1)} %slice.73) | copy-start | bytes 6291460
  243.8 3.0 %copy-start.10 = (bf16[512,768]{1,0:T(8,128)(2,1)S(1)}, bf16[512,768]{1,0:T(8,128)(2,1)}, u32[]{:S(2)}) copy-start(bf16[512,768]{1,0:T(8,128)(2,1)} %copy-done.9) | copy-start | bytes 2359300
  246.8 3.0 %copy-start.12 = (bf16[512,768]{1,0:T(8,128)(2,1)S(1)}, bf16[512,768]{1,0:T(8,128)(2,1)}, u32[]{:S(2)}) copy-start(bf16[512,768]{1,0:T(8,128)(2,1)} %copy-done.11) | copy-start | bytes 2359300
Sparse Core Ops, SparseCore 0:
  10.9 79.2 all-gather.2
  134.7 102.8 reduce-scatter.1

commit v2 on v1

--- a/solution.py
+++ b/solution.py
@@ -1,10 +1,15 @@
+import math
+
 import jax
 import jax.numpy as jnp
 from jax import lax
+from jax.experimental import pallas as pl
+from jax.experimental.pallas import tpu as pltpu
 from jax.sharding import PartitionSpec as P
 
 BF = jnp.bfloat16
 F32 = jnp.float32
+VMEM = 40 * 1024 * 1024
 
 
 def slots(routes, experts, capacity):
@@ -92,97 +97,393 @@
         down_sum[None],
     )
 
-
-def split3(value):
-    high = value.astype(BF)
-    rest = value - high.astype(F32)
-    mid = rest.astype(BF)
-    low = (rest - mid.astype(F32)).astype(BF)
-    return high, mid, low
+def dot(left, right):
+    return jnp.dot(left, right, preferred_element_type=F32)
+
+
+def dot_t(left, right):
+    return lax.dot_general(left, right, CONTRACT, preferred_element_type=F32)
+
+
+def whole(array):
+    return pl.BlockSpec(array.shape, lambda *_: (0,) * array.ndim)
+
+
+def cost(flops, *arrays):
+    moved = sum(math.prod(a.shape) * a.dtype.itemsize for a in arrays)
+    return pl.CostEstimate(flops=flops, bytes_accessed=moved, transcendentals=0)
+
+
+def params(steps=0):
+    order = ("arbitrary",) * steps if steps else None
+    return pltpu.CompilerParams(dimension_semantics=order, vmem_limit_bytes=VMEM)
+
+
+def pack(pick, chunks):
+    room, features = pick.shape[0] // 2, chunks[0].shape[1]
+
+    def body(pick_ref, *refs):
+        mine_ref, theirs_ref = refs[-2:]
+        for at in range(0, features, 512):
+            cols = pl.ds(at, min(512, features - at))
+            rows = jnp.concatenate([ref[:, cols] for ref in refs[:-2]], axis=0)
+            packed = dot(pick_ref[...], rows).astype(BF)
+            mine_ref[:, cols] = packed[:room]
+            theirs_ref[:, cols] = packed[room:]
+
+    out = jax.ShapeDtypeStruct((room, features), BF)
+    return pl.pallas_call(
+        body,
+        out_shape=(out, out),
+        compiler_params=params(),
+        cost_estimate=cost(2 * math.prod(pick.shape) * features, *chunks, out, out),
+        name="pack",
+    )(pick, *chunks)
+
+
+def spread(pick, mine, theirs, parts):
+    room, features = mine.shape
+    length = pick.shape[1] // parts
+
+    def body(pick_ref, mine_ref, theirs_ref, *outs):
+        for at in range(0, features, 512):
+            cols = pl.ds(at, min(512, features - at))
+            rows = jnp.concatenate([mine_ref[:, cols], theirs_ref[:, cols]], axis=0)
+            dense = lax.dot_general(
+                pick_ref[...], rows, (((0,), (0,)), ((), ())), preferred_element_type=F32
+            ).astype(BF)
+            for i, out in enumerate(outs):
+                out[:, cols] = dense[i * length : (i + 1) * length]
+
+    out = jax.ShapeDtypeStruct((length, features), BF)
+    return pl.pallas_call(
+        body,
+        out_shape=(out,) * parts,
+        compiler_params=params(),
+        cost_estimate=cost(2 * math.prod(pick.shape) * features, mine, theirs, *(out,) * parts),
+        name="spread",
+    )(pick, mine, theirs)
+
+
+def forward(mine, theirs, weight, w_gate, w_up, w_down, with_result):
+    room, features = mine.shape
+    rows, hidden = 2 * room, w_gate.shape[2]
+    block = 256 if hidden % 256 == 0 else hidden
+    steps = hidden // block
+
+    def body(mine_ref, theirs_ref, weight_ref, gate_ref, up_ref, down_ref, *refs):
+        act_ref, to_gate_ref, to_up_ref = refs[:3]
+        x = jnp.concatenate([mine_ref[...], theirs_ref[...]], axis=0)
+        pre_gate = dot(x, gate_ref[0])
+        pre_up = dot(x, up_ref[0])
+        s = jax.nn.sigmoid(pre_gate)
+        silu = pre_gate * s
+        act = (silu * pre_up).astype(BF)
+        act_ref[...] = act
+        to_gate_ref[...] = pre_up * s * (1.0 + pre_gate * (1.0 - s))
+        to_up_ref[...] = silu
+        if with_result:
+            mine_out, theirs_out, total = refs[3:]
+            step = pl.program_id(0)
+            part = dot(act, down_ref[0])
+
+            @pl.when(step == 0)
+            def _():
+                total[...] = part
+
+            @pl.when(step > 0)
+            def _():
+                total[...] += part
+
+            @pl.when(step == steps - 1)
+            def _():
+                out = (total[...] * weight_ref[...]).astype(BF)
+                mine_out[...] = out[:room]
+                theirs_out[...] = out[room:]
+
+    row_out = jax.ShapeDtypeStruct((room, features), BF)
+    outs = [jax.ShapeDtypeStruct((rows, hidden), t) for t in (BF, F32, F32)]
+    out_specs = [pl.BlockSpec((rows, block), lambda i: (0, i))] * 3
+    scratch = []
+    if with_result:
+        outs += [row_out, row_out]
+        out_specs += [whole(row_out)] * 2
+        scratch = [pltpu.VMEM((rows, features), F32)]
+    columns = pl.BlockSpec((1, features, block), lambda i: (0, 0, i))
+    return pl.pallas_call(
+        body,
+        grid=(steps,),
+        in_specs=[
+            whole(mine),
+            whole(theirs),
+            whole(weight),
+            columns,
+            columns,
+            pl.BlockSpec((1, block, features), lambda i: (0, i if with_result else 0, 0)),
+        ],
+        out_specs=out_specs,
+        out_shape=outs,
+        scratch_shapes=scratch,
+        compiler_params=params(1),
+        cost_estimate=cost(
+            2 * rows * features * hidden * (3 if with_result else 2),
+            mine, theirs, w_gate, w_up, *outs,
+        ),
+        name="forward",
+    )(mine, theirs, weight, w_gate, w_up, w_down)
+
+
+def backward(mine, theirs, weight, to_gate, to_up, w_gate, w_up, w_down, with_result):
+    room, features = mine.shape
+    rows, hidden = to_gate.shape
+    block = 256 if hidden % 256 == 0 else hidden
+    steps = hidden // block
+
+    def body(
+        mine_ref, theirs_ref, weight_ref, to_gate_ref, to_up_ref, gate_ref, up_ref, down_ref, *refs
+    ):
+        scaled_ref, d_gate_ref, d_up_ref = refs[:3]
+        step = pl.program_id(0)
+
+        @pl.when(step == 0)
+        def _():
+            cot = jnp.concatenate([mine_ref[...], theirs_ref[...]], axis=0)
+            scaled_ref[...] = (cot.astype(F32) * weight_ref[...]).astype(BF)
+
+        d_hidden = dot_t(scaled_ref[...], down_ref[0])
+        d_gate = (d_hidden * to_gate_ref[...]).astype(BF)
+        d_up = (d_hidden * to_up_ref[...]).astype(BF)
+        d_gate_ref[...] = d_gate
+        d_up_ref[...] = d_up
+        if with_result:
+            mine_out, theirs_out, total = refs[3:]
+            part = dot_t(d_gate, gate_ref[0]) + dot_t(d_up, up_ref[0])
+
+            @pl.when(step == 0)
+            def _():
+                total[...] = part
+
+            @pl.when(step > 0)
+            def _():
+                total[...] += part
+
+            @pl.when(step == steps - 1)
+            def _():
+                out = total[...].astype(BF)
+                mine_out[...] = out[:room]
+                theirs_out[...] = out[room:]
+
+    row_out = jax.ShapeDtypeStruct((room, features), BF)
+    scaled = jax.ShapeDtypeStruct((rows, features), BF)
+    part_out = jax.ShapeDtypeStruct((rows, hidden), BF)
+    outs = [scaled, part_out, part_out]
+    part_spec = pl.BlockSpec((rows, block), lambda i: (0, i))
+    out_specs = [whole(scaled), part_spec, part_spec]
+    scratch = []
+    if with_result:
+        outs += [row_out, row_out]
+        out_specs += [whole(row_out)] * 2
+        scratch = [pltpu.VMEM((rows, features), F32)]
+    columns = pl.BlockSpec((1, features, block), lambda i: (0, 0, i if with_result else 0))
+    return pl.pallas_call(
+        body,
+        grid=(steps,),
+        in_specs=[
+            whole(mine),
+            whole(theirs),
+            whole(weight),
+            part_spec,
+            part_spec,
+            columns,
+            columns,
+            pl.BlockSpec((1, block, features), lambda i: (0, i, 0)),
+        ],
+        out_specs=out_specs,
+        out_shape=outs,
+        scratch_shapes=scratch,
+        compiler_params=params(1),
+        cost_estimate=cost(
+            2 * rows * features * hidden * (3 if with_result else 1), mine, theirs, w_down, *outs
+        ),
+        name="backward",
+    )(mine, theirs, weight, to_gate, to_up, w_gate, w_up, w_down)
+
+
+def rows_grad(left, right):
+    return lax.dot_general(left, right, (((0,), (0,)), ((), ())), preferred_element_type=F32)
+
+
+def gate_up_grad(replica, xs, d_gates, d_ups):
+    features, hidden = xs[0].shape[1], d_gates[0].shape[1]
+    half = features // 2
+    block = 256 if half % 256 == 0 else half
+    steps = half // block
+
+    def body(_, *refs):
+        n = len(xs)
+        m = len(d_gates)
+        x = jnp.concatenate([ref[...] for ref in refs[:n]], axis=0)
+        for at, out in ((n, refs[-2]), (n + m, refs[-1])):
+            d = jnp.concatenate([ref[...] for ref in refs[at : at + m]], axis=0)
+            out[0] = rows_grad(x, d).astype(BF)
+
+    out = jax.ShapeDtypeStruct((1, half, hidden), BF)
+    rows = sum(x.shape[0] for x in xs)
+    return pl.pallas_call(
+        body,
+        grid_spec=pltpu.PrefetchScalarGridSpec(
+            num_scalar_prefetch=1,
+            grid=(steps,),
+            in_specs=[
+                pl.BlockSpec((x.shape[0], block), lambda i, r: (0, r[0] * steps + i)) for x in xs
+            ]
+            + [whole(d) for d in (*d_gates, *d_ups)],
+            out_specs=[pl.BlockSpec((1, block, hidden), lambda i, r: (0, i, 0))] * 2,
+        ),
+        out_shape=(out, out),
+        compiler_params=params(1),
+        cost_estimate=cost(4 * rows * half * hidden, *xs, *d_gates, *d_ups, out, out),
+        name="gate_up_grad",
+    )(replica, *xs, *d_gates, *d_ups)
+
+
+def down_grad(replica, acts, scaleds):
+    features, hidden = scaleds[0].shape[1], acts[0].shape[1]
+    half = hidden // 2
+    block = 512 if features % 512 == 0 else features
+
+    def body(_, *refs):
+        n = len(acts)
+        act = jnp.concatenate([ref[...] for ref in refs[:n]], axis=0)
+        cot = jnp.concatenate([ref[...] for ref in refs[n : 2 * n]], axis=0)
+        refs[-1][0] = rows_grad(act, cot).astype(BF)
+
+    out = jax.ShapeDtypeStruct((1, half, features), BF)
+    rows = sum(a.shape[0] for a in acts)
+    return pl.pallas_call(
+        body,
+        grid_spec=pltpu.PrefetchScalarGridSpec(
+            num_scalar_prefetch=1,
+            grid=(features // block,),
+            in_specs=[pl.BlockSpec((a.shape[0], half), lambda i, r: (0, r[0])) for a in acts]
+            + [pl.BlockSpec((c.shape[0], block), lambda i, r: (0, i)) for c in scaleds],
+            out_specs=pl.BlockSpec((1, half, block), lambda i, r: (0, 0, i)),
+        ),
+        out_shape=out,
+        compiler_params=params(1),
+        cost_estimate=cost(2 * rows * half * features, *acts, *scaleds, out),
+        name="down_grad",
+    )(replica, *acts, *scaleds)
+
+
+def route_plan(share, capacity, expert, replica, lines):
+    tok_rows, experts = share.shape
+    z, x, core = expert // 4, (expert // 2) % 2, expert % 2
+    table = lax.all_gather(share.T, ("expert", "replica"), axis=0, tiled=False)
+    table = table.reshape(lines, 2, 2, 2, experts, tok_rows)
+    table = lax.dynamic_slice_in_dim(table, expert - core, 2, axis=4)
+    for axis, index in ((1, x), (2, core), (3, replica), (4, core)):
+        table = jnp.where(index == 0, table, jnp.flip(table, axis))
+    table = jnp.flip(table, 0)
+    table = jnp.concatenate([table, table], axis=0)
+    table = lax.dynamic_slice_in_dim(table, lines - 1 - z, lines, axis=0)
+    table = jnp.transpose(table, (3, 1, 2, 4, 0, 5)).reshape(2, 2, 2, 2, lines * tok_rows)
+    routed = table > 0
+    before = jnp.triu(jnp.ones((lines * tok_rows,) * 2, BF))
+    rank = jnp.einsum("abcdt,tu->abcdu", routed.astype(BF), before, preferred_element_type=F32)
+    slot = jnp.where(routed, rank - 1.0, -1.0)
+    room = lines * capacity
+    places = jnp.arange(room, dtype=F32)[:, None]
+    pick = (slot[:, :, 0, :, None, :] == places).astype(BF)
+    weight = jnp.sum(
+        jnp.where(slot[:, :, :, 0, None, :] == places, table[:, :, :, 0, None, :], 0.0), axis=-1
+    )
+    length = lines * tok_rows
+    return pick.reshape(2, 2, 2 * room, length), weight.reshape(2, 2, 2 * room, 1)
 
 
 def dense_plan(tokens, route_ids, gate_probs, out_cot, w_gate, w_up, w_down):
     experts = lax.axis_size("expert")
     tok_rows, features = tokens.shape
     top_count = route_ids.shape[1]
-    hidden = w_gate.shape[2]
     capacity = max(2, tok_rows * top_count * 4 // (3 * experts))
+    lines = experts // 4
     expert = lax.axis_index("expert")
     replica = lax.axis_index("replica")
-    core = expert % 2
-    gate_weight, up_weight, down_weight = w_gate[0], w_up[0], w_down[0]
+
+    def to_core(rows):
+        return lax.ppermute(rows, "expert", [(i, i ^ 1) for i in range(experts)])
+
+    def to_x(rows):
+        return lax.ppermute(rows, "expert", [(i, i ^ 2) for i in range(experts)])
+
+    def to_z(rows):
+        return lax.ppermute(rows, "expert", [(i, (i + 4) % experts) for i in range(experts)])
+
+    def to_y(rows):
+        return lax.ppermute(rows, "replica", [(0, 1), (1, 0)])
+
+    def gather(rows):
+        near = [rows]
+        for _ in range(lines - 1):
+            near.append(to_z(near[-1]))
+        far = [to_x(a) for a in near]
+        return near, far
 
     chosen = route_ids[:, :, None] == jnp.arange(experts, dtype=jnp.int32)
     share = jnp.sum(jnp.where(chosen, gate_probs[:, :, None], 0.0), axis=1)
-    pad = -(3 * experts) % 128
-    payload = jnp.concatenate(
-        [tokens, out_cot, *split3(share), jnp.zeros((tok_rows, pad), BF)], axis=1
-    )
-    width = payload.shape[1]
-    own = lax.all_gather(payload, "expert", axis=0, tiled=False)
-    mine = lax.dynamic_index_in_dim(own.reshape(experts // 2, 2, tok_rows, width), core, 1, False)
-    relay = lax.ppermute(mine, "replica", [(0, 1), (1, 0)])
-    sibling = lax.ppermute(relay, "expert", [(i, i ^ 1) for i in range(experts)])
-    other = jnp.stack([relay, sibling], axis=1).reshape(experts, tok_rows, width)
-
-    together = 4
-    groups = experts // together
-    length = together * tok_rows
-    room = together * capacity
-
-    def pack(rows):
-        rows = rows.reshape(groups, length, width)
-        at = 2 * features + expert
-        weight = sum(
-            lax.dynamic_slice_in_dim(rows, at + i * experts, 1, 2)[:, :, 0].astype(F32)
-            for i in range(3)
-        )
-        routed = weight > 0
-        rank = jnp.cumsum(routed.astype(jnp.int32), axis=1) - 1
-        pick = (rank[:, None, :] == jnp.arange(room)[None, :, None]) & routed[:, None, :]
-        row_weight = jnp.sum(jnp.where(pick, weight[:, None, :], 0.0), axis=2).reshape(-1, 1)
-        pick = pick.astype(BF)
-        packed = jnp.einsum(
-            "gst,gtd->gsd", pick, rows[:, :, : 2 * features], preferred_element_type=F32
-        ).reshape(groups * room, 2 * features)
-        x = packed[:, :features].astype(BF)
-        cot = (row_weight * packed[:, features:]).astype(BF)
-        return pick, row_weight, x, cot
-
-    def spread(pick, rows):
-        rows = rows.reshape(groups, room, features)
-        return jnp.einsum("gst,gsd->gtd", pick, rows, preferred_element_type=F32).astype(BF)
-
-    def middle(x, cot):
-        pre_gate, pre_up, activation = hidden_rows(x, gate_weight, up_weight)
-        d_gate, d_up = hidden_grads(cot, pre_gate, pre_up, down_weight)
-        return activation, d_gate, d_up
-
-    pick, row_weight, x, cot = pack(own)
-    activation, d_gate, d_up = middle(x, cot)
-    result = jnp.dot(activation, down_weight, preferred_element_type=F32).astype(BF)
-    result = (row_weight * result.astype(F32)).astype(BF)
-    back = input_rows(d_gate, d_up, gate_weight, up_weight)
-    dense = jnp.concatenate([spread(pick, result), spread(pick, back)], axis=2)
-    summed = lax.psum_scatter(
-        dense.reshape(experts * tok_rows, 2 * features),
-        "expert",
-        scatter_dimension=0,
-        tiled=True,
-    )
-    combined, grad_tokens = summed[:, :features], summed[:, features:]
-
-    _, _, x2, cot2 = pack(other)
-    activation2, d_gate2, d_up2 = middle(x2, cot2)
-    both = lambda a, b: jnp.concatenate([a, b], axis=0)
-    half = features // 2
-    xs = lax.dynamic_slice_in_dim(both(x, x2), replica * half, half, 1)
-    acts = lax.dynamic_slice_in_dim(
-        both(activation, activation2), replica * (hidden // 2), hidden // 2, 1
-    )
-    grad_gate = outer_sum(xs, both(d_gate, d_gate2)).astype(BF)[None]
-    grad_up = outer_sum(xs, both(d_up, d_up2)).astype(BF)[None]
-    grad_down = outer_sum(acts, both(cot, cot2)).astype(BF)[None]
+    pick, weight = route_plan(share, capacity, expert, replica, lines)
+
+    token_sets = gather(tokens)
+    cot_sets = gather(out_cot)
+    other_tokens = [[to_y(a) for a in group] for group in token_sets]
+    other_cots = [[to_y(a) for a in group] for group in cot_sets]
+
+    def packed(plane, group, chunks):
+        mine, theirs = pack(pick[plane, group], chunks)
+        return mine, to_core(theirs)
+
+    def home(results):
+        near = spread(pick[0, 0], results[0][0], to_core(results[0][1]), lines)
+        far = spread(pick[0, 1], results[1][0], to_core(results[1][1]), lines)
+        total = None
+        for s in (*range(1, lines), 0):
+            part = near[s].astype(F32) + to_x(far[s]).astype(F32)
+            if total is not None:
+                part = part + to_z(total).astype(F32)
+            total = part.astype(BF)
+        return total
+
+    xs, acts, firsts, results = [], [], [], []
+    for plane, sets in enumerate((token_sets, other_tokens)):
+        for group in range(2):
+            x = packed(plane, group, sets[group])
+            act, to_gate, to_up, *result = forward(
+                *x, weight[plane, group], w_gate, w_up, w_down, plane == 0
+            )
+            xs += x
+            acts.append(act)
+            firsts.append((to_gate, to_up))
+            results.append(result)
+    combined = home(results[:2])
+
+    scaleds, d_gates, d_ups, results = [], [], [], []
+    for plane, sets in enumerate((cot_sets, other_cots)):
+        for group in range(2):
+            cot = packed(plane, group, sets[group])
+            scaled, d_gate, d_up, *result = backward(
+                *cot, weight[plane, group], *firsts[2 * plane + group],
+                w_gate, w_up, w_down, plane == 0,
+            )
+            scaleds.append(scaled)
+            d_gates.append(d_gate)
+            d_ups.append(d_up)
+            results.append(result)
+    grad_tokens = home(results[:2])
+
+    half = replica.astype(jnp.int32).reshape(1)
+    grad_gate, grad_up = gate_up_grad(half, xs, d_gates, d_ups)
+    grad_down = down_grad(half, acts, scaleds)
     return (combined, grad_tokens, grad_gate, grad_up, grad_down)
 
 

time: 262 us -> 308 us (1.18)
  Pallas kernels: 0 us -> 73.6 us
  blocking collectives: 0 us -> 69.9 us
  waiting for transfers between devices: 150 us -> 88.9 us
  matrix products: 42.6 us -> 0.22 us
  starting transfers between devices: 1.58 us -> 38.4 us
  other arithmetic: 20.3 us -> 3.35 us
  between operations: 14.4 us -> 1.67 us
    all_gather x1 -> x0, waiting for transfers between devices: 79.7 us -> none  [dense_plan(): own = lax.all_gather(payload, 'expert', axis=0, tiled=False)]
    pallas_call x0 -> x22, Pallas kernels: none -> 73.6 us  [the longest x4 22.2 us: backward(): pl.pallas_call(body, grid=(steps,), in_specs=[whole(mine), whole(theirs),...]
    all_gather x0 -> x1, blocking collectives: none -> 69.9 us  [route_plan(): table = lax.all_gather(share.T, ('expert', 'replica'), axis=0, tiled=False)]
    dot_general x16 -> x1, matrix products: 42.6 us -> 0.22 us  [route_plan(): jnp.einsum('abcdt,tu->abcdu', routed.astype(BF), before, preferred_elemen...]
    ppermute x2 -> x56, starting transfers between devices: 1.5 us -> 38.4 us  [the longest x16 17.2 us: to_x(): return lax.ppermute(rows, 'expert', [(i, i ^ 2) for i in range(experts)])]
    ppermute x2 -> x56, waiting for transfers between devices: 69.9 us -> 88.9 us  [the longest x12 35.6 us: to_z(): lax.ppermute(rows, 'expert', [(i, (i + 4) % experts) for i in range(exper...]
    unnamed x44 -> x171, local copies, waits for them, and re-layouts: 9.06 us -> 27.1 us
    another operation x5 -> x0, other arithmetic: 10.4 us -> none  [the longest x1 7.91 us: dense_plan(): jnp.stack([relay, sibling], axis=1).reshape(experts, tok_rows, width)]
  transfers between devices with their start and end apart: 4 -> 56, of which waited for: 3 -> 19; matrix products, arithmetic and copies ran while one was open for 28% -> 2% of each run, Pallas kernels for 0% -> 24%
where the time goes in v2:
time: 308 us; the launch traced here: 307 us
  waiting for transfers between devices  88.9 us (29%)
  Pallas kernels  73.6 us (24%)
  blocking collectives  69.9 us (23%)
  starting transfers between devices  38.4 us (12%)
  local copies, waits for them, and re-layouts  30.6 us (10%)
  other arithmetic  3.35 us (1%)
    all_gather x1, blocking collectives, route_plan(): table = lax.all_gather(share.T, ('expert', 'replica'), axis=0, tiled=False)  69.9 us
    ppermute x12, waiting for transfers between devices, to_z(): lax.ppermute(rows, 'expert', [(i, (i + 4) % experts) for i in range(exper...  35.6 us
    ppermute x16, waiting for transfers between devices, to_y(): return lax.ppermute(rows, 'replica', [(0, 1), (1, 0)])  28.2 us
    unnamed x171, local copies, waits for them, and re-layouts  27.1 us
    ppermute x16, waiting for transfers between devices, to_x(): return lax.ppermute(rows, 'expert', [(i, i ^ 2) for i in range(experts)])  25.1 us
    pallas_call x4, Pallas kernels, backward(): pl.pallas_call(body, grid=(steps,), in_specs=[whole(mine), whole(theirs),...  22.2 us
    pallas_call x4, Pallas kernels, forward(): pl.pallas_call(body, grid=(steps,), in_specs=[whole(mine), whole(theirs),...  20.1 us
    pallas_call x8, Pallas kernels, pack(): pl.pallas_call(body, out_shape=(out, out), compiler_params=params(), cost...  17.5 us
  transfers between devices with their start and end apart: 56, of which 19 were waited for; matrix products, arithmetic and copies ran while one was open for 2% of the time, Pallas kernels for 24%

profile of v2, /device:TPU:0, one launch (start us, length us, event | category | flops | bytes accessed | tf_op | source)
XLA Modules:
  0.0 306.7 jit_solution(17509755083024474968)
XLA Ops:
  0.6 3.0 collective-permute-start.5
  9.6 69.9 %all-gather = f32[512,64]{1,0:T(8,128)S(1)} all-gather(f32[16,64]{1,0:T(8,128)S(1)} %bitcast.43), channel_id=2, replica_groups=mesh['expert'=16,'replica'=2] {'expert','replica'}, dimensions={0}, use_global_device_ids=true | all-gather | bytes 135168 | tf_op jit(solution)/shard_map/all_gather | solution.py:382
  82.2 5.0 %collective-permute-done.46.refs_0_ = bf16[64,2048]{1,0:T(8,128)(2,1)S(1)} collective-permute-done((bf16[64,2048]{1,0:T(8,128)(2,1)}, bf16[64,2048]{1,0:T(8,128)(2,1)S(1)}, u32[]{:S(2)}, u32[]{:S(2)}) %collective-permute-start.46) | collective-permute-done | bytes 262176 | tf_op jit(solution)/shard_map/ppermute | solution.py:424
  97.1 5.6 %collective-permute-done.41.refs_0_ = bf16[64,2048]{1,0:T(8,128)(2,1)S(1)} collective-permute-done((bf16[64,2048]{1,0:T(8,128)(2,1)S(1)}, bf16[64,2048]{1,0:T(8,128)(2,1)S(1)}, u32[]{:S(2)}, u32[]{:S(2)}) %collective-permute-start.41) | collective-permute-done | bytes 262176 | tf_op jit(solution)/shard_map/ppermute | solution.py:424
  102.9 3.1 %collective-permute-done.47.refs_1_ = bf16[64,2048]{1,0:T(8,128)(2,1)S(1)} collective-permute-done((bf16[64,2048]{1,0:T(8,128)(2,1)S(1)}, bf16[64,2048]{1,0:T(8,128)(2,1)S(1)}, u32[]{:S(2)}, u32[]{:S(2)}) %collective-permute-start.47) | collective-permute-done | bytes 262176 | tf_op jit(solution)/shard_map/ppermute | solution.py:424
  106.0 4.9 %collective-permute-done.51.refs_0_ = bf16[64,2048]{1,0:T(8,128)(2,1)S(1)} collective-permute-done((bf16[64,2048]{1,0:T(8,128)(2,1)S(1)}, bf16[64,2048]{1,0:T(8,128)(2,1)S(1)}, u32[]{:S(2)}, u32[]{:S(2)}) %collective-permute-start.51) | collective-permute-done | bytes 262176 | tf_op jit(solution)/shard_map/ppermute | solution.py:424
  124.2 4.3 %collective-permute-done.42.refs_1_ = bf16[64,2048]{1,0:T(8,128)(2,1)S(1)} collective-permute-done((bf16[64,2048]{1,0:T(8,128)(2,1)}, bf16[64,2048]{1,0:T(8,128)(2,1)S(1)}, u32[]{:S(2)}, u32[]{:S(2)}) %collective-permute-start.42) | collective-permute-done | bytes 262176 | tf_op jit(solution)/shard_map/ppermute | solution.py:424
  133.1 2.9 collective-permute-done.8.refs_3_
  170.8 6.3 %forward.4 = (bf16[256,768]{1,0:T(8,128)(2,1)S(1)}, f32[256,768]{1,0:T(8,128)S(1)}, f32[256,768]{1,0:T(8,128)S(1)}, bf16[128,2048]{1,0:T(8,128)(2,1)S(1)}, bf16[128,2048]{1,0:T(8,128)(2,1)}) custom-call(bf16[128,2048]{1,0:T(8,128)(2,1)S(1)} %copy-done.23, bf16[128,2048]{1,0:T(8,128)(2,1)} %collective-permute-done.3.theirs_ref.refs_1_, ...), custom_call_target="tpu_custom_call" | custom-call | flops 2415919104 | bytes 10354688 | tf_op jit(solution)/shard_map/forward/pallas_call | solution.py:213
  178.2 8.6 %backward.4 = (bf16[256,2048]{1,0:T(8,128)(2,1)S(1)}, bf16[256,768]{1,0:T(8,128)(2,1)S(1)}, bf16[256,768]{1,0:T(8,128)(2,1)S(1)}, bf16[128,2048]{1,0:T(8,128)(2,1)S(1)}, bf16[128,2048]{1,0:T(8,128)(2,1)}) custom-call(bf16[128,2048]{1,0:T(8,128)(2,1)S(1)} %copy-done.13, bf16[128,2048]{1,0:T(8,128)(2,1)} %collective-permute-done.21.theirs_ref, ...), custom_call_target="tpu_custom_call" | custom-call | flops 2415919104 | bytes 7077888 | tf_op jit(solution)/shard_map/backward/pallas_call | solution.py:288
  192.9 6.3 %forward.5 = (bf16[256,768]{1,0:T(8,128)(2,1)S(1)}, f32[256,768]{1,0:T(8,128)S(1)}, f32[256,768]{1,0:T(8,128)S(1)}, bf16[128,2048]{1,0:T(8,128)(2,1)S(1)}, bf16[128,2048]{1,0:T(8,128)(2,1)}) custom-call(bf16[128,2048]{1,0:T(8,128)(2,1)S(1)} %get-tuple-element.76.mine_ref.refs_2_, bf16[128,2048]{1,0:T(8,128)(2,1)} %collective-permute-done.9.theirs_ref.refs_3_, ...), custom_call_target="tpu_custom_call" | custom-call | flops 2415919104 | bytes 10354688 | tf_op jit(solution)/shard_map/forward/pallas_call | solution.py:213
  200.5 8.4 %backward.5 = (bf16[256,2048]{1,0:T(8,128)(2,1)S(1)}, bf16[256,768]{1,0:T(8,128)(2,1)S(1)}, bf16[256,768]{1,0:T(8,128)(2,1)S(1)}, bf16[128,2048]{1,0:T(8,128)(2,1)S(1)}, bf16[128,2048]{1,0:T(8,128)(2,1)}) custom-call(bf16[128,2048]{1,0:T(8,128)(2,1)S(1)} %get-tuple-element.94.mine_ref, bf16[128,2048]{1,0:T(8,128)(2,1)S(1)} %collective-permute-done.27.theirs_ref, ...), custom_call_target="tpu_custom_call" | custom-call | flops 2415919104 | bytes 7077888 | tf_op jit(solution)/shard_map/backward/pallas_call | solution.py:288
  211.7 3.7 %forward.6 = (bf16[256,768]{1,0:T(8,128)(2,1)S(1)}, f32[256,768]{1,0:T(8,128)S(1)}, f32[256,768]{1,0:T(8,128)S(1)}) custom-call(bf16[128,2048]{1,0:T(8,128)(2,1)S(1)} %copy-done.28, bf16[128,2048]{1,0:T(8,128)(2,1)} %collective-permute-done.40.theirs_ref.refs_5_, f32[256,1]{1,0:T(8,128)S(1)} %copy-done.5, bf16[1,2048,768]{2,1,0:T(8,128)(2,1)S(1)} %copy-done, ...), custom_call_target="tpu_custom_call" | custom-call | flops 1610612736 | bytes 9306112 | tf_op jit(solution)/shard_map/forward/pallas_call | solution.py:213
  215.5 3.0 backward.6
  218.8 3.7 %forward.7 = (bf16[256,768]{1,0:T(8,128)(2,1)S(1)}, f32[256,768]{1,0:T(8,128)S(1)}, f32[256,768]{1,0:T(8,128)S(1)}) custom-call(bf16[128,2048]{1,0:T(8,128)(2,1)S(1)} %copy-done.31, bf16[128,2048]{1,0:T(8,128)(2,1)} %collective-permute-done.45.theirs_ref.refs_7_, f32[256,1]{1,0:T(8,128)S(1)} %copy.37.weight_ref, bf16[1,2048,768]{2,1,0:T(8,128)(2,1)S(1)} %copy-done, ...), custom_call_target="tpu_custom_call" | custom-call | flops 1610612736 | bytes 9306112 | tf_op jit(solution)/shard_map/forward/pallas_call | solution.py:213
  227.0 3.7 %down_grad.1 = bf16[1,384,2048]{2,1,0:T(8,128)(2,1)} custom-call(s32[1]{0:T(128)} %bitcast.14._, bf16[256,768]{1,0:T(8,128)(2,1)S(1)} %copy-done.34, bf16[256,768]{1,0:T(8,128)(2,1)S(1)} %copy-done.36, bf16[256,768]{1,0:T(8,128)(2,1)S(1)} %get-tuple-element.131.refs_2_, bf16[256,768]{1,0:T(8,128)(2,1)S(1)} %get-tuple-element.132.refs_3_, ...), custom_call_target="tpu_custom_call" | custom-call | flops 1610612736 | bytes 7340032 | tf_op jit(solution)/shard_map/down_grad/pallas_call | solution.py:363
  232.4 6.2 %gate_up_grad.1 = (bf16[1,1024,768]{2,1,0:T(8,128)(2,1)}, bf16[1,1024,768]{2,1,0:T(8,128)(2,1)}) custom-call(s32[1]{0:T(128)} %bitcast.14._, bf16[128,2048]{1,0:T(8,128)(2,1)S(1)} %copy-done.24, bf16[128,2048]{1,0:T(8,128)(2,1)} %collective-permute-done.3.theirs_ref.refs_1_, bf16[128,2048]{1,0:T(8,128)(2,1)S(1)} %copy-done.26, ...), custom_call_target="tpu_custom_call" | custom-call | flops 3221225472 | bytes 10485760 | tf_op jit(solution)/shard_map/gate_up_grad/pallas_call | solution.py:332
  245.3 19.3 %collective-permute-done.32 = bf16[64,2048]{1,0:T(8,128)(2,1)S(1)} collective-permute-done((bf16[64,2048]{1,0:T(8,128)(2,1)S(1)}, bf16[64,2048]{1,0:T(8,128)(2,1)S(1)}, u32[]{:S(2)}, u32[]{:S(2)}) %collective-permute-start.32) | collective-permute-done | bytes 262176 | tf_op jit(solution)/shard_map/ppermute | solution.py:418
  267.6 5.7 %collective-permute-done.15 = bf16[64,2048]{1,0:T(8,128)(2,1)S(1)} collective-permute-done((bf16[64,2048]{1,0:T(8,128)(2,1)S(1)}, bf16[64,2048]{1,0:T(8,128)(2,1)S(1)}, u32[]{:S(2)}, u32[]{:S(2)}) %collective-permute-start.15) | collective-permute-done | bytes 262176 | tf_op jit(solution)/shard_map/ppermute | solution.py:421
  275.0 6.4 %collective-permute-done.33 = bf16[64,2048]{1,0:T(8,128)(2,1)S(1)} collective-permute-done((bf16[64,2048]{1,0:T(8,128)(2,1)S(1)}, bf16[64,2048]{1,0:T(8,128)(2,1)S(1)}, u32[]{:S(2)}, u32[]{:S(2)}) %collective-permute-start.33) | collective-permute-done | bytes 262176 | tf_op jit(solution)/shard_map/ppermute | solution.py:421
  281.6 10.4 %collective-permute-done.16 = bf16[64,2048]{1,0:T(8,128)(2,1)S(1)} collective-permute-done((bf16[64,2048]{1,0:T(8,128)(2,1)S(1)}, bf16[64,2048]{1,0:T(8,128)(2,1)S(1)}, u32[]{:S(2)}, u32[]{:S(2)}) %collective-permute-start.16) | collective-permute-done | bytes 262176 | tf_op jit(solution)/shard_map/ppermute | solution.py:421
  292.1 5.4 %collective-permute-done.34 = bf16[64,2048]{1,0:T(8,128)(2,1)S(1)} collective-permute-done((bf16[64,2048]{1,0:T(8,128)(2,1)S(1)}, bf16[64,2048]{1,0:T(8,128)(2,1)S(1)}, u32[]{:S(2)}, u32[]{:S(2)}) %collective-permute-start.34) | collective-permute-done | bytes 262176 | tf_op jit(solution)/shard_map/ppermute | solution.py:421
  297.8 4.3 %collective-permute-done.17 = bf16[64,2048]{1,0:T(8,128)(2,1)S(1)} collective-permute-done((bf16[64,2048]{1,0:T(8,128)(2,1)S(1)}, bf16[64,2048]{1,0:T(8,128)(2,1)S(1)}, u32[]{:S(2)}, u32[]{:S(2)}) %collective-permute-start.17) | collective-permute-done | bytes 262176 | tf_op jit(solution)/shard_map/ppermute | solution.py:421
  302.8 3.1 %collective-permute-done.35 = bf16[64,2048]{1,0:T(8,128)(2,1)S(1)} collective-permute-done((bf16[64,2048]{1,0:T(8,128)(2,1)S(1)}, bf16[64,2048]{1,0:T(8,128)(2,1)S(1)}, u32[]{:S(2)}, u32[]{:S(2)}) %collective-permute-start.35) | collective-permute-done | bytes 262176 | tf_op jit(solution)/shard_map/ppermute | solution.py:421
  (315 shorter events, 101.7 us)
Async XLA Ops:
  0.6 79.1 %collective-permute-start.5 = (bf16[64,2048]{1,0:T(8,128)(2,1)}, bf16[64,2048]{1,0:T(8,128)(2,1)S(1)}, u32[]{:S(2)}, u32[]{:S(2)}) collective-permute-start(bf16[64,2048]{1,0:T(8,128)(2,1)} %refs_0_.2), channel_id=1, source_target_pairs={{0,4},{2,6},{4,0},{6,2},{8,12},{10,14},{12,8},{14,10},{16,20},{18,... | collective-permute-start | bytes 786440 | tf_op jit(solution)/shard_map/ppermute | solution.py:418
  3.6 76.2 %collective-permute-start = (bf16[64,2048]{1,0:T(8,128)(2,1)}, bf16[64,2048]{1,0:T(8,128)(2,1)S(1)}, u32[]{:S(2)}, u32[]{:S(2)}) collective-permute-start(bf16[64,2048]{1,0:T(8,128)(2,1)} %refs_0_.2), channel_id=1, source_target_pairs={{0,8},{2,10},{4,12},{6,14},{8,16},{10,18},{12,20},{14,22},{16,24},... | collective-permute-start | bytes 786440 | tf_op jit(solution)/shard_map/ppermute | solution.py:421
  5.2 74.8 %collective-permute-start.23 = (bf16[64,2048]{1,0:T(8,128)(2,1)}, bf16[64,2048]{1,0:T(8,128)(2,1)S(1)}, u32[]{:S(2)}, u32[]{:S(2)}) collective-permute-start(bf16[64,2048]{1,0:T(8,128)(2,1)} %refs_0_.3), channel_id=1, source_target_pairs={{0,4},{2,6},{4,0},{6,2},{8,12},{10,14},{12,8},{14,10},{16,20},{18,... | collective-permute-start | bytes 786440 | tf_op jit(solution)/shard_map/ppermute | solution.py:418
  5.8 74.3 %collective-permute-start.18 = (bf16[64,2048]{1,0:T(8,128)(2,1)}, bf16[64,2048]{1,0:T(8,128)(2,1)S(1)}, u32[]{:S(2)}, u32[]{:S(2)}) collective-permute-start(bf16[64,2048]{1,0:T(8,128)(2,1)} %refs_0_.3), channel_id=1, source_target_pairs={{0,8},{2,10},{4,12},{6,14},{8,16},{10,18},{12,20},{14,22},{16,24},... | collective-permute-start | bytes 786440 | tf_op jit(solution)/shard_map/ppermute | solution.py:421
  7.3 74.8 %collective-permute-start.36 = (bf16[64,2048]{1,0:T(8,128)(2,1)}, bf16[64,2048]{1,0:T(8,128)(2,1)S(1)}, u32[]{:S(2)}, u32[]{:S(2)}) collective-permute-start(bf16[64,2048]{1,0:T(8,128)(2,1)} %refs_0_.2), channel_id=1, source_target_pairs={{0,1},{1,0},{2,3},{3,2},{4,5},{5,4},{6,7},{7,6},{8,9},{9,8},{10,11... | collective-permute-start | bytes 786440 | tf_op jit(solution)/shard_map/ppermute | solution.py:424
  123.0 44.6 %collective-permute-start.3 = (bf16[128,2048]{1,0:T(8,128)(2,1)}, bf16[128,2048]{1,0:T(8,128)(2,1)}, u32[]{:S(2)}, u32[]{:S(2)}) collective-permute-start(bf16[128,2048]{1,0:T(8,128)(2,1)} %get-tuple-element.72), channel_id=1, source_target_pairs={{0,2},{2,0},{4,6},{6,4},{8,10},{10,8},{12,14},{14,12},{16,18},{18,... | collective-permute-start | bytes 1572872 | tf_op jit(solution)/shard_map/ppermute | solution.py:415
  123.7 44.1 %collective-permute-start.21 = (bf16[128,2048]{1,0:T(8,128)(2,1)}, bf16[128,2048]{1,0:T(8,128)(2,1)}, u32[]{:S(2)}, u32[]{:S(2)}) collective-permute-start(bf16[128,2048]{1,0:T(8,128)(2,1)} %get-tuple-element.88), channel_id=1, source_target_pairs={{0,2},{2,0},{4,6},{6,4},{8,10},{10,8},{12,14},{14,12},{16,18},{18,... | collective-permute-start | bytes 1572872 | tf_op jit(solution)/shard_map/ppermute | solution.py:415
  136.0 26.1 %collective-permute-start.49 = (bf16[64,2048]{1,0:T(8,128)(2,1)}, bf16[64,2048]{1,0:T(8,128)(2,1)}, u32[]{:S(2)}, u32[]{:S(2)}) collective-permute-start(bf16[64,2048]{1,0:T(8,128)(2,1)} %collective-permute-done.20.refs_3_), channel_id=1, source_target_pairs={{0,1},{1,0},{2,3},{3,2},{4,5},{5,4},{6,7},{7,6},{8,9},{9,8},{10,11... | collective-permute-start | bytes 786440 | tf_op jit(solution)/shard_map/ppermute | solution.py:424
  142.8 24.5 %collective-permute-start.53 = (bf16[64,2048]{1,0:T(8,128)(2,1)}, bf16[64,2048]{1,0:T(8,128)(2,1)}, u32[]{:S(2)}, u32[]{:S(2)}) collective-permute-start(bf16[64,2048]{1,0:T(8,128)(2,1)} %collective-permute-done.25.refs_2_), channel_id=1, source_target_pairs={{0,1},{1,0},{2,3},{3,2},{4,5},{5,4},{6,7},{7,6},{8,9},{9,8},{10,11... | collective-permute-start | bytes 786440 | tf_op jit(solution)/shard_map/ppermute | solution.py:424
  154.0 23.1 %collective-permute-start.44 = (bf16[64,2048]{1,0:T(8,128)(2,1)}, bf16[64,2048]{1,0:T(8,128)(2,1)S(1)}, u32[]{:S(2)}, u32[]{:S(2)}) collective-permute-start(bf16[64,2048]{1,0:T(8,128)(2,1)} %copy-done.67), channel_id=1, source_target_pairs={{0,1},{1,0},{2,3},{3,2},{4,5},{5,4},{6,7},{7,6},{8,9},{9,8},{10,11... | collective-permute-start | bytes 786440 | tf_op jit(solution)/shard_map/ppermute | solution.py:424
  162.0 30.5 %collective-permute-start.9 = (bf16[128,2048]{1,0:T(8,128)(2,1)}, bf16[128,2048]{1,0:T(8,128)(2,1)}, u32[]{:S(2)}, u32[]{:S(2)}) collective-permute-start(bf16[128,2048]{1,0:T(8,128)(2,1)} %get-tuple-element.77), channel_id=1, source_target_pairs={{0,2},{2,0},{4,6},{6,4},{8,10},{10,8},{12,14},{14,12},{16,18},{18,... | collective-permute-start | bytes 1572872 | tf_op jit(solution)/shard_map/ppermute | solution.py:415
  167.3 32.7 %collective-permute-start.27 = (bf16[128,2048]{1,0:T(8,128)(2,1)}, bf16[128,2048]{1,0:T(8,128)(2,1)S(1)}, u32[]{:S(2)}, u32[]{:S(2)}) collective-permute-start(bf16[128,2048]{1,0:T(8,128)(2,1)} %get-tuple-element.95), channel_id=1, source_target_pairs={{0,2},{2,0},{4,6},{6,4},{8,10},{10,8},{12,14},{14,12},{16,18},{18,... | collective-permute-start | bytes 1572872 | tf_op jit(solution)/shard_map/ppermute | solution.py:415
  167.6 32.6 %collective-permute-start.40 = (bf16[128,2048]{1,0:T(8,128)(2,1)}, bf16[128,2048]{1,0:T(8,128)(2,1)}, u32[]{:S(2)}, u32[]{:S(2)}) collective-permute-start(bf16[128,2048]{1,0:T(8,128)(2,1)} %get-tuple-element.108), channel_id=1, source_target_pairs={{0,2},{2,0},{4,6},{6,4},{8,10},{10,8},{12,14},{14,12},{16,18},{18,... | collective-permute-start | bytes 1572872 | tf_op jit(solution)/shard_map/ppermute | solution.py:415
  177.8 33.6 %collective-permute-start.50 = (bf16[128,2048]{1,0:T(8,128)(2,1)}, bf16[128,2048]{1,0:T(8,128)(2,1)}, u32[]{:S(2)}, u32[]{:S(2)}) collective-permute-start(bf16[128,2048]{1,0:T(8,128)(2,1)} %get-tuple-element.114), channel_id=1, source_target_pairs={{0,2},{2,0},{4,6},{6,4},{8,10},{10,8},{12,14},{14,12},{16,18},{18,... | collective-permute-start | bytes 1572872 | tf_op jit(solution)/shard_map/ppermute | solution.py:415
  190.1 34.7 %collective-permute-start.4 = (bf16[128,2048]{1,0:T(8,128)(2,1)}, bf16[128,2048]{1,0:T(8,128)(2,1)}, u32[]{:S(2)}, u32[]{:S(2)}) collective-permute-start(bf16[128,2048]{1,0:T(8,128)(2,1)} %get-tuple-element.74), channel_id=1, source_target_pairs={{0,2},{2,0},{4,6},{6,4},{8,10},{10,8},{12,14},{14,12},{16,18},{18,... | collective-permute-start | bytes 1572872 | tf_op jit(solution)/shard_map/ppermute | solution.py:415
  192.6 25.9 %collective-permute-start.45 = (bf16[128,2048]{1,0:T(8,128)(2,1)}, bf16[128,2048]{1,0:T(8,128)(2,1)}, u32[]{:S(2)}, u32[]{:S(2)}) collective-permute-start(bf16[128,2048]{1,0:T(8,128)(2,1)} %get-tuple-element.110), channel_id=1, source_target_pairs={{0,2},{2,0},{4,6},{6,4},{8,10},{10,8},{12,14},{14,12},{16,18},{18,... | collective-permute-start | bytes 1572872 | tf_op jit(solution)/shard_map/ppermute | solution.py:415
  200.0 26.3 %collective-permute-start.22 = (bf16[128,2048]{1,0:T(8,128)(2,1)}, bf16[128,2048]{1,0:T(8,128)(2,1)S(1)}, u32[]{:S(2)}, u32[]{:S(2)}) collective-permute-start(bf16[128,2048]{1,0:T(8,128)(2,1)} %get-tuple-element.92), channel_id=1, source_target_pairs={{0,2},{2,0},{4,6},{6,4},{8,10},{10,8},{12,14},{14,12},{16,18},{18,... | collective-permute-start | bytes 1572872 | tf_op jit(solution)/shard_map/ppermute | solution.py:415
  218.5 24.2 %collective-permute-start.28 = (bf16[128,2048]{1,0:T(8,128)(2,1)}, bf16[128,2048]{1,0:T(8,128)(2,1)S(1)}, u32[]{:S(2)}, u32[]{:S(2)}) collective-permute-start(bf16[128,2048]{1,0:T(8,128)(2,1)} %get-tuple-element.99), channel_id=1, source_target_pairs={{0,2},{2,0},{4,6},{6,4},{8,10},{10,8},{12,14},{14,12},{16,18},{18,... | collective-permute-start | bytes 1572872 | tf_op jit(solution)/shard_map/ppermute | solution.py:415
  238.6 28.6 %collective-permute-start.13 = (bf16[64,2048]{1,0:T(8,128)(2,1)S(1)}, bf16[64,2048]{1,0:T(8,128)(2,1)S(1)}, u32[]{:S(2)}, u32[]{:S(2)}) collective-permute-start(bf16[64,2048]{1,0:T(8,128)(2,1)S(1)} %get-tuple-element.84), channel_id=1, source_target_pairs={{0,4},{2,6},{4,0},{6,2},{8,12},{10,14},{12,8},{14,10},{16,20},{18,... | collective-permute-start | bytes 786440 | tf_op jit(solution)/shard_map/ppermute | solution.py:418
  240.6 40.9 %collective-permute-start.12 = (bf16[64,2048]{1,0:T(8,128)(2,1)S(1)}, bf16[64,2048]{1,0:T(8,128)(2,1)S(1)}, u32[]{:S(2)}, u32[]{:S(2)}) collective-permute-start(bf16[64,2048]{1,0:T(8,128)(2,1)S(1)} %get-tuple-element.82), channel_id=1, source_target_pairs={{0,4},{2,6},{4,0},{6,2},{8,12},{10,14},{12,8},{14,10},{16,20},{18,... | collective-permute-start | bytes 786440 | tf_op jit(solution)/shard_map/ppermute | solution.py:418
  240.7 57.1 %collective-permute-start.11 = (bf16[64,2048]{1,0:T(8,128)(2,1)S(1)}, bf16[64,2048]{1,0:T(8,128)(2,1)S(1)}, u32[]{:S(2)}, u32[]{:S(2)}) collective-permute-start(bf16[64,2048]{1,0:T(8,128)(2,1)S(1)} %get-tuple-element.80), channel_id=1, source_target_pairs={{0,4},{2,6},{4,0},{6,2},{8,12},{10,14},{12,8},{14,10},{16,20},{18,... | collective-permute-start | bytes 786440 | tf_op jit(solution)/shard_map/ppermute | solution.py:418
  243.3 30.5 %collective-permute-start.31 = (bf16[64,2048]{1,0:T(8,128)(2,1)S(1)}, bf16[64,2048]{1,0:T(8,128)(2,1)S(1)}, u32[]{:S(2)}, u32[]{:S(2)}) collective-permute-start(bf16[64,2048]{1,0:T(8,128)(2,1)S(1)} %get-tuple-element.104), channel_id=1, source_target_pairs={{0,4},{2,6},{4,0},{6,2},{8,12},{10,14},{12,8},{14,10},{16,20},{18,... | collective-permute-start | bytes 786440 | tf_op jit(solution)/shard_map/ppermute | solution.py:418
  267.2 24.9 %collective-permute-start.30 = (bf16[64,2048]{1,0:T(8,128)(2,1)S(1)}, bf16[64,2048]{1,0:T(8,128)(2,1)S(1)}, u32[]{:S(2)}, u32[]{:S(2)}) collective-permute-start(bf16[64,2048]{1,0:T(8,128)(2,1)S(1)} %get-tuple-element.102), channel_id=1, source_target_pairs={{0,4},{2,6},{4,0},{6,2},{8,12},{10,14},{12,8},{14,10},{16,20},{18,... | collective-permute-start | bytes 786440 | tf_op jit(solution)/shard_map/ppermute | solution.py:418
  273.8 29.1 %collective-permute-start.29 = (bf16[64,2048]{1,0:T(8,128)(2,1)S(1)}, bf16[64,2048]{1,0:T(8,128)(2,1)S(1)}, u32[]{:S(2)}, u32[]{:S(2)}) collective-permute-start(bf16[64,2048]{1,0:T(8,128)(2,1)S(1)} %get-tuple-element.100), channel_id=1, source_target_pairs={{0,4},{2,6},{4,0},{6,2},{8,12},{10,14},{12,8},{14,10},{16,20},{18,... | collective-permute-start | bytes 786440 | tf_op jit(solution)/shard_map/ppermute | solution.py:418
  (117 other events, 1224.7 us)

commit v3 on v1

v3 whole, which is shorter than its diff:
```python
import math

import jax
import jax.numpy as jnp
from jax import lax
from jax.experimental import pallas as pl
from jax.experimental.pallas import tpu as pltpu
from jax.sharding import PartitionSpec as P

BF = jnp.bfloat16
F32 = jnp.float32
VMEM = 56 * 1024 * 1024
TOGETHER = 4


def slots(routes, experts, capacity):
    flat_ids = routes.reshape(-1)
    one_hot = (flat_ids[:, None] == jnp.arange(experts, dtype=jnp.int32)[None, :]).astype(jnp.int32)
    before = jnp.cumsum(one_hot, axis=0) - one_hot
    slot_rank = jnp.sum(before * one_hot, axis=1)
    return flat_ids * capacity + slot_rank


def place(token_rows, positions, total_rows):
    return (
        jnp.zeros((total_rows, token_rows.shape[1]), token_rows.dtype).at[positions].set(token_rows)
    )


def hidden_rows(token_rows, gate_weight, up_weight):
    pre_gate = jnp.dot(token_rows, gate_weight, preferred_element_type=F32)
    pre_up = jnp.dot(token_rows, up_weight, preferred_element_type=F32)
    activation = (jax.nn.silu(pre_gate) * pre_up).astype(BF)
    return (pre_gate, pre_up, activation)


CONTRACT = (((1,), (1,)), ((), ()))


def hidden_grads(grad_rows, pre_gate, pre_up, down_weight):
    d_hidden = lax.dot_general(grad_rows, down_weight, CONTRACT, preferred_element_type=F32)
    sigmoid_gate = jax.nn.sigmoid(pre_gate)
    d_gate = (d_hidden * pre_up * sigmoid_gate * (1.0 + pre_gate * (1.0 - sigmoid_gate))).astype(BF)
    d_up = (d_hidden * pre_gate * sigmoid_gate).astype(BF)
    return d_gate, d_up


def input_rows(d_gate, d_up, gate_weight, up_weight):
    back_rows = lax.dot_general(d_gate, gate_weight, CONTRACT, preferred_element_type=F32)
    back_rows = back_rows + lax.dot_general(d_up, up_weight, CONTRACT, preferred_element_type=F32)
    return back_rows.astype(BF)


def outer_sum(left, right):
    return lax.dot_general(left, right, (((0,), (0,)), ((), ())), preferred_element_type=F32)


def routed_plan(tokens, route_ids, gate_probs, out_cot, w_gate, w_up, w_down):
    experts = lax.axis_size("expert")
    tok_rows, features = tokens.shape
    top_count = route_ids.shape[1]
    hidden = w_gate.shape[2]
    capacity = max(2, tok_rows * top_count * 4 // (3 * experts))
    total_rows = experts * capacity
    positions = slots(route_ids, experts, capacity)
    gate_weight, up_weight, down_weight = w_gate[0], w_up[0], w_down[0]

    def exchange(rows):
        blocks = rows.reshape(experts, capacity, features)
        return lax.all_to_all(blocks, "expert", 0, 0, tiled=True).reshape(-1, features)

    received = exchange(place(jnp.repeat(tokens, top_count, axis=0), positions, total_rows))
    pre_gate, pre_up, activation = hidden_rows(received, gate_weight, up_weight)
    result = jnp.dot(activation, down_weight, preferred_element_type=F32).astype(BF)
    picked = exchange(result)[positions].reshape(tok_rows, top_count, features)
    combined = jnp.einsum("tk,tkd->td", gate_probs, picked.astype(F32)).astype(BF)
    scaled = (gate_probs[:, :, None] * out_cot[:, None, :].astype(F32)).astype(BF)
    grads_in = exchange(place(scaled.reshape(-1, features), positions, total_rows))
    d_gate, d_up = hidden_grads(grads_in, pre_gate, pre_up, down_weight)
    back = exchange(input_rows(d_gate, d_up, gate_weight, up_weight))
    grad_tokens = jnp.sum(
        back[positions].reshape(tok_rows, top_count, features).astype(F32), axis=1
    ).astype(BF)
    gate_up_sum = lax.psum_scatter(
        outer_sum(received, jnp.concatenate([d_gate, d_up], axis=1)).astype(BF),
        "replica",
        scatter_dimension=0,
        tiled=True,
    )
    down_sum = lax.psum_scatter(
        outer_sum(activation, grads_in).astype(BF), "replica", scatter_dimension=0, tiled=True
    )
    return (
        combined,
        grad_tokens,
        gate_up_sum[:, :hidden][None],
        gate_up_sum[:, hidden:][None],
        down_sum[None],
    )

def dot(left, right):
    return jnp.dot(left, right, preferred_element_type=F32)


def dot_t(left, right):
    return lax.dot_general(left, right, CONTRACT, preferred_element_type=F32)


def whole(array):
    return pl.BlockSpec(array.shape, lambda *_: (0,) * array.ndim)


def cost(flops, *arrays):
    moved = sum(math.prod(a.shape) * a.dtype.itemsize for a in arrays)
    return pl.CostEstimate(flops=flops, bytes_accessed=moved, transcendentals=0)


def params(steps=0):
    order = ("arbitrary",) * steps if steps else None
    return pltpu.CompilerParams(dimension_semantics=order, vmem_limit_bytes=VMEM)


def plan_and_pack(expert, experts, capacity, left, right):
    count, tok_rows, half = right.shape
    lanes = left.shape[2] - half
    length, room = TOGETHER * tok_rows, TOGETHER * capacity
    groups = count // TOGETHER
    width = 2 * half + lanes

    def body(expert_ref, left_ref, right_ref, mine_ref, theirs_ref, pick_ref, place_ref):
        shares = left_ref[:, :, half:].reshape(length, lanes).astype(F32)
        lane = lax.broadcasted_iota(jnp.int32, (length, lanes), 1)
        routed = []
        for index in (expert_ref[0], expert_ref[0] ^ 1):
            held = (lane == index) | (lane == index + experts) | (lane == index + 2 * experts)
            weight = jnp.sum(jnp.where(held, shares, 0.0), axis=1, keepdims=True)
            routed.append(jnp.broadcast_to((weight > 0).astype(F32), (length, room)))
        routed = jnp.concatenate(routed, axis=1)
        row = lax.broadcasted_iota(jnp.int32, (length, length), 0)
        col = lax.broadcasted_iota(jnp.int32, (length, length), 1)
        rank = dot((row >= col).astype(BF), routed.astype(BF))
        slot = lax.broadcasted_iota(jnp.int32, (length, 2 * room), 1) % room
        chosen = (rank == (slot + 1).astype(F32)) & (routed > 0)
        place = jnp.where(chosen, 1.0, 0.0)
        place_ref[0] = place.astype(BF)
        pick = place.T.astype(BF)
        pick_ref[0] = pick
        for ref, start, stop, to in (
            (left_ref, 0, half, 0),
            (right_ref, 0, half, half),
            (left_ref, half, half + lanes, 2 * half),
        ):
            for at in range(start, stop, 512):
                size = min(512, stop - at)
                rows = ref[:, :, at : at + size].reshape(length, size)
                packed = dot(pick, rows).astype(BF)
                out = pl.ds(to + at - start, size)
                mine_ref[:, out] = packed[:room]
                theirs_ref[:, out] = packed[room:]

    rows = jax.ShapeDtypeStruct((groups * room, width), BF)
    pick = jax.ShapeDtypeStruct((groups, 2 * room, length), BF)
    place = jax.ShapeDtypeStruct((groups, length, 2 * room), BF)
    outs = (rows, rows, pick, place)
    return pl.pallas_call(
        body,
        grid_spec=pltpu.PrefetchScalarGridSpec(
            num_scalar_prefetch=1,
            grid=(groups,),
            in_specs=[
                pl.BlockSpec((TOGETHER, tok_rows, half + lanes), lambda i, e: (i, 0, 0)),
                pl.BlockSpec((TOGETHER, tok_rows, half), lambda i, e: (i, 0, 0)),
            ],
            out_specs=[
                pl.BlockSpec((room, width), lambda i, e: (i, 0)),
                pl.BlockSpec((room, width), lambda i, e: (i, 0)),
                pl.BlockSpec((1, 2 * room, length), lambda i, e: (i, 0, 0)),
                pl.BlockSpec((1, length, 2 * room), lambda i, e: (i, 0, 0)),
            ],
        ),
        out_shape=outs,
        compiler_params=params(1),
        cost_estimate=cost(2 * groups * length * 2 * room * width, left, right, *outs),
        name="plan_and_pack",
    )(expert, left, right)


def pack(pick, chunks, first):
    count, tok_rows, features = chunks.shape
    room, length = pick.shape[1] // 2, pick.shape[2]
    groups = count // TOGETHER

    def body(pick_ref, rows_ref, mine_ref, theirs_ref):
        for at in range(0, features, 512):
            cols = pl.ds(at, 512)
            packed = dot(pick_ref[0], rows_ref[:, :, cols].reshape(length, 512)).astype(BF)
            mine_ref[:, cols] = packed[:room]
            theirs_ref[:, cols] = packed[room:]

    out = jax.ShapeDtypeStruct((groups * room, features), BF)
    return pl.pallas_call(
        body,
        grid=(groups,),
        in_specs=[
            pl.BlockSpec((1, 2 * room, length), lambda i: (first + i, 0, 0)),
            pl.BlockSpec((TOGETHER, tok_rows, features), lambda i: (i, 0, 0)),
        ],
        out_specs=[pl.BlockSpec((room, features), lambda i: (i, 0))] * 2,
        out_shape=(out, out),
        compiler_params=params(1),
        cost_estimate=cost(2 * groups * length * 2 * room * features, chunks, out, out),
        name="pack",
    )(pick, chunks)


def spread(place, mine, theirs):
    groups, length, slots_of = place.shape
    room, features = slots_of // 2, mine.shape[1]

    def body(place_ref, mine_ref, theirs_ref, out_ref):
        for at in range(0, features, 512):
            cols = pl.ds(at, 512)
            rows = jnp.concatenate([mine_ref[:, cols], theirs_ref[:, cols]], axis=0)
            out_ref[:, cols] = dot(place_ref[0], rows).astype(BF)

    out = jax.ShapeDtypeStruct((groups * length, features), BF)
    return pl.pallas_call(
        body,
        grid=(groups,),
        in_specs=[
            pl.BlockSpec((1, length, slots_of), lambda i: (i, 0, 0)),
            pl.BlockSpec((room, features), lambda i: (i, 0)),
            pl.BlockSpec((room, features), lambda i: (i, 0)),
        ],
        out_specs=pl.BlockSpec((length, features), lambda i: (i, 0)),
        out_shape=out,
        compiler_params=params(1),
        cost_estimate=cost(2 * math.prod(place.shape) * features, mine, theirs, out),
        name="spread",
    )(place, mine, theirs)


def row_weight(expert, experts, *lane_refs):
    lanes = jnp.concatenate([ref[...] for ref in lane_refs], axis=0).astype(F32)
    lane = lax.broadcasted_iota(jnp.int32, lanes.shape, 1)
    held = (lane == expert) | (lane == expert + experts) | (lane == expert + 2 * experts)
    return jnp.sum(jnp.where(held, lanes, 0.0), axis=1, keepdims=True)


def forward(expert, experts, mine, theirs, w_gate, w_up, w_down, with_result):
    part_rows, width = mine.shape
    _, features, hidden = w_gate.shape
    rows = 2 * part_rows
    block = 256 if hidden % 256 == 0 else hidden
    steps = hidden // block

    def body(expert_ref, mine_ref, theirs_ref, gate_ref, up_ref, down_ref, *refs):
        act_ref, to_gate_ref, to_up_ref = refs[:3]
        x = jnp.concatenate([mine_ref[:, :features], theirs_ref[:, :features]], axis=0)
        pre_gate = dot(x, gate_ref[0])
        pre_up = dot(x, up_ref[0])
        s = jax.nn.sigmoid(pre_gate)
        silu = pre_gate * s
        act = (silu * pre_up).astype(BF)
        act_ref[...] = act
        to_gate_ref[...] = pre_up * s * (1.0 + pre_gate * (1.0 - s))
        to_up_ref[...] = silu
        if with_result:
            mine_out, theirs_out, total = refs[3:]
            step = pl.program_id(0)
            part = dot(act, down_ref[0])

            @pl.when(step == 0)
            def _():
                total[...] = part

            @pl.when(step > 0)
            def _():
                total[...] += part

            @pl.when(step == steps - 1)
            def _():
                weight = row_weight(
                    expert_ref[0],
                    experts,
                    mine_ref.at[:, features:],
                    theirs_ref.at[:, features:],
                )
                out = (total[...] * weight).astype(BF)
                mine_out[...] = out[:part_rows]
                theirs_out[...] = out[part_rows:]

    row_out = jax.ShapeDtypeStruct((part_rows, features), BF)
    outs = [jax.ShapeDtypeStruct((rows, hidden), t) for t in (BF, F32, F32)]
    out_specs = [pl.BlockSpec((rows, block), lambda i, e: (0, i))] * 3
    scratch = []
    if with_result:
        outs += [row_out, row_out]
        out_specs += [whole(row_out)] * 2
        scratch = [pltpu.VMEM((rows, features), F32)]
    columns = pl.BlockSpec((1, features, block), lambda i, e: (0, 0, i))
    return pl.pallas_call(
        body,
        grid_spec=pltpu.PrefetchScalarGridSpec(
            num_scalar_prefetch=1,
            grid=(steps,),
            in_specs=[
                whole(mine),
                whole(theirs),
                columns,
                columns,
                pl.BlockSpec((1, block, features), lambda i, e: (0, i if with_result else 0, 0)),
            ],
            out_specs=out_specs,
            scratch_shapes=scratch,
        ),
        out_shape=outs,
        compiler_params=params(1),
        cost_estimate=cost(
            2 * rows * features * hidden * (3 if with_result else 2),
            mine, theirs, w_gate, w_up, *outs,
        ),
        name="forward",
    )(expert, mine, theirs, w_gate, w_up, w_down)


def backward(
    expert, experts, mine, theirs, x_mine, x_theirs, to_gate, to_up, weights, group, with_result
):
    part_rows, features = mine.shape
    hidden = to_gate.shape[1]
    rows = 2 * part_rows
    skip = to_gate.shape[0] // rows
    lanes = x_mine.shape[1] - features
    block = 256 if hidden % 256 == 0 else hidden
    steps = hidden // block

    def body(expert_ref, mine_ref, theirs_ref, lanes_a, lanes_b, *refs):
        gate_a, gate_b, up_a, up_b, w_gate_ref, w_up_ref, w_down_ref = refs[:7]
        scaled_ref, d_gate_ref, d_up_ref = refs[7:10]
        step = pl.program_id(0)

        @pl.when(step == 0)
        def _():
            weight = row_weight(expert_ref[0], experts, lanes_a, lanes_b)
            cot = jnp.concatenate([mine_ref[...], theirs_ref[...]], axis=0)
            scaled_ref[...] = (cot.astype(F32) * weight).astype(BF)

        d_hidden = dot_t(scaled_ref[...], w_down_ref[0])
        to_gates = jnp.concatenate([gate_a[...], gate_b[...]], axis=0)
        to_ups = jnp.concatenate([up_a[...], up_b[...]], axis=0)
        d_gate = (d_hidden * to_gates).astype(BF)
        d_up = (d_hidden * to_ups).astype(BF)
        d_gate_ref[...] = d_gate
        d_up_ref[...] = d_up
        if with_result:
            mine_out, theirs_out, total = refs[10:]
            part = dot_t(d_gate, w_gate_ref[0]) + dot_t(d_up, w_up_ref[0])

            @pl.when(step == 0)
            def _():
                total[...] = part

            @pl.when(step > 0)
            def _():
                total[...] += part

            @pl.when(step == steps - 1)
            def _():
                out = total[...].astype(BF)
                mine_out[...] = out[:part_rows]
                theirs_out[...] = out[part_rows:]

    row_out = jax.ShapeDtypeStruct((part_rows, features), BF)
    scaled = jax.ShapeDtypeStruct((rows, features), BF)
    part_out = jax.ShapeDtypeStruct((rows, hidden), BF)
    outs = [scaled, part_out, part_out]
    part_spec = pl.BlockSpec((rows, block), lambda i, e: (0, i))
    out_specs = [whole(scaled), part_spec, part_spec]
    scratch = []
    if with_result:
        outs += [row_out, row_out]
        out_specs += [whole(row_out)] * 2
        scratch = [pltpu.VMEM((rows, features), F32)]
    lane_spec = pl.BlockSpec((part_rows, lanes), lambda i, e: (group, features // lanes))
    first = pl.BlockSpec((part_rows, block), lambda i, e: (group, i))
    second = pl.BlockSpec((part_rows, block), lambda i, e: (group + skip, i))
    columns = pl.BlockSpec((1, features, block), lambda i, e: (0, 0, i if with_result else 0))
    return pl.pallas_call(
        body,
        grid_spec=pltpu.PrefetchScalarGridSpec(
            num_scalar_prefetch=1,
            grid=(steps,),
            in_specs=[
                whole(mine),
                whole(theirs),
                lane_spec,
                lane_spec,
                first,
                second,
                first,
                second,
                columns,
                columns,
                pl.BlockSpec((1, block, features), lambda i, e: (0, i, 0)),
            ],
            out_specs=out_specs,
            scratch_shapes=scratch,
        ),
        out_shape=outs,
        compiler_params=params(1),
        cost_estimate=cost(
            2 * rows * features * hidden * (3 if with_result else 1), mine, theirs, *outs
        ),
        name="backward",
    )(expert, mine, theirs, x_mine, x_theirs, to_gate, to_gate, to_up, to_up, *weights)


def rows_grad(left, right):
    return lax.dot_general(left, right, (((0,), (0,)), ((), ())), preferred_element_type=F32)


def in_order(mine, theirs, groups):
    size = mine.shape[0] // groups
    parts = []
    for at in range(0, mine.shape[0], size):
        parts += [mine[at : at + size], theirs[at : at + size]]
    return parts


def gate_up_grad(replica, xs, xs_other, d_gates, d_ups):
    features, hidden = xs[0].shape[1] // 256 * 256, d_gates[0].shape[1]
    half = features // 2
    block = 256
    steps = half // block
    n = len(d_gates)
    groups = n - 1

    def body(_, *refs):
        a, b, c, d = refs[:4]
        x = jnp.concatenate([a[...], b[...], *in_order(c[...], d[...], groups)], axis=0)
        for at, out in ((4, refs[-2]), (4 + n, refs[-1])):
            grads = jnp.concatenate([ref[...] for ref in refs[at : at + n]], axis=0)
            out[0] = rows_grad(x, grads).astype(BF)

    out = jax.ShapeDtypeStruct((1, half, hidden), BF)
    ins = (*xs, *xs_other)
    rows = sum(x.shape[0] for x in ins)
    return pl.pallas_call(
        body,
        grid_spec=pltpu.PrefetchScalarGridSpec(
            num_scalar_prefetch=1,
            grid=(steps,),
            in_specs=[
                pl.BlockSpec((x.shape[0], block), lambda i, r: (0, r[0] * steps + i)) for x in ins
            ]
            + [whole(d) for d in (*d_gates, *d_ups)],
            out_specs=[pl.BlockSpec((1, block, hidden), lambda i, r: (0, i, 0))] * 2,
        ),
        out_shape=(out, out),
        compiler_params=params(1),
        cost_estimate=cost(4 * rows * half * hidden, *ins, *d_gates, *d_ups, out, out),
        name="gate_up_grad",
    )(replica, *ins, *d_gates, *d_ups)


def down_grad(replica, act, act_other, scaleds):
    features, hidden = scaleds[0].shape[1], act.shape[1]
    half, rows = hidden // 2, act.shape[0]
    block = 512
    groups = len(scaleds) - 1

    def body(_, act_ref, other_ref, *refs):
        other = other_ref[...]
        acts = [act_ref[...], *in_order(other[: rows // 2], other[rows // 2 :], groups)]
        cot = jnp.concatenate([ref[...] for ref in refs[:-1]], axis=0)
        refs[-1][0] = rows_grad(jnp.concatenate(acts, axis=0), cot).astype(BF)

    out = jax.ShapeDtypeStruct((1, half, features), BF)
    return pl.pallas_call(
        body,
        grid_spec=pltpu.PrefetchScalarGridSpec(
            num_scalar_prefetch=1,
            grid=(features // block,),
            in_specs=[pl.BlockSpec((rows, half), lambda i, r: (0, r[0]))] * 2
            + [pl.BlockSpec((c.shape[0], block), lambda i, r: (0, i)) for c in scaleds],
            out_specs=pl.BlockSpec((1, half, block), lambda i, r: (0, 0, i)),
        ),
        out_shape=out,
        compiler_params=params(1),
        cost_estimate=cost(4 * rows * half * features, act, act_other, *scaleds, out),
        name="down_grad",
    )(replica, act, act_other, *scaleds)


def split3(value):
    high = value.astype(BF)
    rest = value - high.astype(F32)
    mid = rest.astype(BF)
    low = (rest - mid.astype(F32)).astype(BF)
    return high, mid, low


def dense_plan(tokens, route_ids, gate_probs, out_cot, w_gate, w_up, w_down):
    experts = lax.axis_size("expert")
    tok_rows, features = tokens.shape
    top_count = route_ids.shape[1]
    half = features // 2
    capacity = max(2, tok_rows * top_count * 4 // (3 * experts))
    expert = lax.axis_index("expert").astype(jnp.int32).reshape(1)
    replica = lax.axis_index("replica").astype(jnp.int32).reshape(1)
    same_core = [list(range(core, experts, 2)) for core in range(2)]

    def gather(rows):
        return lax.all_gather(rows, "expert", axis_index_groups=same_core)

    def home(rows):
        return lax.psum_scatter(
            rows, "expert", scatter_dimension=0, axis_index_groups=same_core, tiled=True
        )

    def to_core(rows):
        return lax.ppermute(rows, "expert", [(i, i ^ 1) for i in range(experts)])

    def to_y(rows):
        return lax.ppermute(rows, "replica", [(0, 1), (1, 0)])

    chosen = route_ids[:, :, None] == jnp.arange(experts, dtype=jnp.int32)
    share = jnp.sum(jnp.where(chosen, gate_probs[:, :, None], 0.0), axis=1)
    pad = jnp.zeros((tok_rows, -(3 * experts) % 128), BF)
    left = gather(jnp.concatenate([tokens[:, :half], *split3(share), pad], axis=1))
    right = gather(tokens[:, half:])
    cot = gather(out_cot)
    left_other, right_other = to_y(left), to_y(right)
    cot_other = [to_y(cot[at : at + TOGETHER]) for at in range(0, cot.shape[0], TOGETHER)]

    mine, theirs, pick, place = plan_and_pack(expert, experts, capacity, left, right)
    theirs = to_core(theirs)
    weights = (w_gate, w_up, w_down)
    act, to_gate, to_up, out_mine, out_theirs = forward(
        expert, experts, mine, theirs, *weights, True
    )
    combined = home(spread(place, out_mine, to_core(out_theirs)))

    cot_mine, cot_theirs = pack(pick, cot, 0)
    scaled, d_gate, d_up, out_mine, out_theirs = backward(
        expert, experts, cot_mine, to_core(cot_theirs), mine, theirs, to_gate, to_up,
        weights, 0, True,
    )
    grad_tokens = home(spread(place, out_mine, to_core(out_theirs)))
    scaleds, d_gates, d_ups = [scaled], [d_gate], [d_up]

    mine_other, theirs_other, pick, _ = plan_and_pack(
        expert, experts, capacity, left_other, right_other
    )
    theirs_other = to_core(theirs_other)
    act_other, to_gate, to_up = forward(
        expert, experts, mine_other, theirs_other, *weights, False
    )
    for group, rows in enumerate(cot_other):
        cot_mine, cot_theirs = pack(pick, rows, group)
        scaled, d_gate, d_up = backward(
            expert, experts, cot_mine, to_core(cot_theirs), mine_other, theirs_other,
            to_gate, to_up, weights, group, False,
        )
        scaleds.append(scaled)
        d_gates.append(d_gate)
        d_ups.append(d_up)

    grad_gate, grad_up = gate_up_grad(
        replica, (mine, theirs), (mine_other, theirs_other), d_gates, d_ups
    )
    grad_down = down_grad(replica, act, act_other, scaleds)
    return (combined, grad_tokens, grad_gate, grad_up, grad_down)


def dense_fits(mesh):
    experts, replicas = mesh.shape["expert"], mesh.shape["replica"]
    return replicas == 2 and experts % (2 * TOGETHER) == 0 and experts <= 16


def solution(mesh):
    placed = (
        P(("expert", "replica"), None),
        P(("expert", "replica"), None),
        P(("expert", "replica"), None),
        P(("expert", "replica"), None),
        P("expert", None, None),
        P("expert", None, None),
        P("expert", None, None),
    )
    return jax.shard_map(
        dense_plan if dense_fits(mesh) else routed_plan,
        mesh=mesh,
        in_specs=placed,
        out_specs=(
            P(("expert", "replica"), None),
            P(("expert", "replica"), None),
            P("expert", "replica", None),
            P("expert", "replica", None),
            P("expert", "replica", None),
        ),
        check_vma=False,
    )
```

time: 262 us -> 320 us (1.22)
  Pallas kernels: 0 us -> 84.8 us
  waiting for transfers between devices: 150 us -> 200 us
  matrix products: 42.6 us -> 0 us
  other arithmetic: 20.3 us -> 0.73 us
  local copies, waits for them, and re-layouts: 32.9 us -> 14.7 us
  starting transfers between devices: 1.58 us -> 4.92 us
    pallas_call x0 -> x14, Pallas kernels: none -> 84.8 us  [the longest x3 28.8 us: backward(): pl.pallas_call(body, grid_spec=pltpu.PrefetchScalarGridSpec(num_scalar_pr...]
    dot_general x16 -> x0, matrix products: 42.6 us -> none  [the longest x2 9.53 us: pack(): jnp.einsum('gst,gtd->gsd', pick, rows[:, :, :2 * features], preferred_ele...]
    all_gather x1 -> x3, waiting for transfers between devices: 79.7 us -> 108 us  [gather(): return lax.all_gather(rows, 'expert', axis_index_groups=same_core)]
    ppermute x2 -> x11, waiting for transfers between devices: 69.9 us -> 91.6 us  [the longest x4 80.3 us: to_y(): return lax.ppermute(rows, 'replica', [(0, 1), (1, 0)])]
    another operation x5 -> x0, other arithmetic: 10.4 us -> none  [the longest x1 7.91 us: dense_plan(): jnp.stack([relay, sibling], axis=1).reshape(experts, tok_rows, width)]
    another operation x7 -> x0, local copies, waits for them, and re-layouts: 8.3 us -> none  [the longest x1 7.92 us: dense_plan(): jnp.stack([relay, sibling], axis=1).reshape(experts, tok_rows, width)]
    concatenate x1 -> x0, other arithmetic: 7.85 us -> none  [dense_plan(): dense = jnp.concatenate([spread(pick, result), spread(pick, back)], axis=2)]
    dynamic_slice x2 -> x0, local copies, waits for them, and re-layouts: 4.64 us -> none  [pack(): lax.dynamic_slice_in_dim(rows, at + i * experts, 1, 2)[:, :, 0].astype(F32)]
  transfers between devices with their start and end apart: 4 -> 16, of which waited for: 3 -> 10; matrix products, arithmetic and copies ran while one was open for 28% -> 1% of each run, Pallas kernels for 0% -> 27%
where the time goes in v3:
time: 320 us; the launch traced here: 319 us
  waiting for transfers between devices  200 us (62%)
  Pallas kernels  84.8 us (26%)
  local copies, waits for them, and re-layouts  14.7 us (5%)
  between operations  13.9 us (4%)
  starting transfers between devices  4.92 us (2%)
    all_gather x3, waiting for transfers between devices, gather(): return lax.all_gather(rows, 'expert', axis_index_groups=same_core)  108 us
    ppermute x4, waiting for transfers between devices, to_y(): return lax.ppermute(rows, 'replica', [(0, 1), (1, 0)])  80.3 us
    pallas_call x3, Pallas kernels, backward(): pl.pallas_call(body, grid_spec=pltpu.PrefetchScalarGridSpec(num_scalar_pr...  28.8 us
    pallas_call x2, Pallas kernels, forward(): pl.pallas_call(body, grid_spec=pltpu.PrefetchScalarGridSpec(num_scalar_pr...  20.3 us
    ppermute x7, waiting for transfers between devices, to_core(): return lax.ppermute(rows, 'expert', [(i, i ^ 1) for i in range(experts)])  11.3 us
    unnamed x26, local copies, waits for them, and re-layouts  10.6 us
    pallas_call x3, Pallas kernels, pack(): pl.pallas_call(body, grid=(groups,), in_specs=[pl.BlockSpec((1, 2 * room,...  8.57 us
    pallas_call x2, Pallas kernels, plan_and_pack(): pl.pallas_call(body, grid_spec=pltpu.PrefetchScalarGridSpec(num_scalar_pr...  7.85 us
  transfers between devices with their start and end apart: 16, of which 10 were waited for; matrix products, arithmetic and copies ran while one was open for 1% of the time, Pallas kernels for 27%

profile of v3, /device:TPU:0, one launch (start us, length us, event | category | flops | bytes accessed | tf_op | source)
XLA Modules:
  0.0 319.1 jit_solution(10118258262722964084)
XLA Ops:
  11.5 42.0 %all-gather.9.cloned.1.call-done = bf16[512,1024]{1,0:T(8,128)(2,1)} async-done(((bf16[64,1024]{1,0:T(8,128)(2,1)}), bf16[512,1024]{1,0:T(8,128)(2,1)}) %all-gather.9.cloned.1.call-update) | async-done | bytes 1048592 | tf_op jit(solution)/shard_map/all_gather | solution.py:515
  53.6 42.6 %all-gather.7.cloned.1.call-done = bf16[512,1152]{1,0:T(8,128)(2,1)} async-done(((bf16[64,1152]{1,0:T(8,128)(2,1)}), bf16[512,1152]{1,0:T(8,128)(2,1)}) %all-gather.7.cloned.1.call-update) | async-done | bytes 1179664 | tf_op jit(solution)/shard_map/all_gather | solution.py:515
  96.2 3.9 %plan_and_pack.2 = (bf16[256,2176]{1,0:T(8,128)(2,1)}, bf16[256,2176]{1,0:T(8,128)(2,1)}, bf16[2,256,256]{2,1,0:T(8,128)(2,1)}, bf16[2,256,256]{2,1,0:T(8,128)(2,1)}) custom-call(s32[1]{0:T(128)} %bitcast.expert_ref, bf16[8,64,1152]{2,1,0:T(8,128)(2,1)} %bitcast.8, bf16[8,64,1024]{2,1,0:T(8,128)(2,1)} %bitcast.10), custom_call_target="tpu_custom_call" | custom-call | flops 570425344 | bytes 4980736 | tf_op jit(solution)/shard_map/plan_and_pack/pallas_call | solution.py:165
  100.1 3.0 collective-permute-done.theirs_ref.lanes_b.refs_1_
  104.1 12.0 %forward.2 = (bf16[512,768]{1,0:T(8,128)(2,1)}, f32[512,768]{1,0:T(8,128)}, f32[512,768]{1,0:T(8,128)}, bf16[256,2048]{1,0:T(8,128)(2,1)}, bf16[256,2048]{1,0:T(8,128)(2,1)}) custom-call(s32[1]{0:T(128)} %bitcast.expert_ref, bf16[256,2176]{1,0:T(8,128)(2,1)} %get-tuple-element.40.mine_ref.lanes_a.refs_0_, bf16[256,2176]{1,0:T(8,128)(2,1)} %copy-done.4, ...), custom_call_target="tpu_custom_call" | custom-call | flops 4831838208 | bytes 14548992 | tf_op jit(solution)/shard_map/forward/pallas_call | solution.py:302
  116.3 2.7 collective-permute-done.1.theirs_ref
  120.0 3.1 spread.2
  123.4 23.0 %all-gather.11.cloned.1.call-done = bf16[512,2048]{1,0:T(8,128)(2,1)} async-done(((bf16[64,2048]{1,0:T(8,128)(2,1)}), bf16[512,2048]{1,0:T(8,128)(2,1)}) %all-gather.11.cloned.1.call-update) | async-done | bytes 2097168 | tf_op jit(solution)/shard_map/all_gather | solution.py:515
  146.4 3.2 pack.3
  149.6 2.9 collective-permute-done.2.theirs_ref
  153.4 16.4 %backward.3 = (bf16[512,2048]{1,0:T(8,128)(2,1)}, bf16[512,768]{1,0:T(8,128)(2,1)}, bf16[512,768]{1,0:T(8,128)(2,1)}, bf16[256,2048]{1,0:T(8,128)(2,1)}, bf16[256,2048]{1,0:T(8,128)(2,1)}) custom-call(s32[1]{0:T(128)} %bitcast.expert_ref, bf16[256,2048]{1,0:T(8,128)(2,1)} %get-tuple-element.45.mine_ref, bf16[256,2048]{1,0:T(8,128)(2,1)} %copy-done.5, ...), custom_call_target="tpu_custom_call" | custom-call | flops 4831838208 | bytes 7864320 | tf_op jit(solution)/shard_map/backward/pallas_call | solution.py:389
  170.0 2.7 collective-permute-done.3.theirs_ref
  173.7 3.2 %spread.3 = bf16[512,2048]{1,0:T(8,128)(2,1)} custom-call(bf16[2,256,256]{2,1,0:T(8,128)(2,1)} %get-tuple-element.39.place_ref, bf16[256,2048]{1,0:T(8,128)(2,1)} %get-tuple-element.49.mine_ref, bf16[256,2048]{1,0:T(8,128)(2,1)} %copy-done.6), custom_call_target="tpu_custom_call" | custom-call | flops 536870912 | bytes 4194304 | tf_op jit(solution)/shard_map/spread/pallas_call | solution.py:227
  182.6 45.8 %collective-permute-done.5.right_ref = bf16[8,64,1024]{2,1,0:T(8,128)(2,1)S(1)} collective-permute-done((bf16[8,64,1024]{2,1,0:T(8,128)(2,1)}, bf16[8,64,1024]{2,1,0:T(8,128)(2,1)S(1)}, u32[]{:S(2)}, u32[]{:S(2)}) %collective-permute-start.5) | collective-permute-done | bytes 1048608 | tf_op jit(solution)/shard_map/ppermute | solution.py:526
  230.3 3.9 %plan_and_pack.3 = (bf16[256,2176]{1,0:T(8,128)(2,1)}, bf16[256,2176]{1,0:T(8,128)(2,1)}, bf16[2,256,256]{2,1,0:T(8,128)(2,1)}, bf16[2,256,256]{2,1,0:T(8,128)(2,1)}) custom-call(s32[1]{0:T(128)} %bitcast.expert_ref, bf16[8,64,1152]{2,1,0:T(8,128)(2,1)} %copy-done.3, bf16[8,64,1024]{2,1,0:T(8,128)(2,1)} %copy-done.10), custom_call_target="tpu_custom_call" | custom-call | flops 570425344 | bytes 4980736 | tf_op jit(solution)/shard_map/plan_and_pack/pallas_call | solution.py:165
  234.2 16.6 %collective-permute-done.7.rows_ref = bf16[4,64,2048]{2,1,0:T(8,128)(2,1)S(1)} collective-permute-done((bf16[4,64,2048]{2,1,0:T(8,128)(2,1)}, bf16[4,64,2048]{2,1,0:T(8,128)(2,1)S(1)}, u32[]{:S(2)}, u32[]{:S(2)}) %collective-permute-start.7) | collective-permute-done | bytes 1048608 | tf_op jit(solution)/shard_map/ppermute | solution.py:526
  251.8 2.7 pack.4
  254.5 18.0 %collective-permute-done.9.rows_ref = bf16[4,64,2048]{2,1,0:T(8,128)(2,1)S(1)} collective-permute-done((bf16[4,64,2048]{2,1,0:T(8,128)(2,1)}, bf16[4,64,2048]{2,1,0:T(8,128)(2,1)S(1)}, u32[]{:S(2)}, u32[]{:S(2)}) %collective-permute-start.9) | collective-permute-done | bytes 1048608 | tf_op jit(solution)/shard_map/ppermute | solution.py:526
  273.4 2.7 pack.5
  277.2 8.3 %forward.3 = (bf16[512,768]{1,0:T(8,128)(2,1)}, f32[512,768]{1,0:T(8,128)}, f32[512,768]{1,0:T(8,128)}) custom-call(s32[1]{0:T(128)} %bitcast.expert_ref, bf16[256,2176]{1,0:T(8,128)(2,1)} %get-tuple-element.51.mine_ref.lanes_a.refs_2_, bf16[256,2176]{1,0:T(8,128)(2,1)} %copy-done.1, bf16[1,2048,768]{2,1,0:T(8,128)(2,1)} %refs_4_.5, ...), custom_call_target="tpu_custom_call" | custom-call | flops 3221225472 | bytes 12451840 | tf_op jit(solution)/shard_map/forward/pallas_call | solution.py:302
  286.4 6.2 %backward.4 = (bf16[256,2048]{1,0:T(8,128)(2,1)}, bf16[256,768]{1,0:T(8,128)(2,1)}, bf16[256,768]{1,0:T(8,128)(2,1)}) custom-call(s32[1]{0:T(128)} %bitcast.expert_ref, bf16[128,2048]{1,0:T(8,128)(2,1)} %get-tuple-element.55.mine_ref, bf16[128,2048]{1,0:T(8,128)(2,1)} %copy-done.11, bf16[256,2176]{1,0:T(8,128)(2,1)} %get-tuple-element.51.mine_ref.lanes_a.refs_2_, ...), custom_call_target="tpu_custom_call" | custom-call | flops 805306368 | bytes 2883584 | tf_op jit(solution)/shard_map/backward/pallas_call | solution.py:389
  293.4 6.2 %backward.5 = (bf16[256,2048]{1,0:T(8,128)(2,1)}, bf16[256,768]{1,0:T(8,128)(2,1)}, bf16[256,768]{1,0:T(8,128)(2,1)}) custom-call(s32[1]{0:T(128)} %bitcast.expert_ref, bf16[128,2048]{1,0:T(8,128)(2,1)} %get-tuple-element.60.mine_ref, bf16[128,2048]{1,0:T(8,128)(2,1)} %copy-done.12, bf16[256,2176]{1,0:T(8,128)(2,1)} %get-tuple-element.51.mine_ref.lanes_a.refs_2_, ...), custom_call_target="tpu_custom_call" | custom-call | flops 805306368 | bytes 2883584 | tf_op jit(solution)/shard_map/backward/pallas_call | solution.py:389
  299.7 5.6 %down_grad.1 = bf16[1,384,2048]{2,1,0:T(8,128)(2,1)} custom-call(s32[1]{0:T(128)} %bitcast.4._, bf16[512,768]{1,0:T(8,128)(2,1)} %get-tuple-element.68.act_ref, bf16[512,768]{1,0:T(8,128)(2,1)} %get-tuple-element.69.other_ref, bf16[512,2048]{1,0:T(8,128)(2,1)} %get-tuple-element.70.refs_0_, bf16[256,2048]{1,0:T(8,128)(2,1)} %get-tuple-element.71.refs_1_, ...), custom_call_target="tpu_custom_call" | custom-call | flops 1610612736 | bytes 7340032 | tf_op jit(solution)/shard_map/down_grad/pallas_call | solution.py:480
  305.2 7.3 %gate_up_grad.1 = (bf16[1,1024,768]{2,1,0:T(8,128)(2,1)}, bf16[1,1024,768]{2,1,0:T(8,128)(2,1)}) custom-call(s32[1]{0:T(128)} %bitcast.4._, bf16[256,2176]{1,0:T(8,128)(2,1)} %get-tuple-element.40.mine_ref.lanes_a.refs_0_, bf16[256,2176]{1,0:T(8,128)(2,1)} %copy-done.4, bf16[256,2176]{1,0:T(8,128)(2,1)} %get-tuple-element.51.mine_ref.lanes_a.refs_2_, ...), custom_call_target="tpu_custom_call" | custom-call | flops 3221225472 | bytes 10747904 | tf_op jit(solution)/shard_map/gate_up_grad/pallas_call | solution.py:449
  (62 shorter events, 21.2 us)
Async XLA Ops:
  7.2 46.4 %all-gather.9.cloned.1.call-start = ((), (), s32[]{:S(2)}) async-start(), calls=%async_computation.5 | async-start | bytes 1179648 | tf_op jit(solution)/shard_map/all_gather | solution.py:515
  8.9 87.3 %all-gather.7.cloned.1.call-start = ((), (), s32[]{:S(2)}) async-start(), calls=%async_computation.4 | async-start | bytes 1327104 | tf_op jit(solution)/shard_map/all_gather | solution.py:515
  10.8 135.6 %all-gather.11.cloned.1.call-start = ((), (), s32[]{:S(2)}) async-start(), calls=%async_computation.6 | async-start | bytes 2359296 | tf_op jit(solution)/shard_map/all_gather | solution.py:515
  11.5 301.1 %reduce-scatter.3.cloned.1.call-start = ((), (), s32[]{:S(2)}) async-start(), calls=%async_computation.2 | async-start | bytes 2359296 | tf_op jit(solution)/shard_map/reduce_scatter | solution.py:518
  100.1 3.0 collective-permute-start
  103.1 1.0 copy-start.4
  116.0 2.9 collective-permute-start.1
  119.0 1.0 copy-start.7
  123.1 189.5 %reduce-scatter.5.cloned.1.call-start = ((), (), s32[]{:S(2)}) async-start(), calls=%async_computation.3 | async-start | bytes 2359296 | tf_op jit(solution)/shard_map/reduce_scatter | solution.py:518
  149.6 2.9 collective-permute-start.2
  152.4 1.0 copy-start.5
  169.8 2.9 collective-permute-start.3
  172.7 1.0 copy-start.6
  173.7 3.3 %copy-start.2 = (bf16[512,1152]{1,0:T(8,128)(2,1)S(1)}, bf16[512,1152]{1,0:T(8,128)(2,1)}, u32[]{:S(2)}) copy-start(bf16[512,1152]{1,0:T(8,128)(2,1)} %all-gather.7.cloned.1.call-done) | copy-start | bytes 3538948
  176.9 2.1 copy-start
  177.0 51.4 %collective-permute-start.4 = (bf16[8,64,1152]{2,1,0:T(8,128)(2,1)S(1)}, bf16[8,64,1152]{2,1,0:T(8,128)(2,1)S(1)}, u32[]{:S(2)}, u32[]{:S(2)}) collective-permute-start(bf16[8,64,1152]{2,1,0:T(8,128)(2,1)S(1)} %bitcast.9), channel_id=1, source_target_pairs={{0,1},{1,0},{2,3},{3,2},{4,5},{5,4},{6,7},{7,6},{8,9},{9,8},{10,11... | collective-permute-start | bytes 3538952 | tf_op jit(solution)/shard_map/ppermute | solution.py:526
  178.5 49.8 %collective-permute-start.5 = (bf16[8,64,1024]{2,1,0:T(8,128)(2,1)}, bf16[8,64,1024]{2,1,0:T(8,128)(2,1)S(1)}, u32[]{:S(2)}, u32[]{:S(2)}) collective-permute-start(bf16[8,64,1024]{2,1,0:T(8,128)(2,1)} %bitcast.11), channel_id=1, source_target_pairs={{0,1},{1,0},{2,3},{3,2},{4,5},{5,4},{6,7},{7,6},{8,9},{9,8},{10,11... | collective-permute-start | bytes 3145736 | tf_op jit(solution)/shard_map/ppermute | solution.py:526
  180.5 70.3 %collective-permute-start.7 = (bf16[4,64,2048]{2,1,0:T(8,128)(2,1)}, bf16[4,64,2048]{2,1,0:T(8,128)(2,1)S(1)}, u32[]{:S(2)}, u32[]{:S(2)}) collective-permute-start(bf16[4,64,2048]{2,1,0:T(8,128)(2,1)} %bitcast.5), channel_id=1, source_target_pairs={{0,1},{1,0},{2,3},{3,2},{4,5},{5,4},{6,7},{7,6},{8,9},{9,8},{10,11... | collective-permute-start | bytes 3145736 | tf_op jit(solution)/shard_map/ppermute | solution.py:526
  182.0 90.5 %collective-permute-start.9 = (bf16[4,64,2048]{2,1,0:T(8,128)(2,1)}, bf16[4,64,2048]{2,1,0:T(8,128)(2,1)S(1)}, u32[]{:S(2)}, u32[]{:S(2)}) collective-permute-start(bf16[4,64,2048]{2,1,0:T(8,128)(2,1)} %bitcast.6), channel_id=1, source_target_pairs={{0,1},{1,0},{2,3},{3,2},{4,5},{5,4},{6,7},{7,6},{8,9},{9,8},{10,11... | collective-permute-start | bytes 3145736 | tf_op jit(solution)/shard_map/ppermute | solution.py:526
  229.3 1.0 copy-start.3
  234.2 41.9 %collective-permute-start.6 = (bf16[256,2176]{1,0:T(8,128)(2,1)}, bf16[256,2176]{1,0:T(8,128)(2,1)S(1)}, u32[]{:S(2)}, u32[]{:S(2)}) collective-permute-start(bf16[256,2176]{1,0:T(8,128)(2,1)} %get-tuple-element.52), channel_id=1, source_target_pairs={{0,2},{2,0},{4,6},{6,4},{8,10},{10,8},{12,14},{14,12},{16,18},{18,... | collective-permute-start | bytes 3342344 | tf_op jit(solution)/shard_map/ppermute | solution.py:523
  254.5 31.1 %collective-permute-start.8 = (bf16[128,2048]{1,0:T(8,128)(2,1)}, bf16[128,2048]{1,0:T(8,128)(2,1)S(1)}, u32[]{:S(2)}, u32[]{:S(2)}) collective-permute-start(bf16[128,2048]{1,0:T(8,128)(2,1)} %get-tuple-element.56), channel_id=1, source_target_pairs={{0,2},{2,0},{4,6},{6,4},{8,10},{10,8},{12,14},{14,12},{16,18},{18,... | collective-permute-start | bytes 1572872 | tf_op jit(solution)/shard_map/ppermute | solution.py:523
  276.1 16.5 %collective-permute-start.10 = (bf16[128,2048]{1,0:T(8,128)(2,1)}, bf16[128,2048]{1,0:T(8,128)(2,1)S(1)}, u32[]{:S(2)}, u32[]{:S(2)}) collective-permute-start(bf16[128,2048]{1,0:T(8,128)(2,1)} %get-tuple-element.61), channel_id=1, source_target_pairs={{0,2},{2,0},{4,6},{6,4},{8,10},{10,8},{12,14},{14,12},{16,18},{18,... | collective-permute-start | bytes 1572872 | tf_op jit(solution)/shard_map/ppermute | solution.py:523
  276.2 1.1 copy-start.1
  (5 other events, 4.5 us)
Sparse Core Ops, SparseCore 0:
  10.7 42.8 all-gather.8
  56.3 39.7 all-gather.6
  98.3 48.0 all-gather.10
  150.4 66.1 reduce-scatter.2
  220.5 66.8 reduce-scatter.4

commit v4 on v1

v4 whole, which is shorter than its diff:
```python
import jax
import jax.numpy as jnp
from jax import lax
from jax.experimental import pallas as pl
from jax.experimental.pallas import tpu as pltpu
from jax.sharding import PartitionSpec as P

BF = jnp.bfloat16
F32 = jnp.float32
VMEM = 56 * 1024 * 1024
TOGETHER = 4
LANES = 128
SMALL = pl.CostEstimate(flops=1, bytes_accessed=1, transcendentals=0)


def slots(routes, experts, capacity):
    flat_ids = routes.reshape(-1)
    one_hot = (flat_ids[:, None] == jnp.arange(experts, dtype=jnp.int32)[None, :]).astype(jnp.int32)
    before = jnp.cumsum(one_hot, axis=0) - one_hot
    slot_rank = jnp.sum(before * one_hot, axis=1)
    return flat_ids * capacity + slot_rank


def place(token_rows, positions, total_rows):
    return (
        jnp.zeros((total_rows, token_rows.shape[1]), token_rows.dtype).at[positions].set(token_rows)
    )


def hidden_rows(token_rows, gate_weight, up_weight):
    pre_gate = jnp.dot(token_rows, gate_weight, preferred_element_type=F32)
    pre_up = jnp.dot(token_rows, up_weight, preferred_element_type=F32)
    activation = (jax.nn.silu(pre_gate) * pre_up).astype(BF)
    return (pre_gate, pre_up, activation)


CONTRACT = (((1,), (1,)), ((), ()))


def hidden_grads(grad_rows, pre_gate, pre_up, down_weight):
    d_hidden = lax.dot_general(grad_rows, down_weight, CONTRACT, preferred_element_type=F32)
    sigmoid_gate = jax.nn.sigmoid(pre_gate)
    d_gate = (d_hidden * pre_up * sigmoid_gate * (1.0 + pre_gate * (1.0 - sigmoid_gate))).astype(BF)
    d_up = (d_hidden * pre_gate * sigmoid_gate).astype(BF)
    return d_gate, d_up


def input_rows(d_gate, d_up, gate_weight, up_weight):
    back_rows = lax.dot_general(d_gate, gate_weight, CONTRACT, preferred_element_type=F32)
    back_rows = back_rows + lax.dot_general(d_up, up_weight, CONTRACT, preferred_element_type=F32)
    return back_rows.astype(BF)


def outer_sum(left, right):
    return lax.dot_general(left, right, (((0,), (0,)), ((), ())), preferred_element_type=F32)


def routed_plan(tokens, route_ids, gate_probs, out_cot, w_gate, w_up, w_down):
    experts = lax.axis_size("expert")
    tok_rows, features = tokens.shape
    top_count = route_ids.shape[1]
    hidden = w_gate.shape[2]
    capacity = max(2, tok_rows * top_count * 4 // (3 * experts))
    total_rows = experts * capacity
    positions = slots(route_ids, experts, capacity)
    gate_weight, up_weight, down_weight = w_gate[0], w_up[0], w_down[0]

    def exchange(rows):
        blocks = rows.reshape(experts, capacity, features)
        return lax.all_to_all(blocks, "expert", 0, 0, tiled=True).reshape(-1, features)

    received = exchange(place(jnp.repeat(tokens, top_count, axis=0), positions, total_rows))
    pre_gate, pre_up, activation = hidden_rows(received, gate_weight, up_weight)
    result = jnp.dot(activation, down_weight, preferred_element_type=F32).astype(BF)
    picked = exchange(result)[positions].reshape(tok_rows, top_count, features)
    combined = jnp.einsum("tk,tkd->td", gate_probs, picked.astype(F32)).astype(BF)
    scaled = (gate_probs[:, :, None] * out_cot[:, None, :].astype(F32)).astype(BF)
    grads_in = exchange(place(scaled.reshape(-1, features), positions, total_rows))
    d_gate, d_up = hidden_grads(grads_in, pre_gate, pre_up, down_weight)
    back = exchange(input_rows(d_gate, d_up, gate_weight, up_weight))
    grad_tokens = jnp.sum(
        back[positions].reshape(tok_rows, top_count, features).astype(F32), axis=1
    ).astype(BF)
    gate_up_sum = lax.psum_scatter(
        outer_sum(received, jnp.concatenate([d_gate, d_up], axis=1)).astype(BF),
        "replica",
        scatter_dimension=0,
        tiled=True,
    )
    down_sum = lax.psum_scatter(
        outer_sum(activation, grads_in).astype(BF), "replica", scatter_dimension=0, tiled=True
    )
    return (
        combined,
        grad_tokens,
        gate_up_sum[:, :hidden][None],
        gate_up_sum[:, hidden:][None],
        down_sum[None],
    )

def dot(left, right):
    return jnp.dot(left, right, preferred_element_type=F32)


def whole(array):
    return pl.BlockSpec(array.shape, lambda *_: (0,) * array.ndim)


def params(steps=0):
    order = ("arbitrary",) * steps if steps else None
    return pltpu.CompilerParams(dimension_semantics=order, vmem_limit_bytes=VMEM)


ANYWHERE = pl.BlockSpec(memory_space=pl.ANY)


def landing(chunks):
    tok_rows, width = chunks[0].shape
    return [
        pltpu.VMEM((len(chunks) * tok_rows, width), BF),
        pltpu.SemaphoreType.DMA((len(chunks),)),
    ]


def load(chunk_refs, rows_ref, sems):
    copies = []
    for i, ref in enumerate(chunk_refs):
        size = ref.shape[0]
        copies.append(
            pltpu.make_async_copy(ref, rows_ref.at[i * size : (i + 1) * size], sems.at[i])
        )
        copies[-1].start()
    return copies


def plan_and_pack(expert, experts, capacity, chunks):
    tok_rows, width = chunks[0].shape
    lanes = LANES
    features = width - lanes
    length, room = TOGETHER * tok_rows, TOGETHER * capacity
    groups = len(chunks) // TOGETHER

    def body(expert_ref, *refs):
        mine_ref, theirs_ref, pick_ref, place_ref, rows_ref, sems = refs[len(chunks) :]
        copies = load(refs[: len(chunks)], rows_ref, sems)
        lane = lax.broadcasted_iota(jnp.int32, (length, lanes), 1)
        row = lax.broadcasted_iota(jnp.int32, (length, length), 0)
        col = lax.broadcasted_iota(jnp.int32, (length, length), 1)
        before = (row >= col).astype(BF)
        slot = lax.broadcasted_iota(jnp.int32, (length, 2 * room), 1) % room
        wanted = (slot + 1).astype(F32)
        for group in range(groups):
            for copy in copies[group * TOGETHER : (group + 1) * TOGETHER]:
                copy.wait()
            held_rows = slice(group * length, (group + 1) * length)
            shares = rows_ref[held_rows, features:].astype(F32)
            routed = []
            for index in (expert_ref[0], expert_ref[0] ^ 1):
                held = (lane == index) | (lane == index + experts) | (lane == index + 2 * experts)
                weight = jnp.sum(jnp.where(held, shares, 0.0), axis=1, keepdims=True)
                routed.append(jnp.broadcast_to((weight > 0).astype(F32), (length, room)))
            routed = jnp.concatenate(routed, axis=1)
            rank = dot(before, routed.astype(BF))
            place = jnp.where((rank == wanted) & (routed > 0), 1.0, 0.0)
            place_ref[group] = place.astype(BF)
            pick = place.T.astype(BF)
            pick_ref[group] = pick
            here = slice(group * room, (group + 1) * room)
            for at in range(0, width, 512):
                cols = slice(at, min(at + 512, width))
                packed = dot(pick, rows_ref[held_rows, cols]).astype(BF)
                mine_ref[here, cols] = packed[:room]
                theirs_ref[here, cols] = packed[room:]

    rows = jax.ShapeDtypeStruct((groups * room, width), BF)
    pick = jax.ShapeDtypeStruct((groups, 2 * room, length), BF)
    place = jax.ShapeDtypeStruct((groups, length, 2 * room), BF)
    return pl.pallas_call(
        body,
        grid_spec=pltpu.PrefetchScalarGridSpec(
            num_scalar_prefetch=1,
            grid=(1,),
            in_specs=[ANYWHERE] * len(chunks),
            out_specs=[whole(a) for a in (rows, rows, pick, place)],
            scratch_shapes=landing(chunks),
        ),
        out_shape=(rows, rows, pick, place),
        compiler_params=params(1),
        cost_estimate=SMALL,
        name="plan_and_pack",
    )(expert, *chunks)


def pack(pick, chunks):
    features = chunks[0].shape[1]
    groups, room, length = pick.shape[0], pick.shape[1] // 2, pick.shape[2]

    def body(pick_ref, *refs):
        mine_ref, theirs_ref, rows_ref, sems = refs[-4:]
        copies = load(refs[:-4], rows_ref, sems)
        for group in range(groups):
            for copy in copies[group * TOGETHER : (group + 1) * TOGETHER]:
                copy.wait()
            held_rows = slice(group * length, (group + 1) * length)
            here = slice(group * room, (group + 1) * room)
            for at in range(0, features, 512):
                cols = slice(at, at + 512)
                packed = dot(pick_ref[group], rows_ref[held_rows, cols]).astype(BF)
                mine_ref[here, cols] = packed[:room]
                theirs_ref[here, cols] = packed[room:]

    out = jax.ShapeDtypeStruct((groups * room, features), BF)
    return pl.pallas_call(
        body,
        in_specs=[pl.BlockSpec(memory_space=pltpu.VMEM)] + [ANYWHERE] * len(chunks),
        out_shape=(out, out),
        scratch_shapes=landing(chunks),
        compiler_params=params(),
        cost_estimate=SMALL,
        name="pack",
    )(pick, *chunks)


def spread(place, mine, theirs, parts):
    groups, length, slots_of = place.shape
    room, features = slots_of // 2, mine.shape[1]
    size = groups * length // parts

    def body(place_ref, mine_ref, theirs_ref, *outs):
        for group in reversed(range(groups)):
            here = slice(group * room, (group + 1) * room)
            for at in range(0, features, 512):
                cols = slice(at, at + 512)
                rows = jnp.concatenate([mine_ref[here, cols], theirs_ref[here, cols]], axis=0)
                dense = dot(place_ref[group], rows).astype(BF)
                for i in range(parts // groups):
                    out = outs[group * (parts // groups) + i]
                    out[:, cols] = dense[i * size : (i + 1) * size]

    out = jax.ShapeDtypeStruct((size, features), BF)
    return pl.pallas_call(
        body,
        out_shape=(out,) * parts,
        compiler_params=params(),
        cost_estimate=SMALL,
        name="spread",
    )(place, mine, theirs)


def split3(value):
    high = value.astype(BF)
    rest = value - high.astype(F32)
    mid = rest.astype(BF)
    low = (rest - mid.astype(F32)).astype(BF)
    return high, mid, low


def after(value, *earlier):
    return lax.optimization_barrier((value, *earlier))[0]


def dense_plan(tokens, route_ids, gate_probs, out_cot, w_gate, w_up, w_down):
    experts = lax.axis_size("expert")
    tok_rows, features = tokens.shape
    hidden = w_gate.shape[2]
    top_count = route_ids.shape[1]
    capacity = max(2, tok_rows * top_count * 4 // (3 * experts))
    expert = lax.axis_index("expert").astype(jnp.int32)
    replica = lax.axis_index("replica").astype(jnp.int32)
    w_gate, w_up, w_down = w_gate[0], w_up[0], w_down[0]

    def to_core(rows):
        return lax.ppermute(rows, "expert", [(i, i ^ 1) for i in range(experts)])

    def to_x(rows):
        return lax.ppermute(rows, "expert", [(i, i ^ 2) for i in range(experts)])

    def to_z(rows):
        return lax.ppermute(rows, "expert", [(i, (i + 4) % experts) for i in range(experts)])

    def to_y(rows):
        return lax.ppermute(rows, "replica", [(0, 1), (1, 0)])

    chosen = route_ids[:, :, None] == jnp.arange(experts, dtype=jnp.int32)
    share = jnp.sum(jnp.where(chosen, gate_probs[:, :, None], 0.0), axis=1)
    pad = jnp.zeros((tok_rows, LANES - 3 * experts), BF)

    token_near = [jnp.concatenate([tokens, *split3(share), pad], axis=1)]
    for _ in range(TOGETHER - 1):
        token_near.append(to_z(token_near[-1]))
    token_far = [to_x(a) for a in token_near]
    cot_near = [out_cot, to_z(after(out_cot, token_near[2]))]
    for _ in range(TOGETHER - 2):
        cot_near.append(to_z(cot_near[-1]))
    cot_far = [to_x(a) for a in cot_near]
    relay = [to_y(a) for pair in zip(token_near, token_far) for a in pair]
    relay += [to_y(a) for pair in zip(cot_near, cot_far) for a in pair]
    token_other = relay[0 : 2 * TOGETHER : 2] + relay[1 : 2 * TOGETHER : 2]
    cot_other = relay[2 * TOGETHER :: 2] + relay[2 * TOGETHER + 1 :: 2]

    def join(mine, theirs):
        return jnp.concatenate([mine, to_core(theirs)], axis=0)

    def enter(chunks, *earlier):
        mine, theirs, pick, place = plan_and_pack(
            expert.reshape(1), experts, capacity, chunks
        )
        theirs = after(to_core(theirs), *earlier)
        x = jnp.concatenate([mine[:, :features], theirs[:, :features]], axis=0)
        shares = jnp.concatenate([mine[:, features:], theirs[:, features:]], axis=0)
        held = (jnp.arange(LANES) % experts == expert) & (jnp.arange(LANES) < 3 * experts)
        weight = jnp.sum(jnp.where(held, shares.astype(F32), 0.0), axis=1, keepdims=True)
        pre_gate, pre_up = dot(x, w_gate), dot(x, w_up)
        activation = (jax.nn.silu(pre_gate) * pre_up).astype(BF)
        return x, weight, pick, place, pre_gate, pre_up, activation

    def leave(place, rows_of, *earlier):
        half = place.shape[0] * place.shape[2] // 2
        theirs = after(to_core(rows_of(slice(half, None))), *earlier)
        parts = spread(place, rows_of(slice(0, half)), theirs, 2 * TOGETHER)
        near, far = parts[:TOGETHER], parts[TOGETHER:]
        totals = []
        for s in (*range(1, TOGETHER), 0):
            part = near[s].astype(F32) + to_x(far[s]).astype(F32)
            if totals:
                part = part + to_z(totals[-1]).astype(F32)
            totals.append(part.astype(BF))
        return totals, parts

    def grads(x, activation, cot, d_gate, d_up):
        x = lax.dynamic_slice_in_dim(x, replica * (features // 2), features // 2, 1)
        activation = lax.dynamic_slice_in_dim(activation, replica * (hidden // 2), hidden // 2, 1)
        return outer_sum(x, d_gate), outer_sum(x, d_up), outer_sum(activation, cot)

    chunks = after([*token_near, *token_far], relay[0], relay[1], relay[2], cot_near[1])
    x, weight, pick, place, pre_gate, pre_up, activation = enter(
        chunks, relay[3], cot_near[2], cot_far[0]
    )
    activation = after(activation, relay[4], cot_near[3], cot_far[1])
    totals, sent = leave(
        place,
        lambda rows: (dot(activation[rows], w_down) * weight[rows]).astype(BF),
        relay[5],
        cot_far[2],
    )
    cot_chunks = after([*cot_near, *cot_far], sent, relay[6])
    cot = (join(*pack(pick, cot_chunks)).astype(F32) * weight).astype(BF)
    cot = after(cot, relay[7])
    d_gate, d_up = hidden_grads(cot, pre_gate, pre_up, w_down)
    d_gate, d_up = after((d_gate, d_up), relay[8])
    grad_totals, sent = leave(
        place,
        lambda rows: input_rows(d_gate[rows], d_up[rows], w_gate, w_up),
        relay[9],
        totals[1],
    )
    own = x, activation, cot, d_gate, d_up

    x, weight, pick, _, pre_gate, pre_up, activation = enter(
        after(token_other, sent, relay[10], totals[2]), relay[11], totals[3]
    )
    own = grads(*after(own, activation, relay[12], grad_totals[1]))
    cot_chunks = after(cot_other, own, grad_totals[2])
    cot = (join(*pack(pick, cot_chunks)).astype(F32) * weight).astype(BF)
    d_gate, d_up = hidden_grads(cot, pre_gate, pre_up, w_down)
    other = grads(x, activation, cot, d_gate, d_up)
    grad_gate, grad_up, grad_down = ((a + b).astype(BF)[None] for a, b in zip(own, other))
    return (totals[-1], grad_totals[-1], grad_gate, grad_up, grad_down)


def dense_fits(mesh):
    experts, replicas = mesh.shape["expert"], mesh.shape["replica"]
    return replicas == 2 and experts == 4 * TOGETHER


def solution(mesh):
    placed = (
        P(("expert", "replica"), None),
        P(("expert", "replica"), None),
        P(("expert", "replica"), None),
        P(("expert", "replica"), None),
        P("expert", None, None),
        P("expert", None, None),
        P("expert", None, None),
    )
    return jax.shard_map(
        dense_plan if dense_fits(mesh) else routed_plan,
        mesh=mesh,
        in_specs=placed,
        out_specs=(
            P(("expert", "replica"), None),
            P(("expert", "replica"), None),
            P("expert", "replica", None),
            P("expert", "replica", None),
            P("expert", "replica", None),
        ),
        check_vma=False,
    )
```

time: 262 us -> 236 us (0.901)
  waiting for transfers between devices: 150 us -> 108 us
  starting transfers between devices: 1.58 us -> 37.1 us
  Pallas kernels: 0 us -> 24.3 us
  local copies, waits for them, and re-layouts: 32.9 us -> 11.3 us
  between operations: 14.4 us -> 1.38 us
  other arithmetic: 20.3 us -> 14.2 us
  matrix products: 42.6 us -> 38.9 us
    all_gather x1 -> x0, waiting for transfers between devices: 79.7 us -> none  [dense_plan(): own = lax.all_gather(payload, 'expert', axis=0, tiled=False)]
    ppermute x2 -> x50, waiting for transfers between devices: 69.9 us -> 108 us  [the longest x12 50.6 us: to_z(): lax.ppermute(rows, 'expert', [(i, (i + 4) % experts) for i in range(exper...]
    ppermute x2 -> x50, starting transfers between devices: 1.5 us -> 37.1 us  [the longest x16 17.8 us: to_x(): return lax.ppermute(rows, 'expert', [(i, i ^ 2) for i in range(experts)])]
    pallas_call x0 -> x6, Pallas kernels: none -> 24.3 us  [the longest x2 8.76 us: plan_and_pack(): pl.pallas_call(body, grid_spec=pltpu.PrefetchScalarGridSpec(num_scalar_pr...]
    dot_general x9 -> x6, matrix products: 26.3 us -> 12.8 us  [dot(): return jnp.dot(left, right, preferred_element_type=F32)]
    another operation x5 -> x0, other arithmetic: 10.4 us -> none  [the longest x1 7.91 us: dense_plan(): jnp.stack([relay, sibling], axis=1).reshape(experts, tok_rows, width)]
    convert_element_type x4 -> x10, other arithmetic: 0.58 us -> 10.3 us  [the longest x8 8.22 us: leave(): totals.append(part.astype(BF))]
    another operation x7 -> x0, local copies, waits for them, and re-layouts: 8.3 us -> none  [the longest x1 7.92 us: dense_plan(): jnp.stack([relay, sibling], axis=1).reshape(experts, tok_rows, width)]
  transfers between devices with their start and end apart: 4 -> 50, of which waited for: 3 -> 24; matrix products, arithmetic and copies ran while one was open for 28% -> 18% of each run, Pallas kernels for 0% -> 5%
where the time goes in v4:
time: 236 us; the launch traced here: 235 us
  waiting for transfers between devices  108 us (46%)
  matrix products  38.9 us (16%)
  starting transfers between devices  37.1 us (16%)
  Pallas kernels  24.3 us (10%)
  other arithmetic  14.2 us (6%)
  local copies, waits for them, and re-layouts  11.3 us (5%)
    ppermute x12, waiting for transfers between devices, to_z(): lax.ppermute(rows, 'expert', [(i, (i + 4) % experts) for i in range(exper...  50.6 us
    ppermute x16, waiting for transfers between devices, to_x(): return lax.ppermute(rows, 'expert', [(i, i ^ 2) for i in range(experts)])  32.9 us
    ppermute x16, waiting for transfers between devices, to_y(): return lax.ppermute(rows, 'replica', [(0, 1), (1, 0)])  24.3 us
    ppermute x16, starting transfers between devices, to_x(): return lax.ppermute(rows, 'expert', [(i, i ^ 2) for i in range(experts)])  17.8 us
    ppermute x16, starting transfers between devices, to_y(): return lax.ppermute(rows, 'replica', [(0, 1), (1, 0)])  15.6 us
    dot_general x6, matrix products, outer_sum(): lax.dot_general(left, right, (((0,), (0,)), ((), ())), preferred_element_...  13.2 us
    dot_general x6, matrix products, dot(): return jnp.dot(left, right, preferred_element_type=F32)  12.8 us
    pallas_call x2, Pallas kernels, plan_and_pack(): pl.pallas_call(body, grid_spec=pltpu.PrefetchScalarGridSpec(num_scalar_pr...  8.76 us
  transfers between devices with their start and end apart: 50, of which 24 were waited for; matrix products, arithmetic and copies ran while one was open for 18% of the time, Pallas kernels for 5%

profile of v4, /device:TPU:0, one launch (start us, length us, event | category | flops | bytes accessed | tf_op | source)
XLA Modules:
  0.0 235.1 jit_solution(7430929831105458163)
XLA Ops:
  5.9 8.8 %collective-permute-done.refs_1_ = bf16[64,2176]{1,0:T(8,128)(2,1)} collective-permute-done((bf16[64,2176]{1,0:T(8,128)(2,1)S(1)}, bf16[64,2176]{1,0:T(8,128)(2,1)}, u32[]{:S(2)}, u32[]{:S(2)}) %collective-permute-start) | collective-permute-done | bytes 278560 | tf_op jit(solution)/shard_map/ppermute | solution.py:279
  17.7 6.9 %collective-permute-done.1.refs_2_ = bf16[64,2176]{1,0:T(8,128)(2,1)} collective-permute-done((bf16[64,2176]{1,0:T(8,128)(2,1)}, bf16[64,2176]{1,0:T(8,128)(2,1)}, u32[]{:S(2)}, u32[]{:S(2)}) %collective-permute-start.1) | collective-permute-done | bytes 278560 | tf_op jit(solution)/shard_map/ppermute | solution.py:279
  29.5 4.2 %collective-permute-done.2.refs_3_ = bf16[64,2176]{1,0:T(8,128)(2,1)} collective-permute-done((bf16[64,2176]{1,0:T(8,128)(2,1)}, bf16[64,2176]{1,0:T(8,128)(2,1)}, u32[]{:S(2)}, u32[]{:S(2)}) %collective-permute-start.2) | collective-permute-done | bytes 278560 | tf_op jit(solution)/shard_map/ppermute | solution.py:279
  37.7 5.4 %collective-permute-done.10.refs_1_ = bf16[64,2048]{1,0:T(8,128)(2,1)} collective-permute-done((bf16[64,2048]{1,0:T(8,128)(2,1)}, bf16[64,2048]{1,0:T(8,128)(2,1)}, u32[]{:S(2)}, u32[]{:S(2)}) %collective-permute-start.10) | collective-permute-done | bytes 262176 | tf_op jit(solution)/shard_map/ppermute | solution.py:279
  45.4 4.4 %plan_and_pack.2 = (bf16[256,2176]{1,0:T(8,128)(2,1)}, bf16[256,2176]{1,0:T(8,128)(2,1)}, bf16[2,256,256]{2,1,0:T(8,128)(2,1)}, bf16[2,256,256]{2,1,0:T(8,128)(2,1)}) custom-call(s32[1]{0:T(128)} %bitcast.expert_ref, bf16[64,2176]{1,0:T(8,128)(2,1)} %copy-done.9, bf16[64,2176]{1,0:T(8,128)(2,1)} %collective-permute-done.refs_1_, ...), custom_call_target="tpu_custom_call" | custom-call | flops 1 | bytes 1 | tf_op jit(solution)/shard_map/plan_and_pack/pallas_call | solution.py:178
  55.3 4.3 %collective-permute-done.14.refs_4_ = bf16[64,2048]{1,0:T(8,128)(2,1)} collective-permute-done((bf16[64,2048]{1,0:T(8,128)(2,1)}, bf16[64,2048]{1,0:T(8,128)(2,1)}, u32[]{:S(2)}, u32[]{:S(2)}) %collective-permute-start.14) | collective-permute-done | bytes 262176 | tf_op jit(solution)/shard_map/ppermute | solution.py:276
  68.5 3.4 %collective-permute-done.16.refs_3_ = bf16[64,2048]{1,0:T(8,128)(2,1)S(1)} collective-permute-done((bf16[64,2048]{1,0:T(8,128)(2,1)}, bf16[64,2048]{1,0:T(8,128)(2,1)S(1)}, u32[]{:S(2)}, u32[]{:S(2)}) %collective-permute-start.16) | collective-permute-done | bytes 262176 | tf_op jit(solution)/shard_map/ppermute | solution.py:279
  79.1 3.6 %collective-permute-done.19.refs_6_ = bf16[64,2176]{1,0:T(8,128)(2,1)S(1)} collective-permute-done((bf16[64,2176]{1,0:T(8,128)(2,1)}, bf16[64,2176]{1,0:T(8,128)(2,1)S(1)}, u32[]{:S(2)}, u32[]{:S(2)}) %collective-permute-start.19) | collective-permute-done | bytes 278560 | tf_op jit(solution)/shard_map/ppermute | solution.py:282
  85.4 3.4 %spread.2 = (bf16[64,2048]{1,0:T(8,128)(2,1)}, bf16[64,2048]{1,0:T(8,128)(2,1)}, bf16[64,2048]{1,0:T(8,128)(2,1)}, bf16[64,2048]{1,0:T(8,128)(2,1)}, bf16[64,204...) custom-call(bf16[2,256,256]{2,1,0:T(8,128)(2,1)} %get-tuple-element.87.place_ref,, ...), custom_call_target="tpu_custom_call" | custom-call | flops 1 | bytes 1 | tf_op jit(solution)/shard_map/spread/pallas_call | solution.py:241
  89.7 4.4 %pack.2 = (bf16[256,2048]{1,0:T(8,128)(2,1)}, bf16[256,2048]{1,0:T(8,128)(2,1)}) custom-call(bf16[2,256,256]{2,1,0:T(8,128)(2,1)} %get-tuple-element.101.pick_ref, bf16[64,2048]{1,0:T(8,128)(2,1)} %refs_0_, bf16[64,2048]{1,0:T(8,128)(2,1)} %collective-permute-done.10.refs_1_, bf16[64,2048]{1,0:T(8,128)(2,1)} %collective-permute-done.13.refs_2_, ...), custom_call_target="tpu_custom_call" | custom-call | flops 1 | bytes 1 | tf_op jit(solution)/shard_map/pack/pallas_call | solution.py:213
  97.8 5.4 %collective-permute-done.24 = bf16[64,2048]{1,0:T(8,128)(2,1)} collective-permute-done((bf16[64,2048]{1,0:T(8,128)(2,1)}, bf16[64,2048]{1,0:T(8,128)(2,1)}, u32[]{:S(2)}, u32[]{:S(2)}) %collective-permute-start.24) | collective-permute-done | bytes 262176 | tf_op jit(solution)/shard_map/ppermute | solution.py:276
  108.5 17.6 %collective-permute-done.31.refs_7_ = bf16[64,2176]{1,0:T(8,128)(2,1)S(1)} collective-permute-done((bf16[64,2176]{1,0:T(8,128)(2,1)}, bf16[64,2176]{1,0:T(8,128)(2,1)S(1)}, u32[]{:S(2)}, u32[]{:S(2)}) %collective-permute-start.31) | collective-permute-done | bytes 278560 | tf_op jit(solution)/shard_map/ppermute | solution.py:282
  127.7 3.6 %multiply_convert_fusion.5 = (bf16[512,768]{1,0:T(8,128)(2,1)S(1)}, bf16[512,768]{1,0:T(8,128)(2,1)S(1)}) fusion(f32[512,768]{1,0:T(8,128)S(1)} %copy-done.56, f32[512,768]{1,0:T(8,128)} %get-tuple-element.158, bf16[512,2048]{1,0:T(8,128)(2,1)S(1)} %multiply_convert_fusion.1, bf16[1,768,2048]{2,1,0:T(8,128)(2,1)S(1)} %copy-done.47), kind=kOutput, calls=%fused_computation.46 | convolution fusion | flops 1615724544 | bytes 9961472 | tf_op jit(solution)/shard_map/dot_general | solution.py:41
  135.1 5.5 %collective-permute-done.25 = bf16[64,2048]{1,0:T(8,128)(2,1)S(1)} collective-permute-done((bf16[64,2048]{1,0:T(8,128)(2,1)S(1)}, bf16[64,2048]{1,0:T(8,128)(2,1)S(1)}, u32[]{:S(2)}, u32[]{:S(2)}) %collective-permute-start.25) | collective-permute-done | bytes 262176 | tf_op jit(solution)/shard_map/ppermute | solution.py:279
  144.5 3.4 %spread.3 = (bf16[64,2048]{1,0:T(8,128)(2,1)}, bf16[64,2048]{1,0:T(8,128)(2,1)}, bf16[64,2048]{1,0:T(8,128)(2,1)}, bf16[64,2048]{1,0:T(8,128)(2,1)}, bf16[64,204...) custom-call(bf16[2,256,256]{2,1,0:T(8,128)(2,1)} %get-tuple-element.87.place_ref,, ...), custom_call_target="tpu_custom_call" | custom-call | flops 1 | bytes 1 | tf_op jit(solution)/shard_map/spread/pallas_call | solution.py:241
  152.8 4.5 %collective-permute-done.38 = bf16[64,2048]{1,0:T(8,128)(2,1)S(1)} collective-permute-done((bf16[64,2048]{1,0:T(8,128)(2,1)}, bf16[64,2048]{1,0:T(8,128)(2,1)S(1)}, u32[]{:S(2)}, u32[]{:S(2)}) %collective-permute-start.38) | collective-permute-done | bytes 262176 | tf_op jit(solution)/shard_map/ppermute | solution.py:276
  158.1 4.5 %collective-permute-done.22 = bf16[64,2048]{1,0:T(8,128)(2,1)S(1)} collective-permute-done((bf16[64,2048]{1,0:T(8,128)(2,1)S(1)}, bf16[64,2048]{1,0:T(8,128)(2,1)S(1)}, u32[]{:S(2)}, u32[]{:S(2)}) %collective-permute-start.22) | collective-permute-done | bytes 262176 | tf_op jit(solution)/shard_map/ppermute | solution.py:276
  168.5 4.4 %plan_and_pack.3 = (bf16[256,2176]{1,0:T(8,128)(2,1)}, bf16[256,2176]{1,0:T(8,128)(2,1)}, bf16[2,256,256]{2,1,0:T(8,128)(2,1)}, bf16[2,256,256]{2,1,0:T(8,128)(2,1)}) custom-call(s32[1]{0:T(128)} %bitcast.expert_ref, bf16[64,2176]{1,0:T(8,128)(2,1)} %copy-done.20, bf16[64,2176]{1,0:T(8,128)(2,1)} %collective-permute-done.9.refs_1_, ...), custom_call_target="tpu_custom_call" | custom-call | flops 1 | bytes 1 | tf_op jit(solution)/shard_map/plan_and_pack/pallas_call | solution.py:178
  177.8 3.6 %collective-permute-done.27 = bf16[64,2048]{1,0:T(8,128)(2,1)S(1)} collective-permute-done((bf16[64,2048]{1,0:T(8,128)(2,1)}, bf16[64,2048]{1,0:T(8,128)(2,1)S(1)}, u32[]{:S(2)}, u32[]{:S(2)}) %collective-permute-start.27) | collective-permute-done | bytes 262176 | tf_op jit(solution)/shard_map/ppermute | solution.py:279
  186.2 3.3 %collective-permute-done.40 = bf16[64,2048]{1,0:T(8,128)(2,1)S(1)} collective-permute-done((bf16[64,2048]{1,0:T(8,128)(2,1)S(1)}, bf16[64,2048]{1,0:T(8,128)(2,1)S(1)}, u32[]{:S(2)}, u32[]{:S(2)}) %collective-permute-start.40) | collective-permute-done | bytes 262176 | tf_op jit(solution)/shard_map/ppermute | solution.py:279
  195.3 3.2 %multiply_convert_fusion.4 = (bf16[512,768]{1,0:T(8,128)(2,1)}, f32[512,768]{1,0:T(8,128)}) fusion(f32[512,768]{1,0:T(8,128)S(1)} %fusion.16, bf16[1,2048,768]{2,1,0:T(8,128)(2,1)S(1)} %copy-done, bf16[256,2048]{1,0:T(8,128)(2,1)S(1)} %slice.63, bf16[256,2048]{1,0:T(8,128)(2,1)S(1)} %slice.62), kind=kOutput, calls=%fused_computation.44 | convolution fusion | flops 1617166336 | bytes 9175040 | tf_op jit(solution)/shard_map/dot_general | solution.py:102
  206.6 4.4 %pack.3 = (bf16[256,2048]{1,0:T(8,128)(2,1)}, bf16[256,2048]{1,0:T(8,128)(2,1)}) custom-call(bf16[2,256,256]{2,1,0:T(8,128)(2,1)} %get-tuple-element.137.pick_ref, bf16[64,2048]{1,0:T(8,128)(2,1)} %collective-permute-done.32.refs_0_, bf16[64,2048]{1,0:T(8,128)(2,1)} %collective-permute-done.42.refs_1_, bf16[64,2048]{1,0:T(8,128)(2,1)} %collective-permute-done.45.refs_2_, ...), custom_call_target="tpu_custom_call" | custom-call | flops 1 | bytes 1 | tf_op jit(solution)/shard_map/pack/pallas_call | solution.py:213
  212.2 7.8 %collective-permute-done.35 = bf16[64,2048]{1,0:T(8,128)(2,1)S(1)} collective-permute-done((bf16[64,2048]{1,0:T(8,128)(2,1)}, bf16[64,2048]{1,0:T(8,128)(2,1)S(1)}, u32[]{:S(2)}, u32[]{:S(2)}) %collective-permute-start.35) | collective-permute-done | bytes 262176 | tf_op jit(solution)/shard_map/ppermute | solution.py:276
  223.4 4.2 %fusion = f32[512,768]{1,0:T(8,128)S(1)} fusion(bf16[1,768,2048]{2,1,0:T(8,128)(2,1)} %param.13, bf16[256,2048]{1,0:T(8,128)(2,1)S(1)} %collective-permute-done.49, bf16[256,2048]{1,0:T(8,128)(2,1)} %get-tuple-element.149, f32[512]{0:T(512)S(1)} %select_reduce_fusion), kind=kOutput, calls=%fused_computation.2 | convolution fusion | flops 1616904192 | bytes 6817792 | tf_op jit(solution)/shard_map/dot_general | solution.py:41
  (244 shorter events, 109.6 us)
Async XLA Ops:
  2.8 11.9 %collective-permute-start = (bf16[64,2176]{1,0:T(8,128)(2,1)S(1)}, bf16[64,2176]{1,0:T(8,128)(2,1)}, u32[]{:S(2)}, u32[]{:S(2)}) collective-permute-start(bf16[64,2176]{1,0:T(8,128)(2,1)S(1)} %concatenate.21.refs_0_), channel_id=1, source_target_pairs={{0,8},{2,10},{4,12},{6,14},{8,16},{10,18},{12,20},{14,22},{16,24},... | collective-permute-start | bytes 835592 | tf_op jit(solution)/shard_map/ppermute | solution.py:279
  16.2 11.8 %collective-permute-start.7 = (bf16[64,2176]{1,0:T(8,128)(2,1)S(1)}, bf16[64,2176]{1,0:T(8,128)(2,1)S(1)}, u32[]{:S(2)}, u32[]{:S(2)}) collective-permute-start(bf16[64,2176]{1,0:T(8,128)(2,1)S(1)} %concatenate.21.refs_0_), channel_id=1, source_target_pairs={{0,1},{1,0},{2,3},{3,2},{4,5},{5,4},{6,7},{7,6},{8,9},{9,8},{10,11... | collective-permute-start | bytes 835592 | tf_op jit(solution)/shard_map/ppermute | solution.py:282
  26.0 11.7 %collective-permute-start.9 = (bf16[64,2176]{1,0:T(8,128)(2,1)}, bf16[64,2176]{1,0:T(8,128)(2,1)}, u32[]{:S(2)}, u32[]{:S(2)}) collective-permute-start(bf16[64,2176]{1,0:T(8,128)(2,1)} %collective-permute-done.refs_1_), channel_id=1, source_target_pairs={{0,1},{1,0},{2,3},{3,2},{4,5},{5,4},{6,7},{7,6},{8,9},{9,8},{10,11... | collective-permute-start | bytes 835592 | tf_op jit(solution)/shard_map/ppermute | solution.py:282
  26.7 11.0 %collective-permute-start.4 = (bf16[64,2176]{1,0:T(8,128)(2,1)}, bf16[64,2176]{1,0:T(8,128)(2,1)}, u32[]{:S(2)}, u32[]{:S(2)}) collective-permute-start(bf16[64,2176]{1,0:T(8,128)(2,1)} %collective-permute-done.refs_1_), channel_id=1, source_target_pairs={{0,4},{2,6},{4,0},{6,2},{8,12},{10,14},{12,8},{14,10},{16,20},{18,... | collective-permute-start | bytes 835592 | tf_op jit(solution)/shard_map/ppermute | solution.py:276
  28.7 14.5 %collective-permute-start.5 = (bf16[64,2176]{1,0:T(8,128)(2,1)}, bf16[64,2176]{1,0:T(8,128)(2,1)}, u32[]{:S(2)}, u32[]{:S(2)}) collective-permute-start(bf16[64,2176]{1,0:T(8,128)(2,1)} %collective-permute-done.1.refs_2_), channel_id=1, source_target_pairs={{0,4},{2,6},{4,0},{6,2},{8,12},{10,14},{12,8},{14,10},{16,20},{18,... | collective-permute-start | bytes 835592 | tf_op jit(solution)/shard_map/ppermute | solution.py:276
  33.7 11.7 %collective-permute-start.6 = (bf16[64,2176]{1,0:T(8,128)(2,1)}, bf16[64,2176]{1,0:T(8,128)(2,1)}, u32[]{:S(2)}, u32[]{:S(2)}) collective-permute-start(bf16[64,2176]{1,0:T(8,128)(2,1)} %collective-permute-done.2.refs_3_), channel_id=1, source_target_pairs={{0,4},{2,6},{4,0},{6,2},{8,12},{10,14},{12,8},{14,10},{16,20},{18,... | collective-permute-start | bytes 835592 | tf_op jit(solution)/shard_map/ppermute | solution.py:276
  49.7 12.9 %collective-permute-start.11 = (bf16[256,2176]{1,0:T(8,128)(2,1)}, bf16[256,2176]{1,0:T(8,128)(2,1)S(1)}, u32[]{:S(2)}, u32[]{:S(2)}) collective-permute-start(bf16[256,2176]{1,0:T(8,128)(2,1)} %get-tuple-element.89), channel_id=1, source_target_pairs={{0,2},{2,0},{4,6},{6,4},{8,10},{10,8},{12,14},{14,12},{16,18},{18,... | collective-permute-start | bytes 3342344 | tf_op jit(solution)/shard_map/ppermute | solution.py:273
  49.8 12.8 %collective-permute-start.12 = (bf16[64,2176]{1,0:T(8,128)(2,1)}, bf16[64,2176]{1,0:T(8,128)(2,1)S(1)}, u32[]{:S(2)}, u32[]{:S(2)}) collective-permute-start(bf16[64,2176]{1,0:T(8,128)(2,1)} %collective-permute-done.4.refs_5_), channel_id=1, source_target_pairs={{0,1},{1,0},{2,3},{3,2},{4,5},{5,4},{6,7},{7,6},{8,9},{9,8},{10,11... | collective-permute-start | bytes 835592 | tf_op jit(solution)/shard_map/ppermute | solution.py:282
  52.4 16.1 %collective-permute-start.15 = (bf16[64,2176]{1,0:T(8,128)(2,1)}, bf16[64,2176]{1,0:T(8,128)(2,1)S(1)}, u32[]{:S(2)}, u32[]{:S(2)}) collective-permute-start(bf16[64,2176]{1,0:T(8,128)(2,1)} %collective-permute-done.1.refs_2_), channel_id=1, source_target_pairs={{0,1},{1,0},{2,3},{3,2},{4,5},{5,4},{6,7},{7,6},{8,9},{9,8},{10,11... | collective-permute-start | bytes 835592 | tf_op jit(solution)/shard_map/ppermute | solution.py:282
  72.9 11.6 %collective-permute-start.18 = (bf16[256,2048]{1,0:T(8,128)(2,1)S(1)}, bf16[256,2048]{1,0:T(8,128)(2,1)S(1)}, u32[]{:S(2)}, u32[]{:S(2)}) collective-permute-start(bf16[256,2048]{1,0:T(8,128)(2,1)S(1)} %fusion.37), channel_id=1, source_target_pairs={{0,2},{2,0},{4,6},{6,4},{8,10},{10,8},{12,14},{14,12},{16,18},{18,... | collective-permute-start | bytes 3145736 | tf_op jit(solution)/shard_map/ppermute | solution.py:273
  73.5 15.3 %collective-permute-start.29 = (bf16[64,2176]{1,0:T(8,128)(2,1)}, bf16[64,2176]{1,0:T(8,128)(2,1)}, u32[]{:S(2)}, u32[]{:S(2)}) collective-permute-start(bf16[64,2176]{1,0:T(8,128)(2,1)} %collective-permute-done.2.refs_3_), channel_id=1, source_target_pairs={{0,1},{1,0},{2,3},{3,2},{4,5},{5,4},{6,7},{7,6},{8,9},{9,8},{10,11... | collective-permute-start | bytes 835592 | tf_op jit(solution)/shard_map/ppermute | solution.py:282
  75.6 13.4 %collective-permute-start.28 = (bf16[64,2048]{1,0:T(8,128)(2,1)S(1)}, bf16[64,2048]{1,0:T(8,128)(2,1)S(1)}, u32[]{:S(2)}, u32[]{:S(2)}) collective-permute-start(bf16[64,2048]{1,0:T(8,128)(2,1)S(1)} %collective-permute-done.16.refs_3_), channel_id=1, source_target_pairs={{0,4},{2,6},{4,0},{6,2},{8,12},{10,14},{12,8},{14,10},{16,20},{18,... | collective-permute-start | bytes 786440 | tf_op jit(solution)/shard_map/ppermute | solution.py:276
  94.1 10.8 %collective-permute-start.30 = (bf16[256,2048]{1,0:T(8,128)(2,1)}, bf16[256,2048]{1,0:T(8,128)(2,1)}, u32[]{:S(2)}, u32[]{:S(2)}) collective-permute-start(bf16[256,2048]{1,0:T(8,128)(2,1)} %get-tuple-element.111), channel_id=1, source_target_pairs={{0,2},{2,0},{4,6},{6,4},{8,10},{10,8},{12,14},{14,12},{16,18},{18,... | collective-permute-start | bytes 3145736 | tf_op jit(solution)/shard_map/ppermute | solution.py:273
  94.8 36.5 %collective-permute-start.32 = (bf16[64,2048]{1,0:T(8,128)(2,1)}, bf16[64,2048]{1,0:T(8,128)(2,1)}, u32[]{:S(2)}, u32[]{:S(2)}) collective-permute-start(bf16[64,2048]{1,0:T(8,128)(2,1)} %refs_0_), channel_id=1, source_target_pairs={{0,1},{1,0},{2,3},{3,2},{4,5},{5,4},{6,7},{7,6},{8,9},{9,8},{10,11... | collective-permute-start | bytes 786440 | tf_op jit(solution)/shard_map/ppermute | solution.py:282
  95.7 48.7 %collective-permute-start.34 = (bf16[64,2048]{1,0:T(8,128)(2,1)}, bf16[64,2048]{1,0:T(8,128)(2,1)}, u32[]{:S(2)}, u32[]{:S(2)}) collective-permute-start(bf16[64,2048]{1,0:T(8,128)(2,1)} %collective-permute-done.14.refs_4_), channel_id=1, source_target_pairs={{0,1},{1,0},{2,3},{3,2},{4,5},{5,4},{6,7},{7,6},{8,9},{9,8},{10,11... | collective-permute-start | bytes 786440 | tf_op jit(solution)/shard_map/ppermute | solution.py:282
  96.8 70.7 %collective-permute-start.42 = (bf16[64,2048]{1,0:T(8,128)(2,1)}, bf16[64,2048]{1,0:T(8,128)(2,1)}, u32[]{:S(2)}, u32[]{:S(2)}) collective-permute-start(bf16[64,2048]{1,0:T(8,128)(2,1)} %collective-permute-done.10.refs_1_), channel_id=1, source_target_pairs={{0,1},{1,0},{2,3},{3,2},{4,5},{5,4},{6,7},{7,6},{8,9},{9,8},{10,11... | collective-permute-start | bytes 786440 | tf_op jit(solution)/shard_map/ppermute | solution.py:282
  103.2 87.7 %collective-permute-start.44 = (bf16[64,2048]{1,0:T(8,128)(2,1)}, bf16[64,2048]{1,0:T(8,128)(2,1)}, u32[]{:S(2)}, u32[]{:S(2)}) collective-permute-start(bf16[64,2048]{1,0:T(8,128)(2,1)} %collective-permute-done.17.refs_5_), channel_id=1, source_target_pairs={{0,1},{1,0},{2,3},{3,2},{4,5},{5,4},{6,7},{7,6},{8,9},{9,8},{10,11... | collective-permute-start | bytes 786440 | tf_op jit(solution)/shard_map/ppermute | solution.py:282
  104.8 21.3 %collective-permute-start.31 = (bf16[64,2176]{1,0:T(8,128)(2,1)}, bf16[64,2176]{1,0:T(8,128)(2,1)S(1)}, u32[]{:S(2)}, u32[]{:S(2)}) collective-permute-start(bf16[64,2176]{1,0:T(8,128)(2,1)} %collective-permute-done.6.refs_7_), channel_id=1, source_target_pairs={{0,1},{1,0},{2,3},{3,2},{4,5},{5,4},{6,7},{7,6},{8,9},{9,8},{10,11... | collective-permute-start | bytes 835592 | tf_op jit(solution)/shard_map/ppermute | solution.py:282
  134.5 64.0 %collective-permute-start.45 = (bf16[64,2048]{1,0:T(8,128)(2,1)}, bf16[64,2048]{1,0:T(8,128)(2,1)}, u32[]{:S(2)}, u32[]{:S(2)}) collective-permute-start(bf16[64,2048]{1,0:T(8,128)(2,1)} %collective-permute-done.13.refs_2_), channel_id=1, source_target_pairs={{0,1},{1,0},{2,3},{3,2},{4,5},{5,4},{6,7},{7,6},{8,9},{9,8},{10,11... | collective-permute-start | bytes 786440 | tf_op jit(solution)/shard_map/ppermute | solution.py:282
  175.4 16.9 %collective-permute-start.43 = (bf16[256,2176]{1,0:T(8,128)(2,1)}, bf16[256,2176]{1,0:T(8,128)(2,1)S(1)}, u32[]{:S(2)}, u32[]{:S(2)}) collective-permute-start(bf16[256,2176]{1,0:T(8,128)(2,1)} %get-tuple-element.133), channel_id=1, source_target_pairs={{0,2},{2,0},{4,6},{6,4},{8,10},{10,8},{12,14},{14,12},{16,18},{18,... | collective-permute-start | bytes 3342344 | tf_op jit(solution)/shard_map/ppermute | solution.py:273
  185.7 19.4 %collective-permute-start.47 = (bf16[64,2048]{1,0:T(8,128)(2,1)S(1)}, bf16[64,2048]{1,0:T(8,128)(2,1)S(1)}, u32[]{:S(2)}, u32[]{:S(2)}) collective-permute-start(bf16[64,2048]{1,0:T(8,128)(2,1)S(1)} %copy-done.31), channel_id=1, source_target_pairs={{0,1},{1,0},{2,3},{3,2},{4,5},{5,4},{6,7},{7,6},{8,9},{9,8},{10,11... | collective-permute-start | bytes 786440 | tf_op jit(solution)/shard_map/ppermute | solution.py:282
  189.5 15.6 %collective-permute-start.46 = (bf16[64,2048]{1,0:T(8,128)(2,1)S(1)}, bf16[64,2048]{1,0:T(8,128)(2,1)S(1)}, u32[]{:S(2)}, u32[]{:S(2)}) collective-permute-start(bf16[64,2048]{1,0:T(8,128)(2,1)S(1)} %copy-done.27), channel_id=1, source_target_pairs={{0,1},{1,0},{2,3},{3,2},{4,5},{5,4},{6,7},{7,6},{8,9},{9,8},{10,11... | collective-permute-start | bytes 786440 | tf_op jit(solution)/shard_map/ppermute | solution.py:282
  190.9 14.3 %collective-permute-start.48 = (bf16[64,2048]{1,0:T(8,128)(2,1)S(1)}, bf16[64,2048]{1,0:T(8,128)(2,1)S(1)}, u32[]{:S(2)}, u32[]{:S(2)}) collective-permute-start(bf16[64,2048]{1,0:T(8,128)(2,1)S(1)} %copy-done.29), channel_id=1, source_target_pairs={{0,1},{1,0},{2,3},{3,2},{4,5},{5,4},{6,7},{7,6},{8,9},{9,8},{10,11... | collective-permute-start | bytes 786440 | tf_op jit(solution)/shard_map/ppermute | solution.py:282
  211.0 12.3 %collective-permute-start.49 = (bf16[256,2048]{1,0:T(8,128)(2,1)}, bf16[256,2048]{1,0:T(8,128)(2,1)S(1)}, u32[]{:S(2)}, u32[]{:S(2)}) collective-permute-start(bf16[256,2048]{1,0:T(8,128)(2,1)} %get-tuple-element.150), channel_id=1, source_target_pairs={{0,2},{2,0},{4,6},{6,4},{8,10},{10,8},{12,14},{14,12},{16,18},{18,... | collective-permute-start | bytes 3145736 | tf_op jit(solution)/shard_map/ppermute | solution.py:273
  (84 other events, 738.1 us)

commit v5 on v4

v5 whole, which is shorter than its diff:
```python
import jax
import jax.numpy as jnp
from jax import lax
from jax.experimental import pallas as pl
from jax.experimental.pallas import tpu as pltpu
from jax.sharding import PartitionSpec as P

BF = jnp.bfloat16
F32 = jnp.float32
VMEM = 56 * 1024 * 1024
TOGETHER = 4
LANES = 128
SMALL = pl.CostEstimate(flops=1, bytes_accessed=1, transcendentals=0)


def slots(routes, experts, capacity):
    flat_ids = routes.reshape(-1)
    one_hot = (flat_ids[:, None] == jnp.arange(experts, dtype=jnp.int32)[None, :]).astype(jnp.int32)
    before = jnp.cumsum(one_hot, axis=0) - one_hot
    slot_rank = jnp.sum(before * one_hot, axis=1)
    return flat_ids * capacity + slot_rank


def place(token_rows, positions, total_rows):
    return (
        jnp.zeros((total_rows, token_rows.shape[1]), token_rows.dtype).at[positions].set(token_rows)
    )


def hidden_rows(token_rows, gate_weight, up_weight):
    pre_gate = jnp.dot(token_rows, gate_weight, preferred_element_type=F32)
    pre_up = jnp.dot(token_rows, up_weight, preferred_element_type=F32)
    activation = (jax.nn.silu(pre_gate) * pre_up).astype(BF)
    return (pre_gate, pre_up, activation)


CONTRACT = (((1,), (1,)), ((), ()))


def hidden_grads(grad_rows, pre_gate, pre_up, down_weight):
    d_hidden = lax.dot_general(grad_rows, down_weight, CONTRACT, preferred_element_type=F32)
    sigmoid_gate = jax.nn.sigmoid(pre_gate)
    d_gate = (d_hidden * pre_up * sigmoid_gate * (1.0 + pre_gate * (1.0 - sigmoid_gate))).astype(BF)
    d_up = (d_hidden * pre_gate * sigmoid_gate).astype(BF)
    return d_gate, d_up


def input_rows(d_gate, d_up, gate_weight, up_weight):
    back_rows = lax.dot_general(d_gate, gate_weight, CONTRACT, preferred_element_type=F32)
    back_rows = back_rows + lax.dot_general(d_up, up_weight, CONTRACT, preferred_element_type=F32)
    return back_rows.astype(BF)


def outer_sum(left, right):
    return lax.dot_general(left, right, (((0,), (0,)), ((), ())), preferred_element_type=F32)


def routed_plan(tokens, route_ids, gate_probs, out_cot, w_gate, w_up, w_down):
    experts = lax.axis_size("expert")
    tok_rows, features = tokens.shape
    top_count = route_ids.shape[1]
    hidden = w_gate.shape[2]
    capacity = max(2, tok_rows * top_count * 4 // (3 * experts))
    total_rows = experts * capacity
    positions = slots(route_ids, experts, capacity)
    gate_weight, up_weight, down_weight = w_gate[0], w_up[0], w_down[0]

    def exchange(rows):
        blocks = rows.reshape(experts, capacity, features)
        return lax.all_to_all(blocks, "expert", 0, 0, tiled=True).reshape(-1, features)

    received = exchange(place(jnp.repeat(tokens, top_count, axis=0), positions, total_rows))
    pre_gate, pre_up, activation = hidden_rows(received, gate_weight, up_weight)
    result = jnp.dot(activation, down_weight, preferred_element_type=F32).astype(BF)
    picked = exchange(result)[positions].reshape(tok_rows, top_count, features)
    combined = jnp.einsum("tk,tkd->td", gate_probs, picked.astype(F32)).astype(BF)
    scaled = (gate_probs[:, :, None] * out_cot[:, None, :].astype(F32)).astype(BF)
    grads_in = exchange(place(scaled.reshape(-1, features), positions, total_rows))
    d_gate, d_up = hidden_grads(grads_in, pre_gate, pre_up, down_weight)
    back = exchange(input_rows(d_gate, d_up, gate_weight, up_weight))
    grad_tokens = jnp.sum(
        back[positions].reshape(tok_rows, top_count, features).astype(F32), axis=1
    ).astype(BF)
    gate_up_sum = lax.psum_scatter(
        outer_sum(received, jnp.concatenate([d_gate, d_up], axis=1)).astype(BF),
        "replica",
        scatter_dimension=0,
        tiled=True,
    )
    down_sum = lax.psum_scatter(
        outer_sum(activation, grads_in).astype(BF), "replica", scatter_dimension=0, tiled=True
    )
    return (
        combined,
        grad_tokens,
        gate_up_sum[:, :hidden][None],
        gate_up_sum[:, hidden:][None],
        down_sum[None],
    )

def dot(left, right):
    return jnp.dot(left, right, preferred_element_type=F32)


def whole(array):
    return pl.BlockSpec(array.shape, lambda *_: (0,) * array.ndim)


def params(steps=0):
    order = ("arbitrary",) * steps if steps else None
    return pltpu.CompilerParams(dimension_semantics=order, vmem_limit_bytes=VMEM)


def column_specs(pieces, block):
    return [pl.BlockSpec((a.shape[0], block), lambda i, *_: (0, i)) for a in pieces]


def group_rows(refs, groups):
    each = len(refs) // groups
    return [
        jnp.concatenate([ref[...] for ref in refs[g * each : (g + 1) * each]], axis=0)
        for g in range(groups)
    ]


def plan_and_pack(expert, experts, capacity, pieces):
    features = pieces[0].shape[1] - LANES
    groups, block = 2, 512
    length = sum(a.shape[0] for a in pieces) // groups
    room = TOGETHER * capacity
    n = len(pieces)

    def body(expert_ref, *refs):
        mine_ref, theirs_ref, mine_lanes, theirs_lanes, pick_ref, place_ref = refs[2 * n :]

        @pl.when(pl.program_id(0) == 0)
        def _():
            lane = lax.broadcasted_iota(jnp.int32, (length, LANES), 1)
            row = lax.broadcasted_iota(jnp.int32, (length, length), 0)
            col = lax.broadcasted_iota(jnp.int32, (length, length), 1)
            before = (row >= col).astype(BF)
            slot = lax.broadcasted_iota(jnp.int32, (length, 2 * room), 1) % room
            wanted = (slot + 1).astype(F32)
            for group, lanes in enumerate(group_rows(refs[n : 2 * n], groups)):
                shares = lanes.astype(F32)
                routed = []
                for index in (expert_ref[0], expert_ref[0] ^ 1):
                    held = (lane == index) | (lane == index + experts)
                    held = held | (lane == index + 2 * experts)
                    weight = jnp.sum(jnp.where(held, shares, 0.0), axis=1, keepdims=True)
                    routed.append(jnp.broadcast_to((weight > 0).astype(F32), (length, room)))
                routed = jnp.concatenate(routed, axis=1)
                rank = dot(before, routed.astype(BF))
                place = jnp.where((rank == wanted) & (routed > 0), 1.0, 0.0)
                place_ref[group] = place.astype(BF)
                pick = place.T.astype(BF)
                pick_ref[group] = pick
                packed = dot(pick, lanes).astype(BF)
                here = slice(group * room, (group + 1) * room)
                mine_lanes[here] = packed[:room]
                theirs_lanes[here] = packed[room:]

        for group, rows in enumerate(group_rows(refs[:n], groups)):
            packed = dot(pick_ref[group], rows).astype(BF)
            here = slice(group * room, (group + 1) * room)
            mine_ref[here] = packed[:room]
            theirs_ref[here] = packed[room:]

    rows = jax.ShapeDtypeStruct((groups * room, features), BF)
    lanes = jax.ShapeDtypeStruct((groups * room, LANES), BF)
    pick = jax.ShapeDtypeStruct((groups, 2 * room, length), BF)
    place = jax.ShapeDtypeStruct((groups, length, 2 * room), BF)
    return pl.pallas_call(
        body,
        grid_spec=pltpu.PrefetchScalarGridSpec(
            num_scalar_prefetch=1,
            grid=(features // block,),
            in_specs=column_specs(pieces, block)
            + [
                pl.BlockSpec((a.shape[0], LANES), lambda i, e: (0, features // LANES))
                for a in pieces
            ],
            out_specs=column_specs((rows, rows), block)
            + [whole(a) for a in (lanes, lanes, pick, place)],
        ),
        out_shape=(rows, rows, lanes, lanes, pick, place),
        compiler_params=params(1),
        cost_estimate=SMALL,
        name="plan_and_pack",
    )(expert, *pieces, *pieces)


def pack(pick, pieces):
    features = pieces[0].shape[1]
    groups, room, block = pick.shape[0], pick.shape[1] // 2, 512

    def body(pick_ref, *refs):
        mine_ref, theirs_ref = refs[-2:]
        for group, rows in enumerate(group_rows(refs[:-2], groups)):
            packed = dot(pick_ref[group], rows).astype(BF)
            here = slice(group * room, (group + 1) * room)
            mine_ref[here] = packed[:room]
            theirs_ref[here] = packed[room:]

    out = jax.ShapeDtypeStruct((groups * room, features), BF)
    return pl.pallas_call(
        body,
        grid=(features // block,),
        in_specs=[whole(pick)] + column_specs(pieces, block),
        out_specs=column_specs((out, out), block),
        out_shape=(out, out),
        compiler_params=params(1),
        cost_estimate=SMALL,
        name="pack",
    )(pick, *pieces)


def spread(place, mine, theirs):
    groups, length, slots_of = place.shape
    room, features, block = slots_of // 2, mine.shape[1], 512
    half = length // 2

    def body(place_ref, mine_ref, theirs_ref, near_ref, first_ref, second_ref):
        dense = []
        for group in range(groups):
            here = slice(group * room, (group + 1) * room)
            rows = jnp.concatenate([mine_ref[here], theirs_ref[here]], axis=0)
            dense.append(dot(place_ref[group], rows).astype(BF))
        near_ref[...] = dense[0]
        tok_rows = length // TOGETHER
        first_ref[...] = dense[1][tok_rows : 3 * tok_rows]
        second_ref[...] = jnp.concatenate([dense[1][3 * tok_rows :], dense[1][:tok_rows]], axis=0)

    outs = [jax.ShapeDtypeStruct((size, features), BF) for size in (length, half, half)]
    return pl.pallas_call(
        body,
        grid=(features // block,),
        in_specs=[whole(place)] + column_specs((mine, theirs), block),
        out_specs=column_specs(outs, block),
        out_shape=outs,
        compiler_params=params(1),
        cost_estimate=SMALL,
        name="spread",
    )(place, mine, theirs)


def split3(value):
    high = value.astype(BF)
    rest = value - high.astype(F32)
    mid = rest.astype(BF)
    low = (rest - mid.astype(F32)).astype(BF)
    return high, mid, low


def after(value, *earlier):
    return lax.optimization_barrier((value, *earlier))[0]


def dense_plan(tokens, route_ids, gate_probs, out_cot, w_gate, w_up, w_down):
    experts = lax.axis_size("expert")
    tok_rows, features = tokens.shape
    hidden = w_gate.shape[2]
    top_count = route_ids.shape[1]
    capacity = max(2, tok_rows * top_count * 4 // (3 * experts))
    expert = lax.axis_index("expert").astype(jnp.int32)
    replica = lax.axis_index("replica").astype(jnp.int32)
    w_gate, w_up, w_down = w_gate[0], w_up[0], w_down[0]

    def to_core(rows):
        return lax.ppermute(rows, "expert", [(i, i ^ 1) for i in range(experts)])

    def to_x(rows):
        return lax.ppermute(rows, "expert", [(i, i ^ 2) for i in range(experts)])

    def to_z(rows):
        return lax.ppermute(rows, "expert", [(i, (i + 4) % experts) for i in range(experts)])

    def to_y(rows):
        return lax.ppermute(rows, "replica", [(0, 1), (1, 0)])

    chosen = route_ids[:, :, None] == jnp.arange(experts, dtype=jnp.int32)
    share = jnp.sum(jnp.where(chosen, gate_probs[:, :, None], 0.0), axis=1)
    pad = jnp.zeros((tok_rows, LANES - 3 * experts), BF)

    cot_far_own, cot_relay_own = to_x(out_cot), to_y(out_cot)
    token_own = jnp.concatenate([tokens, *split3(share), pad], axis=1)
    token_far_own, token_relay_own = to_x(token_own), to_y(token_own)
    ring = [after(to_z(token_own), cot_far_own)]
    ring.append(after(to_z(ring[0]), token_far_own, cot_relay_own))
    ring.append(after(to_z(ring[1]), token_relay_own))
    token_ring = jnp.concatenate(ring, axis=0)
    token_far_ring, token_relay_ring = to_x(token_ring), to_y(token_ring)
    token_relay_far_own = to_y(token_far_own)
    cot_relay_far_own = to_y(cot_far_own)
    ring = [after(to_z(after(out_cot, ring[1])), token_relay_far_own)]
    ring.append(to_z(ring[0]))
    ring.append(to_z(ring[1]))
    cot_ring = jnp.concatenate(ring, axis=0)
    cot_far_ring, cot_relay_ring = to_x(cot_ring), to_y(cot_ring)
    token_relay_far_ring = to_y(token_far_ring)
    cot_relay_far_ring = to_y(cot_far_ring)

    def enter(pieces, before_plan, before_dots):
        mine, theirs, mine_lanes, theirs_lanes, pick, place = plan_and_pack(
            after(expert.reshape(1), *before_plan), experts, capacity, pieces
        )
        theirs = after(to_core(theirs), *before_dots)
        x = jnp.concatenate([mine, theirs], axis=0)
        shares = jnp.concatenate([mine_lanes, to_core(theirs_lanes)], axis=0)
        held = (jnp.arange(LANES) % experts == expert) & (jnp.arange(LANES) < 3 * experts)
        weight = jnp.sum(jnp.where(held, shares.astype(F32), 0.0), axis=1, keepdims=True)
        pre_gate, pre_up = dot(x, w_gate), dot(x, w_up)
        activation = (jax.nn.silu(pre_gate) * pre_up).astype(BF)
        return x, weight, pick, place, pre_gate, pre_up, activation

    def enter_cot(pick, pieces, weight, *earlier):
        mine, theirs = pack(pick, pieces)
        cot = jnp.concatenate([mine, after(to_core(theirs), *earlier)], axis=0)
        return (cot.astype(F32) * weight).astype(BF)

    def leave(place, rows_of, *earlier):
        half = place.shape[0] * place.shape[2] // 2
        theirs = after(to_core(rows_of(slice(half, None))), *earlier)
        near, *far = spread(place, rows_of(slice(0, half)), theirs)
        arrived = [to_x(a) for a in far]
        totals = []
        for i, s in enumerate((1, 2, 3, 0)):
            part = near[s * tok_rows : (s + 1) * tok_rows].astype(F32)
            at = i % 2 * tok_rows
            part = part + arrived[i // 2][at : at + tok_rows].astype(F32)
            if totals:
                part = part + to_z(totals[-1]).astype(F32)
            totals.append(part.astype(BF))
        return totals, arrived, near

    def grads(x, activation, cot, d_gate, d_up):
        x = lax.dynamic_slice_in_dim(x, replica * (features // 2), features // 2, 1)
        activation = lax.dynamic_slice_in_dim(activation, replica * (hidden // 2), hidden // 2, 1)
        return outer_sum(x, d_gate), outer_sum(x, d_up), outer_sum(activation, cot)

    x, weight, pick, place, pre_gate, pre_up, activation = enter(
        (token_own, token_ring, token_far_own, token_far_ring),
        (token_relay_far_own, ring[1]),
        (token_relay_ring, cot_ring, cot_relay_far_own),
    )
    totals, arrived, near = leave(
        place, lambda rows: (dot(activation[rows], w_down) * weight[rows]).astype(BF)
    )
    cot = enter_cot(
        after(pick, near),
        (out_cot, cot_ring, cot_far_own, cot_far_ring),
        weight,
        token_relay_far_ring,
    )
    d_gate, d_up = hidden_grads(cot, pre_gate, pre_up, w_down)
    grad_totals, grad_arrived, near = leave(
        place,
        lambda rows: input_rows(d_gate[rows], d_up[rows], w_gate, w_up),
        arrived[0],
    )
    own = x, activation, cot, d_gate, d_up

    x, weight, pick, _, pre_gate, pre_up, activation = enter(
        (token_relay_own, token_relay_ring, token_relay_far_own, token_relay_far_ring),
        (near, totals[1], cot_relay_ring),
        (arrived[1],),
    )
    own = grads(*after(own, activation, totals[3], grad_arrived[0]))
    cot = enter_cot(
        after(pick, own, grad_totals[1]),
        (cot_relay_own, cot_relay_ring, cot_relay_far_own, cot_relay_far_ring),
        weight,
    )
    d_gate, d_up = hidden_grads(cot, pre_gate, pre_up, w_down)
    other = grads(x, activation, cot, d_gate, d_up)
    grad_gate, grad_up, grad_down = ((a + b).astype(BF)[None] for a, b in zip(own, other))
    return (totals[3], grad_totals[3], grad_gate, grad_up, grad_down)


def dense_fits(mesh):
    experts, replicas = mesh.shape["expert"], mesh.shape["replica"]
    return replicas == 2 and experts == 4 * TOGETHER


def solution(mesh):
    placed = (
        P(("expert", "replica"), None),
        P(("expert", "replica"), None),
        P(("expert", "replica"), None),
        P(("expert", "replica"), None),
        P("expert", None, None),
        P("expert", None, None),
        P("expert", None, None),
    )
    return jax.shard_map(
        dense_plan if dense_fits(mesh) else routed_plan,
        mesh=mesh,
        in_specs=placed,
        out_specs=(
            P(("expert", "replica"), None),
            P(("expert", "replica"), None),
            P("expert", "replica", None),
            P("expert", "replica", None),
            P("expert", "replica", None),
        ),
        check_vma=False,
    )
```

time: 236 us -> 215 us (0.911)
  waiting for transfers between devices: 108 us -> 91 us
  starting transfers between devices: 37.1 us -> 25.1 us
  local copies, waits for them, and re-layouts: 11.3 us -> 17.5 us
  Pallas kernels: 24.3 us -> 28.2 us
    ppermute x16 -> x8, waiting for transfers between devices: 24.3 us -> 13.6 us  [to_y(): return lax.ppermute(rows, 'replica', [(0, 1), (1, 0)])]
    ppermute x12, waiting for transfers between devices: 50.6 us -> 41 us  [to_z(): lax.ppermute(rows, 'expert', [(i, (i + 4) % experts) for i in range(exper...]
    ppermute x16 -> x8, starting transfers between devices: 17.8 us -> 9.24 us  [to_x(): return lax.ppermute(rows, 'expert', [(i, i ^ 2) for i in range(experts)])]
    ppermute x16 -> x8, starting transfers between devices: 15.6 us -> 7.12 us  [to_y(): return lax.ppermute(rows, 'replica', [(0, 1), (1, 0)])]
    unnamed x114 -> x96, local copies, waits for them, and re-layouts: 7.4 us -> 14.7 us
    ppermute x12, starting transfers between devices: 3.44 us -> 7.83 us  [to_z(): lax.ppermute(rows, 'expert', [(i, (i + 4) % experts) for i in range(exper...]
    concatenate x1 -> x0, other arithmetic: 2.79 us -> none  [enter(): x = jnp.concatenate([mine[:, :features], theirs[:, :features]], axis=0)]
    convert_element_type x8, other arithmetic: 8.22 us -> 11 us  [leave(): totals.append(part.astype(BF))]
  transfers between devices with their start and end apart: 50 -> 36, of which waited for: 24 -> 17; matrix products, arithmetic and copies ran while one was open for 18% -> 20% of each run, Pallas kernels for 5% -> 11%
where the time goes in v5:
time: 215 us; the launch traced here: 214 us
  waiting for transfers between devices  91 us (42%)
  matrix products  36.9 us (17%)
  Pallas kernels  28.2 us (13%)
  starting transfers between devices  25.1 us (12%)
  local copies, waits for them, and re-layouts  17.5 us (8%)
  other arithmetic  14.1 us (7%)
    ppermute x12, waiting for transfers between devices, to_z(): lax.ppermute(rows, 'expert', [(i, (i + 4) % experts) for i in range(exper...  41 us
    ppermute x8, waiting for transfers between devices, to_x(): return lax.ppermute(rows, 'expert', [(i, i ^ 2) for i in range(experts)])  35.1 us
    unnamed x96, local copies, waits for them, and re-layouts  14.7 us
    ppermute x8, waiting for transfers between devices, to_y(): return lax.ppermute(rows, 'replica', [(0, 1), (1, 0)])  13.6 us
    dot_general x6, matrix products, outer_sum(): lax.dot_general(left, right, (((0,), (0,)), ((), ())), preferred_element_...  13.3 us
    dot_general x6, matrix products, dot(): return jnp.dot(left, right, preferred_element_type=F32)  12.8 us
    convert_element_type x8, other arithmetic, leave(): totals.append(part.astype(BF))  11 us
    pallas_call x2, Pallas kernels, plan_and_pack(): pl.pallas_call(body, grid_spec=pltpu.PrefetchScalarGridSpec(num_scalar_pr...  10.5 us
  transfers between devices with their start and end apart: 36, of which 17 were waited for; matrix products, arithmetic and copies ran while one was open for 20% of the time, Pallas kernels for 11%

profile of v5, /device:TPU:0, one launch (start us, length us, event | category | flops | bytes accessed | tf_op | source)
XLA Modules:
  0.0 213.9 jit_solution(1805632997921085167)
XLA Ops:
  2.8 3.1 %collective-permute-start.2 = (bf16[64,2176]{1,0:T(8,128)(2,1)S(1)}, bf16[64,2176]{1,0:T(8,128)(2,1)S(1)}, u32[]{:S(2)}, u32[]{:S(2)}) collective-permute-start(bf16[64,2176]{1,0:T(8,128)(2,1)S(1)} %concatenate.27.refs_0_.refs_4_), channel_id=1, source_target_pairs={{0,8},{2,10},{4,12},{6,14},{8,16},{10,18},{12,20},{14,22},{16,24},... | collective-permute-start | bytes 835592 | tf_op jit(solution)/shard_map/ppermute | solution.py:276
  9.9 5.4 %collective-permute-done.3.refs_2_ = bf16[64,2048]{1,0:T(8,128)(2,1)S(1)} collective-permute-done((bf16[64,2048]{1,0:T(8,128)(2,1)}, bf16[64,2048]{1,0:T(8,128)(2,1)S(1)}, u32[]{:S(2)}, u32[]{:S(2)}) %collective-permute-start.3) | collective-permute-done | bytes 262176 | tf_op jit(solution)/shard_map/ppermute | solution.py:273
  19.8 4.5 %collective-permute-done.4 = bf16[64,2176]{1,0:T(8,128)(2,1)S(1)} collective-permute-done((bf16[64,2176]{1,0:T(8,128)(2,1)S(1)}, bf16[64,2176]{1,0:T(8,128)(2,1)S(1)}, u32[]{:S(2)}, u32[]{:S(2)}) %collective-permute-start.4) | collective-permute-done | bytes 278560 | tf_op jit(solution)/shard_map/ppermute | solution.py:276
  25.8 6.9 %collective-permute-done.8 = bf16[64,2176]{1,0:T(8,128)(2,1)S(1)} collective-permute-done((bf16[64,2176]{1,0:T(8,128)(2,1)S(1)}, bf16[64,2176]{1,0:T(8,128)(2,1)S(1)}, u32[]{:S(2)}, u32[]{:S(2)}) %collective-permute-start.8) | collective-permute-done | bytes 278560 | tf_op jit(solution)/shard_map/ppermute | solution.py:276
  36.5 5.2 %collective-permute-done.1.refs_2_.refs_6_ = bf16[64,2176]{1,0:T(8,128)(2,1)} collective-permute-done((bf16[64,2176]{1,0:T(8,128)(2,1)S(1)}, bf16[64,2176]{1,0:T(8,128)(2,1)}, u32[]{:S(2)}, u32[]{:S(2)}) %collective-permute-start.1) | collective-permute-done | bytes 278560 | tf_op jit(solution)/shard_map/ppermute | solution.py:279
  41.6 5.0 %collective-permute-done.6 = bf16[64,2048]{1,0:T(8,128)(2,1)} collective-permute-done((bf16[64,2048]{1,0:T(8,128)(2,1)}, bf16[64,2048]{1,0:T(8,128)(2,1)}, u32[]{:S(2)}, u32[]{:S(2)}) %collective-permute-start.6) | collective-permute-done | bytes 262176 | tf_op jit(solution)/shard_map/ppermute | solution.py:276
  47.2 10.7 %collective-permute-done.7 = bf16[64,2048]{1,0:T(8,128)(2,1)} collective-permute-done((bf16[64,2048]{1,0:T(8,128)(2,1)}, bf16[64,2048]{1,0:T(8,128)(2,1)}, u32[]{:S(2)}, u32[]{:S(2)}) %collective-permute-start.7) | collective-permute-done | bytes 262176 | tf_op jit(solution)/shard_map/ppermute | solution.py:276
  60.1 5.2 %plan_and_pack.2 = (bf16[256,2048]{1,0:T(8,128)(2,1)}, bf16[256,2048]{1,0:T(8,128)(2,1)}, bf16[256,128]{1,0:T(8,128)(2,1)}, bf16[256,128]{1,0:T(8,128)(2,1)}, bf...) custom-call(s32[1]{0:T(128)} %bitcast.expert_ref, bf16[64,2176]{1,0:T(8,128)(2,1)} %copy-done.7, ...), custom_call_target="tpu_custom_call" | custom-call | flops 1 | bytes 1 | tf_op jit(solution)/shard_map/plan_and_pack/pallas_call | solution.py:173
  74.3 3.0 %multiply_convert_fusion.7 = (bf16[512,768]{1,0:T(8,128)(2,1)S(1)}, f32[512,768]{1,0:T(8,128)}) fusion(f32[512,768]{1,0:T(8,128)S(1)} %fusion.22, bf16[512,2048]{1,0:T(8,128)(2,1)S(1)} %constant_dynamic-update-slice_fusion.6, bf16[1,2048,768]{2,1,0:T(8,128)(2,1)S(1)} %copy-done), kind=kOutput, calls=%fused_computation.44 | convolution fusion | flops 1612972032 | bytes 9175040 | tf_op jit(solution)/shard_map/dot_general | solution.py:102
  82.0 4.3 %spread.2 = (bf16[256,2048]{1,0:T(8,128)(2,1)}, bf16[128,2048]{1,0:T(8,128)(2,1)}, bf16[128,2048]{1,0:T(8,128)(2,1)}) custom-call(bf16[2,256,256]{2,1,0:T(8,128)(2,1)} %get-tuple-element.50.place_ref, bf16[256,2048]{1,0:T(8,128)(2,1)} %fusion.40.mine_ref, bf16[256,2048]{1,0:T(8,128)(2,1)} %copy-done.12), custom_call_target="tpu_custom_call" | custom-call | flops 1 | bytes 1 | tf_op jit(solution)/shard_map/spread/pallas_call | solution.py:235
  86.4 12.2 %collective-permute-done.22.refs_3_ = bf16[192,2048]{1,0:T(8,128)(2,1)S(1)} collective-permute-done((bf16[192,2048]{1,0:T(8,128)(2,1)}, bf16[192,2048]{1,0:T(8,128)(2,1)S(1)}, u32[]{:S(2)}, u32[]{:S(2)}) %collective-permute-start.22) | collective-permute-done | bytes 786464 | tf_op jit(solution)/shard_map/ppermute | solution.py:273
  99.4 4.6 %pack.2 = (bf16[256,2048]{1,0:T(8,128)(2,1)}, bf16[256,2048]{1,0:T(8,128)(2,1)}) custom-call(bf16[2,256,256]{2,1,0:T(8,128)(2,1)} %get-tuple-element.60.pick_ref, bf16[64,2048]{1,0:T(8,128)(2,1)} %refs_0_.1, bf16[192,2048]{1,0:T(8,128)(2,1)} %constant_dynamic-update-slice_fusion.3.refs_1_, bf16[64,2048]{1,0:T(8,128)(2,1)} %copy-done.27, ...), custom_call_target="tpu_custom_call" | custom-call | flops 1 | bytes 1 | tf_op jit(solution)/shard_map/pack/pallas_call | solution.py:206
  108.1 10.6 %collective-permute-done.18 = bf16[128,2048]{1,0:T(8,128)(2,1)S(1)} collective-permute-done((bf16[128,2048]{1,0:T(8,128)(2,1)S(1)}, bf16[128,2048]{1,0:T(8,128)(2,1)S(1)}, u32[]{:S(2)}, u32[]{:S(2)}) %collective-permute-start.18) | collective-permute-done | bytes 524320 | tf_op jit(solution)/shard_map/ppermute | solution.py:273
  120.2 6.1 %collective-permute-done.24.refs_3_.refs_7_ = bf16[192,2176]{1,0:T(8,128)(2,1)S(1)} collective-permute-done((bf16[192,2176]{1,0:T(8,128)(2,1)}, bf16[192,2176]{1,0:T(8,128)(2,1)S(1)}, u32[]{:S(2)}, u32[]{:S(2)}) %collective-permute-start.24) | collective-permute-done | bytes 835616 | tf_op jit(solution)/shard_map/ppermute | solution.py:279
  128.7 3.8 %multiply_convert_fusion.6 = (bf16[512,768]{1,0:T(8,128)(2,1)S(1)}, bf16[512,768]{1,0:T(8,128)(2,1)S(1)}) fusion(f32[512,768]{1,0:T(8,128)S(1)} %copy-done.44, f32[512,768]{1,0:T(8,128)} %get-tuple-element.90, bf16[512,2048]{1,0:T(8,128)(2,1)S(1)} %multiply_convert_fusion.1, bf16[1,768,2048]{2,1,0:T(8,128)(2,1)S(1)} %copy-done.34), kind=kOutput, calls=%fused_computation.43 | convolution fusion | flops 1615724544 | bytes 9961472 | tf_op jit(solution)/shard_map/dot_general | solution.py:41
  139.9 4.3 %spread.3 = (bf16[256,2048]{1,0:T(8,128)(2,1)}, bf16[128,2048]{1,0:T(8,128)(2,1)}, bf16[128,2048]{1,0:T(8,128)(2,1)}) custom-call(bf16[2,256,256]{2,1,0:T(8,128)(2,1)} %get-tuple-element.50.place_ref, bf16[256,2048]{1,0:T(8,128)(2,1)} %fusion.46.mine_ref, bf16[256,2048]{1,0:T(8,128)(2,1)} %copy-done.11), custom_call_target="tpu_custom_call" | custom-call | flops 1 | bytes 1 | tf_op jit(solution)/shard_map/spread/pallas_call | solution.py:235
  148.1 5.3 %plan_and_pack.3 = (bf16[256,2048]{1,0:T(8,128)(2,1)}, bf16[256,2048]{1,0:T(8,128)(2,1)}, bf16[256,128]{1,0:T(8,128)(2,1)}, bf16[256,128]{1,0:T(8,128)(2,1)}, bf...) custom-call(s32[1]{0:T(128)} %bitcast.expert_ref, bf16[64,2176]{1,0:T(8,128)(2,1)} %copy-done.8, ...), custom_call_target="tpu_custom_call" | custom-call | flops 1 | bytes 1 | tf_op jit(solution)/shard_map/plan_and_pack/pallas_call | solution.py:173
  153.5 5.3 %collective-permute-done.27 = bf16[128,2048]{1,0:T(8,128)(2,1)} collective-permute-done((bf16[128,2048]{1,0:T(8,128)(2,1)}, bf16[128,2048]{1,0:T(8,128)(2,1)}, u32[]{:S(2)}, u32[]{:S(2)}) %collective-permute-start.27) | collective-permute-done | bytes 524320 | tf_op jit(solution)/shard_map/ppermute | solution.py:273
  163.7 6.2 %collective-permute-done.28 = bf16[64,2048]{1,0:T(8,128)(2,1)S(1)} collective-permute-done((bf16[64,2048]{1,0:T(8,128)(2,1)S(1)}, bf16[64,2048]{1,0:T(8,128)(2,1)S(1)}, u32[]{:S(2)}, u32[]{:S(2)}) %collective-permute-start.28) | collective-permute-done | bytes 262176 | tf_op jit(solution)/shard_map/ppermute | solution.py:276
  173.6 3.2 %multiply_convert_fusion.4 = (bf16[512,768]{1,0:T(8,128)(2,1)}, f32[512,768]{1,0:T(8,128)}) fusion(f32[512,768]{1,0:T(8,128)S(1)} %fusion.16, bf16[512,2048]{1,0:T(8,128)(2,1)S(1)} %constant_dynamic-update-slice_fusion.8, bf16[1,2048,768]{2,1,0:T(8,128)(2,1)S(1)} %copy-done), kind=kOutput, calls=%fused_computation.40 | convolution fusion | flops 1612972032 | bytes 9175040 | tf_op jit(solution)/shard_map/dot_general | solution.py:102
  178.7 2.7 %fusion.55 = f32[1024,768]{1,0:T(8,128)} fusion(bf16[512,768]{1,0:T(8,128)(2,1)S(1)} %copy-done.16, bf16[512,2048]{1,0:T(8,128)(2,1)S(1)} %copy-done.22, s32[]{:T(128)S(6)} %select_n.31), kind=kOutput, calls=%fused_computation.52 | convolution fusion | flops 805306368 | bytes 4980740 | tf_op jit(solution)/shard_map/dot_general | solution.py:55
  181.4 2.7 %fusion.53 = f32[1024,768]{1,0:T(8,128)} fusion(bf16[512,768]{1,0:T(8,128)(2,1)S(1)} %copy-done.20, bf16[512,2048]{1,0:T(8,128)(2,1)S(1)} %copy-done.22, s32[]{:T(128)S(6)} %select_n.31), kind=kOutput, calls=%fused_computation.50 | convolution fusion | flops 805306368 | bytes 4980740 | tf_op jit(solution)/shard_map/dot_general | solution.py:55
  185.0 4.5 %pack.3 = (bf16[256,2048]{1,0:T(8,128)(2,1)}, bf16[256,2048]{1,0:T(8,128)(2,1)}) custom-call(bf16[2,256,256]{2,1,0:T(8,128)(2,1)} %get-tuple-element.78.pick_ref, bf16[64,2048]{1,0:T(8,128)(2,1)} %copy-done.25, bf16[192,2048]{1,0:T(8,128)(2,1)} %collective-permute-done.31.refs_1_, bf16[64,2048]{1,0:T(8,128)(2,1)} %copy-done.26, bf16[192,2048]{1,0:T(8,128)(2,1)} %copy-done.18), custom_call_target="tpu_custom_call" | custom-call | flops 1 | bytes 1 | tf_op jit(solution)/shard_map/pack/pallas_call | solution.py:206
  194.6 7.0 %collective-permute-done.30 = bf16[64,2048]{1,0:T(8,128)(2,1)S(1)} collective-permute-done((bf16[64,2048]{1,0:T(8,128)(2,1)S(1)}, bf16[64,2048]{1,0:T(8,128)(2,1)S(1)}, u32[]{:S(2)}, u32[]{:S(2)}) %collective-permute-start.30) | collective-permute-done | bytes 262176 | tf_op jit(solution)/shard_map/ppermute | solution.py:276
  (192 shorter events, 80.8 us)
Async XLA Ops:
  2.8 13.2 %collective-permute-start.2 = (bf16[64,2176]{1,0:T(8,128)(2,1)S(1)}, bf16[64,2176]{1,0:T(8,128)(2,1)S(1)}, u32[]{:S(2)}, u32[]{:S(2)}) collective-permute-start(bf16[64,2176]{1,0:T(8,128)(2,1)S(1)} %concatenate.27.refs_0_.refs_4_), channel_id=1, source_target_pairs={{0,8},{2,10},{4,12},{6,14},{8,16},{10,18},{12,20},{14,22},{16,24},... | collective-permute-start | bytes 835592 | tf_op jit(solution)/shard_map/ppermute | solution.py:276
  7.4 11.0 %collective-permute-start.5 = (bf16[64,2048]{1,0:T(8,128)(2,1)}, bf16[64,2048]{1,0:T(8,128)(2,1)S(1)}, u32[]{:S(2)}, u32[]{:S(2)}) collective-permute-start(bf16[64,2048]{1,0:T(8,128)(2,1)} %refs_0_.1), channel_id=1, source_target_pairs={{0,1},{1,0},{2,3},{3,2},{4,5},{5,4},{6,7},{7,6},{8,9},{9,8},{10,11... | collective-permute-start | bytes 786440 | tf_op jit(solution)/shard_map/ppermute | solution.py:279
  8.9 16.2 %collective-permute-start.9 = (bf16[64,2176]{1,0:T(8,128)(2,1)S(1)}, bf16[64,2176]{1,0:T(8,128)(2,1)S(1)}, u32[]{:S(2)}, u32[]{:S(2)}) collective-permute-start(bf16[64,2176]{1,0:T(8,128)(2,1)S(1)} %concatenate.27.refs_0_.refs_4_), channel_id=1, source_target_pairs={{0,1},{1,0},{2,3},{3,2},{4,5},{5,4},{6,7},{7,6},{8,9},{9,8},{10,11... | collective-permute-start | bytes 835592 | tf_op jit(solution)/shard_map/ppermute | solution.py:279
  9.4 10.4 %collective-permute-start = (bf16[64,2176]{1,0:T(8,128)(2,1)S(1)}, bf16[64,2176]{1,0:T(8,128)(2,1)S(1)}, u32[]{:S(2)}, u32[]{:S(2)}) collective-permute-start(bf16[64,2176]{1,0:T(8,128)(2,1)S(1)} %concatenate.27.refs_0_.refs_4_), channel_id=1, source_target_pairs={{0,4},{2,6},{4,0},{6,2},{8,12},{10,14},{12,8},{14,10},{16,20},{18,... | collective-permute-start | bytes 835592 | tf_op jit(solution)/shard_map/ppermute | solution.py:273
  33.4 26.7 %collective-permute-start.10 = (bf16[192,2176]{1,0:T(8,128)(2,1)}, bf16[192,2176]{1,0:T(8,128)(2,1)}, u32[]{:S(2)}, u32[]{:S(2)}) collective-permute-start(bf16[192,2176]{1,0:T(8,128)(2,1)} %constant_dynamic-update-slice_fusion.refs_1_.refs_5_), channel_id=1, source_target_pairs={{0,4},{2,6},{4,0},{6,2},{8,12},{10,14},{12,8},{14,10},{16,20},{18,... | collective-permute-start | bytes 2506760 | tf_op jit(solution)/shard_map/ppermute | solution.py:273
  46.7 11.2 %collective-permute-start.7 = (bf16[64,2048]{1,0:T(8,128)(2,1)}, bf16[64,2048]{1,0:T(8,128)(2,1)}, u32[]{:S(2)}, u32[]{:S(2)}) collective-permute-start(bf16[64,2048]{1,0:T(8,128)(2,1)} %collective-permute-done.6), channel_id=1, source_target_pairs={{0,8},{2,10},{4,12},{6,14},{8,16},{10,18},{12,20},{14,22},{16,24},... | collective-permute-start | bytes 786440 | tf_op jit(solution)/shard_map/ppermute | solution.py:276
  46.7 23.3 %collective-permute-start.14 = (bf16[64,2048]{1,0:T(8,128)(2,1)}, bf16[64,2048]{1,0:T(8,128)(2,1)S(1)}, u32[]{:S(2)}, u32[]{:S(2)}) collective-permute-start(bf16[64,2048]{1,0:T(8,128)(2,1)} %copy-done.27), channel_id=1, source_target_pairs={{0,1},{1,0},{2,3},{3,2},{4,5},{5,4},{6,7},{7,6},{8,9},{9,8},{10,11... | collective-permute-start | bytes 786440 | tf_op jit(solution)/shard_map/ppermute | solution.py:279
  59.6 12.7 %collective-permute-start.12 = (bf16[192,2176]{1,0:T(8,128)(2,1)}, bf16[192,2176]{1,0:T(8,128)(2,1)S(1)}, u32[]{:S(2)}, u32[]{:S(2)}) collective-permute-start(bf16[192,2176]{1,0:T(8,128)(2,1)} %constant_dynamic-update-slice_fusion.refs_1_.refs_5_), channel_id=1, source_target_pairs={{0,1},{1,0},{2,3},{3,2},{4,5},{5,4},{6,7},{7,6},{8,9},{9,8},{10,11... | collective-permute-start | bytes 2506760 | tf_op jit(solution)/shard_map/ppermute | solution.py:279
  78.4 20.2 %collective-permute-start.22 = (bf16[192,2048]{1,0:T(8,128)(2,1)}, bf16[192,2048]{1,0:T(8,128)(2,1)S(1)}, u32[]{:S(2)}, u32[]{:S(2)}) collective-permute-start(bf16[192,2048]{1,0:T(8,128)(2,1)} %constant_dynamic-update-slice_fusion.3.refs_1_), channel_id=1, source_target_pairs={{0,4},{2,6},{4,0},{6,2},{8,12},{10,14},{12,8},{14,10},{16,20},{18,... | collective-permute-start | bytes 2359304 | tf_op jit(solution)/shard_map/ppermute | solution.py:273
  104.0 22.3 %collective-permute-start.23 = (bf16[256,2048]{1,0:T(8,128)(2,1)}, bf16[256,2048]{1,0:T(8,128)(2,1)S(1)}, u32[]{:S(2)}, u32[]{:S(2)}) collective-permute-start(bf16[256,2048]{1,0:T(8,128)(2,1)} %get-tuple-element.62), channel_id=1, source_target_pairs={{0,2},{2,0},{4,6},{6,4},{8,10},{10,8},{12,14},{14,12},{16,18},{18,... | collective-permute-start | bytes 3145736 | tf_op jit(solution)/shard_map/ppermute | solution.py:270
  104.0 14.8 %collective-permute-start.18 = (bf16[128,2048]{1,0:T(8,128)(2,1)S(1)}, bf16[128,2048]{1,0:T(8,128)(2,1)S(1)}, u32[]{:S(2)}, u32[]{:S(2)}) collective-permute-start(bf16[128,2048]{1,0:T(8,128)(2,1)S(1)} %copy-done.36), channel_id=1, source_target_pairs={{0,4},{2,6},{4,0},{6,2},{8,12},{10,14},{12,8},{14,10},{16,20},{18,... | collective-permute-start | bytes 1572872 | tf_op jit(solution)/shard_map/ppermute | solution.py:273
  104.6 21.6 %collective-permute-start.24 = (bf16[192,2176]{1,0:T(8,128)(2,1)}, bf16[192,2176]{1,0:T(8,128)(2,1)S(1)}, u32[]{:S(2)}, u32[]{:S(2)}) collective-permute-start(bf16[192,2176]{1,0:T(8,128)(2,1)} %collective-permute-done.10.refs_3_.refs_7_), channel_id=1, source_target_pairs={{0,1},{1,0},{2,3},{3,2},{4,5},{5,4},{6,7},{7,6},{8,9},{9,8},{10,11... | collective-permute-start | bytes 2506760 | tf_op jit(solution)/shard_map/ppermute | solution.py:279
  104.8 43.3 %collective-permute-start.31 = (bf16[192,2048]{1,0:T(8,128)(2,1)}, bf16[192,2048]{1,0:T(8,128)(2,1)}, u32[]{:S(2)}, u32[]{:S(2)}) collective-permute-start(bf16[192,2048]{1,0:T(8,128)(2,1)} %constant_dynamic-update-slice_fusion.3.refs_1_), channel_id=1, source_target_pairs={{0,1},{1,0},{2,3},{3,2},{4,5},{5,4},{6,7},{7,6},{8,9},{9,8},{10,11... | collective-permute-start | bytes 2359304 | tf_op jit(solution)/shard_map/ppermute | solution.py:279
  106.6 39.6 %collective-permute-start.17 = (bf16[128,2048]{1,0:T(8,128)(2,1)}, bf16[128,2048]{1,0:T(8,128)(2,1)}, u32[]{:S(2)}, u32[]{:S(2)}) collective-permute-start(bf16[128,2048]{1,0:T(8,128)(2,1)} %get-tuple-element.57), channel_id=1, source_target_pairs={{0,4},{2,6},{4,0},{6,2},{8,12},{10,14},{12,8},{14,10},{16,20},{18,... | collective-permute-start | bytes 1572872 | tf_op jit(solution)/shard_map/ppermute | solution.py:273
  119.9 14.9 %collective-permute-start.19 = (bf16[64,2048]{1,0:T(8,128)(2,1)S(1)}, bf16[64,2048]{1,0:T(8,128)(2,1)S(1)}, u32[]{:S(2)}, u32[]{:S(2)}) collective-permute-start(bf16[64,2048]{1,0:T(8,128)(2,1)S(1)} %add_convert_fusion.10), channel_id=1, source_target_pairs={{0,8},{2,10},{4,12},{6,14},{8,16},{10,18},{12,20},{14,22},{16,24},... | collective-permute-start | bytes 786440 | tf_op jit(solution)/shard_map/ppermute | solution.py:276
  135.8 10.9 %collective-permute-start.20 = (bf16[64,2048]{1,0:T(8,128)(2,1)S(1)}, bf16[64,2048]{1,0:T(8,128)(2,1)}, u32[]{:S(2)}, u32[]{:S(2)}) collective-permute-start(bf16[64,2048]{1,0:T(8,128)(2,1)S(1)} %add_convert_fusion.9), channel_id=1, source_target_pairs={{0,8},{2,10},{4,12},{6,14},{8,16},{10,18},{12,20},{14,22},{16,24},... | collective-permute-start | bytes 786440 | tf_op jit(solution)/shard_map/ppermute | solution.py:276
  144.2 14.6 %collective-permute-start.27 = (bf16[128,2048]{1,0:T(8,128)(2,1)}, bf16[128,2048]{1,0:T(8,128)(2,1)}, u32[]{:S(2)}, u32[]{:S(2)}) collective-permute-start(bf16[128,2048]{1,0:T(8,128)(2,1)} %get-tuple-element.67), channel_id=1, source_target_pairs={{0,4},{2,6},{4,0},{6,2},{8,12},{10,14},{12,8},{14,10},{16,20},{18,... | collective-permute-start | bytes 1572872 | tf_op jit(solution)/shard_map/ppermute | solution.py:273
  145.7 38.4 %collective-permute-start.33 = (bf16[192,2048]{1,0:T(8,128)(2,1)}, bf16[192,2048]{1,0:T(8,128)(2,1)S(1)}, u32[]{:S(2)}, u32[]{:S(2)}) collective-permute-start(bf16[192,2048]{1,0:T(8,128)(2,1)} %copy-done.17), channel_id=1, source_target_pairs={{0,1},{1,0},{2,3},{3,2},{4,5},{5,4},{6,7},{7,6},{8,9},{9,8},{10,11... | collective-permute-start | bytes 2359304 | tf_op jit(solution)/shard_map/ppermute | solution.py:279
  148.0 12.3 %collective-permute-start.21 = (bf16[64,2048]{1,0:T(8,128)(2,1)S(1)}, bf16[64,2048]{1,0:T(8,128)(2,1)S(1)}, u32[]{:S(2)}, u32[]{:S(2)}) collective-permute-start(bf16[64,2048]{1,0:T(8,128)(2,1)S(1)} %add_convert_fusion.8), channel_id=1, source_target_pairs={{0,8},{2,10},{4,12},{6,14},{8,16},{10,18},{12,20},{14,22},{16,24},... | collective-permute-start | bytes 786440 | tf_op jit(solution)/shard_map/ppermute | solution.py:276
  153.4 18.3 %collective-permute-start.32 = (bf16[256,2048]{1,0:T(8,128)(2,1)}, bf16[256,2048]{1,0:T(8,128)(2,1)S(1)}, u32[]{:S(2)}, u32[]{:S(2)}) collective-permute-start(bf16[256,2048]{1,0:T(8,128)(2,1)} %get-tuple-element.70), channel_id=1, source_target_pairs={{0,2},{2,0},{4,6},{6,4},{8,10},{10,8},{12,14},{14,12},{16,18},{18,... | collective-permute-start | bytes 3145736 | tf_op jit(solution)/shard_map/ppermute | solution.py:270
  162.1 27.5 %collective-permute-start.26 = (bf16[128,2048]{1,0:T(8,128)(2,1)}, bf16[128,2048]{1,0:T(8,128)(2,1)}, u32[]{:S(2)}, u32[]{:S(2)}) collective-permute-start(bf16[128,2048]{1,0:T(8,128)(2,1)} %get-tuple-element.66), channel_id=1, source_target_pairs={{0,4},{2,6},{4,0},{6,2},{8,12},{10,14},{12,8},{14,10},{16,20},{18,... | collective-permute-start | bytes 1572872 | tf_op jit(solution)/shard_map/ppermute | solution.py:273
  171.7 18.0 %collective-permute-start.29 = (bf16[64,2048]{1,0:T(8,128)(2,1)}, bf16[64,2048]{1,0:T(8,128)(2,1)}, u32[]{:S(2)}, u32[]{:S(2)}) collective-permute-start(bf16[64,2048]{1,0:T(8,128)(2,1)} %add_convert_fusion.5), channel_id=1, source_target_pairs={{0,8},{2,10},{4,12},{6,14},{8,16},{10,18},{12,20},{14,22},{16,24},... | collective-permute-start | bytes 786440 | tf_op jit(solution)/shard_map/ppermute | solution.py:276
  189.5 13.8 %collective-permute-start.34 = (bf16[256,2048]{1,0:T(8,128)(2,1)}, bf16[256,2048]{1,0:T(8,128)(2,1)S(1)}, u32[]{:S(2)}, u32[]{:S(2)}) collective-permute-start(bf16[256,2048]{1,0:T(8,128)(2,1)} %get-tuple-element.80), channel_id=1, source_target_pairs={{0,2},{2,0},{4,6},{6,4},{8,10},{10,8},{12,14},{14,12},{16,18},{18,... | collective-permute-start | bytes 3145736 | tf_op jit(solution)/shard_map/ppermute | solution.py:270
  190.9 10.7 %collective-permute-start.30 = (bf16[64,2048]{1,0:T(8,128)(2,1)S(1)}, bf16[64,2048]{1,0:T(8,128)(2,1)S(1)}, u32[]{:S(2)}, u32[]{:S(2)}) collective-permute-start(bf16[64,2048]{1,0:T(8,128)(2,1)S(1)} %add_convert_fusion.4), channel_id=1, source_target_pairs={{0,8},{2,10},{4,12},{6,14},{8,16},{10,18},{12,20},{14,22},{16,24},... | collective-permute-start | bytes 786440 | tf_op jit(solution)/shard_map/ppermute | solution.py:276
  (57 other events, 430.0 us)

commit v6 on v4

--- a/solution.py
+++ b/solution.py
@@ -102,6 +102,10 @@
     return jnp.dot(left, right, preferred_element_type=F32)
 
 
+def dot_t(left, right):
+    return lax.dot_general(left, right, CONTRACT, preferred_element_type=F32)
+
+
 def whole(array):
     return pl.BlockSpec(array.shape, lambda *_: (0,) * array.ndim)
 
@@ -135,56 +139,68 @@
 
 def plan_and_pack(expert, experts, capacity, chunks):
     tok_rows, width = chunks[0].shape
-    lanes = LANES
-    features = width - lanes
+    features = width - LANES
+    groups = 2
     length, room = TOGETHER * tok_rows, TOGETHER * capacity
-    groups = len(chunks) // TOGETHER
 
     def body(expert_ref, *refs):
-        mine_ref, theirs_ref, pick_ref, place_ref, rows_ref, sems = refs[len(chunks) :]
+        outs = refs[len(chunks) :]
+        mine_ref, theirs_ref, mine_lanes, theirs_lanes, pick_ref, place_ref = outs[:6]
+        rows_ref, sems = outs[6:]
         copies = load(refs[: len(chunks)], rows_ref, sems)
-        lane = lax.broadcasted_iota(jnp.int32, (length, lanes), 1)
+        lane = lax.broadcasted_iota(jnp.int32, (length, LANES), 1)
         row = lax.broadcasted_iota(jnp.int32, (length, length), 0)
         col = lax.broadcasted_iota(jnp.int32, (length, length), 1)
         before = (row >= col).astype(BF)
         slot = lax.broadcasted_iota(jnp.int32, (length, 2 * room), 1) % room
         wanted = (slot + 1).astype(F32)
-        for group in range(groups):
-            for copy in copies[group * TOGETHER : (group + 1) * TOGETHER]:
-                copy.wait()
-            held_rows = slice(group * length, (group + 1) * length)
-            shares = rows_ref[held_rows, features:].astype(F32)
+
+        def places(shares, first):
             routed = []
-            for index in (expert_ref[0], expert_ref[0] ^ 1):
+            for index in (first, first ^ 1):
                 held = (lane == index) | (lane == index + experts) | (lane == index + 2 * experts)
                 weight = jnp.sum(jnp.where(held, shares, 0.0), axis=1, keepdims=True)
                 routed.append(jnp.broadcast_to((weight > 0).astype(F32), (length, room)))
             routed = jnp.concatenate(routed, axis=1)
             rank = dot(before, routed.astype(BF))
-            place = jnp.where((rank == wanted) & (routed > 0), 1.0, 0.0)
-            place_ref[group] = place.astype(BF)
+            return jnp.where((rank == wanted) & (routed > 0), 1.0, 0.0)
+
+        for group in range(groups):
+            for copy in copies[group * TOGETHER : (group + 1) * TOGETHER]:
+                copy.wait()
+            held_rows = slice(group * length, (group + 1) * length)
+            lanes = rows_ref[held_rows, features:]
+            place = places(lanes.astype(F32), expert_ref[0])
+            if group == 0:
+                place_ref[:, : 2 * room] = place.astype(BF)
+                place_ref[:, 2 * room :] = places(lanes.astype(F32), expert_ref[0] ^ 2).astype(BF)
             pick = place.T.astype(BF)
             pick_ref[group] = pick
             here = slice(group * room, (group + 1) * room)
-            for at in range(0, width, 512):
-                cols = slice(at, min(at + 512, width))
+            packed = dot(pick, lanes).astype(BF)
+            mine_lanes[here] = packed[:room]
+            theirs_lanes[here] = packed[room:]
+            for at in range(0, features, 512):
+                cols = slice(at, at + 512)
                 packed = dot(pick, rows_ref[held_rows, cols]).astype(BF)
                 mine_ref[here, cols] = packed[:room]
                 theirs_ref[here, cols] = packed[room:]
 
-    rows = jax.ShapeDtypeStruct((groups * room, width), BF)
+    rows = jax.ShapeDtypeStruct((groups * room, features), BF)
+    lanes = jax.ShapeDtypeStruct((groups * room, LANES), BF)
     pick = jax.ShapeDtypeStruct((groups, 2 * room, length), BF)
-    place = jax.ShapeDtypeStruct((groups, length, 2 * room), BF)
+    place = jax.ShapeDtypeStruct((length, 4 * room), BF)
+    outs = (rows, rows, lanes, lanes, pick, place)
     return pl.pallas_call(
         body,
         grid_spec=pltpu.PrefetchScalarGridSpec(
             num_scalar_prefetch=1,
             grid=(1,),
             in_specs=[ANYWHERE] * len(chunks),
-            out_specs=[whole(a) for a in (rows, rows, pick, place)],
+            out_specs=[whole(a) for a in outs],
             scratch_shapes=landing(chunks),
         ),
-        out_shape=(rows, rows, pick, place),
+        out_shape=outs,
         compiler_params=params(1),
         cost_estimate=SMALL,
         name="plan_and_pack",
@@ -196,8 +212,8 @@
     groups, room, length = pick.shape[0], pick.shape[1] // 2, pick.shape[2]
 
     def body(pick_ref, *refs):
-        mine_ref, theirs_ref, rows_ref, sems = refs[-4:]
-        copies = load(refs[:-4], rows_ref, sems)
+        mine_ref, theirs_ref, rows_ref, sems = refs[len(chunks) :]
+        copies = load(refs[: len(chunks)], rows_ref, sems)
         for group in range(groups):
             for copy in copies[group * TOGETHER : (group + 1) * TOGETHER]:
                 copy.wait()
@@ -221,30 +237,178 @@
     )(pick, *chunks)
 
 
-def spread(place, mine, theirs, parts):
-    groups, length, slots_of = place.shape
-    room, features = slots_of // 2, mine.shape[1]
-    size = groups * length // parts
-
-    def body(place_ref, mine_ref, theirs_ref, *outs):
-        for group in reversed(range(groups)):
-            here = slice(group * room, (group + 1) * room)
-            for at in range(0, features, 512):
-                cols = slice(at, at + 512)
-                rows = jnp.concatenate([mine_ref[here, cols], theirs_ref[here, cols]], axis=0)
-                dense = dot(place_ref[group], rows).astype(BF)
-                for i in range(parts // groups):
-                    out = outs[group * (parts // groups) + i]
-                    out[:, cols] = dense[i * size : (i + 1) * size]
+def spread(place, parts):
+    length, slots_of = place.shape
+    room, features = parts[0].shape
+    size = length // TOGETHER
+
+    def body(place_ref, *refs):
+        outs = refs[len(parts) :]
+        for at in range(0, features, 512):
+            cols = slice(at, at + 512)
+            rows = jnp.concatenate([ref[:, cols] for ref in refs[: len(parts)]], axis=0)
+            dense = dot(place_ref[...], rows).astype(BF)
+            for i, out in enumerate(outs):
+                out[:, cols] = dense[i * size : (i + 1) * size]
 
     out = jax.ShapeDtypeStruct((size, features), BF)
     return pl.pallas_call(
         body,
-        out_shape=(out,) * parts,
+        out_shape=(out,) * TOGETHER,
         compiler_params=params(),
         cost_estimate=SMALL,
         name="spread",
-    )(place, mine, theirs)
+    )(place, *parts)
+
+
+def row_weight(expert, experts, *lane_refs):
+    lanes = jnp.concatenate([ref[...] for ref in lane_refs], axis=0).astype(F32)
+    lane = lax.broadcasted_iota(jnp.int32, lanes.shape, 1)
+    held = (lane == expert) | (lane == expert + experts) | (lane == expert + 2 * experts)
+    return jnp.sum(jnp.where(held, lanes, 0.0), axis=1, keepdims=True)
+
+
+def forward(expert, experts, mine, theirs, mine_lanes, theirs_lanes, weights, with_result):
+    w_gate, w_up, w_down = weights
+    part, features = mine.shape
+    hidden = w_gate.shape[2]
+    rows, block, wide = 2 * part, 256, 1024
+    first = hidden // block
+    steps = first + (features // wide if with_result else 0)
+
+    def body(expert_ref, mine_ref, theirs_ref, lanes_a, lanes_b, gate_ref, up_ref, *refs):
+        down_ref = refs[0] if with_result else None
+        act_ref, to_gate_ref, to_up_ref, weight_ref, *outs = refs[int(with_result) :]
+        step = pl.program_id(0)
+
+        @pl.when(step == 0)
+        def _():
+            weight = row_weight(expert_ref[0], experts, lanes_a, lanes_b)
+            weight_ref[...] = jnp.broadcast_to(weight, weight_ref.shape)
+
+        @pl.when(step < first)
+        def _():
+            x = jnp.concatenate([mine_ref[...], theirs_ref[...]], axis=0)
+            pre_gate = dot(x, gate_ref[0])
+            pre_up = dot(x, up_ref[0])
+            s = jax.nn.sigmoid(pre_gate)
+            silu = pre_gate * s
+            act_ref[:, pl.ds(pl.multiple_of(step * block, block), block)] = (
+                silu * pre_up
+            ).astype(BF)
+            to_gate_ref[...] = pre_up * s * (1.0 + pre_gate * (1.0 - s))
+            to_up_ref[...] = silu
+
+        if with_result:
+
+            @pl.when(step >= first)
+            def _():
+                out = dot(act_ref[...], down_ref[0])
+                out = (out * weight_ref[:, :1]).astype(BF)
+                near, far, theirs_out = outs
+                near[...] = out[: part // 2]
+                far[...] = out[part // 2 : part]
+                theirs_out[...] = out[part:]
+
+    def early(i):
+        return jnp.minimum(i, first - 1)
+
+    def late(i):
+        return jnp.maximum(i - first, 0)
+
+    act = jax.ShapeDtypeStruct((rows, hidden), BF)
+    factor = jax.ShapeDtypeStruct((rows, hidden), F32)
+    weight = jax.ShapeDtypeStruct((rows, LANES), F32)
+    outs = [act, factor, factor, weight]
+    factor_spec = pl.BlockSpec((rows, block), lambda i, e: (0, early(i)))
+    out_specs = [whole(act), factor_spec, factor_spec, whole(weight)]
+    columns = pl.BlockSpec((1, features, block), lambda i, e: (0, 0, early(i)))
+    in_specs = [whole(a) for a in (mine, theirs, mine_lanes, theirs_lanes)] + [columns, columns]
+    ins = [mine, theirs, mine_lanes, theirs_lanes, w_gate, w_up]
+    if with_result:
+        ins.append(w_down)
+        in_specs.append(pl.BlockSpec((1, hidden, wide), lambda i, e: (0, 0, late(i))))
+        for size in (part // 2, part // 2, part):
+            outs.append(jax.ShapeDtypeStruct((size, features), BF))
+            out_specs.append(pl.BlockSpec((size, wide), lambda i, e: (0, late(i))))
+    return pl.pallas_call(
+        body,
+        grid_spec=pltpu.PrefetchScalarGridSpec(
+            num_scalar_prefetch=1, grid=(steps,), in_specs=in_specs, out_specs=out_specs
+        ),
+        out_shape=outs,
+        compiler_params=params(1),
+        cost_estimate=SMALL,
+        name="forward",
+    )(expert, *ins)
+
+
+def backward(mine, theirs, weight, to_gate, to_up, weights, with_result):
+    w_gate, w_up, w_down = weights
+    part, features = mine.shape
+    rows, hidden = to_gate.shape
+    block, wide = 256, 1024
+    first = hidden // block
+    steps = first + (features // wide if with_result else 0)
+
+    def body(mine_ref, theirs_ref, weight_ref, to_gate_ref, to_up_ref, down_ref, *refs):
+        gate_ref, up_ref = refs[:2] if with_result else (None, None)
+        scaled_ref, d_gate_ref, d_up_ref, *outs = refs[2 * int(with_result) :]
+        step = pl.program_id(0)
+
+        @pl.when(step == 0)
+        def _():
+            cot = jnp.concatenate([mine_ref[...], theirs_ref[...]], axis=0)
+            scaled_ref[...] = (cot.astype(F32) * weight_ref[:, :1]).astype(BF)
+
+        @pl.when(step < first)
+        def _():
+            d_hidden = dot_t(scaled_ref[...], down_ref[0])
+            cols = pl.ds(pl.multiple_of(step * block, block), block)
+            d_gate_ref[:, cols] = (d_hidden * to_gate_ref[...]).astype(BF)
+            d_up_ref[:, cols] = (d_hidden * to_up_ref[...]).astype(BF)
+
+        if with_result:
+
+            @pl.when(step >= first)
+            def _():
+                out = dot_t(d_gate_ref[...], gate_ref[0]) + dot_t(d_up_ref[...], up_ref[0])
+                out = out.astype(BF)
+                near, far, theirs_out = outs
+                near[...] = out[: part // 2]
+                far[...] = out[part // 2 : part]
+                theirs_out[...] = out[part:]
+
+    def early(i):
+        return jnp.minimum(i, first - 1)
+
+    def late(i):
+        return jnp.maximum(i - first, 0)
+
+    scaled = jax.ShapeDtypeStruct((rows, features), BF)
+    grad = jax.ShapeDtypeStruct((rows, hidden), BF)
+    outs = [scaled, grad, grad]
+    out_specs = [whole(a) for a in outs]
+    factor_spec = pl.BlockSpec((rows, block), lambda i: (0, early(i)))
+    in_specs = [whole(a) for a in (mine, theirs, weight)] + [factor_spec] * 2
+    in_specs.append(pl.BlockSpec((1, block, features), lambda i: (0, early(i), 0)))
+    ins = [mine, theirs, weight, to_gate, to_up, w_down]
+    if with_result:
+        ins += [w_gate, w_up]
+        in_specs += [pl.BlockSpec((1, wide, hidden), lambda i: (0, late(i), 0))] * 2
+        for size in (part // 2, part // 2, part):
+            outs.append(jax.ShapeDtypeStruct((size, features), BF))
+            out_specs.append(pl.BlockSpec((size, wide), lambda i: (0, late(i))))
+    return pl.pallas_call(
+        body,
+        grid=(steps,),
+        in_specs=in_specs,
+        out_specs=out_specs,
+        out_shape=outs,
+        compiler_params=params(1),
+        cost_estimate=SMALL,
+        name="backward",
+    )(*ins)
 
 
 def split3(value):
@@ -267,7 +431,7 @@
     capacity = max(2, tok_rows * top_count * 4 // (3 * experts))
     expert = lax.axis_index("expert").astype(jnp.int32)
     replica = lax.axis_index("replica").astype(jnp.int32)
-    w_gate, w_up, w_down = w_gate[0], w_up[0], w_down[0]
+    weights = (w_gate, w_up, w_down)
 
     def to_core(rows):
         return lax.ppermute(rows, "expert", [(i, i ^ 1) for i in range(experts)])
@@ -275,8 +439,10 @@
     def to_x(rows):
         return lax.ppermute(rows, "expert", [(i, i ^ 2) for i in range(experts)])
 
-    def to_z(rows):
-        return lax.ppermute(rows, "expert", [(i, (i + 4) % experts) for i in range(experts)])
+    def to_z(rows, step):
+        return lax.ppermute(
+            rows, "expert", [(i, (i + 4 * step) % experts) for i in range(experts)]
+        )
 
     def to_y(rows):
         return lax.ppermute(rows, "replica", [(0, 1), (1, 0)])
@@ -285,87 +451,78 @@
     share = jnp.sum(jnp.where(chosen, gate_probs[:, :, None], 0.0), axis=1)
     pad = jnp.zeros((tok_rows, LANES - 3 * experts), BF)
 
-    token_near = [jnp.concatenate([tokens, *split3(share), pad], axis=1)]
-    for _ in range(TOGETHER - 1):
-        token_near.append(to_z(token_near[-1]))
-    token_far = [to_x(a) for a in token_near]
-    cot_near = [out_cot, to_z(after(out_cot, token_near[2]))]
-    for _ in range(TOGETHER - 2):
-        cot_near.append(to_z(cot_near[-1]))
-    cot_far = [to_x(a) for a in cot_near]
-    relay = [to_y(a) for pair in zip(token_near, token_far) for a in pair]
-    relay += [to_y(a) for pair in zip(cot_near, cot_far) for a in pair]
-    token_other = relay[0 : 2 * TOGETHER : 2] + relay[1 : 2 * TOGETHER : 2]
-    cot_other = relay[2 * TOGETHER :: 2] + relay[2 * TOGETHER + 1 :: 2]
-
-    def join(mine, theirs):
-        return jnp.concatenate([mine, to_core(theirs)], axis=0)
-
-    def enter(chunks, *earlier):
-        mine, theirs, pick, place = plan_and_pack(
-            expert.reshape(1), experts, capacity, chunks
+    token_own = jnp.concatenate([tokens, *split3(share), pad], axis=1)
+    token_near = [token_own] + [to_z(token_own, step) for step in range(1, TOGETHER)]
+    cot_source = after(out_cot, token_near[2])
+    cot_near = [out_cot] + [to_z(cot_source, step) for step in range(1, TOGETHER)]
+    token_sets = token_near + [to_x(a) for a in token_near]
+    cot_sets = cot_near + [to_x(a) for a in cot_near]
+    token_other = [to_y(a) for a in token_sets]
+    cot_other = [to_y(a) for a in cot_sets]
+    expert = expert.reshape(1)
+
+    def enter(chunks, with_result, before_plan, before_dots):
+        mine, theirs, mine_lanes, theirs_lanes, pick, place = plan_and_pack(
+            after(expert, *before_plan), experts, capacity, chunks
         )
-        theirs = after(to_core(theirs), *earlier)
-        x = jnp.concatenate([mine[:, :features], theirs[:, :features]], axis=0)
-        shares = jnp.concatenate([mine[:, features:], theirs[:, features:]], axis=0)
-        held = (jnp.arange(LANES) % experts == expert) & (jnp.arange(LANES) < 3 * experts)
-        weight = jnp.sum(jnp.where(held, shares.astype(F32), 0.0), axis=1, keepdims=True)
-        pre_gate, pre_up = dot(x, w_gate), dot(x, w_up)
-        activation = (jax.nn.silu(pre_gate) * pre_up).astype(BF)
-        return x, weight, pick, place, pre_gate, pre_up, activation
-
-    def leave(place, rows_of, *earlier):
-        half = place.shape[0] * place.shape[2] // 2
-        theirs = after(to_core(rows_of(slice(half, None))), *earlier)
-        parts = spread(place, rows_of(slice(0, half)), theirs, 2 * TOGETHER)
-        near, far = parts[:TOGETHER], parts[TOGETHER:]
-        totals = []
-        for s in (*range(1, TOGETHER), 0):
-            part = near[s].astype(F32) + to_x(far[s]).astype(F32)
-            if totals:
-                part = part + to_z(totals[-1]).astype(F32)
-            totals.append(part.astype(BF))
-        return totals, parts
-
-    def grads(x, activation, cot, d_gate, d_up):
-        x = lax.dynamic_slice_in_dim(x, replica * (features // 2), features // 2, 1)
-        activation = lax.dynamic_slice_in_dim(activation, replica * (hidden // 2), hidden // 2, 1)
-        return outer_sum(x, d_gate), outer_sum(x, d_up), outer_sum(activation, cot)
-
-    chunks = after([*token_near, *token_far], relay[0], relay[1], relay[2], cot_near[1])
-    x, weight, pick, place, pre_gate, pre_up, activation = enter(
-        chunks, relay[3], cot_near[2], cot_far[0]
-    )
-    activation = after(activation, relay[4], cot_near[3], cot_far[1])
-    totals, sent = leave(
-        place,
-        lambda rows: (dot(activation[rows], w_down) * weight[rows]).astype(BF),
-        relay[5],
-        cot_far[2],
-    )
-    cot_chunks = after([*cot_near, *cot_far], sent, relay[6])
-    cot = (join(*pack(pick, cot_chunks)).astype(F32) * weight).astype(BF)
-    cot = after(cot, relay[7])
-    d_gate, d_up = hidden_grads(cot, pre_gate, pre_up, w_down)
-    d_gate, d_up = after((d_gate, d_up), relay[8])
-    grad_totals, sent = leave(
-        place,
-        lambda rows: input_rows(d_gate[rows], d_up[rows], w_gate, w_up),
-        relay[9],
-        totals[1],
-    )
-    own = x, activation, cot, d_gate, d_up
-
-    x, weight, pick, _, pre_gate, pre_up, activation = enter(
-        after(token_other, sent, relay[10], totals[2]), relay[11], totals[3]
-    )
-    own = grads(*after(own, activation, relay[12], grad_totals[1]))
-    cot_chunks = after(cot_other, own, grad_totals[2])
-    cot = (join(*pack(pick, cot_chunks)).astype(F32) * weight).astype(BF)
-    d_gate, d_up = hidden_grads(cot, pre_gate, pre_up, w_down)
-    other = grads(x, activation, cot, d_gate, d_up)
+        theirs = after(to_core(theirs), *before_dots)
+        act, to_gate, to_up, weight, *results = forward(
+            expert, experts, mine, theirs, mine_lanes, to_core(theirs_lanes), weights, with_result
+        )
+        return (mine, theirs), pick, place, act, to_gate, to_up, weight, results
+
+    def enter_cot(pick, chunks, weight, to_gate, to_up, with_result, *before_dots):
+        mine, theirs = pack(pick, chunks)
+        theirs = after(to_core(theirs), *before_dots)
+        return backward(mine, theirs, weight, to_gate, to_up, weights, with_result)
+
+    def leave(results):
+        near, far, theirs = results
+        theirs = to_core(theirs)
+        half = near.shape[0]
+        return near, theirs[:half], to_x(far), to_x(theirs[half:])
+
+    def home(place, parts):
+        own, *others = spread(place, parts)
+        return [own] + [to_z(a, -step) for step, a in enumerate(others, 1)]
+
+    def total(chunks):
+        return sum(a.astype(F32) for a in chunks).astype(BF)
+
+    def grads(rows, act, cot, d_gate, d_up):
+        x = jnp.concatenate(
+            [
+                lax.dynamic_slice_in_dim(a, replica * (features // 2), features // 2, 1)
+                for a in rows
+            ],
+            axis=0,
+        )
+        act = lax.dynamic_slice_in_dim(act, replica * (hidden // 2), hidden // 2, 1)
+        return outer_sum(x, d_gate), outer_sum(x, d_up), outer_sum(act, cot)
+
+    own_rows, pick, place, own_act, to_gate, to_up, weight, results = enter(
+        token_sets, True, token_other + [cot_other[0]] + cot_sets[1:6], [*cot_sets[6:], cot_other[4]]
+    )
+    parts = leave(results)
+    *own_grads, near, far, theirs = enter_cot(
+        after(pick, results[0], cot_other[1]),
+        cot_sets, weight, to_gate, to_up, True, cot_other[5],
+    )
+    chunks = home(after(place, near), parts)
+    parts = leave((near, far, theirs))
+
+    rows, pick, _, act, to_gate, to_up, weight, _ = enter(
+        token_other, False, (chunks[0], cot_other[2]), (cot_other[6], chunks[1])
+    )
+    grad_chunks = home(after(place, act, cot_other[3], chunks[2]), parts)
+    own_grads = after(tuple(own_grads), grad_chunks[0], cot_other[7], chunks[3])
+    own = grads(own_rows, own_act, *own_grads)
+    scaled, d_gate, d_up = enter_cot(
+        after(pick, *own, grad_chunks[1]), cot_other, weight, to_gate, to_up, False, grad_chunks[2]
+    )
+    other = grads(rows, act, scaled, d_gate, d_up)
     grad_gate, grad_up, grad_down = ((a + b).astype(BF)[None] for a, b in zip(own, other))
-    return (totals[-1], grad_totals[-1], grad_gate, grad_up, grad_down)
+    return (total(chunks), total(grad_chunks), grad_gate, grad_up, grad_down)
 
 
 def dense_fits(mesh):

time: 236 us -> 256 us (1.085)
  Pallas kernels: 24.3 us -> 65.6 us
  matrix products: 38.9 us -> 12.9 us
  starting transfers between devices: 37.1 us -> 62.5 us
  other arithmetic: 14.2 us -> 4.39 us
  waiting for transfers between devices: 108 us -> 99.1 us
    pallas_call x2 -> x6, Pallas kernels: 6.82 us -> 47.7 us  [the longest x2 20.7 us: backward(): pl.pallas_call(body, grid=(steps,), in_specs=in_specs, out_specs=out_spec...]
    ppermute x12, starting transfers between devices: 3.44 us -> 29.7 us  [to_z(): lax.ppermute(rows, 'expert', [(i, (i + 4 * step) % experts) for i in rang...]
    dot_general x12 -> x0, matrix products: 25.7 us -> none  [the longest x6 12.8 us: dot(): return jnp.dot(left, right, preferred_element_type=F32)]
    ppermute x12, waiting for transfers between devices: 50.6 us -> 40 us  [to_z(): lax.ppermute(rows, 'expert', [(i, (i + 4 * step) % experts) for i in rang...]
    convert_element_type x9 -> x2, other arithmetic: 10.3 us -> 3.65 us  [total(): return sum((a.astype(F32) for a in chunks)).astype(BF)]
    ppermute x16, waiting for transfers between devices: 24.3 us -> 29.3 us  [to_y(): return lax.ppermute(rows, 'replica', [(0, 1), (1, 0)])]
    ppermute x16 -> x12, waiting for transfers between devices: 32.9 us -> 28.5 us  [to_x(): return lax.ppermute(rows, 'expert', [(i, i ^ 2) for i in range(experts)])]
    concatenate x1 -> x0, other arithmetic: 2.79 us -> none  [enter(): x = jnp.concatenate([mine[:, :features], theirs[:, :features]], axis=0)]
  transfers between devices with their start and end apart: 50 -> 48, of which waited for: 24 -> 20; matrix products, arithmetic and copies ran while one was open for 18% -> 5% of each run, Pallas kernels for 5% -> 19%
where the time goes in v6:
time: 256 us; the launch traced here: 255 us
  waiting for transfers between devices  99.1 us (39%)
  Pallas kernels  65.6 us (26%)
  starting transfers between devices  62.5 us (24%)
  matrix products  12.9 us (5%)
  local copies, waits for them, and re-layouts  9.63 us (4%)
  other arithmetic  4.39 us (2%)
    ppermute x12, waiting for transfers between devices, to_z(): lax.ppermute(rows, 'expert', [(i, (i + 4 * step) % experts) for i in rang...  40 us
    ppermute x12, starting transfers between devices, to_z(): lax.ppermute(rows, 'expert', [(i, (i + 4 * step) % experts) for i in rang...  29.7 us
    ppermute x16, waiting for transfers between devices, to_y(): return lax.ppermute(rows, 'replica', [(0, 1), (1, 0)])  29.3 us
    ppermute x12, waiting for transfers between devices, to_x(): return lax.ppermute(rows, 'expert', [(i, i ^ 2) for i in range(experts)])  28.5 us
    pallas_call x2, Pallas kernels, backward(): pl.pallas_call(body, grid=(steps,), in_specs=in_specs, out_specs=out_spec...  20.7 us
    pallas_call x2, Pallas kernels, forward(): pl.pallas_call(body, grid_spec=pltpu.PrefetchScalarGridSpec(num_scalar_pr...  20.4 us
    ppermute x16, starting transfers between devices, to_y(): return lax.ppermute(rows, 'replica', [(0, 1), (1, 0)])  16.8 us
    ppermute x12, starting transfers between devices, to_x(): return lax.ppermute(rows, 'expert', [(i, i ^ 2) for i in range(experts)])  15.2 us
  transfers between devices with their start and end apart: 48, of which 20 were waited for; matrix products, arithmetic and copies ran while one was open for 5% of the time, Pallas kernels for 19%

profile of v6, /device:TPU:0, one launch (start us, length us, event | category | flops | bytes accessed | tf_op | source)
XLA Modules:
  0.0 255.3 jit_solution(11065850193683349866)
XLA Ops:
  12.6 15.4 %collective-permute-done.3.refs_2_ = bf16[64,2176]{1,0:T(8,128)(2,1)S(1)} collective-permute-done((bf16[64,2176]{1,0:T(8,128)(2,1)S(1)}, bf16[64,2176]{1,0:T(8,128)(2,1)S(1)}, u32[]{:S(2)}, u32[]{:S(2)}) %collective-permute-start.3) | collective-permute-done | bytes 278560 | tf_op jit(solution)/shard_map/ppermute | solution.py:443
  33.4 11.3 %collective-permute-start.16 = (bf16[64,2048]{1,0:T(8,128)(2,1)}, bf16[64,2048]{1,0:T(8,128)(2,1)}, u32[]{:S(2)}, u32[]{:S(2)}) collective-permute-start(bf16[64,2048]{1,0:T(8,128)(2,1)} %refs_0_.4), channel_id=1, source_target_pairs={{0,8},{2,10},{4,12},{6,14},{8,16},{10,18},{12,20},{14,22},{16,24},... | collective-permute-start | bytes 786440 | tf_op jit(solution)/shard_map/ppermute | solution.py:443
  46.2 9.0 %collective-permute-done.17.refs_2_ = bf16[64,2048]{1,0:T(8,128)(2,1)S(1)} collective-permute-done((bf16[64,2048]{1,0:T(8,128)(2,1)}, bf16[64,2048]{1,0:T(8,128)(2,1)S(1)}, u32[]{:S(2)}, u32[]{:S(2)}) %collective-permute-start.17) | collective-permute-done | bytes 262176 | tf_op jit(solution)/shard_map/ppermute | solution.py:443
  59.7 5.2 %collective-permute-done.11.refs_6_ = bf16[64,2176]{1,0:T(8,128)(2,1)} collective-permute-done((bf16[64,2176]{1,0:T(8,128)(2,1)S(1)}, bf16[64,2176]{1,0:T(8,128)(2,1)}, u32[]{:S(2)}, u32[]{:S(2)}) %collective-permute-start.11) | collective-permute-done | bytes 278560 | tf_op jit(solution)/shard_map/ppermute | solution.py:440
  65.3 3.4 %collective-permute-done.9.refs_5_ = bf16[64,2176]{1,0:T(8,128)(2,1)} collective-permute-done((bf16[64,2176]{1,0:T(8,128)(2,1)}, bf16[64,2176]{1,0:T(8,128)(2,1)}, u32[]{:S(2)}, u32[]{:S(2)}) %collective-permute-start.9) | collective-permute-done | bytes 278560 | tf_op jit(solution)/shard_map/ppermute | solution.py:440
  78.8 6.0 %collective-permute-done.12.refs_6_ = bf16[64,2176]{1,0:T(8,128)(2,1)S(1)} collective-permute-done((bf16[64,2176]{1,0:T(8,128)(2,1)}, bf16[64,2176]{1,0:T(8,128)(2,1)S(1)}, u32[]{:S(2)}, u32[]{:S(2)}) %collective-permute-start.12) | collective-permute-done | bytes 278560 | tf_op jit(solution)/shard_map/ppermute | solution.py:448
  88.1 4.4 %plan_and_pack.2 = (bf16[256,2048]{1,0:T(8,128)(2,1)}, bf16[256,2048]{1,0:T(8,128)(2,1)}, bf16[256,128]{1,0:T(8,128)(2,1)}, bf16[256,128]{1,0:T(8,128)(2,1)}, bf...) custom-call(s32[1]{0:T(128)} %bitcast.expert_ref, bf16[64,2176]{1,0:T(8,128)(2,1)} %copy-done.7, ...), custom_call_target="tpu_custom_call" | custom-call | flops 1 | bytes 1 | tf_op jit(solution)/shard_map/plan_and_pack/pallas_call | solution.py:194
  96.7 5.1 %collective-permute-done.24.refs_4_ = bf16[64,2048]{1,0:T(8,128)(2,1)S(1)} collective-permute-done((bf16[64,2048]{1,0:T(8,128)(2,1)S(1)}, bf16[64,2048]{1,0:T(8,128)(2,1)S(1)}, u32[]{:S(2)}, u32[]{:S(2)}) %collective-permute-start.24) | collective-permute-done | bytes 262176 | tf_op jit(solution)/shard_map/ppermute | solution.py:448
  102.2 4.8 %collective-permute-done.22.refs_6_ = bf16[64,2048]{1,0:T(8,128)(2,1)S(1)} collective-permute-done((bf16[64,2048]{1,0:T(8,128)(2,1)S(1)}, bf16[64,2048]{1,0:T(8,128)(2,1)S(1)}, u32[]{:S(2)}, u32[]{:S(2)}) %collective-permute-start.22) | collective-permute-done | bytes 262176 | tf_op jit(solution)/shard_map/ppermute | solution.py:440
  108.1 11.9 %forward.2 = (bf16[512,768]{1,0:T(8,128)(2,1)}, f32[512,768]{1,0:T(8,128)}, f32[512,768]{1,0:T(8,128)}, f32[512,128]{1,0:T(8,128)}, bf16[128,2048]{1,0:T(8,128)(...) custom-call(s32[1]{0:T(128)} %bitcast.expert_ref, bf16[256,2048]{1,0:T(8,128)(2,1)} %get-tuple-element.66.mine_ref, ...), custom_call_target="tpu_custom_call" | custom-call | flops 1 | bytes 1 | tf_op jit(solution)/shard_map/forward/pallas_call | solution.py:334
  120.2 4.5 %pack.2 = (bf16[256,2048]{1,0:T(8,128)(2,1)}, bf16[256,2048]{1,0:T(8,128)(2,1)}) custom-call(bf16[2,256,256]{2,1,0:T(8,128)(2,1)} %get-tuple-element.72.pick_ref, bf16[64,2048]{1,0:T(8,128)(2,1)} %refs_0_.4, bf16[64,2048]{1,0:T(8,128)(2,1)} %collective-permute-done.16.refs_1_, bf16[64,2048]{1,0:T(8,128)(2,1)} %copy-done.37, bf16[64,2048]{1,0:T(8,128)(2,1)} %copy-done.30, ...), custom_call_target="tpu_custom_call" | custom-call | flops 1 | bytes 1 | tf_op jit(solution)/shard_map/pack/pallas_call | solution.py:229
  128.4 5.5 %collective-permute-done.28.refs_5_ = bf16[64,2048]{1,0:T(8,128)(2,1)S(1)} collective-permute-done((bf16[64,2048]{1,0:T(8,128)(2,1)}, bf16[64,2048]{1,0:T(8,128)(2,1)S(1)}, u32[]{:S(2)}, u32[]{:S(2)}) %collective-permute-start.28) | collective-permute-done | bytes 262176 | tf_op jit(solution)/shard_map/ppermute | solution.py:448
  134.9 12.9 %backward.2 = (bf16[512,2048]{1,0:T(8,128)(2,1)}, bf16[512,768]{1,0:T(8,128)(2,1)}, bf16[512,768]{1,0:T(8,128)(2,1)}, bf16[128,2048]{1,0:T(8,128)(2,1)}, bf16[12...) custom-call(bf16[256,2048]{1,0:T(8,128)(2,1)} %get-tuple-element.73.mine_ref, bf16[256,2048]{1,0:T(8,128)(2,1)} %copy-done.8, ...), custom_call_target="tpu_custom_call" | custom-call | flops 1 | bytes 1 | tf_op jit(solution)/shard_map/backward/pallas_call | solution.py:402
  151.8 11.3 %collective-permute-done.31.refs_3_ = bf16[128,2048]{1,0:T(8,128)(2,1)S(1)} collective-permute-done((bf16[128,2048]{1,0:T(8,128)(2,1)S(1)}, bf16[128,2048]{1,0:T(8,128)(2,1)S(1)}, u32[]{:S(2)}, u32[]{:S(2)}) %collective-permute-start.31) | collective-permute-done | bytes 524320 | tf_op jit(solution)/shard_map/ppermute | solution.py:440
  167.2 4.4 %plan_and_pack.3 = (bf16[256,2048]{1,0:T(8,128)(2,1)}, bf16[256,2048]{1,0:T(8,128)(2,1)}, bf16[256,128]{1,0:T(8,128)(2,1)}, bf16[256,128]{1,0:T(8,128)(2,1)}, bf...) custom-call(s32[1]{0:T(128)} %bitcast.expert_ref, bf16[64,2176]{1,0:T(8,128)(2,1)} %copy-done.17, ...), custom_call_target="tpu_custom_call" | custom-call | flops 1 | bytes 1 | tf_op jit(solution)/shard_map/plan_and_pack/pallas_call | solution.py:194
  182.4 3.6 %collective-permute-done.37.refs_6_ = bf16[64,2048]{1,0:T(8,128)(2,1)S(1)} collective-permute-done((bf16[64,2048]{1,0:T(8,128)(2,1)S(1)}, bf16[64,2048]{1,0:T(8,128)(2,1)S(1)}, u32[]{:S(2)}, u32[]{:S(2)}) %collective-permute-start.37) | collective-permute-done | bytes 262176 | tf_op jit(solution)/shard_map/ppermute | solution.py:448
  189.6 3.5 %collective-permute-start.33 = (bf16[64,2048]{1,0:T(8,128)(2,1)}, bf16[64,2048]{1,0:T(8,128)(2,1)S(1)}, u32[]{:S(2)}, u32[]{:S(2)}) collective-permute-start(bf16[64,2048]{1,0:T(8,128)(2,1)} %get-tuple-element.85), channel_id=1, source_target_pairs={{0,16},{2,18},{4,20},{6,22},{8,24},{10,26},{12,28},{14,30},{16,0},... | collective-permute-start | bytes 786440 | tf_op jit(solution)/shard_map/ppermute | solution.py:443
  194.8 8.5 %forward.3 = (bf16[512,768]{1,0:T(8,128)(2,1)}, f32[512,768]{1,0:T(8,128)}, f32[512,768]{1,0:T(8,128)}, f32[512,128]{1,0:T(8,128)}) custom-call(s32[1]{0:T(128)} %bitcast.expert_ref, bf16[256,2048]{1,0:T(8,128)(2,1)} %get-tuple-element.88.mine_ref, bf16[256,2048]{1,0:T(8,128)(2,1)} %copy-done.4, bf16[256,128]{1,0:T(8,128)(2,1)} %get-tuple-element.91.lanes_a, ...), custom_call_target="tpu_custom_call" | custom-call | flops 1 | bytes 1 | tf_op jit(solution)/shard_map/forward/pallas_call | solution.py:334
  203.2 7.6 %collective-permute-done.33 = bf16[64,2048]{1,0:T(8,128)(2,1)S(1)} collective-permute-done((bf16[64,2048]{1,0:T(8,128)(2,1)}, bf16[64,2048]{1,0:T(8,128)(2,1)S(1)}, u32[]{:S(2)}, u32[]{:S(2)}) %collective-permute-start.33) | collective-permute-done | bytes 262176 | tf_op jit(solution)/shard_map/ppermute | solution.py:443
  210.9 3.3 %spread.3 = (bf16[64,2048]{1,0:T(8,128)(2,1)}, bf16[64,2048]{1,0:T(8,128)(2,1)}, bf16[64,2048]{1,0:T(8,128)(2,1)}, bf16[64,2048]{1,0:T(8,128)(2,1)}) custom-call(bf16[256,512]{1,0:T(8,128)(2,1)} %get-tuple-element.94.place_ref, bf16[128,2048]{1,0:T(8,128)(2,1)} %get-tuple-element.79.refs_0_, bf16[128,2048]{1,0:T(8,128)(2,1)} %get-tuple-element.120.refs_1_, ...), custom_call_target="tpu_custom_call" | custom-call | flops 1 | bytes 1 | tf_op jit(solution)/shard_map/spread/pallas_call | solution.py:255
  223.4 4.5 %pack.3 = (bf16[256,2048]{1,0:T(8,128)(2,1)}, bf16[256,2048]{1,0:T(8,128)(2,1)}) custom-call(bf16[2,256,256]{2,1,0:T(8,128)(2,1)} %get-tuple-element.109.pick_ref, bf16[64,2048]{1,0:T(8,128)(2,1)} %copy-done.28, bf16[64,2048]{1,0:T(8,128)(2,1)} %copy-done.33, bf16[64,2048]{1,0:T(8,128)(2,1)} %copy-done.40, bf16[64,2048]{1,0:T(8,128)(2,1)} %copy-done.46, ...), custom_call_target="tpu_custom_call" | custom-call | flops 1 | bytes 1 | tf_op jit(solution)/shard_map/pack/pallas_call | solution.py:229
  230.9 6.3 %collective-permute-done.44 = bf16[64,2048]{1,0:T(8,128)(2,1)} collective-permute-done((bf16[64,2048]{1,0:T(8,128)(2,1)}, bf16[64,2048]{1,0:T(8,128)(2,1)}, u32[]{:S(2)}, u32[]{:S(2)}) %collective-permute-start.44) | collective-permute-done | bytes 262176 | tf_op jit(solution)/shard_map/ppermute | solution.py:443
  239.0 7.9 %backward.3 = (bf16[512,2048]{1,0:T(8,128)(2,1)}, bf16[512,768]{1,0:T(8,128)(2,1)}, bf16[512,768]{1,0:T(8,128)(2,1)}) custom-call(bf16[256,2048]{1,0:T(8,128)(2,1)} %get-tuple-element.110.mine_ref, bf16[256,2048]{1,0:T(8,128)(2,1)} %collective-permute-done.47.theirs_ref, f32[512,128]{1,0:T(8,128)} %get-tuple-element.113.weight_ref, ...), custom_call_target="tpu_custom_call" | custom-call | flops 1 | bytes 1 | tf_op jit(solution)/shard_map/backward/pallas_call | solution.py:402
  246.9 3.8 %fusion = bf16[1,384,2048]{2,1,0:T(8,128)(2,1)} fusion(f32[384,2048]{1,0:T(8,128)S(1)} %fusion.6, bf16[512,2048]{1,0:T(8,128)(2,1)} %get-tuple-element.118, bf16[512,768]{1,0:T(8,128)(2,1)S(1)} %copy-done.54, s32[]{:T(128)S(6)} %select_n.16), kind=kOutput, calls=%fused_computation.3 | convolution fusion | flops 806879232 | bytes 7208964 | tf_op jit(solution)/shard_map/dot_general | solution.py:55
  (229 shorter events, 90.0 us)
Async XLA Ops:
  5.7 22.3 %collective-permute-start.3 = (bf16[64,2176]{1,0:T(8,128)(2,1)S(1)}, bf16[64,2176]{1,0:T(8,128)(2,1)S(1)}, u32[]{:S(2)}, u32[]{:S(2)}) collective-permute-start(bf16[64,2176]{1,0:T(8,128)(2,1)S(1)} %concatenate.9.refs_0_), channel_id=1, source_target_pairs={{0,16},{2,18},{4,20},{6,22},{8,24},{10,26},{12,28},{14,30},{16,0},... | collective-permute-start | bytes 835592 | tf_op jit(solution)/shard_map/ppermute | solution.py:443
  8.3 22.5 %collective-permute-start.7 = (bf16[64,2176]{1,0:T(8,128)(2,1)S(1)}, bf16[64,2176]{1,0:T(8,128)(2,1)S(1)}, u32[]{:S(2)}, u32[]{:S(2)}) collective-permute-start(bf16[64,2176]{1,0:T(8,128)(2,1)S(1)} %concatenate.9.refs_0_), channel_id=1, source_target_pairs={{0,4},{2,6},{4,0},{6,2},{8,12},{10,14},{12,8},{14,10},{16,20},{18,... | collective-permute-start | bytes 835592 | tf_op jit(solution)/shard_map/ppermute | solution.py:440
  9.8 22.6 %collective-permute-start.5 = (bf16[64,2176]{1,0:T(8,128)(2,1)S(1)}, bf16[64,2176]{1,0:T(8,128)(2,1)S(1)}, u32[]{:S(2)}, u32[]{:S(2)}) collective-permute-start(bf16[64,2176]{1,0:T(8,128)(2,1)S(1)} %concatenate.9.refs_0_), channel_id=1, source_target_pairs={{0,24},{2,26},{4,28},{6,30},{8,0},{10,2},{12,4},{14,6},{16,8},{18,... | collective-permute-start | bytes 835592 | tf_op jit(solution)/shard_map/ppermute | solution.py:443
  11.2 22.3 %collective-permute-start.1 = (bf16[64,2176]{1,0:T(8,128)(2,1)S(1)}, bf16[64,2176]{1,0:T(8,128)(2,1)}, u32[]{:S(2)}, u32[]{:S(2)}) collective-permute-start(bf16[64,2176]{1,0:T(8,128)(2,1)S(1)} %concatenate.9.refs_0_), channel_id=1, source_target_pairs={{0,8},{2,10},{4,12},{6,14},{8,16},{10,18},{12,20},{14,22},{16,24},... | collective-permute-start | bytes 835592 | tf_op jit(solution)/shard_map/ppermute | solution.py:443
  28.0 18.2 %collective-permute-start.18 = (bf16[64,2048]{1,0:T(8,128)(2,1)}, bf16[64,2048]{1,0:T(8,128)(2,1)S(1)}, u32[]{:S(2)}, u32[]{:S(2)}) collective-permute-start(bf16[64,2048]{1,0:T(8,128)(2,1)} %refs_0_.4), channel_id=1, source_target_pairs={{0,24},{2,26},{4,28},{6,30},{8,0},{10,2},{12,4},{14,6},{16,8},{18,... | collective-permute-start | bytes 786440 | tf_op jit(solution)/shard_map/ppermute | solution.py:443
  30.8 26.4 %collective-permute-start.8 = (bf16[64,2176]{1,0:T(8,128)(2,1)S(1)}, bf16[64,2176]{1,0:T(8,128)(2,1)S(1)}, u32[]{:S(2)}, u32[]{:S(2)}) collective-permute-start(bf16[64,2176]{1,0:T(8,128)(2,1)S(1)} %collective-permute-done.7.refs_4_), channel_id=1, source_target_pairs={{0,1},{1,0},{2,3},{3,2},{4,5},{5,4},{6,7},{7,6},{8,9},{9,8},{10,11... | collective-permute-start | bytes 835592 | tf_op jit(solution)/shard_map/ppermute | solution.py:448
  32.4 22.7 %collective-permute-start.17 = (bf16[64,2048]{1,0:T(8,128)(2,1)}, bf16[64,2048]{1,0:T(8,128)(2,1)S(1)}, u32[]{:S(2)}, u32[]{:S(2)}) collective-permute-start(bf16[64,2048]{1,0:T(8,128)(2,1)} %refs_0_.4), channel_id=1, source_target_pairs={{0,16},{2,18},{4,20},{6,22},{8,24},{10,26},{12,28},{14,30},{16,0},... | collective-permute-start | bytes 786440 | tf_op jit(solution)/shard_map/ppermute | solution.py:443
  33.4 23.3 %collective-permute-start.16 = (bf16[64,2048]{1,0:T(8,128)(2,1)}, bf16[64,2048]{1,0:T(8,128)(2,1)}, u32[]{:S(2)}, u32[]{:S(2)}) collective-permute-start(bf16[64,2048]{1,0:T(8,128)(2,1)} %refs_0_.4), channel_id=1, source_target_pairs={{0,8},{2,10},{4,12},{6,14},{8,16},{10,18},{12,20},{14,22},{16,24},... | collective-permute-start | bytes 786440 | tf_op jit(solution)/shard_map/ppermute | solution.py:443
  59.3 19.5 %collective-permute-start.14 = (bf16[64,2176]{1,0:T(8,128)(2,1)}, bf16[64,2176]{1,0:T(8,128)(2,1)S(1)}, u32[]{:S(2)}, u32[]{:S(2)}) collective-permute-start(bf16[64,2176]{1,0:T(8,128)(2,1)} %collective-permute-done.13.refs_7_), channel_id=1, source_target_pairs={{0,1},{1,0},{2,3},{3,2},{4,5},{5,4},{6,7},{7,6},{8,9},{9,8},{10,11... | collective-permute-start | bytes 835592 | tf_op jit(solution)/shard_map/ppermute | solution.py:448
  64.9 19.8 %collective-permute-start.12 = (bf16[64,2176]{1,0:T(8,128)(2,1)}, bf16[64,2176]{1,0:T(8,128)(2,1)S(1)}, u32[]{:S(2)}, u32[]{:S(2)}) collective-permute-start(bf16[64,2176]{1,0:T(8,128)(2,1)} %collective-permute-done.11.refs_6_), channel_id=1, source_target_pairs={{0,1},{1,0},{2,3},{3,2},{4,5},{5,4},{6,7},{7,6},{8,9},{9,8},{10,11... | collective-permute-start | bytes 835592 | tf_op jit(solution)/shard_map/ppermute | solution.py:448
  68.8 19.3 %collective-permute-start.10 = (bf16[64,2176]{1,0:T(8,128)(2,1)}, bf16[64,2176]{1,0:T(8,128)(2,1)S(1)}, u32[]{:S(2)}, u32[]{:S(2)}) collective-permute-start(bf16[64,2176]{1,0:T(8,128)(2,1)} %collective-permute-done.9.refs_5_), channel_id=1, source_target_pairs={{0,1},{1,0},{2,3},{3,2},{4,5},{5,4},{6,7},{7,6},{8,9},{9,8},{10,11... | collective-permute-start | bytes 835592 | tf_op jit(solution)/shard_map/ppermute | solution.py:448
  95.1 25.1 %collective-permute-start.26 = (bf16[64,2048]{1,0:T(8,128)(2,1)}, bf16[64,2048]{1,0:T(8,128)(2,1)S(1)}, u32[]{:S(2)}, u32[]{:S(2)}) collective-permute-start(bf16[64,2048]{1,0:T(8,128)(2,1)} %collective-permute-done.16.refs_1_), channel_id=1, source_target_pairs={{0,1},{1,0},{2,3},{3,2},{4,5},{5,4},{6,7},{7,6},{8,9},{9,8},{10,11... | collective-permute-start | bytes 786440 | tf_op jit(solution)/shard_map/ppermute | solution.py:448
  124.8 23.0 %collective-permute-start.29 = (bf16[256,2048]{1,0:T(8,128)(2,1)S(1)}, bf16[256,2048]{1,0:T(8,128)(2,1)S(1)}, u32[]{:S(2)}, u32[]{:S(2)}) collective-permute-start(bf16[256,2048]{1,0:T(8,128)(2,1)S(1)} %copy-done.58), channel_id=1, source_target_pairs={{0,2},{2,0},{4,6},{6,4},{8,10},{10,8},{12,14},{14,12},{16,18},{18,... | collective-permute-start | bytes 3145736 | tf_op jit(solution)/shard_map/ppermute | solution.py:437
  126.9 24.9 %collective-permute-start.30 = (bf16[128,2048]{1,0:T(8,128)(2,1)S(1)}, bf16[128,2048]{1,0:T(8,128)(2,1)S(1)}, u32[]{:S(2)}, u32[]{:S(2)}) collective-permute-start(bf16[128,2048]{1,0:T(8,128)(2,1)S(1)} %copy-done.61), channel_id=1, source_target_pairs={{0,4},{2,6},{4,0},{6,2},{8,12},{10,14},{12,8},{14,10},{16,20},{18,... | collective-permute-start | bytes 1572872 | tf_op jit(solution)/shard_map/ppermute | solution.py:440
  147.8 27.5 %collective-permute-start.40 = (bf16[256,2048]{1,0:T(8,128)(2,1)}, bf16[256,2048]{1,0:T(8,128)(2,1)S(1)}, u32[]{:S(2)}, u32[]{:S(2)}) collective-permute-start(bf16[256,2048]{1,0:T(8,128)(2,1)} %get-tuple-element.95), channel_id=1, source_target_pairs={{0,2},{2,0},{4,6},{6,4},{8,10},{10,8},{12,14},{14,12},{16,18},{18,... | collective-permute-start | bytes 3145736 | tf_op jit(solution)/shard_map/ppermute | solution.py:437
  150.2 16.9 %collective-permute-start.35 = (bf16[64,2048]{1,0:T(8,128)(2,1)S(1)}, bf16[64,2048]{1,0:T(8,128)(2,1)S(1)}, u32[]{:S(2)}, u32[]{:S(2)}) collective-permute-start(bf16[64,2048]{1,0:T(8,128)(2,1)S(1)} %copy-done.39), channel_id=1, source_target_pairs={{0,1},{1,0},{2,3},{3,2},{4,5},{5,4},{6,7},{7,6},{8,9},{9,8},{10,11... | collective-permute-start | bytes 786440 | tf_op jit(solution)/shard_map/ppermute | solution.py:448
  171.6 21.5 %collective-permute-start.36 = (bf16[256,2048]{1,0:T(8,128)(2,1)}, bf16[256,2048]{1,0:T(8,128)(2,1)S(1)}, u32[]{:S(2)}, u32[]{:S(2)}) collective-permute-start(bf16[256,2048]{1,0:T(8,128)(2,1)} %get-tuple-element.89), channel_id=1, source_target_pairs={{0,2},{2,0},{4,6},{6,4},{8,10},{10,8},{12,14},{14,12},{16,18},{18,... | collective-permute-start | bytes 3145736 | tf_op jit(solution)/shard_map/ppermute | solution.py:437
  173.8 37.1 %collective-permute-start.41 = (bf16[128,2048]{1,0:T(8,128)(2,1)}, bf16[128,2048]{1,0:T(8,128)(2,1)}, u32[]{:S(2)}, u32[]{:S(2)}) collective-permute-start(bf16[128,2048]{1,0:T(8,128)(2,1)} %get-tuple-element.96), channel_id=1, source_target_pairs={{0,4},{2,6},{4,0},{6,2},{8,12},{10,14},{12,8},{14,10},{16,20},{18,... | collective-permute-start | bytes 1572872 | tf_op jit(solution)/shard_map/ppermute | solution.py:440
  180.9 30.0 %collective-permute-start.42 = (bf16[128,2048]{1,0:T(8,128)(2,1)}, bf16[128,2048]{1,0:T(8,128)(2,1)}, u32[]{:S(2)}, u32[]{:S(2)}) collective-permute-start(bf16[128,2048]{1,0:T(8,128)(2,1)} %get-tuple-element.119), channel_id=1, source_target_pairs={{0,4},{2,6},{4,0},{6,2},{8,12},{10,14},{12,8},{14,10},{16,20},{18,... | collective-permute-start | bytes 1572872 | tf_op jit(solution)/shard_map/ppermute | solution.py:440
  188.0 26.2 %collective-permute-start.46 = (bf16[64,2048]{1,0:T(8,128)(2,1)S(1)}, bf16[64,2048]{1,0:T(8,128)(2,1)S(1)}, u32[]{:S(2)}, u32[]{:S(2)}) collective-permute-start(bf16[64,2048]{1,0:T(8,128)(2,1)S(1)} %copy-done.35), channel_id=1, source_target_pairs={{0,1},{1,0},{2,3},{3,2},{4,5},{5,4},{6,7},{7,6},{8,9},{9,8},{10,11... | collective-permute-start | bytes 786440 | tf_op jit(solution)/shard_map/ppermute | solution.py:448
  189.6 21.3 %collective-permute-start.33 = (bf16[64,2048]{1,0:T(8,128)(2,1)}, bf16[64,2048]{1,0:T(8,128)(2,1)S(1)}, u32[]{:S(2)}, u32[]{:S(2)}) collective-permute-start(bf16[64,2048]{1,0:T(8,128)(2,1)} %get-tuple-element.85), channel_id=1, source_target_pairs={{0,16},{2,18},{4,20},{6,22},{8,24},{10,26},{12,28},{14,30},{16,0},... | collective-permute-start | bytes 786440 | tf_op jit(solution)/shard_map/ppermute | solution.py:443
  193.1 21.1 %collective-permute-start.34 = (bf16[64,2048]{1,0:T(8,128)(2,1)}, bf16[64,2048]{1,0:T(8,128)(2,1)S(1)}, u32[]{:S(2)}, u32[]{:S(2)}) collective-permute-start(bf16[64,2048]{1,0:T(8,128)(2,1)} %get-tuple-element.86), channel_id=1, source_target_pairs={{0,8},{2,10},{4,12},{6,14},{8,16},{10,18},{12,20},{14,22},{16,24},... | collective-permute-start | bytes 786440 | tf_op jit(solution)/shard_map/ppermute | solution.py:443
  214.3 22.8 %collective-permute-start.44 = (bf16[64,2048]{1,0:T(8,128)(2,1)}, bf16[64,2048]{1,0:T(8,128)(2,1)}, u32[]{:S(2)}, u32[]{:S(2)}) collective-permute-start(bf16[64,2048]{1,0:T(8,128)(2,1)} %get-tuple-element.99), channel_id=1, source_target_pairs={{0,16},{2,18},{4,20},{6,22},{8,24},{10,26},{12,28},{14,30},{16,0},... | collective-permute-start | bytes 786440 | tf_op jit(solution)/shard_map/ppermute | solution.py:443
  215.0 22.1 %collective-permute-start.45 = (bf16[64,2048]{1,0:T(8,128)(2,1)}, bf16[64,2048]{1,0:T(8,128)(2,1)}, u32[]{:S(2)}, u32[]{:S(2)}) collective-permute-start(bf16[64,2048]{1,0:T(8,128)(2,1)} %get-tuple-element.100), channel_id=1, source_target_pairs={{0,8},{2,10},{4,12},{6,14},{8,16},{10,18},{12,20},{14,22},{16,24},... | collective-permute-start | bytes 786440 | tf_op jit(solution)/shard_map/ppermute | solution.py:443
  (87 other events, 1414.6 us)

commit v7 on v4

v7 whole, which is shorter than its diff:
```python
import jax
import jax.numpy as jnp
from jax import lax
from jax.experimental import pallas as pl
from jax.experimental.pallas import tpu as pltpu
from jax.sharding import PartitionSpec as P

BF = jnp.bfloat16
F32 = jnp.float32
VMEM = 56 * 1024 * 1024
TOGETHER = 4
LANES = 128
SMALL = pl.CostEstimate(flops=1, bytes_accessed=1, transcendentals=0)


def slots(routes, experts, capacity):
    flat_ids = routes.reshape(-1)
    one_hot = (flat_ids[:, None] == jnp.arange(experts, dtype=jnp.int32)[None, :]).astype(jnp.int32)
    before = jnp.cumsum(one_hot, axis=0) - one_hot
    slot_rank = jnp.sum(before * one_hot, axis=1)
    return flat_ids * capacity + slot_rank


def place(token_rows, positions, total_rows):
    return (
        jnp.zeros((total_rows, token_rows.shape[1]), token_rows.dtype).at[positions].set(token_rows)
    )


def hidden_rows(token_rows, gate_weight, up_weight):
    pre_gate = jnp.dot(token_rows, gate_weight, preferred_element_type=F32)
    pre_up = jnp.dot(token_rows, up_weight, preferred_element_type=F32)
    activation = (jax.nn.silu(pre_gate) * pre_up).astype(BF)
    return (pre_gate, pre_up, activation)


CONTRACT = (((1,), (1,)), ((), ()))


def hidden_grads(grad_rows, pre_gate, pre_up, down_weight):
    d_hidden = lax.dot_general(grad_rows, down_weight, CONTRACT, preferred_element_type=F32)
    sigmoid_gate = jax.nn.sigmoid(pre_gate)
    d_gate = (d_hidden * pre_up * sigmoid_gate * (1.0 + pre_gate * (1.0 - sigmoid_gate))).astype(BF)
    d_up = (d_hidden * pre_gate * sigmoid_gate).astype(BF)
    return d_gate, d_up


def input_rows(d_gate, d_up, gate_weight, up_weight):
    back_rows = lax.dot_general(d_gate, gate_weight, CONTRACT, preferred_element_type=F32)
    back_rows = back_rows + lax.dot_general(d_up, up_weight, CONTRACT, preferred_element_type=F32)
    return back_rows.astype(BF)


def outer_sum(left, right):
    return lax.dot_general(left, right, (((0,), (0,)), ((), ())), preferred_element_type=F32)


def routed_plan(tokens, route_ids, gate_probs, out_cot, w_gate, w_up, w_down):
    experts = lax.axis_size("expert")
    tok_rows, features = tokens.shape
    top_count = route_ids.shape[1]
    hidden = w_gate.shape[2]
    capacity = max(2, tok_rows * top_count * 4 // (3 * experts))
    total_rows = experts * capacity
    positions = slots(route_ids, experts, capacity)
    gate_weight, up_weight, down_weight = w_gate[0], w_up[0], w_down[0]

    def exchange(rows):
        blocks = rows.reshape(experts, capacity, features)
        return lax.all_to_all(blocks, "expert", 0, 0, tiled=True).reshape(-1, features)

    received = exchange(place(jnp.repeat(tokens, top_count, axis=0), positions, total_rows))
    pre_gate, pre_up, activation = hidden_rows(received, gate_weight, up_weight)
    result = jnp.dot(activation, down_weight, preferred_element_type=F32).astype(BF)
    picked = exchange(result)[positions].reshape(tok_rows, top_count, features)
    combined = jnp.einsum("tk,tkd->td", gate_probs, picked.astype(F32)).astype(BF)
    scaled = (gate_probs[:, :, None] * out_cot[:, None, :].astype(F32)).astype(BF)
    grads_in = exchange(place(scaled.reshape(-1, features), positions, total_rows))
    d_gate, d_up = hidden_grads(grads_in, pre_gate, pre_up, down_weight)
    back = exchange(input_rows(d_gate, d_up, gate_weight, up_weight))
    grad_tokens = jnp.sum(
        back[positions].reshape(tok_rows, top_count, features).astype(F32), axis=1
    ).astype(BF)
    gate_up_sum = lax.psum_scatter(
        outer_sum(received, jnp.concatenate([d_gate, d_up], axis=1)).astype(BF),
        "replica",
        scatter_dimension=0,
        tiled=True,
    )
    down_sum = lax.psum_scatter(
        outer_sum(activation, grads_in).astype(BF), "replica", scatter_dimension=0, tiled=True
    )
    return (
        combined,
        grad_tokens,
        gate_up_sum[:, :hidden][None],
        gate_up_sum[:, hidden:][None],
        down_sum[None],
    )

def dot(left, right):
    return jnp.dot(left, right, preferred_element_type=F32)


def whole(array):
    return pl.BlockSpec(array.shape, lambda *_: (0,) * array.ndim)


def params(steps=0):
    order = ("arbitrary",) * steps if steps else None
    return pltpu.CompilerParams(dimension_semantics=order, vmem_limit_bytes=VMEM)


ANYWHERE = pl.BlockSpec(memory_space=pl.ANY)


def landing(pieces):
    rows = sum(a.shape[0] for a in pieces)
    return [
        pltpu.VMEM((rows, pieces[0].shape[1]), BF),
        pltpu.SemaphoreType.DMA((len(pieces),)),
    ]


def load(piece_refs, rows_ref, sems):
    copies, at = [], 0
    for i, ref in enumerate(piece_refs):
        size = ref.shape[0]
        copies.append(pltpu.make_async_copy(ref, rows_ref.at[at : at + size], sems.at[i]))
        copies[-1].start()
        at += size
    return copies


def plan_and_pack(expert, experts, capacity, chunks):
    tok_rows, width = chunks[0].shape
    features = width - LANES
    groups, each = 2, len(chunks) // 2
    length, room = TOGETHER * tok_rows, TOGETHER * capacity

    def body(expert_ref, *refs):
        outs = refs[len(chunks) :]
        mine_ref, theirs_ref, mine_lanes, theirs_lanes, pick_ref, place_ref = outs[:6]
        rows_ref, sems = outs[6:]
        copies = load(refs[: len(chunks)], rows_ref, sems)
        lane = lax.broadcasted_iota(jnp.int32, (length, LANES), 1)
        row = lax.broadcasted_iota(jnp.int32, (length, length), 0)
        col = lax.broadcasted_iota(jnp.int32, (length, length), 1)
        before = (row >= col).astype(BF)
        slot = lax.broadcasted_iota(jnp.int32, (length, 2 * room), 1) % room
        wanted = (slot + 1).astype(F32)

        def places(shares, first):
            routed = []
            for index in (first, first ^ 1):
                held = (lane == index) | (lane == index + experts) | (lane == index + 2 * experts)
                weight = jnp.sum(jnp.where(held, shares, 0.0), axis=1, keepdims=True)
                routed.append(jnp.broadcast_to((weight > 0).astype(F32), (length, room)))
            routed = jnp.concatenate(routed, axis=1)
            rank = dot(before, routed.astype(BF))
            return jnp.where((rank == wanted) & (routed > 0), 1.0, 0.0)

        for group in range(groups):
            for copy in copies[group * each : (group + 1) * each]:
                copy.wait()
            held_rows = slice(group * length, (group + 1) * length)
            lanes = rows_ref[held_rows, features:]
            place = places(lanes.astype(F32), expert_ref[0])
            if group == 0:
                place_ref[:, : 2 * room] = place.astype(BF)
                place_ref[:, 2 * room :] = places(lanes.astype(F32), expert_ref[0] ^ 2).astype(BF)
            pick = place.T.astype(BF)
            pick_ref[group] = pick
            here = slice(group * room, (group + 1) * room)
            packed = dot(pick, lanes).astype(BF)
            mine_lanes[here] = packed[:room]
            theirs_lanes[here] = packed[room:]
            for at in range(0, features, 512):
                cols = slice(at, at + 512)
                packed = dot(pick, rows_ref[held_rows, cols]).astype(BF)
                mine_ref[here, cols] = packed[:room]
                theirs_ref[here, cols] = packed[room:]

    rows = jax.ShapeDtypeStruct((groups * room, features), BF)
    lanes = jax.ShapeDtypeStruct((groups * room, LANES), BF)
    pick = jax.ShapeDtypeStruct((groups, 2 * room, length), BF)
    place = jax.ShapeDtypeStruct((length, 4 * room), BF)
    outs = (rows, rows, lanes, lanes, pick, place)
    return pl.pallas_call(
        body,
        grid_spec=pltpu.PrefetchScalarGridSpec(
            num_scalar_prefetch=1,
            grid=(1,),
            in_specs=[ANYWHERE] * len(chunks),
            out_specs=[whole(a) for a in outs],
            scratch_shapes=landing(chunks),
        ),
        out_shape=outs,
        compiler_params=params(1),
        cost_estimate=SMALL,
        name="plan_and_pack",
    )(expert, *chunks)


def pack(pick, chunks):
    features = chunks[0].shape[1]
    groups, room, length = pick.shape[0], pick.shape[1] // 2, pick.shape[2]
    each = len(chunks) // groups

    def body(pick_ref, *refs):
        mine_ref, theirs_ref, rows_ref, sems = refs[len(chunks) :]
        copies = load(refs[: len(chunks)], rows_ref, sems)
        for group in range(groups):
            for copy in copies[group * each : (group + 1) * each]:
                copy.wait()
            held_rows = slice(group * length, (group + 1) * length)
            here = slice(group * room, (group + 1) * room)
            for at in range(0, features, 512):
                cols = slice(at, at + 512)
                packed = dot(pick_ref[group], rows_ref[held_rows, cols]).astype(BF)
                mine_ref[here, cols] = packed[:room]
                theirs_ref[here, cols] = packed[room:]

    out = jax.ShapeDtypeStruct((groups * room, features), BF)
    return pl.pallas_call(
        body,
        in_specs=[pl.BlockSpec(memory_space=pltpu.VMEM)] + [ANYWHERE] * len(chunks),
        out_shape=(out, out),
        scratch_shapes=landing(chunks),
        compiler_params=params(),
        cost_estimate=SMALL,
        name="pack",
    )(pick, *chunks)


def spread(place, mine, theirs, far_mine, far_theirs):
    length, slots_of = place.shape
    room, features = far_mine.shape
    size = length // TOGETHER
    parts = (mine, theirs, far_mine, far_theirs)

    def body(place_ref, *refs):
        outs = refs[len(parts) :]
        for at in range(0, features, 512):
            cols = slice(at, at + 512)
            rows = jnp.concatenate([ref[:, cols] for ref in refs[: len(parts)]], axis=0)
            dense = dot(place_ref[...], rows).astype(BF)
            for i, out in enumerate(outs):
                out[:, cols] = dense[i * size : (i + 1) * size]

    out = jax.ShapeDtypeStruct((size, features), BF)
    return pl.pallas_call(
        body,
        grid=(1,),
        in_specs=[whole(place)] + [pl.BlockSpec((room, features), lambda i: (0, 0))] * len(parts),
        out_specs=[whole(out)] * TOGETHER,
        out_shape=(out,) * TOGETHER,
        compiler_params=params(1),
        cost_estimate=SMALL,
        name="spread",
    )(place, *parts)


def split3(value):
    high = value.astype(BF)
    rest = value - high.astype(F32)
    mid = rest.astype(BF)
    low = (rest - mid.astype(F32)).astype(BF)
    return high, mid, low


def after(value, *earlier):
    return lax.optimization_barrier((value, *earlier))[0]


def dense_plan(tokens, route_ids, gate_probs, out_cot, w_gate, w_up, w_down):
    experts = lax.axis_size("expert")
    tok_rows, features = tokens.shape
    hidden = w_gate.shape[2]
    top_count = route_ids.shape[1]
    capacity = max(2, tok_rows * top_count * 4 // (3 * experts))
    expert = lax.axis_index("expert").astype(jnp.int32)
    replica = lax.axis_index("replica").astype(jnp.int32)
    w_gate, w_up, w_down = w_gate[0], w_up[0], w_down[0]

    def to_core(rows):
        return lax.ppermute(rows, "expert", [(i, i ^ 1) for i in range(experts)])

    def to_x(rows):
        return lax.ppermute(rows, "expert", [(i, i ^ 2) for i in range(experts)])

    def to_z(rows, step):
        return lax.ppermute(
            rows, "expert", [(i, (i + 4 * step) % experts) for i in range(experts)]
        )

    def to_y(rows):
        return lax.ppermute(rows, "replica", [(0, 1), (1, 0)])

    chosen = route_ids[:, :, None] == jnp.arange(experts, dtype=jnp.int32)
    share = jnp.sum(jnp.where(chosen, gate_probs[:, :, None], 0.0), axis=1)
    pad = jnp.zeros((tok_rows, LANES - 3 * experts), BF)

    cot_far, cot_relay = to_x(out_cot), to_y(out_cot)
    near = [jnp.concatenate([tokens, *split3(share), pad], axis=1)]
    far, relay = [to_x(near[0])], [to_y(near[0])]
    near.append(after(to_z(near[0], 1), cot_far))
    near.append(after(to_z(near[1], 1), far[0], cot_relay, relay[0]))
    far.append(to_x(near[1]))
    relay += [to_y(far[0]), to_y(near[1])]
    near.append(after(to_z(near[2], 1), relay[1], relay[2]))
    far += [to_x(near[2]), to_x(near[3])]
    cot_relay_far = to_y(cot_far)
    relay += [to_y(far[1]), to_y(near[2]), to_y(far[2]), to_y(near[3]), to_y(far[3])]
    token_sets = near + far
    token_other = [relay[0], relay[2], relay[4], relay[6], relay[1], relay[3], relay[5], relay[7]]
    ring = [to_z(after(out_cot, near[2]), 1)]
    ring.append(to_z(ring[0], 1))
    ring.append(to_z(ring[1], 1))
    cot_ring = jnp.concatenate(ring, axis=0)
    cot_far_ring, cot_relay_ring = to_x(cot_ring), to_y(cot_ring)
    cot_relay_far_ring = to_y(cot_far_ring)
    expert_index = expert
    expert = expert.reshape(1)

    def enter(chunks, before_plan, before_dots):
        mine, theirs, mine_lanes, theirs_lanes, pick, place = plan_and_pack(
            after(expert, *before_plan), experts, capacity, chunks
        )
        theirs = after(to_core(theirs), *before_dots)
        x = jnp.concatenate([mine, theirs], axis=0)
        shares = jnp.concatenate([mine_lanes, to_core(theirs_lanes)], axis=0)
        held = (jnp.arange(LANES) % experts == expert_index) & (jnp.arange(LANES) < 3 * experts)
        weight = jnp.sum(jnp.where(held, shares.astype(F32), 0.0), axis=1, keepdims=True)
        pre_gate, pre_up = dot(x, w_gate), dot(x, w_up)
        act = (jax.nn.silu(pre_gate) * pre_up).astype(BF)
        return x, weight, pick, place, pre_gate, pre_up, act

    def enter_cot(pick, pieces, weight, pre_gate, pre_up, *before_dots):
        mine, theirs = pack(pick, pieces)
        theirs = after(to_core(theirs), *before_dots)
        cot = jnp.concatenate([mine, theirs], axis=0)
        cot = (cot.astype(F32) * weight).astype(BF)
        return cot, *hidden_grads(cot, pre_gate, pre_up, w_down)

    def leave(rows_of):
        half = TOGETHER * capacity
        theirs = to_core(rows_of(slice(2 * half, None)))
        mine = rows_of(slice(0, 2 * half))
        return mine, theirs, to_x(mine[half:]), to_x(theirs[half:])

    def home(place, parts):
        own, *others = spread(place, *parts)
        return [own] + [to_z(a, -step) for step, a in enumerate(others, 1)]

    def total(chunks):
        return sum(a.astype(F32) for a in chunks).astype(BF)

    def grads(x, act, cot, d_gate, d_up):
        x = lax.dynamic_slice_in_dim(x, replica * (features // 2), features // 2, 1)
        act = lax.dynamic_slice_in_dim(act, replica * (hidden // 2), hidden // 2, 1)
        return outer_sum(x, d_gate), outer_sum(x, d_up), outer_sum(act, cot)

    own_x, weight, pick, place, pre_gate, pre_up, act = enter(
        token_sets, (cot_relay_far, relay[3], ring[1]), (relay[4],)
    )
    act = after(act, cot_ring)
    parts = leave(lambda rows: (dot(act[rows], w_down) * weight[rows]).astype(BF))
    chunks = home(after(place, relay[5]), parts)
    cot, d_gate, d_up = enter_cot(
        after(pick, chunks[0], relay[6], relay[7]),
        (out_cot, cot_ring, cot_far, cot_far_ring),
        weight, pre_gate, pre_up,
    )
    own_grads = cot, d_gate, d_up
    parts = leave(lambda rows: input_rows(d_gate[rows], d_up[rows], w_gate, w_up))

    x, weight, pick, _, pre_gate, pre_up, other_act = enter(
        token_other, (parts[0], cot_relay_ring, chunks[1]), (chunks[2],)
    )
    grad_chunks = home(after(place, other_act), parts)
    own_grads = after(own_grads, grad_chunks[0], chunks[3])
    own = grads(own_x, act, *own_grads)
    cot, d_gate, d_up = enter_cot(
        after(pick, *own, grad_chunks[1]),
        (cot_relay, cot_relay_ring, cot_relay_far, cot_relay_far_ring),
        weight, pre_gate, pre_up, grad_chunks[2],
    )
    other = grads(x, other_act, cot, d_gate, d_up)
    grad_gate, grad_up, grad_down = ((a + b).astype(BF)[None] for a, b in zip(own, other))
    return (total(chunks), total(grad_chunks), grad_gate, grad_up, grad_down)


def dense_fits(mesh):
    experts, replicas = mesh.shape["expert"], mesh.shape["replica"]
    return replicas == 2 and experts == 4 * TOGETHER


def solution(mesh):
    placed = (
        P(("expert", "replica"), None),
        P(("expert", "replica"), None),
        P(("expert", "replica"), None),
        P(("expert", "replica"), None),
        P("expert", None, None),
        P("expert", None, None),
        P("expert", None, None),
    )
    return jax.shard_map(
        dense_plan if dense_fits(mesh) else routed_plan,
        mesh=mesh,
        in_specs=placed,
        out_specs=(
            P(("expert", "replica"), None),
            P(("expert", "replica"), None),
            P("expert", "replica", None),
            P("expert", "replica", None),
            P("expert", "replica", None),
        ),
        check_vma=False,
    )
```

time: 236 us -> 232 us (0.983)
  waiting for transfers between devices: 108 us -> 98.4 us
  local copies, waits for them, and re-layouts: 11.3 us -> 20.7 us
  other arithmetic: 14.2 us -> 6.75 us
  starting transfers between devices: 37.1 us -> 41.6 us
    ppermute x12, waiting for transfers between devices: 50.6 us -> 24.6 us  [to_z(): lax.ppermute(rows, 'expert', [(i, (i + 4 * step) % experts) for i in rang...]
    ppermute x16 -> x10, waiting for transfers between devices: 32.9 us -> 53.4 us  [to_x(): return lax.ppermute(rows, 'expert', [(i, i ^ 2) for i in range(experts)])]
    ppermute x12, starting transfers between devices: 3.44 us -> 16.7 us  [to_z(): lax.ppermute(rows, 'expert', [(i, (i + 4 * step) % experts) for i in rang...]
    unnamed x114 -> x100, local copies, waits for them, and re-layouts: 7.4 us -> 14.9 us
    ppermute x16 -> x10, starting transfers between devices: 17.8 us -> 10.6 us  [to_x(): return lax.ppermute(rows, 'expert', [(i, i ^ 2) for i in range(experts)])]
    convert_element_type x9 -> x3, other arithmetic: 10.3 us -> 5.62 us  [the longest x2 3.85 us: total(): return sum((a.astype(F32) for a in chunks)).astype(BF)]
    ppermute x16 -> x12, waiting for transfers between devices: 24.3 us -> 20.1 us  [to_y(): return lax.ppermute(rows, 'replica', [(0, 1), (1, 0)])]
    concatenate x1 -> x0, other arithmetic: 2.79 us -> none  [enter(): x = jnp.concatenate([mine[:, :features], theirs[:, :features]], axis=0)]
  transfers between devices with their start and end apart: 50 -> 42, of which waited for: 24 -> 17; matrix products, arithmetic and copies ran while one was open for 18% -> 17% of each run, Pallas kernels for 5% -> 8%
where the time goes in v7:
time: 232 us; the launch traced here: 230 us
  waiting for transfers between devices  98.4 us (42%)
  starting transfers between devices  41.6 us (18%)
  matrix products  37.5 us (16%)
  Pallas kernels  23.8 us (10%)
  local copies, waits for them, and re-layouts  20.7 us (9%)
  other arithmetic  6.75 us (3%)
    ppermute x10, waiting for transfers between devices, to_x(): return lax.ppermute(rows, 'expert', [(i, i ^ 2) for i in range(experts)])  53.4 us
    ppermute x12, waiting for transfers between devices, to_z(): lax.ppermute(rows, 'expert', [(i, (i + 4 * step) % experts) for i in rang...  24.6 us
    ppermute x12, waiting for transfers between devices, to_y(): return lax.ppermute(rows, 'replica', [(0, 1), (1, 0)])  20.1 us
    ppermute x12, starting transfers between devices, to_z(): lax.ppermute(rows, 'expert', [(i, (i + 4 * step) % experts) for i in rang...  16.7 us
    unnamed x100, local copies, waits for them, and re-layouts  14.9 us
    dot_general x6, matrix products, outer_sum(): lax.dot_general(left, right, (((0,), (0,)), ((), ())), preferred_element_...  13.4 us
    ppermute x12, starting transfers between devices, to_y(): return lax.ppermute(rows, 'replica', [(0, 1), (1, 0)])  13.3 us
    dot_general x6, matrix products, dot(): return jnp.dot(left, right, preferred_element_type=F32)  11.8 us
  transfers between devices with their start and end apart: 42, of which 17 were waited for; matrix products, arithmetic and copies ran while one was open for 17% of the time, Pallas kernels for 8%

profile of v7, /device:TPU:0, one launch (start us, length us, event | category | flops | bytes accessed | tf_op | source)
XLA Modules:
  0.0 229.8 jit_solution(17894345380836330690)
XLA Ops:
  2.8 3.1 %collective-permute-start.2 = (bf16[64,2176]{1,0:T(8,128)(2,1)S(1)}, bf16[64,2176]{1,0:T(8,128)(2,1)}, u32[]{:S(2)}, u32[]{:S(2)}) collective-permute-start(bf16[64,2176]{1,0:T(8,128)(2,1)S(1)} %concatenate.24.refs_0_), channel_id=1, source_target_pairs={{0,8},{2,10},{4,12},{6,14},{8,16},{10,18},{12,20},{14,22},{16,24},... | collective-permute-start | bytes 835592 | tf_op jit(solution)/shard_map/ppermute | solution.py:293
  9.4 5.9 %collective-permute-done.refs_2_ = bf16[64,2048]{1,0:T(8,128)(2,1)S(1)} collective-permute-done((bf16[64,2048]{1,0:T(8,128)(2,1)}, bf16[64,2048]{1,0:T(8,128)(2,1)S(1)}, u32[]{:S(2)}, u32[]{:S(2)}) %collective-permute-start) | collective-permute-done | bytes 262176 | tf_op jit(solution)/shard_map/ppermute | solution.py:290
  21.5 5.6 %collective-permute-done.7.refs_0_ = bf16[64,2048]{1,0:T(8,128)(2,1)S(1)} collective-permute-done((bf16[64,2048]{1,0:T(8,128)(2,1)}, bf16[64,2048]{1,0:T(8,128)(2,1)S(1)}, u32[]{:S(2)}, u32[]{:S(2)}) %collective-permute-start.7) | collective-permute-done | bytes 262176 | tf_op jit(solution)/shard_map/ppermute | solution.py:298
  31.1 5.0 %collective-permute-done.12.refs_4_ = bf16[64,2176]{1,0:T(8,128)(2,1)} collective-permute-done((bf16[64,2176]{1,0:T(8,128)(2,1)}, bf16[64,2176]{1,0:T(8,128)(2,1)}, u32[]{:S(2)}, u32[]{:S(2)}) %collective-permute-start.12) | collective-permute-done | bytes 278560 | tf_op jit(solution)/shard_map/ppermute | solution.py:298
  39.6 3.3 %collective-permute-done.9 = bf16[64,2048]{1,0:T(8,128)(2,1)} collective-permute-done((bf16[64,2048]{1,0:T(8,128)(2,1)}, bf16[64,2048]{1,0:T(8,128)(2,1)}, u32[]{:S(2)}, u32[]{:S(2)}) %collective-permute-start.9) | collective-permute-done | bytes 262176 | tf_op jit(solution)/shard_map/ppermute | solution.py:293
  49.7 3.7 %collective-permute-done.10 = bf16[64,2048]{1,0:T(8,128)(2,1)S(1)} collective-permute-done((bf16[64,2048]{1,0:T(8,128)(2,1)}, bf16[64,2048]{1,0:T(8,128)(2,1)S(1)}, u32[]{:S(2)}, u32[]{:S(2)}) %collective-permute-start.10) | collective-permute-done | bytes 262176 | tf_op jit(solution)/shard_map/ppermute | solution.py:293
  54.0 4.3 %plan_and_pack.2 = (bf16[256,2048]{1,0:T(8,128)(2,1)}, bf16[256,2048]{1,0:T(8,128)(2,1)}, bf16[256,128]{1,0:T(8,128)(2,1)}, bf16[256,128]{1,0:T(8,128)(2,1)}, bf...) custom-call(s32[1]{0:T(128)} %bitcast.expert_ref, bf16[64,2176]{1,0:T(8,128)(2,1)} %copy-done.7, ...), custom_call_target="tpu_custom_call" | custom-call | flops 1 | bytes 1 | tf_op jit(solution)/shard_map/plan_and_pack/pallas_call | solution.py:189
  74.5 3.3 %collective-permute-done.16.refs_6_ = bf16[64,2176]{1,0:T(8,128)(2,1)S(1)} collective-permute-done((bf16[64,2176]{1,0:T(8,128)(2,1)S(1)}, bf16[64,2176]{1,0:T(8,128)(2,1)S(1)}, u32[]{:S(2)}, u32[]{:S(2)}) %collective-permute-start.16) | collective-permute-done | bytes 278560 | tf_op jit(solution)/shard_map/ppermute | solution.py:298
  79.4 22.4 %collective-permute-done.22.refs_2_ = bf16[128,2048]{1,0:T(8,128)(2,1)S(1)} collective-permute-done((bf16[128,2048]{1,0:T(8,128)(2,1)S(1)}, bf16[128,2048]{1,0:T(8,128)(2,1)S(1)}, u32[]{:S(2)}, u32[]{:S(2)}) %collective-permute-start.22) | collective-permute-done | bytes 524320 | tf_op jit(solution)/shard_map/ppermute | solution.py:290
  102.6 9.7 %collective-permute-done.23.refs_3_ = bf16[128,2048]{1,0:T(8,128)(2,1)} collective-permute-done((bf16[128,2048]{1,0:T(8,128)(2,1)S(1)}, bf16[128,2048]{1,0:T(8,128)(2,1)}, u32[]{:S(2)}, u32[]{:S(2)}) %collective-permute-start.23) | collective-permute-done | bytes 524320 | tf_op jit(solution)/shard_map/ppermute | solution.py:290
  112.3 3.2 %spread.2 = (bf16[64,2048]{1,0:T(8,128)(2,1)}, bf16[64,2048]{1,0:T(8,128)(2,1)}, bf16[64,2048]{1,0:T(8,128)(2,1)}, bf16[64,2048]{1,0:T(8,128)(2,1)}) custom-call(bf16[256,512]{1,0:T(8,128)(2,1)} %get-tuple-element.70.place_ref, bf16[256,2048]{1,0:T(8,128)(2,1)} %copy-done.6, bf16[256,2048]{1,0:T(8,128)(2,1)} %copy-done.5, bf16[128,2048]{1,0:T(8,128)(2,1)} %copy-done.20, ...), custom_call_target="tpu_custom_call" | custom-call | flops 1 | bytes 1 | tf_op jit(solution)/shard_map/spread/pallas_call | solution.py:252
  116.4 4.4 %pack.2 = (bf16[256,2048]{1,0:T(8,128)(2,1)}, bf16[256,2048]{1,0:T(8,128)(2,1)}) custom-call(bf16[2,256,256]{2,1,0:T(8,128)(2,1)} %get-tuple-element.63.pick_ref, bf16[64,2048]{1,0:T(8,128)(2,1)} %refs_0_.1, bf16[192,2048]{1,0:T(8,128)(2,1)} %constant_dynamic-update-slice_fusion.2.refs_1_, bf16[64,2048]{1,0:T(8,128)(2,1)} %copy-done.30, ...), custom_call_target="tpu_custom_call" | custom-call | flops 1 | bytes 1 | tf_op jit(solution)/shard_map/pack/pallas_call | solution.py:225
  121.4 3.8 %collective-permute-start.24 = (bf16[64,2048]{1,0:T(8,128)(2,1)S(1)}, bf16[64,2048]{1,0:T(8,128)(2,1)S(1)}, u32[]{:S(2)}, u32[]{:S(2)}) collective-permute-start(bf16[64,2048]{1,0:T(8,128)(2,1)S(1)} %copy-done.41), channel_id=1, source_target_pairs={{0,24},{2,26},{4,28},{6,30},{8,0},{10,2},{12,4},{14,6},{16,8},{18,... | collective-permute-start | bytes 786440 | tf_op jit(solution)/shard_map/ppermute | solution.py:293
  127.5 4.4 %multiply_convert_fusion.6 = (bf16[512,768]{1,0:T(8,128)(2,1)S(1)}, bf16[512,768]{1,0:T(8,128)(2,1)S(1)}) fusion(f32[512,768]{1,0:T(8,128)} %copy-done.47, f32[512,768]{1,0:T(8,128)} %get-tuple-element.92, bf16[512,2048]{1,0:T(8,128)(2,1)S(1)} %multiply_convert_fusion.1, bf16[1,768,2048]{2,1,0:T(8,128)(2,1)S(1)} %copy-done.39), kind=kOutput, calls=%fused_computation.43 | convolution fusion | flops 1615724544 | bytes 9961472 | tf_op jit(solution)/shard_map/dot_general | solution.py:41
  138.0 3.2 %collective-permute-done.31.refs_1_ = bf16[192,2048]{1,0:T(8,128)(2,1)} collective-permute-done((bf16[192,2048]{1,0:T(8,128)(2,1)}, bf16[192,2048]{1,0:T(8,128)(2,1)}, u32[]{:S(2)}, u32[]{:S(2)}) %collective-permute-start.31) | collective-permute-done | bytes 786464 | tf_op jit(solution)/shard_map/ppermute | solution.py:298
  141.1 4.3 %plan_and_pack.3 = (bf16[256,2048]{1,0:T(8,128)(2,1)}, bf16[256,2048]{1,0:T(8,128)(2,1)}, bf16[256,128]{1,0:T(8,128)(2,1)}, bf16[256,128]{1,0:T(8,128)(2,1)}, bf...) custom-call(s32[1]{0:T(128)} %bitcast.expert_ref, bf16[64,2176]{1,0:T(8,128)(2,1)} %copy-done.23, ...), custom_call_target="tpu_custom_call" | custom-call | flops 1 | bytes 1 | tf_op jit(solution)/shard_map/plan_and_pack/pallas_call | solution.py:189
  146.3 4.2 %collective-permute-start.26 = (bf16[64,2048]{1,0:T(8,128)(2,1)}, bf16[64,2048]{1,0:T(8,128)(2,1)}, u32[]{:S(2)}, u32[]{:S(2)}) collective-permute-start(bf16[64,2048]{1,0:T(8,128)(2,1)} %get-tuple-element.61), channel_id=1, source_target_pairs={{0,8},{2,10},{4,12},{6,14},{8,16},{10,18},{12,20},{14,22},{16,24},... | collective-permute-start | bytes 786440 | tf_op jit(solution)/shard_map/ppermute | solution.py:293
  154.1 12.5 %collective-permute-done.25 = bf16[64,2048]{1,0:T(8,128)(2,1)} collective-permute-done((bf16[64,2048]{1,0:T(8,128)(2,1)}, bf16[64,2048]{1,0:T(8,128)(2,1)}, u32[]{:S(2)}, u32[]{:S(2)}) %collective-permute-start.25) | collective-permute-done | bytes 262176 | tf_op jit(solution)/shard_map/ppermute | solution.py:293
  173.0 3.3 %multiply_convert_fusion.4 = (bf16[512,768]{1,0:T(8,128)(2,1)}, f32[512,768]{1,0:T(8,128)}) fusion(f32[512,768]{1,0:T(8,128)S(1)} %fusion.18, bf16[512,2048]{1,0:T(8,128)(2,1)S(1)} %constant_dynamic-update-slice_fusion.5, bf16[1,2048,768]{2,1,0:T(8,128)(2,1)S(1)} %copy-done), kind=kOutput, calls=%fused_computation.40 | convolution fusion | flops 1612972032 | bytes 9175040 | tf_op jit(solution)/shard_map/dot_general | solution.py:102
  176.2 5.3 %collective-permute-done.34.refs_2_ = bf16[128,2048]{1,0:T(8,128)(2,1)S(1)} collective-permute-done((bf16[128,2048]{1,0:T(8,128)(2,1)S(1)}, bf16[128,2048]{1,0:T(8,128)(2,1)S(1)}, u32[]{:S(2)}, u32[]{:S(2)}) %collective-permute-start.34) | collective-permute-done | bytes 524320 | tf_op jit(solution)/shard_map/ppermute | solution.py:290
  181.5 9.9 %collective-permute-done.35.refs_3_ = bf16[128,2048]{1,0:T(8,128)(2,1)S(1)} collective-permute-done((bf16[128,2048]{1,0:T(8,128)(2,1)S(1)}, bf16[128,2048]{1,0:T(8,128)(2,1)S(1)}, u32[]{:S(2)}, u32[]{:S(2)}) %collective-permute-start.35) | collective-permute-done | bytes 524320 | tf_op jit(solution)/shard_map/ppermute | solution.py:290
  192.2 3.2 %spread.3 = (bf16[64,2048]{1,0:T(8,128)(2,1)}, bf16[64,2048]{1,0:T(8,128)(2,1)}, bf16[64,2048]{1,0:T(8,128)(2,1)}, bf16[64,2048]{1,0:T(8,128)(2,1)}) custom-call(bf16[256,512]{1,0:T(8,128)(2,1)} %get-tuple-element.70.place_ref, bf16[256,2048]{1,0:T(8,128)(2,1)} %fusion.46.refs_0_, bf16[256,2048]{1,0:T(8,128)(2,1)} %collective-permute-done.33.refs_1_, ...), custom_call_target="tpu_custom_call" | custom-call | flops 1 | bytes 1 | tf_op jit(solution)/shard_map/spread/pallas_call | solution.py:252
  205.7 4.4 %pack.3 = (bf16[256,2048]{1,0:T(8,128)(2,1)}, bf16[256,2048]{1,0:T(8,128)(2,1)}) custom-call(bf16[2,256,256]{2,1,0:T(8,128)(2,1)} %get-tuple-element.79.pick_ref, bf16[64,2048]{1,0:T(8,128)(2,1)} %copy-done.28, bf16[192,2048]{1,0:T(8,128)(2,1)} %collective-permute-done.31.refs_1_, bf16[64,2048]{1,0:T(8,128)(2,1)} %copy-done.29, bf16[192,2048]{1,0:T(8,128)(2,1)} %copy-done.12), custom_call_target="tpu_custom_call" | custom-call | flops 1 | bytes 1 | tf_op jit(solution)/shard_map/pack/pallas_call | solution.py:225
  212.3 5.1 %collective-permute-done.37 = bf16[64,2048]{1,0:T(8,128)(2,1)} collective-permute-done((bf16[64,2048]{1,0:T(8,128)(2,1)}, bf16[64,2048]{1,0:T(8,128)(2,1)}, u32[]{:S(2)}, u32[]{:S(2)}) %collective-permute-start.37) | collective-permute-done | bytes 262176 | tf_op jit(solution)/shard_map/ppermute | solution.py:293
  (205 shorter events, 91.4 us)
Async XLA Ops:
  7.4 21.2 %collective-permute-start.8 = (bf16[64,2176]{1,0:T(8,128)(2,1)S(1)}, bf16[64,2176]{1,0:T(8,128)(2,1)S(1)}, u32[]{:S(2)}, u32[]{:S(2)}) collective-permute-start(bf16[64,2176]{1,0:T(8,128)(2,1)S(1)} %concatenate.24.refs_0_), channel_id=1, source_target_pairs={{0,1},{1,0},{2,3},{3,2},{4,5},{5,4},{6,7},{7,6},{8,9},{9,8},{10,11... | collective-permute-start | bytes 835592 | tf_op jit(solution)/shard_map/ppermute | solution.py:298
  16.0 13.2 %collective-permute-start.5 = (bf16[64,2176]{1,0:T(8,128)(2,1)}, bf16[64,2176]{1,0:T(8,128)(2,1)}, u32[]{:S(2)}, u32[]{:S(2)}) collective-permute-start(bf16[64,2176]{1,0:T(8,128)(2,1)} %collective-permute-done.2.refs_1_), channel_id=1, source_target_pairs={{0,8},{2,10},{4,12},{6,14},{8,16},{10,18},{12,20},{14,22},{16,24},... | collective-permute-start | bytes 835592 | tf_op jit(solution)/shard_map/ppermute | solution.py:293
  19.1 18.4 %collective-permute-start.13 = (bf16[64,2176]{1,0:T(8,128)(2,1)}, bf16[64,2176]{1,0:T(8,128)(2,1)}, u32[]{:S(2)}, u32[]{:S(2)}) collective-permute-start(bf16[64,2176]{1,0:T(8,128)(2,1)} %collective-permute-done.2.refs_1_), channel_id=1, source_target_pairs={{0,1},{1,0},{2,3},{3,2},{4,5},{5,4},{6,7},{7,6},{8,9},{9,8},{10,11... | collective-permute-start | bytes 835592 | tf_op jit(solution)/shard_map/ppermute | solution.py:298
  19.9 16.1 %collective-permute-start.12 = (bf16[64,2176]{1,0:T(8,128)(2,1)}, bf16[64,2176]{1,0:T(8,128)(2,1)}, u32[]{:S(2)}, u32[]{:S(2)}) collective-permute-start(bf16[64,2176]{1,0:T(8,128)(2,1)} %collective-permute-done.6.refs_4_), channel_id=1, source_target_pairs={{0,1},{1,0},{2,3},{3,2},{4,5},{5,4},{6,7},{7,6},{8,9},{9,8},{10,11... | collective-permute-start | bytes 835592 | tf_op jit(solution)/shard_map/ppermute | solution.py:298
  29.3 13.6 %collective-permute-start.11 = (bf16[64,2176]{1,0:T(8,128)(2,1)}, bf16[64,2176]{1,0:T(8,128)(2,1)}, u32[]{:S(2)}, u32[]{:S(2)}) collective-permute-start(bf16[64,2176]{1,0:T(8,128)(2,1)} %collective-permute-done.5.refs_2_), channel_id=1, source_target_pairs={{0,8},{2,10},{4,12},{6,14},{8,16},{10,18},{12,20},{14,22},{16,24},... | collective-permute-start | bytes 835592 | tf_op jit(solution)/shard_map/ppermute | solution.py:293
  37.5 15.8 %collective-permute-start.14 = (bf16[64,2176]{1,0:T(8,128)(2,1)}, bf16[64,2176]{1,0:T(8,128)(2,1)S(1)}, u32[]{:S(2)}, u32[]{:S(2)}) collective-permute-start(bf16[64,2176]{1,0:T(8,128)(2,1)} %collective-permute-done.5.refs_2_), channel_id=1, source_target_pairs={{0,4},{2,6},{4,0},{6,2},{8,12},{10,14},{12,8},{14,10},{16,20},{18,... | collective-permute-start | bytes 835592 | tf_op jit(solution)/shard_map/ppermute | solution.py:290
  45.5 16.7 %collective-permute-start.18 = (bf16[64,2176]{1,0:T(8,128)(2,1)}, bf16[64,2176]{1,0:T(8,128)(2,1)S(1)}, u32[]{:S(2)}, u32[]{:S(2)}) collective-permute-start(bf16[64,2176]{1,0:T(8,128)(2,1)} %collective-permute-done.5.refs_2_), channel_id=1, source_target_pairs={{0,1},{1,0},{2,3},{3,2},{4,5},{5,4},{6,7},{7,6},{8,9},{9,8},{10,11... | collective-permute-start | bytes 835592 | tf_op jit(solution)/shard_map/ppermute | solution.py:298
  69.9 45.6 %collective-permute-start.29 = (bf16[192,2048]{1,0:T(8,128)(2,1)}, bf16[192,2048]{1,0:T(8,128)(2,1)S(1)}, u32[]{:S(2)}, u32[]{:S(2)}) collective-permute-start(bf16[192,2048]{1,0:T(8,128)(2,1)} %constant_dynamic-update-slice_fusion.2.refs_1_), channel_id=1, source_target_pairs={{0,4},{2,6},{4,0},{6,2},{8,12},{10,14},{12,8},{14,10},{16,20},{18,... | collective-permute-start | bytes 2359304 | tf_op jit(solution)/shard_map/ppermute | solution.py:290
  71.5 30.3 %collective-permute-start.22 = (bf16[128,2048]{1,0:T(8,128)(2,1)S(1)}, bf16[128,2048]{1,0:T(8,128)(2,1)S(1)}, u32[]{:S(2)}, u32[]{:S(2)}) collective-permute-start(bf16[128,2048]{1,0:T(8,128)(2,1)S(1)} %slice.50), channel_id=1, source_target_pairs={{0,4},{2,6},{4,0},{6,2},{8,12},{10,14},{12,8},{14,10},{16,20},{18,... | collective-permute-start | bytes 1572872 | tf_op jit(solution)/shard_map/ppermute | solution.py:290
  73.1 39.1 %collective-permute-start.23 = (bf16[128,2048]{1,0:T(8,128)(2,1)S(1)}, bf16[128,2048]{1,0:T(8,128)(2,1)}, u32[]{:S(2)}, u32[]{:S(2)}) collective-permute-start(bf16[128,2048]{1,0:T(8,128)(2,1)S(1)} %slice.51), channel_id=1, source_target_pairs={{0,4},{2,6},{4,0},{6,2},{8,12},{10,14},{12,8},{14,10},{16,20},{18,... | collective-permute-start | bytes 1572872 | tf_op jit(solution)/shard_map/ppermute | solution.py:290
  74.0 41.5 %collective-permute-start.27 = (bf16[64,2176]{1,0:T(8,128)(2,1)}, bf16[64,2176]{1,0:T(8,128)(2,1)}, u32[]{:S(2)}, u32[]{:S(2)}) collective-permute-start(bf16[64,2176]{1,0:T(8,128)(2,1)} %collective-permute-done.11.refs_3_), channel_id=1, source_target_pairs={{0,1},{1,0},{2,3},{3,2},{4,5},{5,4},{6,7},{7,6},{8,9},{9,8},{10,11... | collective-permute-start | bytes 835592 | tf_op jit(solution)/shard_map/ppermute | solution.py:298
  77.9 37.6 %collective-permute-start.28 = (bf16[64,2176]{1,0:T(8,128)(2,1)}, bf16[64,2176]{1,0:T(8,128)(2,1)}, u32[]{:S(2)}, u32[]{:S(2)}) collective-permute-start(bf16[64,2176]{1,0:T(8,128)(2,1)} %collective-permute-done.15.refs_7_), channel_id=1, source_target_pairs={{0,1},{1,0},{2,3},{3,2},{4,5},{5,4},{6,7},{7,6},{8,9},{9,8},{10,11... | collective-permute-start | bytes 835592 | tf_op jit(solution)/shard_map/ppermute | solution.py:298
  120.9 20.3 %collective-permute-start.31 = (bf16[192,2048]{1,0:T(8,128)(2,1)}, bf16[192,2048]{1,0:T(8,128)(2,1)}, u32[]{:S(2)}, u32[]{:S(2)}) collective-permute-start(bf16[192,2048]{1,0:T(8,128)(2,1)} %constant_dynamic-update-slice_fusion.2.refs_1_), channel_id=1, source_target_pairs={{0,1},{1,0},{2,3},{3,2},{4,5},{5,4},{6,7},{7,6},{8,9},{9,8},{10,11... | collective-permute-start | bytes 2359304 | tf_op jit(solution)/shard_map/ppermute | solution.py:298
  121.4 19.7 %collective-permute-start.24 = (bf16[64,2048]{1,0:T(8,128)(2,1)S(1)}, bf16[64,2048]{1,0:T(8,128)(2,1)S(1)}, u32[]{:S(2)}, u32[]{:S(2)}) collective-permute-start(bf16[64,2048]{1,0:T(8,128)(2,1)S(1)} %copy-done.41), channel_id=1, source_target_pairs={{0,24},{2,26},{4,28},{6,30},{8,0},{10,2},{12,4},{14,6},{16,8},{18,... | collective-permute-start | bytes 786440 | tf_op jit(solution)/shard_map/ppermute | solution.py:293
  134.9 17.9 %collective-permute-start.33 = (bf16[256,2048]{1,0:T(8,128)(2,1)}, bf16[256,2048]{1,0:T(8,128)(2,1)}, u32[]{:S(2)}, u32[]{:S(2)}) collective-permute-start(bf16[256,2048]{1,0:T(8,128)(2,1)} %fusion.43), channel_id=1, source_target_pairs={{0,2},{2,0},{4,6},{6,4},{8,10},{10,8},{12,14},{14,12},{16,18},{18,... | collective-permute-start | bytes 3145736 | tf_op jit(solution)/shard_map/ppermute | solution.py:287
  145.4 21.8 %collective-permute-start.32 = (bf16[256,2048]{1,0:T(8,128)(2,1)}, bf16[256,2048]{1,0:T(8,128)(2,1)}, u32[]{:S(2)}, u32[]{:S(2)}) collective-permute-start(bf16[256,2048]{1,0:T(8,128)(2,1)} %get-tuple-element.68), channel_id=1, source_target_pairs={{0,2},{2,0},{4,6},{6,4},{8,10},{10,8},{12,14},{14,12},{16,18},{18,... | collective-permute-start | bytes 3145736 | tf_op jit(solution)/shard_map/ppermute | solution.py:287
  145.5 21.2 %collective-permute-start.25 = (bf16[64,2048]{1,0:T(8,128)(2,1)}, bf16[64,2048]{1,0:T(8,128)(2,1)}, u32[]{:S(2)}, u32[]{:S(2)}) collective-permute-start(bf16[64,2048]{1,0:T(8,128)(2,1)} %get-tuple-element.60), channel_id=1, source_target_pairs={{0,16},{2,18},{4,20},{6,22},{8,24},{10,26},{12,28},{14,30},{16,0},... | collective-permute-start | bytes 786440 | tf_op jit(solution)/shard_map/ppermute | solution.py:293
  145.8 59.0 %collective-permute-start.39 = (bf16[192,2048]{1,0:T(8,128)(2,1)}, bf16[192,2048]{1,0:T(8,128)(2,1)S(1)}, u32[]{:S(2)}, u32[]{:S(2)}) collective-permute-start(bf16[192,2048]{1,0:T(8,128)(2,1)} %copy-done.11), channel_id=1, source_target_pairs={{0,1},{1,0},{2,3},{3,2},{4,5},{5,4},{6,7},{7,6},{8,9},{9,8},{10,11... | collective-permute-start | bytes 2359304 | tf_op jit(solution)/shard_map/ppermute | solution.py:298
  146.3 49.1 %collective-permute-start.26 = (bf16[64,2048]{1,0:T(8,128)(2,1)}, bf16[64,2048]{1,0:T(8,128)(2,1)}, u32[]{:S(2)}, u32[]{:S(2)}) collective-permute-start(bf16[64,2048]{1,0:T(8,128)(2,1)} %get-tuple-element.61), channel_id=1, source_target_pairs={{0,8},{2,10},{4,12},{6,14},{8,16},{10,18},{12,20},{14,22},{16,24},... | collective-permute-start | bytes 786440 | tf_op jit(solution)/shard_map/ppermute | solution.py:293
  152.8 59.3 %collective-permute-start.41 = (bf16[256,128]{1,0:T(8,128)(2,1)}, bf16[256,128]{1,0:T(8,128)(2,1)S(1)}, u32[]{:S(2)}, u32[]{:S(2)}) collective-permute-start(bf16[256,128]{1,0:T(8,128)(2,1)} %get-tuple-element.84), channel_id=1, source_target_pairs={{0,2},{2,0},{4,6},{6,4},{8,10},{10,8},{12,14},{14,12},{16,18},{18,... | collective-permute-start | bytes 196616 | tf_op jit(solution)/shard_map/ppermute | solution.py:287
  166.7 14.8 %collective-permute-start.34 = (bf16[128,2048]{1,0:T(8,128)(2,1)S(1)}, bf16[128,2048]{1,0:T(8,128)(2,1)S(1)}, u32[]{:S(2)}, u32[]{:S(2)}) collective-permute-start(bf16[128,2048]{1,0:T(8,128)(2,1)S(1)} %slice.56), channel_id=1, source_target_pairs={{0,4},{2,6},{4,0},{6,2},{8,12},{10,14},{12,8},{14,10},{16,20},{18,... | collective-permute-start | bytes 1572872 | tf_op jit(solution)/shard_map/ppermute | solution.py:290
  167.2 24.2 %collective-permute-start.35 = (bf16[128,2048]{1,0:T(8,128)(2,1)S(1)}, bf16[128,2048]{1,0:T(8,128)(2,1)S(1)}, u32[]{:S(2)}, u32[]{:S(2)}) collective-permute-start(bf16[128,2048]{1,0:T(8,128)(2,1)S(1)} %slice.57), channel_id=1, source_target_pairs={{0,4},{2,6},{4,0},{6,2},{8,12},{10,14},{12,8},{14,10},{16,20},{18,... | collective-permute-start | bytes 1572872 | tf_op jit(solution)/shard_map/ppermute | solution.py:290
  195.4 21.9 %collective-permute-start.37 = (bf16[64,2048]{1,0:T(8,128)(2,1)}, bf16[64,2048]{1,0:T(8,128)(2,1)}, u32[]{:S(2)}, u32[]{:S(2)}) collective-permute-start(bf16[64,2048]{1,0:T(8,128)(2,1)} %get-tuple-element.73), channel_id=1, source_target_pairs={{0,16},{2,18},{4,20},{6,22},{8,24},{10,26},{12,28},{14,30},{16,0},... | collective-permute-start | bytes 786440 | tf_op jit(solution)/shard_map/ppermute | solution.py:293
  195.5 21.8 %collective-permute-start.38 = (bf16[64,2048]{1,0:T(8,128)(2,1)}, bf16[64,2048]{1,0:T(8,128)(2,1)}, u32[]{:S(2)}, u32[]{:S(2)}) collective-permute-start(bf16[64,2048]{1,0:T(8,128)(2,1)} %get-tuple-element.74), channel_id=1, source_target_pairs={{0,8},{2,10},{4,12},{6,14},{8,16},{10,18},{12,20},{14,22},{16,24},... | collective-permute-start | bytes 786440 | tf_op jit(solution)/shard_map/ppermute | solution.py:293
  (66 other events, 547.5 us)

commit v8 on v7

--- a/solution.py
+++ b/solution.py
@@ -301,25 +301,23 @@
     share = jnp.sum(jnp.where(chosen, gate_probs[:, :, None], 0.0), axis=1)
     pad = jnp.zeros((tok_rows, LANES - 3 * experts), BF)
 
-    cot_far, cot_relay = to_x(out_cot), to_y(out_cot)
+    cot_far, cot_relay = [to_x(out_cot)], to_y(out_cot)
     near = [jnp.concatenate([tokens, *split3(share), pad], axis=1)]
-    far, relay = [to_x(near[0])], [to_y(near[0])]
-    near.append(after(to_z(near[0], 1), cot_far))
-    near.append(after(to_z(near[1], 1), far[0], cot_relay, relay[0]))
-    far.append(to_x(near[1]))
-    relay += [to_y(far[0]), to_y(near[1])]
-    near.append(after(to_z(near[2], 1), relay[1], relay[2]))
-    far += [to_x(near[2]), to_x(near[3])]
-    cot_relay_far = to_y(cot_far)
-    relay += [to_y(far[1]), to_y(near[2]), to_y(far[2]), to_y(near[3]), to_y(far[3])]
+    near.append(after(to_z(near[0], 1), cot_far[0]))
+    near.append(to_z(near[1], 1))
+    near.append(to_z(near[2], 1))
+    far = [to_x(a) for a in near]
+    relay = [to_y(a) for pair in zip(near, far) for a in pair]
     token_sets = near + far
-    token_other = [relay[0], relay[2], relay[4], relay[6], relay[1], relay[3], relay[5], relay[7]]
-    ring = [to_z(after(out_cot, near[2]), 1)]
-    ring.append(to_z(ring[0], 1))
-    ring.append(to_z(ring[1], 1))
-    cot_ring = jnp.concatenate(ring, axis=0)
-    cot_far_ring, cot_relay_ring = to_x(cot_ring), to_y(cot_ring)
-    cot_relay_far_ring = to_y(cot_far_ring)
+    token_other = relay[0::2] + relay[1::2]
+    cot_near = [out_cot, to_z(after(out_cot, near[2]), 1)]
+    cot_near.append(to_z(cot_near[1], 1))
+    cot_near.append(to_z(cot_near[2], 1))
+    cot_far += [to_x(a) for a in cot_near[1:]]
+    cot_sets = cot_near + cot_far
+    cot_relay_far = to_y(cot_far[0])
+    cot_relay_ring = to_y(jnp.concatenate(cot_near[1:], axis=0))
+    cot_relay_far_ring = to_y(jnp.concatenate(cot_far[1:], axis=0))
     expert_index = expert
     expert = expert.reshape(1)
 
@@ -362,24 +360,26 @@
         return outer_sum(x, d_gate), outer_sum(x, d_up), outer_sum(act, cot)
 
     own_x, weight, pick, place, pre_gate, pre_up, act = enter(
-        token_sets, (cot_relay_far, relay[3], ring[1]), (relay[4],)
-    )
-    act = after(act, cot_ring)
+        token_sets,
+        (cot_relay, cot_relay_far, *relay[:4], *cot_near[1:3], cot_far[1]),
+        (relay[4], cot_far[2]),
+    )
+    act = after(act, cot_near[3], relay[5])
     parts = leave(lambda rows: (dot(act[rows], w_down) * weight[rows]).astype(BF))
-    chunks = home(after(place, relay[5]), parts)
     cot, d_gate, d_up = enter_cot(
-        after(pick, chunks[0], relay[6], relay[7]),
-        (out_cot, cot_ring, cot_far, cot_far_ring),
-        weight, pre_gate, pre_up,
+        after(pick, parts[0], relay[6]), cot_sets, weight, pre_gate, pre_up, relay[7]
     )
     own_grads = cot, d_gate, d_up
-    parts = leave(lambda rows: input_rows(d_gate[rows], d_up[rows], w_gate, w_up))
+    d_gate, d_up = after((d_gate, d_up), parts[2], cot_relay_ring)
+    grad_parts = leave(lambda rows: input_rows(d_gate[rows], d_up[rows], w_gate, w_up))
+    chunks = home(after(place, grad_parts[0]), parts)
+    parts = grad_parts
 
     x, weight, pick, _, pre_gate, pre_up, other_act = enter(
-        token_other, (parts[0], cot_relay_ring, chunks[1]), (chunks[2],)
-    )
-    grad_chunks = home(after(place, other_act), parts)
-    own_grads = after(own_grads, grad_chunks[0], chunks[3])
+        token_other, (chunks[0], parts[1]), (parts[2], cot_relay_far_ring)
+    )
+    grad_chunks = home(after(place, other_act, *chunks[1:]), parts)
+    own_grads = after(own_grads, grad_chunks[0])
     own = grads(own_x, act, *own_grads)
     cot, d_gate, d_up = enter_cot(
         after(pick, *own, grad_chunks[1]),

time: 232 us -> 221 us (0.953)
  waiting for transfers between devices: 98.4 us -> 80.8 us
  starting transfers between devices: 41.6 us -> 51.7 us
  local copies, waits for them, and re-layouts: 20.7 us -> 18.1 us
    ppermute x10 -> x12, waiting for transfers between devices: 53.4 us -> 27.2 us  [to_x(): return lax.ppermute(rows, 'expert', [(i, i ^ 2) for i in range(experts)])]
    ppermute x12, waiting for transfers between devices: 20.1 us -> 43.9 us  [to_y(): return lax.ppermute(rows, 'replica', [(0, 1), (1, 0)])]
    ppermute x12, waiting for transfers between devices: 24.6 us -> 9.69 us  [to_z(): lax.ppermute(rows, 'expert', [(i, (i + 4 * step) % experts) for i in rang...]
    ppermute x10 -> x12, starting transfers between devices: 10.6 us -> 15.9 us  [to_x(): return lax.ppermute(rows, 'expert', [(i, i ^ 2) for i in range(experts)])]
    ppermute x12, starting transfers between devices: 16.7 us -> 20 us  [to_z(): lax.ppermute(rows, 'expert', [(i, (i + 4 * step) % experts) for i in rang...]
    concatenate x0 -> x2, other arithmetic: none -> 3.04 us  [the longest x1 1.92 us: dense_plan(): cot_relay_far_ring = to_y(jnp.concatenate(cot_far[1:], axis=0))]
    unnamed x100 -> x122, local copies, waits for them, and re-layouts: 14.9 us -> 13.5 us
  transfers between devices with their start and end apart: 42 -> 44, of which waited for: 17 -> 19; matrix products, arithmetic and copies ran while one was open for 17% -> 18% of each run, Pallas kernels for 8% -> 5%
where the time goes in v8:
time: 221 us; the launch traced here: 220 us
  waiting for transfers between devices  80.8 us (37%)
  starting transfers between devices  51.7 us (23%)
  matrix products  36.5 us (17%)
  Pallas kernels  24.2 us (11%)
  local copies, waits for them, and re-layouts  18.1 us (8%)
  other arithmetic  7.22 us (3%)
    ppermute x12, waiting for transfers between devices, to_y(): return lax.ppermute(rows, 'replica', [(0, 1), (1, 0)])  43.9 us
    ppermute x12, waiting for transfers between devices, to_x(): return lax.ppermute(rows, 'expert', [(i, i ^ 2) for i in range(experts)])  27.2 us
    ppermute x12, starting transfers between devices, to_z(): lax.ppermute(rows, 'expert', [(i, (i + 4 * step) % experts) for i in rang...  20 us
    ppermute x12, starting transfers between devices, to_x(): return lax.ppermute(rows, 'expert', [(i, i ^ 2) for i in range(experts)])  15.9 us
    ppermute x12, starting transfers between devices, to_y(): return lax.ppermute(rows, 'replica', [(0, 1), (1, 0)])  15.4 us
    dot_general x6, matrix products, dot(): return jnp.dot(left, right, preferred_element_type=F32)  13.9 us
    unnamed x122, local copies, waits for them, and re-layouts  13.5 us
    dot_general x6, matrix products, outer_sum(): lax.dot_general(left, right, (((0,), (0,)), ((), ())), preferred_element_...  13.5 us
  transfers between devices with their start and end apart: 44, of which 19 were waited for; matrix products, arithmetic and copies ran while one was open for 18% of the time, Pallas kernels for 5%

profile of v8, /device:TPU:0, one launch (start us, length us, event | category | flops | bytes accessed | tf_op | source)
XLA Modules:
  0.0 219.8 jit_solution(5354267652316439048)
XLA Ops:
  2.8 3.1 %collective-permute-start.6 = (bf16[64,2176]{1,0:T(8,128)(2,1)S(1)}, bf16[64,2176]{1,0:T(8,128)(2,1)S(1)}, u32[]{:S(2)}, u32[]{:S(2)}) collective-permute-start(bf16[64,2176]{1,0:T(8,128)(2,1)S(1)} %concatenate.27.refs_0_), channel_id=1, source_target_pairs={{0,8},{2,10},{4,12},{6,14},{8,16},{10,18},{12,20},{14,22},{16,24},... | collective-permute-start | bytes 835592 | tf_op jit(solution)/shard_map/ppermute | solution.py:293
  7.9 7.4 %collective-permute-done.1.refs_4_ = bf16[64,2048]{1,0:T(8,128)(2,1)S(1)} collective-permute-done((bf16[64,2048]{1,0:T(8,128)(2,1)}, bf16[64,2048]{1,0:T(8,128)(2,1)S(1)}, u32[]{:S(2)}, u32[]{:S(2)}) %collective-permute-start.1) | collective-permute-done | bytes 262176 | tf_op jit(solution)/shard_map/ppermute | solution.py:290
  20.5 5.9 %collective-permute-done.refs_0_ = bf16[64,2048]{1,0:T(8,128)(2,1)S(1)} collective-permute-done((bf16[64,2048]{1,0:T(8,128)(2,1)}, bf16[64,2048]{1,0:T(8,128)(2,1)S(1)}, u32[]{:S(2)}, u32[]{:S(2)}) %collective-permute-start) | collective-permute-done | bytes 262176 | tf_op jit(solution)/shard_map/ppermute | solution.py:298
  34.6 3.4 %collective-permute-done.2.refs_2_ = bf16[64,2048]{1,0:T(8,128)(2,1)S(1)} collective-permute-done((bf16[64,2048]{1,0:T(8,128)(2,1)S(1)}, bf16[64,2048]{1,0:T(8,128)(2,1)S(1)}, u32[]{:S(2)}, u32[]{:S(2)}) %collective-permute-start.2) | collective-permute-done | bytes 262176 | tf_op jit(solution)/shard_map/ppermute | solution.py:298
  41.1 3.0 %collective-permute-done.7.refs_1_ = bf16[64,2176]{1,0:T(8,128)(2,1)} collective-permute-done((bf16[64,2176]{1,0:T(8,128)(2,1)S(1)}, bf16[64,2176]{1,0:T(8,128)(2,1)}, u32[]{:S(2)}, u32[]{:S(2)}) %collective-permute-start.7) | collective-permute-done | bytes 278560 | tf_op jit(solution)/shard_map/ppermute | solution.py:298
  51.9 4.9 %collective-permute-done.13.refs_5_ = bf16[64,2048]{1,0:T(8,128)(2,1)} collective-permute-done((bf16[64,2048]{1,0:T(8,128)(2,1)}, bf16[64,2048]{1,0:T(8,128)(2,1)}, u32[]{:S(2)}, u32[]{:S(2)}) %collective-permute-start.13) | collective-permute-done | bytes 262176 | tf_op jit(solution)/shard_map/ppermute | solution.py:290
  57.4 4.3 %plan_and_pack.2 = (bf16[256,2048]{1,0:T(8,128)(2,1)}, bf16[256,2048]{1,0:T(8,128)(2,1)}, bf16[256,128]{1,0:T(8,128)(2,1)}, bf16[256,128]{1,0:T(8,128)(2,1)}, bf...) custom-call(s32[1]{0:T(128)} %bitcast.expert_ref, bf16[64,2176]{1,0:T(8,128)(2,1)} %copy-done.8, ...), custom_call_target="tpu_custom_call" | custom-call | flops 1 | bytes 1 | tf_op jit(solution)/shard_map/plan_and_pack/pallas_call | solution.py:189
  67.9 3.6 %collective-permute-done.18.refs_2_ = bf16[64,2176]{1,0:T(8,128)(2,1)S(1)} collective-permute-done((bf16[64,2176]{1,0:T(8,128)(2,1)}, bf16[64,2176]{1,0:T(8,128)(2,1)S(1)}, u32[]{:S(2)}, u32[]{:S(2)}) %collective-permute-start.18) | collective-permute-done | bytes 278560 | tf_op jit(solution)/shard_map/ppermute | solution.py:298
  77.5 3.0 %multiply_convert_fusion.7 = (bf16[512,768]{1,0:T(8,128)(2,1)S(1)}, f32[512,768]{1,0:T(8,128)}) fusion(f32[512,768]{1,0:T(8,128)S(1)} %fusion.22, bf16[512,2048]{1,0:T(8,128)(2,1)S(1)} %constant_dynamic-update-slice_fusion, bf16[1,2048,768]{2,1,0:T(8,128)(2,1)S(1)} %copy-done), kind=kOutput, calls=%fused_computation.44 | convolution fusion | flops 1612972032 | bytes 9175040 | tf_op jit(solution)/shard_map/dot_general | solution.py:102
  84.4 4.4 %pack.2 = (bf16[256,2048]{1,0:T(8,128)(2,1)}, bf16[256,2048]{1,0:T(8,128)(2,1)}) custom-call(bf16[2,256,256]{2,1,0:T(8,128)(2,1)} %get-tuple-element.57.pick_ref, bf16[64,2048]{1,0:T(8,128)(2,1)} %refs_0_.1, bf16[64,2048]{1,0:T(8,128)(2,1)} %collective-permute-done.11.refs_1_, bf16[64,2048]{1,0:T(8,128)(2,1)} %collective-permute-done.12.refs_2_, ...), custom_call_target="tpu_custom_call" | custom-call | flops 1 | bytes 1 | tf_op jit(solution)/shard_map/pack/pallas_call | solution.py:225
  93.8 3.1 %fusion.37 = bf16[256,2048]{1,0:T(8,128)(2,1)S(1)} fusion(bf16[1,768,2048]{2,1,0:T(8,128)(2,1)} %param.13, f32[256]{0:T(256)S(1)} %get-tuple-element.91, bf16[512,768]{1,0:T(8,128)(2,1)S(1)} %copy-done.43), kind=kOutput, calls=%fused_computation.34 | convolution fusion | flops 806354944 | bytes 4588544 | tf_op jit(solution)/shard_map/dot_general | solution.py:102
  103.7 11.3 %collective-permute-done.28.refs_1_ = bf16[192,2048]{1,0:T(8,128)(2,1)S(1)} collective-permute-done((bf16[192,2048]{1,0:T(8,128)(2,1)S(1)}, bf16[192,2048]{1,0:T(8,128)(2,1)S(1)}, u32[]{:S(2)}, u32[]{:S(2)}) %collective-permute-start.28) | collective-permute-done | bytes 786464 | tf_op jit(solution)/shard_map/ppermute | solution.py:298
  121.8 10.8 %collective-permute-done.30.refs_3_ = bf16[128,2048]{1,0:T(8,128)(2,1)S(1)} collective-permute-done((bf16[128,2048]{1,0:T(8,128)(2,1)S(1)}, bf16[128,2048]{1,0:T(8,128)(2,1)S(1)}, u32[]{:S(2)}, u32[]{:S(2)}) %collective-permute-start.30) | collective-permute-done | bytes 524320 | tf_op jit(solution)/shard_map/ppermute | solution.py:290
  133.4 3.4 %spread.2 = (bf16[64,2048]{1,0:T(8,128)(2,1)}, bf16[64,2048]{1,0:T(8,128)(2,1)}, bf16[64,2048]{1,0:T(8,128)(2,1)}, bf16[64,2048]{1,0:T(8,128)(2,1)}) custom-call(bf16[256,512]{1,0:T(8,128)(2,1)} %get-tuple-element.72.place_ref, bf16[256,2048]{1,0:T(8,128)(2,1)} %copy-done.6, bf16[256,2048]{1,0:T(8,128)(2,1)} %copy-done.7, bf16[128,2048]{1,0:T(8,128)(2,1)} %copy-done.27, ...), custom_call_target="tpu_custom_call" | custom-call | flops 1 | bytes 1 | tf_op jit(solution)/shard_map/spread/pallas_call | solution.py:252
  136.8 4.3 %plan_and_pack.3 = (bf16[256,2048]{1,0:T(8,128)(2,1)}, bf16[256,2048]{1,0:T(8,128)(2,1)}, bf16[256,128]{1,0:T(8,128)(2,1)}, bf16[256,128]{1,0:T(8,128)(2,1)}, bf...) custom-call(s32[1]{0:T(128)} %bitcast.expert_ref, bf16[64,2176]{1,0:T(8,128)(2,1)} %copy-done.30, ...), custom_call_target="tpu_custom_call" | custom-call | flops 1 | bytes 1 | tf_op jit(solution)/shard_map/plan_and_pack/pallas_call | solution.py:189
  147.0 3.2 %collective-permute-start.31 = (bf16[64,2048]{1,0:T(8,128)(2,1)}, bf16[64,2048]{1,0:T(8,128)(2,1)S(1)}, u32[]{:S(2)}, u32[]{:S(2)}) collective-permute-start(bf16[64,2048]{1,0:T(8,128)(2,1)} %get-tuple-element.65), channel_id=1, source_target_pairs={{0,24},{2,26},{4,28},{6,30},{8,0},{10,2},{12,4},{14,6},{16,8},{18,... | collective-permute-start | bytes 786440 | tf_op jit(solution)/shard_map/ppermute | solution.py:293
  152.8 10.6 %collective-permute-done.37.refs_3_ = bf16[192,2048]{1,0:T(8,128)(2,1)} collective-permute-done((bf16[192,2048]{1,0:T(8,128)(2,1)}, bf16[192,2048]{1,0:T(8,128)(2,1)}, u32[]{:S(2)}, u32[]{:S(2)}) %collective-permute-start.37) | collective-permute-done | bytes 786464 | tf_op jit(solution)/shard_map/ppermute | solution.py:298
  170.1 3.2 %multiply_convert_fusion.4 = (bf16[512,768]{1,0:T(8,128)(2,1)}, f32[512,768]{1,0:T(8,128)}) fusion(f32[512,768]{1,0:T(8,128)S(1)} %fusion.16, bf16[512,2048]{1,0:T(8,128)(2,1)S(1)} %constant_dynamic-update-slice_fusion.2, bf16[1,2048,768]{2,1,0:T(8,128)(2,1)S(1)} %copy-done), kind=kOutput, calls=%fused_computation.40 | convolution fusion | flops 1612972032 | bytes 9175040 | tf_op jit(solution)/shard_map/dot_general | solution.py:102
  173.4 4.2 %collective-permute-done.38.refs_3_ = bf16[128,2048]{1,0:T(8,128)(2,1)S(1)} collective-permute-done((bf16[128,2048]{1,0:T(8,128)(2,1)S(1)}, bf16[128,2048]{1,0:T(8,128)(2,1)S(1)}, u32[]{:S(2)}, u32[]{:S(2)}) %collective-permute-start.38) | collective-permute-done | bytes 524320 | tf_op jit(solution)/shard_map/ppermute | solution.py:290
  178.3 3.3 %spread.3 = (bf16[64,2048]{1,0:T(8,128)(2,1)}, bf16[64,2048]{1,0:T(8,128)(2,1)}, bf16[64,2048]{1,0:T(8,128)(2,1)}, bf16[64,2048]{1,0:T(8,128)(2,1)}) custom-call(bf16[256,512]{1,0:T(8,128)(2,1)} %get-tuple-element.72.place_ref, bf16[256,2048]{1,0:T(8,128)(2,1)} %copy-done.5, bf16[256,2048]{1,0:T(8,128)(2,1)} %collective-permute-done.34.refs_1_, ...), custom_call_target="tpu_custom_call" | custom-call | flops 1 | bytes 1 | tf_op jit(solution)/shard_map/spread/pallas_call | solution.py:252
  181.6 3.3 %collective-permute-start.39 = (bf16[64,2048]{1,0:T(8,128)(2,1)}, bf16[64,2048]{1,0:T(8,128)(2,1)S(1)}, u32[]{:S(2)}, u32[]{:S(2)}) collective-permute-start(bf16[64,2048]{1,0:T(8,128)(2,1)} %get-tuple-element.74), channel_id=1, source_target_pairs={{0,24},{2,26},{4,28},{6,30},{8,0},{10,2},{12,4},{14,6},{16,8},{18,... | collective-permute-start | bytes 786440 | tf_op jit(solution)/shard_map/ppermute | solution.py:293
  187.1 2.7 %fusion.55 = f32[1024,768]{1,0:T(8,128)} fusion(bf16[512,768]{1,0:T(8,128)(2,1)S(1)} %copy-done.18, bf16[512,2048]{1,0:T(8,128)(2,1)S(1)} %copy-done.23, s32[]{:T(128)S(6)} %select_n.31), kind=kOutput, calls=%fused_computation.52 | convolution fusion | flops 805306368 | bytes 4980740 | tf_op jit(solution)/shard_map/dot_general | solution.py:55
  194.3 4.5 %pack.3 = (bf16[256,2048]{1,0:T(8,128)(2,1)}, bf16[256,2048]{1,0:T(8,128)(2,1)}) custom-call(bf16[2,256,256]{2,1,0:T(8,128)(2,1)} %get-tuple-element.81.pick_ref, bf16[64,2048]{1,0:T(8,128)(2,1)} %copy-done.37, bf16[192,2048]{1,0:T(8,128)(2,1)} %copy-done.19, bf16[64,2048]{1,0:T(8,128)(2,1)} %copy-done.38, bf16[192,2048]{1,0:T(8,128)(2,1)} %collective-permute-done.37.refs_3_), custom_call_target="tpu_custom_call" | custom-call | flops 1 | bytes 1 | tf_op jit(solution)/shard_map/pack/pallas_call | solution.py:225
  199.9 7.4 %collective-permute-done.40 = bf16[64,2048]{1,0:T(8,128)(2,1)S(1)} collective-permute-done((bf16[64,2048]{1,0:T(8,128)(2,1)}, bf16[64,2048]{1,0:T(8,128)(2,1)S(1)}, u32[]{:S(2)}, u32[]{:S(2)}) %collective-permute-start.40) | collective-permute-done | bytes 262176 | tf_op jit(solution)/shard_map/ppermute | solution.py:293
  (232 shorter events, 100.5 us)
Async XLA Ops:
  7.4 20.5 %collective-permute-start.4 = (bf16[64,2176]{1,0:T(8,128)(2,1)S(1)}, bf16[64,2176]{1,0:T(8,128)(2,1)S(1)}, u32[]{:S(2)}, u32[]{:S(2)}) collective-permute-start(bf16[64,2176]{1,0:T(8,128)(2,1)S(1)} %concatenate.27.refs_0_), channel_id=1, source_target_pairs={{0,4},{2,6},{4,0},{6,2},{8,12},{10,14},{12,8},{14,10},{16,20},{18,... | collective-permute-start | bytes 835592 | tf_op jit(solution)/shard_map/ppermute | solution.py:290
  15.3 14.1 %collective-permute-start.10 = (bf16[64,2176]{1,0:T(8,128)(2,1)S(1)}, bf16[64,2176]{1,0:T(8,128)(2,1)}, u32[]{:S(2)}, u32[]{:S(2)}) collective-permute-start(bf16[64,2176]{1,0:T(8,128)(2,1)S(1)} %collective-permute-done.6.refs_1_), channel_id=1, source_target_pairs={{0,8},{2,10},{4,12},{6,14},{8,16},{10,18},{12,20},{14,22},{16,24},... | collective-permute-start | bytes 835592 | tf_op jit(solution)/shard_map/ppermute | solution.py:293
  18.5 13.9 %collective-permute-start.3 = (bf16[64,2176]{1,0:T(8,128)(2,1)S(1)}, bf16[64,2176]{1,0:T(8,128)(2,1)S(1)}, u32[]{:S(2)}, u32[]{:S(2)}) collective-permute-start(bf16[64,2176]{1,0:T(8,128)(2,1)S(1)} %concatenate.27.refs_0_), channel_id=1, source_target_pairs={{0,1},{1,0},{2,3},{3,2},{4,5},{5,4},{6,7},{7,6},{8,9},{9,8},{10,11... | collective-permute-start | bytes 835592 | tf_op jit(solution)/shard_map/ppermute | solution.py:298
  19.0 19.0 %collective-permute-start.2 = (bf16[64,2048]{1,0:T(8,128)(2,1)S(1)}, bf16[64,2048]{1,0:T(8,128)(2,1)S(1)}, u32[]{:S(2)}, u32[]{:S(2)}) collective-permute-start(bf16[64,2048]{1,0:T(8,128)(2,1)S(1)} %collective-permute-done.1.refs_4_), channel_id=1, source_target_pairs={{0,1},{1,0},{2,3},{3,2},{4,5},{5,4},{6,7},{7,6},{8,9},{9,8},{10,11... | collective-permute-start | bytes 786440 | tf_op jit(solution)/shard_map/ppermute | solution.py:298
  27.9 16.2 %collective-permute-start.7 = (bf16[64,2176]{1,0:T(8,128)(2,1)S(1)}, bf16[64,2176]{1,0:T(8,128)(2,1)}, u32[]{:S(2)}, u32[]{:S(2)}) collective-permute-start(bf16[64,2176]{1,0:T(8,128)(2,1)S(1)} %collective-permute-done.6.refs_1_), channel_id=1, source_target_pairs={{0,1},{1,0},{2,3},{3,2},{4,5},{5,4},{6,7},{7,6},{8,9},{9,8},{10,11... | collective-permute-start | bytes 835592 | tf_op jit(solution)/shard_map/ppermute | solution.py:298
  29.4 16.1 %collective-permute-start.14 = (bf16[64,2176]{1,0:T(8,128)(2,1)}, bf16[64,2176]{1,0:T(8,128)(2,1)}, u32[]{:S(2)}, u32[]{:S(2)}) collective-permute-start(bf16[64,2176]{1,0:T(8,128)(2,1)} %collective-permute-done.10.refs_2_), channel_id=1, source_target_pairs={{0,8},{2,10},{4,12},{6,14},{8,16},{10,18},{12,20},{14,22},{16,24},... | collective-permute-start | bytes 835592 | tf_op jit(solution)/shard_map/ppermute | solution.py:293
  33.1 15.8 %collective-permute-start.5 = (bf16[64,2176]{1,0:T(8,128)(2,1)S(1)}, bf16[64,2176]{1,0:T(8,128)(2,1)}, u32[]{:S(2)}, u32[]{:S(2)}) collective-permute-start(bf16[64,2176]{1,0:T(8,128)(2,1)S(1)} %collective-permute-done.4.refs_4_), channel_id=1, source_target_pairs={{0,1},{1,0},{2,3},{3,2},{4,5},{5,4},{6,7},{7,6},{8,9},{9,8},{10,11... | collective-permute-start | bytes 835592 | tf_op jit(solution)/shard_map/ppermute | solution.py:298
  44.1 13.3 %collective-permute-start.15 = (bf16[64,2176]{1,0:T(8,128)(2,1)}, bf16[64,2176]{1,0:T(8,128)(2,1)}, u32[]{:S(2)}, u32[]{:S(2)}) collective-permute-start(bf16[64,2176]{1,0:T(8,128)(2,1)} %collective-permute-done.10.refs_2_), channel_id=1, source_target_pairs={{0,4},{2,6},{4,0},{6,2},{8,12},{10,14},{12,8},{14,10},{16,20},{18,... | collective-permute-start | bytes 835592 | tf_op jit(solution)/shard_map/ppermute | solution.py:290
  61.7 13.8 %collective-permute-start.17 = (bf16[256,2048]{1,0:T(8,128)(2,1)}, bf16[256,2048]{1,0:T(8,128)(2,1)S(1)}, u32[]{:S(2)}, u32[]{:S(2)}) collective-permute-start(bf16[256,2048]{1,0:T(8,128)(2,1)} %get-tuple-element.52), channel_id=1, source_target_pairs={{0,2},{2,0},{4,6},{6,4},{8,10},{10,8},{12,14},{14,12},{16,18},{18,... | collective-permute-start | bytes 3145736 | tf_op jit(solution)/shard_map/ppermute | solution.py:287
  63.4 17.1 %collective-permute-start.21 = (bf16[64,2176]{1,0:T(8,128)(2,1)}, bf16[64,2176]{1,0:T(8,128)(2,1)S(1)}, u32[]{:S(2)}, u32[]{:S(2)}) collective-permute-start(bf16[64,2176]{1,0:T(8,128)(2,1)} %collective-permute-done.15.refs_6_), channel_id=1, source_target_pairs={{0,1},{1,0},{2,3},{3,2},{4,5},{5,4},{6,7},{7,6},{8,9},{9,8},{10,11... | collective-permute-start | bytes 835592 | tf_op jit(solution)/shard_map/ppermute | solution.py:298
  91.6 23.4 %collective-permute-start.28 = (bf16[192,2048]{1,0:T(8,128)(2,1)S(1)}, bf16[192,2048]{1,0:T(8,128)(2,1)S(1)}, u32[]{:S(2)}, u32[]{:S(2)}) collective-permute-start(bf16[192,2048]{1,0:T(8,128)(2,1)S(1)} %pad_maximum_fusion), channel_id=1, source_target_pairs={{0,1},{1,0},{2,3},{3,2},{4,5},{5,4},{6,7},{7,6},{8,9},{9,8},{10,11... | collective-permute-start | bytes 2359304 | tf_op jit(solution)/shard_map/ppermute | solution.py:298
  92.2 22.8 %collective-permute-start.27 = (bf16[128,2048]{1,0:T(8,128)(2,1)S(1)}, bf16[128,2048]{1,0:T(8,128)(2,1)S(1)}, u32[]{:S(2)}, u32[]{:S(2)}) collective-permute-start(bf16[128,2048]{1,0:T(8,128)(2,1)S(1)} %slice.50), channel_id=1, source_target_pairs={{0,4},{2,6},{4,0},{6,2},{8,12},{10,14},{12,8},{14,10},{16,20},{18,... | collective-permute-start | bytes 1572872 | tf_op jit(solution)/shard_map/ppermute | solution.py:290
  96.9 21.2 %collective-permute-start.29 = (bf16[256,2048]{1,0:T(8,128)(2,1)S(1)}, bf16[256,2048]{1,0:T(8,128)(2,1)S(1)}, u32[]{:S(2)}, u32[]{:S(2)}) collective-permute-start(bf16[256,2048]{1,0:T(8,128)(2,1)S(1)} %fusion.37), channel_id=1, source_target_pairs={{0,2},{2,0},{4,6},{6,4},{8,10},{10,8},{12,14},{14,12},{16,18},{18,... | collective-permute-start | bytes 3145736 | tf_op jit(solution)/shard_map/ppermute | solution.py:287
  118.1 18.7 %collective-permute-start.34 = (bf16[256,2048]{1,0:T(8,128)(2,1)}, bf16[256,2048]{1,0:T(8,128)(2,1)}, u32[]{:S(2)}, u32[]{:S(2)}) collective-permute-start(bf16[256,2048]{1,0:T(8,128)(2,1)} %fusion.43), channel_id=1, source_target_pairs={{0,2},{2,0},{4,6},{6,4},{8,10},{10,8},{12,14},{14,12},{16,18},{18,... | collective-permute-start | bytes 3145736 | tf_op jit(solution)/shard_map/ppermute | solution.py:287
  118.2 14.4 %collective-permute-start.30 = (bf16[128,2048]{1,0:T(8,128)(2,1)S(1)}, bf16[128,2048]{1,0:T(8,128)(2,1)S(1)}, u32[]{:S(2)}, u32[]{:S(2)}) collective-permute-start(bf16[128,2048]{1,0:T(8,128)(2,1)S(1)} %slice.51), channel_id=1, source_target_pairs={{0,4},{2,6},{4,0},{6,2},{8,12},{10,14},{12,8},{14,10},{16,20},{18,... | collective-permute-start | bytes 1572872 | tf_op jit(solution)/shard_map/ppermute | solution.py:290
  141.1 24.7 %collective-permute-start.35 = (bf16[256,2048]{1,0:T(8,128)(2,1)}, bf16[256,2048]{1,0:T(8,128)(2,1)}, u32[]{:S(2)}, u32[]{:S(2)}) collective-permute-start(bf16[256,2048]{1,0:T(8,128)(2,1)} %get-tuple-element.70), channel_id=1, source_target_pairs={{0,2},{2,0},{4,6},{6,4},{8,10},{10,8},{12,14},{14,12},{16,18},{18,... | collective-permute-start | bytes 3145736 | tf_op jit(solution)/shard_map/ppermute | solution.py:287
  143.1 20.2 %collective-permute-start.37 = (bf16[192,2048]{1,0:T(8,128)(2,1)}, bf16[192,2048]{1,0:T(8,128)(2,1)}, u32[]{:S(2)}, u32[]{:S(2)}) collective-permute-start(bf16[192,2048]{1,0:T(8,128)(2,1)} %pad_maximum_fusion.1), channel_id=1, source_target_pairs={{0,1},{1,0},{2,3},{3,2},{4,5},{5,4},{6,7},{7,6},{8,9},{9,8},{10,11... | collective-permute-start | bytes 2359304 | tf_op jit(solution)/shard_map/ppermute | solution.py:298
  145.5 18.8 %collective-permute-start.36 = (bf16[128,2048]{1,0:T(8,128)(2,1)}, bf16[128,2048]{1,0:T(8,128)(2,1)}, u32[]{:S(2)}, u32[]{:S(2)}) collective-permute-start(bf16[128,2048]{1,0:T(8,128)(2,1)} %slice.52), channel_id=1, source_target_pairs={{0,4},{2,6},{4,0},{6,2},{8,12},{10,14},{12,8},{14,10},{16,20},{18,... | collective-permute-start | bytes 1572872 | tf_op jit(solution)/shard_map/ppermute | solution.py:290
  147.0 26.3 %collective-permute-start.31 = (bf16[64,2048]{1,0:T(8,128)(2,1)}, bf16[64,2048]{1,0:T(8,128)(2,1)S(1)}, u32[]{:S(2)}, u32[]{:S(2)}) collective-permute-start(bf16[64,2048]{1,0:T(8,128)(2,1)} %get-tuple-element.65), channel_id=1, source_target_pairs={{0,24},{2,26},{4,28},{6,30},{8,0},{10,2},{12,4},{14,6},{16,8},{18,... | collective-permute-start | bytes 786440 | tf_op jit(solution)/shard_map/ppermute | solution.py:293
  150.2 23.1 %collective-permute-start.32 = (bf16[64,2048]{1,0:T(8,128)(2,1)}, bf16[64,2048]{1,0:T(8,128)(2,1)S(1)}, u32[]{:S(2)}, u32[]{:S(2)}) collective-permute-start(bf16[64,2048]{1,0:T(8,128)(2,1)} %get-tuple-element.66), channel_id=1, source_target_pairs={{0,16},{2,18},{4,20},{6,22},{8,24},{10,26},{12,28},{14,30},{16,0},... | collective-permute-start | bytes 786440 | tf_op jit(solution)/shard_map/ppermute | solution.py:293
  164.3 13.2 %collective-permute-start.38 = (bf16[128,2048]{1,0:T(8,128)(2,1)S(1)}, bf16[128,2048]{1,0:T(8,128)(2,1)S(1)}, u32[]{:S(2)}, u32[]{:S(2)}) collective-permute-start(bf16[128,2048]{1,0:T(8,128)(2,1)S(1)} %slice.53), channel_id=1, source_target_pairs={{0,4},{2,6},{4,0},{6,2},{8,12},{10,14},{12,8},{14,10},{16,20},{18,... | collective-permute-start | bytes 1572872 | tf_op jit(solution)/shard_map/ppermute | solution.py:290
  165.8 34.0 %collective-permute-start.43 = (bf16[256,128]{1,0:T(8,128)(2,1)}, bf16[256,128]{1,0:T(8,128)(2,1)S(1)}, u32[]{:S(2)}, u32[]{:S(2)}) collective-permute-start(bf16[256,128]{1,0:T(8,128)(2,1)} %get-tuple-element.86), channel_id=1, source_target_pairs={{0,2},{2,0},{4,6},{6,4},{8,10},{10,8},{12,14},{14,12},{16,18},{18,... | collective-permute-start | bytes 196616 | tf_op jit(solution)/shard_map/ppermute | solution.py:287
  184.9 22.5 %collective-permute-start.40 = (bf16[64,2048]{1,0:T(8,128)(2,1)}, bf16[64,2048]{1,0:T(8,128)(2,1)S(1)}, u32[]{:S(2)}, u32[]{:S(2)}) collective-permute-start(bf16[64,2048]{1,0:T(8,128)(2,1)} %get-tuple-element.75), channel_id=1, source_target_pairs={{0,16},{2,18},{4,20},{6,22},{8,24},{10,26},{12,28},{14,30},{16,0},... | collective-permute-start | bytes 786440 | tf_op jit(solution)/shard_map/ppermute | solution.py:293
  185.6 21.7 %collective-permute-start.41 = (bf16[64,2048]{1,0:T(8,128)(2,1)}, bf16[64,2048]{1,0:T(8,128)(2,1)}, u32[]{:S(2)}, u32[]{:S(2)}) collective-permute-start(bf16[64,2048]{1,0:T(8,128)(2,1)} %get-tuple-element.76), channel_id=1, source_target_pairs={{0,8},{2,10},{4,12},{6,14},{8,16},{10,18},{12,20},{14,22},{16,24},... | collective-permute-start | bytes 786440 | tf_op jit(solution)/shard_map/ppermute | solution.py:293
  (80 other events, 763.6 us)

commit v9 on v8

--- a/solution.py
+++ b/solution.py
@@ -361,30 +361,29 @@
 
     own_x, weight, pick, place, pre_gate, pre_up, act = enter(
         token_sets,
-        (cot_relay, cot_relay_far, *relay[:4], *cot_near[1:3], cot_far[1]),
-        (relay[4], cot_far[2]),
-    )
-    act = after(act, cot_near[3], relay[5])
+        (*relay[:3], cot_relay, cot_near[1]),
+        (relay[3], cot_relay_far, cot_near[2], cot_far[1]),
+    )
+    act = after(act, relay[4], cot_near[3], cot_far[2])
     parts = leave(lambda rows: (dot(act[rows], w_down) * weight[rows]).astype(BF))
     cot, d_gate, d_up = enter_cot(
-        after(pick, parts[0], relay[6]), cot_sets, weight, pre_gate, pre_up, relay[7]
+        after(pick, parts[0], parts[1], relay[5]), cot_sets, weight, pre_gate, pre_up, relay[6]
     )
     own_grads = cot, d_gate, d_up
-    d_gate, d_up = after((d_gate, d_up), parts[2], cot_relay_ring)
+    d_gate, d_up = after((d_gate, d_up), parts[2], relay[7])
     grad_parts = leave(lambda rows: input_rows(d_gate[rows], d_up[rows], w_gate, w_up))
     chunks = home(after(place, grad_parts[0]), parts)
-    parts = grad_parts
 
     x, weight, pick, _, pre_gate, pre_up, other_act = enter(
-        token_other, (chunks[0], parts[1]), (parts[2], cot_relay_far_ring)
-    )
-    grad_chunks = home(after(place, other_act, *chunks[1:]), parts)
+        token_other, (chunks[0], *grad_parts[1:3]), (grad_parts[3], cot_relay_ring)
+    )
+    grad_chunks = home(after(place, other_act, *chunks[1:]), grad_parts)
     own_grads = after(own_grads, grad_chunks[0])
     own = grads(own_x, act, *own_grads)
     cot, d_gate, d_up = enter_cot(
         after(pick, *own, grad_chunks[1]),
         (cot_relay, cot_relay_ring, cot_relay_far, cot_relay_far_ring),
-        weight, pre_gate, pre_up, grad_chunks[2],
+        weight, pre_gate, pre_up,
     )
     other = grads(x, other_act, cot, d_gate, d_up)
     grad_gate, grad_up, grad_down = ((a + b).astype(BF)[None] for a, b in zip(own, other))

time: 221 us -> 230 us (1.041); the launches traced: 220 us -> 226 us
  waiting for transfers between devices: 80.8 us -> 103 us
  starting transfers between devices: 51.7 us -> 34.8 us
    ppermute x12, waiting for transfers between devices: 9.69 us -> 37.8 us  [to_z(): lax.ppermute(rows, 'expert', [(i, (i + 4 * step) % experts) for i in rang...]
    ppermute x12, starting transfers between devices: 20 us -> 7.85 us  [to_z(): lax.ppermute(rows, 'expert', [(i, (i + 4 * step) % experts) for i in rang...]
    ppermute x12, waiting for transfers between devices: 43.9 us -> 40.4 us  [to_y(): return lax.ppermute(rows, 'replica', [(0, 1), (1, 0)])]
    ppermute x12, starting transfers between devices: 15.4 us -> 12.3 us  [to_y(): return lax.ppermute(rows, 'replica', [(0, 1), (1, 0)])]
    ppermute x12, waiting for transfers between devices: 27.2 us -> 24.4 us  [to_x(): return lax.ppermute(rows, 'expert', [(i, i ^ 2) for i in range(experts)])]
    unnamed x122 -> x124, local copies, waits for them, and re-layouts: 13.5 us -> 11.9 us
where the time goes in v9:
time: 230 us; the launch traced here: 226 us
  waiting for transfers between devices  103 us (45%)
  matrix products  36.5 us (16%)
  starting transfers between devices  34.8 us (15%)
  Pallas kernels  24.4 us (11%)
  local copies, waits for them, and re-layouts  17.6 us (8%)
  other arithmetic  8.7 us (4%)
    ppermute x12, waiting for transfers between devices, to_y(): return lax.ppermute(rows, 'replica', [(0, 1), (1, 0)])  40.4 us
    ppermute x12, waiting for transfers between devices, to_z(): lax.ppermute(rows, 'expert', [(i, (i + 4 * step) % experts) for i in rang...  37.8 us
    ppermute x12, waiting for transfers between devices, to_x(): return lax.ppermute(rows, 'expert', [(i, i ^ 2) for i in range(experts)])  24.4 us
    ppermute x12, starting transfers between devices, to_x(): return lax.ppermute(rows, 'expert', [(i, i ^ 2) for i in range(experts)])  14.3 us
    dot_general x6, matrix products, outer_sum(): lax.dot_general(left, right, (((0,), (0,)), ((), ())), preferred_element_...  13.3 us
    dot_general x6, matrix products, dot(): return jnp.dot(left, right, preferred_element_type=F32)  12.7 us
    ppermute x12, starting transfers between devices, to_y(): return lax.ppermute(rows, 'replica', [(0, 1), (1, 0)])  12.3 us
    unnamed x124, local copies, waits for them, and re-layouts  11.9 us
  transfers between devices with their start and end apart: 44, of which 19 were waited for; matrix products, arithmetic and copies ran while one was open for 18% of the time, Pallas kernels for 5%

profile of v9, /device:TPU:0, one launch (start us, length us, event | category | flops | bytes accessed | tf_op | source)
XLA Modules:
  0.0 226.0 jit_solution(14711148417575228398)
XLA Ops:
  2.8 3.1 %collective-permute-start.3 = (bf16[64,2176]{1,0:T(8,128)(2,1)S(1)}, bf16[64,2176]{1,0:T(8,128)(2,1)}, u32[]{:S(2)}, u32[]{:S(2)}) collective-permute-start(bf16[64,2176]{1,0:T(8,128)(2,1)S(1)} %concatenate.27.refs_0_), channel_id=1, source_target_pairs={{0,8},{2,10},{4,12},{6,14},{8,16},{10,18},{12,20},{14,22},{16,24},... | collective-permute-start | bytes 835592 | tf_op jit(solution)/shard_map/ppermute | solution.py:293
  7.4 6.5 %collective-permute-done.4.refs_4_ = bf16[64,2048]{1,0:T(8,128)(2,1)S(1)} collective-permute-done((bf16[64,2048]{1,0:T(8,128)(2,1)}, bf16[64,2048]{1,0:T(8,128)(2,1)S(1)}, u32[]{:S(2)}, u32[]{:S(2)}) %collective-permute-start.4) | collective-permute-done | bytes 262176 | tf_op jit(solution)/shard_map/ppermute | solution.py:290
  18.5 6.2 %collective-permute-done.7.refs_2_ = bf16[64,2176]{1,0:T(8,128)(2,1)} collective-permute-done((bf16[64,2176]{1,0:T(8,128)(2,1)}, bf16[64,2176]{1,0:T(8,128)(2,1)}, u32[]{:S(2)}, u32[]{:S(2)}) %collective-permute-start.7) | collective-permute-done | bytes 278560 | tf_op jit(solution)/shard_map/ppermute | solution.py:293
  27.9 12.1 %collective-permute-done.6.refs_0_ = bf16[64,2048]{1,0:T(8,128)(2,1)S(1)} collective-permute-done((bf16[64,2048]{1,0:T(8,128)(2,1)}, bf16[64,2048]{1,0:T(8,128)(2,1)S(1)}, u32[]{:S(2)}, u32[]{:S(2)}) %collective-permute-start.6) | collective-permute-done | bytes 262176 | tf_op jit(solution)/shard_map/ppermute | solution.py:298
  44.1 8.5 %collective-permute-done.8.refs_1_ = bf16[64,2048]{1,0:T(8,128)(2,1)} collective-permute-done((bf16[64,2048]{1,0:T(8,128)(2,1)}, bf16[64,2048]{1,0:T(8,128)(2,1)}, u32[]{:S(2)}, u32[]{:S(2)}) %collective-permute-start.8) | collective-permute-done | bytes 262176 | tf_op jit(solution)/shard_map/ppermute | solution.py:293
  52.7 3.0 %collective-permute-done.12.refs_7_ = bf16[64,2176]{1,0:T(8,128)(2,1)} collective-permute-done((bf16[64,2176]{1,0:T(8,128)(2,1)}, bf16[64,2176]{1,0:T(8,128)(2,1)}, u32[]{:S(2)}, u32[]{:S(2)}) %collective-permute-start.12) | collective-permute-done | bytes 278560 | tf_op jit(solution)/shard_map/ppermute | solution.py:290
  55.6 4.3 %plan_and_pack.2 = (bf16[256,2048]{1,0:T(8,128)(2,1)}, bf16[256,2048]{1,0:T(8,128)(2,1)}, bf16[256,128]{1,0:T(8,128)(2,1)}, bf16[256,128]{1,0:T(8,128)(2,1)}, bf...) custom-call(s32[1]{0:T(128)} %bitcast.expert_ref, bf16[64,2176]{1,0:T(8,128)(2,1)} %copy-done.7, ...), custom_call_target="tpu_custom_call" | custom-call | flops 1 | bytes 1 | tf_op jit(solution)/shard_map/plan_and_pack/pallas_call | solution.py:189
  64.7 4.6 %collective-permute-done.15.refs_2_ = bf16[64,2048]{1,0:T(8,128)(2,1)S(1)} collective-permute-done((bf16[64,2048]{1,0:T(8,128)(2,1)S(1)}, bf16[64,2048]{1,0:T(8,128)(2,1)S(1)}, u32[]{:S(2)}, u32[]{:S(2)}) %collective-permute-start.15) | collective-permute-done | bytes 262176 | tf_op jit(solution)/shard_map/ppermute | solution.py:298
  70.1 5.1 %collective-permute-done.16.refs_2_ = bf16[64,2048]{1,0:T(8,128)(2,1)S(1)} collective-permute-done((bf16[64,2048]{1,0:T(8,128)(2,1)}, bf16[64,2048]{1,0:T(8,128)(2,1)S(1)}, u32[]{:S(2)}, u32[]{:S(2)}) %collective-permute-start.16) | collective-permute-done | bytes 262176 | tf_op jit(solution)/shard_map/ppermute | solution.py:293
  79.1 3.0 %multiply_convert_fusion.7 = (bf16[512,768]{1,0:T(8,128)(2,1)S(1)}, f32[512,768]{1,0:T(8,128)}) fusion(f32[512,768]{1,0:T(8,128)S(1)} %fusion.22, bf16[512,2048]{1,0:T(8,128)(2,1)S(1)} %constant_dynamic-update-slice_fusion, bf16[1,2048,768]{2,1,0:T(8,128)(2,1)S(1)} %copy-done), kind=kOutput, calls=%fused_computation.44 | convolution fusion | flops 1612972032 | bytes 9175040 | tf_op jit(solution)/shard_map/dot_general | solution.py:102
  91.6 4.9 %collective-permute-done.23.refs_6_ = bf16[64,2176]{1,0:T(8,128)(2,1)S(1)} collective-permute-done((bf16[64,2176]{1,0:T(8,128)(2,1)}, bf16[64,2176]{1,0:T(8,128)(2,1)S(1)}, u32[]{:S(2)}, u32[]{:S(2)}) %collective-permute-start.23) | collective-permute-done | bytes 278560 | tf_op jit(solution)/shard_map/ppermute | solution.py:298
  97.9 4.4 %pack.2 = (bf16[256,2048]{1,0:T(8,128)(2,1)}, bf16[256,2048]{1,0:T(8,128)(2,1)}) custom-call(bf16[2,256,256]{2,1,0:T(8,128)(2,1)} %get-tuple-element.56.pick_ref, bf16[64,2048]{1,0:T(8,128)(2,1)} %refs_0_.1, bf16[64,2048]{1,0:T(8,128)(2,1)} %collective-permute-done.8.refs_1_, bf16[64,2048]{1,0:T(8,128)(2,1)} %copy-done.12, bf16[64,2048]{1,0:T(8,128)(2,1)} %copy-done.14, ...), custom_call_target="tpu_custom_call" | custom-call | flops 1 | bytes 1 | tf_op jit(solution)/shard_map/pack/pallas_call | solution.py:225
  107.8 4.3 %collective-permute-done.26.refs_3_ = bf16[64,2176]{1,0:T(8,128)(2,1)S(1)} collective-permute-done((bf16[64,2176]{1,0:T(8,128)(2,1)}, bf16[64,2176]{1,0:T(8,128)(2,1)S(1)}, u32[]{:S(2)}, u32[]{:S(2)}) %collective-permute-start.26) | collective-permute-done | bytes 278560 | tf_op jit(solution)/shard_map/ppermute | solution.py:298
  114.9 3.6 %multiply_convert_fusion.5 = (bf16[512,768]{1,0:T(8,128)(2,1)S(1)}, bf16[512,768]{1,0:T(8,128)(2,1)S(1)}) fusion(f32[512,768]{1,0:T(8,128)S(1)} %copy-done.60, f32[512,768]{1,0:T(8,128)} %get-tuple-element.92, bf16[512,2048]{1,0:T(8,128)(2,1)S(1)} %multiply_convert_fusion.1, bf16[1,768,2048]{2,1,0:T(8,128)(2,1)S(1)} %copy-done.50), kind=kOutput, calls=%fused_computation.42 | convolution fusion | flops 1615724544 | bytes 9961472 | tf_op jit(solution)/shard_map/dot_general | solution.py:41
  126.6 5.2 %collective-permute-done.29.refs_3_ = bf16[128,2048]{1,0:T(8,128)(2,1)} collective-permute-done((bf16[128,2048]{1,0:T(8,128)(2,1)S(1)}, bf16[128,2048]{1,0:T(8,128)(2,1)}, u32[]{:S(2)}, u32[]{:S(2)}) %collective-permute-start.29) | collective-permute-done | bytes 524320 | tf_op jit(solution)/shard_map/ppermute | solution.py:290
  131.8 3.4 %spread.2 = (bf16[64,2048]{1,0:T(8,128)(2,1)}, bf16[64,2048]{1,0:T(8,128)(2,1)}, bf16[64,2048]{1,0:T(8,128)(2,1)}, bf16[64,2048]{1,0:T(8,128)(2,1)}) custom-call(bf16[256,512]{1,0:T(8,128)(2,1)} %get-tuple-element.71.place_ref, bf16[256,2048]{1,0:T(8,128)(2,1)} %fusion.40.refs_0_, bf16[256,2048]{1,0:T(8,128)(2,1)} %copy-done.6, ...), custom_call_target="tpu_custom_call" | custom-call | flops 1 | bytes 1 | tf_op jit(solution)/shard_map/spread/pallas_call | solution.py:252
  135.3 6.6 %collective-permute-done.34.refs_2_ = bf16[128,2048]{1,0:T(8,128)(2,1)S(1)} collective-permute-done((bf16[128,2048]{1,0:T(8,128)(2,1)S(1)}, bf16[128,2048]{1,0:T(8,128)(2,1)S(1)}, u32[]{:S(2)}, u32[]{:S(2)}) %collective-permute-start.34) | collective-permute-done | bytes 524320 | tf_op jit(solution)/shard_map/ppermute | solution.py:290
  141.9 4.5 %plan_and_pack.3 = (bf16[256,2048]{1,0:T(8,128)(2,1)}, bf16[256,2048]{1,0:T(8,128)(2,1)}, bf16[256,128]{1,0:T(8,128)(2,1)}, bf16[256,128]{1,0:T(8,128)(2,1)}, bf...) custom-call(s32[1]{0:T(128)} %bitcast.expert_ref, bf16[64,2176]{1,0:T(8,128)(2,1)} %copy-done.31, ...), custom_call_target="tpu_custom_call" | custom-call | flops 1 | bytes 1 | tf_op jit(solution)/shard_map/plan_and_pack/pallas_call | solution.py:189
  154.6 14.5 %collective-permute-done.37.refs_1_ = bf16[192,2048]{1,0:T(8,128)(2,1)} collective-permute-done((bf16[192,2048]{1,0:T(8,128)(2,1)}, bf16[192,2048]{1,0:T(8,128)(2,1)}, u32[]{:S(2)}, u32[]{:S(2)}) %collective-permute-start.37) | collective-permute-done | bytes 786464 | tf_op jit(solution)/shard_map/ppermute | solution.py:298
  173.9 3.2 %multiply_convert_fusion.4 = (bf16[512,768]{1,0:T(8,128)(2,1)}, f32[512,768]{1,0:T(8,128)}) fusion(f32[512,768]{1,0:T(8,128)S(1)} %fusion.16, bf16[512,2048]{1,0:T(8,128)(2,1)S(1)} %constant_dynamic-update-slice_fusion.2, bf16[1,2048,768]{2,1,0:T(8,128)(2,1)S(1)} %copy-done), kind=kOutput, calls=%fused_computation.40 | convolution fusion | flops 1612972032 | bytes 9175040 | tf_op jit(solution)/shard_map/dot_general | solution.py:102
  177.1 9.6 %collective-permute-done.31 = bf16[64,2048]{1,0:T(8,128)(2,1)} collective-permute-done((bf16[64,2048]{1,0:T(8,128)(2,1)S(1)}, bf16[64,2048]{1,0:T(8,128)(2,1)}, u32[]{:S(2)}, u32[]{:S(2)}) %collective-permute-start.31) | collective-permute-done | bytes 262176 | tf_op jit(solution)/shard_map/ppermute | solution.py:293
  186.7 3.2 %spread.3 = (bf16[64,2048]{1,0:T(8,128)(2,1)}, bf16[64,2048]{1,0:T(8,128)(2,1)}, bf16[64,2048]{1,0:T(8,128)(2,1)}, bf16[64,2048]{1,0:T(8,128)(2,1)}) custom-call(bf16[256,512]{1,0:T(8,128)(2,1)} %get-tuple-element.71.place_ref, bf16[256,2048]{1,0:T(8,128)(2,1)} %copy-done.5, bf16[256,2048]{1,0:T(8,128)(2,1)} %collective-permute-done.33.refs_1_, ...), custom_call_target="tpu_custom_call" | custom-call | flops 1 | bytes 1 | tf_op jit(solution)/shard_map/spread/pallas_call | solution.py:252
  202.0 4.5 %pack.3 = (bf16[256,2048]{1,0:T(8,128)(2,1)}, bf16[256,2048]{1,0:T(8,128)(2,1)}) custom-call(bf16[2,256,256]{2,1,0:T(8,128)(2,1)} %get-tuple-element.80.pick_ref, bf16[64,2048]{1,0:T(8,128)(2,1)} %copy-done.37, bf16[192,2048]{1,0:T(8,128)(2,1)} %collective-permute-done.37.refs_1_, bf16[64,2048]{1,0:T(8,128)(2,1)} %copy-done.38, bf16[192,2048]{1,0:T(8,128)(2,1)} %copy-done.21), custom_call_target="tpu_custom_call" | custom-call | flops 1 | bytes 1 | tf_op jit(solution)/shard_map/pack/pallas_call | solution.py:225
  208.8 4.7 %collective-permute-done.39 = bf16[64,2048]{1,0:T(8,128)(2,1)} collective-permute-done((bf16[64,2048]{1,0:T(8,128)(2,1)}, bf16[64,2048]{1,0:T(8,128)(2,1)}, u32[]{:S(2)}, u32[]{:S(2)}) %collective-permute-start.39) | collective-permute-done | bytes 262176 | tf_op jit(solution)/shard_map/ppermute | solution.py:293
  (234 shorter events, 91.7 us)
Async XLA Ops:
  16.9 24.4 %collective-permute-start = (bf16[64,2176]{1,0:T(8,128)(2,1)S(1)}, bf16[64,2176]{1,0:T(8,128)(2,1)S(1)}, u32[]{:S(2)}, u32[]{:S(2)}) collective-permute-start(bf16[64,2176]{1,0:T(8,128)(2,1)S(1)} %concatenate.27.refs_0_), channel_id=1, source_target_pairs={{0,1},{1,0},{2,3},{3,2},{4,5},{5,4},{6,7},{7,6},{8,9},{9,8},{10,11... | collective-permute-start | bytes 835592 | tf_op jit(solution)/shard_map/ppermute | solution.py:298
  24.6 18.2 %collective-permute-start.9 = (bf16[64,2176]{1,0:T(8,128)(2,1)}, bf16[64,2176]{1,0:T(8,128)(2,1)}, u32[]{:S(2)}, u32[]{:S(2)}) collective-permute-start(bf16[64,2176]{1,0:T(8,128)(2,1)} %collective-permute-done.7.refs_2_), channel_id=1, source_target_pairs={{0,8},{2,10},{4,12},{6,14},{8,16},{10,18},{12,20},{14,22},{16,24},... | collective-permute-start | bytes 835592 | tf_op jit(solution)/shard_map/ppermute | solution.py:293
  24.6 19.4 %collective-permute-start.5 = (bf16[64,2176]{1,0:T(8,128)(2,1)}, bf16[64,2176]{1,0:T(8,128)(2,1)}, u32[]{:S(2)}, u32[]{:S(2)}) collective-permute-start(bf16[64,2176]{1,0:T(8,128)(2,1)} %collective-permute-done.3.refs_1_), channel_id=1, source_target_pairs={{0,1},{1,0},{2,3},{3,2},{4,5},{5,4},{6,7},{7,6},{8,9},{9,8},{10,11... | collective-permute-start | bytes 835592 | tf_op jit(solution)/shard_map/ppermute | solution.py:298
  25.9 14.1 %collective-permute-start.6 = (bf16[64,2048]{1,0:T(8,128)(2,1)}, bf16[64,2048]{1,0:T(8,128)(2,1)S(1)}, u32[]{:S(2)}, u32[]{:S(2)}) collective-permute-start(bf16[64,2048]{1,0:T(8,128)(2,1)} %refs_0_.1), channel_id=1, source_target_pairs={{0,1},{1,0},{2,3},{3,2},{4,5},{5,4},{6,7},{7,6},{8,9},{9,8},{10,11... | collective-permute-start | bytes 786440 | tf_op jit(solution)/shard_map/ppermute | solution.py:298
  26.7 17.4 %collective-permute-start.2 = (bf16[64,2176]{1,0:T(8,128)(2,1)}, bf16[64,2176]{1,0:T(8,128)(2,1)}, u32[]{:S(2)}, u32[]{:S(2)}) collective-permute-start(bf16[64,2176]{1,0:T(8,128)(2,1)} %collective-permute-done.1.refs_4_), channel_id=1, source_target_pairs={{0,1},{1,0},{2,3},{3,2},{4,5},{5,4},{6,7},{7,6},{8,9},{9,8},{10,11... | collective-permute-start | bytes 835592 | tf_op jit(solution)/shard_map/ppermute | solution.py:298
  59.9 16.7 %collective-permute-start.13 = (bf16[256,2048]{1,0:T(8,128)(2,1)}, bf16[256,2048]{1,0:T(8,128)(2,1)S(1)}, u32[]{:S(2)}, u32[]{:S(2)}) collective-permute-start(bf16[256,2048]{1,0:T(8,128)(2,1)} %get-tuple-element.51), channel_id=1, source_target_pairs={{0,2},{2,0},{4,6},{6,4},{8,10},{10,8},{12,14},{14,12},{16,18},{18,... | collective-permute-start | bytes 3145736 | tf_op jit(solution)/shard_map/ppermute | solution.py:287
  61.0 15.4 %collective-permute-start.14 = (bf16[64,2176]{1,0:T(8,128)(2,1)}, bf16[64,2176]{1,0:T(8,128)(2,1)S(1)}, u32[]{:S(2)}, u32[]{:S(2)}) collective-permute-start(bf16[64,2176]{1,0:T(8,128)(2,1)} %collective-permute-done.10.refs_5_), channel_id=1, source_target_pairs={{0,1},{1,0},{2,3},{3,2},{4,5},{5,4},{6,7},{7,6},{8,9},{9,8},{10,11... | collective-permute-start | bytes 835592 | tf_op jit(solution)/shard_map/ppermute | solution.py:298
  62.1 14.5 %collective-permute-start.17 = (bf16[64,2048]{1,0:T(8,128)(2,1)}, bf16[64,2048]{1,0:T(8,128)(2,1)S(1)}, u32[]{:S(2)}, u32[]{:S(2)}) collective-permute-start(bf16[64,2048]{1,0:T(8,128)(2,1)} %collective-permute-done.8.refs_1_), channel_id=1, source_target_pairs={{0,4},{2,6},{4,0},{6,2},{8,12},{10,14},{12,8},{14,10},{16,20},{18,... | collective-permute-start | bytes 786440 | tf_op jit(solution)/shard_map/ppermute | solution.py:290
  69.2 12.9 %collective-permute-start.18 = (bf16[64,2176]{1,0:T(8,128)(2,1)}, bf16[64,2176]{1,0:T(8,128)(2,1)S(1)}, u32[]{:S(2)}, u32[]{:S(2)}) collective-permute-start(bf16[64,2176]{1,0:T(8,128)(2,1)} %collective-permute-done.7.refs_2_), channel_id=1, source_target_pairs={{0,1},{1,0},{2,3},{3,2},{4,5},{5,4},{6,7},{7,6},{8,9},{9,8},{10,11... | collective-permute-start | bytes 835592 | tf_op jit(solution)/shard_map/ppermute | solution.py:298
  103.4 15.2 %collective-permute-start.28 = (bf16[64,2176]{1,0:T(8,128)(2,1)}, bf16[64,2176]{1,0:T(8,128)(2,1)S(1)}, u32[]{:S(2)}, u32[]{:S(2)}) collective-permute-start(bf16[64,2176]{1,0:T(8,128)(2,1)} %collective-permute-done.12.refs_7_), channel_id=1, source_target_pairs={{0,1},{1,0},{2,3},{3,2},{4,5},{5,4},{6,7},{7,6},{8,9},{9,8},{10,11... | collective-permute-start | bytes 835592 | tf_op jit(solution)/shard_map/ppermute | solution.py:298
  105.6 14.9 %collective-permute-start.27 = (bf16[128,2048]{1,0:T(8,128)(2,1)S(1)}, bf16[128,2048]{1,0:T(8,128)(2,1)S(1)}, u32[]{:S(2)}, u32[]{:S(2)}) collective-permute-start(bf16[128,2048]{1,0:T(8,128)(2,1)S(1)} %slice.50), channel_id=1, source_target_pairs={{0,4},{2,6},{4,0},{6,2},{8,12},{10,14},{12,8},{14,10},{16,20},{18,... | collective-permute-start | bytes 1572872 | tf_op jit(solution)/shard_map/ppermute | solution.py:290
  106.6 25.2 %collective-permute-start.29 = (bf16[128,2048]{1,0:T(8,128)(2,1)S(1)}, bf16[128,2048]{1,0:T(8,128)(2,1)}, u32[]{:S(2)}, u32[]{:S(2)}) collective-permute-start(bf16[128,2048]{1,0:T(8,128)(2,1)S(1)} %slice.51), channel_id=1, source_target_pairs={{0,4},{2,6},{4,0},{6,2},{8,12},{10,14},{12,8},{14,10},{16,20},{18,... | collective-permute-start | bytes 1572872 | tf_op jit(solution)/shard_map/ppermute | solution.py:290
  123.5 18.3 %collective-permute-start.33 = (bf16[256,2048]{1,0:T(8,128)(2,1)}, bf16[256,2048]{1,0:T(8,128)(2,1)}, u32[]{:S(2)}, u32[]{:S(2)}) collective-permute-start(bf16[256,2048]{1,0:T(8,128)(2,1)} %fusion.43), channel_id=1, source_target_pairs={{0,2},{2,0},{4,6},{6,4},{8,10},{10,8},{12,14},{14,12},{16,18},{18,... | collective-permute-start | bytes 3145736 | tf_op jit(solution)/shard_map/ppermute | solution.py:287
  125.7 16.2 %collective-permute-start.34 = (bf16[128,2048]{1,0:T(8,128)(2,1)S(1)}, bf16[128,2048]{1,0:T(8,128)(2,1)S(1)}, u32[]{:S(2)}, u32[]{:S(2)}) collective-permute-start(bf16[128,2048]{1,0:T(8,128)(2,1)S(1)} %slice.52), channel_id=1, source_target_pairs={{0,4},{2,6},{4,0},{6,2},{8,12},{10,14},{12,8},{14,10},{16,20},{18,... | collective-permute-start | bytes 1572872 | tf_op jit(solution)/shard_map/ppermute | solution.py:290
  146.3 23.2 %collective-permute-start.35 = (bf16[256,2048]{1,0:T(8,128)(2,1)}, bf16[256,2048]{1,0:T(8,128)(2,1)}, u32[]{:S(2)}, u32[]{:S(2)}) collective-permute-start(bf16[256,2048]{1,0:T(8,128)(2,1)} %get-tuple-element.69), channel_id=1, source_target_pairs={{0,2},{2,0},{4,6},{6,4},{8,10},{10,8},{12,14},{14,12},{16,18},{18,... | collective-permute-start | bytes 3145736 | tf_op jit(solution)/shard_map/ppermute | solution.py:287
  148.4 20.7 %collective-permute-start.37 = (bf16[192,2048]{1,0:T(8,128)(2,1)}, bf16[192,2048]{1,0:T(8,128)(2,1)}, u32[]{:S(2)}, u32[]{:S(2)}) collective-permute-start(bf16[192,2048]{1,0:T(8,128)(2,1)} %pad_maximum_fusion), channel_id=1, source_target_pairs={{0,1},{1,0},{2,3},{3,2},{4,5},{5,4},{6,7},{7,6},{8,9},{9,8},{10,11... | collective-permute-start | bytes 2359304 | tf_op jit(solution)/shard_map/ppermute | solution.py:298
  151.2 17.9 %collective-permute-start.36 = (bf16[128,2048]{1,0:T(8,128)(2,1)}, bf16[128,2048]{1,0:T(8,128)(2,1)}, u32[]{:S(2)}, u32[]{:S(2)}) collective-permute-start(bf16[128,2048]{1,0:T(8,128)(2,1)} %slice.53), channel_id=1, source_target_pairs={{0,4},{2,6},{4,0},{6,2},{8,12},{10,14},{12,8},{14,10},{16,20},{18,... | collective-permute-start | bytes 1572872 | tf_op jit(solution)/shard_map/ppermute | solution.py:290
  153.9 47.2 %collective-permute-start.41 = (bf16[192,2048]{1,0:T(8,128)(2,1)S(1)}, bf16[192,2048]{1,0:T(8,128)(2,1)S(1)}, u32[]{:S(2)}, u32[]{:S(2)}) collective-permute-start(bf16[192,2048]{1,0:T(8,128)(2,1)S(1)} %pad_maximum_fusion.1), channel_id=1, source_target_pairs={{0,1},{1,0},{2,3},{3,2},{4,5},{5,4},{6,7},{7,6},{8,9},{9,8},{10,11... | collective-permute-start | bytes 2359304 | tf_op jit(solution)/shard_map/ppermute | solution.py:298
  154.5 22.6 %collective-permute-start.30 = (bf16[64,2048]{1,0:T(8,128)(2,1)}, bf16[64,2048]{1,0:T(8,128)(2,1)}, u32[]{:S(2)}, u32[]{:S(2)}) collective-permute-start(bf16[64,2048]{1,0:T(8,128)(2,1)} %get-tuple-element.64), channel_id=1, source_target_pairs={{0,24},{2,26},{4,28},{6,30},{8,0},{10,2},{12,4},{14,6},{16,8},{18,... | collective-permute-start | bytes 786440 | tf_op jit(solution)/shard_map/ppermute | solution.py:293
  169.1 17.7 %collective-permute-start.31 = (bf16[64,2048]{1,0:T(8,128)(2,1)S(1)}, bf16[64,2048]{1,0:T(8,128)(2,1)}, u32[]{:S(2)}, u32[]{:S(2)}) collective-permute-start(bf16[64,2048]{1,0:T(8,128)(2,1)S(1)} %copy-done.53), channel_id=1, source_target_pairs={{0,16},{2,18},{4,20},{6,22},{8,24},{10,26},{12,28},{14,30},{16,0},... | collective-permute-start | bytes 786440 | tf_op jit(solution)/shard_map/ppermute | solution.py:293
  169.1 17.6 %collective-permute-start.32 = (bf16[64,2048]{1,0:T(8,128)(2,1)S(1)}, bf16[64,2048]{1,0:T(8,128)(2,1)}, u32[]{:S(2)}, u32[]{:S(2)}) collective-permute-start(bf16[64,2048]{1,0:T(8,128)(2,1)S(1)} %copy-done.52), channel_id=1, source_target_pairs={{0,8},{2,10},{4,12},{6,14},{8,16},{10,18},{12,20},{14,22},{16,24},... | collective-permute-start | bytes 786440 | tf_op jit(solution)/shard_map/ppermute | solution.py:293
  169.6 39.0 %collective-permute-start.43 = (bf16[256,128]{1,0:T(8,128)(2,1)}, bf16[256,128]{1,0:T(8,128)(2,1)S(1)}, u32[]{:S(2)}, u32[]{:S(2)}) collective-permute-start(bf16[256,128]{1,0:T(8,128)(2,1)} %get-tuple-element.84), channel_id=1, source_target_pairs={{0,2},{2,0},{4,6},{6,4},{8,10},{10,8},{12,14},{14,12},{16,18},{18,... | collective-permute-start | bytes 196616 | tf_op jit(solution)/shard_map/ppermute | solution.py:287
  190.0 23.5 %collective-permute-start.39 = (bf16[64,2048]{1,0:T(8,128)(2,1)}, bf16[64,2048]{1,0:T(8,128)(2,1)}, u32[]{:S(2)}, u32[]{:S(2)}) collective-permute-start(bf16[64,2048]{1,0:T(8,128)(2,1)} %get-tuple-element.74), channel_id=1, source_target_pairs={{0,16},{2,18},{4,20},{6,22},{8,24},{10,26},{12,28},{14,30},{16,0},... | collective-permute-start | bytes 786440 | tf_op jit(solution)/shard_map/ppermute | solution.py:293
  191.1 22.4 %collective-permute-start.40 = (bf16[64,2048]{1,0:T(8,128)(2,1)}, bf16[64,2048]{1,0:T(8,128)(2,1)}, u32[]{:S(2)}, u32[]{:S(2)}) collective-permute-start(bf16[64,2048]{1,0:T(8,128)(2,1)} %get-tuple-element.75), channel_id=1, source_target_pairs={{0,8},{2,10},{4,12},{6,14},{8,16},{10,18},{12,20},{14,22},{16,24},... | collective-permute-start | bytes 786440 | tf_op jit(solution)/shard_map/ppermute | solution.py:293
  (81 other events, 686.0 us)

commit v10 on v9

--- a/solution.py
+++ b/solution.py
@@ -114,35 +114,33 @@
 ANYWHERE = pl.BlockSpec(memory_space=pl.ANY)
 
 
-def landing(pieces):
-    rows = sum(a.shape[0] for a in pieces)
-    return [
-        pltpu.VMEM((rows, pieces[0].shape[1]), BF),
-        pltpu.SemaphoreType.DMA((len(pieces),)),
+def plan_and_pack(expert, experts, capacity, tok_rows, pieces):
+    arrays = []
+    for array, _ in pieces:
+        if not any(array is a for a in arrays):
+            arrays.append(array)
+    sources = [
+        (next(k for k, a in enumerate(arrays) if a is array), chunk) for array, chunk in pieces
     ]
-
-
-def load(piece_refs, rows_ref, sems):
-    copies, at = [], 0
-    for i, ref in enumerate(piece_refs):
-        size = ref.shape[0]
-        copies.append(pltpu.make_async_copy(ref, rows_ref.at[at : at + size], sems.at[i]))
-        copies[-1].start()
-        at += size
-    return copies
-
-
-def plan_and_pack(expert, experts, capacity, chunks):
-    tok_rows, width = chunks[0].shape
-    features = width - LANES
-    groups, each = 2, len(chunks) // 2
+    width = arrays[0].shape[1]
+    features = (width - LANES) // 2
+    groups, each = 2, len(pieces) // 2
     length, room = TOGETHER * tok_rows, TOGETHER * capacity
 
     def body(expert_ref, *refs):
-        outs = refs[len(chunks) :]
-        mine_ref, theirs_ref, mine_lanes, theirs_lanes, pick_ref, place_ref = outs[:6]
-        rows_ref, sems = outs[6:]
-        copies = load(refs[: len(chunks)], rows_ref, sems)
+        outs = refs[len(arrays) :]
+        token_mine, token_theirs, cot_mine, cot_theirs, lane_mine, lane_theirs = outs[:6]
+        place_ref, rows_ref, sems = outs[6:]
+        copies = []
+        for i, (source, chunk) in enumerate(sources):
+            copies.append(
+                pltpu.make_async_copy(
+                    refs[source].at[chunk * tok_rows : (chunk + 1) * tok_rows],
+                    rows_ref.at[i * tok_rows : (i + 1) * tok_rows],
+                    sems.at[i],
+                )
+            )
+            copies[-1].start()
         lane = lax.broadcasted_iota(jnp.int32, (length, LANES), 1)
         row = lax.broadcasted_iota(jnp.int32, (length, length), 0)
         col = lax.broadcasted_iota(jnp.int32, (length, length), 1)
@@ -164,73 +162,46 @@
             for copy in copies[group * each : (group + 1) * each]:
                 copy.wait()
             held_rows = slice(group * length, (group + 1) * length)
-            lanes = rows_ref[held_rows, features:]
+            lanes = rows_ref[held_rows, 2 * features :]
             place = places(lanes.astype(F32), expert_ref[0])
             if group == 0:
                 place_ref[:, : 2 * room] = place.astype(BF)
                 place_ref[:, 2 * room :] = places(lanes.astype(F32), expert_ref[0] ^ 2).astype(BF)
             pick = place.T.astype(BF)
-            pick_ref[group] = pick
             here = slice(group * room, (group + 1) * room)
             packed = dot(pick, lanes).astype(BF)
-            mine_lanes[here] = packed[:room]
-            theirs_lanes[here] = packed[room:]
-            for at in range(0, features, 512):
-                cols = slice(at, at + 512)
-                packed = dot(pick, rows_ref[held_rows, cols]).astype(BF)
-                mine_ref[here, cols] = packed[:room]
-                theirs_ref[here, cols] = packed[room:]
+            lane_mine[here] = packed[:room]
+            lane_theirs[here] = packed[room:]
+            for at in range(0, 2 * features, 512):
+                packed = dot(pick, rows_ref[held_rows, at : at + 512]).astype(BF)
+                mine, theirs = (
+                    (token_mine, token_theirs) if at < features else (cot_mine, cot_theirs)
+                )
+                cols = slice(at % features, at % features + 512)
+                mine[here, cols] = packed[:room]
+                theirs[here, cols] = packed[room:]
 
     rows = jax.ShapeDtypeStruct((groups * room, features), BF)
     lanes = jax.ShapeDtypeStruct((groups * room, LANES), BF)
-    pick = jax.ShapeDtypeStruct((groups, 2 * room, length), BF)
     place = jax.ShapeDtypeStruct((length, 4 * room), BF)
-    outs = (rows, rows, lanes, lanes, pick, place)
+    outs = (rows, rows, rows, rows, lanes, lanes, place)
     return pl.pallas_call(
         body,
         grid_spec=pltpu.PrefetchScalarGridSpec(
             num_scalar_prefetch=1,
             grid=(1,),
-            in_specs=[ANYWHERE] * len(chunks),
+            in_specs=[ANYWHERE] * len(arrays),
             out_specs=[whole(a) for a in outs],
-            scratch_shapes=landing(chunks),
+            scratch_shapes=[
+                pltpu.VMEM((groups * length, width), BF),
+                pltpu.SemaphoreType.DMA((len(pieces),)),
+            ],
         ),
         out_shape=outs,
         compiler_params=params(1),
         cost_estimate=SMALL,
         name="plan_and_pack",
-    )(expert, *chunks)
-
-
-def pack(pick, chunks):
-    features = chunks[0].shape[1]
-    groups, room, length = pick.shape[0], pick.shape[1] // 2, pick.shape[2]
-    each = len(chunks) // groups
-
-    def body(pick_ref, *refs):
-        mine_ref, theirs_ref, rows_ref, sems = refs[len(chunks) :]
-        copies = load(refs[: len(chunks)], rows_ref, sems)
-        for group in range(groups):
-            for copy in copies[group * each : (group + 1) * each]:
-                copy.wait()
-            held_rows = slice(group * length, (group + 1) * length)
-            here = slice(group * room, (group + 1) * room)
-            for at in range(0, features, 512):
-                cols = slice(at, at + 512)
-                packed = dot(pick_ref[group], rows_ref[held_rows, cols]).astype(BF)
-                mine_ref[here, cols] = packed[:room]
-                theirs_ref[here, cols] = packed[room:]
-
-    out = jax.ShapeDtypeStruct((groups * room, features), BF)
-    return pl.pallas_call(
-        body,
-        in_specs=[pl.BlockSpec(memory_space=pltpu.VMEM)] + [ANYWHERE] * len(chunks),
-        out_shape=(out, out),
-        scratch_shapes=landing(chunks),
-        compiler_params=params(),
-        cost_estimate=SMALL,
-        name="pack",
-    )(pick, *chunks)
+    )(expert, *arrays)
 
 
 def spread(place, mine, theirs, far_mine, far_theirs):
@@ -301,45 +272,36 @@
     share = jnp.sum(jnp.where(chosen, gate_probs[:, :, None], 0.0), axis=1)
     pad = jnp.zeros((tok_rows, LANES - 3 * experts), BF)
 
-    cot_far, cot_relay = [to_x(out_cot)], to_y(out_cot)
-    near = [jnp.concatenate([tokens, *split3(share), pad], axis=1)]
-    near.append(after(to_z(near[0], 1), cot_far[0]))
-    near.append(to_z(near[1], 1))
+    near = [jnp.concatenate([tokens, out_cot, *split3(share), pad], axis=1)]
+    far, relay = [to_x(near[0])], [to_y(near[0])]
+    near.append(to_z(near[0], 1))
+    far.append(to_x(near[1]))
+    near.append(after(to_z(near[1], 1), far[0], relay[0]))
+    far.append(to_x(near[2]))
     near.append(to_z(near[2], 1))
-    far = [to_x(a) for a in near]
-    relay = [to_y(a) for pair in zip(near, far) for a in pair]
-    token_sets = near + far
-    token_other = relay[0::2] + relay[1::2]
-    cot_near = [out_cot, to_z(after(out_cot, near[2]), 1)]
-    cot_near.append(to_z(cot_near[1], 1))
-    cot_near.append(to_z(cot_near[2], 1))
-    cot_far += [to_x(a) for a in cot_near[1:]]
-    cot_sets = cot_near + cot_far
-    cot_relay_far = to_y(cot_far[0])
-    cot_relay_ring = to_y(jnp.concatenate(cot_near[1:], axis=0))
-    cot_relay_far_ring = to_y(jnp.concatenate(cot_far[1:], axis=0))
+    far.append(to_x(near[3]))
+    relay += [to_y(far[0]), to_y(near[1]), to_y(far[1])]
+    joined = jnp.concatenate([near[2], near[3], far[2], far[3]], axis=0)
+    last = to_y(joined)
+    own_pieces = [(a, 0) for a in near + far]
+    other_pieces = [(relay[0], 0), (relay[2], 0), (last, 0), (last, 1)]
+    other_pieces += [(relay[1], 0), (relay[3], 0), (last, 2), (last, 3)]
     expert_index = expert
     expert = expert.reshape(1)
 
-    def enter(chunks, before_plan, before_dots):
-        mine, theirs, mine_lanes, theirs_lanes, pick, place = plan_and_pack(
-            after(expert, *before_plan), experts, capacity, chunks
+    def enter(pieces, *earlier):
+        mine, theirs, cot_mine, cot_theirs, mine_lanes, theirs_lanes, place = plan_and_pack(
+            after(expert, *earlier), experts, capacity, tok_rows, pieces
         )
-        theirs = after(to_core(theirs), *before_dots)
-        x = jnp.concatenate([mine, theirs], axis=0)
+        x = jnp.concatenate([mine, to_core(theirs)], axis=0)
         shares = jnp.concatenate([mine_lanes, to_core(theirs_lanes)], axis=0)
         held = (jnp.arange(LANES) % experts == expert_index) & (jnp.arange(LANES) < 3 * experts)
         weight = jnp.sum(jnp.where(held, shares.astype(F32), 0.0), axis=1, keepdims=True)
+        cot = jnp.concatenate([cot_mine, to_core(cot_theirs)], axis=0)
+        cot = (cot.astype(F32) * weight).astype(BF)
         pre_gate, pre_up = dot(x, w_gate), dot(x, w_up)
         act = (jax.nn.silu(pre_gate) * pre_up).astype(BF)
-        return x, weight, pick, place, pre_gate, pre_up, act
-
-    def enter_cot(pick, pieces, weight, pre_gate, pre_up, *before_dots):
-        mine, theirs = pack(pick, pieces)
-        theirs = after(to_core(theirs), *before_dots)
-        cot = jnp.concatenate([mine, theirs], axis=0)
-        cot = (cot.astype(F32) * weight).astype(BF)
-        return cot, *hidden_grads(cot, pre_gate, pre_up, w_down)
+        return x, weight, place, pre_gate, pre_up, act, cot
 
     def leave(rows_of):
         half = TOGETHER * capacity
@@ -359,33 +321,21 @@
         act = lax.dynamic_slice_in_dim(act, replica * (hidden // 2), hidden // 2, 1)
         return outer_sum(x, d_gate), outer_sum(x, d_up), outer_sum(act, cot)
 
-    own_x, weight, pick, place, pre_gate, pre_up, act = enter(
-        token_sets,
-        (*relay[:3], cot_relay, cot_near[1]),
-        (relay[3], cot_relay_far, cot_near[2], cot_far[1]),
-    )
-    act = after(act, relay[4], cot_near[3], cot_far[2])
+    own_x, weight, place, pre_gate, pre_up, act, cot = enter(own_pieces, *relay[1:4], joined)
     parts = leave(lambda rows: (dot(act[rows], w_down) * weight[rows]).astype(BF))
-    cot, d_gate, d_up = enter_cot(
-        after(pick, parts[0], parts[1], relay[5]), cot_sets, weight, pre_gate, pre_up, relay[6]
-    )
-    own_grads = cot, d_gate, d_up
-    d_gate, d_up = after((d_gate, d_up), parts[2], relay[7])
+    cot = after(cot, parts[0], parts[1])
+    own_grads = cot, *hidden_grads(cot, pre_gate, pre_up, w_down)
+    d_gate, d_up = after(own_grads[1:], parts[2])
     grad_parts = leave(lambda rows: input_rows(d_gate[rows], d_up[rows], w_gate, w_up))
-    chunks = home(after(place, grad_parts[0]), parts)
-
-    x, weight, pick, _, pre_gate, pre_up, other_act = enter(
-        token_other, (chunks[0], *grad_parts[1:3]), (grad_parts[3], cot_relay_ring)
-    )
-    grad_chunks = home(after(place, other_act, *chunks[1:]), grad_parts)
-    own_grads = after(own_grads, grad_chunks[0])
+    chunks = home(after(place, grad_parts[0], grad_parts[1]), parts)
+    own_grads = after(own_grads[0], grad_parts[2]), *after(own_grads[1:], chunks[0])
     own = grads(own_x, act, *own_grads)
-    cot, d_gate, d_up = enter_cot(
-        after(pick, *own, grad_chunks[1]),
-        (cot_relay, cot_relay_ring, cot_relay_far, cot_relay_far_ring),
-        weight, pre_gate, pre_up,
-    )
-    other = grads(x, other_act, cot, d_gate, d_up)
+    grad_chunks = home(after(place, *own), grad_parts)
+
+    x, weight, _, pre_gate, pre_up, act, cot = enter(other_pieces, grad_chunks[0], *chunks[1:])
+    cot = after(cot, act, grad_chunks[1], grad_chunks[2])
+    d_gate, d_up = hidden_grads(cot, pre_gate, pre_up, w_down)
+    other = grads(x, act, cot, d_gate, d_up)
     grad_gate, grad_up, grad_down = ((a + b).astype(BF)[None] for a, b in zip(own, other))
     return (total(chunks), total(grad_chunks), grad_gate, grad_up, grad_down)
 

time: 230 us -> 203 us (0.88); the launches traced: 226 us -> 203 us
  starting transfers between devices: 34.8 us -> 26.5 us
  Pallas kernels: 24.4 us -> 17.7 us
  other arithmetic: 8.7 us -> 4.8 us
  local copies, waits for them, and re-layouts: 17.6 us -> 14.7 us
    ppermute x12 -> x5, waiting for transfers between devices: 40.4 us -> 0.01 us  [to_y(): return lax.ppermute(rows, 'replica', [(0, 1), (1, 0)])]
    ppermute x12 -> x9, waiting for transfers between devices: 37.8 us -> 64.7 us  [to_z(): lax.ppermute(rows, 'expert', [(i, (i + 4 * step) % experts) for i in rang...]
    ppermute x12 -> x8, waiting for transfers between devices: 24.4 us -> 37.6 us  [to_x(): return lax.ppermute(rows, 'expert', [(i, i ^ 2) for i in range(experts)])]
    pallas_call x2 -> x0, Pallas kernels: 8.94 us -> none  [pack(): pl.pallas_call(body, in_specs=[pl.BlockSpec(memory_space=pltpu.VMEM)] + [...]
    ppermute x12 -> x8, starting transfers between devices: 14.3 us -> 8.47 us  [to_x(): return lax.ppermute(rows, 'expert', [(i, i ^ 2) for i in range(experts)])]
    ppermute x12 -> x5, starting transfers between devices: 12.3 us -> 6.6 us  [to_y(): return lax.ppermute(rows, 'replica', [(0, 1), (1, 0)])]
    unnamed x124 -> x69, local copies, waits for them, and re-layouts: 11.9 us -> 8.65 us
    dot_general x6, matrix products: 12.7 us -> 9.47 us  [dot(): return jnp.dot(left, right, preferred_element_type=F32)]
  transfers between devices with their start and end apart: 44 -> 30, of which waited for: 19 -> 11; matrix products, arithmetic and copies ran while one was open for 18% -> 20% of each run, Pallas kernels for 5% -> 3%
where the time goes in v10:
time: 203 us
  waiting for transfers between devices  103 us (51%)
  matrix products  35 us (17%)
  starting transfers between devices  26.5 us (13%)
  Pallas kernels  17.7 us (9%)
  local copies, waits for them, and re-layouts  14.7 us (7%)
  other arithmetic  4.8 us (2%)
    ppermute x9, waiting for transfers between devices, to_z(): lax.ppermute(rows, 'expert', [(i, (i + 4 * step) % experts) for i in rang...  64.7 us
    ppermute x8, waiting for transfers between devices, to_x(): return lax.ppermute(rows, 'expert', [(i, i ^ 2) for i in range(experts)])  37.6 us
    dot_general x6, matrix products, outer_sum(): lax.dot_general(left, right, (((0,), (0,)), ((), ())), preferred_element_...  16.2 us
    pallas_call x2, Pallas kernels, plan_and_pack(): pl.pallas_call(body, grid_spec=pltpu.PrefetchScalarGridSpec(num_scalar_pr...  11.2 us
    ppermute x9, starting transfers between devices, to_z(): lax.ppermute(rows, 'expert', [(i, (i + 4 * step) % experts) for i in rang...  9.98 us
    dot_general x6, matrix products, dot(): return jnp.dot(left, right, preferred_element_type=F32)  9.47 us
    unnamed x69, local copies, waits for them, and re-layouts  8.65 us
    ppermute x8, starting transfers between devices, to_x(): return lax.ppermute(rows, 'expert', [(i, i ^ 2) for i in range(experts)])  8.47 us
  transfers between devices with their start and end apart: 30, of which 11 were waited for; matrix products, arithmetic and copies ran while one was open for 20% of the time, Pallas kernels for 3%

profile of v10, /device:TPU:0, one launch (start us, length us, event | category | flops | bytes accessed | tf_op | source)
XLA Modules:
  0.0 203.0 jit_solution(9845217726961939038)
XLA Ops:
  3.6 3.0 %collective-permute-start.2 = (bf16[64,4224]{1,0:T(8,128)(2,1)}, bf16[64,4224]{1,0:T(8,128)(2,1)}, u32[]{:S(2)}, u32[]{:S(2)}) collective-permute-start(bf16[64,4224]{1,0:T(8,128)(2,1)} %concatenate.24.refs_0_), channel_id=1, source_target_pairs={{0,8},{2,10},{4,12},{6,14},{8,16},{10,18},{12,20},{14,22},{16,24},... | collective-permute-start | bytes 1622024 | tf_op jit(solution)/shard_map/ppermute | solution.py:264
  9.7 11.6 %collective-permute-done.2.refs_1_ = bf16[64,4224]{1,0:T(8,128)(2,1)} collective-permute-done((bf16[64,4224]{1,0:T(8,128)(2,1)}, bf16[64,4224]{1,0:T(8,128)(2,1)}, u32[]{:S(2)}, u32[]{:S(2)}) %collective-permute-start.2) | collective-permute-done | bytes 540704 | tf_op jit(solution)/shard_map/ppermute | solution.py:264
  24.8 12.0 %collective-permute-done.6.refs_2_ = bf16[64,4224]{1,0:T(8,128)(2,1)} collective-permute-done((bf16[64,4224]{1,0:T(8,128)(2,1)}, bf16[64,4224]{1,0:T(8,128)(2,1)}, u32[]{:S(2)}, u32[]{:S(2)}) %collective-permute-start.6) | collective-permute-done | bytes 540704 | tf_op jit(solution)/shard_map/ppermute | solution.py:264
  41.5 10.6 %collective-permute-done.8.refs_3_ = bf16[64,4224]{1,0:T(8,128)(2,1)S(1)} collective-permute-done((bf16[64,4224]{1,0:T(8,128)(2,1)}, bf16[64,4224]{1,0:T(8,128)(2,1)S(1)}, u32[]{:S(2)}, u32[]{:S(2)}) %collective-permute-start.8) | collective-permute-done | bytes 540704 | tf_op jit(solution)/shard_map/ppermute | solution.py:264
  54.9 8.3 %collective-permute-done.10.refs_7_ = bf16[64,4224]{1,0:T(8,128)(2,1)S(1)} collective-permute-done((bf16[64,4224]{1,0:T(8,128)(2,1)S(1)}, bf16[64,4224]{1,0:T(8,128)(2,1)S(1)}, u32[]{:S(2)}, u32[]{:S(2)}) %collective-permute-start.10) | collective-permute-done | bytes 540704 | tf_op jit(solution)/shard_map/ppermute | solution.py:261
  64.2 5.6 %plan_and_pack.2 = (bf16[256,2048]{1,0:T(8,128)(2,1)}, bf16[256,2048]{1,0:T(8,128)(2,1)}, bf16[256,2048]{1,0:T(8,128)(2,1)}, bf16[256,2048]{1,0:T(8,128)(2,1)}, ...) custom-call(s32[1]{0:T(128)} %bitcast.expert_ref, ...), custom_call_target="tpu_custom_call" | custom-call | flops 1 | bytes 1 | tf_op jit(solution)/shard_map/plan_and_pack/pallas_call | solution.py:188
  82.1 2.2 %multiply_convert_fusion.5 = (bf16[512,768]{1,0:T(8,128)(2,1)S(1)}, bf16[512,768]{1,0:T(8,128)(2,1)S(1)}) fusion(f32[512,768]{1,0:T(8,128)S(1)} %fusion.22, f32[512,768]{1,0:T(8,128)S(1)} %get-tuple-element.78, bf16[512,2048]{1,0:T(8,128)(2,1)S(1)} %multiply_convert_fusion.1, bf16[1,768,2048]{2,1,0:T(8,128)(2,1)S(1)} %copy-done.25), kind=kOutput, calls=%fused_computation.42 | convolution fusion | flops 1615724544 | bytes 9961472 | tf_op jit(solution)/shard_map/dot_general | solution.py:41
  84.3 10.4 %collective-permute-done.15.refs_2_ = bf16[128,2048]{1,0:T(8,128)(2,1)S(1)} collective-permute-done((bf16[128,2048]{1,0:T(8,128)(2,1)S(1)}, bf16[128,2048]{1,0:T(8,128)(2,1)S(1)}, u32[]{:S(2)}, u32[]{:S(2)}) %collective-permute-start.15) | collective-permute-done | bytes 524320 | tf_op jit(solution)/shard_map/ppermute | solution.py:261
  104.7 12.1 %collective-permute-done.21.refs_2_ = bf16[128,2048]{1,0:T(8,128)(2,1)} collective-permute-done((bf16[128,2048]{1,0:T(8,128)(2,1)}, bf16[128,2048]{1,0:T(8,128)(2,1)}, u32[]{:S(2)}, u32[]{:S(2)}) %collective-permute-start.21) | collective-permute-done | bytes 524320 | tf_op jit(solution)/shard_map/ppermute | solution.py:261
  116.8 2.7 %fusion.62 = f32[384,2048]{1,0:T(8,128)S(1)} fusion(bf16[512,2048]{1,0:T(8,128)(2,1)} %copy-done.3, bf16[512,768]{1,0:T(8,128)(2,1)} %copy-done.22, s32[]{:T(128)S(6)} %select_n.32), kind=kOutput, calls=%fused_computation.61 | convolution fusion | flops 805306368 | bytes 5636100 | tf_op jit(solution)/shard_map/dot_general | solution.py:55
  121.3 6.7 %collective-permute-done.17.refs_3_ = bf16[128,2048]{1,0:T(8,128)(2,1)} collective-permute-done((bf16[128,2048]{1,0:T(8,128)(2,1)}, bf16[128,2048]{1,0:T(8,128)(2,1)}, u32[]{:S(2)}, u32[]{:S(2)}) %collective-permute-start.17) | collective-permute-done | bytes 524320 | tf_op jit(solution)/shard_map/ppermute | solution.py:261
  128.0 3.2 %spread.2 = (bf16[64,2048]{1,0:T(8,128)(2,1)}, bf16[64,2048]{1,0:T(8,128)(2,1)}, bf16[64,2048]{1,0:T(8,128)(2,1)}, bf16[64,2048]{1,0:T(8,128)(2,1)}) custom-call(bf16[256,512]{1,0:T(8,128)(2,1)} %get-tuple-element.58.place_ref, bf16[256,2048]{1,0:T(8,128)(2,1)} %copy-done.6, bf16[256,2048]{1,0:T(8,128)(2,1)} %copy-done.5, bf16[128,2048]{1,0:T(8,128)(2,1)} %copy-done.18, ...), custom_call_target="tpu_custom_call" | custom-call | flops 1 | bytes 1 | tf_op jit(solution)/shard_map/spread/pallas_call | solution.py:223
  133.3 3.9 %fusion.55 = f32[1024,768]{1,0:T(8,128)} fusion(bf16[512,768]{1,0:T(8,128)(2,1)S(1)} %copy-done.13, bf16[512,2048]{1,0:T(8,128)(2,1)} %copy-done.16, s32[]{:T(128)S(6)} %select_n.31), kind=kOutput, calls=%fused_computation.52 | convolution fusion | flops 805306368 | bytes 4980740 | tf_op jit(solution)/shard_map/dot_general | solution.py:55
  137.2 2.7 %fusion.53 = f32[1024,768]{1,0:T(8,128)} fusion(bf16[512,768]{1,0:T(8,128)(2,1)S(1)} %copy-done.15, bf16[512,2048]{1,0:T(8,128)(2,1)S(1)} %copy-done.17, s32[]{:T(128)S(6)} %select_n.31), kind=kOutput, calls=%fused_computation.50 | convolution fusion | flops 805306368 | bytes 4980740 | tf_op jit(solution)/shard_map/dot_general | solution.py:55
  140.7 3.3 %spread.3 = (bf16[64,2048]{1,0:T(8,128)(2,1)}, bf16[64,2048]{1,0:T(8,128)(2,1)}, bf16[64,2048]{1,0:T(8,128)(2,1)}, bf16[64,2048]{1,0:T(8,128)(2,1)}) custom-call(bf16[256,512]{1,0:T(8,128)(2,1)} %get-tuple-element.58.place_ref, bf16[256,2048]{1,0:T(8,128)(2,1)} %copy-done.4, bf16[256,2048]{1,0:T(8,128)(2,1)} %collective-permute-done.16.refs_1_, ...), custom_call_target="tpu_custom_call" | custom-call | flops 1 | bytes 1 | tf_op jit(solution)/shard_map/spread/pallas_call | solution.py:223
  143.9 10.4 %collective-permute-done.19 = bf16[64,2048]{1,0:T(8,128)(2,1)} collective-permute-done((bf16[64,2048]{1,0:T(8,128)(2,1)}, bf16[64,2048]{1,0:T(8,128)(2,1)}, u32[]{:S(2)}, u32[]{:S(2)}) %collective-permute-start.19) | collective-permute-done | bytes 262176 | tf_op jit(solution)/shard_map/ppermute | solution.py:264
  154.3 5.6 %plan_and_pack.3 = (bf16[256,2048]{1,0:T(8,128)(2,1)}, bf16[256,2048]{1,0:T(8,128)(2,1)}, bf16[256,2048]{1,0:T(8,128)(2,1)}, bf16[256,2048]{1,0:T(8,128)(2,1)}, ...) custom-call(s32[1]{0:T(128)} %bitcast.expert_ref, ...), custom_call_target="tpu_custom_call" | custom-call | flops 1 | bytes 1 | tf_op jit(solution)/shard_map/plan_and_pack/pallas_call | solution.py:188
  160.1 2.0 %add_convert_fusion.4 = bf16[64,2048]{1,0:T(8,128)(2,1)} fusion(bf16[64,2048]{1,0:T(8,128)(2,1)} %collective-permute-done.20, bf16[64,2048]{1,0:T(8,128)(2,1)} %collective-permute-done.19, bf16[64,2048]{1,0:T(8,128)(2,1)} %collective-permute-done.18, bf16[64,2048]{1,0:T(8,128)(2,1)S(1)} %copy-done.21), kind=kLoop, calls=%fused_computation.57 | loop fusion | flops 1048576 | bytes 1310720 | tf_op jit(solution)/shard_map/convert_element_type | solution.py:317
  162.5 2.9 %collective-permute-start.24 = (bf16[64,2048]{1,0:T(8,128)(2,1)S(1)}, bf16[64,2048]{1,0:T(8,128)(2,1)S(1)}, u32[]{:S(2)}, u32[]{:S(2)}) collective-permute-start(bf16[64,2048]{1,0:T(8,128)(2,1)S(1)} %copy-done.29), channel_id=1, source_target_pairs={{0,16},{2,18},{4,20},{6,22},{8,24},{10,26},{12,28},{14,30},{16,0},... | collective-permute-start | bytes 786440 | tf_op jit(solution)/shard_map/ppermute | solution.py:264
  169.0 2.0 %collective-permute-done.23 = bf16[64,2048]{1,0:T(8,128)(2,1)S(1)} collective-permute-done((bf16[64,2048]{1,0:T(8,128)(2,1)}, bf16[64,2048]{1,0:T(8,128)(2,1)S(1)}, u32[]{:S(2)}, u32[]{:S(2)}) %collective-permute-start.23) | collective-permute-done | bytes 262176 | tf_op jit(solution)/shard_map/ppermute | solution.py:264
  171.0 18.0 %collective-permute-done.24 = bf16[64,2048]{1,0:T(8,128)(2,1)S(1)} collective-permute-done((bf16[64,2048]{1,0:T(8,128)(2,1)S(1)}, bf16[64,2048]{1,0:T(8,128)(2,1)S(1)}, u32[]{:S(2)}, u32[]{:S(2)}) %collective-permute-start.24) | collective-permute-done | bytes 262176 | tf_op jit(solution)/shard_map/ppermute | solution.py:264
  194.2 2.2 %fusion.36 = bf16[1,384,2048]{2,1,0:T(8,128)(2,1)} fusion(f32[384,2048]{1,0:T(8,128)S(1)} %fusion.62, bf16[512,2048]{1,0:T(8,128)(2,1)S(1)} %multiply_convert_fusion, bf16[512,768]{1,0:T(8,128)(2,1)S(1)} %get-tuple-element.79, s32[]{:T(128)S(6)} %select_n.32), kind=kOutput, calls=%fused_computation.33 | convolution fusion | flops 806879232 | bytes 7208964 | tf_op jit(solution)/shard_map/dot_general | solution.py:55
  198.3 2.3 %fusion.50 = bf16[1,1024,768]{2,1,0:T(8,128)(2,1)} fusion(f32[1024,768]{1,0:T(8,128)S(1)} %copy-done.31, bf16[512,2048]{1,0:T(8,128)(2,1)S(1)} %constant_dynamic-update-slice_fusion.6, s32[]{:T(128)S(6)} %select_n.31, f32[512,768]{1,0:T(8,128)S(1)} %fusion, f32[512,768]{1,0:T(8,128)S(1)} %fusion.16), kind=kOutput, calls=%fused_computation.47 | convolution fusion | flops 809238528 | bytes 8912900 | tf_op jit(solution)/shard_map/dot_general | solution.py:55
  200.6 2.4 %fusion.49 = bf16[1,1024,768]{2,1,0:T(8,128)(2,1)} fusion(f32[1024,768]{1,0:T(8,128)S(1)} %copy-done.30, bf16[512,2048]{1,0:T(8,128)(2,1)S(1)} %constant_dynamic-update-slice_fusion.6, s32[]{:T(128)S(6)} %select_n.31, f32[512,768]{1,0:T(8,128)S(1)} %fusion.16, f32[512,768]{1,0:T(8,128)S(1)} %fusion, f32[512,768]{1,0:T(8,128)S(1)} %get-tuple-element.80), kind=kOutput, calls=%fused_computation.46 | convolution fusion | flops 810811392 | bytes 10485764 | tf_op jit(solution)/shard_map/dot_general | solution.py:55
  (149 shorter events, 55.5 us)
Async XLA Ops:
  3.6 17.6 %collective-permute-start.2 = (bf16[64,4224]{1,0:T(8,128)(2,1)}, bf16[64,4224]{1,0:T(8,128)(2,1)}, u32[]{:S(2)}, u32[]{:S(2)}) collective-permute-start(bf16[64,4224]{1,0:T(8,128)(2,1)} %concatenate.24.refs_0_), channel_id=1, source_target_pairs={{0,8},{2,10},{4,12},{6,14},{8,16},{10,18},{12,20},{14,22},{16,24},... | collective-permute-start | bytes 1622024 | tf_op jit(solution)/shard_map/ppermute | solution.py:264
  6.7 17.6 %collective-permute-start = (bf16[64,4224]{1,0:T(8,128)(2,1)}, bf16[64,4224]{1,0:T(8,128)(2,1)}, u32[]{:S(2)}, u32[]{:S(2)}) collective-permute-start(bf16[64,4224]{1,0:T(8,128)(2,1)} %concatenate.24.refs_0_), channel_id=1, source_target_pairs={{0,4},{2,6},{4,0},{6,2},{8,12},{10,14},{12,8},{14,10},{16,20},{18,... | collective-permute-start | bytes 1622024 | tf_op jit(solution)/shard_map/ppermute | solution.py:261
  8.2 16.6 %collective-permute-start.7 = (bf16[64,4224]{1,0:T(8,128)(2,1)}, bf16[64,4224]{1,0:T(8,128)(2,1)}, u32[]{:S(2)}, u32[]{:S(2)}) collective-permute-start(bf16[64,4224]{1,0:T(8,128)(2,1)} %concatenate.24.refs_0_), channel_id=1, source_target_pairs={{0,1},{1,0},{2,3},{3,2},{4,5},{5,4},{6,7},{7,6},{8,9},{9,8},{10,11... | collective-permute-start | bytes 1622024 | tf_op jit(solution)/shard_map/ppermute | solution.py:269
  21.3 15.6 %collective-permute-start.6 = (bf16[64,4224]{1,0:T(8,128)(2,1)}, bf16[64,4224]{1,0:T(8,128)(2,1)}, u32[]{:S(2)}, u32[]{:S(2)}) collective-permute-start(bf16[64,4224]{1,0:T(8,128)(2,1)} %collective-permute-done.2.refs_1_), channel_id=1, source_target_pairs={{0,8},{2,10},{4,12},{6,14},{8,16},{10,18},{12,20},{14,22},{16,24},... | collective-permute-start | bytes 1622024 | tf_op jit(solution)/shard_map/ppermute | solution.py:264
  21.3 16.8 %collective-permute-start.4 = (bf16[64,4224]{1,0:T(8,128)(2,1)}, bf16[64,4224]{1,0:T(8,128)(2,1)}, u32[]{:S(2)}, u32[]{:S(2)}) collective-permute-start(bf16[64,4224]{1,0:T(8,128)(2,1)} %collective-permute-done.2.refs_1_), channel_id=1, source_target_pairs={{0,4},{2,6},{4,0},{6,2},{8,12},{10,14},{12,8},{14,10},{16,20},{18,... | collective-permute-start | bytes 1622024 | tf_op jit(solution)/shard_map/ppermute | solution.py:261
  22.8 41.4 %collective-permute-start.3 = (bf16[64,4224]{1,0:T(8,128)(2,1)}, bf16[64,4224]{1,0:T(8,128)(2,1)}, u32[]{:S(2)}, u32[]{:S(2)}) collective-permute-start(bf16[64,4224]{1,0:T(8,128)(2,1)} %collective-permute-done.2.refs_1_), channel_id=1, source_target_pairs={{0,1},{1,0},{2,3},{3,2},{4,5},{5,4},{6,7},{7,6},{8,9},{9,8},{10,11... | collective-permute-start | bytes 1622024 | tf_op jit(solution)/shard_map/ppermute | solution.py:269
  24.3 39.8 %collective-permute-start.1 = (bf16[64,4224]{1,0:T(8,128)(2,1)}, bf16[64,4224]{1,0:T(8,128)(2,1)}, u32[]{:S(2)}, u32[]{:S(2)}) collective-permute-start(bf16[64,4224]{1,0:T(8,128)(2,1)} %collective-permute-done.refs_4_), channel_id=1, source_target_pairs={{0,1},{1,0},{2,3},{3,2},{4,5},{5,4},{6,7},{7,6},{8,9},{9,8},{10,11... | collective-permute-start | bytes 1622024 | tf_op jit(solution)/shard_map/ppermute | solution.py:269
  36.8 17.1 %collective-permute-start.9 = (bf16[64,4224]{1,0:T(8,128)(2,1)}, bf16[64,4224]{1,0:T(8,128)(2,1)S(1)}, u32[]{:S(2)}, u32[]{:S(2)}) collective-permute-start(bf16[64,4224]{1,0:T(8,128)(2,1)} %collective-permute-done.6.refs_2_), channel_id=1, source_target_pairs={{0,4},{2,6},{4,0},{6,2},{8,12},{10,14},{12,8},{14,10},{16,20},{18,... | collective-permute-start | bytes 1622024 | tf_op jit(solution)/shard_map/ppermute | solution.py:261
  38.1 14.0 %collective-permute-start.8 = (bf16[64,4224]{1,0:T(8,128)(2,1)}, bf16[64,4224]{1,0:T(8,128)(2,1)S(1)}, u32[]{:S(2)}, u32[]{:S(2)}) collective-permute-start(bf16[64,4224]{1,0:T(8,128)(2,1)} %collective-permute-done.6.refs_2_), channel_id=1, source_target_pairs={{0,8},{2,10},{4,12},{6,14},{8,16},{10,18},{12,20},{14,22},{16,24},... | collective-permute-start | bytes 1622024 | tf_op jit(solution)/shard_map/ppermute | solution.py:264
  38.1 26.0 %collective-permute-start.5 = (bf16[64,4224]{1,0:T(8,128)(2,1)}, bf16[64,4224]{1,0:T(8,128)(2,1)}, u32[]{:S(2)}, u32[]{:S(2)}) collective-permute-start(bf16[64,4224]{1,0:T(8,128)(2,1)} %collective-permute-done.4.refs_5_), channel_id=1, source_target_pairs={{0,1},{1,0},{2,3},{3,2},{4,5},{5,4},{6,7},{7,6},{8,9},{9,8},{10,11... | collective-permute-start | bytes 1622024 | tf_op jit(solution)/shard_map/ppermute | solution.py:269
  52.1 11.1 %collective-permute-start.10 = (bf16[64,4224]{1,0:T(8,128)(2,1)S(1)}, bf16[64,4224]{1,0:T(8,128)(2,1)S(1)}, u32[]{:S(2)}, u32[]{:S(2)}) collective-permute-start(bf16[64,4224]{1,0:T(8,128)(2,1)S(1)} %collective-permute-done.8.refs_3_), channel_id=1, source_target_pairs={{0,4},{2,6},{4,0},{6,2},{8,12},{10,14},{12,8},{14,10},{16,20},{18,... | collective-permute-start | bytes 1622024 | tf_op jit(solution)/shard_map/ppermute | solution.py:261
  78.1 76.3 %collective-permute-start.26 = (bf16[256,4224]{1,0:T(8,128)(2,1)}, bf16[256,4224]{1,0:T(8,128)(2,1)}, u32[]{:S(2)}, u32[]{:S(2)}) collective-permute-start(bf16[256,4224]{1,0:T(8,128)(2,1)} %constant_dynamic-update-slice_fusion), channel_id=1, source_target_pairs={{0,1},{1,0},{2,3},{3,2},{4,5},{5,4},{6,7},{7,6},{8,9},{9,8},{10,11... | collective-permute-start | bytes 6488072 | tf_op jit(solution)/shard_map/ppermute | solution.py:269
  80.7 14.0 %collective-permute-start.15 = (bf16[128,2048]{1,0:T(8,128)(2,1)S(1)}, bf16[128,2048]{1,0:T(8,128)(2,1)S(1)}, u32[]{:S(2)}, u32[]{:S(2)}) collective-permute-start(bf16[128,2048]{1,0:T(8,128)(2,1)S(1)} %slice.52), channel_id=1, source_target_pairs={{0,4},{2,6},{4,0},{6,2},{8,12},{10,14},{12,8},{14,10},{16,20},{18,... | collective-permute-start | bytes 1572872 | tf_op jit(solution)/shard_map/ppermute | solution.py:261
  97.7 21.8 %collective-permute-start.16 = (bf16[256,2048]{1,0:T(8,128)(2,1)}, bf16[256,2048]{1,0:T(8,128)(2,1)}, u32[]{:S(2)}, u32[]{:S(2)}) collective-permute-start(bf16[256,2048]{1,0:T(8,128)(2,1)} %fusion.43), channel_id=1, source_target_pairs={{0,2},{2,0},{4,6},{6,4},{8,10},{10,8},{12,14},{14,12},{16,18},{18,... | collective-permute-start | bytes 3145736 | tf_op jit(solution)/shard_map/ppermute | solution.py:258
  101.8 15.0 %collective-permute-start.21 = (bf16[128,2048]{1,0:T(8,128)(2,1)}, bf16[128,2048]{1,0:T(8,128)(2,1)}, u32[]{:S(2)}, u32[]{:S(2)}) collective-permute-start(bf16[128,2048]{1,0:T(8,128)(2,1)} %slice.54), channel_id=1, source_target_pairs={{0,4},{2,6},{4,0},{6,2},{8,12},{10,14},{12,8},{14,10},{16,20},{18,... | collective-permute-start | bytes 1572872 | tf_op jit(solution)/shard_map/ppermute | solution.py:261
  103.2 24.9 %collective-permute-start.17 = (bf16[128,2048]{1,0:T(8,128)(2,1)}, bf16[128,2048]{1,0:T(8,128)(2,1)}, u32[]{:S(2)}, u32[]{:S(2)}) collective-permute-start(bf16[128,2048]{1,0:T(8,128)(2,1)} %slice.53), channel_id=1, source_target_pairs={{0,4},{2,6},{4,0},{6,2},{8,12},{10,14},{12,8},{14,10},{16,20},{18,... | collective-permute-start | bytes 1572872 | tf_op jit(solution)/shard_map/ppermute | solution.py:261
  120.7 19.1 %collective-permute-start.22 = (bf16[128,2048]{1,0:T(8,128)(2,1)S(1)}, bf16[128,2048]{1,0:T(8,128)(2,1)S(1)}, u32[]{:S(2)}, u32[]{:S(2)}) collective-permute-start(bf16[128,2048]{1,0:T(8,128)(2,1)S(1)} %slice.55), channel_id=1, source_target_pairs={{0,4},{2,6},{4,0},{6,2},{8,12},{10,14},{12,8},{14,10},{16,20},{18,... | collective-permute-start | bytes 1572872 | tf_op jit(solution)/shard_map/ppermute | solution.py:261
  131.3 12.7 %collective-permute-start.18 = (bf16[64,2048]{1,0:T(8,128)(2,1)}, bf16[64,2048]{1,0:T(8,128)(2,1)}, u32[]{:S(2)}, u32[]{:S(2)}) collective-permute-start(bf16[64,2048]{1,0:T(8,128)(2,1)} %get-tuple-element.52), channel_id=1, source_target_pairs={{0,24},{2,26},{4,28},{6,30},{8,0},{10,2},{12,4},{14,6},{16,8},{18,... | collective-permute-start | bytes 786440 | tf_op jit(solution)/shard_map/ppermute | solution.py:264
  131.3 23.1 %collective-permute-start.19 = (bf16[64,2048]{1,0:T(8,128)(2,1)}, bf16[64,2048]{1,0:T(8,128)(2,1)}, u32[]{:S(2)}, u32[]{:S(2)}) collective-permute-start(bf16[64,2048]{1,0:T(8,128)(2,1)} %get-tuple-element.53), channel_id=1, source_target_pairs={{0,16},{2,18},{4,20},{6,22},{8,24},{10,26},{12,28},{14,30},{16,0},... | collective-permute-start | bytes 786440 | tf_op jit(solution)/shard_map/ppermute | solution.py:264
  131.6 22.7 %collective-permute-start.20 = (bf16[64,2048]{1,0:T(8,128)(2,1)}, bf16[64,2048]{1,0:T(8,128)(2,1)}, u32[]{:S(2)}, u32[]{:S(2)}) collective-permute-start(bf16[64,2048]{1,0:T(8,128)(2,1)} %get-tuple-element.54), channel_id=1, source_target_pairs={{0,8},{2,10},{4,12},{6,14},{8,16},{10,18},{12,20},{14,22},{16,24},... | collective-permute-start | bytes 786440 | tf_op jit(solution)/shard_map/ppermute | solution.py:264
  160.0 29.9 %collective-permute-start.27 = (bf16[256,2048]{1,0:T(8,128)(2,1)}, bf16[256,2048]{1,0:T(8,128)(2,1)S(1)}, u32[]{:S(2)}, u32[]{:S(2)}) collective-permute-start(bf16[256,2048]{1,0:T(8,128)(2,1)} %get-tuple-element.65), channel_id=1, source_target_pairs={{0,2},{2,0},{4,6},{6,4},{8,10},{10,8},{12,14},{14,12},{16,18},{18,... | collective-permute-start | bytes 3145736 | tf_op jit(solution)/shard_map/ppermute | solution.py:258
  162.5 26.5 %collective-permute-start.24 = (bf16[64,2048]{1,0:T(8,128)(2,1)S(1)}, bf16[64,2048]{1,0:T(8,128)(2,1)S(1)}, u32[]{:S(2)}, u32[]{:S(2)}) collective-permute-start(bf16[64,2048]{1,0:T(8,128)(2,1)S(1)} %copy-done.29), channel_id=1, source_target_pairs={{0,16},{2,18},{4,20},{6,22},{8,24},{10,26},{12,28},{14,30},{16,0},... | collective-permute-start | bytes 786440 | tf_op jit(solution)/shard_map/ppermute | solution.py:264
  165.4 23.6 %collective-permute-start.25 = (bf16[64,2048]{1,0:T(8,128)(2,1)S(1)}, bf16[64,2048]{1,0:T(8,128)(2,1)S(1)}, u32[]{:S(2)}, u32[]{:S(2)}) collective-permute-start(bf16[64,2048]{1,0:T(8,128)(2,1)S(1)} %copy-done.28), channel_id=1, source_target_pairs={{0,8},{2,10},{4,12},{6,14},{8,16},{10,18},{12,20},{14,22},{16,24},... | collective-permute-start | bytes 786440 | tf_op jit(solution)/shard_map/ppermute | solution.py:264
  168.8 24.9 %collective-permute-start.28 = (bf16[256,2048]{1,0:T(8,128)(2,1)S(1)}, bf16[256,2048]{1,0:T(8,128)(2,1)S(1)}, u32[]{:S(2)}, u32[]{:S(2)}) collective-permute-start(bf16[256,2048]{1,0:T(8,128)(2,1)S(1)} %copy-done.27), channel_id=1, source_target_pairs={{0,2},{2,0},{4,6},{6,4},{8,10},{10,8},{12,14},{14,12},{16,18},{18,... | collective-permute-start | bytes 3145736 | tf_op jit(solution)/shard_map/ppermute | solution.py:258
  (38 other events, 328.6 us)

commit v11 on v10

--- a/solution.py
+++ b/solution.py
@@ -129,8 +129,7 @@
 
     def body(expert_ref, *refs):
         outs = refs[len(arrays) :]
-        token_mine, token_theirs, cot_mine, cot_theirs, lane_mine, lane_theirs = outs[:6]
-        place_ref, rows_ref, sems = outs[6:]
+        token_mine, cot_mine, lane_mine, theirs_ref, place_ref, rows_ref, sems = outs
         copies = []
         for i, (source, chunk) in enumerate(sources):
             copies.append(
@@ -171,20 +170,18 @@
             here = slice(group * room, (group + 1) * room)
             packed = dot(pick, lanes).astype(BF)
             lane_mine[here] = packed[:room]
-            lane_theirs[here] = packed[room:]
+            theirs_ref[here, 2 * features :] = packed[room:]
             for at in range(0, 2 * features, 512):
                 packed = dot(pick, rows_ref[held_rows, at : at + 512]).astype(BF)
-                mine, theirs = (
-                    (token_mine, token_theirs) if at < features else (cot_mine, cot_theirs)
-                )
-                cols = slice(at % features, at % features + 512)
-                mine[here, cols] = packed[:room]
-                theirs[here, cols] = packed[room:]
+                mine_ref = token_mine if at < features else cot_mine
+                mine_ref[here, at % features : at % features + 512] = packed[:room]
+                theirs_ref[here, at : at + 512] = packed[room:]
 
     rows = jax.ShapeDtypeStruct((groups * room, features), BF)
     lanes = jax.ShapeDtypeStruct((groups * room, LANES), BF)
+    theirs = jax.ShapeDtypeStruct((groups * room, width), BF)
     place = jax.ShapeDtypeStruct((length, 4 * room), BF)
-    outs = (rows, rows, rows, rows, lanes, lanes, place)
+    outs = (rows, rows, lanes, theirs, place)
     return pl.pallas_call(
         body,
         grid_spec=pltpu.PrefetchScalarGridSpec(
@@ -280,33 +277,35 @@
     far.append(to_x(near[2]))
     near.append(to_z(near[2], 1))
     far.append(to_x(near[3]))
-    relay += [to_y(far[0]), to_y(near[1]), to_y(far[1])]
-    joined = jnp.concatenate([near[2], near[3], far[2], far[3]], axis=0)
+    relay += [to_y(far[0]), to_y(near[1]), to_y(far[1]), to_y(near[2])]
+    joined = jnp.concatenate([near[3], far[2], far[3]], axis=0)
     last = to_y(joined)
     own_pieces = [(a, 0) for a in near + far]
-    other_pieces = [(relay[0], 0), (relay[2], 0), (last, 0), (last, 1)]
-    other_pieces += [(relay[1], 0), (relay[3], 0), (last, 2), (last, 3)]
+    other_pieces = [(relay[0], 0), (relay[2], 0), (relay[4], 0), (last, 0)]
+    other_pieces += [(relay[1], 0), (relay[3], 0), (last, 1), (last, 2)]
     expert_index = expert
     expert = expert.reshape(1)
 
-    def enter(pieces, *earlier):
-        mine, theirs, cot_mine, cot_theirs, mine_lanes, theirs_lanes, place = plan_and_pack(
-            after(expert, *earlier), experts, capacity, tok_rows, pieces
-        )
-        x = jnp.concatenate([mine, to_core(theirs)], axis=0)
-        shares = jnp.concatenate([mine_lanes, to_core(theirs_lanes)], axis=0)
+    def plan(pieces, *earlier):
+        return plan_and_pack(after(expert, *earlier), experts, capacity, tok_rows, pieces)
+
+    def enter(packed):
+        mine, cot_mine, mine_lanes, theirs, _ = packed
+        theirs = to_core(theirs)
+        x = jnp.concatenate([mine, theirs[:, :features]], axis=0)
+        shares = jnp.concatenate([mine_lanes, theirs[:, 2 * features :]], axis=0)
         held = (jnp.arange(LANES) % experts == expert_index) & (jnp.arange(LANES) < 3 * experts)
         weight = jnp.sum(jnp.where(held, shares.astype(F32), 0.0), axis=1, keepdims=True)
-        cot = jnp.concatenate([cot_mine, to_core(cot_theirs)], axis=0)
+        cot = jnp.concatenate([cot_mine, theirs[:, features : 2 * features]], axis=0)
         cot = (cot.astype(F32) * weight).astype(BF)
         pre_gate, pre_up = dot(x, w_gate), dot(x, w_up)
         act = (jax.nn.silu(pre_gate) * pre_up).astype(BF)
-        return x, weight, place, pre_gate, pre_up, act, cot
-
-    def leave(rows_of):
+        return x, weight, pre_gate, pre_up, act, cot
+
+    def leave(rows_of, *before_mine):
         half = TOGETHER * capacity
         theirs = to_core(rows_of(slice(2 * half, None)))
-        mine = rows_of(slice(0, 2 * half))
+        mine = rows_of(slice(0, 2 * half), *before_mine)
         return mine, theirs, to_x(mine[half:]), to_x(theirs[half:])
 
     def home(place, parts):
@@ -321,21 +320,27 @@
         act = lax.dynamic_slice_in_dim(act, replica * (hidden // 2), hidden // 2, 1)
         return outer_sum(x, d_gate), outer_sum(x, d_up), outer_sum(act, cot)
 
-    own_x, weight, place, pre_gate, pre_up, act, cot = enter(own_pieces, *relay[1:4], joined)
+    packed = plan(own_pieces, *relay[1:5], joined)
+    place = packed[-1]
+    own_x, weight, pre_gate, pre_up, act, cot = enter(packed)
     parts = leave(lambda rows: (dot(act[rows], w_down) * weight[rows]).astype(BF))
     cot = after(cot, parts[0], parts[1])
-    own_grads = cot, *hidden_grads(cot, pre_gate, pre_up, w_down)
-    d_gate, d_up = after(own_grads[1:], parts[2])
-    grad_parts = leave(lambda rows: input_rows(d_gate[rows], d_up[rows], w_gate, w_up))
+    d_gate, d_up = hidden_grads(cot, pre_gate, pre_up, w_down)
+
+    def token_grads(rows, *earlier):
+        return input_rows(*after((d_gate[rows], d_up[rows]), *earlier), w_gate, w_up)
+
+    grad_parts = leave(token_grads, parts[2])
     chunks = home(after(place, grad_parts[0], grad_parts[1]), parts)
-    own_grads = after(own_grads[0], grad_parts[2]), *after(own_grads[1:], chunks[0])
-    own = grads(own_x, act, *own_grads)
-    grad_chunks = home(after(place, *own), grad_parts)
-
-    x, weight, _, pre_gate, pre_up, act, cot = enter(other_pieces, grad_chunks[0], *chunks[1:])
-    cot = after(cot, act, grad_chunks[1], grad_chunks[2])
+    own_grads = after((cot, d_gate, d_up), chunks[0], last)
+    own = grads(own_x, act, after(own_grads[0], chunks[1]), *own_grads[1:])
+    packed = list(plan(other_pieces, *own, grad_parts[2]))
+    packed[0] = after(packed[0], grad_parts[3])
+    x, weight, pre_gate, pre_up, act, cot = enter(packed)
+    grad_chunks = home(after(place, act, *chunks[1:]), grad_parts)
+    cot = after(cot, grad_chunks[0])
     d_gate, d_up = hidden_grads(cot, pre_gate, pre_up, w_down)
-    other = grads(x, act, cot, d_gate, d_up)
+    other = grads(x, act, cot, d_gate, after(d_up, grad_chunks[1]))
     grad_gate, grad_up, grad_down = ((a + b).astype(BF)[None] for a, b in zip(own, other))
     return (total(chunks), total(grad_chunks), grad_gate, grad_up, grad_down)
 

time: 203 us -> 224 us (1.10)
  waiting for transfers between devices: 103 us -> 113 us
  starting transfers between devices: 26.5 us -> 31.1 us
  matrix products: 35 us -> 38.2 us
    ppermute x5 -> x6, waiting for transfers between devices: 0.01 us -> 23.4 us  [to_y(): return lax.ppermute(rows, 'replica', [(0, 1), (1, 0)])]
    ppermute x8, waiting for transfers between devices: 37.6 us -> 20.4 us  [to_x(): return lax.ppermute(rows, 'expert', [(i, i ^ 2) for i in range(experts)])]
    ppermute x8 -> x4, waiting for transfers between devices: 0.93 us -> 4.45 us  [to_core(): return lax.ppermute(rows, 'expert', [(i, i ^ 1) for i in range(experts)])]
    ppermute x9, starting transfers between devices: 9.98 us -> 13.2 us  [to_z(): lax.ppermute(rows, 'expert', [(i, (i + 4 * step) % experts) for i in rang...]
    dot_general x2, matrix products: 4.06 us -> 7.26 us  [hidden_grads(): lax.dot_general(grad_rows, down_weight, CONTRACT, preferred_element_type=...]
    unnamed x69 -> x80, local copies, waits for them, and re-layouts: 8.65 us -> 7.31 us
    ppermute x5 -> x6, starting transfers between devices: 6.6 us -> 7.14 us  [to_y(): return lax.ppermute(rows, 'replica', [(0, 1), (1, 0)])]
  transfers between devices with their start and end apart: 30 -> 27, of which waited for: 11 -> 12; matrix products, arithmetic and copies ran while one was open for 20% -> 15% of each run, Pallas kernels for 3% -> 1%
where the time goes in v11:
time: 224 us; the launch traced here: 223 us
  waiting for transfers between devices  113 us (50%)
  matrix products  38.2 us (17%)
  starting transfers between devices  31.1 us (14%)
  Pallas kernels  18 us (8%)
  local copies, waits for them, and re-layouts  14.8 us (7%)
  other arithmetic  6.79 us (3%)
    ppermute x9, waiting for transfers between devices, to_z(): lax.ppermute(rows, 'expert', [(i, (i + 4 * step) % experts) for i in rang...  65 us
    ppermute x6, waiting for transfers between devices, to_y(): return lax.ppermute(rows, 'replica', [(0, 1), (1, 0)])  23.4 us
    ppermute x8, waiting for transfers between devices, to_x(): return lax.ppermute(rows, 'expert', [(i, i ^ 2) for i in range(experts)])  20.4 us
    dot_general x6, matrix products, outer_sum(): lax.dot_general(left, right, (((0,), (0,)), ((), ())), preferred_element_...  14.1 us
    ppermute x9, starting transfers between devices, to_z(): lax.ppermute(rows, 'expert', [(i, (i + 4 * step) % experts) for i in rang...  13.2 us
    pallas_call x2, Pallas kernels, plan_and_pack(): pl.pallas_call(body, grid_spec=pltpu.PrefetchScalarGridSpec(num_scalar_pr...  11.6 us
    ppermute x8, starting transfers between devices, to_x(): return lax.ppermute(rows, 'expert', [(i, i ^ 2) for i in range(experts)])  10.4 us
    dot_general x6, matrix products, dot(): return jnp.dot(left, right, preferred_element_type=F32)  10.4 us
  transfers between devices with their start and end apart: 27, of which 12 were waited for; matrix products, arithmetic and copies ran while one was open for 15% of the time, Pallas kernels for 1%

profile of v11, /device:TPU:0, one launch (start us, length us, event | category | flops | bytes accessed | tf_op | source)
XLA Modules:
  0.0 223.4 jit_solution(13757779332956773854)
XLA Ops:
  3.6 3.0 %collective-permute-start.2 = (bf16[64,4224]{1,0:T(8,128)(2,1)}, bf16[64,4224]{1,0:T(8,128)(2,1)}, u32[]{:S(2)}, u32[]{:S(2)}) collective-permute-start(bf16[64,4224]{1,0:T(8,128)(2,1)} %concatenate.24.refs_0_), channel_id=1, source_target_pairs={{0,8},{2,10},{4,12},{6,14},{8,16},{10,18},{12,20},{14,22},{16,24},... | collective-permute-start | bytes 1622024 | tf_op jit(solution)/shard_map/ppermute | solution.py:261
  9.7 11.6 %collective-permute-done.2.refs_1_ = bf16[64,4224]{1,0:T(8,128)(2,1)} collective-permute-done((bf16[64,4224]{1,0:T(8,128)(2,1)}, bf16[64,4224]{1,0:T(8,128)(2,1)}, u32[]{:S(2)}, u32[]{:S(2)}) %collective-permute-start.2) | collective-permute-done | bytes 540704 | tf_op jit(solution)/shard_map/ppermute | solution.py:261
  22.8 14.1 %collective-permute-done.6.refs_2_ = bf16[64,4224]{1,0:T(8,128)(2,1)} collective-permute-done((bf16[64,4224]{1,0:T(8,128)(2,1)}, bf16[64,4224]{1,0:T(8,128)(2,1)}, u32[]{:S(2)}, u32[]{:S(2)}) %collective-permute-start.6) | collective-permute-done | bytes 540704 | tf_op jit(solution)/shard_map/ppermute | solution.py:261
  41.7 9.9 %collective-permute-done.9.refs_3_ = bf16[64,4224]{1,0:T(8,128)(2,1)} collective-permute-done((bf16[64,4224]{1,0:T(8,128)(2,1)}, bf16[64,4224]{1,0:T(8,128)(2,1)}, u32[]{:S(2)}, u32[]{:S(2)}) %collective-permute-start.9) | collective-permute-done | bytes 540704 | tf_op jit(solution)/shard_map/ppermute | solution.py:261
  56.8 9.0 %collective-permute-done.11.refs_7_ = bf16[64,4224]{1,0:T(8,128)(2,1)S(1)} collective-permute-done((bf16[64,4224]{1,0:T(8,128)(2,1)}, bf16[64,4224]{1,0:T(8,128)(2,1)S(1)}, u32[]{:S(2)}, u32[]{:S(2)}) %collective-permute-start.11) | collective-permute-done | bytes 540704 | tf_op jit(solution)/shard_map/ppermute | solution.py:258
  66.6 17.8 %collective-permute-done.5.refs_5_ = bf16[64,4224]{1,0:T(8,128)(2,1)} collective-permute-done((bf16[64,4224]{1,0:T(8,128)(2,1)}, bf16[64,4224]{1,0:T(8,128)(2,1)}, u32[]{:S(2)}, u32[]{:S(2)}) %collective-permute-start.5) | collective-permute-done | bytes 540704 | tf_op jit(solution)/shard_map/ppermute | solution.py:266
  84.5 5.7 %plan_and_pack.2 = (bf16[256,2048]{1,0:T(8,128)(2,1)}, bf16[256,2048]{1,0:T(8,128)(2,1)}, bf16[256,128]{1,0:T(8,128)(2,1)}, bf16[256,4224]{1,0:T(8,128)(2,1)}, bf16[256,512]{1,0:T(8,128)(2,1)}) custom-call(s32[1]{0:T(128)} %bitcast.expert_ref, bf16[64,4224]{1,0:T(8,128)(2,1)} %concatenate.24.refs_0_, bf16[64,4224]{1,0:T(8,128)(2,1)} %collective-permute-done.2.refs_1_, ...), custom_call_target="tpu_custom_call" | custom-call | flops 1 | bytes 1 | tf_op jit(solution)/shard_map/plan_and_pack/pallas_call | solution.py:185
  90.3 4.4 %collective-permute-done.12 = bf16[256,4224]{1,0:T(8,128)(2,1)S(1)} collective-permute-done((bf16[256,4224]{1,0:T(8,128)(2,1)}, bf16[256,4224]{1,0:T(8,128)(2,1)S(1)}, u32[]{:S(2)}, u32[]{:S(2)}) %collective-permute-start.12) | collective-permute-done | bytes 2162720 | tf_op jit(solution)/shard_map/ppermute | solution.py:255
  116.0 5.2 %collective-permute-done.14.refs_2_ = bf16[128,2048]{1,0:T(8,128)(2,1)} collective-permute-done((bf16[128,2048]{1,0:T(8,128)(2,1)}, bf16[128,2048]{1,0:T(8,128)(2,1)}, u32[]{:S(2)}, u32[]{:S(2)}) %collective-permute-start.14) | collective-permute-done | bytes 524320 | tf_op jit(solution)/shard_map/ppermute | solution.py:258
  121.2 2.3 %fusion.12 = f32[256,2048]{1,0:T(8,128)S(1)} fusion(bf16[256,768]{1,0:T(8,128)(2,1)} %get-tuple-element.48, bf16[1,2048,768]{2,1,0:T(8,128)(2,1)S(1)} %copy-done), kind=kOutput, calls=%fused_computation.14 | convolution fusion | flops 805306368 | bytes 5636096 | tf_op jit(solution)/shard_map/dot_general | solution.py:50
  126.3 6.2 %collective-permute-done.16.refs_3_ = bf16[128,2048]{1,0:T(8,128)(2,1)} collective-permute-done((bf16[128,2048]{1,0:T(8,128)(2,1)S(1)}, bf16[128,2048]{1,0:T(8,128)(2,1)}, u32[]{:S(2)}, u32[]{:S(2)}) %collective-permute-start.16) | collective-permute-done | bytes 524320 | tf_op jit(solution)/shard_map/ppermute | solution.py:258
  132.5 3.2 %spread.2 = (bf16[64,2048]{1,0:T(8,128)(2,1)}, bf16[64,2048]{1,0:T(8,128)(2,1)}, bf16[64,2048]{1,0:T(8,128)(2,1)}, bf16[64,2048]{1,0:T(8,128)(2,1)}) custom-call(bf16[256,512]{1,0:T(8,128)(2,1)} %get-tuple-element.64.place_ref, bf16[256,2048]{1,0:T(8,128)(2,1)} %copy-done.9, bf16[256,2048]{1,0:T(8,128)(2,1)} %collective-permute-done.13.refs_1_, ...), custom_call_target="tpu_custom_call" | custom-call | flops 1 | bytes 1 | tf_op jit(solution)/shard_map/spread/pallas_call | solution.py:220
  135.7 5.5 %collective-permute-done.20.refs_3_ = bf16[192,4224]{1,0:T(8,128)(2,1)} collective-permute-done((bf16[192,4224]{1,0:T(8,128)(2,1)}, bf16[192,4224]{1,0:T(8,128)(2,1)}, u32[]{:S(2)}, u32[]{:S(2)}) %collective-permute-start.20) | collective-permute-done | bytes 1622048 | tf_op jit(solution)/shard_map/ppermute | solution.py:266
  141.2 3.5 %collective-permute-start.17 = (bf16[64,2048]{1,0:T(8,128)(2,1)}, bf16[64,2048]{1,0:T(8,128)(2,1)}, u32[]{:S(2)}, u32[]{:S(2)}) collective-permute-start(bf16[64,2048]{1,0:T(8,128)(2,1)} %get-tuple-element.53), channel_id=1, source_target_pairs={{0,24},{2,26},{4,28},{6,30},{8,0},{10,2},{12,4},{14,6},{16,8},{18,... | collective-permute-start | bytes 786440 | tf_op jit(solution)/shard_map/ppermute | solution.py:261
  144.8 3.7 %fusion.69 = f32[1024,768]{1,0:T(8,128)} fusion(bf16[512,768]{1,0:T(8,128)(2,1)S(1)} %copy-done.21, s32[]{:T(128)S(6)} %select_n.31, bf16[256,2048]{1,0:T(8,128)(2,1)} %get-tuple-element.45, bf16[256,2048]{1,0:T(8,128)(2,1)S(1)} %copy-done.13), kind=kOutput, calls=%fused_computation.84 | convolution fusion | flops 807403520 | bytes 6029316 | tf_op jit(solution)/shard_map/dot_general | solution.py:55
  148.5 2.7 %fusion.67 = f32[1024,768]{1,0:T(8,128)} fusion(bf16[512,768]{1,0:T(8,128)(2,1)S(1)} %copy-done.19, s32[]{:T(128)S(6)} %select_n.31, bf16[256,2048]{1,0:T(8,128)(2,1)S(1)} %copy-done.31, bf16[256,2048]{1,0:T(8,128)(2,1)S(1)} %copy-done.13), kind=kOutput, calls=%fused_computation.83 | convolution fusion | flops 807403520 | bytes 6029316 | tf_op jit(solution)/shard_map/dot_general | solution.py:55
  152.2 5.9 %plan_and_pack.3 = (bf16[256,2048]{1,0:T(8,128)(2,1)}, bf16[256,2048]{1,0:T(8,128)(2,1)}, bf16[256,128]{1,0:T(8,128)(2,1)}, bf16[256,4224]{1,0:T(8,128)(2,1)}, bf16[256,512]{1,0:T(8,128)(2,1)}) custom-call(s32[1]{0:T(128)} %bitcast.expert_ref, bf16[64,4224]{1,0:T(8,128)(2,1)} %collective-permute-done.7.refs_0_, ...), custom_call_target="tpu_custom_call" | custom-call | flops 1 | bytes 1 | tf_op jit(solution)/shard_map/plan_and_pack/pallas_call | solution.py:185
  158.8 3.5 %collective-permute-start.19 = (bf16[64,2048]{1,0:T(8,128)(2,1)}, bf16[64,2048]{1,0:T(8,128)(2,1)S(1)}, u32[]{:S(2)}, u32[]{:S(2)}) collective-permute-start(bf16[64,2048]{1,0:T(8,128)(2,1)} %get-tuple-element.55), channel_id=1, source_target_pairs={{0,8},{2,10},{4,12},{6,14},{8,16},{10,18},{12,20},{14,22},{16,24},... | collective-permute-start | bytes 786440 | tf_op jit(solution)/shard_map/ppermute | solution.py:261
  164.4 14.8 %collective-permute-done.18 = bf16[64,2048]{1,0:T(8,128)(2,1)S(1)} collective-permute-done((bf16[64,2048]{1,0:T(8,128)(2,1)}, bf16[64,2048]{1,0:T(8,128)(2,1)S(1)}, u32[]{:S(2)}, u32[]{:S(2)}) %collective-permute-start.18) | collective-permute-done | bytes 262176 | tf_op jit(solution)/shard_map/ppermute | solution.py:261
  185.3 3.0 %multiply_convert_fusion.4 = (bf16[512,768]{1,0:T(8,128)(2,1)S(1)}, f32[512,768]{1,0:T(8,128)}) fusion(f32[512,768]{1,0:T(8,128)S(1)} %fusion.16, bf16[1,2048,768]{2,1,0:T(8,128)(2,1)S(1)} %copy-done, bf16[256,2048]{1,0:T(8,128)(2,1)S(1)} %get-tuple-element.76, bf16[256,2048]{1,0:T(8,128)(2,1)S(1)} %copy-done.14), kind=kOutput, calls=%fused_computation.46 | convolution fusion | flops 1617166336 | bytes 9175040 | tf_op jit(solution)/shard_map/dot_general | solution.py:102
  190.2 3.2 %spread.3 = (bf16[64,2048]{1,0:T(8,128)(2,1)}, bf16[64,2048]{1,0:T(8,128)(2,1)}, bf16[64,2048]{1,0:T(8,128)(2,1)}, bf16[64,2048]{1,0:T(8,128)(2,1)}) custom-call(bf16[256,512]{1,0:T(8,128)(2,1)} %get-tuple-element.64.place_ref, bf16[256,2048]{1,0:T(8,128)(2,1)} %copy-done.7, bf16[256,2048]{1,0:T(8,128)(2,1)} %collective-permute-done.15.refs_1_, ...), custom_call_target="tpu_custom_call" | custom-call | flops 1 | bytes 1 | tf_op jit(solution)/shard_map/spread/pallas_call | solution.py:220
  193.5 5.0 %multiply_convert_fusion.2 = (bf16[512,768]{1,0:T(8,128)(2,1)S(1)}, f32[512,768]{1,0:T(8,128)S(1)}) fusion(f32[512,768]{1,0:T(8,128)} %copy-done.36, bf16[512,2048]{1,0:T(8,128)(2,1)} %multiply_convert_fusion, bf16[1,768,2048]{2,1,0:T(8,128)(2,1)} %param.13), kind=kOutput, calls=%fused_computation.44 | convolution fusion | flops 1612972032 | bytes 9175040 | tf_op jit(solution)/shard_map/dot_general | solution.py:41
  201.2 2.3 %fusion.49 = bf16[1,1024,768]{2,1,0:T(8,128)(2,1)} fusion(f32[1024,768]{1,0:T(8,128)S(1)} %copy-done.35, f32[512,768]{1,0:T(8,128)S(1)} %copy-done.37, f32[512,768]{1,0:T(8,128)S(1)} %get-tuple-element.92, f32[512,768]{1,0:T(8,128)S(1)} %copy-done.38, s32[]{:T(128)S(6)} %select_n.31, bf16[256,2048]{1,0:T(8,128)(2,1)S(1)} %copy-done.15, ...), kind=kOutput, calls=%fused_computation.52 | convolution fusion | flops 812908544 | bytes 11534340 | tf_op jit(solution)/shard_map/dot_general | solution.py:55
  209.8 12.7 %collective-permute-done.25 = bf16[64,2048]{1,0:T(8,128)(2,1)S(1)} collective-permute-done((bf16[64,2048]{1,0:T(8,128)(2,1)S(1)}, bf16[64,2048]{1,0:T(8,128)(2,1)S(1)}, u32[]{:S(2)}, u32[]{:S(2)}) %collective-permute-start.25) | collective-permute-done | bytes 262176 | tf_op jit(solution)/shard_map/ppermute | solution.py:261
  (157 shorter events, 63.8 us)
Async XLA Ops:
  3.6 17.6 %collective-permute-start.2 = (bf16[64,4224]{1,0:T(8,128)(2,1)}, bf16[64,4224]{1,0:T(8,128)(2,1)}, u32[]{:S(2)}, u32[]{:S(2)}) collective-permute-start(bf16[64,4224]{1,0:T(8,128)(2,1)} %concatenate.24.refs_0_), channel_id=1, source_target_pairs={{0,8},{2,10},{4,12},{6,14},{8,16},{10,18},{12,20},{14,22},{16,24},... | collective-permute-start | bytes 1622024 | tf_op jit(solution)/shard_map/ppermute | solution.py:261
  6.7 16.1 %collective-permute-start.7 = (bf16[64,4224]{1,0:T(8,128)(2,1)}, bf16[64,4224]{1,0:T(8,128)(2,1)}, u32[]{:S(2)}, u32[]{:S(2)}) collective-permute-start(bf16[64,4224]{1,0:T(8,128)(2,1)} %concatenate.24.refs_0_), channel_id=1, source_target_pairs={{0,1},{1,0},{2,3},{3,2},{4,5},{5,4},{6,7},{7,6},{8,9},{9,8},{10,11... | collective-permute-start | bytes 1622024 | tf_op jit(solution)/shard_map/ppermute | solution.py:266
  8.2 14.6 %collective-permute-start = (bf16[64,4224]{1,0:T(8,128)(2,1)}, bf16[64,4224]{1,0:T(8,128)(2,1)}, u32[]{:S(2)}, u32[]{:S(2)}) collective-permute-start(bf16[64,4224]{1,0:T(8,128)(2,1)} %concatenate.24.refs_0_), channel_id=1, source_target_pairs={{0,4},{2,6},{4,0},{6,2},{8,12},{10,14},{12,8},{14,10},{16,20},{18,... | collective-permute-start | bytes 1622024 | tf_op jit(solution)/shard_map/ppermute | solution.py:258
  21.3 15.6 %collective-permute-start.6 = (bf16[64,4224]{1,0:T(8,128)(2,1)}, bf16[64,4224]{1,0:T(8,128)(2,1)}, u32[]{:S(2)}, u32[]{:S(2)}) collective-permute-start(bf16[64,4224]{1,0:T(8,128)(2,1)} %collective-permute-done.2.refs_1_), channel_id=1, source_target_pairs={{0,8},{2,10},{4,12},{6,14},{8,16},{10,18},{12,20},{14,22},{16,24},... | collective-permute-start | bytes 1622024 | tf_op jit(solution)/shard_map/ppermute | solution.py:261
  21.3 18.9 %collective-permute-start.4 = (bf16[64,4224]{1,0:T(8,128)(2,1)}, bf16[64,4224]{1,0:T(8,128)(2,1)}, u32[]{:S(2)}, u32[]{:S(2)}) collective-permute-start(bf16[64,4224]{1,0:T(8,128)(2,1)} %collective-permute-done.2.refs_1_), channel_id=1, source_target_pairs={{0,4},{2,6},{4,0},{6,2},{8,12},{10,14},{12,8},{14,10},{16,20},{18,... | collective-permute-start | bytes 1622024 | tf_op jit(solution)/shard_map/ppermute | solution.py:258
  36.9 14.7 %collective-permute-start.9 = (bf16[64,4224]{1,0:T(8,128)(2,1)}, bf16[64,4224]{1,0:T(8,128)(2,1)}, u32[]{:S(2)}, u32[]{:S(2)}) collective-permute-start(bf16[64,4224]{1,0:T(8,128)(2,1)} %collective-permute-done.6.refs_2_), channel_id=1, source_target_pairs={{0,8},{2,10},{4,12},{6,14},{8,16},{10,18},{12,20},{14,22},{16,24},... | collective-permute-start | bytes 1622024 | tf_op jit(solution)/shard_map/ppermute | solution.py:261
  36.9 29.8 %collective-permute-start.3 = (bf16[64,4224]{1,0:T(8,128)(2,1)}, bf16[64,4224]{1,0:T(8,128)(2,1)}, u32[]{:S(2)}, u32[]{:S(2)}) collective-permute-start(bf16[64,4224]{1,0:T(8,128)(2,1)} %collective-permute-done.2.refs_1_), channel_id=1, source_target_pairs={{0,1},{1,0},{2,3},{3,2},{4,5},{5,4},{6,7},{7,6},{8,9},{9,8},{10,11... | collective-permute-start | bytes 1622024 | tf_op jit(solution)/shard_map/ppermute | solution.py:266
  38.1 28.5 %collective-permute-start.1 = (bf16[64,4224]{1,0:T(8,128)(2,1)}, bf16[64,4224]{1,0:T(8,128)(2,1)}, u32[]{:S(2)}, u32[]{:S(2)}) collective-permute-start(bf16[64,4224]{1,0:T(8,128)(2,1)} %collective-permute-done.refs_4_), channel_id=1, source_target_pairs={{0,1},{1,0},{2,3},{3,2},{4,5},{5,4},{6,7},{7,6},{8,9},{9,8},{10,11... | collective-permute-start | bytes 1622024 | tf_op jit(solution)/shard_map/ppermute | solution.py:266
  38.9 15.6 %collective-permute-start.10 = (bf16[64,4224]{1,0:T(8,128)(2,1)}, bf16[64,4224]{1,0:T(8,128)(2,1)S(1)}, u32[]{:S(2)}, u32[]{:S(2)}) collective-permute-start(bf16[64,4224]{1,0:T(8,128)(2,1)} %collective-permute-done.6.refs_2_), channel_id=1, source_target_pairs={{0,4},{2,6},{4,0},{6,2},{8,12},{10,14},{12,8},{14,10},{16,20},{18,... | collective-permute-start | bytes 1622024 | tf_op jit(solution)/shard_map/ppermute | solution.py:258
  40.1 44.3 %collective-permute-start.8 = (bf16[64,4224]{1,0:T(8,128)(2,1)}, bf16[64,4224]{1,0:T(8,128)(2,1)}, u32[]{:S(2)}, u32[]{:S(2)}) collective-permute-start(bf16[64,4224]{1,0:T(8,128)(2,1)} %collective-permute-done.6.refs_2_), channel_id=1, source_target_pairs={{0,1},{1,0},{2,3},{3,2},{4,5},{5,4},{6,7},{7,6},{8,9},{9,8},{10,11... | collective-permute-start | bytes 1622024 | tf_op jit(solution)/shard_map/ppermute | solution.py:266
  51.5 33.0 %collective-permute-start.5 = (bf16[64,4224]{1,0:T(8,128)(2,1)}, bf16[64,4224]{1,0:T(8,128)(2,1)}, u32[]{:S(2)}, u32[]{:S(2)}) collective-permute-start(bf16[64,4224]{1,0:T(8,128)(2,1)} %collective-permute-done.4.refs_5_), channel_id=1, source_target_pairs={{0,1},{1,0},{2,3},{3,2},{4,5},{5,4},{6,7},{7,6},{8,9},{9,8},{10,11... | collective-permute-start | bytes 1622024 | tf_op jit(solution)/shard_map/ppermute | solution.py:266
  54.4 11.3 %collective-permute-start.11 = (bf16[64,4224]{1,0:T(8,128)(2,1)}, bf16[64,4224]{1,0:T(8,128)(2,1)S(1)}, u32[]{:S(2)}, u32[]{:S(2)}) collective-permute-start(bf16[64,4224]{1,0:T(8,128)(2,1)} %collective-permute-done.9.refs_3_), channel_id=1, source_target_pairs={{0,4},{2,6},{4,0},{6,2},{8,12},{10,14},{12,8},{14,10},{16,20},{18,... | collective-permute-start | bytes 1622024 | tf_op jit(solution)/shard_map/ppermute | solution.py:258
  103.2 38.0 %collective-permute-start.20 = (bf16[192,4224]{1,0:T(8,128)(2,1)}, bf16[192,4224]{1,0:T(8,128)(2,1)}, u32[]{:S(2)}, u32[]{:S(2)}) collective-permute-start(bf16[192,4224]{1,0:T(8,128)(2,1)} %constant_dynamic-update-slice_fusion), channel_id=1, source_target_pairs={{0,1},{1,0},{2,3},{3,2},{4,5},{5,4},{6,7},{7,6},{8,9},{9,8},{10,11... | collective-permute-start | bytes 4866056 | tf_op jit(solution)/shard_map/ppermute | solution.py:266
  106.1 15.1 %collective-permute-start.14 = (bf16[128,2048]{1,0:T(8,128)(2,1)}, bf16[128,2048]{1,0:T(8,128)(2,1)}, u32[]{:S(2)}, u32[]{:S(2)}) collective-permute-start(bf16[128,2048]{1,0:T(8,128)(2,1)} %slice.81), channel_id=1, source_target_pairs={{0,4},{2,6},{4,0},{6,2},{8,12},{10,14},{12,8},{14,10},{16,20},{18,... | collective-permute-start | bytes 1572872 | tf_op jit(solution)/shard_map/ppermute | solution.py:258
  114.3 11.9 %collective-permute-start.15 = (bf16[256,2048]{1,0:T(8,128)(2,1)}, bf16[256,2048]{1,0:T(8,128)(2,1)}, u32[]{:S(2)}, u32[]{:S(2)}) collective-permute-start(bf16[256,2048]{1,0:T(8,128)(2,1)} %fusion.43), channel_id=1, source_target_pairs={{0,2},{2,0},{4,6},{6,4},{8,10},{10,8},{12,14},{14,12},{16,18},{18,... | collective-permute-start | bytes 3145736 | tf_op jit(solution)/shard_map/ppermute | solution.py:255
  115.4 17.0 %collective-permute-start.16 = (bf16[128,2048]{1,0:T(8,128)(2,1)S(1)}, bf16[128,2048]{1,0:T(8,128)(2,1)}, u32[]{:S(2)}, u32[]{:S(2)}) collective-permute-start(bf16[128,2048]{1,0:T(8,128)(2,1)S(1)} %slice.84), channel_id=1, source_target_pairs={{0,4},{2,6},{4,0},{6,2},{8,12},{10,14},{12,8},{14,10},{16,20},{18,... | collective-permute-start | bytes 1572872 | tf_op jit(solution)/shard_map/ppermute | solution.py:258
  124.7 27.5 %collective-permute-start.21 = (bf16[128,2048]{1,0:T(8,128)(2,1)S(1)}, bf16[128,2048]{1,0:T(8,128)(2,1)S(1)}, u32[]{:S(2)}, u32[]{:S(2)}) collective-permute-start(bf16[128,2048]{1,0:T(8,128)(2,1)S(1)} %slice.85), channel_id=1, source_target_pairs={{0,4},{2,6},{4,0},{6,2},{8,12},{10,14},{12,8},{14,10},{16,20},{18,... | collective-permute-start | bytes 1572872 | tf_op jit(solution)/shard_map/ppermute | solution.py:258
  141.2 10.0 %collective-permute-start.17 = (bf16[64,2048]{1,0:T(8,128)(2,1)}, bf16[64,2048]{1,0:T(8,128)(2,1)}, u32[]{:S(2)}, u32[]{:S(2)}) collective-permute-start(bf16[64,2048]{1,0:T(8,128)(2,1)} %get-tuple-element.53), channel_id=1, source_target_pairs={{0,24},{2,26},{4,28},{6,30},{8,0},{10,2},{12,4},{14,6},{16,8},{18,... | collective-permute-start | bytes 786440 | tf_op jit(solution)/shard_map/ppermute | solution.py:261
  158.1 23.0 %collective-permute-start.23 = (bf16[256,4224]{1,0:T(8,128)(2,1)}, bf16[256,4224]{1,0:T(8,128)(2,1)S(1)}, u32[]{:S(2)}, u32[]{:S(2)}) collective-permute-start(bf16[256,4224]{1,0:T(8,128)(2,1)} %get-tuple-element.63), channel_id=1, source_target_pairs={{0,2},{2,0},{4,6},{6,4},{8,10},{10,8},{12,14},{14,12},{16,18},{18,... | collective-permute-start | bytes 6488072 | tf_op jit(solution)/shard_map/ppermute | solution.py:255
  158.2 21.1 %collective-permute-start.18 = (bf16[64,2048]{1,0:T(8,128)(2,1)}, bf16[64,2048]{1,0:T(8,128)(2,1)S(1)}, u32[]{:S(2)}, u32[]{:S(2)}) collective-permute-start(bf16[64,2048]{1,0:T(8,128)(2,1)} %get-tuple-element.54), channel_id=1, source_target_pairs={{0,16},{2,18},{4,20},{6,22},{8,24},{10,26},{12,28},{14,30},{16,0},... | collective-permute-start | bytes 786440 | tf_op jit(solution)/shard_map/ppermute | solution.py:261
  158.8 20.5 %collective-permute-start.19 = (bf16[64,2048]{1,0:T(8,128)(2,1)}, bf16[64,2048]{1,0:T(8,128)(2,1)S(1)}, u32[]{:S(2)}, u32[]{:S(2)}) collective-permute-start(bf16[64,2048]{1,0:T(8,128)(2,1)} %get-tuple-element.55), channel_id=1, source_target_pairs={{0,8},{2,10},{4,12},{6,14},{8,16},{10,18},{12,20},{14,22},{16,24},... | collective-permute-start | bytes 786440 | tf_op jit(solution)/shard_map/ppermute | solution.py:261
  163.4 17.7 %collective-permute-start.22 = (bf16[128,2048]{1,0:T(8,128)(2,1)S(1)}, bf16[128,2048]{1,0:T(8,128)(2,1)S(1)}, u32[]{:S(2)}, u32[]{:S(2)}) collective-permute-start(bf16[128,2048]{1,0:T(8,128)(2,1)S(1)} %slice.86), channel_id=1, source_target_pairs={{0,4},{2,6},{4,0},{6,2},{8,12},{10,14},{12,8},{14,10},{16,20},{18,... | collective-permute-start | bytes 1572872 | tf_op jit(solution)/shard_map/ppermute | solution.py:258
  198.6 23.9 %collective-permute-start.25 = (bf16[64,2048]{1,0:T(8,128)(2,1)S(1)}, bf16[64,2048]{1,0:T(8,128)(2,1)S(1)}, u32[]{:S(2)}, u32[]{:S(2)}) collective-permute-start(bf16[64,2048]{1,0:T(8,128)(2,1)S(1)} %copy-done.33), channel_id=1, source_target_pairs={{0,16},{2,18},{4,20},{6,22},{8,24},{10,26},{12,28},{14,30},{16,0},... | collective-permute-start | bytes 786440 | tf_op jit(solution)/shard_map/ppermute | solution.py:261
  199.2 23.3 %collective-permute-start.26 = (bf16[64,2048]{1,0:T(8,128)(2,1)S(1)}, bf16[64,2048]{1,0:T(8,128)(2,1)S(1)}, u32[]{:S(2)}, u32[]{:S(2)}) collective-permute-start(bf16[64,2048]{1,0:T(8,128)(2,1)S(1)} %copy-done.32), channel_id=1, source_target_pairs={{0,8},{2,10},{4,12},{6,14},{8,16},{10,18},{12,20},{14,22},{16,24},... | collective-permute-start | bytes 786440 | tf_op jit(solution)/shard_map/ppermute | solution.py:261
  (42 other events, 381.5 us)

commit v12 on v11

--- a/solution.py
+++ b/solution.py
@@ -275,9 +275,9 @@
     far.append(to_x(near[1]))
     near.append(after(to_z(near[1], 1), far[0], relay[0]))
     far.append(to_x(near[2]))
-    near.append(to_z(near[2], 1))
+    relay += [to_y(far[0]), to_y(near[1]), to_y(far[1]), to_y(near[2])]
+    near.append(after(to_z(near[2], 1), relay[1], relay[2]))
     far.append(to_x(near[3]))
-    relay += [to_y(far[0]), to_y(near[1]), to_y(far[1]), to_y(near[2])]
     joined = jnp.concatenate([near[3], far[2], far[3]], axis=0)
     last = to_y(joined)
     own_pieces = [(a, 0) for a in near + far]
@@ -302,11 +302,11 @@
         act = (jax.nn.silu(pre_gate) * pre_up).astype(BF)
         return x, weight, pre_gate, pre_up, act, cot
 
-    def leave(rows_of, *before_mine):
+    def leave(rows_of, before_mine=(), before_far=()):
         half = TOGETHER * capacity
         theirs = to_core(rows_of(slice(2 * half, None)))
         mine = rows_of(slice(0, 2 * half), *before_mine)
-        return mine, theirs, to_x(mine[half:]), to_x(theirs[half:])
+        return mine, theirs, to_x(after(mine[half:], *before_far)), to_x(theirs[half:])
 
     def home(place, parts):
         own, *others = spread(place, *parts)
@@ -320,7 +320,7 @@
         act = lax.dynamic_slice_in_dim(act, replica * (hidden // 2), hidden // 2, 1)
         return outer_sum(x, d_gate), outer_sum(x, d_up), outer_sum(act, cot)
 
-    packed = plan(own_pieces, *relay[1:5], joined)
+    packed = plan(own_pieces, *relay[3:5], joined)
     place = packed[-1]
     own_x, weight, pre_gate, pre_up, act, cot = enter(packed)
     parts = leave(lambda rows: (dot(act[rows], w_down) * weight[rows]).astype(BF))
@@ -330,17 +330,17 @@
     def token_grads(rows, *earlier):
         return input_rows(*after((d_gate[rows], d_up[rows]), *earlier), w_gate, w_up)
 
-    grad_parts = leave(token_grads, parts[2])
+    grad_parts = leave(token_grads, parts[2:3], parts[3:4])
     chunks = home(after(place, grad_parts[0], grad_parts[1]), parts)
-    own_grads = after((cot, d_gate, d_up), chunks[0], last)
-    own = grads(own_x, act, after(own_grads[0], chunks[1]), *own_grads[1:])
-    packed = list(plan(other_pieces, *own, grad_parts[2]))
-    packed[0] = after(packed[0], grad_parts[3])
+    own_grads = after((cot, d_gate, d_up), chunks[0])
+    own = grads(own_x, act, *own_grads)
+    grad_chunks = home(after(place, *own, *chunks[1:]), grad_parts)
+
+    packed = plan(other_pieces, grad_chunks[0])
     x, weight, pre_gate, pre_up, act, cot = enter(packed)
-    grad_chunks = home(after(place, act, *chunks[1:]), grad_parts)
-    cot = after(cot, grad_chunks[0])
     d_gate, d_up = hidden_grads(cot, pre_gate, pre_up, w_down)
     other = grads(x, act, cot, d_gate, after(d_up, grad_chunks[1]))
+    grad_chunks = after(grad_chunks, other[0])
     grad_gate, grad_up, grad_down = ((a + b).astype(BF)[None] for a, b in zip(own, other))
     return (total(chunks), total(grad_chunks), grad_gate, grad_up, grad_down)
 

time: 224 us -> 190 us (0.85)
  waiting for transfers between devices: 113 us -> 72.3 us
  starting transfers between devices: 31.1 us -> 37.8 us
  local copies, waits for them, and re-layouts: 14.8 us -> 18.9 us
  matrix products: 38.2 us -> 34.5 us
    ppermute x9, waiting for transfers between devices: 65 us -> 35.2 us  [to_z(): lax.ppermute(rows, 'expert', [(i, (i + 4 * step) % experts) for i in rang...]
    ppermute x9, starting transfers between devices: 13.2 us -> 21.3 us  [to_z(): lax.ppermute(rows, 'expert', [(i, (i + 4 * step) % experts) for i in rang...]
    ppermute x6, waiting for transfers between devices: 23.4 us -> 15.3 us  [to_y(): return lax.ppermute(rows, 'replica', [(0, 1), (1, 0)])]
    dot_general x2, matrix products: 7.26 us -> 4.04 us  [hidden_grads(): lax.dot_general(grad_rows, down_weight, CONTRACT, preferred_element_type=...]
    ppermute x8, waiting for transfers between devices: 20.4 us -> 17.4 us  [to_x(): return lax.ppermute(rows, 'expert', [(i, i ^ 2) for i in range(experts)])]
    unnamed x80 -> x66, local copies, waits for them, and re-layouts: 7.31 us -> 10.2 us
  transfers between devices with their start and end apart: 27 -> 27, of which waited for: 12 -> 11; matrix products, arithmetic and copies ran while one was open for 15% -> 22% of each run, Pallas kernels for 1% -> 3%
where the time goes in v12:
time: 190 us
  waiting for transfers between devices  72.3 us (38%)
  starting transfers between devices  37.8 us (20%)
  matrix products  34.5 us (18%)
  local copies, waits for them, and re-layouts  18.9 us (10%)
  Pallas kernels  17.8 us (9%)
  other arithmetic  7.43 us (4%)
    ppermute x9, waiting for transfers between devices, to_z(): lax.ppermute(rows, 'expert', [(i, (i + 4 * step) % experts) for i in rang...  35.2 us
    ppermute x9, starting transfers between devices, to_z(): lax.ppermute(rows, 'expert', [(i, (i + 4 * step) % experts) for i in rang...  21.3 us
    ppermute x8, waiting for transfers between devices, to_x(): return lax.ppermute(rows, 'expert', [(i, i ^ 2) for i in range(experts)])  17.4 us
    ppermute x6, waiting for transfers between devices, to_y(): return lax.ppermute(rows, 'replica', [(0, 1), (1, 0)])  15.3 us
    dot_general x6, matrix products, outer_sum(): lax.dot_general(left, right, (((0,), (0,)), ((), ())), preferred_element_...  13.7 us
    pallas_call x2, Pallas kernels, plan_and_pack(): pl.pallas_call(body, grid_spec=pltpu.PrefetchScalarGridSpec(num_scalar_pr...  11.3 us
    unnamed x66, local copies, waits for them, and re-layouts  10.2 us
    dot_general x6, matrix products, dot(): return jnp.dot(left, right, preferred_element_type=F32)  9.41 us
  transfers between devices with their start and end apart: 27, of which 11 were waited for; matrix products, arithmetic and copies ran while one was open for 22% of the time, Pallas kernels for 3%

profile of v12, /device:TPU:0, one launch (start us, length us, event | category | flops | bytes accessed | tf_op | source)
XLA Modules:
  0.0 189.8 jit_solution(13930042021878454144)
XLA Ops:
  3.6 3.0 %collective-permute-start = (bf16[64,4224]{1,0:T(8,128)(2,1)}, bf16[64,4224]{1,0:T(8,128)(2,1)}, u32[]{:S(2)}, u32[]{:S(2)}) collective-permute-start(bf16[64,4224]{1,0:T(8,128)(2,1)} %concatenate.24.refs_0_), channel_id=1, source_target_pairs={{0,8},{2,10},{4,12},{6,14},{8,16},{10,18},{12,20},{14,22},{16,24},... | collective-permute-start | bytes 1622024 | tf_op jit(solution)/shard_map/ppermute | solution.py:261
  9.7 11.6 %collective-permute-done.refs_1_ = bf16[64,4224]{1,0:T(8,128)(2,1)} collective-permute-done((bf16[64,4224]{1,0:T(8,128)(2,1)}, bf16[64,4224]{1,0:T(8,128)(2,1)}, u32[]{:S(2)}, u32[]{:S(2)}) %collective-permute-start) | collective-permute-done | bytes 540704 | tf_op jit(solution)/shard_map/ppermute | solution.py:261
  24.8 12.0 %collective-permute-done.3.refs_2_ = bf16[64,4224]{1,0:T(8,128)(2,1)} collective-permute-done((bf16[64,4224]{1,0:T(8,128)(2,1)}, bf16[64,4224]{1,0:T(8,128)(2,1)}, u32[]{:S(2)}, u32[]{:S(2)}) %collective-permute-start.3) | collective-permute-done | bytes 540704 | tf_op jit(solution)/shard_map/ppermute | solution.py:261
  38.1 8.5 %collective-permute-done.8.refs_4_ = bf16[64,4224]{1,0:T(8,128)(2,1)} collective-permute-done((bf16[64,4224]{1,0:T(8,128)(2,1)}, bf16[64,4224]{1,0:T(8,128)(2,1)}, u32[]{:S(2)}, u32[]{:S(2)}) %collective-permute-start.8) | collective-permute-done | bytes 540704 | tf_op jit(solution)/shard_map/ppermute | solution.py:266
  48.7 2.8 %collective-permute-done.7.refs_3_ = bf16[64,4224]{1,0:T(8,128)(2,1)} collective-permute-done((bf16[64,4224]{1,0:T(8,128)(2,1)}, bf16[64,4224]{1,0:T(8,128)(2,1)}, u32[]{:S(2)}, u32[]{:S(2)}) %collective-permute-start.7) | collective-permute-done | bytes 540704 | tf_op jit(solution)/shard_map/ppermute | solution.py:261
  55.3 8.0 %collective-permute-done.11.refs_7_ = bf16[64,4224]{1,0:T(8,128)(2,1)S(1)} collective-permute-done((bf16[64,4224]{1,0:T(8,128)(2,1)}, bf16[64,4224]{1,0:T(8,128)(2,1)S(1)}, u32[]{:S(2)}, u32[]{:S(2)}) %collective-permute-start.11) | collective-permute-done | bytes 540704 | tf_op jit(solution)/shard_map/ppermute | solution.py:258
  64.3 6.8 %collective-permute-done.2.refs_5_ = bf16[64,4224]{1,0:T(8,128)(2,1)} collective-permute-done((bf16[64,4224]{1,0:T(8,128)(2,1)}, bf16[64,4224]{1,0:T(8,128)(2,1)}, u32[]{:S(2)}, u32[]{:S(2)}) %collective-permute-start.2) | collective-permute-done | bytes 540704 | tf_op jit(solution)/shard_map/ppermute | solution.py:266
  71.1 5.7 %plan_and_pack.2 = (bf16[256,2048]{1,0:T(8,128)(2,1)}, bf16[256,2048]{1,0:T(8,128)(2,1)}, bf16[256,128]{1,0:T(8,128)(2,1)}, bf16[256,4224]{1,0:T(8,128)(2,1)}, bf16[256,512]{1,0:T(8,128)(2,1)}) custom-call(s32[1]{0:T(128)} %bitcast.expert_ref, bf16[64,4224]{1,0:T(8,128)(2,1)} %concatenate.24.refs_0_, bf16[64,4224]{1,0:T(8,128)(2,1)} %collective-permute-done.refs_1_, ...), custom_call_target="tpu_custom_call" | custom-call | flops 1 | bytes 1 | tf_op jit(solution)/shard_map/plan_and_pack/pallas_call | solution.py:185
  76.9 4.4 %collective-permute-done.12 = bf16[256,4224]{1,0:T(8,128)(2,1)S(1)} collective-permute-done((bf16[256,4224]{1,0:T(8,128)(2,1)}, bf16[256,4224]{1,0:T(8,128)(2,1)S(1)}, u32[]{:S(2)}, u32[]{:S(2)}) %collective-permute-start.12) | collective-permute-done | bytes 2162720 | tf_op jit(solution)/shard_map/ppermute | solution.py:255
  91.9 2.2 %multiply_convert_fusion.4 = (bf16[512,768]{1,0:T(8,128)(2,1)S(1)}, bf16[512,768]{1,0:T(8,128)(2,1)S(1)}) fusion(f32[512,768]{1,0:T(8,128)S(1)} %fusion.22, f32[512,768]{1,0:T(8,128)S(1)} %get-tuple-element.96, bf16[512,2048]{1,0:T(8,128)(2,1)S(1)} %multiply_convert_fusion.1, bf16[1,768,2048]{2,1,0:T(8,128)(2,1)S(1)} %copy-done.27), kind=kOutput, calls=%fused_computation.48 | convolution fusion | flops 1615724544 | bytes 9961472 | tf_op jit(solution)/shard_map/dot_general | solution.py:41
  101.5 4.0 %collective-permute-done.14.refs_2_ = bf16[128,2048]{1,0:T(8,128)(2,1)} collective-permute-done((bf16[128,2048]{1,0:T(8,128)(2,1)}, bf16[128,2048]{1,0:T(8,128)(2,1)}, u32[]{:S(2)}, u32[]{:S(2)}) %collective-permute-start.14) | collective-permute-done | bytes 524320 | tf_op jit(solution)/shard_map/ppermute | solution.py:258
  105.5 3.2 %fusion.12 = f32[256,2048]{1,0:T(8,128)S(1)} fusion(bf16[256,768]{1,0:T(8,128)(2,1)} %get-tuple-element.52, bf16[1,2048,768]{2,1,0:T(8,128)(2,1)} %param.12), kind=kOutput, calls=%fused_computation.14 | convolution fusion | flops 805306368 | bytes 5636096 | tf_op jit(solution)/shard_map/dot_general | solution.py:50
  110.7 5.4 %collective-permute-done.16.refs_3_ = bf16[128,2048]{1,0:T(8,128)(2,1)S(1)} collective-permute-done((bf16[128,2048]{1,0:T(8,128)(2,1)S(1)}, bf16[128,2048]{1,0:T(8,128)(2,1)S(1)}, u32[]{:S(2)}, u32[]{:S(2)}) %collective-permute-start.16) | collective-permute-done | bytes 524320 | tf_op jit(solution)/shard_map/ppermute | solution.py:258
  117.9 3.2 %spread.2 = (bf16[64,2048]{1,0:T(8,128)(2,1)}, bf16[64,2048]{1,0:T(8,128)(2,1)}, bf16[64,2048]{1,0:T(8,128)(2,1)}, bf16[64,2048]{1,0:T(8,128)(2,1)}) custom-call(bf16[256,512]{1,0:T(8,128)(2,1)} %get-tuple-element.63.place_ref, bf16[256,2048]{1,0:T(8,128)(2,1)} %copy-done.7, bf16[256,2048]{1,0:T(8,128)(2,1)} %collective-permute-done.13.refs_1_, ...), custom_call_target="tpu_custom_call" | custom-call | flops 1 | bytes 1 | tf_op jit(solution)/shard_map/spread/pallas_call | solution.py:220
  121.1 3.3 %collective-permute-start.17 = (bf16[64,2048]{1,0:T(8,128)(2,1)}, bf16[64,2048]{1,0:T(8,128)(2,1)S(1)}, u32[]{:S(2)}, u32[]{:S(2)}) collective-permute-start(bf16[64,2048]{1,0:T(8,128)(2,1)} %get-tuple-element.57), channel_id=1, source_target_pairs={{0,24},{2,26},{4,28},{6,30},{8,0},{10,2},{12,4},{14,6},{16,8},{18,... | collective-permute-start | bytes 786440 | tf_op jit(solution)/shard_map/ppermute | solution.py:261
  126.6 2.7 %fusion.59 = f32[384,2048]{1,0:T(8,128)S(1)} fusion(bf16[512,2048]{1,0:T(8,128)(2,1)} %copy-done.3, bf16[512,768]{1,0:T(8,128)(2,1)} %copy-done.26, s32[]{:T(128)S(6)} %select_n.32), kind=kOutput, calls=%fused_computation.64 | convolution fusion | flops 805306368 | bytes 5636100 | tf_op jit(solution)/shard_map/dot_general | solution.py:55
  129.4 2.7 %fusion.73 = f32[1024,768]{1,0:T(8,128)} fusion(bf16[512,768]{1,0:T(8,128)(2,1)S(1)} %copy-done.19, s32[]{:T(128)S(6)} %select_n.31, bf16[256,2048]{1,0:T(8,128)(2,1)S(1)} %copy-done.30, bf16[256,2048]{1,0:T(8,128)(2,1)S(1)} %copy-done.13), kind=kOutput, calls=%fused_computation.88 | convolution fusion | flops 807403520 | bytes 6029316 | tf_op jit(solution)/shard_map/dot_general | solution.py:55
  132.0 10.4 %collective-permute-start.19 = (bf16[64,2048]{1,0:T(8,128)(2,1)S(1)}, bf16[64,2048]{1,0:T(8,128)(2,1)S(1)}, u32[]{:S(2)}, u32[]{:S(2)}) collective-permute-start(bf16[64,2048]{1,0:T(8,128)(2,1)S(1)} %copy-done.31), channel_id=1, source_target_pairs={{0,8},{2,10},{4,12},{6,14},{8,16},{10,18},{12,20},{14,22},{16,24},... | collective-permute-start | bytes 786440 | tf_op jit(solution)/shard_map/ppermute | solution.py:261
  142.4 2.7 %fusion.71 = f32[1024,768]{1,0:T(8,128)} fusion(bf16[512,768]{1,0:T(8,128)(2,1)S(1)} %copy-done.17, s32[]{:T(128)S(6)} %select_n.31, bf16[256,2048]{1,0:T(8,128)(2,1)S(1)} %copy-done.30, bf16[256,2048]{1,0:T(8,128)(2,1)S(1)} %copy-done.13), kind=kOutput, calls=%fused_computation.87 | convolution fusion | flops 807403520 | bytes 6029316 | tf_op jit(solution)/shard_map/dot_general | solution.py:55
  147.1 3.2 %spread.3 = (bf16[64,2048]{1,0:T(8,128)(2,1)}, bf16[64,2048]{1,0:T(8,128)(2,1)}, bf16[64,2048]{1,0:T(8,128)(2,1)}, bf16[64,2048]{1,0:T(8,128)(2,1)}) custom-call(bf16[256,512]{1,0:T(8,128)(2,1)} %get-tuple-element.63.place_ref, bf16[256,2048]{1,0:T(8,128)(2,1)} %copy-done.4, bf16[256,2048]{1,0:T(8,128)(2,1)} %collective-permute-done.15.refs_1_, ...), custom_call_target="tpu_custom_call" | custom-call | flops 1 | bytes 1 | tf_op jit(solution)/shard_map/spread/pallas_call | solution.py:220
  151.5 5.7 %plan_and_pack.3 = (bf16[256,2048]{1,0:T(8,128)(2,1)}, bf16[256,2048]{1,0:T(8,128)(2,1)}, bf16[256,128]{1,0:T(8,128)(2,1)}, bf16[256,4224]{1,0:T(8,128)(2,1)}, bf16[256,512]{1,0:T(8,128)(2,1)}) custom-call(s32[1]{0:T(128)} %bitcast.expert_ref, bf16[64,4224]{1,0:T(8,128)(2,1)} %collective-permute-done.5.refs_0_, ...), custom_call_target="tpu_custom_call" | custom-call | flops 1 | bytes 1 | tf_op jit(solution)/shard_map/plan_and_pack/pallas_call | solution.py:185
  159.2 3.8 %collective-permute-start.23 = (bf16[64,2048]{1,0:T(8,128)(2,1)}, bf16[64,2048]{1,0:T(8,128)(2,1)S(1)}, u32[]{:S(2)}, u32[]{:S(2)}) collective-permute-start(bf16[64,2048]{1,0:T(8,128)(2,1)} %get-tuple-element.67), channel_id=1, source_target_pairs={{0,16},{2,18},{4,20},{6,22},{8,24},{10,26},{12,28},{14,30},{16,0},... | collective-permute-start | bytes 786440 | tf_op jit(solution)/shard_map/ppermute | solution.py:261
  176.4 2.3 %fusion.36 = bf16[1,384,2048]{2,1,0:T(8,128)(2,1)} fusion(f32[384,2048]{1,0:T(8,128)S(1)} %fusion.59, f32[512,768]{1,0:T(8,128)S(1)} %fusion.8, s32[]{:T(128)S(6)} %select_n.32, f32[512,768]{1,0:T(8,128)S(1)} %get-tuple-element.85, f32[512,768]{1,0:T(8,128)S(1)} %get-tuple-element.97, bf16[256,2048]{1,0:T(8,128)(2,1)S(1)} %get-tuple-element.81, ...), kind=kOutput, calls=%fused_computation.33 | convolution fusion | flops 813760512 | bytes 9177092 | tf_op jit(solution)/shard_map/dot_general | solution.py:55
  178.7 8.1 %collective-permute-done.23 = bf16[64,2048]{1,0:T(8,128)(2,1)S(1)} collective-permute-done((bf16[64,2048]{1,0:T(8,128)(2,1)}, bf16[64,2048]{1,0:T(8,128)(2,1)S(1)}, u32[]{:S(2)}, u32[]{:S(2)}) %collective-permute-start.23) | collective-permute-done | bytes 262176 | tf_op jit(solution)/shard_map/ppermute | solution.py:261
  (143 shorter events, 62.9 us)
Async XLA Ops:
  3.6 17.6 %collective-permute-start = (bf16[64,4224]{1,0:T(8,128)(2,1)}, bf16[64,4224]{1,0:T(8,128)(2,1)}, u32[]{:S(2)}, u32[]{:S(2)}) collective-permute-start(bf16[64,4224]{1,0:T(8,128)(2,1)} %concatenate.24.refs_0_), channel_id=1, source_target_pairs={{0,8},{2,10},{4,12},{6,14},{8,16},{10,18},{12,20},{14,22},{16,24},... | collective-permute-start | bytes 1622024 | tf_op jit(solution)/shard_map/ppermute | solution.py:261
  6.7 17.6 %collective-permute-start.4 = (bf16[64,4224]{1,0:T(8,128)(2,1)}, bf16[64,4224]{1,0:T(8,128)(2,1)}, u32[]{:S(2)}, u32[]{:S(2)}) collective-permute-start(bf16[64,4224]{1,0:T(8,128)(2,1)} %concatenate.24.refs_0_), channel_id=1, source_target_pairs={{0,4},{2,6},{4,0},{6,2},{8,12},{10,14},{12,8},{14,10},{16,20},{18,... | collective-permute-start | bytes 1622024 | tf_op jit(solution)/shard_map/ppermute | solution.py:258
  8.2 16.6 %collective-permute-start.5 = (bf16[64,4224]{1,0:T(8,128)(2,1)}, bf16[64,4224]{1,0:T(8,128)(2,1)}, u32[]{:S(2)}, u32[]{:S(2)}) collective-permute-start(bf16[64,4224]{1,0:T(8,128)(2,1)} %concatenate.24.refs_0_), channel_id=1, source_target_pairs={{0,1},{1,0},{2,3},{3,2},{4,5},{5,4},{6,7},{7,6},{8,9},{9,8},{10,11... | collective-permute-start | bytes 1622024 | tf_op jit(solution)/shard_map/ppermute | solution.py:266
  21.3 15.6 %collective-permute-start.3 = (bf16[64,4224]{1,0:T(8,128)(2,1)}, bf16[64,4224]{1,0:T(8,128)(2,1)}, u32[]{:S(2)}, u32[]{:S(2)}) collective-permute-start(bf16[64,4224]{1,0:T(8,128)(2,1)} %collective-permute-done.refs_1_), channel_id=1, source_target_pairs={{0,8},{2,10},{4,12},{6,14},{8,16},{10,18},{12,20},{14,22},{16,24},... | collective-permute-start | bytes 1622024 | tf_op jit(solution)/shard_map/ppermute | solution.py:261
  21.3 27.4 %collective-permute-start.9 = (bf16[64,4224]{1,0:T(8,128)(2,1)}, bf16[64,4224]{1,0:T(8,128)(2,1)}, u32[]{:S(2)}, u32[]{:S(2)}) collective-permute-start(bf16[64,4224]{1,0:T(8,128)(2,1)} %collective-permute-done.refs_1_), channel_id=1, source_target_pairs={{0,1},{1,0},{2,3},{3,2},{4,5},{5,4},{6,7},{7,6},{8,9},{9,8},{10,11... | collective-permute-start | bytes 1622024 | tf_op jit(solution)/shard_map/ppermute | solution.py:266
  22.8 25.1 %collective-permute-start.1 = (bf16[64,4224]{1,0:T(8,128)(2,1)}, bf16[64,4224]{1,0:T(8,128)(2,1)}, u32[]{:S(2)}, u32[]{:S(2)}) collective-permute-start(bf16[64,4224]{1,0:T(8,128)(2,1)} %collective-permute-done.refs_1_), channel_id=1, source_target_pairs={{0,4},{2,6},{4,0},{6,2},{8,12},{10,14},{12,8},{14,10},{16,20},{18,... | collective-permute-start | bytes 1622024 | tf_op jit(solution)/shard_map/ppermute | solution.py:258
  24.3 22.3 %collective-permute-start.8 = (bf16[64,4224]{1,0:T(8,128)(2,1)}, bf16[64,4224]{1,0:T(8,128)(2,1)}, u32[]{:S(2)}, u32[]{:S(2)}) collective-permute-start(bf16[64,4224]{1,0:T(8,128)(2,1)} %collective-permute-done.4.refs_4_), channel_id=1, source_target_pairs={{0,1},{1,0},{2,3},{3,2},{4,5},{5,4},{6,7},{7,6},{8,9},{9,8},{10,11... | collective-permute-start | bytes 1622024 | tf_op jit(solution)/shard_map/ppermute | solution.py:266
  36.9 14.7 %collective-permute-start.7 = (bf16[64,4224]{1,0:T(8,128)(2,1)}, bf16[64,4224]{1,0:T(8,128)(2,1)}, u32[]{:S(2)}, u32[]{:S(2)}) collective-permute-start(bf16[64,4224]{1,0:T(8,128)(2,1)} %collective-permute-done.3.refs_2_), channel_id=1, source_target_pairs={{0,8},{2,10},{4,12},{6,14},{8,16},{10,18},{12,20},{14,22},{16,24},... | collective-permute-start | bytes 1622024 | tf_op jit(solution)/shard_map/ppermute | solution.py:261
  36.9 17.6 %collective-permute-start.10 = (bf16[64,4224]{1,0:T(8,128)(2,1)}, bf16[64,4224]{1,0:T(8,128)(2,1)S(1)}, u32[]{:S(2)}, u32[]{:S(2)}) collective-permute-start(bf16[64,4224]{1,0:T(8,128)(2,1)} %collective-permute-done.3.refs_2_), channel_id=1, source_target_pairs={{0,4},{2,6},{4,0},{6,2},{8,12},{10,14},{12,8},{14,10},{16,20},{18,... | collective-permute-start | bytes 1622024 | tf_op jit(solution)/shard_map/ppermute | solution.py:258
  46.6 17.7 %collective-permute-start.6 = (bf16[64,4224]{1,0:T(8,128)(2,1)}, bf16[64,4224]{1,0:T(8,128)(2,1)}, u32[]{:S(2)}, u32[]{:S(2)}) collective-permute-start(bf16[64,4224]{1,0:T(8,128)(2,1)} %collective-permute-done.3.refs_2_), channel_id=1, source_target_pairs={{0,1},{1,0},{2,3},{3,2},{4,5},{5,4},{6,7},{7,6},{8,9},{9,8},{10,11... | collective-permute-start | bytes 1622024 | tf_op jit(solution)/shard_map/ppermute | solution.py:266
  47.9 23.2 %collective-permute-start.2 = (bf16[64,4224]{1,0:T(8,128)(2,1)}, bf16[64,4224]{1,0:T(8,128)(2,1)}, u32[]{:S(2)}, u32[]{:S(2)}) collective-permute-start(bf16[64,4224]{1,0:T(8,128)(2,1)} %collective-permute-done.1.refs_5_), channel_id=1, source_target_pairs={{0,1},{1,0},{2,3},{3,2},{4,5},{5,4},{6,7},{7,6},{8,9},{9,8},{10,11... | collective-permute-start | bytes 1622024 | tf_op jit(solution)/shard_map/ppermute | solution.py:266
  51.5 11.8 %collective-permute-start.11 = (bf16[64,4224]{1,0:T(8,128)(2,1)}, bf16[64,4224]{1,0:T(8,128)(2,1)S(1)}, u32[]{:S(2)}, u32[]{:S(2)}) collective-permute-start(bf16[64,4224]{1,0:T(8,128)(2,1)} %collective-permute-done.7.refs_3_), channel_id=1, source_target_pairs={{0,4},{2,6},{4,0},{6,2},{8,12},{10,14},{12,8},{14,10},{16,20},{18,... | collective-permute-start | bytes 1622024 | tf_op jit(solution)/shard_map/ppermute | solution.py:258
  90.4 15.1 %collective-permute-start.14 = (bf16[128,2048]{1,0:T(8,128)(2,1)}, bf16[128,2048]{1,0:T(8,128)(2,1)}, u32[]{:S(2)}, u32[]{:S(2)}) collective-permute-start(bf16[128,2048]{1,0:T(8,128)(2,1)} %slice.81), channel_id=1, source_target_pairs={{0,4},{2,6},{4,0},{6,2},{8,12},{10,14},{12,8},{14,10},{16,20},{18,... | collective-permute-start | bytes 1572872 | tf_op jit(solution)/shard_map/ppermute | solution.py:258
  98.2 19.7 %collective-permute-start.15 = (bf16[256,2048]{1,0:T(8,128)(2,1)}, bf16[256,2048]{1,0:T(8,128)(2,1)}, u32[]{:S(2)}, u32[]{:S(2)}) collective-permute-start(bf16[256,2048]{1,0:T(8,128)(2,1)} %fusion.43), channel_id=1, source_target_pairs={{0,2},{2,0},{4,6},{6,4},{8,10},{10,8},{12,14},{14,12},{16,18},{18,... | collective-permute-start | bytes 3145736 | tf_op jit(solution)/shard_map/ppermute | solution.py:255
  98.3 52.1 %collective-permute-start.25 = (bf16[192,4224]{1,0:T(8,128)(2,1)}, bf16[192,4224]{1,0:T(8,128)(2,1)S(1)}, u32[]{:S(2)}, u32[]{:S(2)}) collective-permute-start(bf16[192,4224]{1,0:T(8,128)(2,1)} %constant_dynamic-update-slice_fusion), channel_id=1, source_target_pairs={{0,1},{1,0},{2,3},{3,2},{4,5},{5,4},{6,7},{7,6},{8,9},{9,8},{10,11... | collective-permute-start | bytes 4866056 | tf_op jit(solution)/shard_map/ppermute | solution.py:266
  100.9 15.2 %collective-permute-start.16 = (bf16[128,2048]{1,0:T(8,128)(2,1)S(1)}, bf16[128,2048]{1,0:T(8,128)(2,1)S(1)}, u32[]{:S(2)}, u32[]{:S(2)}) collective-permute-start(bf16[128,2048]{1,0:T(8,128)(2,1)S(1)} %slice.84), channel_id=1, source_target_pairs={{0,4},{2,6},{4,0},{6,2},{8,12},{10,14},{12,8},{14,10},{16,20},{18,... | collective-permute-start | bytes 1572872 | tf_op jit(solution)/shard_map/ppermute | solution.py:258
  116.9 30.2 %collective-permute-start.20 = (bf16[128,2048]{1,0:T(8,128)(2,1)}, bf16[128,2048]{1,0:T(8,128)(2,1)}, u32[]{:S(2)}, u32[]{:S(2)}) collective-permute-start(bf16[128,2048]{1,0:T(8,128)(2,1)} %slice.85), channel_id=1, source_target_pairs={{0,4},{2,6},{4,0},{6,2},{8,12},{10,14},{12,8},{14,10},{16,20},{18,... | collective-permute-start | bytes 1572872 | tf_op jit(solution)/shard_map/ppermute | solution.py:258
  121.1 10.9 %collective-permute-start.17 = (bf16[64,2048]{1,0:T(8,128)(2,1)}, bf16[64,2048]{1,0:T(8,128)(2,1)S(1)}, u32[]{:S(2)}, u32[]{:S(2)}) collective-permute-start(bf16[64,2048]{1,0:T(8,128)(2,1)} %get-tuple-element.57), channel_id=1, source_target_pairs={{0,24},{2,26},{4,28},{6,30},{8,0},{10,2},{12,4},{14,6},{16,8},{18,... | collective-permute-start | bytes 786440 | tf_op jit(solution)/shard_map/ppermute | solution.py:261
  124.4 21.3 %collective-permute-start.18 = (bf16[64,2048]{1,0:T(8,128)(2,1)}, bf16[64,2048]{1,0:T(8,128)(2,1)S(1)}, u32[]{:S(2)}, u32[]{:S(2)}) collective-permute-start(bf16[64,2048]{1,0:T(8,128)(2,1)} %get-tuple-element.58), channel_id=1, source_target_pairs={{0,16},{2,18},{4,20},{6,22},{8,24},{10,26},{12,28},{14,30},{16,0},... | collective-permute-start | bytes 786440 | tf_op jit(solution)/shard_map/ppermute | solution.py:261
  125.5 21.6 %collective-permute-start.21 = (bf16[128,2048]{1,0:T(8,128)(2,1)S(1)}, bf16[128,2048]{1,0:T(8,128)(2,1)}, u32[]{:S(2)}, u32[]{:S(2)}) collective-permute-start(bf16[128,2048]{1,0:T(8,128)(2,1)S(1)} %slice.86), channel_id=1, source_target_pairs={{0,4},{2,6},{4,0},{6,2},{8,12},{10,14},{12,8},{14,10},{16,20},{18,... | collective-permute-start | bytes 1572872 | tf_op jit(solution)/shard_map/ppermute | solution.py:258
  132.0 14.3 %collective-permute-start.19 = (bf16[64,2048]{1,0:T(8,128)(2,1)S(1)}, bf16[64,2048]{1,0:T(8,128)(2,1)S(1)}, u32[]{:S(2)}, u32[]{:S(2)}) collective-permute-start(bf16[64,2048]{1,0:T(8,128)(2,1)S(1)} %copy-done.31), channel_id=1, source_target_pairs={{0,8},{2,10},{4,12},{6,14},{8,16},{10,18},{12,20},{14,22},{16,24},... | collective-permute-start | bytes 786440 | tf_op jit(solution)/shard_map/ppermute | solution.py:261
  159.2 19.4 %collective-permute-start.22 = (bf16[64,2048]{1,0:T(8,128)(2,1)}, bf16[64,2048]{1,0:T(8,128)(2,1)S(1)}, u32[]{:S(2)}, u32[]{:S(2)}) collective-permute-start(bf16[64,2048]{1,0:T(8,128)(2,1)} %get-tuple-element.66), channel_id=1, source_target_pairs={{0,24},{2,26},{4,28},{6,30},{8,0},{10,2},{12,4},{14,6},{16,8},{18,... | collective-permute-start | bytes 786440 | tf_op jit(solution)/shard_map/ppermute | solution.py:261
  159.2 27.6 %collective-permute-start.23 = (bf16[64,2048]{1,0:T(8,128)(2,1)}, bf16[64,2048]{1,0:T(8,128)(2,1)S(1)}, u32[]{:S(2)}, u32[]{:S(2)}) collective-permute-start(bf16[64,2048]{1,0:T(8,128)(2,1)} %get-tuple-element.67), channel_id=1, source_target_pairs={{0,16},{2,18},{4,20},{6,22},{8,24},{10,26},{12,28},{14,30},{16,0},... | collective-permute-start | bytes 786440 | tf_op jit(solution)/shard_map/ppermute | solution.py:261
  163.1 23.7 %collective-permute-start.24 = (bf16[64,2048]{1,0:T(8,128)(2,1)}, bf16[64,2048]{1,0:T(8,128)(2,1)S(1)}, u32[]{:S(2)}, u32[]{:S(2)}) collective-permute-start(bf16[64,2048]{1,0:T(8,128)(2,1)} %get-tuple-element.68), channel_id=1, source_target_pairs={{0,8},{2,10},{4,12},{6,14},{8,16},{10,18},{12,20},{14,22},{16,24},... | collective-permute-start | bytes 786440 | tf_op jit(solution)/shard_map/ppermute | solution.py:261
  (35 other events, 226.4 us)

commit v13 on v12

--- a/solution.py
+++ b/solution.py
@@ -201,32 +201,37 @@
     )(expert, *arrays)
 
 
-def spread(place, mine, theirs, far_mine, far_theirs):
+def spread(line, place, mine, theirs, far_mine, far_theirs):
     length, slots_of = place.shape
     room, features = far_mine.shape
     size = length // TOGETHER
     parts = (mine, theirs, far_mine, far_theirs)
 
-    def body(place_ref, *refs):
-        outs = refs[len(parts) :]
+    def body(line_ref, place_ref, *refs):
+        out_ref = refs[-1]
         for at in range(0, features, 512):
             cols = slice(at, at + 512)
             rows = jnp.concatenate([ref[:, cols] for ref in refs[: len(parts)]], axis=0)
             dense = dot(place_ref[...], rows).astype(BF)
-            for i, out in enumerate(outs):
-                out[:, cols] = dense[i * size : (i + 1) * size]
-
-    out = jax.ShapeDtypeStruct((size, features), BF)
+            for i in range(TOGETHER):
+                home = (line_ref[0] + TOGETHER - i) % TOGETHER
+                out_ref[home, :, cols] = dense[i * size : (i + 1) * size]
+
+    out = jax.ShapeDtypeStruct((TOGETHER, size, features), BF)
+    part_spec = pl.BlockSpec((room, features), lambda i, e: (0, 0))
     return pl.pallas_call(
         body,
-        grid=(1,),
-        in_specs=[whole(place)] + [pl.BlockSpec((room, features), lambda i: (0, 0))] * len(parts),
-        out_specs=[whole(out)] * TOGETHER,
-        out_shape=(out,) * TOGETHER,
+        grid_spec=pltpu.PrefetchScalarGridSpec(
+            num_scalar_prefetch=1,
+            grid=(1,),
+            in_specs=[whole(place)] + [part_spec] * len(parts),
+            out_specs=whole(out),
+        ),
+        out_shape=out,
         compiler_params=params(1),
         cost_estimate=SMALL,
         name="spread",
-    )(place, *parts)
+    )(line, place, *parts)
 
 
 def split3(value):
@@ -276,7 +281,7 @@
     near.append(after(to_z(near[1], 1), far[0], relay[0]))
     far.append(to_x(near[2]))
     relay += [to_y(far[0]), to_y(near[1]), to_y(far[1]), to_y(near[2])]
-    near.append(after(to_z(near[2], 1), relay[1], relay[2]))
+    near.append(to_z(near[2], 1))
     far.append(to_x(near[3]))
     joined = jnp.concatenate([near[3], far[2], far[3]], axis=0)
     last = to_y(joined)
@@ -308,39 +313,40 @@
         mine = rows_of(slice(0, 2 * half), *before_mine)
         return mine, theirs, to_x(after(mine[half:], *before_far)), to_x(theirs[half:])
 
+    lines = [list(range(first, experts, 4)) for first in range(4)]
+
     def home(place, parts):
-        own, *others = spread(place, *parts)
-        return [own] + [to_z(a, -step) for step, a in enumerate(others, 1)]
+        dense = spread(expert // 4, place, *parts)
+        return dense, lax.all_to_all(dense, "expert", 0, 0, axis_index_groups=lines, tiled=True)
 
     def total(chunks):
-        return sum(a.astype(F32) for a in chunks).astype(BF)
+        return jnp.sum(chunks.astype(F32), axis=0).astype(BF)
 
     def grads(x, act, cot, d_gate, d_up):
         x = lax.dynamic_slice_in_dim(x, replica * (features // 2), features // 2, 1)
         act = lax.dynamic_slice_in_dim(act, replica * (hidden // 2), hidden // 2, 1)
         return outer_sum(x, d_gate), outer_sum(x, d_up), outer_sum(act, cot)
 
-    packed = plan(own_pieces, *relay[3:5], joined)
+    packed = plan(own_pieces, *relay[1:4], joined)
     place = packed[-1]
     own_x, weight, pre_gate, pre_up, act, cot = enter(packed)
     parts = leave(lambda rows: (dot(act[rows], w_down) * weight[rows]).astype(BF))
-    cot = after(cot, parts[0], parts[1])
+    cot = after(cot, parts[0], parts[1], relay[4])
     d_gate, d_up = hidden_grads(cot, pre_gate, pre_up, w_down)
 
     def token_grads(rows, *earlier):
         return input_rows(*after((d_gate[rows], d_up[rows]), *earlier), w_gate, w_up)
 
     grad_parts = leave(token_grads, parts[2:3], parts[3:4])
-    chunks = home(after(place, grad_parts[0], grad_parts[1]), parts)
-    own_grads = after((cot, d_gate, d_up), chunks[0])
-    own = grads(own_x, act, *own_grads)
-    grad_chunks = home(after(place, *own, *chunks[1:]), grad_parts)
-
-    packed = plan(other_pieces, grad_chunks[0])
+    dense, chunks = home(after(place, grad_parts[0], grad_parts[1]), parts)
+    own = grads(own_x, act, *after((cot, d_gate, d_up), dense))
+    dense, grad_chunks = home(after(place, *own), grad_parts)
+
+    packed = plan(other_pieces, dense)
     x, weight, pre_gate, pre_up, act, cot = enter(packed)
     d_gate, d_up = hidden_grads(cot, pre_gate, pre_up, w_down)
-    other = grads(x, act, cot, d_gate, after(d_up, grad_chunks[1]))
-    grad_chunks = after(grad_chunks, other[0])
+    other = grads(x, act, cot, d_gate, d_up)
+    chunks, grad_chunks = after(chunks, other[0]), after(grad_chunks, other[0])
     grad_gate, grad_up, grad_down = ((a + b).astype(BF)[None] for a, b in zip(own, other))
     return (total(chunks), total(grad_chunks), grad_gate, grad_up, grad_down)
 

time: 190 us -> 230 us (1.21)
  waiting for transfers between devices: 72.3 us -> 104 us
  matrix products: 34.5 us -> 46.3 us
  starting transfers between devices: 37.8 us -> 30.2 us
  local copies, waits for them, and re-layouts: 18.9 us -> 21.4 us
    all_to_all x0 -> x2, waiting for transfers between devices: none -> 20.2 us  [home(): lax.all_to_all(dense, 'expert', 0, 0, axis_index_groups=lines, tiled=True)]
    ppermute x9 -> x3, starting transfers between devices: 21.3 us -> 3.03 us  [to_z(): lax.ppermute(rows, 'expert', [(i, (i + 4 * step) % experts) for i in rang...]
    all_to_all x0 -> x2, starting transfers between devices: none -> 9.1 us  [home(): lax.all_to_all(dense, 'expert', 0, 0, axis_index_groups=lines, tiled=True)]
    dot_general x6, matrix products: 13.7 us -> 22.6 us  [outer_sum(): lax.dot_general(left, right, (((0,), (0,)), ((), ())), preferred_element_...]
    ppermute x8, waiting for transfers between devices: 17.4 us -> 25 us  [to_x(): return lax.ppermute(rows, 'expert', [(i, i ^ 2) for i in range(experts)])]
    reduce_sum x0 -> x2, other arithmetic: none -> 4.32 us  [total(): return jnp.sum(chunks.astype(F32), axis=0).astype(BF)]
    ppermute x6, waiting for transfers between devices: 15.3 us -> 18.6 us  [to_y(): return lax.ppermute(rows, 'replica', [(0, 1), (1, 0)])]
    convert_element_type x2 -> x0, other arithmetic: 2.78 us -> none  [total(): return sum((a.astype(F32) for a in chunks)).astype(BF)]
  transfers between devices with their start and end apart: 27 -> 23, of which waited for: 11 -> 11; matrix products, arithmetic and copies ran while one was open for 22% -> 25% of each run, Pallas kernels for 3% -> 3%
where the time goes in v13:
time: 230 us; the launch traced here: 229 us
  waiting for transfers between devices  104 us (45%)
  matrix products  46.3 us (20%)
  starting transfers between devices  30.2 us (13%)
  local copies, waits for them, and re-layouts  21.4 us (9%)
  Pallas kernels  18 us (8%)
  other arithmetic  8.13 us (4%)
    ppermute x3, waiting for transfers between devices, to_z(): lax.ppermute(rows, 'expert', [(i, (i + 4 * step) % experts) for i in rang...  35.5 us
    ppermute x8, waiting for transfers between devices, to_x(): return lax.ppermute(rows, 'expert', [(i, i ^ 2) for i in range(experts)])  25 us
    dot_general x6, matrix products, outer_sum(): lax.dot_general(left, right, (((0,), (0,)), ((), ())), preferred_element_...  22.6 us
    all_to_all x2, waiting for transfers between devices, home(): lax.all_to_all(dense, 'expert', 0, 0, axis_index_groups=lines, tiled=True)  20.2 us
    ppermute x6, waiting for transfers between devices, to_y(): return lax.ppermute(rows, 'replica', [(0, 1), (1, 0)])  18.6 us
    dot_general x6, matrix products, dot(): return jnp.dot(left, right, preferred_element_type=F32)  12.1 us
    pallas_call x2, Pallas kernels, plan_and_pack(): pl.pallas_call(body, grid_spec=pltpu.PrefetchScalarGridSpec(num_scalar_pr...  11.3 us
    ppermute x8, starting transfers between devices, to_x(): return lax.ppermute(rows, 'expert', [(i, i ^ 2) for i in range(experts)])  10.6 us
  transfers between devices with their start and end apart: 23, of which 11 were waited for; matrix products, arithmetic and copies ran while one was open for 25% of the time, Pallas kernels for 3%

profile of v13, /device:TPU:0, one launch (start us, length us, event | category | flops | bytes accessed | tf_op | source)
XLA Modules:
  0.0 228.8 jit_solution(14829087924804054407)
XLA Ops:
  3.6 3.0 %collective-permute-start.2 = (bf16[64,4224]{1,0:T(8,128)(2,1)}, bf16[64,4224]{1,0:T(8,128)(2,1)}, u32[]{:S(2)}, u32[]{:S(2)}) collective-permute-start(bf16[64,4224]{1,0:T(8,128)(2,1)} %concatenate.24.refs_0_), channel_id=1, source_target_pairs={{0,8},{2,10},{4,12},{6,14},{8,16},{10,18},{12,20},{14,22},{16,24},... | collective-permute-start | bytes 1622024 | tf_op jit(solution)/shard_map/ppermute | solution.py:266
  9.7 11.6 %collective-permute-done.2.refs_1_ = bf16[64,4224]{1,0:T(8,128)(2,1)} collective-permute-done((bf16[64,4224]{1,0:T(8,128)(2,1)}, bf16[64,4224]{1,0:T(8,128)(2,1)}, u32[]{:S(2)}, u32[]{:S(2)}) %collective-permute-start.2) | collective-permute-done | bytes 540704 | tf_op jit(solution)/shard_map/ppermute | solution.py:266
  22.8 14.1 %collective-permute-done.6.refs_2_ = bf16[64,4224]{1,0:T(8,128)(2,1)} collective-permute-done((bf16[64,4224]{1,0:T(8,128)(2,1)}, bf16[64,4224]{1,0:T(8,128)(2,1)}, u32[]{:S(2)}, u32[]{:S(2)}) %collective-permute-start.6) | collective-permute-done | bytes 540704 | tf_op jit(solution)/shard_map/ppermute | solution.py:266
  41.7 9.9 %collective-permute-done.8.refs_3_ = bf16[64,4224]{1,0:T(8,128)(2,1)} collective-permute-done((bf16[64,4224]{1,0:T(8,128)(2,1)}, bf16[64,4224]{1,0:T(8,128)(2,1)}, u32[]{:S(2)}, u32[]{:S(2)}) %collective-permute-start.8) | collective-permute-done | bytes 540704 | tf_op jit(solution)/shard_map/ppermute | solution.py:266
  55.4 8.0 %collective-permute-done.10.refs_7_ = bf16[64,4224]{1,0:T(8,128)(2,1)S(1)} collective-permute-done((bf16[64,4224]{1,0:T(8,128)(2,1)}, bf16[64,4224]{1,0:T(8,128)(2,1)S(1)}, u32[]{:S(2)}, u32[]{:S(2)}) %collective-permute-start.10) | collective-permute-done | bytes 540704 | tf_op jit(solution)/shard_map/ppermute | solution.py:263
  64.2 8.7 %collective-permute-done.5.refs_5_ = bf16[64,4224]{1,0:T(8,128)(2,1)} collective-permute-done((bf16[64,4224]{1,0:T(8,128)(2,1)}, bf16[64,4224]{1,0:T(8,128)(2,1)}, u32[]{:S(2)}, u32[]{:S(2)}) %collective-permute-start.5) | collective-permute-done | bytes 540704 | tf_op jit(solution)/shard_map/ppermute | solution.py:271
  72.9 5.7 %plan_and_pack.2 = (bf16[256,2048]{1,0:T(8,128)(2,1)}, bf16[256,2048]{1,0:T(8,128)(2,1)}, bf16[256,128]{1,0:T(8,128)(2,1)}, bf16[256,4224]{1,0:T(8,128)(2,1)}, bf16[256,512]{1,0:T(8,128)(2,1)}) custom-call(s32[1]{0:T(128)} %bitcast.expert_ref, bf16[64,4224]{1,0:T(8,128)(2,1)} %concatenate.24.refs_0_, bf16[64,4224]{1,0:T(8,128)(2,1)} %collective-permute-done.2.refs_1_, ...), custom_call_target="tpu_custom_call" | custom-call | flops 1 | bytes 1 | tf_op jit(solution)/shard_map/plan_and_pack/pallas_call | solution.py:185
  78.7 4.4 %collective-permute-done.11 = bf16[256,4224]{1,0:T(8,128)(2,1)S(1)} collective-permute-done((bf16[256,4224]{1,0:T(8,128)(2,1)}, bf16[256,4224]{1,0:T(8,128)(2,1)S(1)}, u32[]{:S(2)}, u32[]{:S(2)}) %collective-permute-start.11) | collective-permute-done | bytes 2162720 | tf_op jit(solution)/shard_map/ppermute | solution.py:260
  96.4 9.9 %collective-permute-done.13.refs_2_ = bf16[64,4224]{1,0:T(8,128)(2,1)S(1)} collective-permute-done((bf16[64,4224]{1,0:T(8,128)(2,1)}, bf16[64,4224]{1,0:T(8,128)(2,1)S(1)}, u32[]{:S(2)}, u32[]{:S(2)}) %collective-permute-start.13) | collective-permute-done | bytes 540704 | tf_op jit(solution)/shard_map/ppermute | solution.py:271
  121.3 8.4 %collective-permute-done.16.refs_3_ = bf16[128,2048]{1,0:T(8,128)(2,1)S(1)} collective-permute-done((bf16[128,2048]{1,0:T(8,128)(2,1)S(1)}, bf16[128,2048]{1,0:T(8,128)(2,1)S(1)}, u32[]{:S(2)}, u32[]{:S(2)}) %collective-permute-start.16) | collective-permute-done | bytes 524320 | tf_op jit(solution)/shard_map/ppermute | solution.py:263
  131.2 3.4 %spread.2 = bf16[4,64,2048]{2,1,0:T(8,128)(2,1)} custom-call(s32[1]{0:T(128)S(6)} %select_n.34.line_ref, bf16[256,512]{1,0:T(8,128)(2,1)} %get-tuple-element.46.place_ref, bf16[256,2048]{1,0:T(8,128)(2,1)} %copy-done.10, bf16[256,2048]{1,0:T(8,128)(2,1)} %collective-permute-done.12.refs_1_, bf16[128,2048]{1,0:T(8,128)(2,1)} %collective-permute-done.14.refs_2_, ...), custom_call_target="tpu_custom_call" | custom-call | flops 1 | bytes 1 | tf_op jit(solution)/shard_map/spread/pallas_call | solution.py:222
  136.6 3.7 %fusion.71 = f32[1024,768]{1,0:T(8,128)} fusion(bf16[512,768]{1,0:T(8,128)(2,1)S(1)} %copy-done.23, s32[]{:T(128)S(6)} %select_n.38, bf16[256,2048]{1,0:T(8,128)(2,1)} %get-tuple-element.36, bf16[256,2048]{1,0:T(8,128)(2,1)S(1)} %copy-done.16), kind=kOutput, calls=%fused_computation.85 | convolution fusion | flops 807403520 | bytes 6029316 | tf_op jit(solution)/shard_map/dot_general | solution.py:55
  145.7 8.7 %collective-permute-done.18.refs_3_ = bf16[128,2048]{1,0:T(8,128)(2,1)S(1)} collective-permute-done((bf16[128,2048]{1,0:T(8,128)(2,1)S(1)}, bf16[128,2048]{1,0:T(8,128)(2,1)S(1)}, u32[]{:S(2)}, u32[]{:S(2)}) %collective-permute-start.18) | collective-permute-done | bytes 524320 | tf_op jit(solution)/shard_map/ppermute | solution.py:263
  155.2 3.3 %spread.3 = bf16[4,64,2048]{2,1,0:T(8,128)(2,1)} custom-call(s32[1]{0:T(128)S(6)} %select_n.34.line_ref, bf16[256,512]{1,0:T(8,128)(2,1)} %get-tuple-element.46.place_ref, bf16[256,2048]{1,0:T(8,128)(2,1)} %copy-done.6, bf16[256,2048]{1,0:T(8,128)(2,1)} %collective-permute-done.15.refs_1_, bf16[128,2048]{1,0:T(8,128)(2,1)} %copy-done.25, ...), custom_call_target="tpu_custom_call" | custom-call | flops 1 | bytes 1 | tf_op jit(solution)/shard_map/spread/pallas_call | solution.py:222
  159.7 5.7 %plan_and_pack.3 = (bf16[256,2048]{1,0:T(8,128)(2,1)}, bf16[256,2048]{1,0:T(8,128)(2,1)}, bf16[256,128]{1,0:T(8,128)(2,1)}, bf16[256,4224]{1,0:T(8,128)(2,1)}, bf16[256,512]{1,0:T(8,128)(2,1)}) custom-call(s32[1]{0:T(128)} %bitcast.expert_ref, bf16[64,4224]{1,0:T(8,128)(2,1)} %collective-permute-done.7.refs_0_, ...), custom_call_target="tpu_custom_call" | custom-call | flops 1 | bytes 1 | tf_op jit(solution)/shard_map/plan_and_pack/pallas_call | solution.py:185
  165.5 4.8 %all-to-all-start.1 = ((bf16[4,64,2048]{2,1,0:T(8,128)(2,1)}), bf16[4,64,2048]{2,1,0:T(8,128)(2,1)}, u32[]{:S(2)}, u32[]{:S(2)}) async-start(bf16[4,64,2048]{2,1,0:T(8,128)(2,1)} %spread.3), calls=%async_computation.1 | async-start | bytes 2097152 | tf_op jit(solution)/shard_map/all_to_all | solution.py:320
  173.1 2.9 %fusion.8 = f32[512,768]{1,0:T(8,128)} fusion(bf16[1,2048,768]{2,1,0:T(8,128)(2,1)S(1)} %copy-done, bf16[256,2048]{1,0:T(8,128)(2,1)S(1)} %get-tuple-element.58, bf16[256,2048]{1,0:T(8,128)(2,1)S(1)} %copy-done.36), kind=kOutput, calls=%fused_computation.10 | convolution fusion | flops 1614807040 | bytes 6815744 | tf_op jit(solution)/shard_map/dot_general | solution.py:102
  176.4 3.0 %fusion = f32[512,768]{1,0:T(8,128)} fusion(bf16[1,768,2048]{2,1,0:T(8,128)(2,1)S(1)} %copy-done.33, bf16[256,2048]{1,0:T(8,128)(2,1)S(1)} %get-tuple-element.57, bf16[256,2048]{1,0:T(8,128)(2,1)S(1)} %copy-done.14, f32[512]{0:T(512)S(1)} %select_reduce_fusion), kind=kOutput, calls=%fused_computation.2 | convolution fusion | flops 1616904192 | bytes 6817792 | tf_op jit(solution)/shard_map/dot_general | solution.py:41
  179.4 3.5 %add_divide_fusion = (f32[512,768]{1,0:T(8,128)}, f32[512,768]{1,0:T(8,128)}) fusion(bf16[1,2048,768]{2,1,0:T(8,128)(2,1)S(1)} %copy-done.3, bf16[256,2048]{1,0:T(8,128)(2,1)S(1)} %get-tuple-element.58, bf16[256,2048]{1,0:T(8,128)(2,1)S(1)} %copy-done.36), kind=kOutput, calls=%fused_computation.47 | convolution fusion | flops 1615986688 | bytes 8388608 | tf_op jit(solution)/shard_map/dot_general | solution.py:102
  182.9 13.8 %all-to-all-done.1 = bf16[4,64,2048]{2,1,0:T(8,128)(2,1)} async-done(((bf16[4,64,2048]{2,1,0:T(8,128)(2,1)}), bf16[4,64,2048]{2,1,0:T(8,128)(2,1)}, u32[]{:S(2)}, u32[]{:S(2)}) %all-to-all-start.1) | async-done | bytes 1048608 | tf_op jit(solution)/shard_map/all_to_all | solution.py:320
  196.8 4.3 %all-to-all-start = ((bf16[4,64,2048]{2,1,0:T(8,128)(2,1)}), bf16[4,64,2048]{2,1,0:T(8,128)(2,1)}, u32[]{:S(2)}, u32[]{:S(2)}) async-start(bf16[4,64,2048]{2,1,0:T(8,128)(2,1)} %spread.2), calls=%async_computation | async-start | bytes 2097152 | tf_op jit(solution)/shard_map/all_to_all | solution.py:320
  201.1 5.6 %fusion.53 = f32[1024,768]{1,0:T(8,128)} fusion(f32[512,768]{1,0:T(8,128)} %get-tuple-element.72, f32[512,768]{1,0:T(8,128)} %fusion, f32[512,768]{1,0:T(8,128)} %fusion.8, s32[]{:T(128)S(6)} %select_n.38, bf16[256,2048]{1,0:T(8,128)(2,1)} %get-tuple-element.49, bf16[256,2048]{1,0:T(8,128)(2,1)} %copy-done.18), kind=kOutput, calls=%fused_computation.55 | convolution fusion | flops 811335680 | bytes 9961476 | tf_op jit(solution)/shard_map/dot_general | solution.py:55
  208.9 5.6 %fusion.36 = bf16[1,384,2048]{2,1,0:T(8,128)(2,1)} fusion(f32[384,2048]{1,0:T(8,128)} %fusion.59, f32[512,768]{1,0:T(8,128)} %fusion.8, s32[]{:T(128)S(6)} %select_n.39, f32[512,768]{1,0:T(8,128)} %get-tuple-element.71, f32[512,768]{1,0:T(8,128)} %get-tuple-element.72, bf16[256,2048]{1,0:T(8,128)(2,1)} %copy-done.7, ...), kind=kOutput, calls=%fused_computation.33 | convolution fusion | flops 813760512 | bytes 9177092 | tf_op jit(solution)/shard_map/dot_general | solution.py:55
  220.4 6.3 %all-to-all-done = bf16[4,64,2048]{2,1,0:T(8,128)(2,1)} async-done(((bf16[4,64,2048]{2,1,0:T(8,128)(2,1)}), bf16[4,64,2048]{2,1,0:T(8,128)(2,1)}, u32[]{:S(2)}, u32[]{:S(2)}) %all-to-all-start) | async-done | bytes 1048608 | tf_op jit(solution)/shard_map/all_to_all | solution.py:320
  (151 shorter events, 69.5 us)
Async XLA Ops:
  0.6 87.8 %copy-start = (bf16[1,2048,768]{2,1,0:T(8,128)(2,1)S(1)}, bf16[1,2048,768]{2,1,0:T(8,128)(2,1)}, u32[]{:S(2)}) copy-start(bf16[1,2048,768]{2,1,0:T(8,128)(2,1)} %param.12) | copy-start | bytes 9437188
  3.6 17.6 %collective-permute-start.2 = (bf16[64,4224]{1,0:T(8,128)(2,1)}, bf16[64,4224]{1,0:T(8,128)(2,1)}, u32[]{:S(2)}, u32[]{:S(2)}) collective-permute-start(bf16[64,4224]{1,0:T(8,128)(2,1)} %concatenate.24.refs_0_), channel_id=1, source_target_pairs={{0,8},{2,10},{4,12},{6,14},{8,16},{10,18},{12,20},{14,22},{16,24},... | collective-permute-start | bytes 1622024 | tf_op jit(solution)/shard_map/ppermute | solution.py:266
  6.7 16.1 %collective-permute-start = (bf16[64,4224]{1,0:T(8,128)(2,1)}, bf16[64,4224]{1,0:T(8,128)(2,1)}, u32[]{:S(2)}, u32[]{:S(2)}) collective-permute-start(bf16[64,4224]{1,0:T(8,128)(2,1)} %concatenate.24.refs_0_), channel_id=1, source_target_pairs={{0,4},{2,6},{4,0},{6,2},{8,12},{10,14},{12,8},{14,10},{16,20},{18,... | collective-permute-start | bytes 1622024 | tf_op jit(solution)/shard_map/ppermute | solution.py:263
  8.2 14.6 %collective-permute-start.7 = (bf16[64,4224]{1,0:T(8,128)(2,1)}, bf16[64,4224]{1,0:T(8,128)(2,1)}, u32[]{:S(2)}, u32[]{:S(2)}) collective-permute-start(bf16[64,4224]{1,0:T(8,128)(2,1)} %concatenate.24.refs_0_), channel_id=1, source_target_pairs={{0,1},{1,0},{2,3},{3,2},{4,5},{5,4},{6,7},{7,6},{8,9},{9,8},{10,11... | collective-permute-start | bytes 1622024 | tf_op jit(solution)/shard_map/ppermute | solution.py:271
  21.3 15.6 %collective-permute-start.6 = (bf16[64,4224]{1,0:T(8,128)(2,1)}, bf16[64,4224]{1,0:T(8,128)(2,1)}, u32[]{:S(2)}, u32[]{:S(2)}) collective-permute-start(bf16[64,4224]{1,0:T(8,128)(2,1)} %collective-permute-done.2.refs_1_), channel_id=1, source_target_pairs={{0,8},{2,10},{4,12},{6,14},{8,16},{10,18},{12,20},{14,22},{16,24},... | collective-permute-start | bytes 1622024 | tf_op jit(solution)/shard_map/ppermute | solution.py:266
  21.3 18.9 %collective-permute-start.4 = (bf16[64,4224]{1,0:T(8,128)(2,1)}, bf16[64,4224]{1,0:T(8,128)(2,1)}, u32[]{:S(2)}, u32[]{:S(2)}) collective-permute-start(bf16[64,4224]{1,0:T(8,128)(2,1)} %collective-permute-done.2.refs_1_), channel_id=1, source_target_pairs={{0,4},{2,6},{4,0},{6,2},{8,12},{10,14},{12,8},{14,10},{16,20},{18,... | collective-permute-start | bytes 1622024 | tf_op jit(solution)/shard_map/ppermute | solution.py:263
  36.9 14.7 %collective-permute-start.8 = (bf16[64,4224]{1,0:T(8,128)(2,1)}, bf16[64,4224]{1,0:T(8,128)(2,1)}, u32[]{:S(2)}, u32[]{:S(2)}) collective-permute-start(bf16[64,4224]{1,0:T(8,128)(2,1)} %collective-permute-done.6.refs_2_), channel_id=1, source_target_pairs={{0,8},{2,10},{4,12},{6,14},{8,16},{10,18},{12,20},{14,22},{16,24},... | collective-permute-start | bytes 1622024 | tf_op jit(solution)/shard_map/ppermute | solution.py:266
  36.9 27.4 %collective-permute-start.3 = (bf16[64,4224]{1,0:T(8,128)(2,1)}, bf16[64,4224]{1,0:T(8,128)(2,1)}, u32[]{:S(2)}, u32[]{:S(2)}) collective-permute-start(bf16[64,4224]{1,0:T(8,128)(2,1)} %collective-permute-done.2.refs_1_), channel_id=1, source_target_pairs={{0,1},{1,0},{2,3},{3,2},{4,5},{5,4},{6,7},{7,6},{8,9},{9,8},{10,11... | collective-permute-start | bytes 1622024 | tf_op jit(solution)/shard_map/ppermute | solution.py:271
  38.1 26.1 %collective-permute-start.1 = (bf16[64,4224]{1,0:T(8,128)(2,1)}, bf16[64,4224]{1,0:T(8,128)(2,1)}, u32[]{:S(2)}, u32[]{:S(2)}) collective-permute-start(bf16[64,4224]{1,0:T(8,128)(2,1)} %collective-permute-done.refs_4_), channel_id=1, source_target_pairs={{0,1},{1,0},{2,3},{3,2},{4,5},{5,4},{6,7},{7,6},{8,9},{9,8},{10,11... | collective-permute-start | bytes 1622024 | tf_op jit(solution)/shard_map/ppermute | solution.py:271
  38.9 15.6 %collective-permute-start.9 = (bf16[64,4224]{1,0:T(8,128)(2,1)}, bf16[64,4224]{1,0:T(8,128)(2,1)S(1)}, u32[]{:S(2)}, u32[]{:S(2)}) collective-permute-start(bf16[64,4224]{1,0:T(8,128)(2,1)} %collective-permute-done.6.refs_2_), channel_id=1, source_target_pairs={{0,4},{2,6},{4,0},{6,2},{8,12},{10,14},{12,8},{14,10},{16,20},{18,... | collective-permute-start | bytes 1622024 | tf_op jit(solution)/shard_map/ppermute | solution.py:263
  40.1 32.8 %collective-permute-start.5 = (bf16[64,4224]{1,0:T(8,128)(2,1)}, bf16[64,4224]{1,0:T(8,128)(2,1)}, u32[]{:S(2)}, u32[]{:S(2)}) collective-permute-start(bf16[64,4224]{1,0:T(8,128)(2,1)} %collective-permute-done.4.refs_5_), channel_id=1, source_target_pairs={{0,1},{1,0},{2,3},{3,2},{4,5},{5,4},{6,7},{7,6},{8,9},{9,8},{10,11... | collective-permute-start | bytes 1622024 | tf_op jit(solution)/shard_map/ppermute | solution.py:271
  51.5 11.8 %collective-permute-start.10 = (bf16[64,4224]{1,0:T(8,128)(2,1)}, bf16[64,4224]{1,0:T(8,128)(2,1)S(1)}, u32[]{:S(2)}, u32[]{:S(2)}) collective-permute-start(bf16[64,4224]{1,0:T(8,128)(2,1)} %collective-permute-done.8.refs_3_), channel_id=1, source_target_pairs={{0,4},{2,6},{4,0},{6,2},{8,12},{10,14},{12,8},{14,10},{16,20},{18,... | collective-permute-start | bytes 1622024 | tf_op jit(solution)/shard_map/ppermute | solution.py:263
  78.6 4.5 %collective-permute-start.11 = (bf16[256,4224]{1,0:T(8,128)(2,1)}, bf16[256,4224]{1,0:T(8,128)(2,1)S(1)}, u32[]{:S(2)}, u32[]{:S(2)}) collective-permute-start(bf16[256,4224]{1,0:T(8,128)(2,1)} %get-tuple-element.34), channel_id=1, source_target_pairs={{0,2},{2,0},{4,6},{6,4},{8,10},{10,8},{12,14},{14,12},{16,18},{18,... | collective-permute-start | bytes 6488072 | tf_op jit(solution)/shard_map/ppermute | solution.py:260
  91.4 15.0 %collective-permute-start.12 = (bf16[256,2048]{1,0:T(8,128)(2,1)S(1)}, bf16[256,2048]{1,0:T(8,128)(2,1)}, u32[]{:S(2)}, u32[]{:S(2)}) collective-permute-start(bf16[256,2048]{1,0:T(8,128)(2,1)S(1)} %fusion.37), channel_id=1, source_target_pairs={{0,2},{2,0},{4,6},{6,4},{8,10},{10,8},{12,14},{14,12},{16,18},{18,... | collective-permute-start | bytes 3145736 | tf_op jit(solution)/shard_map/ppermute | solution.py:260
  91.6 14.8 %collective-permute-start.13 = (bf16[64,4224]{1,0:T(8,128)(2,1)}, bf16[64,4224]{1,0:T(8,128)(2,1)S(1)}, u32[]{:S(2)}, u32[]{:S(2)}) collective-permute-start(bf16[64,4224]{1,0:T(8,128)(2,1)} %collective-permute-done.6.refs_2_), channel_id=1, source_target_pairs={{0,1},{1,0},{2,3},{3,2},{4,5},{5,4},{6,7},{7,6},{8,9},{9,8},{10,11... | collective-permute-start | bytes 1622024 | tf_op jit(solution)/shard_map/ppermute | solution.py:271
  94.5 20.0 %collective-permute-start.14 = (bf16[128,2048]{1,0:T(8,128)(2,1)}, bf16[128,2048]{1,0:T(8,128)(2,1)}, u32[]{:S(2)}, u32[]{:S(2)}) collective-permute-start(bf16[128,2048]{1,0:T(8,128)(2,1)} %slice.81), channel_id=1, source_target_pairs={{0,4},{2,6},{4,0},{6,2},{8,12},{10,14},{12,8},{14,10},{16,20},{18,... | collective-permute-start | bytes 1572872 | tf_op jit(solution)/shard_map/ppermute | solution.py:263
  113.5 17.8 %collective-permute-start.15 = (bf16[256,2048]{1,0:T(8,128)(2,1)}, bf16[256,2048]{1,0:T(8,128)(2,1)}, u32[]{:S(2)}, u32[]{:S(2)}) collective-permute-start(bf16[256,2048]{1,0:T(8,128)(2,1)} %fusion.43), channel_id=1, source_target_pairs={{0,2},{2,0},{4,6},{6,4},{8,10},{10,8},{12,14},{14,12},{16,18},{18,... | collective-permute-start | bytes 3145736 | tf_op jit(solution)/shard_map/ppermute | solution.py:260
  113.5 45.0 %collective-permute-start.19 = (bf16[192,4224]{1,0:T(8,128)(2,1)}, bf16[192,4224]{1,0:T(8,128)(2,1)S(1)}, u32[]{:S(2)}, u32[]{:S(2)}) collective-permute-start(bf16[192,4224]{1,0:T(8,128)(2,1)} %constant_dynamic-update-slice_fusion), channel_id=1, source_target_pairs={{0,1},{1,0},{2,3},{3,2},{4,5},{5,4},{6,7},{7,6},{8,9},{9,8},{10,11... | collective-permute-start | bytes 4866056 | tf_op jit(solution)/shard_map/ppermute | solution.py:271
  115.6 14.1 %collective-permute-start.16 = (bf16[128,2048]{1,0:T(8,128)(2,1)S(1)}, bf16[128,2048]{1,0:T(8,128)(2,1)S(1)}, u32[]{:S(2)}, u32[]{:S(2)}) collective-permute-start(bf16[128,2048]{1,0:T(8,128)(2,1)S(1)} %slice.84), channel_id=1, source_target_pairs={{0,4},{2,6},{4,0},{6,2},{8,12},{10,14},{12,8},{14,10},{16,20},{18,... | collective-permute-start | bytes 1572872 | tf_op jit(solution)/shard_map/ppermute | solution.py:263
  129.7 16.0 %collective-permute-start.17 = (bf16[128,2048]{1,0:T(8,128)(2,1)}, bf16[128,2048]{1,0:T(8,128)(2,1)S(1)}, u32[]{:S(2)}, u32[]{:S(2)}) collective-permute-start(bf16[128,2048]{1,0:T(8,128)(2,1)} %slice.85), channel_id=1, source_target_pairs={{0,4},{2,6},{4,0},{6,2},{8,12},{10,14},{12,8},{14,10},{16,20},{18,... | collective-permute-start | bytes 1572872 | tf_op jit(solution)/shard_map/ppermute | solution.py:263
  135.8 18.6 %collective-permute-start.18 = (bf16[128,2048]{1,0:T(8,128)(2,1)S(1)}, bf16[128,2048]{1,0:T(8,128)(2,1)S(1)}, u32[]{:S(2)}, u32[]{:S(2)}) collective-permute-start(bf16[128,2048]{1,0:T(8,128)(2,1)S(1)} %slice.86), channel_id=1, source_target_pairs={{0,4},{2,6},{4,0},{6,2},{8,12},{10,14},{12,8},{14,10},{16,20},{18,... | collective-permute-start | bytes 1572872 | tf_op jit(solution)/shard_map/ppermute | solution.py:263
  165.4 4.9 %collective-permute-start.20 = (bf16[256,4224]{1,0:T(8,128)(2,1)}, bf16[256,4224]{1,0:T(8,128)(2,1)}, u32[]{:S(2)}, u32[]{:S(2)}) collective-permute-start(bf16[256,4224]{1,0:T(8,128)(2,1)} %get-tuple-element.50), channel_id=1, source_target_pairs={{0,2},{2,0},{4,6},{6,4},{8,10},{10,8},{12,14},{14,12},{16,18},{18,... | collective-permute-start | bytes 6488072 | tf_op jit(solution)/shard_map/ppermute | solution.py:260
  165.5 31.3 %all-to-all-start.1 = ((bf16[4,64,2048]{2,1,0:T(8,128)(2,1)}), bf16[4,64,2048]{2,1,0:T(8,128)(2,1)}, u32[]{:S(2)}, u32[]{:S(2)}) async-start(bf16[4,64,2048]{2,1,0:T(8,128)(2,1)} %spread.3), calls=%async_computation.1 | async-start | bytes 2097152 | tf_op jit(solution)/shard_map/all_to_all | solution.py:320
  196.8 29.9 %all-to-all-start = ((bf16[4,64,2048]{2,1,0:T(8,128)(2,1)}), bf16[4,64,2048]{2,1,0:T(8,128)(2,1)}, u32[]{:S(2)}, u32[]{:S(2)}) async-start(bf16[4,64,2048]{2,1,0:T(8,128)(2,1)} %spread.2), calls=%async_computation | async-start | bytes 2097152 | tf_op jit(solution)/shard_map/all_to_all | solution.py:320
  (39 other events, 175.0 us)

commit v14 on v12

--- a/solution.py
+++ b/solution.py
@@ -275,14 +275,14 @@
     far.append(to_x(near[1]))
     near.append(after(to_z(near[1], 1), far[0], relay[0]))
     far.append(to_x(near[2]))
-    relay += [to_y(far[0]), to_y(near[1]), to_y(far[1]), to_y(near[2])]
-    near.append(after(to_z(near[2], 1), relay[1], relay[2]))
+    near.append(to_z(near[2], 1))
     far.append(to_x(near[3]))
-    joined = jnp.concatenate([near[3], far[2], far[3]], axis=0)
+    relay += [to_y(far[0]), to_y(near[1]), to_y(far[1])]
+    joined = jnp.concatenate([near[2], near[3], far[2], far[3]], axis=0)
     last = to_y(joined)
     own_pieces = [(a, 0) for a in near + far]
-    other_pieces = [(relay[0], 0), (relay[2], 0), (relay[4], 0), (last, 0)]
-    other_pieces += [(relay[1], 0), (relay[3], 0), (last, 1), (last, 2)]
+    other_pieces = [(relay[0], 0), (relay[2], 0), (last, 0), (last, 1)]
+    other_pieces += [(relay[1], 0), (relay[3], 0), (last, 2), (last, 3)]
     expert_index = expert
     expert = expert.reshape(1)
 
@@ -320,7 +320,7 @@
         act = lax.dynamic_slice_in_dim(act, replica * (hidden // 2), hidden // 2, 1)
         return outer_sum(x, d_gate), outer_sum(x, d_up), outer_sum(act, cot)
 
-    packed = plan(own_pieces, *relay[3:5], joined)
+    packed = plan(own_pieces, *relay[1:4], joined)
     place = packed[-1]
     own_x, weight, pre_gate, pre_up, act, cot = enter(packed)
     parts = leave(lambda rows: (dot(act[rows], w_down) * weight[rows]).astype(BF))
@@ -334,13 +334,13 @@
     chunks = home(after(place, grad_parts[0], grad_parts[1]), parts)
     own_grads = after((cot, d_gate, d_up), chunks[0])
     own = grads(own_x, act, *own_grads)
-    grad_chunks = home(after(place, *own, *chunks[1:]), grad_parts)
-
-    packed = plan(other_pieces, grad_chunks[0])
+    packed = plan(other_pieces, *own, *grad_parts[2:], *chunks[1:])
+    grad_chunks = home(after(place, packed[-1]), grad_parts)
+
     x, weight, pre_gate, pre_up, act, cot = enter(packed)
     d_gate, d_up = hidden_grads(cot, pre_gate, pre_up, w_down)
     other = grads(x, act, cot, d_gate, after(d_up, grad_chunks[1]))
-    grad_chunks = after(grad_chunks, other[0])
+    chunks, grad_chunks = after((chunks, grad_chunks), other[0])
     grad_gate, grad_up, grad_down = ((a + b).astype(BF)[None] for a, b in zip(own, other))
     return (total(chunks), total(grad_chunks), grad_gate, grad_up, grad_down)
 

time: 190 us -> 176 us (0.926)
  starting transfers between devices: 37.8 us -> 23.8 us
  waiting for transfers between devices: 72.3 us -> 74.5 us
  other arithmetic: 7.43 us -> 5.48 us
    ppermute x6 -> x5, waiting for transfers between devices: 15.3 us -> 0.01 us  [to_y(): return lax.ppermute(rows, 'replica', [(0, 1), (1, 0)])]
    ppermute x9, starting transfers between devices: 21.3 us -> 7.63 us  [to_z(): lax.ppermute(rows, 'expert', [(i, (i + 4 * step) % experts) for i in rang...]
    ppermute x9, waiting for transfers between devices: 35.2 us -> 48.1 us  [to_z(): lax.ppermute(rows, 'expert', [(i, (i + 4 * step) % experts) for i in rang...]
    ppermute x8, waiting for transfers between devices: 17.4 us -> 22 us  [to_x(): return lax.ppermute(rows, 'expert', [(i, i ^ 2) for i in range(experts)])]
    unnamed x66 -> x71, local copies, waits for them, and re-layouts: 10.2 us -> 7.65 us
    ppermute x6 -> x5, starting transfers between devices: 7.09 us -> 6.6 us  [to_y(): return lax.ppermute(rows, 'replica', [(0, 1), (1, 0)])]
  transfers between devices with their start and end apart: 27 -> 26, of which waited for: 11 -> 10; matrix products, arithmetic and copies ran while one was open for 22% -> 25% of each run, Pallas kernels for 3% -> 4%
where the time goes in v14:
time: 176 us; the launch traced here: 175 us
  waiting for transfers between devices  74.5 us (42%)
  matrix products  34.5 us (20%)
  starting transfers between devices  23.8 us (14%)
  Pallas kernels  18 us (10%)
  local copies, waits for them, and re-layouts  17.8 us (10%)
  other arithmetic  5.48 us (3%)
    ppermute x9, waiting for transfers between devices, to_z(): lax.ppermute(rows, 'expert', [(i, (i + 4 * step) % experts) for i in rang...  48.1 us
    ppermute x8, waiting for transfers between devices, to_x(): return lax.ppermute(rows, 'expert', [(i, i ^ 2) for i in range(experts)])  22 us
    dot_general x6, matrix products, outer_sum(): lax.dot_general(left, right, (((0,), (0,)), ((), ())), preferred_element_...  13.7 us
    pallas_call x2, Pallas kernels, plan_and_pack(): pl.pallas_call(body, grid_spec=pltpu.PrefetchScalarGridSpec(num_scalar_pr...  11.5 us
    dot_general x6, matrix products, dot(): return jnp.dot(left, right, preferred_element_type=F32)  9.41 us
    ppermute x8, starting transfers between devices, to_x(): return lax.ppermute(rows, 'expert', [(i, i ^ 2) for i in range(experts)])  9.18 us
    unnamed x71, local copies, waits for them, and re-layouts  7.65 us
    ppermute x9, starting transfers between devices, to_z(): lax.ppermute(rows, 'expert', [(i, (i + 4 * step) % experts) for i in rang...  7.63 us
  transfers between devices with their start and end apart: 26, of which 10 were waited for; matrix products, arithmetic and copies ran while one was open for 25% of the time, Pallas kernels for 4%

profile of v14, /device:TPU:0, one launch (start us, length us, event | category | flops | bytes accessed | tf_op | source)
XLA Modules:
  0.0 175.3 jit_solution(13279077978656587241)
XLA Ops:
  3.6 3.0 %collective-permute-start.2 = (bf16[64,4224]{1,0:T(8,128)(2,1)}, bf16[64,4224]{1,0:T(8,128)(2,1)}, u32[]{:S(2)}, u32[]{:S(2)}) collective-permute-start(bf16[64,4224]{1,0:T(8,128)(2,1)} %concatenate.24.refs_0_), channel_id=1, source_target_pairs={{0,8},{2,10},{4,12},{6,14},{8,16},{10,18},{12,20},{14,22},{16,24},... | collective-permute-start | bytes 1622024 | tf_op jit(solution)/shard_map/ppermute | solution.py:261
  9.7 11.6 %collective-permute-done.2.refs_1_ = bf16[64,4224]{1,0:T(8,128)(2,1)} collective-permute-done((bf16[64,4224]{1,0:T(8,128)(2,1)}, bf16[64,4224]{1,0:T(8,128)(2,1)}, u32[]{:S(2)}, u32[]{:S(2)}) %collective-permute-start.2) | collective-permute-done | bytes 540704 | tf_op jit(solution)/shard_map/ppermute | solution.py:261
  24.8 12.0 %collective-permute-done.6.refs_2_ = bf16[64,4224]{1,0:T(8,128)(2,1)} collective-permute-done((bf16[64,4224]{1,0:T(8,128)(2,1)}, bf16[64,4224]{1,0:T(8,128)(2,1)}, u32[]{:S(2)}, u32[]{:S(2)}) %collective-permute-start.6) | collective-permute-done | bytes 540704 | tf_op jit(solution)/shard_map/ppermute | solution.py:261
  41.5 10.6 %collective-permute-done.8.refs_3_ = bf16[64,4224]{1,0:T(8,128)(2,1)S(1)} collective-permute-done((bf16[64,4224]{1,0:T(8,128)(2,1)}, bf16[64,4224]{1,0:T(8,128)(2,1)S(1)}, u32[]{:S(2)}, u32[]{:S(2)}) %collective-permute-start.8) | collective-permute-done | bytes 540704 | tf_op jit(solution)/shard_map/ppermute | solution.py:261
  54.9 8.3 %collective-permute-done.10.refs_7_ = bf16[64,4224]{1,0:T(8,128)(2,1)S(1)} collective-permute-done((bf16[64,4224]{1,0:T(8,128)(2,1)S(1)}, bf16[64,4224]{1,0:T(8,128)(2,1)S(1)}, u32[]{:S(2)}, u32[]{:S(2)}) %collective-permute-start.10) | collective-permute-done | bytes 540704 | tf_op jit(solution)/shard_map/ppermute | solution.py:258
  64.2 5.7 %plan_and_pack.2 = (bf16[256,2048]{1,0:T(8,128)(2,1)}, bf16[256,2048]{1,0:T(8,128)(2,1)}, bf16[256,128]{1,0:T(8,128)(2,1)}, bf16[256,4224]{1,0:T(8,128)(2,1)}, bf16[256,512]{1,0:T(8,128)(2,1)}) custom-call(s32[1]{0:T(128)} %bitcast.expert_ref, bf16[64,4224]{1,0:T(8,128)(2,1)} %concatenate.24.refs_0_, bf16[64,4224]{1,0:T(8,128)(2,1)} %collective-permute-done.2.refs_1_, ...), custom_call_target="tpu_custom_call" | custom-call | flops 1 | bytes 1 | tf_op jit(solution)/shard_map/plan_and_pack/pallas_call | solution.py:185
  70.0 4.4 %collective-permute-done.11 = bf16[256,4224]{1,0:T(8,128)(2,1)S(1)} collective-permute-done((bf16[256,4224]{1,0:T(8,128)(2,1)}, bf16[256,4224]{1,0:T(8,128)(2,1)S(1)}, u32[]{:S(2)}, u32[]{:S(2)}) %collective-permute-start.11) | collective-permute-done | bytes 2162720 | tf_op jit(solution)/shard_map/ppermute | solution.py:255
  86.1 2.2 %multiply_convert_fusion.4 = (bf16[512,768]{1,0:T(8,128)(2,1)S(1)}, bf16[512,768]{1,0:T(8,128)(2,1)S(1)}) fusion(f32[512,768]{1,0:T(8,128)S(1)} %fusion.22, f32[512,768]{1,0:T(8,128)S(1)} %get-tuple-element.100, bf16[512,2048]{1,0:T(8,128)(2,1)S(1)} %multiply_convert_fusion.1, bf16[1,768,2048]{2,1,0:T(8,128)(2,1)S(1)} %copy-done.29), kind=kOutput, calls=%fused_computation.48 | convolution fusion | flops 1615724544 | bytes 9961472 | tf_op jit(solution)/shard_map/dot_general | solution.py:41
  90.3 2.1 %fusion.43 = bf16[256,2048]{1,0:T(8,128)(2,1)} fusion(f32[256,2048]{1,0:T(8,128)S(1)} %fusion.10, bf16[256,768]{1,0:T(8,128)(2,1)S(1)} %get-tuple-element.54, bf16[1,2048,768]{2,1,0:T(8,128)(2,1)S(1)} %copy-done), kind=kOutput, calls=%fused_computation.36 | convolution fusion | flops 806354944 | bytes 6684672 | tf_op jit(solution)/shard_map/dot_general | solution.py:49
  95.1 5.1 %collective-permute-done.13.refs_2_ = bf16[128,2048]{1,0:T(8,128)(2,1)} collective-permute-done((bf16[128,2048]{1,0:T(8,128)(2,1)}, bf16[128,2048]{1,0:T(8,128)(2,1)}, u32[]{:S(2)}, u32[]{:S(2)}) %collective-permute-start.13) | collective-permute-done | bytes 524320 | tf_op jit(solution)/shard_map/ppermute | solution.py:258
  100.2 3.2 %fusion.12 = f32[256,2048]{1,0:T(8,128)S(1)} fusion(bf16[256,768]{1,0:T(8,128)(2,1)} %get-tuple-element.53, bf16[1,2048,768]{2,1,0:T(8,128)(2,1)} %param.12), kind=kOutput, calls=%fused_computation.14 | convolution fusion | flops 805306368 | bytes 5636096 | tf_op jit(solution)/shard_map/dot_general | solution.py:50
  104.5 6.0 %collective-permute-done.15.refs_3_ = bf16[128,2048]{1,0:T(8,128)(2,1)S(1)} collective-permute-done((bf16[128,2048]{1,0:T(8,128)(2,1)S(1)}, bf16[128,2048]{1,0:T(8,128)(2,1)S(1)}, u32[]{:S(2)}, u32[]{:S(2)}) %collective-permute-start.15) | collective-permute-done | bytes 524320 | tf_op jit(solution)/shard_map/ppermute | solution.py:258
  111.3 3.2 %spread.2 = (bf16[64,2048]{1,0:T(8,128)(2,1)}, bf16[64,2048]{1,0:T(8,128)(2,1)}, bf16[64,2048]{1,0:T(8,128)(2,1)}, bf16[64,2048]{1,0:T(8,128)(2,1)}) custom-call(bf16[256,512]{1,0:T(8,128)(2,1)} %get-tuple-element.56.place_ref, bf16[256,2048]{1,0:T(8,128)(2,1)} %copy-done.7, bf16[256,2048]{1,0:T(8,128)(2,1)} %collective-permute-done.12.refs_1_, ...), custom_call_target="tpu_custom_call" | custom-call | flops 1 | bytes 1 | tf_op jit(solution)/shard_map/spread/pallas_call | solution.py:220
  117.3 2.7 %fusion.59 = f32[384,2048]{1,0:T(8,128)S(1)} fusion(bf16[512,2048]{1,0:T(8,128)(2,1)} %copy-done.3, bf16[512,768]{1,0:T(8,128)(2,1)} %copy-done.27, s32[]{:T(128)S(6)} %select_n.32), kind=kOutput, calls=%fused_computation.64 | convolution fusion | flops 805306368 | bytes 5636100 | tf_op jit(solution)/shard_map/dot_general | solution.py:55
  120.1 2.6 %fusion.73 = f32[1024,768]{1,0:T(8,128)} fusion(bf16[512,768]{1,0:T(8,128)(2,1)S(1)} %copy-done.19, s32[]{:T(128)S(6)} %select_n.31, bf16[256,2048]{1,0:T(8,128)(2,1)S(1)} %copy-done.32, bf16[256,2048]{1,0:T(8,128)(2,1)S(1)} %copy-done.13), kind=kOutput, calls=%fused_computation.89 | convolution fusion | flops 807403520 | bytes 6029316 | tf_op jit(solution)/shard_map/dot_general | solution.py:55
  122.7 2.6 %collective-permute-done.19.refs_2_ = bf16[128,2048]{1,0:T(8,128)(2,1)S(1)} collective-permute-done((bf16[128,2048]{1,0:T(8,128)(2,1)S(1)}, bf16[128,2048]{1,0:T(8,128)(2,1)S(1)}, u32[]{:S(2)}, u32[]{:S(2)}) %collective-permute-start.19) | collective-permute-done | bytes 524320 | tf_op jit(solution)/shard_map/ppermute | solution.py:258
  125.3 2.7 %fusion.71 = f32[1024,768]{1,0:T(8,128)} fusion(bf16[512,768]{1,0:T(8,128)(2,1)S(1)} %copy-done.17, s32[]{:T(128)S(6)} %select_n.31, bf16[256,2048]{1,0:T(8,128)(2,1)S(1)} %copy-done.32, bf16[256,2048]{1,0:T(8,128)(2,1)S(1)} %copy-done.13), kind=kOutput, calls=%fused_computation.88 | convolution fusion | flops 807403520 | bytes 6029316 | tf_op jit(solution)/shard_map/dot_general | solution.py:55
  128.1 9.4 %collective-permute-done.17 = bf16[64,2048]{1,0:T(8,128)(2,1)S(1)} collective-permute-done((bf16[64,2048]{1,0:T(8,128)(2,1)}, bf16[64,2048]{1,0:T(8,128)(2,1)S(1)}, u32[]{:S(2)}, u32[]{:S(2)}) %collective-permute-start.17) | collective-permute-done | bytes 262176 | tf_op jit(solution)/shard_map/ppermute | solution.py:261
  138.1 5.9 %plan_and_pack.3 = (bf16[256,2048]{1,0:T(8,128)(2,1)}, bf16[256,2048]{1,0:T(8,128)(2,1)}, bf16[256,128]{1,0:T(8,128)(2,1)}, bf16[256,4224]{1,0:T(8,128)(2,1)}, bf16[256,512]{1,0:T(8,128)(2,1)}) custom-call(s32[1]{0:T(128)} %bitcast.expert_ref, bf16[64,4224]{1,0:T(8,128)(2,1)} %collective-permute-done.7.refs_0_, ...), custom_call_target="tpu_custom_call" | custom-call | flops 1 | bytes 1 | tf_op jit(solution)/shard_map/plan_and_pack/pallas_call | solution.py:185
  144.1 3.2 %spread.3 = (bf16[64,2048]{1,0:T(8,128)(2,1)}, bf16[64,2048]{1,0:T(8,128)(2,1)}, bf16[64,2048]{1,0:T(8,128)(2,1)}, bf16[64,2048]{1,0:T(8,128)(2,1)}) custom-call(bf16[256,512]{1,0:T(8,128)(2,1)} %get-tuple-element.56.place_ref, bf16[256,2048]{1,0:T(8,128)(2,1)} %copy-done.4, bf16[256,2048]{1,0:T(8,128)(2,1)} %collective-permute-done.14.refs_1_, ...), custom_call_target="tpu_custom_call" | custom-call | flops 1 | bytes 1 | tf_op jit(solution)/shard_map/spread/pallas_call | solution.py:220
  149.6 2.0 %collective-permute-start.23 = (bf16[64,2048]{1,0:T(8,128)(2,1)}, bf16[64,2048]{1,0:T(8,128)(2,1)S(1)}, u32[]{:S(2)}, u32[]{:S(2)}) collective-permute-start(bf16[64,2048]{1,0:T(8,128)(2,1)} %get-tuple-element.65), channel_id=1, source_target_pairs={{0,8},{2,10},{4,12},{6,14},{8,16},{10,18},{12,20},{14,22},{16,24},... | collective-permute-start | bytes 786440 | tf_op jit(solution)/shard_map/ppermute | solution.py:261
  164.7 2.3 %fusion.36 = bf16[1,384,2048]{2,1,0:T(8,128)(2,1)} fusion(f32[384,2048]{1,0:T(8,128)S(1)} %fusion.59, f32[512,768]{1,0:T(8,128)S(1)} %fusion.8, s32[]{:T(128)S(6)} %select_n.32, f32[512,768]{1,0:T(8,128)S(1)} %get-tuple-element.89, f32[512,768]{1,0:T(8,128)S(1)} %get-tuple-element.101, bf16[256,2048]{1,0:T(8,128)(2,1)S(1)} %get-tuple-element.85, ...), kind=kOutput, calls=%fused_computation.33 | convolution fusion | flops 813760512 | bytes 9177092 | tf_op jit(solution)/shard_map/dot_general | solution.py:55
  167.0 2.2 %fusion.50 = bf16[1,1024,768]{2,1,0:T(8,128)(2,1)} fusion(f32[1024,768]{1,0:T(8,128)S(1)} %copy-done.5, bf16[512,768]{1,0:T(8,128)(2,1)S(1)} %get-tuple-element.82, s32[]{:T(128)S(6)} %select_n.31, bf16[256,2048]{1,0:T(8,128)(2,1)S(1)} %copy-done.14, bf16[256,2048]{1,0:T(8,128)(2,1)S(1)} %get-tuple-element.86), kind=kOutput, calls=%fused_computation.52 | convolution fusion | flops 808976384 | bytes 7602180 | tf_op jit(solution)/shard_map/dot_general | solution.py:55
  169.2 4.4 %collective-permute-done.22 = bf16[64,2048]{1,0:T(8,128)(2,1)S(1)} collective-permute-done((bf16[64,2048]{1,0:T(8,128)(2,1)}, bf16[64,2048]{1,0:T(8,128)(2,1)S(1)}, u32[]{:S(2)}, u32[]{:S(2)}) %collective-permute-start.22) | collective-permute-done | bytes 262176 | tf_op jit(solution)/shard_map/ppermute | solution.py:261
  (146 shorter events, 56.5 us)
Async XLA Ops:
  3.6 17.6 %collective-permute-start.2 = (bf16[64,4224]{1,0:T(8,128)(2,1)}, bf16[64,4224]{1,0:T(8,128)(2,1)}, u32[]{:S(2)}, u32[]{:S(2)}) collective-permute-start(bf16[64,4224]{1,0:T(8,128)(2,1)} %concatenate.24.refs_0_), channel_id=1, source_target_pairs={{0,8},{2,10},{4,12},{6,14},{8,16},{10,18},{12,20},{14,22},{16,24},... | collective-permute-start | bytes 1622024 | tf_op jit(solution)/shard_map/ppermute | solution.py:261
  6.7 17.6 %collective-permute-start = (bf16[64,4224]{1,0:T(8,128)(2,1)}, bf16[64,4224]{1,0:T(8,128)(2,1)}, u32[]{:S(2)}, u32[]{:S(2)}) collective-permute-start(bf16[64,4224]{1,0:T(8,128)(2,1)} %concatenate.24.refs_0_), channel_id=1, source_target_pairs={{0,4},{2,6},{4,0},{6,2},{8,12},{10,14},{12,8},{14,10},{16,20},{18,... | collective-permute-start | bytes 1622024 | tf_op jit(solution)/shard_map/ppermute | solution.py:258
  8.2 16.6 %collective-permute-start.7 = (bf16[64,4224]{1,0:T(8,128)(2,1)}, bf16[64,4224]{1,0:T(8,128)(2,1)}, u32[]{:S(2)}, u32[]{:S(2)}) collective-permute-start(bf16[64,4224]{1,0:T(8,128)(2,1)} %concatenate.24.refs_0_), channel_id=1, source_target_pairs={{0,1},{1,0},{2,3},{3,2},{4,5},{5,4},{6,7},{7,6},{8,9},{9,8},{10,11... | collective-permute-start | bytes 1622024 | tf_op jit(solution)/shard_map/ppermute | solution.py:266
  21.3 15.6 %collective-permute-start.6 = (bf16[64,4224]{1,0:T(8,128)(2,1)}, bf16[64,4224]{1,0:T(8,128)(2,1)}, u32[]{:S(2)}, u32[]{:S(2)}) collective-permute-start(bf16[64,4224]{1,0:T(8,128)(2,1)} %collective-permute-done.2.refs_1_), channel_id=1, source_target_pairs={{0,8},{2,10},{4,12},{6,14},{8,16},{10,18},{12,20},{14,22},{16,24},... | collective-permute-start | bytes 1622024 | tf_op jit(solution)/shard_map/ppermute | solution.py:261
  21.3 16.8 %collective-permute-start.4 = (bf16[64,4224]{1,0:T(8,128)(2,1)}, bf16[64,4224]{1,0:T(8,128)(2,1)}, u32[]{:S(2)}, u32[]{:S(2)}) collective-permute-start(bf16[64,4224]{1,0:T(8,128)(2,1)} %collective-permute-done.2.refs_1_), channel_id=1, source_target_pairs={{0,4},{2,6},{4,0},{6,2},{8,12},{10,14},{12,8},{14,10},{16,20},{18,... | collective-permute-start | bytes 1622024 | tf_op jit(solution)/shard_map/ppermute | solution.py:258
  22.8 41.4 %collective-permute-start.3 = (bf16[64,4224]{1,0:T(8,128)(2,1)}, bf16[64,4224]{1,0:T(8,128)(2,1)}, u32[]{:S(2)}, u32[]{:S(2)}) collective-permute-start(bf16[64,4224]{1,0:T(8,128)(2,1)} %collective-permute-done.2.refs_1_), channel_id=1, source_target_pairs={{0,1},{1,0},{2,3},{3,2},{4,5},{5,4},{6,7},{7,6},{8,9},{9,8},{10,11... | collective-permute-start | bytes 1622024 | tf_op jit(solution)/shard_map/ppermute | solution.py:266
  24.3 39.8 %collective-permute-start.1 = (bf16[64,4224]{1,0:T(8,128)(2,1)}, bf16[64,4224]{1,0:T(8,128)(2,1)}, u32[]{:S(2)}, u32[]{:S(2)}) collective-permute-start(bf16[64,4224]{1,0:T(8,128)(2,1)} %collective-permute-done.refs_4_), channel_id=1, source_target_pairs={{0,1},{1,0},{2,3},{3,2},{4,5},{5,4},{6,7},{7,6},{8,9},{9,8},{10,11... | collective-permute-start | bytes 1622024 | tf_op jit(solution)/shard_map/ppermute | solution.py:266
  36.9 17.1 %collective-permute-start.9 = (bf16[64,4224]{1,0:T(8,128)(2,1)}, bf16[64,4224]{1,0:T(8,128)(2,1)S(1)}, u32[]{:S(2)}, u32[]{:S(2)}) collective-permute-start(bf16[64,4224]{1,0:T(8,128)(2,1)} %collective-permute-done.6.refs_2_), channel_id=1, source_target_pairs={{0,4},{2,6},{4,0},{6,2},{8,12},{10,14},{12,8},{14,10},{16,20},{18,... | collective-permute-start | bytes 1622024 | tf_op jit(solution)/shard_map/ppermute | solution.py:258
  38.1 14.0 %collective-permute-start.8 = (bf16[64,4224]{1,0:T(8,128)(2,1)}, bf16[64,4224]{1,0:T(8,128)(2,1)S(1)}, u32[]{:S(2)}, u32[]{:S(2)}) collective-permute-start(bf16[64,4224]{1,0:T(8,128)(2,1)} %collective-permute-done.6.refs_2_), channel_id=1, source_target_pairs={{0,8},{2,10},{4,12},{6,14},{8,16},{10,18},{12,20},{14,22},{16,24},... | collective-permute-start | bytes 1622024 | tf_op jit(solution)/shard_map/ppermute | solution.py:261
  38.1 26.0 %collective-permute-start.5 = (bf16[64,4224]{1,0:T(8,128)(2,1)}, bf16[64,4224]{1,0:T(8,128)(2,1)}, u32[]{:S(2)}, u32[]{:S(2)}) collective-permute-start(bf16[64,4224]{1,0:T(8,128)(2,1)} %collective-permute-done.4.refs_5_), channel_id=1, source_target_pairs={{0,1},{1,0},{2,3},{3,2},{4,5},{5,4},{6,7},{7,6},{8,9},{9,8},{10,11... | collective-permute-start | bytes 1622024 | tf_op jit(solution)/shard_map/ppermute | solution.py:266
  52.1 11.1 %collective-permute-start.10 = (bf16[64,4224]{1,0:T(8,128)(2,1)S(1)}, bf16[64,4224]{1,0:T(8,128)(2,1)S(1)}, u32[]{:S(2)}, u32[]{:S(2)}) collective-permute-start(bf16[64,4224]{1,0:T(8,128)(2,1)S(1)} %collective-permute-done.8.refs_3_), channel_id=1, source_target_pairs={{0,4},{2,6},{4,0},{6,2},{8,12},{10,14},{12,8},{14,10},{16,20},{18,... | collective-permute-start | bytes 1622024 | tf_op jit(solution)/shard_map/ppermute | solution.py:258
  81.6 56.5 %collective-permute-start.24 = (bf16[256,4224]{1,0:T(8,128)(2,1)}, bf16[256,4224]{1,0:T(8,128)(2,1)}, u32[]{:S(2)}, u32[]{:S(2)}) collective-permute-start(bf16[256,4224]{1,0:T(8,128)(2,1)} %constant_dynamic-update-slice_fusion), channel_id=1, source_target_pairs={{0,1},{1,0},{2,3},{3,2},{4,5},{5,4},{6,7},{7,6},{8,9},{9,8},{10,11... | collective-permute-start | bytes 6488072 | tf_op jit(solution)/shard_map/ppermute | solution.py:266
  85.1 15.1 %collective-permute-start.13 = (bf16[128,2048]{1,0:T(8,128)(2,1)}, bf16[128,2048]{1,0:T(8,128)(2,1)}, u32[]{:S(2)}, u32[]{:S(2)}) collective-permute-start(bf16[128,2048]{1,0:T(8,128)(2,1)} %slice.81), channel_id=1, source_target_pairs={{0,4},{2,6},{4,0},{6,2},{8,12},{10,14},{12,8},{14,10},{16,20},{18,... | collective-permute-start | bytes 1572872 | tf_op jit(solution)/shard_map/ppermute | solution.py:258
  92.4 18.6 %collective-permute-start.14 = (bf16[256,2048]{1,0:T(8,128)(2,1)}, bf16[256,2048]{1,0:T(8,128)(2,1)}, u32[]{:S(2)}, u32[]{:S(2)}) collective-permute-start(bf16[256,2048]{1,0:T(8,128)(2,1)} %fusion.43), channel_id=1, source_target_pairs={{0,2},{2,0},{4,6},{6,4},{8,10},{10,8},{12,14},{14,12},{16,18},{18,... | collective-permute-start | bytes 3145736 | tf_op jit(solution)/shard_map/ppermute | solution.py:255
  93.5 17.0 %collective-permute-start.15 = (bf16[128,2048]{1,0:T(8,128)(2,1)S(1)}, bf16[128,2048]{1,0:T(8,128)(2,1)S(1)}, u32[]{:S(2)}, u32[]{:S(2)}) collective-permute-start(bf16[128,2048]{1,0:T(8,128)(2,1)S(1)} %slice.84), channel_id=1, source_target_pairs={{0,4},{2,6},{4,0},{6,2},{8,12},{10,14},{12,8},{14,10},{16,20},{18,... | collective-permute-start | bytes 1572872 | tf_op jit(solution)/shard_map/ppermute | solution.py:258
  110.5 14.9 %collective-permute-start.19 = (bf16[128,2048]{1,0:T(8,128)(2,1)S(1)}, bf16[128,2048]{1,0:T(8,128)(2,1)S(1)}, u32[]{:S(2)}, u32[]{:S(2)}) collective-permute-start(bf16[128,2048]{1,0:T(8,128)(2,1)S(1)} %slice.85), channel_id=1, source_target_pairs={{0,4},{2,6},{4,0},{6,2},{8,12},{10,14},{12,8},{14,10},{16,20},{18,... | collective-permute-start | bytes 1572872 | tf_op jit(solution)/shard_map/ppermute | solution.py:258
  114.5 13.6 %collective-permute-start.16 = (bf16[64,2048]{1,0:T(8,128)(2,1)}, bf16[64,2048]{1,0:T(8,128)(2,1)S(1)}, u32[]{:S(2)}, u32[]{:S(2)}) collective-permute-start(bf16[64,2048]{1,0:T(8,128)(2,1)} %get-tuple-element.58), channel_id=1, source_target_pairs={{0,24},{2,26},{4,28},{6,30},{8,0},{10,2},{12,4},{14,6},{16,8},{18,... | collective-permute-start | bytes 786440 | tf_op jit(solution)/shard_map/ppermute | solution.py:261
  114.5 22.9 %collective-permute-start.17 = (bf16[64,2048]{1,0:T(8,128)(2,1)}, bf16[64,2048]{1,0:T(8,128)(2,1)S(1)}, u32[]{:S(2)}, u32[]{:S(2)}) collective-permute-start(bf16[64,2048]{1,0:T(8,128)(2,1)} %get-tuple-element.59), channel_id=1, source_target_pairs={{0,16},{2,18},{4,20},{6,22},{8,24},{10,26},{12,28},{14,30},{16,0},... | collective-permute-start | bytes 786440 | tf_op jit(solution)/shard_map/ppermute | solution.py:261
  116.0 21.5 %collective-permute-start.20 = (bf16[128,2048]{1,0:T(8,128)(2,1)S(1)}, bf16[128,2048]{1,0:T(8,128)(2,1)S(1)}, u32[]{:S(2)}, u32[]{:S(2)}) collective-permute-start(bf16[128,2048]{1,0:T(8,128)(2,1)S(1)} %slice.86), channel_id=1, source_target_pairs={{0,4},{2,6},{4,0},{6,2},{8,12},{10,14},{12,8},{14,10},{16,20},{18,... | collective-permute-start | bytes 1572872 | tf_op jit(solution)/shard_map/ppermute | solution.py:258
  125.3 12.1 %collective-permute-start.18 = (bf16[64,2048]{1,0:T(8,128)(2,1)S(1)}, bf16[64,2048]{1,0:T(8,128)(2,1)S(1)}, u32[]{:S(2)}, u32[]{:S(2)}) collective-permute-start(bf16[64,2048]{1,0:T(8,128)(2,1)S(1)} %copy-done.33), channel_id=1, source_target_pairs={{0,8},{2,10},{4,12},{6,14},{8,16},{10,18},{12,20},{14,22},{16,24},... | collective-permute-start | bytes 786440 | tf_op jit(solution)/shard_map/ppermute | solution.py:261
  144.0 7.6 %collective-permute-start.25 = (bf16[256,4224]{1,0:T(8,128)(2,1)}, bf16[256,4224]{1,0:T(8,128)(2,1)}, u32[]{:S(2)}, u32[]{:S(2)}) collective-permute-start(bf16[256,4224]{1,0:T(8,128)(2,1)} %get-tuple-element.71), channel_id=1, source_target_pairs={{0,2},{2,0},{4,6},{6,4},{8,10},{10,8},{12,14},{14,12},{16,18},{18,... | collective-permute-start | bytes 6488072 | tf_op jit(solution)/shard_map/ppermute | solution.py:255
  147.4 19.6 %collective-permute-start.21 = (bf16[64,2048]{1,0:T(8,128)(2,1)}, bf16[64,2048]{1,0:T(8,128)(2,1)S(1)}, u32[]{:S(2)}, u32[]{:S(2)}) collective-permute-start(bf16[64,2048]{1,0:T(8,128)(2,1)} %get-tuple-element.63), channel_id=1, source_target_pairs={{0,24},{2,26},{4,28},{6,30},{8,0},{10,2},{12,4},{14,6},{16,8},{18,... | collective-permute-start | bytes 786440 | tf_op jit(solution)/shard_map/ppermute | solution.py:261
  148.0 25.6 %collective-permute-start.22 = (bf16[64,2048]{1,0:T(8,128)(2,1)}, bf16[64,2048]{1,0:T(8,128)(2,1)S(1)}, u32[]{:S(2)}, u32[]{:S(2)}) collective-permute-start(bf16[64,2048]{1,0:T(8,128)(2,1)} %get-tuple-element.64), channel_id=1, source_target_pairs={{0,16},{2,18},{4,20},{6,22},{8,24},{10,26},{12,28},{14,30},{16,0},... | collective-permute-start | bytes 786440 | tf_op jit(solution)/shard_map/ppermute | solution.py:261
  149.6 24.0 %collective-permute-start.23 = (bf16[64,2048]{1,0:T(8,128)(2,1)}, bf16[64,2048]{1,0:T(8,128)(2,1)S(1)}, u32[]{:S(2)}, u32[]{:S(2)}) collective-permute-start(bf16[64,2048]{1,0:T(8,128)(2,1)} %get-tuple-element.65), channel_id=1, source_target_pairs={{0,8},{2,10},{4,12},{6,14},{8,16},{10,18},{12,20},{14,22},{16,24},... | collective-permute-start | bytes 786440 | tf_op jit(solution)/shard_map/ppermute | solution.py:261
  (36 other events, 214.2 us)

commit v15 on v14

--- a/solution.py
+++ b/solution.py
@@ -302,11 +302,14 @@
         act = (jax.nn.silu(pre_gate) * pre_up).astype(BF)
         return x, weight, pre_gate, pre_up, act, cot
 
-    def leave(rows_of, before_mine=(), before_far=()):
-        half = TOGETHER * capacity
-        theirs = to_core(rows_of(slice(2 * half, None)))
-        mine = rows_of(slice(0, 2 * half), *before_mine)
-        return mine, theirs, to_x(after(mine[half:], *before_far)), to_x(theirs[half:])
+    def leave(rows_of, before_mine=(), before_theirs=()):
+        room = TOGETHER * capacity
+        far_theirs = to_core(rows_of(slice(3 * room, None)))
+        far_mine = rows_of(slice(room, 2 * room))
+        theirs = to_core(rows_of(slice(2 * room, 3 * room)))
+        mine = rows_of(slice(0, room))
+        far_mine = to_x(after(far_mine, *before_mine))
+        return mine, theirs, far_mine, to_x(after(far_theirs, *before_theirs))
 
     def home(place, parts):
         own, *others = spread(place, *parts)
@@ -320,17 +323,16 @@
         act = lax.dynamic_slice_in_dim(act, replica * (hidden // 2), hidden // 2, 1)
         return outer_sum(x, d_gate), outer_sum(x, d_up), outer_sum(act, cot)
 
-    packed = plan(own_pieces, *relay[1:4], joined)
+    packed = plan(own_pieces, *relay[1:4])
     place = packed[-1]
     own_x, weight, pre_gate, pre_up, act, cot = enter(packed)
     parts = leave(lambda rows: (dot(act[rows], w_down) * weight[rows]).astype(BF))
     cot = after(cot, parts[0], parts[1])
     d_gate, d_up = hidden_grads(cot, pre_gate, pre_up, w_down)
 
-    def token_grads(rows, *earlier):
-        return input_rows(*after((d_gate[rows], d_up[rows]), *earlier), w_gate, w_up)
-
-    grad_parts = leave(token_grads, parts[2:3], parts[3:4])
+    grad_parts = leave(
+        lambda rows: input_rows(d_gate[rows], d_up[rows], w_gate, w_up), parts[2:3], parts[3:4]
+    )
     chunks = home(after(place, grad_parts[0], grad_parts[1]), parts)
     own_grads = after((cot, d_gate, d_up), chunks[0])
     own = grads(own_x, act, *own_grads)

time: 176 us -> 188 us (1.068)
  starting transfers between devices: 23.8 us -> 30.6 us
  matrix products: 34.5 us -> 41.3 us
  local copies, waits for them, and re-layouts: 17.8 us -> 11.3 us
  waiting for transfers between devices: 74.5 us -> 77.4 us
  other arithmetic: 5.48 us -> 8.29 us
    ppermute x5, waiting for transfers between devices: 0.01 us -> 20.4 us  [to_y(): return lax.ppermute(rows, 'replica', [(0, 1), (1, 0)])]
    ppermute x8, waiting for transfers between devices: 22 us -> 7.89 us  [to_x(): return lax.ppermute(rows, 'expert', [(i, i ^ 2) for i in range(experts)])]
    ppermute x9, starting transfers between devices: 7.63 us -> 14.2 us  [to_z(): lax.ppermute(rows, 'expert', [(i, (i + 4 * step) % experts) for i in rang...]
    ppermute x4 -> x6, waiting for transfers between devices: 4.45 us -> 0.44 us  [to_core(): return lax.ppermute(rows, 'expert', [(i, i ^ 1) for i in range(experts)])]
    unnamed x71 -> x52, local copies, waits for them, and re-layouts: 7.65 us -> 3.82 us
    dot_general x2 -> x4, matrix products: 3.08 us -> 6.34 us  [input_rows(): lax.dot_general(d_gate, gate_weight, CONTRACT, preferred_element_type=F32)]
    concatenate x0 -> x1, other arithmetic: none -> 3.08 us  [dense_plan(): joined = jnp.concatenate([near[2], near[3], far[2], far[3]], axis=0)]
    slice x5 -> x1, local copies, waits for them, and re-layouts: 4.1 us -> 1.81 us  [enter(): x = jnp.concatenate([mine, theirs[:, :features]], axis=0)]
  transfers between devices with their start and end apart: 26 -> 28, of which waited for: 10 -> 10; matrix products, arithmetic and copies ran while one was open for 25% -> 28% of each run, Pallas kernels for 4% -> 3%
where the time goes in v15:
time: 188 us
  waiting for transfers between devices  77.4 us (41%)
  matrix products  41.3 us (22%)
  starting transfers between devices  30.6 us (16%)
  Pallas kernels  17.8 us (9%)
  local copies, waits for them, and re-layouts  11.3 us (6%)
  other arithmetic  8.29 us (4%)
    ppermute x9, waiting for transfers between devices, to_z(): lax.ppermute(rows, 'expert', [(i, (i + 4 * step) % experts) for i in rang...  48.6 us
    ppermute x5, waiting for transfers between devices, to_y(): return lax.ppermute(rows, 'replica', [(0, 1), (1, 0)])  20.4 us
    dot_general x6, matrix products, outer_sum(): lax.dot_general(left, right, (((0,), (0,)), ((), ())), preferred_element_...  15.7 us
    ppermute x9, starting transfers between devices, to_z(): lax.ppermute(rows, 'expert', [(i, (i + 4 * step) % experts) for i in rang...  14.2 us
    pallas_call x2, Pallas kernels, plan_and_pack(): pl.pallas_call(body, grid_spec=pltpu.PrefetchScalarGridSpec(num_scalar_pr...  11.3 us
    dot_general x8, matrix products, dot(): return jnp.dot(left, right, preferred_element_type=F32)  10.6 us
    ppermute x8, starting transfers between devices, to_x(): return lax.ppermute(rows, 'expert', [(i, i ^ 2) for i in range(experts)])  9.84 us
    ppermute x8, waiting for transfers between devices, to_x(): return lax.ppermute(rows, 'expert', [(i, i ^ 2) for i in range(experts)])  7.89 us
  transfers between devices with their start and end apart: 28, of which 10 were waited for; matrix products, arithmetic and copies ran while one was open for 28% of the time, Pallas kernels for 3%

profile of v15, /device:TPU:0, one launch (start us, length us, event | category | flops | bytes accessed | tf_op | source)
XLA Modules:
  0.0 187.7 jit_solution(9471832393585527871)
XLA Ops:
  3.6 3.0 %collective-permute-start.2 = (bf16[64,4224]{1,0:T(8,128)(2,1)}, bf16[64,4224]{1,0:T(8,128)(2,1)}, u32[]{:S(2)}, u32[]{:S(2)}) collective-permute-start(bf16[64,4224]{1,0:T(8,128)(2,1)} %concatenate.24.refs_0_), channel_id=1, source_target_pairs={{0,8},{2,10},{4,12},{6,14},{8,16},{10,18},{12,20},{14,22},{16,24},... | collective-permute-start | bytes 1622024 | tf_op jit(solution)/shard_map/ppermute | solution.py:261
  9.7 11.6 %collective-permute-done.2.refs_1_ = bf16[64,4224]{1,0:T(8,128)(2,1)} collective-permute-done((bf16[64,4224]{1,0:T(8,128)(2,1)}, bf16[64,4224]{1,0:T(8,128)(2,1)}, u32[]{:S(2)}, u32[]{:S(2)}) %collective-permute-start.2) | collective-permute-done | bytes 540704 | tf_op jit(solution)/shard_map/ppermute | solution.py:261
  22.8 14.1 %collective-permute-done.6.refs_2_ = bf16[64,4224]{1,0:T(8,128)(2,1)} collective-permute-done((bf16[64,4224]{1,0:T(8,128)(2,1)}, bf16[64,4224]{1,0:T(8,128)(2,1)}, u32[]{:S(2)}, u32[]{:S(2)}) %collective-permute-start.6) | collective-permute-done | bytes 540704 | tf_op jit(solution)/shard_map/ppermute | solution.py:261
  41.7 9.9 %collective-permute-done.8.refs_3_ = bf16[64,4224]{1,0:T(8,128)(2,1)} collective-permute-done((bf16[64,4224]{1,0:T(8,128)(2,1)}, bf16[64,4224]{1,0:T(8,128)(2,1)}, u32[]{:S(2)}, u32[]{:S(2)}) %collective-permute-start.8) | collective-permute-done | bytes 540704 | tf_op jit(solution)/shard_map/ppermute | solution.py:261
  52.5 11.5 %collective-permute-done.1.refs_3_ = bf16[64,4224]{1,0:T(8,128)(2,1)} collective-permute-done((bf16[64,4224]{1,0:T(8,128)(2,1)}, bf16[64,4224]{1,0:T(8,128)(2,1)}, u32[]{:S(2)}, u32[]{:S(2)}) %collective-permute-start.1) | collective-permute-done | bytes 540704 | tf_op jit(solution)/shard_map/ppermute | solution.py:266
  64.0 8.9 %collective-permute-done.5.refs_4_ = bf16[64,4224]{1,0:T(8,128)(2,1)} collective-permute-done((bf16[64,4224]{1,0:T(8,128)(2,1)}, bf16[64,4224]{1,0:T(8,128)(2,1)}, u32[]{:S(2)}, u32[]{:S(2)}) %collective-permute-start.5) | collective-permute-done | bytes 540704 | tf_op jit(solution)/shard_map/ppermute | solution.py:266
  72.9 5.7 %plan_and_pack.2 = (bf16[256,2048]{1,0:T(8,128)(2,1)}, bf16[256,2048]{1,0:T(8,128)(2,1)}, bf16[256,128]{1,0:T(8,128)(2,1)}, bf16[256,4224]{1,0:T(8,128)(2,1)}, bf16[256,512]{1,0:T(8,128)(2,1)}) custom-call(s32[1]{0:T(128)} %bitcast.expert_ref, bf16[64,4224]{1,0:T(8,128)(2,1)} %concatenate.24.refs_0_, bf16[64,4224]{1,0:T(8,128)(2,1)} %collective-permute-done.2.refs_1_, ...), custom_call_target="tpu_custom_call" | custom-call | flops 1 | bytes 1 | tf_op jit(solution)/shard_map/plan_and_pack/pallas_call | solution.py:185
  78.7 3.1 %pad_maximum_fusion.2 = bf16[256,4224]{1,0:T(8,128)(2,1)} fusion(bf16[64,4224]{1,0:T(8,128)(2,1)} %collective-permute-done.10.refs_7_, bf16[64,4224]{1,0:T(8,128)(2,1)} %collective-permute-done.9.refs_6_, bf16[64,4224]{1,0:T(8,128)(2,1)} %collective-permute-done.8.refs_3_, bf16[64,4224]{1,0:T(8,128)(2,1)} %collective-permute-done.6.refs_2_), kind=kLoop, calls=%fused_computation.64 | loop fusion | flops 8650752 | bytes 4325376 | tf_op jit(solution)/shard_map/concatenate | solution.py:281
  95.8 2.2 %multiply_convert_fusion.5 = (bf16[512,768]{1,0:T(8,128)(2,1)S(1)}, bf16[512,768]{1,0:T(8,128)(2,1)S(1)}) fusion(f32[512,768]{1,0:T(8,128)S(1)} %fusion.34, f32[512,768]{1,0:T(8,128)S(1)} %get-tuple-element.92, bf16[512,2048]{1,0:T(8,128)(2,1)S(1)} %multiply_convert_fusion.1, bf16[1,768,2048]{2,1,0:T(8,128)(2,1)S(1)} %copy-done.2), kind=kOutput, calls=%fused_computation.70 | convolution fusion | flops 1615724544 | bytes 9961472 | tf_op jit(solution)/shard_map/dot_general | solution.py:41
  106.1 2.1 %collective-permute-done.14.refs_2_ = bf16[128,2048]{1,0:T(8,128)(2,1)S(1)} collective-permute-done((bf16[128,2048]{1,0:T(8,128)(2,1)S(1)}, bf16[128,2048]{1,0:T(8,128)(2,1)S(1)}, u32[]{:S(2)}, u32[]{:S(2)}) %collective-permute-start.14) | collective-permute-done | bytes 524320 | tf_op jit(solution)/shard_map/ppermute | solution.py:258
  113.6 5.8 %collective-permute-done.16.refs_3_ = bf16[128,2048]{1,0:T(8,128)(2,1)S(1)} collective-permute-done((bf16[128,2048]{1,0:T(8,128)(2,1)S(1)}, bf16[128,2048]{1,0:T(8,128)(2,1)S(1)}, u32[]{:S(2)}, u32[]{:S(2)}) %collective-permute-start.16) | collective-permute-done | bytes 524320 | tf_op jit(solution)/shard_map/ppermute | solution.py:258
  121.3 3.2 %spread.2 = (bf16[64,2048]{1,0:T(8,128)(2,1)}, bf16[64,2048]{1,0:T(8,128)(2,1)}, bf16[64,2048]{1,0:T(8,128)(2,1)}, bf16[64,2048]{1,0:T(8,128)(2,1)}) custom-call(bf16[256,512]{1,0:T(8,128)(2,1)} %get-tuple-element.49.place_ref, bf16[128,2048]{1,0:T(8,128)(2,1)} %fusion.70.refs_0_, bf16[128,2048]{1,0:T(8,128)(2,1)} %copy-done.16, ...), custom_call_target="tpu_custom_call" | custom-call | flops 1 | bytes 1 | tf_op jit(solution)/shard_map/spread/pallas_call | solution.py:220
  124.5 3.6 %collective-permute-start.17 = (bf16[64,2048]{1,0:T(8,128)(2,1)}, bf16[64,2048]{1,0:T(8,128)(2,1)}, u32[]{:S(2)}, u32[]{:S(2)}) collective-permute-start(bf16[64,2048]{1,0:T(8,128)(2,1)} %get-tuple-element.51), channel_id=1, source_target_pairs={{0,24},{2,26},{4,28},{6,30},{8,0},{10,2},{12,4},{14,6},{16,8},{18,... | collective-permute-start | bytes 786440 | tf_op jit(solution)/shard_map/ppermute | solution.py:261
  128.1 4.4 %fusion.93 = f32[384,2048]{1,0:T(8,128)} fusion(bf16[512,2048]{1,0:T(8,128)(2,1)} %copy-done.5, bf16[512,768]{1,0:T(8,128)(2,1)S(1)} %get-tuple-element.91, s32[]{:T(128)S(6)} %select_n.32), kind=kOutput, calls=%fused_computation.83 | convolution fusion | flops 805306368 | bytes 5636100 | tf_op jit(solution)/shard_map/dot_general | solution.py:55
  132.4 2.7 %fusion.119 = f32[1024,768]{1,0:T(8,128)} fusion(bf16[512,768]{1,0:T(8,128)(2,1)S(1)} %copy-done.14, s32[]{:T(128)S(6)} %select_n.31, bf16[256,2048]{1,0:T(8,128)(2,1)S(1)} %copy-done.24, bf16[256,2048]{1,0:T(8,128)(2,1)S(1)} %get-tuple-element.81), kind=kOutput, calls=%fused_computation.116 | convolution fusion | flops 807403520 | bytes 6029316 | tf_op jit(solution)/shard_map/dot_general | solution.py:55
  135.6 2.7 %fusion.117 = f32[1024,768]{1,0:T(8,128)} fusion(bf16[512,768]{1,0:T(8,128)(2,1)S(1)} %copy-done.12, s32[]{:T(128)S(6)} %select_n.31, bf16[256,2048]{1,0:T(8,128)(2,1)S(1)} %copy-done.24, bf16[256,2048]{1,0:T(8,128)(2,1)S(1)} %get-tuple-element.81), kind=kOutput, calls=%fused_computation.115 | convolution fusion | flops 807403520 | bytes 6029316 | tf_op jit(solution)/shard_map/dot_general | solution.py:55
  138.4 9.0 %collective-permute-done.18 = bf16[64,2048]{1,0:T(8,128)(2,1)} collective-permute-done((bf16[64,2048]{1,0:T(8,128)(2,1)}, bf16[64,2048]{1,0:T(8,128)(2,1)}, u32[]{:S(2)}, u32[]{:S(2)}) %collective-permute-start.18) | collective-permute-done | bytes 262176 | tf_op jit(solution)/shard_map/ppermute | solution.py:261
  147.3 5.7 %plan_and_pack.3 = (bf16[256,2048]{1,0:T(8,128)(2,1)}, bf16[256,2048]{1,0:T(8,128)(2,1)}, bf16[256,128]{1,0:T(8,128)(2,1)}, bf16[256,4224]{1,0:T(8,128)(2,1)}, bf16[256,512]{1,0:T(8,128)(2,1)}) custom-call(s32[1]{0:T(128)} %bitcast.expert_ref, bf16[64,4224]{1,0:T(8,128)(2,1)} %collective-permute-done.7.refs_0_, ...), custom_call_target="tpu_custom_call" | custom-call | flops 1 | bytes 1 | tf_op jit(solution)/shard_map/plan_and_pack/pallas_call | solution.py:185
  153.1 3.2 %spread.3 = (bf16[64,2048]{1,0:T(8,128)(2,1)}, bf16[64,2048]{1,0:T(8,128)(2,1)}, bf16[64,2048]{1,0:T(8,128)(2,1)}, bf16[64,2048]{1,0:T(8,128)(2,1)}) custom-call(bf16[256,512]{1,0:T(8,128)(2,1)} %get-tuple-element.49.place_ref, bf16[128,2048]{1,0:T(8,128)(2,1)} %fusion.82.refs_0_, bf16[128,2048]{1,0:T(8,128)(2,1)} %copy-done.15, ...), custom_call_target="tpu_custom_call" | custom-call | flops 1 | bytes 1 | tf_op jit(solution)/shard_map/spread/pallas_call | solution.py:220
  158.4 3.0 %collective-permute-start.24 = (bf16[64,2048]{1,0:T(8,128)(2,1)}, bf16[64,2048]{1,0:T(8,128)(2,1)S(1)}, u32[]{:S(2)}, u32[]{:S(2)}) collective-permute-start(bf16[64,2048]{1,0:T(8,128)(2,1)} %get-tuple-element.58), channel_id=1, source_target_pairs={{0,16},{2,18},{4,20},{6,22},{8,24},{10,26},{12,28},{14,30},{16,0},... | collective-permute-start | bytes 786440 | tf_op jit(solution)/shard_map/ppermute | solution.py:261
  176.6 2.4 %fusion.36 = bf16[1,384,2048]{2,1,0:T(8,128)(2,1)} fusion(f32[384,2048]{1,0:T(8,128)S(1)} %copy-done.4, f32[512,768]{1,0:T(8,128)S(1)} %fusion.12, s32[]{:T(128)S(6)} %select_n.32, f32[512,768]{1,0:T(8,128)S(1)} %get-tuple-element.83, f32[512,768]{1,0:T(8,128)S(1)} %get-tuple-element.93, bf16[256,2048]{1,0:T(8,128)(2,1)S(1)} %get-tuple-element.79, ...), kind=kOutput, calls=%fused_computation.41 | convolution fusion | flops 813760512 | bytes 9177092 | tf_op jit(solution)/shard_map/dot_general | solution.py:55
  179.0 2.2 %fusion.86 = bf16[1,1024,768]{2,1,0:T(8,128)(2,1)} fusion(f32[1024,768]{1,0:T(8,128)S(1)} %copy-done.6, bf16[512,768]{1,0:T(8,128)(2,1)S(1)} %get-tuple-element.76, s32[]{:T(128)S(6)} %select_n.31, bf16[256,2048]{1,0:T(8,128)(2,1)S(1)} %copy-done.10, bf16[256,2048]{1,0:T(8,128)(2,1)S(1)} %get-tuple-element.80), kind=kOutput, calls=%fused_computation.73 | convolution fusion | flops 808976384 | bytes 7602180 | tf_op jit(solution)/shard_map/dot_general | solution.py:55
  181.2 4.2 %collective-permute-done.24 = bf16[64,2048]{1,0:T(8,128)(2,1)S(1)} collective-permute-done((bf16[64,2048]{1,0:T(8,128)(2,1)}, bf16[64,2048]{1,0:T(8,128)(2,1)S(1)}, u32[]{:S(2)}, u32[]{:S(2)}) %collective-permute-start.24) | collective-permute-done | bytes 262176 | tf_op jit(solution)/shard_map/ppermute | solution.py:261
  185.4 2.2 %add_convert_fusion.3 = (bf16[64,2048]{1,0:T(8,128)(2,1)}, bf16[64,2048]{1,0:T(8,128)(2,1)}) fusion(bf16[64,2048]{1,0:T(8,128)(2,1)S(1)} %collective-permute-done.25, bf16[64,2048]{1,0:T(8,128)(2,1)S(1)} %collective-permute-done.24, bf16[64,2048]{1,0:T(8,128)(2,1)S(1)} %collective-permute-done.23, bf16[64,2048]{1,0:T(8,128)(2,1)S(1)} %copy-done.20, ...), kind=kLoop, calls=%fused_computation.81 | loop fusion | flops 2097152 | bytes 2621440 | tf_op jit(solution)/shard_map/convert_element_type | solution.py:319
  (131 shorter events, 60.3 us)
Async XLA Ops:
  3.6 17.6 %collective-permute-start.2 = (bf16[64,4224]{1,0:T(8,128)(2,1)}, bf16[64,4224]{1,0:T(8,128)(2,1)}, u32[]{:S(2)}, u32[]{:S(2)}) collective-permute-start(bf16[64,4224]{1,0:T(8,128)(2,1)} %concatenate.24.refs_0_), channel_id=1, source_target_pairs={{0,8},{2,10},{4,12},{6,14},{8,16},{10,18},{12,20},{14,22},{16,24},... | collective-permute-start | bytes 1622024 | tf_op jit(solution)/shard_map/ppermute | solution.py:261
  6.7 16.1 %collective-permute-start.7 = (bf16[64,4224]{1,0:T(8,128)(2,1)}, bf16[64,4224]{1,0:T(8,128)(2,1)}, u32[]{:S(2)}, u32[]{:S(2)}) collective-permute-start(bf16[64,4224]{1,0:T(8,128)(2,1)} %concatenate.24.refs_0_), channel_id=1, source_target_pairs={{0,1},{1,0},{2,3},{3,2},{4,5},{5,4},{6,7},{7,6},{8,9},{9,8},{10,11... | collective-permute-start | bytes 1622024 | tf_op jit(solution)/shard_map/ppermute | solution.py:266
  8.2 14.6 %collective-permute-start = (bf16[64,4224]{1,0:T(8,128)(2,1)}, bf16[64,4224]{1,0:T(8,128)(2,1)}, u32[]{:S(2)}, u32[]{:S(2)}) collective-permute-start(bf16[64,4224]{1,0:T(8,128)(2,1)} %concatenate.24.refs_0_), channel_id=1, source_target_pairs={{0,4},{2,6},{4,0},{6,2},{8,12},{10,14},{12,8},{14,10},{16,20},{18,... | collective-permute-start | bytes 1622024 | tf_op jit(solution)/shard_map/ppermute | solution.py:258
  21.3 15.6 %collective-permute-start.6 = (bf16[64,4224]{1,0:T(8,128)(2,1)}, bf16[64,4224]{1,0:T(8,128)(2,1)}, u32[]{:S(2)}, u32[]{:S(2)}) collective-permute-start(bf16[64,4224]{1,0:T(8,128)(2,1)} %collective-permute-done.2.refs_1_), channel_id=1, source_target_pairs={{0,8},{2,10},{4,12},{6,14},{8,16},{10,18},{12,20},{14,22},{16,24},... | collective-permute-start | bytes 1622024 | tf_op jit(solution)/shard_map/ppermute | solution.py:261
  21.3 17.6 %collective-permute-start.4 = (bf16[64,4224]{1,0:T(8,128)(2,1)}, bf16[64,4224]{1,0:T(8,128)(2,1)}, u32[]{:S(2)}, u32[]{:S(2)}) collective-permute-start(bf16[64,4224]{1,0:T(8,128)(2,1)} %collective-permute-done.2.refs_1_), channel_id=1, source_target_pairs={{0,4},{2,6},{4,0},{6,2},{8,12},{10,14},{12,8},{14,10},{16,20},{18,... | collective-permute-start | bytes 1622024 | tf_op jit(solution)/shard_map/ppermute | solution.py:258
  36.9 14.7 %collective-permute-start.8 = (bf16[64,4224]{1,0:T(8,128)(2,1)}, bf16[64,4224]{1,0:T(8,128)(2,1)}, u32[]{:S(2)}, u32[]{:S(2)}) collective-permute-start(bf16[64,4224]{1,0:T(8,128)(2,1)} %collective-permute-done.6.refs_2_), channel_id=1, source_target_pairs={{0,8},{2,10},{4,12},{6,14},{8,16},{10,18},{12,20},{14,22},{16,24},... | collective-permute-start | bytes 1622024 | tf_op jit(solution)/shard_map/ppermute | solution.py:261
  36.9 15.7 %collective-permute-start.3 = (bf16[64,4224]{1,0:T(8,128)(2,1)}, bf16[64,4224]{1,0:T(8,128)(2,1)}, u32[]{:S(2)}, u32[]{:S(2)}) collective-permute-start(bf16[64,4224]{1,0:T(8,128)(2,1)} %collective-permute-done.2.refs_1_), channel_id=1, source_target_pairs={{0,1},{1,0},{2,3},{3,2},{4,5},{5,4},{6,7},{7,6},{8,9},{9,8},{10,11... | collective-permute-start | bytes 1622024 | tf_op jit(solution)/shard_map/ppermute | solution.py:266
  38.1 25.8 %collective-permute-start.1 = (bf16[64,4224]{1,0:T(8,128)(2,1)}, bf16[64,4224]{1,0:T(8,128)(2,1)}, u32[]{:S(2)}, u32[]{:S(2)}) collective-permute-start(bf16[64,4224]{1,0:T(8,128)(2,1)} %collective-permute-done.refs_4_), channel_id=1, source_target_pairs={{0,1},{1,0},{2,3},{3,2},{4,5},{5,4},{6,7},{7,6},{8,9},{9,8},{10,11... | collective-permute-start | bytes 1622024 | tf_op jit(solution)/shard_map/ppermute | solution.py:266
  38.9 34.0 %collective-permute-start.5 = (bf16[64,4224]{1,0:T(8,128)(2,1)}, bf16[64,4224]{1,0:T(8,128)(2,1)}, u32[]{:S(2)}, u32[]{:S(2)}) collective-permute-start(bf16[64,4224]{1,0:T(8,128)(2,1)} %collective-permute-done.4.refs_5_), channel_id=1, source_target_pairs={{0,1},{1,0},{2,3},{3,2},{4,5},{5,4},{6,7},{7,6},{8,9},{9,8},{10,11... | collective-permute-start | bytes 1622024 | tf_op jit(solution)/shard_map/ppermute | solution.py:266
  40.2 32.7 %collective-permute-start.9 = (bf16[64,4224]{1,0:T(8,128)(2,1)}, bf16[64,4224]{1,0:T(8,128)(2,1)}, u32[]{:S(2)}, u32[]{:S(2)}) collective-permute-start(bf16[64,4224]{1,0:T(8,128)(2,1)} %collective-permute-done.6.refs_2_), channel_id=1, source_target_pairs={{0,4},{2,6},{4,0},{6,2},{8,12},{10,14},{12,8},{14,10},{16,20},{18,... | collective-permute-start | bytes 1622024 | tf_op jit(solution)/shard_map/ppermute | solution.py:258
  51.5 21.4 %collective-permute-start.10 = (bf16[64,4224]{1,0:T(8,128)(2,1)}, bf16[64,4224]{1,0:T(8,128)(2,1)}, u32[]{:S(2)}, u32[]{:S(2)}) collective-permute-start(bf16[64,4224]{1,0:T(8,128)(2,1)} %collective-permute-done.8.refs_3_), channel_id=1, source_target_pairs={{0,4},{2,6},{4,0},{6,2},{8,12},{10,14},{12,8},{14,10},{16,20},{18,... | collective-permute-start | bytes 1622024 | tf_op jit(solution)/shard_map/ppermute | solution.py:258
  81.8 65.6 %collective-permute-start.26 = (bf16[256,4224]{1,0:T(8,128)(2,1)}, bf16[256,4224]{1,0:T(8,128)(2,1)}, u32[]{:S(2)}, u32[]{:S(2)}) collective-permute-start(bf16[256,4224]{1,0:T(8,128)(2,1)} %pad_maximum_fusion.2), channel_id=1, source_target_pairs={{0,1},{1,0},{2,3},{3,2},{4,5},{5,4},{6,7},{7,6},{8,9},{9,8},{10,11... | collective-permute-start | bytes 6488072 | tf_op jit(solution)/shard_map/ppermute | solution.py:266
  93.3 14.8 %collective-permute-start.14 = (bf16[128,2048]{1,0:T(8,128)(2,1)S(1)}, bf16[128,2048]{1,0:T(8,128)(2,1)S(1)}, u32[]{:S(2)}, u32[]{:S(2)}) collective-permute-start(bf16[128,2048]{1,0:T(8,128)(2,1)S(1)} %fusion.64), channel_id=1, source_target_pairs={{0,4},{2,6},{4,0},{6,2},{8,12},{10,14},{12,8},{14,10},{16,20},{18,... | collective-permute-start | bytes 1572872 | tf_op jit(solution)/shard_map/ppermute | solution.py:258
  100.4 19.0 %collective-permute-start.16 = (bf16[128,2048]{1,0:T(8,128)(2,1)S(1)}, bf16[128,2048]{1,0:T(8,128)(2,1)S(1)}, u32[]{:S(2)}, u32[]{:S(2)}) collective-permute-start(bf16[128,2048]{1,0:T(8,128)(2,1)S(1)} %collective-permute-done.15), channel_id=1, source_target_pairs={{0,4},{2,6},{4,0},{6,2},{8,12},{10,14},{12,8},{14,10},{16,20},{18,... | collective-permute-start | bytes 1572872 | tf_op jit(solution)/shard_map/ppermute | solution.py:258
  102.7 16.7 %collective-permute-start.21 = (bf16[128,2048]{1,0:T(8,128)(2,1)S(1)}, bf16[128,2048]{1,0:T(8,128)(2,1)}, u32[]{:S(2)}, u32[]{:S(2)}) collective-permute-start(bf16[128,2048]{1,0:T(8,128)(2,1)S(1)} %fusion.73), channel_id=1, source_target_pairs={{0,2},{2,0},{4,6},{6,4},{8,10},{10,8},{12,14},{14,12},{16,18},{18,... | collective-permute-start | bytes 1572872 | tf_op jit(solution)/shard_map/ppermute | solution.py:255
  108.1 27.0 %collective-permute-start.20 = (bf16[128,2048]{1,0:T(8,128)(2,1)}, bf16[128,2048]{1,0:T(8,128)(2,1)}, u32[]{:S(2)}, u32[]{:S(2)}) collective-permute-start(bf16[128,2048]{1,0:T(8,128)(2,1)} %fusion.76), channel_id=1, source_target_pairs={{0,4},{2,6},{4,0},{6,2},{8,12},{10,14},{12,8},{14,10},{16,20},{18,... | collective-permute-start | bytes 1572872 | tf_op jit(solution)/shard_map/ppermute | solution.py:258
  119.4 28.0 %collective-permute-start.22 = (bf16[128,2048]{1,0:T(8,128)(2,1)}, bf16[128,2048]{1,0:T(8,128)(2,1)}, u32[]{:S(2)}, u32[]{:S(2)}) collective-permute-start(bf16[128,2048]{1,0:T(8,128)(2,1)} %collective-permute-done.21), channel_id=1, source_target_pairs={{0,4},{2,6},{4,0},{6,2},{8,12},{10,14},{12,8},{14,10},{16,20},{18,... | collective-permute-start | bytes 1572872 | tf_op jit(solution)/shard_map/ppermute | solution.py:258
  124.5 13.9 %collective-permute-start.17 = (bf16[64,2048]{1,0:T(8,128)(2,1)}, bf16[64,2048]{1,0:T(8,128)(2,1)}, u32[]{:S(2)}, u32[]{:S(2)}) collective-permute-start(bf16[64,2048]{1,0:T(8,128)(2,1)} %get-tuple-element.51), channel_id=1, source_target_pairs={{0,24},{2,26},{4,28},{6,30},{8,0},{10,2},{12,4},{14,6},{16,8},{18,... | collective-permute-start | bytes 786440 | tf_op jit(solution)/shard_map/ppermute | solution.py:261
  128.1 19.3 %collective-permute-start.18 = (bf16[64,2048]{1,0:T(8,128)(2,1)}, bf16[64,2048]{1,0:T(8,128)(2,1)}, u32[]{:S(2)}, u32[]{:S(2)}) collective-permute-start(bf16[64,2048]{1,0:T(8,128)(2,1)} %get-tuple-element.52), channel_id=1, source_target_pairs={{0,16},{2,18},{4,20},{6,22},{8,24},{10,26},{12,28},{14,30},{16,0},... | collective-permute-start | bytes 786440 | tf_op jit(solution)/shard_map/ppermute | solution.py:261
  135.1 12.2 %collective-permute-start.19 = (bf16[64,2048]{1,0:T(8,128)(2,1)S(1)}, bf16[64,2048]{1,0:T(8,128)(2,1)}, u32[]{:S(2)}, u32[]{:S(2)}) collective-permute-start(bf16[64,2048]{1,0:T(8,128)(2,1)S(1)} %copy-done.25), channel_id=1, source_target_pairs={{0,8},{2,10},{4,12},{6,14},{8,16},{10,18},{12,20},{14,22},{16,24},... | collective-permute-start | bytes 786440 | tf_op jit(solution)/shard_map/ppermute | solution.py:261
  153.0 10.4 %collective-permute-start.27 = (bf16[256,4224]{1,0:T(8,128)(2,1)}, bf16[256,4224]{1,0:T(8,128)(2,1)}, u32[]{:S(2)}, u32[]{:S(2)}) collective-permute-start(bf16[256,4224]{1,0:T(8,128)(2,1)} %get-tuple-element.65), channel_id=1, source_target_pairs={{0,2},{2,0},{4,6},{6,4},{8,10},{10,8},{12,14},{14,12},{16,18},{18,... | collective-permute-start | bytes 6488072 | tf_op jit(solution)/shard_map/ppermute | solution.py:255
  156.3 22.7 %collective-permute-start.23 = (bf16[64,2048]{1,0:T(8,128)(2,1)}, bf16[64,2048]{1,0:T(8,128)(2,1)S(1)}, u32[]{:S(2)}, u32[]{:S(2)}) collective-permute-start(bf16[64,2048]{1,0:T(8,128)(2,1)} %get-tuple-element.57), channel_id=1, source_target_pairs={{0,24},{2,26},{4,28},{6,30},{8,0},{10,2},{12,4},{14,6},{16,8},{18,... | collective-permute-start | bytes 786440 | tf_op jit(solution)/shard_map/ppermute | solution.py:261
  158.4 27.1 %collective-permute-start.24 = (bf16[64,2048]{1,0:T(8,128)(2,1)}, bf16[64,2048]{1,0:T(8,128)(2,1)S(1)}, u32[]{:S(2)}, u32[]{:S(2)}) collective-permute-start(bf16[64,2048]{1,0:T(8,128)(2,1)} %get-tuple-element.58), channel_id=1, source_target_pairs={{0,16},{2,18},{4,20},{6,22},{8,24},{10,26},{12,28},{14,30},{16,0},... | collective-permute-start | bytes 786440 | tf_op jit(solution)/shard_map/ppermute | solution.py:261
  161.4 24.0 %collective-permute-start.25 = (bf16[64,2048]{1,0:T(8,128)(2,1)}, bf16[64,2048]{1,0:T(8,128)(2,1)S(1)}, u32[]{:S(2)}, u32[]{:S(2)}) collective-permute-start(bf16[64,2048]{1,0:T(8,128)(2,1)} %get-tuple-element.59), channel_id=1, source_target_pairs={{0,8},{2,10},{4,12},{6,14},{8,16},{10,18},{12,20},{14,22},{16,24},... | collective-permute-start | bytes 786440 | tf_op jit(solution)/shard_map/ppermute | solution.py:261
  (30 other events, 207.1 us)

commit v16 on v14

--- a/solution.py
+++ b/solution.py
@@ -229,12 +229,31 @@
     )(place, *parts)
 
 
-def split3(value):
-    high = value.astype(BF)
-    rest = value - high.astype(F32)
-    mid = rest.astype(BF)
-    low = (rest - mid.astype(F32)).astype(BF)
-    return high, mid, low
+def pair_up(tokens, cots, route_ids, gate_probs, experts):
+    tok_rows, features = tokens.shape
+
+    def body(tokens_ref, cots_ref, ids_ref, probs_ref, out_ref):
+        out_ref[:, :features] = tokens_ref[...]
+        out_ref[:, features : 2 * features] = cots_ref[...]
+        lane = lax.broadcasted_iota(jnp.int32, (tok_rows, LANES), 1)
+        share = jnp.zeros((tok_rows, LANES), F32)
+        for k in range(ids_ref.shape[1]):
+            chosen = ids_ref[:, k : k + 1] == lane % experts
+            share = share + jnp.where(chosen, probs_ref[:, k : k + 1], 0.0)
+        high = share.astype(BF).astype(F32)
+        mid = (share - high).astype(BF).astype(F32)
+        low = share - high - mid
+        term = jnp.where(lane < experts, high, jnp.where(lane < 2 * experts, mid, low))
+        out_ref[:, 2 * features :] = jnp.where(lane < 3 * experts, term, 0.0).astype(BF)
+
+    out = jax.ShapeDtypeStruct((tok_rows, 2 * features + LANES), BF)
+    return pl.pallas_call(
+        body,
+        out_shape=out,
+        compiler_params=params(),
+        cost_estimate=SMALL,
+        name="pair_up",
+    )(tokens, cots, route_ids, gate_probs)
 
 
 def after(value, *earlier):
@@ -245,8 +264,7 @@
     experts = lax.axis_size("expert")
     tok_rows, features = tokens.shape
     hidden = w_gate.shape[2]
-    top_count = route_ids.shape[1]
-    capacity = max(2, tok_rows * top_count * 4 // (3 * experts))
+    capacity = max(2, tok_rows * route_ids.shape[1] * 4 // (3 * experts))
     expert = lax.axis_index("expert").astype(jnp.int32)
     replica = lax.axis_index("replica").astype(jnp.int32)
     w_gate, w_up, w_down = w_gate[0], w_up[0], w_down[0]
@@ -265,11 +283,7 @@
     def to_y(rows):
         return lax.ppermute(rows, "replica", [(0, 1), (1, 0)])
 
-    chosen = route_ids[:, :, None] == jnp.arange(experts, dtype=jnp.int32)
-    share = jnp.sum(jnp.where(chosen, gate_probs[:, :, None], 0.0), axis=1)
-    pad = jnp.zeros((tok_rows, LANES - 3 * experts), BF)
-
-    near = [jnp.concatenate([tokens, out_cot, *split3(share), pad], axis=1)]
+    near = [pair_up(tokens, out_cot, route_ids, gate_probs, experts)]
     far, relay = [to_x(near[0])], [to_y(near[0])]
     near.append(to_z(near[0], 1))
     far.append(to_x(near[1]))
@@ -330,11 +344,11 @@
     def token_grads(rows, *earlier):
         return input_rows(*after((d_gate[rows], d_up[rows]), *earlier), w_gate, w_up)
 
-    grad_parts = leave(token_grads, parts[2:3], parts[3:4])
+    grad_parts = leave(token_grads, parts[2:3])
     chunks = home(after(place, grad_parts[0], grad_parts[1]), parts)
     own_grads = after((cot, d_gate, d_up), chunks[0])
     own = grads(own_x, act, *own_grads)
-    packed = plan(other_pieces, *own, *grad_parts[2:], *chunks[1:])
+    packed = plan(other_pieces, *own, *grad_parts[2:], *chunks[1:3])
     grad_chunks = home(after(place, packed[-1]), grad_parts)
 
     x, weight, pre_gate, pre_up, act, cot = enter(packed)

time: 176 us -> 176 us (level)
  Pallas kernels: 18 us -> 20 us
    pallas_call x0 -> x1, Pallas kernels: none -> 2.02 us  [pair_up(): pl.pallas_call(body, out_shape=out, compiler_params=params(), cost_estima...]
    unnamed x71 -> x69, local copies, waits for them, and re-layouts: 7.65 us -> 9.63 us
    concatenate x1 -> x0, local copies, waits for them, and re-layouts: 1.9 us -> none  [dense_plan(): near = [jnp.concatenate([tokens, out_cot, *split3(share), pad], axis=1)]]
where the time goes in v16:
time: 176 us
  waiting for transfers between devices  73.5 us (42%)
  matrix products  34.7 us (20%)
  starting transfers between devices  24 us (14%)
  Pallas kernels  20 us (11%)
  local copies, waits for them, and re-layouts  17.7 us (10%)
  other arithmetic  4.59 us (3%)
    ppermute x9, waiting for transfers between devices, to_z(): lax.ppermute(rows, 'expert', [(i, (i + 4 * step) % experts) for i in rang...  47.4 us
    ppermute x8, waiting for transfers between devices, to_x(): return lax.ppermute(rows, 'expert', [(i, i ^ 2) for i in range(experts)])  21.7 us
    dot_general x6, matrix products, outer_sum(): lax.dot_general(left, right, (((0,), (0,)), ((), ())), preferred_element_...  13.9 us
    pallas_call x2, Pallas kernels, plan_and_pack(): pl.pallas_call(body, grid_spec=pltpu.PrefetchScalarGridSpec(num_scalar_pr...  11.5 us
    unnamed x69, local copies, waits for them, and re-layouts  9.63 us
    dot_general x6, matrix products, dot(): return jnp.dot(left, right, preferred_element_type=F32)  9.41 us
    ppermute x9, starting transfers between devices, to_z(): lax.ppermute(rows, 'expert', [(i, (i + 4 * step) % experts) for i in rang...  8.55 us
    ppermute x8, starting transfers between devices, to_x(): return lax.ppermute(rows, 'expert', [(i, i ^ 2) for i in range(experts)])  8.55 us
  transfers between devices with their start and end apart: 26, of which 10 were waited for; matrix products, arithmetic and copies ran while one was open for 25% of the time, Pallas kernels for 4%

profile of v16, /device:TPU:0, one launch (start us, length us, event | category | flops | bytes accessed | tf_op | source)
XLA Modules:
  0.0 175.7 jit_solution(1230579817085321837)
XLA Ops:
  3.6 2.0 %pair_up.1.refs_0_ = bf16[64,4224]{1,0:T(8,128)(2,1)} custom-call(bf16[64,2048]{1,0:T(8,128)(2,1)} %tokens_ref.1, bf16[64,2048]{1,0:T(8,128)(2,1)} %cots_ref.1, s32[64,6]{1,0:T(8,128)} %copy.12.ids_ref, f32[64,6]{1,0:T(8,128)} %copy.13.probs_ref), custom_call_target="tpu_custom_call" | custom-call | flops 1 | bytes 1 | tf_op jit(solution)/shard_map/pair_up/pallas_call | solution.py:250
  5.6 3.0 %collective-permute-start.2 = (bf16[64,4224]{1,0:T(8,128)(2,1)}, bf16[64,4224]{1,0:T(8,128)(2,1)}, u32[]{:S(2)}, u32[]{:S(2)}) collective-permute-start(bf16[64,4224]{1,0:T(8,128)(2,1)} %pair_up.1.refs_0_), channel_id=1, source_target_pairs={{0,8},{2,10},{4,12},{6,14},{8,16},{10,18},{12,20},{14,22},{16,24},... | collective-permute-start | bytes 1622024 | tf_op jit(solution)/shard_map/ppermute | solution.py:279
  11.6 11.6 %collective-permute-done.2.refs_1_ = bf16[64,4224]{1,0:T(8,128)(2,1)} collective-permute-done((bf16[64,4224]{1,0:T(8,128)(2,1)}, bf16[64,4224]{1,0:T(8,128)(2,1)}, u32[]{:S(2)}, u32[]{:S(2)}) %collective-permute-start.2) | collective-permute-done | bytes 540704 | tf_op jit(solution)/shard_map/ppermute | solution.py:279
  26.8 12.0 %collective-permute-done.6.refs_2_ = bf16[64,4224]{1,0:T(8,128)(2,1)} collective-permute-done((bf16[64,4224]{1,0:T(8,128)(2,1)}, bf16[64,4224]{1,0:T(8,128)(2,1)}, u32[]{:S(2)}, u32[]{:S(2)}) %collective-permute-start.6) | collective-permute-done | bytes 540704 | tf_op jit(solution)/shard_map/ppermute | solution.py:279
  43.5 10.6 %collective-permute-done.8.refs_3_ = bf16[64,4224]{1,0:T(8,128)(2,1)S(1)} collective-permute-done((bf16[64,4224]{1,0:T(8,128)(2,1)}, bf16[64,4224]{1,0:T(8,128)(2,1)S(1)}, u32[]{:S(2)}, u32[]{:S(2)}) %collective-permute-start.8) | collective-permute-done | bytes 540704 | tf_op jit(solution)/shard_map/ppermute | solution.py:279
  56.9 8.3 %collective-permute-done.10.refs_7_ = bf16[64,4224]{1,0:T(8,128)(2,1)S(1)} collective-permute-done((bf16[64,4224]{1,0:T(8,128)(2,1)S(1)}, bf16[64,4224]{1,0:T(8,128)(2,1)S(1)}, u32[]{:S(2)}, u32[]{:S(2)}) %collective-permute-start.10) | collective-permute-done | bytes 540704 | tf_op jit(solution)/shard_map/ppermute | solution.py:276
  66.2 5.7 %plan_and_pack.2 = (bf16[256,2048]{1,0:T(8,128)(2,1)}, bf16[256,2048]{1,0:T(8,128)(2,1)}, bf16[256,128]{1,0:T(8,128)(2,1)}, bf16[256,4224]{1,0:T(8,128)(2,1)}, bf16[256,512]{1,0:T(8,128)(2,1)}) custom-call(s32[1]{0:T(128)} %bitcast.expert_ref, bf16[64,4224]{1,0:T(8,128)(2,1)} %pair_up.1.refs_0_, bf16[64,4224]{1,0:T(8,128)(2,1)} %collective-permute-done.2.refs_1_, ...), custom_call_target="tpu_custom_call" | custom-call | flops 1 | bytes 1 | tf_op jit(solution)/shard_map/plan_and_pack/pallas_call | solution.py:185
  71.9 4.4 %collective-permute-done.11 = bf16[256,4224]{1,0:T(8,128)(2,1)S(1)} collective-permute-done((bf16[256,4224]{1,0:T(8,128)(2,1)}, bf16[256,4224]{1,0:T(8,128)(2,1)S(1)}, u32[]{:S(2)}, u32[]{:S(2)}) %collective-permute-start.11) | collective-permute-done | bytes 2162720 | tf_op jit(solution)/shard_map/ppermute | solution.py:273
  88.0 2.2 %multiply_convert_fusion.4 = (bf16[512,768]{1,0:T(8,128)(2,1)S(1)}, bf16[512,768]{1,0:T(8,128)(2,1)S(1)}) fusion(f32[512,768]{1,0:T(8,128)S(1)} %fusion.22, f32[512,768]{1,0:T(8,128)S(1)} %get-tuple-element.96, bf16[512,2048]{1,0:T(8,128)(2,1)S(1)} %multiply_convert_fusion.1, bf16[1,768,2048]{2,1,0:T(8,128)(2,1)S(1)} %copy-done.28), kind=kOutput, calls=%fused_computation.48 | convolution fusion | flops 1615724544 | bytes 9961472 | tf_op jit(solution)/shard_map/dot_general | solution.py:41
  92.3 2.1 %fusion.43 = bf16[256,2048]{1,0:T(8,128)(2,1)} fusion(f32[256,2048]{1,0:T(8,128)S(1)} %fusion.10, bf16[256,768]{1,0:T(8,128)(2,1)S(1)} %get-tuple-element.53, bf16[1,2048,768]{2,1,0:T(8,128)(2,1)S(1)} %copy-done), kind=kOutput, calls=%fused_computation.36 | convolution fusion | flops 806354944 | bytes 6684672 | tf_op jit(solution)/shard_map/dot_general | solution.py:49
  97.0 5.2 %collective-permute-done.13.refs_2_ = bf16[128,2048]{1,0:T(8,128)(2,1)} collective-permute-done((bf16[128,2048]{1,0:T(8,128)(2,1)}, bf16[128,2048]{1,0:T(8,128)(2,1)}, u32[]{:S(2)}, u32[]{:S(2)}) %collective-permute-start.13) | collective-permute-done | bytes 524320 | tf_op jit(solution)/shard_map/ppermute | solution.py:276
  102.1 3.2 %fusion.12 = f32[256,2048]{1,0:T(8,128)S(1)} fusion(bf16[256,768]{1,0:T(8,128)(2,1)} %get-tuple-element.52, bf16[1,2048,768]{2,1,0:T(8,128)(2,1)} %param.12), kind=kOutput, calls=%fused_computation.14 | convolution fusion | flops 805306368 | bytes 5636096 | tf_op jit(solution)/shard_map/dot_general | solution.py:50
  107.1 6.3 %collective-permute-done.15.refs_3_ = bf16[128,2048]{1,0:T(8,128)(2,1)} collective-permute-done((bf16[128,2048]{1,0:T(8,128)(2,1)S(1)}, bf16[128,2048]{1,0:T(8,128)(2,1)}, u32[]{:S(2)}, u32[]{:S(2)}) %collective-permute-start.15) | collective-permute-done | bytes 524320 | tf_op jit(solution)/shard_map/ppermute | solution.py:276
  113.4 3.2 %spread.2 = (bf16[64,2048]{1,0:T(8,128)(2,1)}, bf16[64,2048]{1,0:T(8,128)(2,1)}, bf16[64,2048]{1,0:T(8,128)(2,1)}, bf16[64,2048]{1,0:T(8,128)(2,1)}) custom-call(bf16[256,512]{1,0:T(8,128)(2,1)} %get-tuple-element.55.place_ref, bf16[256,2048]{1,0:T(8,128)(2,1)} %copy-done.7, bf16[256,2048]{1,0:T(8,128)(2,1)} %collective-permute-done.12.refs_1_, ...), custom_call_target="tpu_custom_call" | custom-call | flops 1 | bytes 1 | tf_op jit(solution)/shard_map/spread/pallas_call | solution.py:220
  118.7 2.9 %fusion.59 = f32[384,2048]{1,0:T(8,128)S(1)} fusion(bf16[512,2048]{1,0:T(8,128)(2,1)} %copy-done.3, bf16[512,768]{1,0:T(8,128)(2,1)} %copy-done.26, s32[]{:T(128)S(6)} %select_n.27), kind=kOutput, calls=%fused_computation.64 | convolution fusion | flops 805306368 | bytes 5636100 | tf_op jit(solution)/shard_map/dot_general | solution.py:55
  121.7 2.6 %fusion.72 = f32[1024,768]{1,0:T(8,128)} fusion(bf16[512,768]{1,0:T(8,128)(2,1)S(1)} %copy-done.19, s32[]{:T(128)S(6)} %select_n.26, bf16[256,2048]{1,0:T(8,128)(2,1)S(1)} %copy-done.31, bf16[256,2048]{1,0:T(8,128)(2,1)S(1)} %copy-done.13), kind=kOutput, calls=%fused_computation.84 | convolution fusion | flops 807403520 | bytes 6029316 | tf_op jit(solution)/shard_map/dot_general | solution.py:55
  124.3 2.7 %fusion.70 = f32[1024,768]{1,0:T(8,128)} fusion(bf16[512,768]{1,0:T(8,128)(2,1)S(1)} %copy-done.17, s32[]{:T(128)S(6)} %select_n.26, bf16[256,2048]{1,0:T(8,128)(2,1)S(1)} %copy-done.31, bf16[256,2048]{1,0:T(8,128)(2,1)S(1)} %copy-done.13), kind=kOutput, calls=%fused_computation.83 | convolution fusion | flops 807403520 | bytes 6029316 | tf_op jit(solution)/shard_map/dot_general | solution.py:55
  127.1 5.9 %collective-permute-done.17 = bf16[64,2048]{1,0:T(8,128)(2,1)S(1)} collective-permute-done((bf16[64,2048]{1,0:T(8,128)(2,1)}, bf16[64,2048]{1,0:T(8,128)(2,1)S(1)}, u32[]{:S(2)}, u32[]{:S(2)}) %collective-permute-start.17) | collective-permute-done | bytes 262176 | tf_op jit(solution)/shard_map/ppermute | solution.py:279
  134.9 5.9 %plan_and_pack.3 = (bf16[256,2048]{1,0:T(8,128)(2,1)}, bf16[256,2048]{1,0:T(8,128)(2,1)}, bf16[256,128]{1,0:T(8,128)(2,1)}, bf16[256,4224]{1,0:T(8,128)(2,1)}, bf16[256,512]{1,0:T(8,128)(2,1)}) custom-call(s32[1]{0:T(128)} %bitcast.expert_ref, bf16[64,4224]{1,0:T(8,128)(2,1)} %collective-permute-done.7.refs_0_, ...), custom_call_target="tpu_custom_call" | custom-call | flops 1 | bytes 1 | tf_op jit(solution)/shard_map/plan_and_pack/pallas_call | solution.py:185
  140.9 3.2 %spread.3 = (bf16[64,2048]{1,0:T(8,128)(2,1)}, bf16[64,2048]{1,0:T(8,128)(2,1)}, bf16[64,2048]{1,0:T(8,128)(2,1)}, bf16[64,2048]{1,0:T(8,128)(2,1)}) custom-call(bf16[256,512]{1,0:T(8,128)(2,1)} %get-tuple-element.55.place_ref, bf16[256,2048]{1,0:T(8,128)(2,1)} %copy-done.4, bf16[256,2048]{1,0:T(8,128)(2,1)} %collective-permute-done.14.refs_1_, ...), custom_call_target="tpu_custom_call" | custom-call | flops 1 | bytes 1 | tf_op jit(solution)/shard_map/spread/pallas_call | solution.py:220
  144.2 3.8 %collective-permute-start.21 = (bf16[64,2048]{1,0:T(8,128)(2,1)}, bf16[64,2048]{1,0:T(8,128)(2,1)S(1)}, u32[]{:S(2)}, u32[]{:S(2)}) collective-permute-start(bf16[64,2048]{1,0:T(8,128)(2,1)} %get-tuple-element.61), channel_id=1, source_target_pairs={{0,24},{2,26},{4,28},{6,30},{8,0},{10,2},{12,4},{14,6},{16,8},{18,... | collective-permute-start | bytes 786440 | tf_op jit(solution)/shard_map/ppermute | solution.py:279
  162.4 2.3 %fusion.36 = bf16[1,384,2048]{2,1,0:T(8,128)(2,1)} fusion(f32[384,2048]{1,0:T(8,128)S(1)} %fusion.59, f32[512,768]{1,0:T(8,128)S(1)} %fusion.8, s32[]{:T(128)S(6)} %select_n.27, f32[512,768]{1,0:T(8,128)S(1)} %get-tuple-element.87, f32[512,768]{1,0:T(8,128)S(1)} %get-tuple-element.97, bf16[256,2048]{1,0:T(8,128)(2,1)S(1)} %get-tuple-element.83, ...), kind=kOutput, calls=%fused_computation.33 | convolution fusion | flops 813760512 | bytes 9177092 | tf_op jit(solution)/shard_map/dot_general | solution.py:55
  164.7 2.2 %fusion.50 = bf16[1,1024,768]{2,1,0:T(8,128)(2,1)} fusion(f32[1024,768]{1,0:T(8,128)S(1)} %copy-done.5, bf16[512,768]{1,0:T(8,128)(2,1)S(1)} %get-tuple-element.80, s32[]{:T(128)S(6)} %select_n.26, bf16[256,2048]{1,0:T(8,128)(2,1)S(1)} %copy-done.14, bf16[256,2048]{1,0:T(8,128)(2,1)S(1)} %get-tuple-element.84), kind=kOutput, calls=%fused_computation.52 | convolution fusion | flops 808976384 | bytes 7602180 | tf_op jit(solution)/shard_map/dot_general | solution.py:55
  166.9 7.2 %collective-permute-done.22 = bf16[64,2048]{1,0:T(8,128)(2,1)S(1)} collective-permute-done((bf16[64,2048]{1,0:T(8,128)(2,1)}, bf16[64,2048]{1,0:T(8,128)(2,1)S(1)}, u32[]{:S(2)}, u32[]{:S(2)}) %collective-permute-start.22) | collective-permute-done | bytes 262176 | tf_op jit(solution)/shard_map/ppermute | solution.py:279
  (138 shorter events, 55.9 us)
Async XLA Ops:
  5.6 17.6 %collective-permute-start.2 = (bf16[64,4224]{1,0:T(8,128)(2,1)}, bf16[64,4224]{1,0:T(8,128)(2,1)}, u32[]{:S(2)}, u32[]{:S(2)}) collective-permute-start(bf16[64,4224]{1,0:T(8,128)(2,1)} %pair_up.1.refs_0_), channel_id=1, source_target_pairs={{0,8},{2,10},{4,12},{6,14},{8,16},{10,18},{12,20},{14,22},{16,24},... | collective-permute-start | bytes 1622024 | tf_op jit(solution)/shard_map/ppermute | solution.py:279
  8.6 17.6 %collective-permute-start = (bf16[64,4224]{1,0:T(8,128)(2,1)}, bf16[64,4224]{1,0:T(8,128)(2,1)}, u32[]{:S(2)}, u32[]{:S(2)}) collective-permute-start(bf16[64,4224]{1,0:T(8,128)(2,1)} %pair_up.1.refs_0_), channel_id=1, source_target_pairs={{0,4},{2,6},{4,0},{6,2},{8,12},{10,14},{12,8},{14,10},{16,20},{18,... | collective-permute-start | bytes 1622024 | tf_op jit(solution)/shard_map/ppermute | solution.py:276
  10.1 16.6 %collective-permute-start.7 = (bf16[64,4224]{1,0:T(8,128)(2,1)}, bf16[64,4224]{1,0:T(8,128)(2,1)}, u32[]{:S(2)}, u32[]{:S(2)}) collective-permute-start(bf16[64,4224]{1,0:T(8,128)(2,1)} %pair_up.1.refs_0_), channel_id=1, source_target_pairs={{0,1},{1,0},{2,3},{3,2},{4,5},{5,4},{6,7},{7,6},{8,9},{9,8},{10,11... | collective-permute-start | bytes 1622024 | tf_op jit(solution)/shard_map/ppermute | solution.py:284
  23.2 15.6 %collective-permute-start.6 = (bf16[64,4224]{1,0:T(8,128)(2,1)}, bf16[64,4224]{1,0:T(8,128)(2,1)}, u32[]{:S(2)}, u32[]{:S(2)}) collective-permute-start(bf16[64,4224]{1,0:T(8,128)(2,1)} %collective-permute-done.2.refs_1_), channel_id=1, source_target_pairs={{0,8},{2,10},{4,12},{6,14},{8,16},{10,18},{12,20},{14,22},{16,24},... | collective-permute-start | bytes 1622024 | tf_op jit(solution)/shard_map/ppermute | solution.py:279
  23.2 16.8 %collective-permute-start.4 = (bf16[64,4224]{1,0:T(8,128)(2,1)}, bf16[64,4224]{1,0:T(8,128)(2,1)}, u32[]{:S(2)}, u32[]{:S(2)}) collective-permute-start(bf16[64,4224]{1,0:T(8,128)(2,1)} %collective-permute-done.2.refs_1_), channel_id=1, source_target_pairs={{0,4},{2,6},{4,0},{6,2},{8,12},{10,14},{12,8},{14,10},{16,20},{18,... | collective-permute-start | bytes 1622024 | tf_op jit(solution)/shard_map/ppermute | solution.py:276
  24.7 41.4 %collective-permute-start.3 = (bf16[64,4224]{1,0:T(8,128)(2,1)}, bf16[64,4224]{1,0:T(8,128)(2,1)}, u32[]{:S(2)}, u32[]{:S(2)}) collective-permute-start(bf16[64,4224]{1,0:T(8,128)(2,1)} %collective-permute-done.2.refs_1_), channel_id=1, source_target_pairs={{0,1},{1,0},{2,3},{3,2},{4,5},{5,4},{6,7},{7,6},{8,9},{9,8},{10,11... | collective-permute-start | bytes 1622024 | tf_op jit(solution)/shard_map/ppermute | solution.py:284
  26.3 39.8 %collective-permute-start.1 = (bf16[64,4224]{1,0:T(8,128)(2,1)}, bf16[64,4224]{1,0:T(8,128)(2,1)}, u32[]{:S(2)}, u32[]{:S(2)}) collective-permute-start(bf16[64,4224]{1,0:T(8,128)(2,1)} %collective-permute-done.refs_4_), channel_id=1, source_target_pairs={{0,1},{1,0},{2,3},{3,2},{4,5},{5,4},{6,7},{7,6},{8,9},{9,8},{10,11... | collective-permute-start | bytes 1622024 | tf_op jit(solution)/shard_map/ppermute | solution.py:284
  38.8 17.1 %collective-permute-start.9 = (bf16[64,4224]{1,0:T(8,128)(2,1)}, bf16[64,4224]{1,0:T(8,128)(2,1)S(1)}, u32[]{:S(2)}, u32[]{:S(2)}) collective-permute-start(bf16[64,4224]{1,0:T(8,128)(2,1)} %collective-permute-done.6.refs_2_), channel_id=1, source_target_pairs={{0,4},{2,6},{4,0},{6,2},{8,12},{10,14},{12,8},{14,10},{16,20},{18,... | collective-permute-start | bytes 1622024 | tf_op jit(solution)/shard_map/ppermute | solution.py:276
  40.1 14.0 %collective-permute-start.8 = (bf16[64,4224]{1,0:T(8,128)(2,1)}, bf16[64,4224]{1,0:T(8,128)(2,1)S(1)}, u32[]{:S(2)}, u32[]{:S(2)}) collective-permute-start(bf16[64,4224]{1,0:T(8,128)(2,1)} %collective-permute-done.6.refs_2_), channel_id=1, source_target_pairs={{0,8},{2,10},{4,12},{6,14},{8,16},{10,18},{12,20},{14,22},{16,24},... | collective-permute-start | bytes 1622024 | tf_op jit(solution)/shard_map/ppermute | solution.py:279
  40.1 26.0 %collective-permute-start.5 = (bf16[64,4224]{1,0:T(8,128)(2,1)}, bf16[64,4224]{1,0:T(8,128)(2,1)}, u32[]{:S(2)}, u32[]{:S(2)}) collective-permute-start(bf16[64,4224]{1,0:T(8,128)(2,1)} %collective-permute-done.4.refs_5_), channel_id=1, source_target_pairs={{0,1},{1,0},{2,3},{3,2},{4,5},{5,4},{6,7},{7,6},{8,9},{9,8},{10,11... | collective-permute-start | bytes 1622024 | tf_op jit(solution)/shard_map/ppermute | solution.py:284
  54.1 11.1 %collective-permute-start.10 = (bf16[64,4224]{1,0:T(8,128)(2,1)S(1)}, bf16[64,4224]{1,0:T(8,128)(2,1)S(1)}, u32[]{:S(2)}, u32[]{:S(2)}) collective-permute-start(bf16[64,4224]{1,0:T(8,128)(2,1)S(1)} %collective-permute-done.8.refs_3_), channel_id=1, source_target_pairs={{0,4},{2,6},{4,0},{6,2},{8,12},{10,14},{12,8},{14,10},{16,20},{18,... | collective-permute-start | bytes 1622024 | tf_op jit(solution)/shard_map/ppermute | solution.py:276
  83.6 51.3 %collective-permute-start.24 = (bf16[256,4224]{1,0:T(8,128)(2,1)}, bf16[256,4224]{1,0:T(8,128)(2,1)}, u32[]{:S(2)}, u32[]{:S(2)}) collective-permute-start(bf16[256,4224]{1,0:T(8,128)(2,1)} %constant_dynamic-update-slice_fusion), channel_id=1, source_target_pairs={{0,1},{1,0},{2,3},{3,2},{4,5},{5,4},{6,7},{7,6},{8,9},{9,8},{10,11... | collective-permute-start | bytes 6488072 | tf_op jit(solution)/shard_map/ppermute | solution.py:284
  87.1 15.1 %collective-permute-start.13 = (bf16[128,2048]{1,0:T(8,128)(2,1)}, bf16[128,2048]{1,0:T(8,128)(2,1)}, u32[]{:S(2)}, u32[]{:S(2)}) collective-permute-start(bf16[128,2048]{1,0:T(8,128)(2,1)} %slice.81), channel_id=1, source_target_pairs={{0,4},{2,6},{4,0},{6,2},{8,12},{10,14},{12,8},{14,10},{16,20},{18,... | collective-permute-start | bytes 1572872 | tf_op jit(solution)/shard_map/ppermute | solution.py:276
  94.3 12.7 %collective-permute-start.14 = (bf16[256,2048]{1,0:T(8,128)(2,1)}, bf16[256,2048]{1,0:T(8,128)(2,1)}, u32[]{:S(2)}, u32[]{:S(2)}) collective-permute-start(bf16[256,2048]{1,0:T(8,128)(2,1)} %fusion.43), channel_id=1, source_target_pairs={{0,2},{2,0},{4,6},{6,4},{8,10},{10,8},{12,14},{14,12},{16,18},{18,... | collective-permute-start | bytes 3145736 | tf_op jit(solution)/shard_map/ppermute | solution.py:273
  95.4 18.0 %collective-permute-start.15 = (bf16[128,2048]{1,0:T(8,128)(2,1)S(1)}, bf16[128,2048]{1,0:T(8,128)(2,1)}, u32[]{:S(2)}, u32[]{:S(2)}) collective-permute-start(bf16[128,2048]{1,0:T(8,128)(2,1)S(1)} %slice.84), channel_id=1, source_target_pairs={{0,4},{2,6},{4,0},{6,2},{8,12},{10,14},{12,8},{14,10},{16,20},{18,... | collective-permute-start | bytes 1572872 | tf_op jit(solution)/shard_map/ppermute | solution.py:276
  106.5 20.6 %collective-permute-start.19 = (bf16[128,2048]{1,0:T(8,128)(2,1)S(1)}, bf16[128,2048]{1,0:T(8,128)(2,1)S(1)}, u32[]{:S(2)}, u32[]{:S(2)}) collective-permute-start(bf16[128,2048]{1,0:T(8,128)(2,1)S(1)} %slice.85), channel_id=1, source_target_pairs={{0,4},{2,6},{4,0},{6,2},{8,12},{10,14},{12,8},{14,10},{16,20},{18,... | collective-permute-start | bytes 1572872 | tf_op jit(solution)/shard_map/ppermute | solution.py:276
  116.6 10.4 %collective-permute-start.16 = (bf16[64,2048]{1,0:T(8,128)(2,1)}, bf16[64,2048]{1,0:T(8,128)(2,1)S(1)}, u32[]{:S(2)}, u32[]{:S(2)}) collective-permute-start(bf16[64,2048]{1,0:T(8,128)(2,1)} %get-tuple-element.57), channel_id=1, source_target_pairs={{0,24},{2,26},{4,28},{6,30},{8,0},{10,2},{12,4},{14,6},{16,8},{18,... | collective-permute-start | bytes 786440 | tf_op jit(solution)/shard_map/ppermute | solution.py:279
  116.6 16.4 %collective-permute-start.17 = (bf16[64,2048]{1,0:T(8,128)(2,1)}, bf16[64,2048]{1,0:T(8,128)(2,1)S(1)}, u32[]{:S(2)}, u32[]{:S(2)}) collective-permute-start(bf16[64,2048]{1,0:T(8,128)(2,1)} %get-tuple-element.58), channel_id=1, source_target_pairs={{0,16},{2,18},{4,20},{6,22},{8,24},{10,26},{12,28},{14,30},{16,0},... | collective-permute-start | bytes 786440 | tf_op jit(solution)/shard_map/ppermute | solution.py:279
  118.1 16.8 %collective-permute-start.20 = (bf16[128,2048]{1,0:T(8,128)(2,1)S(1)}, bf16[128,2048]{1,0:T(8,128)(2,1)S(1)}, u32[]{:S(2)}, u32[]{:S(2)}) collective-permute-start(bf16[128,2048]{1,0:T(8,128)(2,1)S(1)} %slice.86), channel_id=1, source_target_pairs={{0,4},{2,6},{4,0},{6,2},{8,12},{10,14},{12,8},{14,10},{16,20},{18,... | collective-permute-start | bytes 1572872 | tf_op jit(solution)/shard_map/ppermute | solution.py:276
  140.8 8.5 %collective-permute-start.25 = (bf16[256,4224]{1,0:T(8,128)(2,1)}, bf16[256,4224]{1,0:T(8,128)(2,1)}, u32[]{:S(2)}, u32[]{:S(2)}) collective-permute-start(bf16[256,4224]{1,0:T(8,128)(2,1)} %get-tuple-element.69), channel_id=1, source_target_pairs={{0,2},{2,0},{4,6},{6,4},{8,10},{10,8},{12,14},{14,12},{16,18},{18,... | collective-permute-start | bytes 6488072 | tf_op jit(solution)/shard_map/ppermute | solution.py:273
  140.9 26.0 %collective-permute-start.18 = (bf16[64,2048]{1,0:T(8,128)(2,1)}, bf16[64,2048]{1,0:T(8,128)(2,1)S(1)}, u32[]{:S(2)}, u32[]{:S(2)}) collective-permute-start(bf16[64,2048]{1,0:T(8,128)(2,1)} %get-tuple-element.59), channel_id=1, source_target_pairs={{0,8},{2,10},{4,12},{6,14},{8,16},{10,18},{12,20},{14,22},{16,24},... | collective-permute-start | bytes 786440 | tf_op jit(solution)/shard_map/ppermute | solution.py:279
  144.2 20.5 %collective-permute-start.21 = (bf16[64,2048]{1,0:T(8,128)(2,1)}, bf16[64,2048]{1,0:T(8,128)(2,1)S(1)}, u32[]{:S(2)}, u32[]{:S(2)}) collective-permute-start(bf16[64,2048]{1,0:T(8,128)(2,1)} %get-tuple-element.61), channel_id=1, source_target_pairs={{0,24},{2,26},{4,28},{6,30},{8,0},{10,2},{12,4},{14,6},{16,8},{18,... | collective-permute-start | bytes 786440 | tf_op jit(solution)/shard_map/ppermute | solution.py:279
  148.0 26.1 %collective-permute-start.22 = (bf16[64,2048]{1,0:T(8,128)(2,1)}, bf16[64,2048]{1,0:T(8,128)(2,1)S(1)}, u32[]{:S(2)}, u32[]{:S(2)}) collective-permute-start(bf16[64,2048]{1,0:T(8,128)(2,1)} %get-tuple-element.62), channel_id=1, source_target_pairs={{0,16},{2,18},{4,20},{6,22},{8,24},{10,26},{12,28},{14,30},{16,0},... | collective-permute-start | bytes 786440 | tf_op jit(solution)/shard_map/ppermute | solution.py:279
  148.0 26.1 %collective-permute-start.23 = (bf16[64,2048]{1,0:T(8,128)(2,1)}, bf16[64,2048]{1,0:T(8,128)(2,1)S(1)}, u32[]{:S(2)}, u32[]{:S(2)}) collective-permute-start(bf16[64,2048]{1,0:T(8,128)(2,1)} %get-tuple-element.63), channel_id=1, source_target_pairs={{0,8},{2,10},{4,12},{6,14},{8,16},{10,18},{12,20},{14,22},{16,24},... | collective-permute-start | bytes 786440 | tf_op jit(solution)/shard_map/ppermute | solution.py:279
  (34 other events, 227.5 us)

commit v17 on v16

--- a/solution.py
+++ b/solution.py
@@ -235,16 +235,18 @@
     def body(tokens_ref, cots_ref, ids_ref, probs_ref, out_ref):
         out_ref[:, :features] = tokens_ref[...]
         out_ref[:, features : 2 * features] = cots_ref[...]
-        lane = lax.broadcasted_iota(jnp.int32, (tok_rows, LANES), 1)
-        share = jnp.zeros((tok_rows, LANES), F32)
-        for k in range(ids_ref.shape[1]):
-            chosen = ids_ref[:, k : k + 1] == lane % experts
-            share = share + jnp.where(chosen, probs_ref[:, k : k + 1], 0.0)
+        row = lax.broadcasted_iota(jnp.int32, (LANES, tok_rows), 0)
+        share = jnp.zeros((LANES, tok_rows), F32)
+        for k in range(ids_ref.shape[0]):
+            chosen = ids_ref[k : k + 1, :] == row % experts
+            share = share + jnp.where(chosen, probs_ref[k : k + 1, :], 0.0)
         high = share.astype(BF).astype(F32)
         mid = (share - high).astype(BF).astype(F32)
         low = share - high - mid
-        term = jnp.where(lane < experts, high, jnp.where(lane < 2 * experts, mid, low))
-        out_ref[:, 2 * features :] = jnp.where(lane < 3 * experts, term, 0.0).astype(BF)
+        term = jnp.where(row < experts, high, jnp.where(row < 2 * experts, mid, low))
+        term = jnp.where(row < 3 * experts, term, 0.0)
+        rest = jnp.zeros((LANES, LANES - tok_rows), F32)
+        out_ref[:, 2 * features :] = jnp.concatenate([term, rest], axis=1).T[:tok_rows].astype(BF)
 
     out = jax.ShapeDtypeStruct((tok_rows, 2 * features + LANES), BF)
     return pl.pallas_call(
@@ -253,7 +255,7 @@
         compiler_params=params(),
         cost_estimate=SMALL,
         name="pair_up",
-    )(tokens, cots, route_ids, gate_probs)
+    )(tokens, cots, route_ids.T, gate_probs.T)
 
 
 def after(value, *earlier):
@@ -348,7 +350,8 @@
     chunks = home(after(place, grad_parts[0], grad_parts[1]), parts)
     own_grads = after((cot, d_gate, d_up), chunks[0])
     own = grads(own_x, act, *own_grads)
-    packed = plan(other_pieces, *own, *grad_parts[2:], *chunks[1:3])
+    packed = list(plan(other_pieces, *own, grad_parts[2]))
+    packed[3] = after(packed[3], grad_parts[3], *chunks[1:])
     grad_chunks = home(after(place, packed[-1]), grad_parts)
 
     x, weight, pre_gate, pre_up, act, cot = enter(packed)

time: 176 us -> 169 us (0.960)
  waiting for transfers between devices: 73.5 us -> 67.6 us
  local copies, waits for them, and re-layouts: 17.7 us -> 14.7 us
    ppermute x9, waiting for transfers between devices: 47.4 us -> 38.7 us  [to_z(): lax.ppermute(rows, 'expert', [(i, (i + 4 * step) % experts) for i in rang...]
    ppermute x5, waiting for transfers between devices: 0.01 us -> 4.53 us  [to_y(): return lax.ppermute(rows, 'replica', [(0, 1), (1, 0)])]
    unnamed x69 -> x61, local copies, waits for them, and re-layouts: 9.63 us -> 6.69 us
  transfers between devices with their start and end apart: 26 -> 26, of which waited for: 10 -> 10; matrix products, arithmetic and copies ran while one was open for 25% -> 26% of each run, Pallas kernels for 4% -> 7%
where the time goes in v17:
time: 169 us
  waiting for transfers between devices  67.6 us (40%)
  matrix products  34.7 us (21%)
  starting transfers between devices  24.9 us (15%)
  Pallas kernels  19.9 us (12%)
  local copies, waits for them, and re-layouts  14.7 us (9%)
  other arithmetic  5.54 us (3%)
    ppermute x9, waiting for transfers between devices, to_z(): lax.ppermute(rows, 'expert', [(i, (i + 4 * step) % experts) for i in rang...  38.7 us
    ppermute x8, waiting for transfers between devices, to_x(): return lax.ppermute(rows, 'expert', [(i, i ^ 2) for i in range(experts)])  20 us
    dot_general x6, matrix products, outer_sum(): lax.dot_general(left, right, (((0,), (0,)), ((), ())), preferred_element_...  13.9 us
    pallas_call x2, Pallas kernels, plan_and_pack(): pl.pallas_call(body, grid_spec=pltpu.PrefetchScalarGridSpec(num_scalar_pr...  11.3 us
    dot_general x6, matrix products, dot(): return jnp.dot(left, right, preferred_element_type=F32)  9.4 us
    ppermute x9, starting transfers between devices, to_z(): lax.ppermute(rows, 'expert', [(i, (i + 4 * step) % experts) for i in rang...  9.35 us
    ppermute x8, starting transfers between devices, to_x(): return lax.ppermute(rows, 'expert', [(i, i ^ 2) for i in range(experts)])  8.55 us
    unnamed x61, local copies, waits for them, and re-layouts  6.69 us
  transfers between devices with their start and end apart: 26, of which 10 were waited for; matrix products, arithmetic and copies ran while one was open for 26% of the time, Pallas kernels for 7%

profile of v17, /device:TPU:0, one launch (start us, length us, event | category | flops | bytes accessed | tf_op | source)
XLA Modules:
  0.0 168.5 jit_solution(3745598311625757746)
XLA Ops:
  0.6 2.1 %pair_up.1.refs_0_ = bf16[64,4224]{1,0:T(8,128)(2,1)} custom-call(bf16[64,2048]{1,0:T(8,128)(2,1)} %tokens_ref.1, bf16[64,2048]{1,0:T(8,128)(2,1)} %cots_ref.1, s32[6,64]{1,0:T(8,128)} %bitcast.67, f32[6,64]{1,0:T(8,128)} %bitcast.68), custom_call_target="tpu_custom_call" | custom-call | flops 1 | bytes 1 | tf_op jit(solution)/shard_map/pair_up/pallas_call | solution.py:252
  2.7 3.0 %collective-permute-start.2 = (bf16[64,4224]{1,0:T(8,128)(2,1)}, bf16[64,4224]{1,0:T(8,128)(2,1)}, u32[]{:S(2)}, u32[]{:S(2)}) collective-permute-start(bf16[64,4224]{1,0:T(8,128)(2,1)} %pair_up.1.refs_0_), channel_id=1, source_target_pairs={{0,8},{2,10},{4,12},{6,14},{8,16},{10,18},{12,20},{14,22},{16,24},... | collective-permute-start | bytes 1622024 | tf_op jit(solution)/shard_map/ppermute | solution.py:281
  8.8 11.6 %collective-permute-done.2.refs_1_ = bf16[64,4224]{1,0:T(8,128)(2,1)} collective-permute-done((bf16[64,4224]{1,0:T(8,128)(2,1)}, bf16[64,4224]{1,0:T(8,128)(2,1)}, u32[]{:S(2)}, u32[]{:S(2)}) %collective-permute-start.2) | collective-permute-done | bytes 540704 | tf_op jit(solution)/shard_map/ppermute | solution.py:281
  23.9 12.0 %collective-permute-done.6.refs_2_ = bf16[64,4224]{1,0:T(8,128)(2,1)} collective-permute-done((bf16[64,4224]{1,0:T(8,128)(2,1)}, bf16[64,4224]{1,0:T(8,128)(2,1)}, u32[]{:S(2)}, u32[]{:S(2)}) %collective-permute-start.6) | collective-permute-done | bytes 540704 | tf_op jit(solution)/shard_map/ppermute | solution.py:281
  40.6 10.6 %collective-permute-done.8.refs_3_ = bf16[64,4224]{1,0:T(8,128)(2,1)S(1)} collective-permute-done((bf16[64,4224]{1,0:T(8,128)(2,1)}, bf16[64,4224]{1,0:T(8,128)(2,1)S(1)}, u32[]{:S(2)}, u32[]{:S(2)}) %collective-permute-start.8) | collective-permute-done | bytes 540704 | tf_op jit(solution)/shard_map/ppermute | solution.py:281
  54.0 8.3 %collective-permute-done.10.refs_7_ = bf16[64,4224]{1,0:T(8,128)(2,1)S(1)} collective-permute-done((bf16[64,4224]{1,0:T(8,128)(2,1)S(1)}, bf16[64,4224]{1,0:T(8,128)(2,1)S(1)}, u32[]{:S(2)}, u32[]{:S(2)}) %collective-permute-start.10) | collective-permute-done | bytes 540704 | tf_op jit(solution)/shard_map/ppermute | solution.py:278
  63.3 5.7 %plan_and_pack.2 = (bf16[256,2048]{1,0:T(8,128)(2,1)}, bf16[256,2048]{1,0:T(8,128)(2,1)}, bf16[256,128]{1,0:T(8,128)(2,1)}, bf16[256,4224]{1,0:T(8,128)(2,1)}, bf16[256,512]{1,0:T(8,128)(2,1)}) custom-call(s32[1]{0:T(128)} %bitcast.expert_ref, bf16[64,4224]{1,0:T(8,128)(2,1)} %pair_up.1.refs_0_, bf16[64,4224]{1,0:T(8,128)(2,1)} %collective-permute-done.2.refs_1_, ...), custom_call_target="tpu_custom_call" | custom-call | flops 1 | bytes 1 | tf_op jit(solution)/shard_map/plan_and_pack/pallas_call | solution.py:185
  69.1 4.4 %collective-permute-done.11 = bf16[256,4224]{1,0:T(8,128)(2,1)S(1)} collective-permute-done((bf16[256,4224]{1,0:T(8,128)(2,1)}, bf16[256,4224]{1,0:T(8,128)(2,1)S(1)}, u32[]{:S(2)}, u32[]{:S(2)}) %collective-permute-start.11) | collective-permute-done | bytes 2162720 | tf_op jit(solution)/shard_map/ppermute | solution.py:275
  85.1 2.2 %multiply_convert_fusion.4 = (bf16[512,768]{1,0:T(8,128)(2,1)S(1)}, bf16[512,768]{1,0:T(8,128)(2,1)S(1)}) fusion(f32[512,768]{1,0:T(8,128)S(1)} %fusion.22, f32[512,768]{1,0:T(8,128)S(1)} %get-tuple-element.98, bf16[512,2048]{1,0:T(8,128)(2,1)S(1)} %multiply_convert_fusion.1, bf16[1,768,2048]{2,1,0:T(8,128)(2,1)S(1)} %copy-done.25), kind=kOutput, calls=%fused_computation.48 | convolution fusion | flops 1615724544 | bytes 9961472 | tf_op jit(solution)/shard_map/dot_general | solution.py:41
  89.4 2.1 %fusion.43 = bf16[256,2048]{1,0:T(8,128)(2,1)} fusion(f32[256,2048]{1,0:T(8,128)S(1)} %fusion.10, bf16[256,768]{1,0:T(8,128)(2,1)S(1)} %get-tuple-element.54, bf16[1,2048,768]{2,1,0:T(8,128)(2,1)S(1)} %copy-done), kind=kOutput, calls=%fused_computation.36 | convolution fusion | flops 806354944 | bytes 6684672 | tf_op jit(solution)/shard_map/dot_general | solution.py:49
  94.1 5.1 %collective-permute-done.13.refs_2_ = bf16[128,2048]{1,0:T(8,128)(2,1)} collective-permute-done((bf16[128,2048]{1,0:T(8,128)(2,1)}, bf16[128,2048]{1,0:T(8,128)(2,1)}, u32[]{:S(2)}, u32[]{:S(2)}) %collective-permute-start.13) | collective-permute-done | bytes 524320 | tf_op jit(solution)/shard_map/ppermute | solution.py:278
  99.3 3.2 %fusion.12 = f32[256,2048]{1,0:T(8,128)S(1)} fusion(bf16[256,768]{1,0:T(8,128)(2,1)} %get-tuple-element.53, bf16[1,2048,768]{2,1,0:T(8,128)(2,1)} %param.12), kind=kOutput, calls=%fused_computation.14 | convolution fusion | flops 805306368 | bytes 5636096 | tf_op jit(solution)/shard_map/dot_general | solution.py:50
  104.2 6.3 %collective-permute-done.15.refs_3_ = bf16[128,2048]{1,0:T(8,128)(2,1)} collective-permute-done((bf16[128,2048]{1,0:T(8,128)(2,1)S(1)}, bf16[128,2048]{1,0:T(8,128)(2,1)}, u32[]{:S(2)}, u32[]{:S(2)}) %collective-permute-start.15) | collective-permute-done | bytes 524320 | tf_op jit(solution)/shard_map/ppermute | solution.py:278
  110.5 3.2 %spread.2 = (bf16[64,2048]{1,0:T(8,128)(2,1)}, bf16[64,2048]{1,0:T(8,128)(2,1)}, bf16[64,2048]{1,0:T(8,128)(2,1)}, bf16[64,2048]{1,0:T(8,128)(2,1)}) custom-call(bf16[256,512]{1,0:T(8,128)(2,1)} %get-tuple-element.56.place_ref, bf16[256,2048]{1,0:T(8,128)(2,1)} %copy-done.7, bf16[256,2048]{1,0:T(8,128)(2,1)} %collective-permute-done.12.refs_1_, ...), custom_call_target="tpu_custom_call" | custom-call | flops 1 | bytes 1 | tf_op jit(solution)/shard_map/spread/pallas_call | solution.py:220
  115.8 2.9 %fusion.59 = f32[384,2048]{1,0:T(8,128)S(1)} fusion(bf16[512,2048]{1,0:T(8,128)(2,1)} %copy-done.3, bf16[512,768]{1,0:T(8,128)(2,1)} %copy-done.23, s32[]{:T(128)S(6)} %select_n.27), kind=kOutput, calls=%fused_computation.64 | convolution fusion | flops 805306368 | bytes 5636100 | tf_op jit(solution)/shard_map/dot_general | solution.py:55
  118.8 2.7 %fusion.72 = f32[1024,768]{1,0:T(8,128)} fusion(bf16[512,768]{1,0:T(8,128)(2,1)S(1)} %copy-done.19, s32[]{:T(128)S(6)} %select_n.26, bf16[256,2048]{1,0:T(8,128)(2,1)S(1)} %copy-done.28, bf16[256,2048]{1,0:T(8,128)(2,1)S(1)} %copy-done.13), kind=kOutput, calls=%fused_computation.84 | convolution fusion | flops 807403520 | bytes 6029316 | tf_op jit(solution)/shard_map/dot_general | solution.py:55
  123.1 2.7 %fusion.70 = f32[1024,768]{1,0:T(8,128)} fusion(bf16[512,768]{1,0:T(8,128)(2,1)S(1)} %copy-done.17, s32[]{:T(128)S(6)} %select_n.26, bf16[256,2048]{1,0:T(8,128)(2,1)S(1)} %copy-done.28, bf16[256,2048]{1,0:T(8,128)(2,1)S(1)} %copy-done.13), kind=kOutput, calls=%fused_computation.83 | convolution fusion | flops 807403520 | bytes 6029316 | tf_op jit(solution)/shard_map/dot_general | solution.py:55
  125.8 4.5 %collective-permute-done.24.refs_2_ = bf16[256,4224]{1,0:T(8,128)(2,1)} collective-permute-done((bf16[256,4224]{1,0:T(8,128)(2,1)}, bf16[256,4224]{1,0:T(8,128)(2,1)}, u32[]{:S(2)}, u32[]{:S(2)}) %collective-permute-start.24) | collective-permute-done | bytes 2162720 | tf_op jit(solution)/shard_map/ppermute | solution.py:286
  130.3 5.7 %plan_and_pack.3 = (bf16[256,2048]{1,0:T(8,128)(2,1)}, bf16[256,2048]{1,0:T(8,128)(2,1)}, bf16[256,128]{1,0:T(8,128)(2,1)}, bf16[256,4224]{1,0:T(8,128)(2,1)}, bf16[256,512]{1,0:T(8,128)(2,1)}) custom-call(s32[1]{0:T(128)} %bitcast.expert_ref, bf16[64,4224]{1,0:T(8,128)(2,1)} %collective-permute-done.7.refs_0_, ...), custom_call_target="tpu_custom_call" | custom-call | flops 1 | bytes 1 | tf_op jit(solution)/shard_map/plan_and_pack/pallas_call | solution.py:185
  136.2 3.3 %spread.3 = (bf16[64,2048]{1,0:T(8,128)(2,1)}, bf16[64,2048]{1,0:T(8,128)(2,1)}, bf16[64,2048]{1,0:T(8,128)(2,1)}, bf16[64,2048]{1,0:T(8,128)(2,1)}) custom-call(bf16[256,512]{1,0:T(8,128)(2,1)} %get-tuple-element.56.place_ref, bf16[256,2048]{1,0:T(8,128)(2,1)} %copy-done.4, bf16[256,2048]{1,0:T(8,128)(2,1)} %collective-permute-done.14.refs_1_, ...), custom_call_target="tpu_custom_call" | custom-call | flops 1 | bytes 1 | tf_op jit(solution)/shard_map/spread/pallas_call | solution.py:220
  141.9 2.0 %collective-permute-start.23 = (bf16[64,2048]{1,0:T(8,128)(2,1)}, bf16[64,2048]{1,0:T(8,128)(2,1)S(1)}, u32[]{:S(2)}, u32[]{:S(2)}) collective-permute-start(bf16[64,2048]{1,0:T(8,128)(2,1)} %get-tuple-element.64), channel_id=1, source_target_pairs={{0,8},{2,10},{4,12},{6,14},{8,16},{10,18},{12,20},{14,22},{16,24},... | collective-permute-start | bytes 786440 | tf_op jit(solution)/shard_map/ppermute | solution.py:281
  157.0 2.3 %fusion.36 = bf16[1,384,2048]{2,1,0:T(8,128)(2,1)} fusion(f32[384,2048]{1,0:T(8,128)S(1)} %fusion.59, f32[512,768]{1,0:T(8,128)S(1)} %fusion.8, s32[]{:T(128)S(6)} %select_n.27, f32[512,768]{1,0:T(8,128)S(1)} %get-tuple-element.89, f32[512,768]{1,0:T(8,128)S(1)} %get-tuple-element.99, bf16[256,2048]{1,0:T(8,128)(2,1)S(1)} %get-tuple-element.85, ...), kind=kOutput, calls=%fused_computation.33 | convolution fusion | flops 813760512 | bytes 9177092 | tf_op jit(solution)/shard_map/dot_general | solution.py:55
  159.3 2.2 %fusion.50 = bf16[1,1024,768]{2,1,0:T(8,128)(2,1)} fusion(f32[1024,768]{1,0:T(8,128)S(1)} %copy-done.5, bf16[512,768]{1,0:T(8,128)(2,1)S(1)} %get-tuple-element.82, s32[]{:T(128)S(6)} %select_n.26, bf16[256,2048]{1,0:T(8,128)(2,1)S(1)} %copy-done.14, bf16[256,2048]{1,0:T(8,128)(2,1)S(1)} %get-tuple-element.86), kind=kOutput, calls=%fused_computation.52 | convolution fusion | flops 808976384 | bytes 7602180 | tf_op jit(solution)/shard_map/dot_general | solution.py:55
  161.5 4.4 %collective-permute-done.22 = bf16[64,2048]{1,0:T(8,128)(2,1)S(1)} collective-permute-done((bf16[64,2048]{1,0:T(8,128)(2,1)}, bf16[64,2048]{1,0:T(8,128)(2,1)S(1)}, u32[]{:S(2)}, u32[]{:S(2)}) %collective-permute-start.22) | collective-permute-done | bytes 262176 | tf_op jit(solution)/shard_map/ppermute | solution.py:281
  (130 shorter events, 54.8 us)
Async XLA Ops:
  2.7 17.6 %collective-permute-start.2 = (bf16[64,4224]{1,0:T(8,128)(2,1)}, bf16[64,4224]{1,0:T(8,128)(2,1)}, u32[]{:S(2)}, u32[]{:S(2)}) collective-permute-start(bf16[64,4224]{1,0:T(8,128)(2,1)} %pair_up.1.refs_0_), channel_id=1, source_target_pairs={{0,8},{2,10},{4,12},{6,14},{8,16},{10,18},{12,20},{14,22},{16,24},... | collective-permute-start | bytes 1622024 | tf_op jit(solution)/shard_map/ppermute | solution.py:281
  5.8 17.6 %collective-permute-start = (bf16[64,4224]{1,0:T(8,128)(2,1)}, bf16[64,4224]{1,0:T(8,128)(2,1)}, u32[]{:S(2)}, u32[]{:S(2)}) collective-permute-start(bf16[64,4224]{1,0:T(8,128)(2,1)} %pair_up.1.refs_0_), channel_id=1, source_target_pairs={{0,4},{2,6},{4,0},{6,2},{8,12},{10,14},{12,8},{14,10},{16,20},{18,... | collective-permute-start | bytes 1622024 | tf_op jit(solution)/shard_map/ppermute | solution.py:278
  7.2 16.6 %collective-permute-start.7 = (bf16[64,4224]{1,0:T(8,128)(2,1)}, bf16[64,4224]{1,0:T(8,128)(2,1)}, u32[]{:S(2)}, u32[]{:S(2)}) collective-permute-start(bf16[64,4224]{1,0:T(8,128)(2,1)} %pair_up.1.refs_0_), channel_id=1, source_target_pairs={{0,1},{1,0},{2,3},{3,2},{4,5},{5,4},{6,7},{7,6},{8,9},{9,8},{10,11... | collective-permute-start | bytes 1622024 | tf_op jit(solution)/shard_map/ppermute | solution.py:286
  20.4 15.6 %collective-permute-start.6 = (bf16[64,4224]{1,0:T(8,128)(2,1)}, bf16[64,4224]{1,0:T(8,128)(2,1)}, u32[]{:S(2)}, u32[]{:S(2)}) collective-permute-start(bf16[64,4224]{1,0:T(8,128)(2,1)} %collective-permute-done.2.refs_1_), channel_id=1, source_target_pairs={{0,8},{2,10},{4,12},{6,14},{8,16},{10,18},{12,20},{14,22},{16,24},... | collective-permute-start | bytes 1622024 | tf_op jit(solution)/shard_map/ppermute | solution.py:281
  20.4 16.8 %collective-permute-start.4 = (bf16[64,4224]{1,0:T(8,128)(2,1)}, bf16[64,4224]{1,0:T(8,128)(2,1)}, u32[]{:S(2)}, u32[]{:S(2)}) collective-permute-start(bf16[64,4224]{1,0:T(8,128)(2,1)} %collective-permute-done.2.refs_1_), channel_id=1, source_target_pairs={{0,4},{2,6},{4,0},{6,2},{8,12},{10,14},{12,8},{14,10},{16,20},{18,... | collective-permute-start | bytes 1622024 | tf_op jit(solution)/shard_map/ppermute | solution.py:278
  21.9 41.4 %collective-permute-start.3 = (bf16[64,4224]{1,0:T(8,128)(2,1)}, bf16[64,4224]{1,0:T(8,128)(2,1)}, u32[]{:S(2)}, u32[]{:S(2)}) collective-permute-start(bf16[64,4224]{1,0:T(8,128)(2,1)} %collective-permute-done.2.refs_1_), channel_id=1, source_target_pairs={{0,1},{1,0},{2,3},{3,2},{4,5},{5,4},{6,7},{7,6},{8,9},{9,8},{10,11... | collective-permute-start | bytes 1622024 | tf_op jit(solution)/shard_map/ppermute | solution.py:286
  23.4 39.8 %collective-permute-start.1 = (bf16[64,4224]{1,0:T(8,128)(2,1)}, bf16[64,4224]{1,0:T(8,128)(2,1)}, u32[]{:S(2)}, u32[]{:S(2)}) collective-permute-start(bf16[64,4224]{1,0:T(8,128)(2,1)} %collective-permute-done.refs_4_), channel_id=1, source_target_pairs={{0,1},{1,0},{2,3},{3,2},{4,5},{5,4},{6,7},{7,6},{8,9},{9,8},{10,11... | collective-permute-start | bytes 1622024 | tf_op jit(solution)/shard_map/ppermute | solution.py:286
  35.9 17.1 %collective-permute-start.9 = (bf16[64,4224]{1,0:T(8,128)(2,1)}, bf16[64,4224]{1,0:T(8,128)(2,1)S(1)}, u32[]{:S(2)}, u32[]{:S(2)}) collective-permute-start(bf16[64,4224]{1,0:T(8,128)(2,1)} %collective-permute-done.6.refs_2_), channel_id=1, source_target_pairs={{0,4},{2,6},{4,0},{6,2},{8,12},{10,14},{12,8},{14,10},{16,20},{18,... | collective-permute-start | bytes 1622024 | tf_op jit(solution)/shard_map/ppermute | solution.py:278
  37.2 14.0 %collective-permute-start.8 = (bf16[64,4224]{1,0:T(8,128)(2,1)}, bf16[64,4224]{1,0:T(8,128)(2,1)S(1)}, u32[]{:S(2)}, u32[]{:S(2)}) collective-permute-start(bf16[64,4224]{1,0:T(8,128)(2,1)} %collective-permute-done.6.refs_2_), channel_id=1, source_target_pairs={{0,8},{2,10},{4,12},{6,14},{8,16},{10,18},{12,20},{14,22},{16,24},... | collective-permute-start | bytes 1622024 | tf_op jit(solution)/shard_map/ppermute | solution.py:281
  37.2 26.0 %collective-permute-start.5 = (bf16[64,4224]{1,0:T(8,128)(2,1)}, bf16[64,4224]{1,0:T(8,128)(2,1)}, u32[]{:S(2)}, u32[]{:S(2)}) collective-permute-start(bf16[64,4224]{1,0:T(8,128)(2,1)} %collective-permute-done.4.refs_5_), channel_id=1, source_target_pairs={{0,1},{1,0},{2,3},{3,2},{4,5},{5,4},{6,7},{7,6},{8,9},{9,8},{10,11... | collective-permute-start | bytes 1622024 | tf_op jit(solution)/shard_map/ppermute | solution.py:286
  51.2 11.1 %collective-permute-start.10 = (bf16[64,4224]{1,0:T(8,128)(2,1)S(1)}, bf16[64,4224]{1,0:T(8,128)(2,1)S(1)}, u32[]{:S(2)}, u32[]{:S(2)}) collective-permute-start(bf16[64,4224]{1,0:T(8,128)(2,1)S(1)} %collective-permute-done.8.refs_3_), channel_id=1, source_target_pairs={{0,4},{2,6},{4,0},{6,2},{8,12},{10,14},{12,8},{14,10},{16,20},{18,... | collective-permute-start | bytes 1622024 | tf_op jit(solution)/shard_map/ppermute | solution.py:278
  80.7 49.6 %collective-permute-start.24 = (bf16[256,4224]{1,0:T(8,128)(2,1)}, bf16[256,4224]{1,0:T(8,128)(2,1)}, u32[]{:S(2)}, u32[]{:S(2)}) collective-permute-start(bf16[256,4224]{1,0:T(8,128)(2,1)} %constant_dynamic-update-slice_fusion), channel_id=1, source_target_pairs={{0,1},{1,0},{2,3},{3,2},{4,5},{5,4},{6,7},{7,6},{8,9},{9,8},{10,11... | collective-permute-start | bytes 6488072 | tf_op jit(solution)/shard_map/ppermute | solution.py:286
  84.2 15.1 %collective-permute-start.13 = (bf16[128,2048]{1,0:T(8,128)(2,1)}, bf16[128,2048]{1,0:T(8,128)(2,1)}, u32[]{:S(2)}, u32[]{:S(2)}) collective-permute-start(bf16[128,2048]{1,0:T(8,128)(2,1)} %slice.81), channel_id=1, source_target_pairs={{0,4},{2,6},{4,0},{6,2},{8,12},{10,14},{12,8},{14,10},{16,20},{18,... | collective-permute-start | bytes 1572872 | tf_op jit(solution)/shard_map/ppermute | solution.py:278
  91.5 12.7 %collective-permute-start.14 = (bf16[256,2048]{1,0:T(8,128)(2,1)}, bf16[256,2048]{1,0:T(8,128)(2,1)}, u32[]{:S(2)}, u32[]{:S(2)}) collective-permute-start(bf16[256,2048]{1,0:T(8,128)(2,1)} %fusion.43), channel_id=1, source_target_pairs={{0,2},{2,0},{4,6},{6,4},{8,10},{10,8},{12,14},{14,12},{16,18},{18,... | collective-permute-start | bytes 3145736 | tf_op jit(solution)/shard_map/ppermute | solution.py:275
  92.6 17.9 %collective-permute-start.15 = (bf16[128,2048]{1,0:T(8,128)(2,1)S(1)}, bf16[128,2048]{1,0:T(8,128)(2,1)}, u32[]{:S(2)}, u32[]{:S(2)}) collective-permute-start(bf16[128,2048]{1,0:T(8,128)(2,1)S(1)} %slice.84), channel_id=1, source_target_pairs={{0,4},{2,6},{4,0},{6,2},{8,12},{10,14},{12,8},{14,10},{16,20},{18,... | collective-permute-start | bytes 1572872 | tf_op jit(solution)/shard_map/ppermute | solution.py:278
  103.6 18.1 %collective-permute-start.19 = (bf16[128,2048]{1,0:T(8,128)(2,1)S(1)}, bf16[128,2048]{1,0:T(8,128)(2,1)S(1)}, u32[]{:S(2)}, u32[]{:S(2)}) collective-permute-start(bf16[128,2048]{1,0:T(8,128)(2,1)S(1)} %slice.85), channel_id=1, source_target_pairs={{0,4},{2,6},{4,0},{6,2},{8,12},{10,14},{12,8},{14,10},{16,20},{18,... | collective-permute-start | bytes 1572872 | tf_op jit(solution)/shard_map/ppermute | solution.py:278
  113.7 22.3 %collective-permute-start.16 = (bf16[64,2048]{1,0:T(8,128)(2,1)}, bf16[64,2048]{1,0:T(8,128)(2,1)S(1)}, u32[]{:S(2)}, u32[]{:S(2)}) collective-permute-start(bf16[64,2048]{1,0:T(8,128)(2,1)} %get-tuple-element.58), channel_id=1, source_target_pairs={{0,24},{2,26},{4,28},{6,30},{8,0},{10,2},{12,4},{14,6},{16,8},{18,... | collective-permute-start | bytes 786440 | tf_op jit(solution)/shard_map/ppermute | solution.py:281
  113.7 22.3 %collective-permute-start.17 = (bf16[64,2048]{1,0:T(8,128)(2,1)}, bf16[64,2048]{1,0:T(8,128)(2,1)}, u32[]{:S(2)}, u32[]{:S(2)}) collective-permute-start(bf16[64,2048]{1,0:T(8,128)(2,1)} %get-tuple-element.59), channel_id=1, source_target_pairs={{0,16},{2,18},{4,20},{6,22},{8,24},{10,26},{12,28},{14,30},{16,0},... | collective-permute-start | bytes 786440 | tf_op jit(solution)/shard_map/ppermute | solution.py:281
  115.2 20.9 %collective-permute-start.20 = (bf16[128,2048]{1,0:T(8,128)(2,1)S(1)}, bf16[128,2048]{1,0:T(8,128)(2,1)}, u32[]{:S(2)}, u32[]{:S(2)}) collective-permute-start(bf16[128,2048]{1,0:T(8,128)(2,1)S(1)} %slice.86), channel_id=1, source_target_pairs={{0,4},{2,6},{4,0},{6,2},{8,12},{10,14},{12,8},{14,10},{16,20},{18,... | collective-permute-start | bytes 1572872 | tf_op jit(solution)/shard_map/ppermute | solution.py:278
  121.6 14.4 %collective-permute-start.18 = (bf16[64,2048]{1,0:T(8,128)(2,1)}, bf16[64,2048]{1,0:T(8,128)(2,1)S(1)}, u32[]{:S(2)}, u32[]{:S(2)}) collective-permute-start(bf16[64,2048]{1,0:T(8,128)(2,1)} %get-tuple-element.60), channel_id=1, source_target_pairs={{0,8},{2,10},{4,12},{6,14},{8,16},{10,18},{12,20},{14,22},{16,24},... | collective-permute-start | bytes 786440 | tf_op jit(solution)/shard_map/ppermute | solution.py:281
  136.1 7.8 %collective-permute-start.25 = (bf16[256,4224]{1,0:T(8,128)(2,1)}, bf16[256,4224]{1,0:T(8,128)(2,1)}, u32[]{:S(2)}, u32[]{:S(2)}) collective-permute-start(bf16[256,4224]{1,0:T(8,128)(2,1)} %get-tuple-element.71), channel_id=1, source_target_pairs={{0,2},{2,0},{4,6},{6,4},{8,10},{10,8},{12,14},{14,12},{16,18},{18,... | collective-permute-start | bytes 6488072 | tf_op jit(solution)/shard_map/ppermute | solution.py:275
  139.4 19.9 %collective-permute-start.21 = (bf16[64,2048]{1,0:T(8,128)(2,1)}, bf16[64,2048]{1,0:T(8,128)(2,1)S(1)}, u32[]{:S(2)}, u32[]{:S(2)}) collective-permute-start(bf16[64,2048]{1,0:T(8,128)(2,1)} %get-tuple-element.62), channel_id=1, source_target_pairs={{0,24},{2,26},{4,28},{6,30},{8,0},{10,2},{12,4},{14,6},{16,8},{18,... | collective-permute-start | bytes 786440 | tf_op jit(solution)/shard_map/ppermute | solution.py:281
  140.1 25.7 %collective-permute-start.22 = (bf16[64,2048]{1,0:T(8,128)(2,1)}, bf16[64,2048]{1,0:T(8,128)(2,1)S(1)}, u32[]{:S(2)}, u32[]{:S(2)}) collective-permute-start(bf16[64,2048]{1,0:T(8,128)(2,1)} %get-tuple-element.63), channel_id=1, source_target_pairs={{0,16},{2,18},{4,20},{6,22},{8,24},{10,26},{12,28},{14,30},{16,0},... | collective-permute-start | bytes 786440 | tf_op jit(solution)/shard_map/ppermute | solution.py:281
  141.9 24.0 %collective-permute-start.23 = (bf16[64,2048]{1,0:T(8,128)(2,1)}, bf16[64,2048]{1,0:T(8,128)(2,1)S(1)}, u32[]{:S(2)}, u32[]{:S(2)}) collective-permute-start(bf16[64,2048]{1,0:T(8,128)(2,1)} %get-tuple-element.64), channel_id=1, source_target_pairs={{0,8},{2,10},{4,12},{6,14},{8,16},{10,18},{12,20},{14,22},{16,24},... | collective-permute-start | bytes 786440 | tf_op jit(solution)/shard_map/ppermute | solution.py:281
  (31 other events, 194.4 us)

commit v18 on v17

--- a/solution.py
+++ b/solution.py
@@ -318,11 +318,11 @@
         act = (jax.nn.silu(pre_gate) * pre_up).astype(BF)
         return x, weight, pre_gate, pre_up, act, cot
 
-    def leave(rows_of, before_mine=(), before_far=()):
-        half = TOGETHER * capacity
-        theirs = to_core(rows_of(slice(2 * half, None)))
-        mine = rows_of(slice(0, 2 * half), *before_mine)
-        return mine, theirs, to_x(after(mine[half:], *before_far)), to_x(theirs[half:])
+    def leave(rows_of, *before_far):
+        room = TOGETHER * capacity
+        theirs = to_core(rows_of(slice(2 * room, None)))
+        far = to_x(after(rows_of(slice(room, 2 * room)), *before_far))
+        return rows_of(slice(0, room)), theirs, far, to_x(theirs[room:])
 
     def home(place, parts):
         own, *others = spread(place, *parts)
@@ -343,10 +343,9 @@
     cot = after(cot, parts[0], parts[1])
     d_gate, d_up = hidden_grads(cot, pre_gate, pre_up, w_down)
 
-    def token_grads(rows, *earlier):
-        return input_rows(*after((d_gate[rows], d_up[rows]), *earlier), w_gate, w_up)
-
-    grad_parts = leave(token_grads, parts[2:3])
+    grad_parts = leave(
+        lambda rows: input_rows(d_gate[rows], d_up[rows], w_gate, w_up), parts[2]
+    )
     chunks = home(after(place, grad_parts[0], grad_parts[1]), parts)
     own_grads = after((cot, d_gate, d_up), chunks[0])
     own = grads(own_x, act, *own_grads)
@@ -356,8 +355,9 @@
 
     x, weight, pre_gate, pre_up, act, cot = enter(packed)
     d_gate, d_up = hidden_grads(cot, pre_gate, pre_up, w_down)
+    chunks = after(chunks, d_gate)
     other = grads(x, act, cot, d_gate, after(d_up, grad_chunks[1]))
-    chunks, grad_chunks = after((chunks, grad_chunks), other[0])
+    grad_chunks = after(grad_chunks, other[0])
     grad_gate, grad_up, grad_down = ((a + b).astype(BF)[None] for a, b in zip(own, other))
     return (total(chunks), total(grad_chunks), grad_gate, grad_up, grad_down)
 

time: 169 us -> 169 us (level)
  waiting for transfers between devices: 67.6 us -> 62.6 us
  matrix products: 34.7 us -> 38.8 us
  starting transfers between devices: 24.9 us -> 26.9 us
    ppermute x5, waiting for transfers between devices: 4.53 us -> 0.01 us  [to_y(): return lax.ppermute(rows, 'replica', [(0, 1), (1, 0)])]
    ppermute x9, waiting for transfers between devices: 38.7 us -> 41.4 us  [to_z(): lax.ppermute(rows, 'expert', [(i, (i + 4 * step) % experts) for i in rang...]
    dot_general x2 -> x3, matrix products: 3.08 us -> 5.05 us  [input_rows(): lax.dot_general(d_gate, gate_weight, CONTRACT, preferred_element_type=F32)]
    ppermute x8, waiting for transfers between devices: 20 us -> 18.2 us  [to_x(): return lax.ppermute(rows, 'expert', [(i, i ^ 2) for i in range(experts)])]
    slice x5 -> x3, local copies, waits for them, and re-layouts: 4.09 us -> 2.7 us  [the longest x1 1.83 us: enter(): x = jnp.concatenate([mine, theirs[:, :features]], axis=0)]
    dot_general x6 -> x7, matrix products: 9.4 us -> 10.3 us  [dot(): return jnp.dot(left, right, preferred_element_type=F32)]
    dot_general x2 -> x3, matrix products: 4.23 us -> 3.42 us  [input_rows(): lax.dot_general(d_up, up_weight, CONTRACT, preferred_element_type=F32)]
  transfers between devices with their start and end apart: 26 -> 26, of which waited for: 10 -> 9; matrix products, arithmetic and copies ran while one was open for 26% -> 31% of each run, Pallas kernels for 7% -> 7%
where the time goes in v18:
time: 169 us; the launch traced here: 168 us
  waiting for transfers between devices  62.6 us (37%)
  matrix products  38.8 us (23%)
  starting transfers between devices  26.9 us (16%)
  Pallas kernels  19.9 us (12%)
  local copies, waits for them, and re-layouts  13.8 us (8%)
  other arithmetic  5.19 us (3%)
    ppermute x9, waiting for transfers between devices, to_z(): lax.ppermute(rows, 'expert', [(i, (i + 4 * step) % experts) for i in rang...  41.4 us
    ppermute x8, waiting for transfers between devices, to_x(): return lax.ppermute(rows, 'expert', [(i, i ^ 2) for i in range(experts)])  18.2 us
    dot_general x6, matrix products, outer_sum(): lax.dot_general(left, right, (((0,), (0,)), ((), ())), preferred_element_...  15.4 us
    pallas_call x2, Pallas kernels, plan_and_pack(): pl.pallas_call(body, grid_spec=pltpu.PrefetchScalarGridSpec(num_scalar_pr...  11.3 us
    dot_general x7, matrix products, dot(): return jnp.dot(left, right, preferred_element_type=F32)  10.3 us
    ppermute x8, starting transfers between devices, to_x(): return lax.ppermute(rows, 'expert', [(i, i ^ 2) for i in range(experts)])  9.99 us
    ppermute x9, starting transfers between devices, to_z(): lax.ppermute(rows, 'expert', [(i, (i + 4 * step) % experts) for i in rang...  9.85 us
    unnamed x61, local copies, waits for them, and re-layouts  6.73 us
  transfers between devices with their start and end apart: 26, of which 9 were waited for; matrix products, arithmetic and copies ran while one was open for 31% of the time, Pallas kernels for 7%

profile of v18, /device:TPU:0, one launch (start us, length us, event | category | flops | bytes accessed | tf_op | source)
XLA Modules:
  0.0 168.3 jit_solution(10416841700728460524)
XLA Ops:
  0.6 2.1 %pair_up.1.refs_0_ = bf16[64,4224]{1,0:T(8,128)(2,1)} custom-call(bf16[64,2048]{1,0:T(8,128)(2,1)} %tokens_ref.1, bf16[64,2048]{1,0:T(8,128)(2,1)} %cots_ref.1, s32[6,64]{1,0:T(8,128)} %bitcast.78, f32[6,64]{1,0:T(8,128)} %bitcast.79), custom_call_target="tpu_custom_call" | custom-call | flops 1 | bytes 1 | tf_op jit(solution)/shard_map/pair_up/pallas_call | solution.py:252
  2.7 3.0 %collective-permute-start.2 = (bf16[64,4224]{1,0:T(8,128)(2,1)}, bf16[64,4224]{1,0:T(8,128)(2,1)}, u32[]{:S(2)}, u32[]{:S(2)}) collective-permute-start(bf16[64,4224]{1,0:T(8,128)(2,1)} %pair_up.1.refs_0_), channel_id=1, source_target_pairs={{0,8},{2,10},{4,12},{6,14},{8,16},{10,18},{12,20},{14,22},{16,24},... | collective-permute-start | bytes 1622024 | tf_op jit(solution)/shard_map/ppermute | solution.py:281
  8.8 11.6 %collective-permute-done.2.refs_1_ = bf16[64,4224]{1,0:T(8,128)(2,1)} collective-permute-done((bf16[64,4224]{1,0:T(8,128)(2,1)}, bf16[64,4224]{1,0:T(8,128)(2,1)}, u32[]{:S(2)}, u32[]{:S(2)}) %collective-permute-start.2) | collective-permute-done | bytes 540704 | tf_op jit(solution)/shard_map/ppermute | solution.py:281
  23.9 12.0 %collective-permute-done.6.refs_2_ = bf16[64,4224]{1,0:T(8,128)(2,1)} collective-permute-done((bf16[64,4224]{1,0:T(8,128)(2,1)}, bf16[64,4224]{1,0:T(8,128)(2,1)}, u32[]{:S(2)}, u32[]{:S(2)}) %collective-permute-start.6) | collective-permute-done | bytes 540704 | tf_op jit(solution)/shard_map/ppermute | solution.py:281
  40.6 10.6 %collective-permute-done.8.refs_3_ = bf16[64,4224]{1,0:T(8,128)(2,1)S(1)} collective-permute-done((bf16[64,4224]{1,0:T(8,128)(2,1)}, bf16[64,4224]{1,0:T(8,128)(2,1)S(1)}, u32[]{:S(2)}, u32[]{:S(2)}) %collective-permute-start.8) | collective-permute-done | bytes 540704 | tf_op jit(solution)/shard_map/ppermute | solution.py:281
  54.0 8.3 %collective-permute-done.10.refs_7_ = bf16[64,4224]{1,0:T(8,128)(2,1)S(1)} collective-permute-done((bf16[64,4224]{1,0:T(8,128)(2,1)S(1)}, bf16[64,4224]{1,0:T(8,128)(2,1)S(1)}, u32[]{:S(2)}, u32[]{:S(2)}) %collective-permute-start.10) | collective-permute-done | bytes 540704 | tf_op jit(solution)/shard_map/ppermute | solution.py:278
  63.3 5.7 %plan_and_pack.2 = (bf16[256,2048]{1,0:T(8,128)(2,1)}, bf16[256,2048]{1,0:T(8,128)(2,1)}, bf16[256,128]{1,0:T(8,128)(2,1)}, bf16[256,4224]{1,0:T(8,128)(2,1)}, bf16[256,512]{1,0:T(8,128)(2,1)}) custom-call(s32[1]{0:T(128)} %bitcast.expert_ref, bf16[64,4224]{1,0:T(8,128)(2,1)} %pair_up.1.refs_0_, bf16[64,4224]{1,0:T(8,128)(2,1)} %collective-permute-done.2.refs_1_, ...), custom_call_target="tpu_custom_call" | custom-call | flops 1 | bytes 1 | tf_op jit(solution)/shard_map/plan_and_pack/pallas_call | solution.py:185
  70.7 3.0 %collective-permute-done.11 = bf16[256,4224]{1,0:T(8,128)(2,1)} collective-permute-done((bf16[256,4224]{1,0:T(8,128)(2,1)}, bf16[256,4224]{1,0:T(8,128)(2,1)}, u32[]{:S(2)}, u32[]{:S(2)}) %collective-permute-start.11) | collective-permute-done | bytes 2162720 | tf_op jit(solution)/shard_map/ppermute | solution.py:275
  87.2 2.2 %multiply_convert_fusion.5 = (bf16[512,768]{1,0:T(8,128)(2,1)S(1)}, bf16[512,768]{1,0:T(8,128)(2,1)S(1)}) fusion(f32[512,768]{1,0:T(8,128)S(1)} %fusion.28, f32[512,768]{1,0:T(8,128)S(1)} %get-tuple-element.89, bf16[512,2048]{1,0:T(8,128)(2,1)S(1)} %multiply_convert_fusion.1, bf16[1,768,2048]{2,1,0:T(8,128)(2,1)S(1)} %copy-done), kind=kOutput, calls=%fused_computation.59 | convolution fusion | flops 1615724544 | bytes 9961472 | tf_op jit(solution)/shard_map/dot_general | solution.py:41
  95.8 3.0 %collective-permute-done.14.refs_2_ = bf16[128,2048]{1,0:T(8,128)(2,1)S(1)} collective-permute-done((bf16[128,2048]{1,0:T(8,128)(2,1)S(1)}, bf16[128,2048]{1,0:T(8,128)(2,1)S(1)}, u32[]{:S(2)}, u32[]{:S(2)}) %collective-permute-start.14) | collective-permute-done | bytes 524320 | tf_op jit(solution)/shard_map/ppermute | solution.py:278
  103.2 6.9 %collective-permute-done.15.refs_3_ = bf16[128,2048]{1,0:T(8,128)(2,1)} collective-permute-done((bf16[128,2048]{1,0:T(8,128)(2,1)S(1)}, bf16[128,2048]{1,0:T(8,128)(2,1)}, u32[]{:S(2)}, u32[]{:S(2)}) %collective-permute-start.15) | collective-permute-done | bytes 524320 | tf_op jit(solution)/shard_map/ppermute | solution.py:278
  110.1 3.2 %spread.2 = (bf16[64,2048]{1,0:T(8,128)(2,1)}, bf16[64,2048]{1,0:T(8,128)(2,1)}, bf16[64,2048]{1,0:T(8,128)(2,1)}, bf16[64,2048]{1,0:T(8,128)(2,1)}) custom-call(bf16[256,512]{1,0:T(8,128)(2,1)} %get-tuple-element.49.place_ref, bf16[128,2048]{1,0:T(8,128)(2,1)} %fusion.58.refs_0_, bf16[256,2048]{1,0:T(8,128)(2,1)} %copy-done.9, ...), custom_call_target="tpu_custom_call" | custom-call | flops 1 | bytes 1 | tf_op jit(solution)/shard_map/spread/pallas_call | solution.py:220
  115.8 4.2 %fusion.76 = f32[384,2048]{1,0:T(8,128)} fusion(bf16[512,2048]{1,0:T(8,128)(2,1)} %copy-done.5, bf16[512,768]{1,0:T(8,128)(2,1)S(1)} %get-tuple-element.88, s32[]{:T(128)S(6)} %select_n.27), kind=kOutput, calls=%fused_computation.73 | convolution fusion | flops 805306368 | bytes 5636100 | tf_op jit(solution)/shard_map/dot_general | solution.py:55
  120.1 2.7 %fusion.94 = f32[1024,768]{1,0:T(8,128)} fusion(bf16[512,768]{1,0:T(8,128)(2,1)S(1)} %copy-done.19, s32[]{:T(128)S(6)} %select_n.26, bf16[256,2048]{1,0:T(8,128)(2,1)S(1)} %copy-done.27, bf16[256,2048]{1,0:T(8,128)(2,1)S(1)} %copy-done.15), kind=kOutput, calls=%fused_computation.98 | convolution fusion | flops 807403520 | bytes 6029316 | tf_op jit(solution)/shard_map/dot_general | solution.py:55
  124.5 2.8 %fusion.92 = f32[1024,768]{1,0:T(8,128)} fusion(bf16[512,768]{1,0:T(8,128)(2,1)S(1)} %copy-done.21, s32[]{:T(128)S(6)} %select_n.26, bf16[256,2048]{1,0:T(8,128)(2,1)S(1)} %copy-done.27, bf16[256,2048]{1,0:T(8,128)(2,1)S(1)} %copy-done.15), kind=kOutput, calls=%fused_computation.97 | convolution fusion | flops 807403520 | bytes 6029316 | tf_op jit(solution)/shard_map/dot_general | solution.py:55
  127.2 5.7 %plan_and_pack.3 = (bf16[256,2048]{1,0:T(8,128)(2,1)}, bf16[256,2048]{1,0:T(8,128)(2,1)}, bf16[256,128]{1,0:T(8,128)(2,1)}, bf16[256,4224]{1,0:T(8,128)(2,1)}, bf16[256,512]{1,0:T(8,128)(2,1)}) custom-call(s32[1]{0:T(128)} %bitcast.expert_ref, bf16[64,4224]{1,0:T(8,128)(2,1)} %collective-permute-done.7.refs_0_, ...), custom_call_target="tpu_custom_call" | custom-call | flops 1 | bytes 1 | tf_op jit(solution)/shard_map/plan_and_pack/pallas_call | solution.py:185
  132.9 3.1 %collective-permute-done.17 = bf16[64,2048]{1,0:T(8,128)(2,1)} collective-permute-done((bf16[64,2048]{1,0:T(8,128)(2,1)}, bf16[64,2048]{1,0:T(8,128)(2,1)}, u32[]{:S(2)}, u32[]{:S(2)}) %collective-permute-start.17) | collective-permute-done | bytes 262176 | tf_op jit(solution)/shard_map/ppermute | solution.py:281
  136.1 3.2 %spread.3 = (bf16[64,2048]{1,0:T(8,128)(2,1)}, bf16[64,2048]{1,0:T(8,128)(2,1)}, bf16[64,2048]{1,0:T(8,128)(2,1)}, bf16[64,2048]{1,0:T(8,128)(2,1)}) custom-call(bf16[256,512]{1,0:T(8,128)(2,1)} %get-tuple-element.49.place_ref, bf16[128,2048]{1,0:T(8,128)(2,1)} %fusion.64.refs_0_, bf16[256,2048]{1,0:T(8,128)(2,1)} %copy-done.8, ...), custom_call_target="tpu_custom_call" | custom-call | flops 1 | bytes 1 | tf_op jit(solution)/shard_map/spread/pallas_call | solution.py:220
  139.3 2.6 %collective-permute-start.23 = (bf16[64,2048]{1,0:T(8,128)(2,1)}, bf16[64,2048]{1,0:T(8,128)(2,1)S(1)}, u32[]{:S(2)}, u32[]{:S(2)}) collective-permute-start(bf16[64,2048]{1,0:T(8,128)(2,1)} %get-tuple-element.69), channel_id=1, source_target_pairs={{0,24},{2,26},{4,28},{6,30},{8,0},{10,2},{12,4},{14,6},{16,8},{18,... | collective-permute-start | bytes 786440 | tf_op jit(solution)/shard_map/ppermute | solution.py:281
  150.6 2.3 %multiply_convert_fusion.2 = (bf16[512,768]{1,0:T(8,128)(2,1)S(1)}, bf16[512,768]{1,0:T(8,128)(2,1)S(1)}, f32[512,768]{1,0:T(8,128)S(1)}) fusion(f32[512,768]{1,0:T(8,128)S(1)} %fusion.20, f32[512,768]{1,0:T(8,128)S(1)} %fusion.10, bf16[1,768,2048]{2,1,0:T(8,128)(2,1)S(1)} %copy-done, bf16[256,2048]{1,0:T(8,128)(2,1)S(1)} %get-tuple-element.81, ...), kind=kOutput, calls=%fused_computation.55 | convolution fusion | flops 1622016000 | bytes 11536384 | tf_op jit(solution)/shard_map/dot_general | solution.py:41
  153.0 2.5 %fusion.36 = bf16[1,384,2048]{2,1,0:T(8,128)(2,1)} fusion(f32[384,2048]{1,0:T(8,128)S(1)} %copy-done.4, f32[512,768]{1,0:T(8,128)S(1)} %fusion.10, s32[]{:T(128)S(6)} %select_n.27, f32[512,768]{1,0:T(8,128)S(1)} %get-tuple-element.85, f32[512,768]{1,0:T(8,128)S(1)} %fusion.20, bf16[256,2048]{1,0:T(8,128)(2,1)S(1)} %get-tuple-element.81, ...), kind=kOutput, calls=%fused_computation.37 | convolution fusion | flops 813760512 | bytes 9177092 | tf_op jit(solution)/shard_map/dot_general | solution.py:55
  159.8 2.2 %fusion.68 = bf16[1,1024,768]{2,1,0:T(8,128)(2,1)} fusion(f32[1024,768]{1,0:T(8,128)S(1)} %copy-done.7, bf16[512,768]{1,0:T(8,128)(2,1)S(1)} %get-tuple-element.76, s32[]{:T(128)S(6)} %select_n.26, bf16[256,2048]{1,0:T(8,128)(2,1)S(1)} %copy-done.16, bf16[256,2048]{1,0:T(8,128)(2,1)S(1)} %get-tuple-element.82), kind=kOutput, calls=%fused_computation.62 | convolution fusion | flops 808976384 | bytes 7602180 | tf_op jit(solution)/shard_map/dot_general | solution.py:55
  162.0 4.1 %collective-permute-done.24 = bf16[64,2048]{1,0:T(8,128)(2,1)S(1)} collective-permute-done((bf16[64,2048]{1,0:T(8,128)(2,1)}, bf16[64,2048]{1,0:T(8,128)(2,1)S(1)}, u32[]{:S(2)}, u32[]{:S(2)}) %collective-permute-start.24) | collective-permute-done | bytes 262176 | tf_op jit(solution)/shard_map/ppermute | solution.py:281
  166.1 2.2 %add_convert_fusion.3 = (bf16[64,2048]{1,0:T(8,128)(2,1)}, bf16[64,2048]{1,0:T(8,128)(2,1)}) fusion(bf16[64,2048]{1,0:T(8,128)(2,1)S(1)} %collective-permute-done.25, bf16[64,2048]{1,0:T(8,128)(2,1)S(1)} %collective-permute-done.24, bf16[64,2048]{1,0:T(8,128)(2,1)S(1)} %collective-permute-done.23, bf16[64,2048]{1,0:T(8,128)(2,1)S(1)} %copy-done.24, ...), kind=kLoop, calls=%fused_computation.68 | loop fusion | flops 2097152 | bytes 2621440 | tf_op jit(solution)/shard_map/convert_element_type | solution.py:332
  (130 shorter events, 58.0 us)
Async XLA Ops:
  2.7 17.6 %collective-permute-start.2 = (bf16[64,4224]{1,0:T(8,128)(2,1)}, bf16[64,4224]{1,0:T(8,128)(2,1)}, u32[]{:S(2)}, u32[]{:S(2)}) collective-permute-start(bf16[64,4224]{1,0:T(8,128)(2,1)} %pair_up.1.refs_0_), channel_id=1, source_target_pairs={{0,8},{2,10},{4,12},{6,14},{8,16},{10,18},{12,20},{14,22},{16,24},... | collective-permute-start | bytes 1622024 | tf_op jit(solution)/shard_map/ppermute | solution.py:281
  5.8 17.6 %collective-permute-start = (bf16[64,4224]{1,0:T(8,128)(2,1)}, bf16[64,4224]{1,0:T(8,128)(2,1)}, u32[]{:S(2)}, u32[]{:S(2)}) collective-permute-start(bf16[64,4224]{1,0:T(8,128)(2,1)} %pair_up.1.refs_0_), channel_id=1, source_target_pairs={{0,4},{2,6},{4,0},{6,2},{8,12},{10,14},{12,8},{14,10},{16,20},{18,... | collective-permute-start | bytes 1622024 | tf_op jit(solution)/shard_map/ppermute | solution.py:278
  7.2 16.6 %collective-permute-start.7 = (bf16[64,4224]{1,0:T(8,128)(2,1)}, bf16[64,4224]{1,0:T(8,128)(2,1)}, u32[]{:S(2)}, u32[]{:S(2)}) collective-permute-start(bf16[64,4224]{1,0:T(8,128)(2,1)} %pair_up.1.refs_0_), channel_id=1, source_target_pairs={{0,1},{1,0},{2,3},{3,2},{4,5},{5,4},{6,7},{7,6},{8,9},{9,8},{10,11... | collective-permute-start | bytes 1622024 | tf_op jit(solution)/shard_map/ppermute | solution.py:286
  20.4 15.6 %collective-permute-start.6 = (bf16[64,4224]{1,0:T(8,128)(2,1)}, bf16[64,4224]{1,0:T(8,128)(2,1)}, u32[]{:S(2)}, u32[]{:S(2)}) collective-permute-start(bf16[64,4224]{1,0:T(8,128)(2,1)} %collective-permute-done.2.refs_1_), channel_id=1, source_target_pairs={{0,8},{2,10},{4,12},{6,14},{8,16},{10,18},{12,20},{14,22},{16,24},... | collective-permute-start | bytes 1622024 | tf_op jit(solution)/shard_map/ppermute | solution.py:281
  20.4 16.8 %collective-permute-start.4 = (bf16[64,4224]{1,0:T(8,128)(2,1)}, bf16[64,4224]{1,0:T(8,128)(2,1)}, u32[]{:S(2)}, u32[]{:S(2)}) collective-permute-start(bf16[64,4224]{1,0:T(8,128)(2,1)} %collective-permute-done.2.refs_1_), channel_id=1, source_target_pairs={{0,4},{2,6},{4,0},{6,2},{8,12},{10,14},{12,8},{14,10},{16,20},{18,... | collective-permute-start | bytes 1622024 | tf_op jit(solution)/shard_map/ppermute | solution.py:278
  21.9 41.3 %collective-permute-start.3 = (bf16[64,4224]{1,0:T(8,128)(2,1)}, bf16[64,4224]{1,0:T(8,128)(2,1)}, u32[]{:S(2)}, u32[]{:S(2)}) collective-permute-start(bf16[64,4224]{1,0:T(8,128)(2,1)} %collective-permute-done.2.refs_1_), channel_id=1, source_target_pairs={{0,1},{1,0},{2,3},{3,2},{4,5},{5,4},{6,7},{7,6},{8,9},{9,8},{10,11... | collective-permute-start | bytes 1622024 | tf_op jit(solution)/shard_map/ppermute | solution.py:286
  23.4 39.8 %collective-permute-start.1 = (bf16[64,4224]{1,0:T(8,128)(2,1)}, bf16[64,4224]{1,0:T(8,128)(2,1)}, u32[]{:S(2)}, u32[]{:S(2)}) collective-permute-start(bf16[64,4224]{1,0:T(8,128)(2,1)} %collective-permute-done.refs_4_), channel_id=1, source_target_pairs={{0,1},{1,0},{2,3},{3,2},{4,5},{5,4},{6,7},{7,6},{8,9},{9,8},{10,11... | collective-permute-start | bytes 1622024 | tf_op jit(solution)/shard_map/ppermute | solution.py:286
  35.9 17.2 %collective-permute-start.9 = (bf16[64,4224]{1,0:T(8,128)(2,1)}, bf16[64,4224]{1,0:T(8,128)(2,1)S(1)}, u32[]{:S(2)}, u32[]{:S(2)}) collective-permute-start(bf16[64,4224]{1,0:T(8,128)(2,1)} %collective-permute-done.6.refs_2_), channel_id=1, source_target_pairs={{0,4},{2,6},{4,0},{6,2},{8,12},{10,14},{12,8},{14,10},{16,20},{18,... | collective-permute-start | bytes 1622024 | tf_op jit(solution)/shard_map/ppermute | solution.py:278
  37.2 14.0 %collective-permute-start.8 = (bf16[64,4224]{1,0:T(8,128)(2,1)}, bf16[64,4224]{1,0:T(8,128)(2,1)S(1)}, u32[]{:S(2)}, u32[]{:S(2)}) collective-permute-start(bf16[64,4224]{1,0:T(8,128)(2,1)} %collective-permute-done.6.refs_2_), channel_id=1, source_target_pairs={{0,8},{2,10},{4,12},{6,14},{8,16},{10,18},{12,20},{14,22},{16,24},... | collective-permute-start | bytes 1622024 | tf_op jit(solution)/shard_map/ppermute | solution.py:281
  37.2 26.0 %collective-permute-start.5 = (bf16[64,4224]{1,0:T(8,128)(2,1)}, bf16[64,4224]{1,0:T(8,128)(2,1)}, u32[]{:S(2)}, u32[]{:S(2)}) collective-permute-start(bf16[64,4224]{1,0:T(8,128)(2,1)} %collective-permute-done.4.refs_5_), channel_id=1, source_target_pairs={{0,1},{1,0},{2,3},{3,2},{4,5},{5,4},{6,7},{7,6},{8,9},{9,8},{10,11... | collective-permute-start | bytes 1622024 | tf_op jit(solution)/shard_map/ppermute | solution.py:286
  51.2 11.1 %collective-permute-start.10 = (bf16[64,4224]{1,0:T(8,128)(2,1)S(1)}, bf16[64,4224]{1,0:T(8,128)(2,1)S(1)}, u32[]{:S(2)}, u32[]{:S(2)}) collective-permute-start(bf16[64,4224]{1,0:T(8,128)(2,1)S(1)} %collective-permute-done.8.refs_3_), channel_id=1, source_target_pairs={{0,4},{2,6},{4,0},{6,2},{8,12},{10,14},{12,8},{14,10},{16,20},{18,... | collective-permute-start | bytes 1622024 | tf_op jit(solution)/shard_map/ppermute | solution.py:278
  69.1 58.1 %collective-permute-start.20 = (bf16[256,4224]{1,0:T(8,128)(2,1)}, bf16[256,4224]{1,0:T(8,128)(2,1)}, u32[]{:S(2)}, u32[]{:S(2)}) collective-permute-start(bf16[256,4224]{1,0:T(8,128)(2,1)} %constant_dynamic-update-slice_fusion), channel_id=1, source_target_pairs={{0,1},{1,0},{2,3},{3,2},{4,5},{5,4},{6,7},{7,6},{8,9},{9,8},{10,11... | collective-permute-start | bytes 6488072 | tf_op jit(solution)/shard_map/ppermute | solution.py:286
  83.9 14.8 %collective-permute-start.14 = (bf16[128,2048]{1,0:T(8,128)(2,1)S(1)}, bf16[128,2048]{1,0:T(8,128)(2,1)S(1)}, u32[]{:S(2)}, u32[]{:S(2)}) collective-permute-start(bf16[128,2048]{1,0:T(8,128)(2,1)S(1)} %fusion.55), channel_id=1, source_target_pairs={{0,4},{2,6},{4,0},{6,2},{8,12},{10,14},{12,8},{14,10},{16,20},{18,... | collective-permute-start | bytes 1572872 | tf_op jit(solution)/shard_map/ppermute | solution.py:278
  91.5 11.7 %collective-permute-start.13 = (bf16[256,2048]{1,0:T(8,128)(2,1)S(1)}, bf16[256,2048]{1,0:T(8,128)(2,1)S(1)}, u32[]{:S(2)}, u32[]{:S(2)}) collective-permute-start(bf16[256,2048]{1,0:T(8,128)(2,1)S(1)} %fusion.40), channel_id=1, source_target_pairs={{0,2},{2,0},{4,6},{6,4},{8,10},{10,8},{12,14},{14,12},{16,18},{18,... | collective-permute-start | bytes 3145736 | tf_op jit(solution)/shard_map/ppermute | solution.py:275
  93.0 17.1 %collective-permute-start.15 = (bf16[128,2048]{1,0:T(8,128)(2,1)S(1)}, bf16[128,2048]{1,0:T(8,128)(2,1)}, u32[]{:S(2)}, u32[]{:S(2)}) collective-permute-start(bf16[128,2048]{1,0:T(8,128)(2,1)S(1)} %slice.93), channel_id=1, source_target_pairs={{0,4},{2,6},{4,0},{6,2},{8,12},{10,14},{12,8},{14,10},{16,20},{18,... | collective-permute-start | bytes 1572872 | tf_op jit(solution)/shard_map/ppermute | solution.py:278
  98.8 24.0 %collective-permute-start.19 = (bf16[128,2048]{1,0:T(8,128)(2,1)}, bf16[128,2048]{1,0:T(8,128)(2,1)}, u32[]{:S(2)}, u32[]{:S(2)}) collective-permute-start(bf16[128,2048]{1,0:T(8,128)(2,1)} %fusion.61), channel_id=1, source_target_pairs={{0,4},{2,6},{4,0},{6,2},{8,12},{10,14},{12,8},{14,10},{16,20},{18,... | collective-permute-start | bytes 1572872 | tf_op jit(solution)/shard_map/ppermute | solution.py:278
  113.3 19.6 %collective-permute-start.16 = (bf16[64,2048]{1,0:T(8,128)(2,1)}, bf16[64,2048]{1,0:T(8,128)(2,1)}, u32[]{:S(2)}, u32[]{:S(2)}) collective-permute-start(bf16[64,2048]{1,0:T(8,128)(2,1)} %get-tuple-element.51), channel_id=1, source_target_pairs={{0,24},{2,26},{4,28},{6,30},{8,0},{10,2},{12,4},{14,6},{16,8},{18,... | collective-permute-start | bytes 786440 | tf_op jit(solution)/shard_map/ppermute | solution.py:281
  113.3 22.7 %collective-permute-start.17 = (bf16[64,2048]{1,0:T(8,128)(2,1)}, bf16[64,2048]{1,0:T(8,128)(2,1)}, u32[]{:S(2)}, u32[]{:S(2)}) collective-permute-start(bf16[64,2048]{1,0:T(8,128)(2,1)} %get-tuple-element.52), channel_id=1, source_target_pairs={{0,16},{2,18},{4,20},{6,22},{8,24},{10,26},{12,28},{14,30},{16,0},... | collective-permute-start | bytes 786440 | tf_op jit(solution)/shard_map/ppermute | solution.py:281
  114.5 21.5 %collective-permute-start.21 = (bf16[128,2048]{1,0:T(8,128)(2,1)}, bf16[128,2048]{1,0:T(8,128)(2,1)}, u32[]{:S(2)}, u32[]{:S(2)}) collective-permute-start(bf16[128,2048]{1,0:T(8,128)(2,1)} %slice.96), channel_id=1, source_target_pairs={{0,4},{2,6},{4,0},{6,2},{8,12},{10,14},{12,8},{14,10},{16,20},{18,... | collective-permute-start | bytes 1572872 | tf_op jit(solution)/shard_map/ppermute | solution.py:278
  122.8 13.3 %collective-permute-start.18 = (bf16[64,2048]{1,0:T(8,128)(2,1)S(1)}, bf16[64,2048]{1,0:T(8,128)(2,1)S(1)}, u32[]{:S(2)}, u32[]{:S(2)}) collective-permute-start(bf16[64,2048]{1,0:T(8,128)(2,1)S(1)} %copy-done.28), channel_id=1, source_target_pairs={{0,8},{2,10},{4,12},{6,14},{8,16},{10,18},{12,20},{14,22},{16,24},... | collective-permute-start | bytes 786440 | tf_op jit(solution)/shard_map/ppermute | solution.py:281
  136.1 8.0 %collective-permute-start.22 = (bf16[256,4224]{1,0:T(8,128)(2,1)}, bf16[256,4224]{1,0:T(8,128)(2,1)}, u32[]{:S(2)}, u32[]{:S(2)}) collective-permute-start(bf16[256,4224]{1,0:T(8,128)(2,1)} %get-tuple-element.61), channel_id=1, source_target_pairs={{0,2},{2,0},{4,6},{6,4},{8,10},{10,8},{12,14},{14,12},{16,18},{18,... | collective-permute-start | bytes 6488072 | tf_op jit(solution)/shard_map/ppermute | solution.py:275
  139.3 16.1 %collective-permute-start.23 = (bf16[64,2048]{1,0:T(8,128)(2,1)}, bf16[64,2048]{1,0:T(8,128)(2,1)S(1)}, u32[]{:S(2)}, u32[]{:S(2)}) collective-permute-start(bf16[64,2048]{1,0:T(8,128)(2,1)} %get-tuple-element.69), channel_id=1, source_target_pairs={{0,24},{2,26},{4,28},{6,30},{8,0},{10,2},{12,4},{14,6},{16,8},{18,... | collective-permute-start | bytes 786440 | tf_op jit(solution)/shard_map/ppermute | solution.py:281
  141.9 24.2 %collective-permute-start.24 = (bf16[64,2048]{1,0:T(8,128)(2,1)}, bf16[64,2048]{1,0:T(8,128)(2,1)S(1)}, u32[]{:S(2)}, u32[]{:S(2)}) collective-permute-start(bf16[64,2048]{1,0:T(8,128)(2,1)} %get-tuple-element.70), channel_id=1, source_target_pairs={{0,16},{2,18},{4,20},{6,22},{8,24},{10,26},{12,28},{14,30},{16,0},... | collective-permute-start | bytes 786440 | tf_op jit(solution)/shard_map/ppermute | solution.py:281
  142.1 24.0 %collective-permute-start.25 = (bf16[64,2048]{1,0:T(8,128)(2,1)}, bf16[64,2048]{1,0:T(8,128)(2,1)S(1)}, u32[]{:S(2)}, u32[]{:S(2)}) collective-permute-start(bf16[64,2048]{1,0:T(8,128)(2,1)} %get-tuple-element.71), channel_id=1, source_target_pairs={{0,8},{2,10},{4,12},{6,14},{8,16},{10,18},{12,20},{14,22},{16,24},... | collective-permute-start | bytes 786440 | tf_op jit(solution)/shard_map/ppermute | solution.py:281
  (31 other events, 230.1 us)

commit v19 on v18

--- a/solution.py
+++ b/solution.py
@@ -114,7 +114,7 @@
 ANYWHERE = pl.BlockSpec(memory_space=pl.ANY)
 
 
-def plan_and_pack(expert, experts, capacity, tok_rows, pieces):
+def sources_of(pieces):
     arrays = []
     for array, _ in pieces:
         if not any(array is a for a in arrays):
@@ -122,6 +122,25 @@
     sources = [
         (next(k for k, a in enumerate(arrays) if a is array), chunk) for array, chunk in pieces
     ]
+    return arrays, sources
+
+
+def load(refs, sources, tok_rows, rows_ref, sems):
+    copies = []
+    for i, (source, chunk) in enumerate(sources):
+        copies.append(
+            pltpu.make_async_copy(
+                refs[source].at[chunk * tok_rows : (chunk + 1) * tok_rows],
+                rows_ref.at[i * tok_rows : (i + 1) * tok_rows],
+                sems.at[i],
+            )
+        )
+        copies[-1].start()
+    return copies
+
+
+def plan_and_pack(expert, experts, capacity, tok_rows, pieces, with_mine):
+    arrays, sources = sources_of(pieces)
     width = arrays[0].shape[1]
     features = (width - LANES) // 2
     groups, each = 2, len(pieces) // 2
@@ -129,17 +148,8 @@
 
     def body(expert_ref, *refs):
         outs = refs[len(arrays) :]
-        token_mine, cot_mine, lane_mine, theirs_ref, place_ref, rows_ref, sems = outs
-        copies = []
-        for i, (source, chunk) in enumerate(sources):
-            copies.append(
-                pltpu.make_async_copy(
-                    refs[source].at[chunk * tok_rows : (chunk + 1) * tok_rows],
-                    rows_ref.at[i * tok_rows : (i + 1) * tok_rows],
-                    sems.at[i],
-                )
-            )
-            copies[-1].start()
+        mine_refs, (theirs_ref, place_ref, rows_ref, sems) = outs[:-4], outs[-4:]
+        copies = load(refs, sources, tok_rows, rows_ref, sems)
         lane = lax.broadcasted_iota(jnp.int32, (length, LANES), 1)
         row = lax.broadcasted_iota(jnp.int32, (length, length), 0)
         col = lax.broadcasted_iota(jnp.int32, (length, length), 1)
@@ -168,20 +178,26 @@
                 place_ref[:, 2 * room :] = places(lanes.astype(F32), expert_ref[0] ^ 2).astype(BF)
             pick = place.T.astype(BF)
             here = slice(group * room, (group + 1) * room)
+            if not with_mine:
+                mine_refs[0][group] = pick[:room]
+                pick = pick[room:]
             packed = dot(pick, lanes).astype(BF)
-            lane_mine[here] = packed[:room]
-            theirs_ref[here, 2 * features :] = packed[room:]
+            if with_mine:
+                mine_refs[2][here] = packed[:room]
+            theirs_ref[here, 2 * features :] = packed[-room:]
             for at in range(0, 2 * features, 512):
                 packed = dot(pick, rows_ref[held_rows, at : at + 512]).astype(BF)
-                mine_ref = token_mine if at < features else cot_mine
-                mine_ref[here, at % features : at % features + 512] = packed[:room]
-                theirs_ref[here, at : at + 512] = packed[room:]
+                if with_mine:
+                    mine_ref = mine_refs[at // features]
+                    mine_ref[here, at % features : at % features + 512] = packed[:room]
+                theirs_ref[here, at : at + 512] = packed[-room:]
 
     rows = jax.ShapeDtypeStruct((groups * room, features), BF)
     lanes = jax.ShapeDtypeStruct((groups * room, LANES), BF)
     theirs = jax.ShapeDtypeStruct((groups * room, width), BF)
     place = jax.ShapeDtypeStruct((length, 4 * room), BF)
-    outs = (rows, rows, lanes, theirs, place)
+    pick = jax.ShapeDtypeStruct((groups, room, length), BF)
+    outs = ((rows, rows, lanes) if with_mine else (pick,)) + (theirs, place)
     return pl.pallas_call(
         body,
         grid_spec=pltpu.PrefetchScalarGridSpec(
@@ -201,6 +217,43 @@
     )(expert, *arrays)
 
 
+def pack_mine(pick, tok_rows, pieces):
+    arrays, sources = sources_of(pieces)
+    groups, room, length = pick.shape
+    width = arrays[0].shape[1]
+    features = (width - LANES) // 2
+    each = len(pieces) // groups
+
+    def body(pick_ref, *refs):
+        outs, (rows_ref, sems) = refs[len(arrays) : -2], refs[-2:]
+        copies = load(refs, sources, tok_rows, rows_ref, sems)
+        for group in range(groups):
+            for copy in copies[group * each : (group + 1) * each]:
+                copy.wait()
+            held_rows = slice(group * length, (group + 1) * length)
+            here = slice(group * room, (group + 1) * room)
+            for at in range(0, width, 512):
+                cols = slice(at, min(at + 512, width))
+                packed = dot(pick_ref[group], rows_ref[held_rows, cols]).astype(BF)
+                start = at % features
+                outs[at // features][here, start : start + cols.stop - at] = packed
+
+    rows = jax.ShapeDtypeStruct((groups * room, features), BF)
+    lanes = jax.ShapeDtypeStruct((groups * room, LANES), BF)
+    return pl.pallas_call(
+        body,
+        in_specs=[pl.BlockSpec(memory_space=pltpu.VMEM)] + [ANYWHERE] * len(arrays),
+        out_shape=(rows, rows, lanes),
+        scratch_shapes=[
+            pltpu.VMEM((groups * length, width), BF),
+            pltpu.SemaphoreType.DMA((len(pieces),)),
+        ],
+        compiler_params=params(),
+        cost_estimate=SMALL,
+        name="pack_mine",
+    )(pick, *arrays)
+
+
 def spread(place, mine, theirs, far_mine, far_theirs):
     length, slots_of = place.shape
     room, features = far_mine.shape
@@ -302,12 +355,12 @@
     expert_index = expert
     expert = expert.reshape(1)
 
-    def plan(pieces, *earlier):
-        return plan_and_pack(after(expert, *earlier), experts, capacity, tok_rows, pieces)
-
-    def enter(packed):
-        mine, cot_mine, mine_lanes, theirs, _ = packed
-        theirs = to_core(theirs)
+    def plan(pieces, with_mine, *earlier):
+        return plan_and_pack(
+            after(expert, *earlier), experts, capacity, tok_rows, pieces, with_mine
+        )
+
+    def enter(mine, cot_mine, mine_lanes, theirs):
         x = jnp.concatenate([mine, theirs[:, :features]], axis=0)
         shares = jnp.concatenate([mine_lanes, theirs[:, 2 * features :]], axis=0)
         held = (jnp.arange(LANES) % experts == expert_index) & (jnp.arange(LANES) < 3 * experts)
@@ -336,9 +389,9 @@
         act = lax.dynamic_slice_in_dim(act, replica * (hidden // 2), hidden // 2, 1)
         return outer_sum(x, d_gate), outer_sum(x, d_up), outer_sum(act, cot)
 
-    packed = plan(own_pieces, *relay[1:4], joined)
-    place = packed[-1]
-    own_x, weight, pre_gate, pre_up, act, cot = enter(packed)
+    pick, theirs, place = plan(own_pieces, False, *relay[1:4], joined)
+    mine = pack_mine(pick, tok_rows, own_pieces)
+    own_x, weight, pre_gate, pre_up, act, cot = enter(*mine, to_core(theirs))
     parts = leave(lambda rows: (dot(act[rows], w_down) * weight[rows]).astype(BF))
     cot = after(cot, parts[0], parts[1])
     d_gate, d_up = hidden_grads(cot, pre_gate, pre_up, w_down)
@@ -349,11 +402,11 @@
     chunks = home(after(place, grad_parts[0], grad_parts[1]), parts)
     own_grads = after((cot, d_gate, d_up), chunks[0])
     own = grads(own_x, act, *own_grads)
-    packed = list(plan(other_pieces, *own, grad_parts[2]))
-    packed[3] = after(packed[3], grad_parts[3], *chunks[1:])
-    grad_chunks = home(after(place, packed[-1]), grad_parts)
-
-    x, weight, pre_gate, pre_up, act, cot = enter(packed)
+    *mine, theirs, _ = plan(other_pieces, True, *own, grad_parts[2])
+    theirs = to_core(after(theirs, grad_parts[3], *chunks[1:]))
+    grad_chunks = home(after(place, mine[0]), grad_parts)
+
+    x, weight, pre_gate, pre_up, act, cot = enter(*mine, theirs)
     d_gate, d_up = hidden_grads(cot, pre_gate, pre_up, w_down)
     chunks = after(chunks, d_gate)
     other = grads(x, act, cot, d_gate, after(d_up, grad_chunks[1]))

time: 169 us -> 170 us (level)
  Pallas kernels: 19.9 us -> 23.6 us
    pallas_call x0 -> x1, Pallas kernels: none -> 4.78 us  [pack_mine(): pl.pallas_call(body, in_specs=[pl.BlockSpec(memory_space=pltpu.VMEM)] + [...]
    ppermute x4, waiting for transfers between devices: 2.99 us -> 0.01 us  [to_core(): return lax.ppermute(rows, 'expert', [(i, i ^ 1) for i in range(experts)])]
  transfers between devices with their start and end apart: 26 -> 26, of which waited for: 9 -> 8; matrix products, arithmetic and copies ran while one was open for 31% -> 31% of each run, Pallas kernels for 7% -> 10%
where the time goes in v19:
time: 170 us; the launch traced here: 169 us
  waiting for transfers between devices  61.1 us (36%)
  matrix products  38.8 us (23%)
  starting transfers between devices  25.4 us (15%)
  Pallas kernels  23.6 us (14%)
  local copies, waits for them, and re-layouts  13.8 us (8%)
  other arithmetic  5.13 us (3%)
    ppermute x9, waiting for transfers between devices, to_z(): lax.ppermute(rows, 'expert', [(i, (i + 4 * step) % experts) for i in rang...  42.2 us
    ppermute x8, waiting for transfers between devices, to_x(): return lax.ppermute(rows, 'expert', [(i, i ^ 2) for i in range(experts)])  18.9 us
    dot_general x6, matrix products, outer_sum(): lax.dot_general(left, right, (((0,), (0,)), ((), ())), preferred_element_...  15.5 us
    pallas_call x2, Pallas kernels, plan_and_pack(): pl.pallas_call(body, grid_spec=pltpu.PrefetchScalarGridSpec(num_scalar_pr...  10.3 us
    dot_general x7, matrix products, dot(): return jnp.dot(left, right, preferred_element_type=F32)  10.3 us
    ppermute x9, starting transfers between devices, to_z(): lax.ppermute(rows, 'expert', [(i, (i + 4 * step) % experts) for i in rang...  9.88 us
    ppermute x8, starting transfers between devices, to_x(): return lax.ppermute(rows, 'expert', [(i, i ^ 2) for i in range(experts)])  8.49 us
    unnamed x61, local copies, waits for them, and re-layouts  6.77 us
  transfers between devices with their start and end apart: 26, of which 8 were waited for; matrix products, arithmetic and copies ran while one was open for 31% of the time, Pallas kernels for 10%

profile of v19, /device:TPU:0, one launch (start us, length us, event | category | flops | bytes accessed | tf_op | source)
XLA Modules:
  0.0 169.1 jit_solution(17442811589257190210)
XLA Ops:
  0.6 2.1 %pair_up.1.refs_0_ = bf16[64,4224]{1,0:T(8,128)(2,1)} custom-call(bf16[64,2048]{1,0:T(8,128)(2,1)} %tokens_ref.1, bf16[64,2048]{1,0:T(8,128)(2,1)} %cots_ref.1, s32[6,64]{1,0:T(8,128)} %bitcast.78, f32[6,64]{1,0:T(8,128)} %bitcast.79), custom_call_target="tpu_custom_call" | custom-call | flops 1 | bytes 1 | tf_op jit(solution)/shard_map/pair_up/pallas_call | solution.py:305
  2.7 3.0 %collective-permute-start.2 = (bf16[64,4224]{1,0:T(8,128)(2,1)}, bf16[64,4224]{1,0:T(8,128)(2,1)}, u32[]{:S(2)}, u32[]{:S(2)}) collective-permute-start(bf16[64,4224]{1,0:T(8,128)(2,1)} %pair_up.1.refs_0_), channel_id=1, source_target_pairs={{0,8},{2,10},{4,12},{6,14},{8,16},{10,18},{12,20},{14,22},{16,24},... | collective-permute-start | bytes 1622024 | tf_op jit(solution)/shard_map/ppermute | solution.py:334
  8.8 11.6 %collective-permute-done.2.refs_1_ = bf16[64,4224]{1,0:T(8,128)(2,1)} collective-permute-done((bf16[64,4224]{1,0:T(8,128)(2,1)}, bf16[64,4224]{1,0:T(8,128)(2,1)}, u32[]{:S(2)}, u32[]{:S(2)}) %collective-permute-start.2) | collective-permute-done | bytes 540704 | tf_op jit(solution)/shard_map/ppermute | solution.py:334
  23.9 12.0 %collective-permute-done.6.refs_2_ = bf16[64,4224]{1,0:T(8,128)(2,1)} collective-permute-done((bf16[64,4224]{1,0:T(8,128)(2,1)}, bf16[64,4224]{1,0:T(8,128)(2,1)}, u32[]{:S(2)}, u32[]{:S(2)}) %collective-permute-start.6) | collective-permute-done | bytes 540704 | tf_op jit(solution)/shard_map/ppermute | solution.py:334
  40.6 10.6 %collective-permute-done.8.refs_3_ = bf16[64,4224]{1,0:T(8,128)(2,1)S(1)} collective-permute-done((bf16[64,4224]{1,0:T(8,128)(2,1)}, bf16[64,4224]{1,0:T(8,128)(2,1)S(1)}, u32[]{:S(2)}, u32[]{:S(2)}) %collective-permute-start.8) | collective-permute-done | bytes 540704 | tf_op jit(solution)/shard_map/ppermute | solution.py:334
  54.0 8.3 %collective-permute-done.10.refs_7_ = bf16[64,4224]{1,0:T(8,128)(2,1)S(1)} collective-permute-done((bf16[64,4224]{1,0:T(8,128)(2,1)S(1)}, bf16[64,4224]{1,0:T(8,128)(2,1)S(1)}, u32[]{:S(2)}, u32[]{:S(2)}) %collective-permute-start.10) | collective-permute-done | bytes 540704 | tf_op jit(solution)/shard_map/ppermute | solution.py:331
  63.3 4.7 %plan_and_pack.2 = (bf16[2,128,256]{2,1,0:T(8,128)(2,1)}, bf16[256,4224]{1,0:T(8,128)(2,1)}, bf16[256,512]{1,0:T(8,128)(2,1)}) custom-call(s32[1]{0:T(128)} %bitcast.expert_ref, bf16[64,4224]{1,0:T(8,128)(2,1)} %pair_up.1.refs_0_, bf16[64,4224]{1,0:T(8,128)(2,1)} %collective-permute-done.2.refs_1_, bf16[64,4224]{1,0:T(8,128)(2,1)} %collective-permute-done.6.refs_2_, ...), custom_call_target="tpu_custom_call" | custom-call | flops 1 | bytes 1 | tf_op jit(solution)/shard_map/plan_and_pack/pallas_call | solution.py:201
  69.7 4.8 %pack_mine.1 = (bf16[256,2048]{1,0:T(8,128)(2,1)}, bf16[256,2048]{1,0:T(8,128)(2,1)}, bf16[256,128]{1,0:T(8,128)(2,1)}) custom-call(bf16[2,128,256]{2,1,0:T(8,128)(2,1)} %get-tuple-element.46.pick_ref, bf16[64,4224]{1,0:T(8,128)(2,1)} %pair_up.1.refs_0_, bf16[64,4224]{1,0:T(8,128)(2,1)} %collective-permute-done.2.refs_1_, ...), custom_call_target="tpu_custom_call" | custom-call | flops 1 | bytes 1 | tf_op jit(solution)/shard_map/pack_mine/pallas_call | solution.py:243
  87.3 2.4 %multiply_convert_fusion.5 = (bf16[512,768]{1,0:T(8,128)(2,1)S(1)}, bf16[512,768]{1,0:T(8,128)(2,1)S(1)}) fusion(f32[512,768]{1,0:T(8,128)S(1)} %fusion.28, f32[512,768]{1,0:T(8,128)S(1)} %get-tuple-element.93, bf16[512,2048]{1,0:T(8,128)(2,1)S(1)} %multiply_convert_fusion.1, bf16[1,768,2048]{2,1,0:T(8,128)(2,1)S(1)} %copy-done), kind=kOutput, calls=%fused_computation.59 | convolution fusion | flops 1615724544 | bytes 9961472 | tf_op jit(solution)/shard_map/dot_general | solution.py:41
  96.8 2.9 %collective-permute-done.14.refs_2_ = bf16[128,2048]{1,0:T(8,128)(2,1)S(1)} collective-permute-done((bf16[128,2048]{1,0:T(8,128)(2,1)S(1)}, bf16[128,2048]{1,0:T(8,128)(2,1)S(1)}, u32[]{:S(2)}, u32[]{:S(2)}) %collective-permute-start.14) | collective-permute-done | bytes 524320 | tf_op jit(solution)/shard_map/ppermute | solution.py:331
  103.3 7.7 %collective-permute-done.15.refs_3_ = bf16[128,2048]{1,0:T(8,128)(2,1)} collective-permute-done((bf16[128,2048]{1,0:T(8,128)(2,1)S(1)}, bf16[128,2048]{1,0:T(8,128)(2,1)}, u32[]{:S(2)}, u32[]{:S(2)}) %collective-permute-start.15) | collective-permute-done | bytes 524320 | tf_op jit(solution)/shard_map/ppermute | solution.py:331
  111.0 3.2 %spread.2 = (bf16[64,2048]{1,0:T(8,128)(2,1)}, bf16[64,2048]{1,0:T(8,128)(2,1)}, bf16[64,2048]{1,0:T(8,128)(2,1)}, bf16[64,2048]{1,0:T(8,128)(2,1)}) custom-call(bf16[256,512]{1,0:T(8,128)(2,1)} %get-tuple-element.71.place_ref, bf16[128,2048]{1,0:T(8,128)(2,1)} %fusion.58.refs_0_, bf16[256,2048]{1,0:T(8,128)(2,1)} %copy-done.12, ...), custom_call_target="tpu_custom_call" | custom-call | flops 1 | bytes 1 | tf_op jit(solution)/shard_map/spread/pallas_call | solution.py:273
  115.9 4.5 %fusion.76 = f32[384,2048]{1,0:T(8,128)} fusion(bf16[512,2048]{1,0:T(8,128)(2,1)} %copy-done.5, bf16[512,768]{1,0:T(8,128)(2,1)S(1)} %get-tuple-element.92, s32[]{:T(128)S(6)} %select_n.27), kind=kOutput, calls=%fused_computation.73 | convolution fusion | flops 805306368 | bytes 5636100 | tf_op jit(solution)/shard_map/dot_general | solution.py:55
  120.5 2.7 %fusion.94 = f32[1024,768]{1,0:T(8,128)} fusion(bf16[512,768]{1,0:T(8,128)(2,1)S(1)} %copy-done.19, s32[]{:T(128)S(6)} %select_n.26, bf16[256,2048]{1,0:T(8,128)(2,1)S(1)} %copy-done.27, bf16[256,2048]{1,0:T(8,128)(2,1)S(1)} %copy-done.15), kind=kOutput, calls=%fused_computation.98 | convolution fusion | flops 807403520 | bytes 6029316 | tf_op jit(solution)/shard_map/dot_general | solution.py:55
  124.8 2.7 %fusion.92 = f32[1024,768]{1,0:T(8,128)} fusion(bf16[512,768]{1,0:T(8,128)(2,1)S(1)} %copy-done.21, s32[]{:T(128)S(6)} %select_n.26, bf16[256,2048]{1,0:T(8,128)(2,1)S(1)} %copy-done.27, bf16[256,2048]{1,0:T(8,128)(2,1)S(1)} %copy-done.15), kind=kOutput, calls=%fused_computation.97 | convolution fusion | flops 807403520 | bytes 6029316 | tf_op jit(solution)/shard_map/dot_general | solution.py:55
  127.6 5.7 %plan_and_pack.3 = (bf16[256,2048]{1,0:T(8,128)(2,1)}, bf16[256,2048]{1,0:T(8,128)(2,1)}, bf16[256,128]{1,0:T(8,128)(2,1)}, bf16[256,4224]{1,0:T(8,128)(2,1)}, bf16[256,512]{1,0:T(8,128)(2,1)}) custom-call(s32[1]{0:T(128)} %bitcast.expert_ref, bf16[64,4224]{1,0:T(8,128)(2,1)} %collective-permute-done.7.refs_0_, ...), custom_call_target="tpu_custom_call" | custom-call | flops 1 | bytes 1 | tf_op jit(solution)/shard_map/plan_and_pack/pallas_call | solution.py:201
  133.3 3.6 %collective-permute-done.17 = bf16[64,2048]{1,0:T(8,128)(2,1)} collective-permute-done((bf16[64,2048]{1,0:T(8,128)(2,1)}, bf16[64,2048]{1,0:T(8,128)(2,1)}, u32[]{:S(2)}, u32[]{:S(2)}) %collective-permute-start.17) | collective-permute-done | bytes 262176 | tf_op jit(solution)/shard_map/ppermute | solution.py:334
  136.9 3.2 %spread.3 = (bf16[64,2048]{1,0:T(8,128)(2,1)}, bf16[64,2048]{1,0:T(8,128)(2,1)}, bf16[64,2048]{1,0:T(8,128)(2,1)}, bf16[64,2048]{1,0:T(8,128)(2,1)}) custom-call(bf16[256,512]{1,0:T(8,128)(2,1)} %get-tuple-element.71.place_ref, bf16[128,2048]{1,0:T(8,128)(2,1)} %fusion.64.refs_0_, bf16[256,2048]{1,0:T(8,128)(2,1)} %copy-done.11, ...), custom_call_target="tpu_custom_call" | custom-call | flops 1 | bytes 1 | tf_op jit(solution)/shard_map/spread/pallas_call | solution.py:273
  142.9 2.0 %collective-permute-start.25 = (bf16[64,2048]{1,0:T(8,128)(2,1)}, bf16[64,2048]{1,0:T(8,128)(2,1)S(1)}, u32[]{:S(2)}, u32[]{:S(2)}) collective-permute-start(bf16[64,2048]{1,0:T(8,128)(2,1)} %get-tuple-element.75), channel_id=1, source_target_pairs={{0,8},{2,10},{4,12},{6,14},{8,16},{10,18},{12,20},{14,22},{16,24},... | collective-permute-start | bytes 786440 | tf_op jit(solution)/shard_map/ppermute | solution.py:334
  151.4 2.2 %multiply_convert_fusion.2 = (bf16[512,768]{1,0:T(8,128)(2,1)S(1)}, bf16[512,768]{1,0:T(8,128)(2,1)S(1)}, f32[512,768]{1,0:T(8,128)S(1)}) fusion(f32[512,768]{1,0:T(8,128)S(1)} %fusion.20, f32[512,768]{1,0:T(8,128)S(1)} %fusion.10, bf16[1,768,2048]{2,1,0:T(8,128)(2,1)S(1)} %copy-done, bf16[256,2048]{1,0:T(8,128)(2,1)S(1)} %get-tuple-element.85, ...), kind=kOutput, calls=%fused_computation.55 | convolution fusion | flops 1622016000 | bytes 11536384 | tf_op jit(solution)/shard_map/dot_general | solution.py:41
  153.7 2.4 %fusion.36 = bf16[1,384,2048]{2,1,0:T(8,128)(2,1)} fusion(f32[384,2048]{1,0:T(8,128)S(1)} %copy-done.4, f32[512,768]{1,0:T(8,128)S(1)} %fusion.10, s32[]{:T(128)S(6)} %select_n.27, f32[512,768]{1,0:T(8,128)S(1)} %get-tuple-element.89, f32[512,768]{1,0:T(8,128)S(1)} %fusion.20, bf16[256,2048]{1,0:T(8,128)(2,1)S(1)} %get-tuple-element.85, ...), kind=kOutput, calls=%fused_computation.37 | convolution fusion | flops 813760512 | bytes 9177092 | tf_op jit(solution)/shard_map/dot_general | solution.py:55
  160.4 2.2 %fusion.68 = bf16[1,1024,768]{2,1,0:T(8,128)(2,1)} fusion(f32[1024,768]{1,0:T(8,128)S(1)} %copy-done.10, bf16[512,768]{1,0:T(8,128)(2,1)S(1)} %get-tuple-element.80, s32[]{:T(128)S(6)} %select_n.26, bf16[256,2048]{1,0:T(8,128)(2,1)S(1)} %copy-done.16, bf16[256,2048]{1,0:T(8,128)(2,1)S(1)} %get-tuple-element.86), kind=kOutput, calls=%fused_computation.62 | convolution fusion | flops 808976384 | bytes 7602180 | tf_op jit(solution)/shard_map/dot_general | solution.py:55
  162.5 4.4 %collective-permute-done.24 = bf16[64,2048]{1,0:T(8,128)(2,1)S(1)} collective-permute-done((bf16[64,2048]{1,0:T(8,128)(2,1)}, bf16[64,2048]{1,0:T(8,128)(2,1)S(1)}, u32[]{:S(2)}, u32[]{:S(2)}) %collective-permute-start.24) | collective-permute-done | bytes 262176 | tf_op jit(solution)/shard_map/ppermute | solution.py:334
  166.9 2.1 %add_convert_fusion.3 = (bf16[64,2048]{1,0:T(8,128)(2,1)}, bf16[64,2048]{1,0:T(8,128)(2,1)}) fusion(bf16[64,2048]{1,0:T(8,128)(2,1)S(1)} %collective-permute-done.25, bf16[64,2048]{1,0:T(8,128)(2,1)S(1)} %collective-permute-done.24, bf16[64,2048]{1,0:T(8,128)(2,1)S(1)} %collective-permute-done.23, bf16[64,2048]{1,0:T(8,128)(2,1)S(1)} %copy-done.24, ...), kind=kLoop, calls=%fused_computation.68 | loop fusion | flops 2097152 | bytes 2621440 | tf_op jit(solution)/shard_map/convert_element_type | solution.py:385
  (131 shorter events, 57.1 us)
Async XLA Ops:
  2.7 17.6 %collective-permute-start.2 = (bf16[64,4224]{1,0:T(8,128)(2,1)}, bf16[64,4224]{1,0:T(8,128)(2,1)}, u32[]{:S(2)}, u32[]{:S(2)}) collective-permute-start(bf16[64,4224]{1,0:T(8,128)(2,1)} %pair_up.1.refs_0_), channel_id=1, source_target_pairs={{0,8},{2,10},{4,12},{6,14},{8,16},{10,18},{12,20},{14,22},{16,24},... | collective-permute-start | bytes 1622024 | tf_op jit(solution)/shard_map/ppermute | solution.py:334
  5.8 17.6 %collective-permute-start = (bf16[64,4224]{1,0:T(8,128)(2,1)}, bf16[64,4224]{1,0:T(8,128)(2,1)}, u32[]{:S(2)}, u32[]{:S(2)}) collective-permute-start(bf16[64,4224]{1,0:T(8,128)(2,1)} %pair_up.1.refs_0_), channel_id=1, source_target_pairs={{0,4},{2,6},{4,0},{6,2},{8,12},{10,14},{12,8},{14,10},{16,20},{18,... | collective-permute-start | bytes 1622024 | tf_op jit(solution)/shard_map/ppermute | solution.py:331
  7.2 16.6 %collective-permute-start.7 = (bf16[64,4224]{1,0:T(8,128)(2,1)}, bf16[64,4224]{1,0:T(8,128)(2,1)}, u32[]{:S(2)}, u32[]{:S(2)}) collective-permute-start(bf16[64,4224]{1,0:T(8,128)(2,1)} %pair_up.1.refs_0_), channel_id=1, source_target_pairs={{0,1},{1,0},{2,3},{3,2},{4,5},{5,4},{6,7},{7,6},{8,9},{9,8},{10,11... | collective-permute-start | bytes 1622024 | tf_op jit(solution)/shard_map/ppermute | solution.py:339
  20.4 15.6 %collective-permute-start.6 = (bf16[64,4224]{1,0:T(8,128)(2,1)}, bf16[64,4224]{1,0:T(8,128)(2,1)}, u32[]{:S(2)}, u32[]{:S(2)}) collective-permute-start(bf16[64,4224]{1,0:T(8,128)(2,1)} %collective-permute-done.2.refs_1_), channel_id=1, source_target_pairs={{0,8},{2,10},{4,12},{6,14},{8,16},{10,18},{12,20},{14,22},{16,24},... | collective-permute-start | bytes 1622024 | tf_op jit(solution)/shard_map/ppermute | solution.py:334
  20.4 16.8 %collective-permute-start.4 = (bf16[64,4224]{1,0:T(8,128)(2,1)}, bf16[64,4224]{1,0:T(8,128)(2,1)}, u32[]{:S(2)}, u32[]{:S(2)}) collective-permute-start(bf16[64,4224]{1,0:T(8,128)(2,1)} %collective-permute-done.2.refs_1_), channel_id=1, source_target_pairs={{0,4},{2,6},{4,0},{6,2},{8,12},{10,14},{12,8},{14,10},{16,20},{18,... | collective-permute-start | bytes 1622024 | tf_op jit(solution)/shard_map/ppermute | solution.py:331
  21.9 41.3 %collective-permute-start.3 = (bf16[64,4224]{1,0:T(8,128)(2,1)}, bf16[64,4224]{1,0:T(8,128)(2,1)}, u32[]{:S(2)}, u32[]{:S(2)}) collective-permute-start(bf16[64,4224]{1,0:T(8,128)(2,1)} %collective-permute-done.2.refs_1_), channel_id=1, source_target_pairs={{0,1},{1,0},{2,3},{3,2},{4,5},{5,4},{6,7},{7,6},{8,9},{9,8},{10,11... | collective-permute-start | bytes 1622024 | tf_op jit(solution)/shard_map/ppermute | solution.py:339
  23.4 39.8 %collective-permute-start.1 = (bf16[64,4224]{1,0:T(8,128)(2,1)}, bf16[64,4224]{1,0:T(8,128)(2,1)}, u32[]{:S(2)}, u32[]{:S(2)}) collective-permute-start(bf16[64,4224]{1,0:T(8,128)(2,1)} %collective-permute-done.refs_4_), channel_id=1, source_target_pairs={{0,1},{1,0},{2,3},{3,2},{4,5},{5,4},{6,7},{7,6},{8,9},{9,8},{10,11... | collective-permute-start | bytes 1622024 | tf_op jit(solution)/shard_map/ppermute | solution.py:339
  35.9 17.2 %collective-permute-start.9 = (bf16[64,4224]{1,0:T(8,128)(2,1)}, bf16[64,4224]{1,0:T(8,128)(2,1)S(1)}, u32[]{:S(2)}, u32[]{:S(2)}) collective-permute-start(bf16[64,4224]{1,0:T(8,128)(2,1)} %collective-permute-done.6.refs_2_), channel_id=1, source_target_pairs={{0,4},{2,6},{4,0},{6,2},{8,12},{10,14},{12,8},{14,10},{16,20},{18,... | collective-permute-start | bytes 1622024 | tf_op jit(solution)/shard_map/ppermute | solution.py:331
  37.2 14.0 %collective-permute-start.8 = (bf16[64,4224]{1,0:T(8,128)(2,1)}, bf16[64,4224]{1,0:T(8,128)(2,1)S(1)}, u32[]{:S(2)}, u32[]{:S(2)}) collective-permute-start(bf16[64,4224]{1,0:T(8,128)(2,1)} %collective-permute-done.6.refs_2_), channel_id=1, source_target_pairs={{0,8},{2,10},{4,12},{6,14},{8,16},{10,18},{12,20},{14,22},{16,24},... | collective-permute-start | bytes 1622024 | tf_op jit(solution)/shard_map/ppermute | solution.py:334
  37.2 26.0 %collective-permute-start.5 = (bf16[64,4224]{1,0:T(8,128)(2,1)}, bf16[64,4224]{1,0:T(8,128)(2,1)}, u32[]{:S(2)}, u32[]{:S(2)}) collective-permute-start(bf16[64,4224]{1,0:T(8,128)(2,1)} %collective-permute-done.4.refs_5_), channel_id=1, source_target_pairs={{0,1},{1,0},{2,3},{3,2},{4,5},{5,4},{6,7},{7,6},{8,9},{9,8},{10,11... | collective-permute-start | bytes 1622024 | tf_op jit(solution)/shard_map/ppermute | solution.py:339
  51.2 11.1 %collective-permute-start.10 = (bf16[64,4224]{1,0:T(8,128)(2,1)S(1)}, bf16[64,4224]{1,0:T(8,128)(2,1)S(1)}, u32[]{:S(2)}, u32[]{:S(2)}) collective-permute-start(bf16[64,4224]{1,0:T(8,128)(2,1)S(1)} %collective-permute-done.8.refs_3_), channel_id=1, source_target_pairs={{0,4},{2,6},{4,0},{6,2},{8,12},{10,14},{12,8},{14,10},{16,20},{18,... | collective-permute-start | bytes 1622024 | tf_op jit(solution)/shard_map/ppermute | solution.py:331
  68.1 59.5 %collective-permute-start.20 = (bf16[256,4224]{1,0:T(8,128)(2,1)}, bf16[256,4224]{1,0:T(8,128)(2,1)}, u32[]{:S(2)}, u32[]{:S(2)}) collective-permute-start(bf16[256,4224]{1,0:T(8,128)(2,1)} %constant_dynamic-update-slice_fusion), channel_id=1, source_target_pairs={{0,1},{1,0},{2,3},{3,2},{4,5},{5,4},{6,7},{7,6},{8,9},{9,8},{10,11... | collective-permute-start | bytes 6488072 | tf_op jit(solution)/shard_map/ppermute | solution.py:339
  84.8 14.8 %collective-permute-start.14 = (bf16[128,2048]{1,0:T(8,128)(2,1)S(1)}, bf16[128,2048]{1,0:T(8,128)(2,1)S(1)}, u32[]{:S(2)}, u32[]{:S(2)}) collective-permute-start(bf16[128,2048]{1,0:T(8,128)(2,1)S(1)} %fusion.55), channel_id=1, source_target_pairs={{0,4},{2,6},{4,0},{6,2},{8,12},{10,14},{12,8},{14,10},{16,20},{18,... | collective-permute-start | bytes 1572872 | tf_op jit(solution)/shard_map/ppermute | solution.py:331
  91.7 11.6 %collective-permute-start.13 = (bf16[256,2048]{1,0:T(8,128)(2,1)S(1)}, bf16[256,2048]{1,0:T(8,128)(2,1)S(1)}, u32[]{:S(2)}, u32[]{:S(2)}) collective-permute-start(bf16[256,2048]{1,0:T(8,128)(2,1)S(1)} %fusion.40), channel_id=1, source_target_pairs={{0,2},{2,0},{4,6},{6,4},{8,10},{10,8},{12,14},{14,12},{16,18},{18,... | collective-permute-start | bytes 3145736 | tf_op jit(solution)/shard_map/ppermute | solution.py:328
  93.2 17.8 %collective-permute-start.15 = (bf16[128,2048]{1,0:T(8,128)(2,1)S(1)}, bf16[128,2048]{1,0:T(8,128)(2,1)}, u32[]{:S(2)}, u32[]{:S(2)}) collective-permute-start(bf16[128,2048]{1,0:T(8,128)(2,1)S(1)} %slice.93), channel_id=1, source_target_pairs={{0,4},{2,6},{4,0},{6,2},{8,12},{10,14},{12,8},{14,10},{16,20},{18,... | collective-permute-start | bytes 1572872 | tf_op jit(solution)/shard_map/ppermute | solution.py:331
  99.6 23.5 %collective-permute-start.19 = (bf16[128,2048]{1,0:T(8,128)(2,1)}, bf16[128,2048]{1,0:T(8,128)(2,1)}, u32[]{:S(2)}, u32[]{:S(2)}) collective-permute-start(bf16[128,2048]{1,0:T(8,128)(2,1)} %fusion.61), channel_id=1, source_target_pairs={{0,4},{2,6},{4,0},{6,2},{8,12},{10,14},{12,8},{14,10},{16,20},{18,... | collective-permute-start | bytes 1572872 | tf_op jit(solution)/shard_map/ppermute | solution.py:331
  114.2 19.0 %collective-permute-start.16 = (bf16[64,2048]{1,0:T(8,128)(2,1)}, bf16[64,2048]{1,0:T(8,128)(2,1)}, u32[]{:S(2)}, u32[]{:S(2)}) collective-permute-start(bf16[64,2048]{1,0:T(8,128)(2,1)} %get-tuple-element.54), channel_id=1, source_target_pairs={{0,24},{2,26},{4,28},{6,30},{8,0},{10,2},{12,4},{14,6},{16,8},{18,... | collective-permute-start | bytes 786440 | tf_op jit(solution)/shard_map/ppermute | solution.py:334
  114.2 22.7 %collective-permute-start.17 = (bf16[64,2048]{1,0:T(8,128)(2,1)}, bf16[64,2048]{1,0:T(8,128)(2,1)}, u32[]{:S(2)}, u32[]{:S(2)}) collective-permute-start(bf16[64,2048]{1,0:T(8,128)(2,1)} %get-tuple-element.55), channel_id=1, source_target_pairs={{0,16},{2,18},{4,20},{6,22},{8,24},{10,26},{12,28},{14,30},{16,0},... | collective-permute-start | bytes 786440 | tf_op jit(solution)/shard_map/ppermute | solution.py:334
  115.4 21.5 %collective-permute-start.21 = (bf16[128,2048]{1,0:T(8,128)(2,1)}, bf16[128,2048]{1,0:T(8,128)(2,1)}, u32[]{:S(2)}, u32[]{:S(2)}) collective-permute-start(bf16[128,2048]{1,0:T(8,128)(2,1)} %slice.96), channel_id=1, source_target_pairs={{0,4},{2,6},{4,0},{6,2},{8,12},{10,14},{12,8},{14,10},{16,20},{18,... | collective-permute-start | bytes 1572872 | tf_op jit(solution)/shard_map/ppermute | solution.py:331
  123.2 13.7 %collective-permute-start.18 = (bf16[64,2048]{1,0:T(8,128)(2,1)S(1)}, bf16[64,2048]{1,0:T(8,128)(2,1)S(1)}, u32[]{:S(2)}, u32[]{:S(2)}) collective-permute-start(bf16[64,2048]{1,0:T(8,128)(2,1)S(1)} %copy-done.28), channel_id=1, source_target_pairs={{0,8},{2,10},{4,12},{6,14},{8,16},{10,18},{12,20},{14,22},{16,24},... | collective-permute-start | bytes 786440 | tf_op jit(solution)/shard_map/ppermute | solution.py:334
  136.9 8.0 %collective-permute-start.22 = (bf16[256,4224]{1,0:T(8,128)(2,1)}, bf16[256,4224]{1,0:T(8,128)(2,1)}, u32[]{:S(2)}, u32[]{:S(2)}) collective-permute-start(bf16[256,4224]{1,0:T(8,128)(2,1)} %get-tuple-element.64), channel_id=1, source_target_pairs={{0,2},{2,0},{4,6},{6,4},{8,10},{10,8},{12,14},{14,12},{16,18},{18,... | collective-permute-start | bytes 6488072 | tf_op jit(solution)/shard_map/ppermute | solution.py:328
  140.1 15.9 %collective-permute-start.23 = (bf16[64,2048]{1,0:T(8,128)(2,1)}, bf16[64,2048]{1,0:T(8,128)(2,1)S(1)}, u32[]{:S(2)}, u32[]{:S(2)}) collective-permute-start(bf16[64,2048]{1,0:T(8,128)(2,1)} %get-tuple-element.73), channel_id=1, source_target_pairs={{0,24},{2,26},{4,28},{6,30},{8,0},{10,2},{12,4},{14,6},{16,8},{18,... | collective-permute-start | bytes 786440 | tf_op jit(solution)/shard_map/ppermute | solution.py:334
  142.1 24.8 %collective-permute-start.24 = (bf16[64,2048]{1,0:T(8,128)(2,1)}, bf16[64,2048]{1,0:T(8,128)(2,1)S(1)}, u32[]{:S(2)}, u32[]{:S(2)}) collective-permute-start(bf16[64,2048]{1,0:T(8,128)(2,1)} %get-tuple-element.74), channel_id=1, source_target_pairs={{0,16},{2,18},{4,20},{6,22},{8,24},{10,26},{12,28},{14,30},{16,0},... | collective-permute-start | bytes 786440 | tf_op jit(solution)/shard_map/ppermute | solution.py:334
  142.9 24.0 %collective-permute-start.25 = (bf16[64,2048]{1,0:T(8,128)(2,1)}, bf16[64,2048]{1,0:T(8,128)(2,1)S(1)}, u32[]{:S(2)}, u32[]{:S(2)}) collective-permute-start(bf16[64,2048]{1,0:T(8,128)(2,1)} %get-tuple-element.75), channel_id=1, source_target_pairs={{0,8},{2,10},{4,12},{6,14},{8,16},{10,18},{12,20},{14,22},{16,24},... | collective-permute-start | bytes 786440 | tf_op jit(solution)/shard_map/ppermute | solution.py:334
  (31 other events, 229.6 us)

commit v20 on v18

--- a/solution.py
+++ b/solution.py
@@ -350,8 +350,8 @@
     own_grads = after((cot, d_gate, d_up), chunks[0])
     own = grads(own_x, act, *own_grads)
     packed = list(plan(other_pieces, *own, grad_parts[2]))
-    packed[3] = after(packed[3], grad_parts[3], *chunks[1:])
     grad_chunks = home(after(place, packed[-1]), grad_parts)
+    packed[3] = after(packed[3], grad_chunks[0], *chunks[1:])
 
     x, weight, pre_gate, pre_up, act, cot = enter(packed)
     d_gate, d_up = hidden_grads(cot, pre_gate, pre_up, w_down)

time: 169 us -> 166 us (0.982)
  local copies, waits for them, and re-layouts: 13.8 us -> 11.5 us
  transfers between devices with their start and end apart: 26 -> 26, of which waited for: 9 -> 8; matrix products, arithmetic and copies ran while one was open for 31% -> 30% of each run, Pallas kernels for 7% -> 7%
where the time goes in v20:
time: 166 us; the launch traced here: 165 us
  waiting for transfers between devices  62 us (37%)
  matrix products  38.5 us (23%)
  starting transfers between devices  27.1 us (16%)
  Pallas kernels  19.9 us (12%)
  local copies, waits for them, and re-layouts  11.5 us (7%)
  other arithmetic  5.13 us (3%)
    ppermute x9, waiting for transfers between devices, to_z(): lax.ppermute(rows, 'expert', [(i, (i + 4 * step) % experts) for i in rang...  40.9 us
    ppermute x8, waiting for transfers between devices, to_x(): return lax.ppermute(rows, 'expert', [(i, i ^ 2) for i in range(experts)])  18.1 us
    dot_general x6, matrix products, outer_sum(): lax.dot_general(left, right, (((0,), (0,)), ((), ())), preferred_element_...  15.2 us
    pallas_call x2, Pallas kernels, plan_and_pack(): pl.pallas_call(body, grid_spec=pltpu.PrefetchScalarGridSpec(num_scalar_pr...  11.3 us
    dot_general x7, matrix products, dot(): return jnp.dot(left, right, preferred_element_type=F32)  10.3 us
    ppermute x9, starting transfers between devices, to_z(): lax.ppermute(rows, 'expert', [(i, (i + 4 * step) % experts) for i in rang...  10 us
    ppermute x8, starting transfers between devices, to_x(): return lax.ppermute(rows, 'expert', [(i, i ^ 2) for i in range(experts)])  9.96 us
    unnamed x61, local copies, waits for them, and re-layouts  6.79 us
  transfers between devices with their start and end apart: 26, of which 8 were waited for; matrix products, arithmetic and copies ran while one was open for 30% of the time, Pallas kernels for 7%

profile of v20, /device:TPU:0, one launch (start us, length us, event | category | flops | bytes accessed | tf_op | source)
XLA Modules:
  0.0 165.3 jit_solution(9753687604618985238)
XLA Ops:
  0.6 2.1 %pair_up.1.refs_0_ = bf16[64,4224]{1,0:T(8,128)(2,1)} custom-call(bf16[64,2048]{1,0:T(8,128)(2,1)} %tokens_ref.1, bf16[64,2048]{1,0:T(8,128)(2,1)} %cots_ref.1, s32[6,64]{1,0:T(8,128)} %bitcast.78, f32[6,64]{1,0:T(8,128)} %bitcast.79), custom_call_target="tpu_custom_call" | custom-call | flops 1 | bytes 1 | tf_op jit(solution)/shard_map/pair_up/pallas_call | solution.py:252
  2.7 3.0 %collective-permute-start.2 = (bf16[64,4224]{1,0:T(8,128)(2,1)}, bf16[64,4224]{1,0:T(8,128)(2,1)}, u32[]{:S(2)}, u32[]{:S(2)}) collective-permute-start(bf16[64,4224]{1,0:T(8,128)(2,1)} %pair_up.1.refs_0_), channel_id=1, source_target_pairs={{0,8},{2,10},{4,12},{6,14},{8,16},{10,18},{12,20},{14,22},{16,24},... | collective-permute-start | bytes 1622024 | tf_op jit(solution)/shard_map/ppermute | solution.py:281
  8.8 11.6 %collective-permute-done.2.refs_1_ = bf16[64,4224]{1,0:T(8,128)(2,1)} collective-permute-done((bf16[64,4224]{1,0:T(8,128)(2,1)}, bf16[64,4224]{1,0:T(8,128)(2,1)}, u32[]{:S(2)}, u32[]{:S(2)}) %collective-permute-start.2) | collective-permute-done | bytes 540704 | tf_op jit(solution)/shard_map/ppermute | solution.py:281
  23.9 12.0 %collective-permute-done.6.refs_2_ = bf16[64,4224]{1,0:T(8,128)(2,1)} collective-permute-done((bf16[64,4224]{1,0:T(8,128)(2,1)}, bf16[64,4224]{1,0:T(8,128)(2,1)}, u32[]{:S(2)}, u32[]{:S(2)}) %collective-permute-start.6) | collective-permute-done | bytes 540704 | tf_op jit(solution)/shard_map/ppermute | solution.py:281
  40.6 10.6 %collective-permute-done.8.refs_3_ = bf16[64,4224]{1,0:T(8,128)(2,1)S(1)} collective-permute-done((bf16[64,4224]{1,0:T(8,128)(2,1)}, bf16[64,4224]{1,0:T(8,128)(2,1)S(1)}, u32[]{:S(2)}, u32[]{:S(2)}) %collective-permute-start.8) | collective-permute-done | bytes 540704 | tf_op jit(solution)/shard_map/ppermute | solution.py:281
  54.0 8.3 %collective-permute-done.10.refs_7_ = bf16[64,4224]{1,0:T(8,128)(2,1)S(1)} collective-permute-done((bf16[64,4224]{1,0:T(8,128)(2,1)S(1)}, bf16[64,4224]{1,0:T(8,128)(2,1)S(1)}, u32[]{:S(2)}, u32[]{:S(2)}) %collective-permute-start.10) | collective-permute-done | bytes 540704 | tf_op jit(solution)/shard_map/ppermute | solution.py:278
  63.3 5.7 %plan_and_pack.2 = (bf16[256,2048]{1,0:T(8,128)(2,1)}, bf16[256,2048]{1,0:T(8,128)(2,1)}, bf16[256,128]{1,0:T(8,128)(2,1)}, bf16[256,4224]{1,0:T(8,128)(2,1)}, bf16[256,512]{1,0:T(8,128)(2,1)}) custom-call(s32[1]{0:T(128)} %bitcast.expert_ref, bf16[64,4224]{1,0:T(8,128)(2,1)} %pair_up.1.refs_0_, bf16[64,4224]{1,0:T(8,128)(2,1)} %collective-permute-done.2.refs_1_, ...), custom_call_target="tpu_custom_call" | custom-call | flops 1 | bytes 1 | tf_op jit(solution)/shard_map/plan_and_pack/pallas_call | solution.py:185
  70.7 3.0 %collective-permute-done.11 = bf16[256,4224]{1,0:T(8,128)(2,1)} collective-permute-done((bf16[256,4224]{1,0:T(8,128)(2,1)}, bf16[256,4224]{1,0:T(8,128)(2,1)}, u32[]{:S(2)}, u32[]{:S(2)}) %collective-permute-start.11) | collective-permute-done | bytes 2162720 | tf_op jit(solution)/shard_map/ppermute | solution.py:275
  87.2 2.4 %multiply_convert_fusion.5 = (bf16[512,768]{1,0:T(8,128)(2,1)S(1)}, bf16[512,768]{1,0:T(8,128)(2,1)S(1)}) fusion(f32[512,768]{1,0:T(8,128)S(1)} %fusion.28, f32[512,768]{1,0:T(8,128)S(1)} %get-tuple-element.89, bf16[512,2048]{1,0:T(8,128)(2,1)S(1)} %multiply_convert_fusion.1, bf16[1,768,2048]{2,1,0:T(8,128)(2,1)S(1)} %copy-done), kind=kOutput, calls=%fused_computation.59 | convolution fusion | flops 1615724544 | bytes 9961472 | tf_op jit(solution)/shard_map/dot_general | solution.py:41
  93.9 2.0 %fusion.61 = bf16[128,2048]{1,0:T(8,128)(2,1)} fusion(f32[128,2048]{1,0:T(8,128)S(1)} %fusion.12, bf16[1,2048,768]{2,1,0:T(8,128)(2,1)S(1)} %copy-done.1, bf16[512,768]{1,0:T(8,128)(2,1)S(1)} %get-tuple-element.54), kind=kOutput, calls=%fused_computation.46 | convolution fusion | flops 403177472 | bytes 4915200 | tf_op jit(solution)/shard_map/dot_general | solution.py:49
  96.0 2.8 %collective-permute-done.14.refs_2_ = bf16[128,2048]{1,0:T(8,128)(2,1)S(1)} collective-permute-done((bf16[128,2048]{1,0:T(8,128)(2,1)S(1)}, bf16[128,2048]{1,0:T(8,128)(2,1)S(1)}, u32[]{:S(2)}, u32[]{:S(2)}) %collective-permute-start.14) | collective-permute-done | bytes 524320 | tf_op jit(solution)/shard_map/ppermute | solution.py:278
  103.2 7.0 %collective-permute-done.15.refs_3_ = bf16[128,2048]{1,0:T(8,128)(2,1)} collective-permute-done((bf16[128,2048]{1,0:T(8,128)(2,1)S(1)}, bf16[128,2048]{1,0:T(8,128)(2,1)}, u32[]{:S(2)}, u32[]{:S(2)}) %collective-permute-start.15) | collective-permute-done | bytes 524320 | tf_op jit(solution)/shard_map/ppermute | solution.py:278
  110.1 3.2 %spread.2 = (bf16[64,2048]{1,0:T(8,128)(2,1)}, bf16[64,2048]{1,0:T(8,128)(2,1)}, bf16[64,2048]{1,0:T(8,128)(2,1)}, bf16[64,2048]{1,0:T(8,128)(2,1)}) custom-call(bf16[256,512]{1,0:T(8,128)(2,1)} %get-tuple-element.49.place_ref, bf16[128,2048]{1,0:T(8,128)(2,1)} %fusion.58.refs_0_, bf16[256,2048]{1,0:T(8,128)(2,1)} %copy-done.9, ...), custom_call_target="tpu_custom_call" | custom-call | flops 1 | bytes 1 | tf_op jit(solution)/shard_map/spread/pallas_call | solution.py:220
  115.8 4.2 %fusion.76 = f32[384,2048]{1,0:T(8,128)} fusion(bf16[512,2048]{1,0:T(8,128)(2,1)} %copy-done.5, bf16[512,768]{1,0:T(8,128)(2,1)S(1)} %get-tuple-element.88, s32[]{:T(128)S(6)} %select_n.27), kind=kOutput, calls=%fused_computation.73 | convolution fusion | flops 805306368 | bytes 5636100 | tf_op jit(solution)/shard_map/dot_general | solution.py:55
  120.1 2.7 %fusion.94 = f32[1024,768]{1,0:T(8,128)} fusion(bf16[512,768]{1,0:T(8,128)(2,1)S(1)} %copy-done.19, s32[]{:T(128)S(6)} %select_n.26, bf16[256,2048]{1,0:T(8,128)(2,1)S(1)} %copy-done.27, bf16[256,2048]{1,0:T(8,128)(2,1)S(1)} %copy-done.15), kind=kOutput, calls=%fused_computation.98 | convolution fusion | flops 807403520 | bytes 6029316 | tf_op jit(solution)/shard_map/dot_general | solution.py:55
  124.5 2.7 %fusion.92 = f32[1024,768]{1,0:T(8,128)} fusion(bf16[512,768]{1,0:T(8,128)(2,1)S(1)} %copy-done.21, s32[]{:T(128)S(6)} %select_n.26, bf16[256,2048]{1,0:T(8,128)(2,1)S(1)} %copy-done.27, bf16[256,2048]{1,0:T(8,128)(2,1)S(1)} %copy-done.15), kind=kOutput, calls=%fused_computation.97 | convolution fusion | flops 807403520 | bytes 6029316 | tf_op jit(solution)/shard_map/dot_general | solution.py:55
  127.2 5.7 %plan_and_pack.3 = (bf16[256,2048]{1,0:T(8,128)(2,1)}, bf16[256,2048]{1,0:T(8,128)(2,1)}, bf16[256,128]{1,0:T(8,128)(2,1)}, bf16[256,4224]{1,0:T(8,128)(2,1)}, bf16[256,512]{1,0:T(8,128)(2,1)}) custom-call(s32[1]{0:T(128)} %bitcast.expert_ref, bf16[64,4224]{1,0:T(8,128)(2,1)} %collective-permute-done.7.refs_0_, ...), custom_call_target="tpu_custom_call" | custom-call | flops 1 | bytes 1 | tf_op jit(solution)/shard_map/plan_and_pack/pallas_call | solution.py:185
  132.9 3.2 %spread.3 = (bf16[64,2048]{1,0:T(8,128)(2,1)}, bf16[64,2048]{1,0:T(8,128)(2,1)}, bf16[64,2048]{1,0:T(8,128)(2,1)}, bf16[64,2048]{1,0:T(8,128)(2,1)}) custom-call(bf16[256,512]{1,0:T(8,128)(2,1)} %get-tuple-element.49.place_ref, bf16[128,2048]{1,0:T(8,128)(2,1)} %fusion.64.refs_0_, bf16[256,2048]{1,0:T(8,128)(2,1)} %copy-done.8, ...), custom_call_target="tpu_custom_call" | custom-call | flops 1 | bytes 1 | tf_op jit(solution)/shard_map/spread/pallas_call | solution.py:220
  136.2 2.5 %collective-permute-start.23 = (bf16[64,2048]{1,0:T(8,128)(2,1)}, bf16[64,2048]{1,0:T(8,128)(2,1)S(1)}, u32[]{:S(2)}, u32[]{:S(2)}) collective-permute-start(bf16[64,2048]{1,0:T(8,128)(2,1)} %get-tuple-element.69), channel_id=1, source_target_pairs={{0,24},{2,26},{4,28},{6,30},{8,0},{10,2},{12,4},{14,6},{16,8},{18,... | collective-permute-start | bytes 786440 | tf_op jit(solution)/shard_map/ppermute | solution.py:281
  145.4 2.2 %multiply_convert_fusion.2 = (bf16[512,768]{1,0:T(8,128)(2,1)S(1)}, bf16[512,768]{1,0:T(8,128)(2,1)S(1)}, f32[512,768]{1,0:T(8,128)S(1)}) fusion(f32[512,768]{1,0:T(8,128)S(1)} %fusion.20, f32[512,768]{1,0:T(8,128)S(1)} %fusion.10, bf16[1,768,2048]{2,1,0:T(8,128)(2,1)S(1)} %copy-done, bf16[256,2048]{1,0:T(8,128)(2,1)S(1)} %get-tuple-element.81, ...), kind=kOutput, calls=%fused_computation.55 | convolution fusion | flops 1622016000 | bytes 11536384 | tf_op jit(solution)/shard_map/dot_general | solution.py:41
  147.6 2.4 %fusion.36 = bf16[1,384,2048]{2,1,0:T(8,128)(2,1)} fusion(f32[384,2048]{1,0:T(8,128)S(1)} %copy-done.4, f32[512,768]{1,0:T(8,128)S(1)} %fusion.10, s32[]{:T(128)S(6)} %select_n.27, f32[512,768]{1,0:T(8,128)S(1)} %get-tuple-element.85, f32[512,768]{1,0:T(8,128)S(1)} %fusion.20, bf16[256,2048]{1,0:T(8,128)(2,1)S(1)} %get-tuple-element.81, ...), kind=kOutput, calls=%fused_computation.37 | convolution fusion | flops 813760512 | bytes 9177092 | tf_op jit(solution)/shard_map/dot_general | solution.py:55
  154.3 2.2 %fusion.68 = bf16[1,1024,768]{2,1,0:T(8,128)(2,1)} fusion(f32[1024,768]{1,0:T(8,128)S(1)} %copy-done.7, bf16[512,768]{1,0:T(8,128)(2,1)S(1)} %get-tuple-element.76, s32[]{:T(128)S(6)} %select_n.26, bf16[256,2048]{1,0:T(8,128)(2,1)S(1)} %copy-done.16, bf16[256,2048]{1,0:T(8,128)(2,1)S(1)} %get-tuple-element.82), kind=kOutput, calls=%fused_computation.62 | convolution fusion | flops 808976384 | bytes 7602180 | tf_op jit(solution)/shard_map/dot_general | solution.py:55
  156.5 6.7 %collective-permute-done.24 = bf16[64,2048]{1,0:T(8,128)(2,1)S(1)} collective-permute-done((bf16[64,2048]{1,0:T(8,128)(2,1)}, bf16[64,2048]{1,0:T(8,128)(2,1)S(1)}, u32[]{:S(2)}, u32[]{:S(2)}) %collective-permute-start.24) | collective-permute-done | bytes 262176 | tf_op jit(solution)/shard_map/ppermute | solution.py:281
  163.2 2.1 %add_convert_fusion.3 = (bf16[64,2048]{1,0:T(8,128)(2,1)}, bf16[64,2048]{1,0:T(8,128)(2,1)}) fusion(bf16[64,2048]{1,0:T(8,128)(2,1)S(1)} %collective-permute-done.25, bf16[64,2048]{1,0:T(8,128)(2,1)S(1)} %collective-permute-done.24, bf16[64,2048]{1,0:T(8,128)(2,1)S(1)} %collective-permute-done.23, bf16[64,2048]{1,0:T(8,128)(2,1)S(1)} %copy-done.24, ...), kind=kLoop, calls=%fused_computation.68 | loop fusion | flops 2097152 | bytes 2621440 | tf_op jit(solution)/shard_map/convert_element_type | solution.py:332
  (130 shorter events, 54.0 us)
Async XLA Ops:
  2.7 17.6 %collective-permute-start.2 = (bf16[64,4224]{1,0:T(8,128)(2,1)}, bf16[64,4224]{1,0:T(8,128)(2,1)}, u32[]{:S(2)}, u32[]{:S(2)}) collective-permute-start(bf16[64,4224]{1,0:T(8,128)(2,1)} %pair_up.1.refs_0_), channel_id=1, source_target_pairs={{0,8},{2,10},{4,12},{6,14},{8,16},{10,18},{12,20},{14,22},{16,24},... | collective-permute-start | bytes 1622024 | tf_op jit(solution)/shard_map/ppermute | solution.py:281
  5.8 17.6 %collective-permute-start = (bf16[64,4224]{1,0:T(8,128)(2,1)}, bf16[64,4224]{1,0:T(8,128)(2,1)}, u32[]{:S(2)}, u32[]{:S(2)}) collective-permute-start(bf16[64,4224]{1,0:T(8,128)(2,1)} %pair_up.1.refs_0_), channel_id=1, source_target_pairs={{0,4},{2,6},{4,0},{6,2},{8,12},{10,14},{12,8},{14,10},{16,20},{18,... | collective-permute-start | bytes 1622024 | tf_op jit(solution)/shard_map/ppermute | solution.py:278
  7.2 16.6 %collective-permute-start.7 = (bf16[64,4224]{1,0:T(8,128)(2,1)}, bf16[64,4224]{1,0:T(8,128)(2,1)}, u32[]{:S(2)}, u32[]{:S(2)}) collective-permute-start(bf16[64,4224]{1,0:T(8,128)(2,1)} %pair_up.1.refs_0_), channel_id=1, source_target_pairs={{0,1},{1,0},{2,3},{3,2},{4,5},{5,4},{6,7},{7,6},{8,9},{9,8},{10,11... | collective-permute-start | bytes 1622024 | tf_op jit(solution)/shard_map/ppermute | solution.py:286
  20.4 15.6 %collective-permute-start.6 = (bf16[64,4224]{1,0:T(8,128)(2,1)}, bf16[64,4224]{1,0:T(8,128)(2,1)}, u32[]{:S(2)}, u32[]{:S(2)}) collective-permute-start(bf16[64,4224]{1,0:T(8,128)(2,1)} %collective-permute-done.2.refs_1_), channel_id=1, source_target_pairs={{0,8},{2,10},{4,12},{6,14},{8,16},{10,18},{12,20},{14,22},{16,24},... | collective-permute-start | bytes 1622024 | tf_op jit(solution)/shard_map/ppermute | solution.py:281
  20.4 16.8 %collective-permute-start.4 = (bf16[64,4224]{1,0:T(8,128)(2,1)}, bf16[64,4224]{1,0:T(8,128)(2,1)}, u32[]{:S(2)}, u32[]{:S(2)}) collective-permute-start(bf16[64,4224]{1,0:T(8,128)(2,1)} %collective-permute-done.2.refs_1_), channel_id=1, source_target_pairs={{0,4},{2,6},{4,0},{6,2},{8,12},{10,14},{12,8},{14,10},{16,20},{18,... | collective-permute-start | bytes 1622024 | tf_op jit(solution)/shard_map/ppermute | solution.py:278
  21.9 41.3 %collective-permute-start.3 = (bf16[64,4224]{1,0:T(8,128)(2,1)}, bf16[64,4224]{1,0:T(8,128)(2,1)}, u32[]{:S(2)}, u32[]{:S(2)}) collective-permute-start(bf16[64,4224]{1,0:T(8,128)(2,1)} %collective-permute-done.2.refs_1_), channel_id=1, source_target_pairs={{0,1},{1,0},{2,3},{3,2},{4,5},{5,4},{6,7},{7,6},{8,9},{9,8},{10,11... | collective-permute-start | bytes 1622024 | tf_op jit(solution)/shard_map/ppermute | solution.py:286
  23.4 39.8 %collective-permute-start.1 = (bf16[64,4224]{1,0:T(8,128)(2,1)}, bf16[64,4224]{1,0:T(8,128)(2,1)}, u32[]{:S(2)}, u32[]{:S(2)}) collective-permute-start(bf16[64,4224]{1,0:T(8,128)(2,1)} %collective-permute-done.refs_4_), channel_id=1, source_target_pairs={{0,1},{1,0},{2,3},{3,2},{4,5},{5,4},{6,7},{7,6},{8,9},{9,8},{10,11... | collective-permute-start | bytes 1622024 | tf_op jit(solution)/shard_map/ppermute | solution.py:286
  35.9 17.2 %collective-permute-start.9 = (bf16[64,4224]{1,0:T(8,128)(2,1)}, bf16[64,4224]{1,0:T(8,128)(2,1)S(1)}, u32[]{:S(2)}, u32[]{:S(2)}) collective-permute-start(bf16[64,4224]{1,0:T(8,128)(2,1)} %collective-permute-done.6.refs_2_), channel_id=1, source_target_pairs={{0,4},{2,6},{4,0},{6,2},{8,12},{10,14},{12,8},{14,10},{16,20},{18,... | collective-permute-start | bytes 1622024 | tf_op jit(solution)/shard_map/ppermute | solution.py:278
  37.2 14.0 %collective-permute-start.8 = (bf16[64,4224]{1,0:T(8,128)(2,1)}, bf16[64,4224]{1,0:T(8,128)(2,1)S(1)}, u32[]{:S(2)}, u32[]{:S(2)}) collective-permute-start(bf16[64,4224]{1,0:T(8,128)(2,1)} %collective-permute-done.6.refs_2_), channel_id=1, source_target_pairs={{0,8},{2,10},{4,12},{6,14},{8,16},{10,18},{12,20},{14,22},{16,24},... | collective-permute-start | bytes 1622024 | tf_op jit(solution)/shard_map/ppermute | solution.py:281
  37.2 26.0 %collective-permute-start.5 = (bf16[64,4224]{1,0:T(8,128)(2,1)}, bf16[64,4224]{1,0:T(8,128)(2,1)}, u32[]{:S(2)}, u32[]{:S(2)}) collective-permute-start(bf16[64,4224]{1,0:T(8,128)(2,1)} %collective-permute-done.4.refs_5_), channel_id=1, source_target_pairs={{0,1},{1,0},{2,3},{3,2},{4,5},{5,4},{6,7},{7,6},{8,9},{9,8},{10,11... | collective-permute-start | bytes 1622024 | tf_op jit(solution)/shard_map/ppermute | solution.py:286
  51.2 11.1 %collective-permute-start.10 = (bf16[64,4224]{1,0:T(8,128)(2,1)S(1)}, bf16[64,4224]{1,0:T(8,128)(2,1)S(1)}, u32[]{:S(2)}, u32[]{:S(2)}) collective-permute-start(bf16[64,4224]{1,0:T(8,128)(2,1)S(1)} %collective-permute-done.8.refs_3_), channel_id=1, source_target_pairs={{0,4},{2,6},{4,0},{6,2},{8,12},{10,14},{12,8},{14,10},{16,20},{18,... | collective-permute-start | bytes 1622024 | tf_op jit(solution)/shard_map/ppermute | solution.py:278
  69.1 58.1 %collective-permute-start.20 = (bf16[256,4224]{1,0:T(8,128)(2,1)}, bf16[256,4224]{1,0:T(8,128)(2,1)}, u32[]{:S(2)}, u32[]{:S(2)}) collective-permute-start(bf16[256,4224]{1,0:T(8,128)(2,1)} %constant_dynamic-update-slice_fusion), channel_id=1, source_target_pairs={{0,1},{1,0},{2,3},{3,2},{4,5},{5,4},{6,7},{7,6},{8,9},{9,8},{10,11... | collective-permute-start | bytes 6488072 | tf_op jit(solution)/shard_map/ppermute | solution.py:286
  84.0 14.8 %collective-permute-start.14 = (bf16[128,2048]{1,0:T(8,128)(2,1)S(1)}, bf16[128,2048]{1,0:T(8,128)(2,1)S(1)}, u32[]{:S(2)}, u32[]{:S(2)}) collective-permute-start(bf16[128,2048]{1,0:T(8,128)(2,1)S(1)} %fusion.55), channel_id=1, source_target_pairs={{0,4},{2,6},{4,0},{6,2},{8,12},{10,14},{12,8},{14,10},{16,20},{18,... | collective-permute-start | bytes 1572872 | tf_op jit(solution)/shard_map/ppermute | solution.py:278
  91.6 11.6 %collective-permute-start.13 = (bf16[256,2048]{1,0:T(8,128)(2,1)S(1)}, bf16[256,2048]{1,0:T(8,128)(2,1)S(1)}, u32[]{:S(2)}, u32[]{:S(2)}) collective-permute-start(bf16[256,2048]{1,0:T(8,128)(2,1)S(1)} %fusion.40), channel_id=1, source_target_pairs={{0,2},{2,0},{4,6},{6,4},{8,10},{10,8},{12,14},{14,12},{16,18},{18,... | collective-permute-start | bytes 3145736 | tf_op jit(solution)/shard_map/ppermute | solution.py:275
  93.1 17.0 %collective-permute-start.15 = (bf16[128,2048]{1,0:T(8,128)(2,1)S(1)}, bf16[128,2048]{1,0:T(8,128)(2,1)}, u32[]{:S(2)}, u32[]{:S(2)}) collective-permute-start(bf16[128,2048]{1,0:T(8,128)(2,1)S(1)} %slice.93), channel_id=1, source_target_pairs={{0,4},{2,6},{4,0},{6,2},{8,12},{10,14},{12,8},{14,10},{16,20},{18,... | collective-permute-start | bytes 1572872 | tf_op jit(solution)/shard_map/ppermute | solution.py:278
  98.8 24.0 %collective-permute-start.19 = (bf16[128,2048]{1,0:T(8,128)(2,1)}, bf16[128,2048]{1,0:T(8,128)(2,1)}, u32[]{:S(2)}, u32[]{:S(2)}) collective-permute-start(bf16[128,2048]{1,0:T(8,128)(2,1)} %fusion.61), channel_id=1, source_target_pairs={{0,4},{2,6},{4,0},{6,2},{8,12},{10,14},{12,8},{14,10},{16,20},{18,... | collective-permute-start | bytes 1572872 | tf_op jit(solution)/shard_map/ppermute | solution.py:278
  113.4 22.8 %collective-permute-start.16 = (bf16[64,2048]{1,0:T(8,128)(2,1)}, bf16[64,2048]{1,0:T(8,128)(2,1)}, u32[]{:S(2)}, u32[]{:S(2)}) collective-permute-start(bf16[64,2048]{1,0:T(8,128)(2,1)} %get-tuple-element.51), channel_id=1, source_target_pairs={{0,24},{2,26},{4,28},{6,30},{8,0},{10,2},{12,4},{14,6},{16,8},{18,... | collective-permute-start | bytes 786440 | tf_op jit(solution)/shard_map/ppermute | solution.py:281
  113.4 22.8 %collective-permute-start.17 = (bf16[64,2048]{1,0:T(8,128)(2,1)}, bf16[64,2048]{1,0:T(8,128)(2,1)}, u32[]{:S(2)}, u32[]{:S(2)}) collective-permute-start(bf16[64,2048]{1,0:T(8,128)(2,1)} %get-tuple-element.52), channel_id=1, source_target_pairs={{0,16},{2,18},{4,20},{6,22},{8,24},{10,26},{12,28},{14,30},{16,0},... | collective-permute-start | bytes 786440 | tf_op jit(solution)/shard_map/ppermute | solution.py:281
  114.6 18.3 %collective-permute-start.21 = (bf16[128,2048]{1,0:T(8,128)(2,1)}, bf16[128,2048]{1,0:T(8,128)(2,1)}, u32[]{:S(2)}, u32[]{:S(2)}) collective-permute-start(bf16[128,2048]{1,0:T(8,128)(2,1)} %slice.96), channel_id=1, source_target_pairs={{0,4},{2,6},{4,0},{6,2},{8,12},{10,14},{12,8},{14,10},{16,20},{18,... | collective-permute-start | bytes 1572872 | tf_op jit(solution)/shard_map/ppermute | solution.py:278
  122.8 13.3 %collective-permute-start.18 = (bf16[64,2048]{1,0:T(8,128)(2,1)S(1)}, bf16[64,2048]{1,0:T(8,128)(2,1)S(1)}, u32[]{:S(2)}, u32[]{:S(2)}) collective-permute-start(bf16[64,2048]{1,0:T(8,128)(2,1)S(1)} %copy-done.28), channel_id=1, source_target_pairs={{0,8},{2,10},{4,12},{6,14},{8,16},{10,18},{12,20},{14,22},{16,24},... | collective-permute-start | bytes 786440 | tf_op jit(solution)/shard_map/ppermute | solution.py:281
  136.1 5.1 %collective-permute-start.22 = (bf16[256,4224]{1,0:T(8,128)(2,1)}, bf16[256,4224]{1,0:T(8,128)(2,1)S(1)}, u32[]{:S(2)}, u32[]{:S(2)}) collective-permute-start(bf16[256,4224]{1,0:T(8,128)(2,1)} %get-tuple-element.62), channel_id=1, source_target_pairs={{0,2},{2,0},{4,6},{6,4},{8,10},{10,8},{12,14},{14,12},{16,18},{18,... | collective-permute-start | bytes 6488072 | tf_op jit(solution)/shard_map/ppermute | solution.py:275
  136.2 13.8 %collective-permute-start.23 = (bf16[64,2048]{1,0:T(8,128)(2,1)}, bf16[64,2048]{1,0:T(8,128)(2,1)S(1)}, u32[]{:S(2)}, u32[]{:S(2)}) collective-permute-start(bf16[64,2048]{1,0:T(8,128)(2,1)} %get-tuple-element.69), channel_id=1, source_target_pairs={{0,24},{2,26},{4,28},{6,30},{8,0},{10,2},{12,4},{14,6},{16,8},{18,... | collective-permute-start | bytes 786440 | tf_op jit(solution)/shard_map/ppermute | solution.py:281
  138.7 24.5 %collective-permute-start.24 = (bf16[64,2048]{1,0:T(8,128)(2,1)}, bf16[64,2048]{1,0:T(8,128)(2,1)S(1)}, u32[]{:S(2)}, u32[]{:S(2)}) collective-permute-start(bf16[64,2048]{1,0:T(8,128)(2,1)} %get-tuple-element.70), channel_id=1, source_target_pairs={{0,16},{2,18},{4,20},{6,22},{8,24},{10,26},{12,28},{14,30},{16,0},... | collective-permute-start | bytes 786440 | tf_op jit(solution)/shard_map/ppermute | solution.py:281
  139.3 23.9 %collective-permute-start.25 = (bf16[64,2048]{1,0:T(8,128)(2,1)}, bf16[64,2048]{1,0:T(8,128)(2,1)S(1)}, u32[]{:S(2)}, u32[]{:S(2)}) collective-permute-start(bf16[64,2048]{1,0:T(8,128)(2,1)} %get-tuple-element.71), channel_id=1, source_target_pairs={{0,8},{2,10},{4,12},{6,14},{8,16},{10,18},{12,20},{14,22},{16,24},... | collective-permute-start | bytes 786440 | tf_op jit(solution)/shard_map/ppermute | solution.py:281
  (31 other events, 231.7 us)

commit v21 on v20

--- a/solution.py
+++ b/solution.py
@@ -344,7 +344,7 @@
     d_gate, d_up = hidden_grads(cot, pre_gate, pre_up, w_down)
 
     grad_parts = leave(
-        lambda rows: input_rows(d_gate[rows], d_up[rows], w_gate, w_up), parts[2]
+        lambda rows: input_rows(d_gate[rows], d_up[rows], w_gate, w_up), *parts[2:]
     )
     chunks = home(after(place, grad_parts[0], grad_parts[1]), parts)
     own_grads = after((cot, d_gate, d_up), chunks[0])

time: 166 us -> 167 us (level)
  waiting for transfers between devices: 62 us -> 64.9 us
  starting transfers between devices: 27.1 us -> 25 us
    ppermute x8, waiting for transfers between devices: 18.1 us -> 21 us  [to_x(): return lax.ppermute(rows, 'expert', [(i, i ^ 2) for i in range(experts)])]
    ppermute x9, starting transfers between devices: 10 us -> 8.29 us  [to_z(): lax.ppermute(rows, 'expert', [(i, (i + 4 * step) % experts) for i in rang...]
    unnamed x61 -> x63, local copies, waits for them, and re-layouts: 6.79 us -> 6.75 us
  transfers between devices with their start and end apart: 26 -> 26, of which waited for: 8 -> 9; matrix products, arithmetic and copies ran while one was open for 30% -> 30% of each run, Pallas kernels for 7% -> 7%
where the time goes in v21:
time: 167 us; the launch traced here: 166 us
  waiting for transfers between devices  64.9 us (39%)
  matrix products  38.6 us (23%)
  starting transfers between devices  25 us (15%)
  Pallas kernels  20.2 us (12%)
  local copies, waits for them, and re-layouts  11.5 us (7%)
  other arithmetic  5.13 us (3%)
    ppermute x9, waiting for transfers between devices, to_z(): lax.ppermute(rows, 'expert', [(i, (i + 4 * step) % experts) for i in rang...  41 us
    ppermute x8, waiting for transfers between devices, to_x(): return lax.ppermute(rows, 'expert', [(i, i ^ 2) for i in range(experts)])  21 us
    dot_general x6, matrix products, outer_sum(): lax.dot_general(left, right, (((0,), (0,)), ((), ())), preferred_element_...  15.3 us
    pallas_call x2, Pallas kernels, plan_and_pack(): pl.pallas_call(body, grid_spec=pltpu.PrefetchScalarGridSpec(num_scalar_pr...  11.3 us
    dot_general x7, matrix products, dot(): return jnp.dot(left, right, preferred_element_type=F32)  10.3 us
    ppermute x8, starting transfers between devices, to_x(): return lax.ppermute(rows, 'expert', [(i, i ^ 2) for i in range(experts)])  9.51 us
    ppermute x9, starting transfers between devices, to_z(): lax.ppermute(rows, 'expert', [(i, (i + 4 * step) % experts) for i in rang...  8.29 us
    pallas_call x2, Pallas kernels, spread(): pl.pallas_call(body, grid=(1,), in_specs=[whole(place)] + [pl.BlockSpec((...  6.81 us
  transfers between devices with their start and end apart: 26, of which 9 were waited for; matrix products, arithmetic and copies ran while one was open for 30% of the time, Pallas kernels for 7%

profile of v21, /device:TPU:0, one launch (start us, length us, event | category | flops | bytes accessed | tf_op | source)
XLA Modules:
  0.0 166.4 jit_solution(7133198500498142906)
XLA Ops:
  0.6 2.1 %pair_up.1.refs_0_ = bf16[64,4224]{1,0:T(8,128)(2,1)} custom-call(bf16[64,2048]{1,0:T(8,128)(2,1)} %tokens_ref.1, bf16[64,2048]{1,0:T(8,128)(2,1)} %cots_ref.1, s32[6,64]{1,0:T(8,128)} %bitcast.78, f32[6,64]{1,0:T(8,128)} %bitcast.79), custom_call_target="tpu_custom_call" | custom-call | flops 1 | bytes 1 | tf_op jit(solution)/shard_map/pair_up/pallas_call | solution.py:252
  2.7 3.0 %collective-permute-start.2 = (bf16[64,4224]{1,0:T(8,128)(2,1)}, bf16[64,4224]{1,0:T(8,128)(2,1)}, u32[]{:S(2)}, u32[]{:S(2)}) collective-permute-start(bf16[64,4224]{1,0:T(8,128)(2,1)} %pair_up.1.refs_0_), channel_id=1, source_target_pairs={{0,8},{2,10},{4,12},{6,14},{8,16},{10,18},{12,20},{14,22},{16,24},... | collective-permute-start | bytes 1622024 | tf_op jit(solution)/shard_map/ppermute | solution.py:281
  8.8 11.6 %collective-permute-done.2.refs_1_ = bf16[64,4224]{1,0:T(8,128)(2,1)} collective-permute-done((bf16[64,4224]{1,0:T(8,128)(2,1)}, bf16[64,4224]{1,0:T(8,128)(2,1)}, u32[]{:S(2)}, u32[]{:S(2)}) %collective-permute-start.2) | collective-permute-done | bytes 540704 | tf_op jit(solution)/shard_map/ppermute | solution.py:281
  23.9 12.0 %collective-permute-done.6.refs_2_ = bf16[64,4224]{1,0:T(8,128)(2,1)} collective-permute-done((bf16[64,4224]{1,0:T(8,128)(2,1)}, bf16[64,4224]{1,0:T(8,128)(2,1)}, u32[]{:S(2)}, u32[]{:S(2)}) %collective-permute-start.6) | collective-permute-done | bytes 540704 | tf_op jit(solution)/shard_map/ppermute | solution.py:281
  40.6 10.6 %collective-permute-done.8.refs_3_ = bf16[64,4224]{1,0:T(8,128)(2,1)S(1)} collective-permute-done((bf16[64,4224]{1,0:T(8,128)(2,1)}, bf16[64,4224]{1,0:T(8,128)(2,1)S(1)}, u32[]{:S(2)}, u32[]{:S(2)}) %collective-permute-start.8) | collective-permute-done | bytes 540704 | tf_op jit(solution)/shard_map/ppermute | solution.py:281
  54.0 8.3 %collective-permute-done.10.refs_7_ = bf16[64,4224]{1,0:T(8,128)(2,1)S(1)} collective-permute-done((bf16[64,4224]{1,0:T(8,128)(2,1)S(1)}, bf16[64,4224]{1,0:T(8,128)(2,1)S(1)}, u32[]{:S(2)}, u32[]{:S(2)}) %collective-permute-start.10) | collective-permute-done | bytes 540704 | tf_op jit(solution)/shard_map/ppermute | solution.py:278
  63.3 5.7 %plan_and_pack.2 = (bf16[256,2048]{1,0:T(8,128)(2,1)}, bf16[256,2048]{1,0:T(8,128)(2,1)}, bf16[256,128]{1,0:T(8,128)(2,1)}, bf16[256,4224]{1,0:T(8,128)(2,1)}, bf16[256,512]{1,0:T(8,128)(2,1)}) custom-call(s32[1]{0:T(128)} %bitcast.expert_ref, bf16[64,4224]{1,0:T(8,128)(2,1)} %pair_up.1.refs_0_, bf16[64,4224]{1,0:T(8,128)(2,1)} %collective-permute-done.2.refs_1_, ...), custom_call_target="tpu_custom_call" | custom-call | flops 1 | bytes 1 | tf_op jit(solution)/shard_map/plan_and_pack/pallas_call | solution.py:185
  70.6 3.0 %collective-permute-done.11 = bf16[256,4224]{1,0:T(8,128)(2,1)} collective-permute-done((bf16[256,4224]{1,0:T(8,128)(2,1)}, bf16[256,4224]{1,0:T(8,128)(2,1)}, u32[]{:S(2)}, u32[]{:S(2)}) %collective-permute-start.11) | collective-permute-done | bytes 2162720 | tf_op jit(solution)/shard_map/ppermute | solution.py:275
  87.1 2.4 %multiply_convert_fusion.5 = (bf16[512,768]{1,0:T(8,128)(2,1)S(1)}, bf16[512,768]{1,0:T(8,128)(2,1)S(1)}) fusion(f32[512,768]{1,0:T(8,128)S(1)} %fusion.28, f32[512,768]{1,0:T(8,128)S(1)} %get-tuple-element.89, bf16[512,2048]{1,0:T(8,128)(2,1)S(1)} %multiply_convert_fusion.1, bf16[1,768,2048]{2,1,0:T(8,128)(2,1)S(1)} %copy-done), kind=kOutput, calls=%fused_computation.59 | convolution fusion | flops 1615724544 | bytes 9961472 | tf_op jit(solution)/shard_map/dot_general | solution.py:41
  93.9 2.0 %fusion.61 = bf16[128,2048]{1,0:T(8,128)(2,1)} fusion(f32[128,2048]{1,0:T(8,128)S(1)} %fusion.12, bf16[1,2048,768]{2,1,0:T(8,128)(2,1)S(1)} %copy-done.1, bf16[512,768]{1,0:T(8,128)(2,1)S(1)} %get-tuple-element.54), kind=kOutput, calls=%fused_computation.46 | convolution fusion | flops 403177472 | bytes 4915200 | tf_op jit(solution)/shard_map/dot_general | solution.py:49
  99.0 10.4 %collective-permute-done.15.refs_3_ = bf16[128,2048]{1,0:T(8,128)(2,1)S(1)} collective-permute-done((bf16[128,2048]{1,0:T(8,128)(2,1)S(1)}, bf16[128,2048]{1,0:T(8,128)(2,1)S(1)}, u32[]{:S(2)}, u32[]{:S(2)}) %collective-permute-start.15) | collective-permute-done | bytes 524320 | tf_op jit(solution)/shard_map/ppermute | solution.py:278
  110.7 3.6 %spread.2 = (bf16[64,2048]{1,0:T(8,128)(2,1)}, bf16[64,2048]{1,0:T(8,128)(2,1)}, bf16[64,2048]{1,0:T(8,128)(2,1)}, bf16[64,2048]{1,0:T(8,128)(2,1)}) custom-call(bf16[256,512]{1,0:T(8,128)(2,1)} %get-tuple-element.49.place_ref, bf16[128,2048]{1,0:T(8,128)(2,1)} %fusion.58.refs_0_, bf16[256,2048]{1,0:T(8,128)(2,1)} %copy-done.9, ...), custom_call_target="tpu_custom_call" | custom-call | flops 1 | bytes 1 | tf_op jit(solution)/shard_map/spread/pallas_call | solution.py:220
  116.3 4.3 %fusion.76 = f32[384,2048]{1,0:T(8,128)} fusion(bf16[512,2048]{1,0:T(8,128)(2,1)} %copy-done.5, bf16[512,768]{1,0:T(8,128)(2,1)S(1)} %get-tuple-element.88, s32[]{:T(128)S(6)} %select_n.27), kind=kOutput, calls=%fused_computation.73 | convolution fusion | flops 805306368 | bytes 5636100 | tf_op jit(solution)/shard_map/dot_general | solution.py:55
  120.7 2.7 %fusion.94 = f32[1024,768]{1,0:T(8,128)} fusion(bf16[512,768]{1,0:T(8,128)(2,1)S(1)} %copy-done.19, s32[]{:T(128)S(6)} %select_n.26, bf16[256,2048]{1,0:T(8,128)(2,1)S(1)} %copy-done.28, bf16[256,2048]{1,0:T(8,128)(2,1)S(1)} %copy-done.15), kind=kOutput, calls=%fused_computation.98 | convolution fusion | flops 807403520 | bytes 6029316 | tf_op jit(solution)/shard_map/dot_general | solution.py:55
  125.0 2.7 %fusion.92 = f32[1024,768]{1,0:T(8,128)} fusion(bf16[512,768]{1,0:T(8,128)(2,1)S(1)} %copy-done.21, s32[]{:T(128)S(6)} %select_n.26, bf16[256,2048]{1,0:T(8,128)(2,1)S(1)} %copy-done.28, bf16[256,2048]{1,0:T(8,128)(2,1)S(1)} %copy-done.15), kind=kOutput, calls=%fused_computation.97 | convolution fusion | flops 807403520 | bytes 6029316 | tf_op jit(solution)/shard_map/dot_general | solution.py:55
  127.8 5.7 %plan_and_pack.3 = (bf16[256,2048]{1,0:T(8,128)(2,1)}, bf16[256,2048]{1,0:T(8,128)(2,1)}, bf16[256,128]{1,0:T(8,128)(2,1)}, bf16[256,4224]{1,0:T(8,128)(2,1)}, bf16[256,512]{1,0:T(8,128)(2,1)}) custom-call(s32[1]{0:T(128)} %bitcast.expert_ref, bf16[64,4224]{1,0:T(8,128)(2,1)} %collective-permute-done.7.refs_0_, ...), custom_call_target="tpu_custom_call" | custom-call | flops 1 | bytes 1 | tf_op jit(solution)/shard_map/plan_and_pack/pallas_call | solution.py:185
  134.5 3.2 %spread.3 = (bf16[64,2048]{1,0:T(8,128)(2,1)}, bf16[64,2048]{1,0:T(8,128)(2,1)}, bf16[64,2048]{1,0:T(8,128)(2,1)}, bf16[64,2048]{1,0:T(8,128)(2,1)}) custom-call(bf16[256,512]{1,0:T(8,128)(2,1)} %get-tuple-element.49.place_ref, bf16[128,2048]{1,0:T(8,128)(2,1)} %fusion.64.refs_0_, bf16[256,2048]{1,0:T(8,128)(2,1)} %copy-done.8, ...), custom_call_target="tpu_custom_call" | custom-call | flops 1 | bytes 1 | tf_op jit(solution)/shard_map/spread/pallas_call | solution.py:220
  137.8 2.4 %collective-permute-start.23 = (bf16[64,2048]{1,0:T(8,128)(2,1)}, bf16[64,2048]{1,0:T(8,128)(2,1)S(1)}, u32[]{:S(2)}, u32[]{:S(2)}) collective-permute-start(bf16[64,2048]{1,0:T(8,128)(2,1)} %get-tuple-element.69), channel_id=1, source_target_pairs={{0,24},{2,26},{4,28},{6,30},{8,0},{10,2},{12,4},{14,6},{16,8},{18,... | collective-permute-start | bytes 786440 | tf_op jit(solution)/shard_map/ppermute | solution.py:281
  140.3 2.0 %collective-permute-start.25 = (bf16[64,2048]{1,0:T(8,128)(2,1)}, bf16[64,2048]{1,0:T(8,128)(2,1)S(1)}, u32[]{:S(2)}, u32[]{:S(2)}) collective-permute-start(bf16[64,2048]{1,0:T(8,128)(2,1)} %get-tuple-element.71), channel_id=1, source_target_pairs={{0,8},{2,10},{4,12},{6,14},{8,16},{10,18},{12,20},{14,22},{16,24},... | collective-permute-start | bytes 786440 | tf_op jit(solution)/shard_map/ppermute | solution.py:281
  146.4 2.2 %multiply_convert_fusion.2 = (bf16[512,768]{1,0:T(8,128)(2,1)S(1)}, bf16[512,768]{1,0:T(8,128)(2,1)S(1)}, f32[512,768]{1,0:T(8,128)S(1)}) fusion(f32[512,768]{1,0:T(8,128)S(1)} %fusion.20, f32[512,768]{1,0:T(8,128)S(1)} %fusion.10, bf16[1,768,2048]{2,1,0:T(8,128)(2,1)S(1)} %copy-done, bf16[256,2048]{1,0:T(8,128)(2,1)S(1)} %get-tuple-element.81, ...), kind=kOutput, calls=%fused_computation.55 | convolution fusion | flops 1622016000 | bytes 11536384 | tf_op jit(solution)/shard_map/dot_general | solution.py:41
  148.7 2.4 %fusion.36 = bf16[1,384,2048]{2,1,0:T(8,128)(2,1)} fusion(f32[384,2048]{1,0:T(8,128)S(1)} %copy-done.4, f32[512,768]{1,0:T(8,128)S(1)} %fusion.10, s32[]{:T(128)S(6)} %select_n.27, f32[512,768]{1,0:T(8,128)S(1)} %get-tuple-element.85, f32[512,768]{1,0:T(8,128)S(1)} %fusion.20, bf16[256,2048]{1,0:T(8,128)(2,1)S(1)} %get-tuple-element.81, ...), kind=kOutput, calls=%fused_computation.37 | convolution fusion | flops 813760512 | bytes 9177092 | tf_op jit(solution)/shard_map/dot_general | solution.py:55
  155.4 2.2 %fusion.68 = bf16[1,1024,768]{2,1,0:T(8,128)(2,1)} fusion(f32[1024,768]{1,0:T(8,128)S(1)} %copy-done.7, bf16[512,768]{1,0:T(8,128)(2,1)S(1)} %get-tuple-element.76, s32[]{:T(128)S(6)} %select_n.26, bf16[256,2048]{1,0:T(8,128)(2,1)S(1)} %copy-done.16, bf16[256,2048]{1,0:T(8,128)(2,1)S(1)} %get-tuple-element.82), kind=kOutput, calls=%fused_computation.62 | convolution fusion | flops 808976384 | bytes 7602180 | tf_op jit(solution)/shard_map/dot_general | solution.py:55
  157.6 6.7 %collective-permute-done.24 = bf16[64,2048]{1,0:T(8,128)(2,1)S(1)} collective-permute-done((bf16[64,2048]{1,0:T(8,128)(2,1)}, bf16[64,2048]{1,0:T(8,128)(2,1)S(1)}, u32[]{:S(2)}, u32[]{:S(2)}) %collective-permute-start.24) | collective-permute-done | bytes 262176 | tf_op jit(solution)/shard_map/ppermute | solution.py:281
  164.3 2.1 %add_convert_fusion.3 = (bf16[64,2048]{1,0:T(8,128)(2,1)}, bf16[64,2048]{1,0:T(8,128)(2,1)}) fusion(bf16[64,2048]{1,0:T(8,128)(2,1)S(1)} %collective-permute-done.25, bf16[64,2048]{1,0:T(8,128)(2,1)S(1)} %collective-permute-done.24, bf16[64,2048]{1,0:T(8,128)(2,1)S(1)} %collective-permute-done.23, bf16[64,2048]{1,0:T(8,128)(2,1)S(1)} %copy-done.25, ...), kind=kLoop, calls=%fused_computation.68 | loop fusion | flops 2097152 | bytes 2621440 | tf_op jit(solution)/shard_map/convert_element_type | solution.py:332
  (132 shorter events, 52.0 us)
Async XLA Ops:
  2.7 17.6 %collective-permute-start.2 = (bf16[64,4224]{1,0:T(8,128)(2,1)}, bf16[64,4224]{1,0:T(8,128)(2,1)}, u32[]{:S(2)}, u32[]{:S(2)}) collective-permute-start(bf16[64,4224]{1,0:T(8,128)(2,1)} %pair_up.1.refs_0_), channel_id=1, source_target_pairs={{0,8},{2,10},{4,12},{6,14},{8,16},{10,18},{12,20},{14,22},{16,24},... | collective-permute-start | bytes 1622024 | tf_op jit(solution)/shard_map/ppermute | solution.py:281
  5.8 17.6 %collective-permute-start = (bf16[64,4224]{1,0:T(8,128)(2,1)}, bf16[64,4224]{1,0:T(8,128)(2,1)}, u32[]{:S(2)}, u32[]{:S(2)}) collective-permute-start(bf16[64,4224]{1,0:T(8,128)(2,1)} %pair_up.1.refs_0_), channel_id=1, source_target_pairs={{0,4},{2,6},{4,0},{6,2},{8,12},{10,14},{12,8},{14,10},{16,20},{18,... | collective-permute-start | bytes 1622024 | tf_op jit(solution)/shard_map/ppermute | solution.py:278
  7.2 16.6 %collective-permute-start.7 = (bf16[64,4224]{1,0:T(8,128)(2,1)}, bf16[64,4224]{1,0:T(8,128)(2,1)}, u32[]{:S(2)}, u32[]{:S(2)}) collective-permute-start(bf16[64,4224]{1,0:T(8,128)(2,1)} %pair_up.1.refs_0_), channel_id=1, source_target_pairs={{0,1},{1,0},{2,3},{3,2},{4,5},{5,4},{6,7},{7,6},{8,9},{9,8},{10,11... | collective-permute-start | bytes 1622024 | tf_op jit(solution)/shard_map/ppermute | solution.py:286
  20.4 15.6 %collective-permute-start.6 = (bf16[64,4224]{1,0:T(8,128)(2,1)}, bf16[64,4224]{1,0:T(8,128)(2,1)}, u32[]{:S(2)}, u32[]{:S(2)}) collective-permute-start(bf16[64,4224]{1,0:T(8,128)(2,1)} %collective-permute-done.2.refs_1_), channel_id=1, source_target_pairs={{0,8},{2,10},{4,12},{6,14},{8,16},{10,18},{12,20},{14,22},{16,24},... | collective-permute-start | bytes 1622024 | tf_op jit(solution)/shard_map/ppermute | solution.py:281
  20.4 16.8 %collective-permute-start.4 = (bf16[64,4224]{1,0:T(8,128)(2,1)}, bf16[64,4224]{1,0:T(8,128)(2,1)}, u32[]{:S(2)}, u32[]{:S(2)}) collective-permute-start(bf16[64,4224]{1,0:T(8,128)(2,1)} %collective-permute-done.2.refs_1_), channel_id=1, source_target_pairs={{0,4},{2,6},{4,0},{6,2},{8,12},{10,14},{12,8},{14,10},{16,20},{18,... | collective-permute-start | bytes 1622024 | tf_op jit(solution)/shard_map/ppermute | solution.py:278
  21.9 41.3 %collective-permute-start.3 = (bf16[64,4224]{1,0:T(8,128)(2,1)}, bf16[64,4224]{1,0:T(8,128)(2,1)}, u32[]{:S(2)}, u32[]{:S(2)}) collective-permute-start(bf16[64,4224]{1,0:T(8,128)(2,1)} %collective-permute-done.2.refs_1_), channel_id=1, source_target_pairs={{0,1},{1,0},{2,3},{3,2},{4,5},{5,4},{6,7},{7,6},{8,9},{9,8},{10,11... | collective-permute-start | bytes 1622024 | tf_op jit(solution)/shard_map/ppermute | solution.py:286
  23.4 39.8 %collective-permute-start.1 = (bf16[64,4224]{1,0:T(8,128)(2,1)}, bf16[64,4224]{1,0:T(8,128)(2,1)}, u32[]{:S(2)}, u32[]{:S(2)}) collective-permute-start(bf16[64,4224]{1,0:T(8,128)(2,1)} %collective-permute-done.refs_4_), channel_id=1, source_target_pairs={{0,1},{1,0},{2,3},{3,2},{4,5},{5,4},{6,7},{7,6},{8,9},{9,8},{10,11... | collective-permute-start | bytes 1622024 | tf_op jit(solution)/shard_map/ppermute | solution.py:286
  35.9 17.2 %collective-permute-start.9 = (bf16[64,4224]{1,0:T(8,128)(2,1)}, bf16[64,4224]{1,0:T(8,128)(2,1)S(1)}, u32[]{:S(2)}, u32[]{:S(2)}) collective-permute-start(bf16[64,4224]{1,0:T(8,128)(2,1)} %collective-permute-done.6.refs_2_), channel_id=1, source_target_pairs={{0,4},{2,6},{4,0},{6,2},{8,12},{10,14},{12,8},{14,10},{16,20},{18,... | collective-permute-start | bytes 1622024 | tf_op jit(solution)/shard_map/ppermute | solution.py:278
  37.2 14.0 %collective-permute-start.8 = (bf16[64,4224]{1,0:T(8,128)(2,1)}, bf16[64,4224]{1,0:T(8,128)(2,1)S(1)}, u32[]{:S(2)}, u32[]{:S(2)}) collective-permute-start(bf16[64,4224]{1,0:T(8,128)(2,1)} %collective-permute-done.6.refs_2_), channel_id=1, source_target_pairs={{0,8},{2,10},{4,12},{6,14},{8,16},{10,18},{12,20},{14,22},{16,24},... | collective-permute-start | bytes 1622024 | tf_op jit(solution)/shard_map/ppermute | solution.py:281
  37.2 26.0 %collective-permute-start.5 = (bf16[64,4224]{1,0:T(8,128)(2,1)}, bf16[64,4224]{1,0:T(8,128)(2,1)}, u32[]{:S(2)}, u32[]{:S(2)}) collective-permute-start(bf16[64,4224]{1,0:T(8,128)(2,1)} %collective-permute-done.4.refs_5_), channel_id=1, source_target_pairs={{0,1},{1,0},{2,3},{3,2},{4,5},{5,4},{6,7},{7,6},{8,9},{9,8},{10,11... | collective-permute-start | bytes 1622024 | tf_op jit(solution)/shard_map/ppermute | solution.py:286
  51.2 11.1 %collective-permute-start.10 = (bf16[64,4224]{1,0:T(8,128)(2,1)S(1)}, bf16[64,4224]{1,0:T(8,128)(2,1)S(1)}, u32[]{:S(2)}, u32[]{:S(2)}) collective-permute-start(bf16[64,4224]{1,0:T(8,128)(2,1)S(1)} %collective-permute-done.8.refs_3_), channel_id=1, source_target_pairs={{0,4},{2,6},{4,0},{6,2},{8,12},{10,14},{12,8},{14,10},{16,20},{18,... | collective-permute-start | bytes 1622024 | tf_op jit(solution)/shard_map/ppermute | solution.py:278
  69.0 4.7 %collective-permute-start.11 = (bf16[256,4224]{1,0:T(8,128)(2,1)}, bf16[256,4224]{1,0:T(8,128)(2,1)}, u32[]{:S(2)}, u32[]{:S(2)}) collective-permute-start(bf16[256,4224]{1,0:T(8,128)(2,1)} %get-tuple-element.45), channel_id=1, source_target_pairs={{0,2},{2,0},{4,6},{6,4},{8,10},{10,8},{12,14},{14,12},{16,18},{18,... | collective-permute-start | bytes 6488072 | tf_op jit(solution)/shard_map/ppermute | solution.py:275
  69.1 58.7 %collective-permute-start.20 = (bf16[256,4224]{1,0:T(8,128)(2,1)}, bf16[256,4224]{1,0:T(8,128)(2,1)}, u32[]{:S(2)}, u32[]{:S(2)}) collective-permute-start(bf16[256,4224]{1,0:T(8,128)(2,1)} %constant_dynamic-update-slice_fusion), channel_id=1, source_target_pairs={{0,1},{1,0},{2,3},{3,2},{4,5},{5,4},{6,7},{7,6},{8,9},{9,8},{10,11... | collective-permute-start | bytes 6488072 | tf_op jit(solution)/shard_map/ppermute | solution.py:286
  84.0 15.1 %collective-permute-start.14 = (bf16[128,2048]{1,0:T(8,128)(2,1)S(1)}, bf16[128,2048]{1,0:T(8,128)(2,1)S(1)}, u32[]{:S(2)}, u32[]{:S(2)}) collective-permute-start(bf16[128,2048]{1,0:T(8,128)(2,1)S(1)} %fusion.55), channel_id=1, source_target_pairs={{0,4},{2,6},{4,0},{6,2},{8,12},{10,14},{12,8},{14,10},{16,20},{18,... | collective-permute-start | bytes 1572872 | tf_op jit(solution)/shard_map/ppermute | solution.py:278
  91.6 19.1 %collective-permute-start.13 = (bf16[256,2048]{1,0:T(8,128)(2,1)S(1)}, bf16[256,2048]{1,0:T(8,128)(2,1)S(1)}, u32[]{:S(2)}, u32[]{:S(2)}) collective-permute-start(bf16[256,2048]{1,0:T(8,128)(2,1)S(1)} %fusion.40), channel_id=1, source_target_pairs={{0,2},{2,0},{4,6},{6,4},{8,10},{10,8},{12,14},{14,12},{16,18},{18,... | collective-permute-start | bytes 3145736 | tf_op jit(solution)/shard_map/ppermute | solution.py:275
  93.1 16.3 %collective-permute-start.15 = (bf16[128,2048]{1,0:T(8,128)(2,1)S(1)}, bf16[128,2048]{1,0:T(8,128)(2,1)S(1)}, u32[]{:S(2)}, u32[]{:S(2)}) collective-permute-start(bf16[128,2048]{1,0:T(8,128)(2,1)S(1)} %slice.93), channel_id=1, source_target_pairs={{0,4},{2,6},{4,0},{6,2},{8,12},{10,14},{12,8},{14,10},{16,20},{18,... | collective-permute-start | bytes 1572872 | tf_op jit(solution)/shard_map/ppermute | solution.py:278
  109.5 15.2 %collective-permute-start.19 = (bf16[128,2048]{1,0:T(8,128)(2,1)}, bf16[128,2048]{1,0:T(8,128)(2,1)}, u32[]{:S(2)}, u32[]{:S(2)}) collective-permute-start(bf16[128,2048]{1,0:T(8,128)(2,1)} %fusion.61), channel_id=1, source_target_pairs={{0,4},{2,6},{4,0},{6,2},{8,12},{10,14},{12,8},{14,10},{16,20},{18,... | collective-permute-start | bytes 1572872 | tf_op jit(solution)/shard_map/ppermute | solution.py:278
  114.3 23.4 %collective-permute-start.16 = (bf16[64,2048]{1,0:T(8,128)(2,1)}, bf16[64,2048]{1,0:T(8,128)(2,1)}, u32[]{:S(2)}, u32[]{:S(2)}) collective-permute-start(bf16[64,2048]{1,0:T(8,128)(2,1)} %get-tuple-element.51), channel_id=1, source_target_pairs={{0,24},{2,26},{4,28},{6,30},{8,0},{10,2},{12,4},{14,6},{16,8},{18,... | collective-permute-start | bytes 786440 | tf_op jit(solution)/shard_map/ppermute | solution.py:281
  114.3 23.4 %collective-permute-start.17 = (bf16[64,2048]{1,0:T(8,128)(2,1)}, bf16[64,2048]{1,0:T(8,128)(2,1)}, u32[]{:S(2)}, u32[]{:S(2)}) collective-permute-start(bf16[64,2048]{1,0:T(8,128)(2,1)} %get-tuple-element.52), channel_id=1, source_target_pairs={{0,16},{2,18},{4,20},{6,22},{8,24},{10,26},{12,28},{14,30},{16,0},... | collective-permute-start | bytes 786440 | tf_op jit(solution)/shard_map/ppermute | solution.py:281
  115.5 18.9 %collective-permute-start.21 = (bf16[128,2048]{1,0:T(8,128)(2,1)}, bf16[128,2048]{1,0:T(8,128)(2,1)}, u32[]{:S(2)}, u32[]{:S(2)}) collective-permute-start(bf16[128,2048]{1,0:T(8,128)(2,1)} %slice.96), channel_id=1, source_target_pairs={{0,4},{2,6},{4,0},{6,2},{8,12},{10,14},{12,8},{14,10},{16,20},{18,... | collective-permute-start | bytes 1572872 | tf_op jit(solution)/shard_map/ppermute | solution.py:278
  124.6 13.1 %collective-permute-start.18 = (bf16[64,2048]{1,0:T(8,128)(2,1)S(1)}, bf16[64,2048]{1,0:T(8,128)(2,1)S(1)}, u32[]{:S(2)}, u32[]{:S(2)}) collective-permute-start(bf16[64,2048]{1,0:T(8,128)(2,1)S(1)} %copy-done.29), channel_id=1, source_target_pairs={{0,8},{2,10},{4,12},{6,14},{8,16},{10,18},{12,20},{14,22},{16,24},... | collective-permute-start | bytes 786440 | tf_op jit(solution)/shard_map/ppermute | solution.py:281
  137.8 13.2 %collective-permute-start.23 = (bf16[64,2048]{1,0:T(8,128)(2,1)}, bf16[64,2048]{1,0:T(8,128)(2,1)S(1)}, u32[]{:S(2)}, u32[]{:S(2)}) collective-permute-start(bf16[64,2048]{1,0:T(8,128)(2,1)} %get-tuple-element.69), channel_id=1, source_target_pairs={{0,24},{2,26},{4,28},{6,30},{8,0},{10,2},{12,4},{14,6},{16,8},{18,... | collective-permute-start | bytes 786440 | tf_op jit(solution)/shard_map/ppermute | solution.py:281
  140.2 24.0 %collective-permute-start.24 = (bf16[64,2048]{1,0:T(8,128)(2,1)}, bf16[64,2048]{1,0:T(8,128)(2,1)S(1)}, u32[]{:S(2)}, u32[]{:S(2)}) collective-permute-start(bf16[64,2048]{1,0:T(8,128)(2,1)} %get-tuple-element.70), channel_id=1, source_target_pairs={{0,16},{2,18},{4,20},{6,22},{8,24},{10,26},{12,28},{14,30},{16,0},... | collective-permute-start | bytes 786440 | tf_op jit(solution)/shard_map/ppermute | solution.py:281
  140.3 24.0 %collective-permute-start.25 = (bf16[64,2048]{1,0:T(8,128)(2,1)}, bf16[64,2048]{1,0:T(8,128)(2,1)S(1)}, u32[]{:S(2)}, u32[]{:S(2)}) collective-permute-start(bf16[64,2048]{1,0:T(8,128)(2,1)} %get-tuple-element.71), channel_id=1, source_target_pairs={{0,8},{2,10},{4,12},{6,14},{8,16},{10,18},{12,20},{14,22},{16,24},... | collective-permute-start | bytes 786440 | tf_op jit(solution)/shard_map/ppermute | solution.py:281
  (32 other events, 225.8 us)
